TPU v7x, 32 devices: a whole 2x2x4 slice. The times are simulated.
32 devices in a mesh: row: 8 (over y, x, core), col: 4 (over z).
Axes of the slice: x: 2, y: 2, z: 4, core: 2. Of those that a mesh axis runs over, the one named last changes fastest.
Arguments:
- tile_entries: float32 [8, 4, 64, 128, 128], P('row', 'col'), may hold values from 0 to 65520, as said below
- tile_rows: int32 [8, 4, 64], P('row', 'col'), may hold values from 0 to 7, as said below
- tile_cols: int32 [8, 4, 64], P('row', 'col'), may hold values from 0 to 15, as said below
- tile_count: int32 [8, 4], P('row', 'col'), may hold values from 8 to 64, as said below
- block_x: float32 [64, 8192], P(None, ('row', 'col')), may hold values from 0 to 65520, as said below
- block_y: float32 [64, 8192], P(None, ('row', 'col')), may hold values from 0 to 65520, as said below
Outputs:
- matrix_poly: float32 [3, 64, 64], replicated
- vector_last: float32 [64, 8192], P(None, ('row', 'col'))
Inputs may be any that keep to these rules, and one draw needn't show every extreme that they name: `tile_entries`: whole numbers. `block_x`: whole numbers. `block_y`: whole numbers. The slots of one device name distinct block pairs (tile_rows, tile_cols), among them (0, 0) and (7, 15) in some slot. `tile_cols`: block column k of column group c is the global block column (k // 2) * 8 + c * 2 + k % 2. Slots 0 to tile_count - 1 of a device hold its tiles, the rest are unused; some device fills all 64 slots.
All inputs are finite; a program needn't handle non-finite values.
Results may differ from a plain program's by a relative error of at most 0.0003.
Values sent between devices are 32-bit elements; how exact they have to be, the bound alone decides.
No kernel may reach another device: no remote copies, remote signals or barrier semaphores. Data moves between devices by JAX's collectives and lax.ppermute only.
A program may use at most 64 MiB of HBM per device.

v0:
```python
import jax
import jax.numpy as jnp
from jax import lax
from jax.sharding import PartitionSpec as P

STEP_COUNT = 3


MODULUS = 65521.0
HALF_MODULUS = 32760.0


def reduce_mod(values):
    quotient = jnp.floor(values / MODULUS)
    leftover = values - quotient * MODULUS
    leftover = jnp.where(leftover < 0, leftover + MODULUS, leftover)
    return jnp.where(leftover >= MODULUS, leftover - MODULUS, leftover)


def split_digits(values):
    high_digit = jnp.floor(values / 256.0)
    return (high_digit, values - 256.0 * high_digit)


def combine_parts(high_part, middle_part, low_part):
    return reduce_mod(
        15.0 * reduce_mod(high_part)
        + reduce_mod(256.0 * reduce_mod(middle_part))
        + reduce_mod(low_part)
    )


def centered(residues):
    return jnp.where(residues > HALF_MODULUS, residues - MODULUS, residues)


def vector_digits(vector):
    high_v, low_v = split_digits(vector)
    return jnp.concatenate([high_v, low_v], 0).astype(jnp.bfloat16)


def poly_product(left_side, right_side):
    span_width = left_side.shape[-1]
    left_high, left_low = split_digits(left_side)
    right_high, right_low = split_digits(right_side)
    stacked_left = jnp.concatenate([left_high, left_low], 1).astype(jnp.bfloat16)
    stacked_right = jnp.concatenate([right_high, right_low], 2).astype(jnp.bfloat16)
    products = jnp.einsum(
        "kmj,kjn->kmn", stacked_left, stacked_right, preferred_element_type=jnp.float32
    )
    return combine_parts(
        products[:, :span_width, :span_width],
        products[:, :span_width, span_width:] + products[:, span_width:, :span_width],
        products[:, span_width:, span_width:],
    )


def sigma_update(projections):
    span_width = projections[0].shape[0]
    term_count = len(projections) + 1
    identity = jnp.eye(span_width, dtype=jnp.float32)[None]
    polynomial = jnp.concatenate(
        [identity, jnp.zeros((term_count - 1, span_width, span_width), jnp.float32)], 0
    )
    for step_index in range(1, term_count):
        known_terms = jnp.stack(
            [projections[step_index - 1 - shift] for shift in range(step_index)]
        )
        discrepancy = reduce_mod(jnp.sum(poly_product(polynomial[:step_index], known_terms), 0))
        scaled = poly_product(jnp.broadcast_to(discrepancy, polynomial.shape), polynomial)
        shifted = jnp.concatenate(
            [jnp.zeros((1, span_width, span_width), jnp.float32), polynomial[:-1]], 0
        )
        polynomial = reduce_mod(shifted - scaled)
    return polynomial


def project_local(x_part, v_part, tile_len):
    span_width = x_part.shape[0]
    block_total = x_part.shape[1] // tile_len
    x_digits = vector_digits(x_part).reshape(2 * span_width, block_total, tile_len)
    v_digits = vector_digits(v_part).reshape(2 * span_width, block_total, tile_len)
    products = jnp.einsum("mbk,nbk->bmn", x_digits, v_digits, preferred_element_type=jnp.float32)
    residues = combine_parts(
        products[:, :span_width, :span_width],
        products[:, :span_width, span_width:] + products[:, span_width:, :span_width],
        products[:, span_width:, span_width:],
    )
    return reduce_mod(jnp.sum(residues, 0))


def local(tile_entries, tile_rows, tile_cols, tile_count, block_x, block_y):
    entries = tile_entries[0, 0]
    rows_here = tile_rows[0, 0]
    cols_here = tile_cols[0, 0]
    count_here = tile_count[0, 0]
    slot_count = entries.shape[0]
    tile_len = entries.shape[1]
    span_width = block_y.shape[0]
    piece_len = block_y.shape[1]
    row_blocks = piece_len // tile_len * lax.axis_size("col")
    high_a, low_a = split_digits(entries)
    a_digits = jnp.stack([high_a, low_a], 1).astype(jnp.bfloat16)
    live_slots = (jnp.arange(slot_count, dtype=jnp.int32) < count_here).astype(jnp.float32)
    onehot = (rows_here[None, :] == jnp.arange(row_blocks, dtype=jnp.int32)[:, None]).astype(
        jnp.float32
    )
    onehot = onehot * live_slots[None, :]
    vector = block_y
    projections = []
    for step_index in range(STEP_COUNT):
        gathered = lax.all_gather(vector, "row", axis=1, tiled=True)
        v_digits = vector_digits(gathered).reshape(2 * span_width, -1, tile_len)
        picked = jnp.take(v_digits, cols_here, axis=1)
        products = jnp.einsum(
            "ntk,tdik->tdni", picked, a_digits, preferred_element_type=jnp.float32
        )
        residues = combine_parts(
            products[:, 0, :span_width],
            products[:, 0, span_width:] + products[:, 1, :span_width],
            products[:, 1, span_width:],
        )
        summed = jnp.einsum("bt,twi->wbi", onehot, residues, precision=lax.Precision.HIGHEST)
        partial_rows = reduce_mod(summed).reshape(span_width, row_blocks * tile_len)
        reduced = lax.psum_scatter(partial_rows, "col", scatter_dimension=1, tiled=True)
        vector = reduce_mod(reduced)
        partial_terms = centered(project_local(block_x, vector, tile_len))
        projections.append(reduce_mod(lax.psum(partial_terms, ("row", "col"))))
    polynomial = sigma_update(projections)
    return (polynomial[:-1] / MODULUS, vector / MODULUS)


def solution(mesh):
    placed = (
        P("row", "col", None, None, None),
        P("row", "col", None),
        P("row", "col", None),
        P("row", "col"),
        P(None, ("row", "col")),
        P(None, ("row", "col")),
    )
    return jax.shard_map(
        local, mesh=mesh, in_specs=placed, out_specs=(P(), P(None, ("row", "col"))), check_vma=False
    )
```

profile of v0, /device:TPU:0, one launch (start us, length us, event | category | flops | bytes accessed | tf_op | source)
XLA Modules:
  0.0 193.8 jit_solution(13098423190701030125)
XLA Ops:
  7.2 0.7 compare_select_fusion.159
  7.9 0.7 compare_and_fusion
  8.5 11.6 %all_gather.9 = f32[64,2048]{1,0:T(8,128)S(1)} all-gather(f32[64,256]{1,0:T(8,128)} %param.13), channel_id=1, replica_groups=mesh['row'=8,'col'=4] {'row'}, dimensions={1}, use_global_device_ids=true | all-gather | bytes 589824 | tf_op jit(solution)/shard_map/all_gather | solution.py:112
  20.3 4.8 %fusion.2 = (bf16[64,1,128,128]{3,2,1,0:T(8,128)(2,1)S(1)}, bf16[64,1,128,128]{3,2,1,0:T(8,128)(2,1)}) fusion(f32[1,1,64,128,128]{4,3,2,1,0:T(8,128)} %param.8), kind=kLoop, calls=%fused_computation.38 | loop fusion | flops 6291456 | bytes 8388608 | tf_op jit(solution)/shard_map/convert.48
  25.0 0.1 copy_bitcast_fusion.7
  25.2 2.1 %gather_fusion = bf16[64,128,128]{2,1,0:T(8,128)(2,1)} fusion(bf16[128,16,128]{2,0,1:T(8,128)(2,1)S(1)} %pad_maximum_fusion.1, s32[1024]{0:T(1024)S(1)} %pad_clamp_fusion), kind=kCustom, calls=%fused_computation.clone | custom fusion | bytes 4194560 | tf_op jit(solution)/shard_map/jit(_take)/gather | solution.py:114
  27.3 3.5 %convolution_bitcast_fusion = f32[64,2,128,128]{3,2,1,0:T(8,128)S(1)} fusion(bf16[64,128,128]{2,1,0:T(8,128)(2,1)} %gather_fusion, pred[64]{0:T(512)(128)(4,1)S(1)} %compare_and_fusion, bf16[64,1,128,128]{3,2,1,0:T(8,128)(2,1)} %get-tuple-element.15, bf16[64,1,128,128]{3,2,1,0:T(8,128)(2,1)S(1)} %get-tuple-element.14), kind=kOutput, calls=%fused_computation.45 | convolution fusion | flops 540016640 | bytes 14680128 | tf_op jit(solution)/shard_map/ntk,tdik->tdni/dot_general | solution.py:115
  30.9 3.8 %compare_select_fusion.20 = f32[64,64,128]{2,1,0:T(8,128)S(1)} fusion(f32[64,2,128,128]{3,2,1,0:T(8,128)S(1)} %convolution_bitcast_fusion), kind=kLoop, calls=%fused_computation.23 | loop fusion | flops 28835840 | bytes 10485760 | tf_op jit(solution)/shard_map/jit(_where)/select_n | solution.py:17
  35.4 2.4 %compare_select_fusion.34 = f32[64,8,128]{2,1,0:T(8,128)S(1)} fusion(f32[64,64,128]{2,1,0:T(8,128)S(1)} %compare_select_fusion.20, f32[64]{0:T(128)S(1)} %compare_convert_fusion, s32[64]{0:T(128)S(1)} %bitcast.244), kind=kOutput, calls=%fused_computation.95 | convolution fusion | flops 50988032 | bytes 2359808 | tf_op jit(solution)/shard_map/bt,twi->wbi/dot_general | solution.py:123
  37.8 0.7 copy.149
  38.8 19.8 %reduce-scatter.4.cloned.1.call-done = f32[64,256]{1,0:T(8,128)} async-done(((f32[64,1024]{1,0:T(8,128)}), f32[64,256]{1,0:T(8,128)}) %reduce-scatter.4.cloned.1.call-update) | async-done | bytes 65552 | tf_op jit(solution)/shard_map/reduce_scatter | solution.py:125
  58.6 0.9 compare_select_fusion.126
  59.5 10.1 %all_gather.10 = f32[64,2048]{1,0:T(8,128)S(1)} all-gather(f32[64,256]{1,0:T(8,128)S(1)} %get-tuple-element.37), channel_id=1, replica_groups=mesh['row'=8,'col'=4] {'row'}, dimensions={1}, use_global_device_ids=true | all-gather | bytes 589824 | tf_op jit(solution)/shard_map/all_gather | solution.py:112
  69.9 2.1 %gather_fusion.1 = bf16[64,128,128]{2,1,0:T(8,128)(2,1)} fusion(bf16[128,16,128]{2,0,1:T(8,128)(2,1)S(1)} %pad_maximum_fusion.2, s32[1024]{0:T(1024)S(1)} %pad_clamp_fusion), kind=kCustom, calls=%fused_computation.1.clone | custom fusion | bytes 4194560 | tf_op jit(solution)/shard_map/jit(_take)/gather | solution.py:114
  72.0 3.5 %fusion.7 = f32[64,2,128,128]{3,2,0,1:T(8,128)S(1)} fusion(bf16[64,128,128]{2,1,0:T(8,128)(2,1)} %gather_fusion.1, pred[64]{0:T(512)(128)(4,1)S(1)} %compare_and_fusion, bf16[64,1,128,128]{3,2,1,0:T(8,128)(2,1)} %get-tuple-element.15, bf16[64,1,128,128]{3,2,1,0:T(8,128)(2,1)S(1)} %get-tuple-element.14), kind=kOutput, calls=%fused_computation.43 | convolution fusion | flops 540016640 | bytes 14680128 | tf_op jit(solution)/shard_map/ntk,tdik->tdni/dot_general | solution.py:115
  75.6 3.8 %compare_select_fusion.10 = f32[64,64,128]{2,1,0:T(8,128)S(1)} fusion(f32[64,2,128,128]{3,2,0,1:T(8,128)S(1)} %fusion.7), kind=kLoop, calls=%fused_computation.13 | loop fusion | flops 28835840 | bytes 10485760 | tf_op jit(solution)/shard_map/jit(_where)/select_n | solution.py:17
  79.4 2.4 %compare_select_fusion.32 = f32[64,8,128]{2,1,0:T(8,128)S(1)} fusion(f32[64,64,128]{2,1,0:T(8,128)S(1)} %compare_select_fusion.10, f32[64]{0:T(128)S(1)} %compare_convert_fusion, s32[64]{0:T(128)S(1)} %bitcast.245), kind=kOutput, calls=%fused_computation.93 | convolution fusion | flops 50988032 | bytes 2359808 | tf_op jit(solution)/shard_map/bt,twi->wbi/dot_general | solution.py:123
  81.8 0.7 copy.148
  82.6 0.2 fusion.114
  82.8 0.2 fusion.101
  83.0 16.6 %reduce-scatter.6.cloned.1.call-done = f32[64,256]{1,0:T(8,128)} async-done(((f32[64,1024]{1,0:T(8,128)}), f32[64,256]{1,0:T(8,128)}) %reduce-scatter.6.cloned.1.call-update) | async-done | bytes 65552 | tf_op jit(solution)/shard_map/reduce_scatter | solution.py:125
  99.6 0.9 compare_select_fusion.114
  100.5 10.1 %all_gather.11 = f32[64,2048]{1,0:T(8,128)S(1)} all-gather(f32[64,256]{1,0:T(8,128)S(1)} %get-tuple-element.34), channel_id=1, replica_groups=mesh['row'=8,'col'=4] {'row'}, dimensions={1}, use_global_device_ids=true | all-gather | bytes 589824 | tf_op jit(solution)/shard_map/all_gather | solution.py:112
  110.9 2.1 %gather_fusion.2 = bf16[64,128,128]{2,1,0:T(8,128)(2,1)} fusion(bf16[128,16,128]{2,0,1:T(8,128)(2,1)S(1)} %pad_maximum_fusion.3, s32[1024]{0:T(1024)S(1)} %pad_clamp_fusion), kind=kCustom, calls=%fused_computation.2.clone | custom fusion | bytes 4194560 | tf_op jit(solution)/shard_map/jit(_take)/gather | solution.py:114
  113.1 3.5 %fusion.10 = f32[64,2,128,128]{3,2,0,1:T(8,128)S(1)} fusion(bf16[64,128,128]{2,1,0:T(8,128)(2,1)} %gather_fusion.2, pred[64]{0:T(512)(128)(4,1)S(1)} %compare_and_fusion, bf16[64,1,128,128]{3,2,1,0:T(8,128)(2,1)} %get-tuple-element.15, bf16[64,1,128,128]{3,2,1,0:T(8,128)(2,1)S(1)} %get-tuple-element.14), kind=kOutput, calls=%fused_computation.44 | convolution fusion | flops 540016640 | bytes 14680128 | tf_op jit(solution)/shard_map/ntk,tdik->tdni/dot_general | solution.py:115
  116.6 3.8 %compare_select_fusion = f32[64,64,128]{2,1,0:T(8,128)S(1)} fusion(f32[64,2,128,128]{3,2,0,1:T(8,128)S(1)} %fusion.10), kind=kLoop, calls=%fused_computation.3 | loop fusion | flops 28835840 | bytes 10485760 | tf_op jit(solution)/shard_map/jit(_where)/select_n | solution.py:17
  120.4 2.4 %compare_select_fusion.30 = f32[64,8,128]{2,1,0:T(8,128)S(1)} fusion(f32[64,64,128]{2,1,0:T(8,128)S(1)} %compare_select_fusion, f32[64]{0:T(128)S(1)} %compare_convert_fusion, s32[64]{0:T(128)S(1)} %bitcast.246), kind=kOutput, calls=%fused_computation.91 | convolution fusion | flops 50988032 | bytes 2359808 | tf_op jit(solution)/shard_map/bt,twi->wbi/dot_general | solution.py:123
  122.8 0.8 copy.147
  123.6 0.2 fusion.129
  123.8 0.2 fusion.105
  124.0 16.7 %reduce-scatter.8.cloned.1.call-done = f32[64,256]{1,0:T(8,128)} async-done(((f32[64,1024]{1,0:T(8,128)}), f32[64,256]{1,0:T(8,128)}) %reduce-scatter.8.cloned.1.call-update) | async-done | bytes 65552 | tf_op jit(solution)/shard_map/reduce_scatter | solution.py:125
  140.7 1.5 broadcast_multiply_fusion
  142.2 0.2 fusion.140
  142.4 0.2 fusion.113
  142.6 39.6 %all-reduce.4 = (f32[64,64]{1,0:T(8,128)S(1)}, f32[64,64]{1,0:T(8,128)S(1)}, f32[64,64]{1,0:T(8,128)S(1)}) all-reduce(f32[64,64]{1,0:T(8,128)S(1)} %compare_select_fusion.156, f32[64,64]{1,0:T(8,128)S(1)} %compare_select_fusion.139, f32[64,64]{1,0:T(8,128)S(1)} %compare_select_fusion.132), channel_id=1, replica_groups=mesh['row'=8,'col'=4] {'row','col'}, use_global_device_ids=true, to_apply=%region_2.4 | all-reduce | flops 12288 | bytes 98304 | tf_op jit(solution)/shard_map/psum | solution.py:128
  182.3 0.2 convolution_bitcast_fusion.1
  182.5 0.2 fusion.182
  182.9 0.3 fusion.118
  183.2 0.4 fusion.86
  183.7 0.2 fusion.125
  183.9 0.2 fusion.109
  184.4 0.3 fusion.133
  184.7 0.4 fusion.85
  185.2 0.2 fusion.92
  185.4 0.3 fusion.90
  186.0 0.3 fusion.144
  186.3 0.3 multiply_floor_fusion.3
  186.6 0.7 fusion.91
  (67 shorter events, 2.0 us)
Async XLA Ops:
  7.2 51.4 %reduce-scatter.4.cloned.1.call-start = ((), (), s32[]{:S(2)}) async-start(), calls=%async_computation.3 | async-start | bytes 327680 | tf_op jit(solution)/shard_map/reduce_scatter | solution.py:125
  30.9 4.5 %copy-start.2 = (s32[1,1,64]{2,1,0:T(1,128)S(1)}, s32[1,1,64]{2,1,0:T(1,128)}, u32[]{:S(2)}) copy-start(s32[1,1,64]{2,1,0:T(1,128)} %param.9) | copy-start | bytes 772
  34.7 4.0 %copy-start.1 = (f32[64,256]{1,0:T(8,128)S(1)}, f32[64,256]{1,0:T(8,128)}, u32[]{:S(2)}) copy-start(f32[64,256]{1,0:T(8,128)} %param.12) | copy-start | bytes 196612
  38.6 61.0 %reduce-scatter.6.cloned.1.call-start = ((), (), s32[]{:S(2)}) async-start(), calls=%async_computation.4 | async-start | bytes 327680 | tf_op jit(solution)/shard_map/reduce_scatter | solution.py:125
  38.7 31.2 %copy-start = (f32[4,64,64]{2,1,0:T(8,128)}, f32[4,64,64]{2,1,0:T(8,128)S(1)}, u32[]{:S(2)}) copy-start(f32[4,64,64]{2,1,0:T(8,128)S(1)} %pad_convert_fusion) | copy-start | bytes 196612
  82.5 58.1 %reduce-scatter.8.cloned.1.call-start = ((), (), s32[]{:S(2)}) async-start(), calls=%async_computation.5 | async-start | bytes 327680 | tf_op jit(solution)/shard_map/reduce_scatter | solution.py:125
  122.8 60.4 %slice-start = ((f32[4,64,64]{2,1,0:T(8,128)}), f32[3,64,64]{2,1,0:T(8,128)S(1)}, s32[]{:S(2)}) async-start(f32[4,64,64]{2,1,0:T(8,128)} %copy-done), calls=%async_computation.6 | async-start | bytes 196608 | tf_op jit(solution)/shard_map/slice | solution.py:72
Sparse Core Ops, SparseCore 0:
  38.7 19.8 reduce-scatter.3
  82.7 16.9 reduce-scatter.5
  123.7 16.9 reduce-scatter.7
where the time goes:
time: 194 us
  blocking collectives  71.4 us (37%)
  waiting for transfers between devices  53.1 us (27%)
  other arithmetic  24.6 us (13%)
  matrix products  19.7 us (10%)
  between operations  15 us (8%)
  local copies, waits for them, and re-layouts  9.75 us (5%)
    reduce_scatter x3, waiting for transfers between devices, local(): lax.psum_scatter(partial_rows, 'col', scatter_dimension=1, tiled=True)  53.1 us
    psum x1, blocking collectives, local(): projections.append(reduce_mod(lax.psum(partial_terms, ('row', 'col'))))  39.6 us
    all_gather x3, blocking collectives, local(): gathered = lax.all_gather(vector, 'row', axis=1, tiled=True)  31.8 us
    select_n x5, other arithmetic, reduce_mod(): return jnp.where(leftover >= MODULUS, leftover - MODULUS, leftover)  13.2 us
    dot_general x3, matrix products, local(): jnp.einsum('ntk,tdik->tdni', picked, a_digits, preferred_element_type=jnp...  10.6 us
    dot_general x3, matrix products, local(): jnp.einsum('bt,twi->wbi', onehot, residues, precision=lax.Precision.HIGHEST)  7.1 us
    gather x3, local copies, waits for them, and re-layouts, local(): picked = jnp.take(v_digits, cols_here, axis=1)  6.42 us
    another operation x14, other arithmetic  5.89 us
  transfers between devices with their start and end apart: 3, of which 3 were waited for; matrix products, arithmetic and copies ran while one was open for 0% of the time, Pallas kernels for 0%

commit v1 on v0

v1 whole, which is shorter than its diff:
```python
import functools

import jax
import jax.numpy as jnp
from jax import lax
from jax.experimental import pallas as pl
from jax.experimental.pallas import tpu as pltpu
from jax.sharding import PartitionSpec as P

STEP_COUNT = 3

MODULUS = 65521.0
HALF_MODULUS = 32760.0
BASE = 256.0
EXACT_DEPTH = 1024
DENSE_CELLS = 4
VMEM_LIMIT = 48 * 1024 * 1024


def reduce_centered(values):
    return values - MODULUS * jnp.floor(values * (1.0 / MODULUS) + 0.5)


def canonical(values):
    reduced = reduce_centered(values)
    return jnp.where(reduced < 0, reduced + MODULUS, reduced)


def balanced_digits(values):
    high = jnp.floor(values * (1.0 / BASE) + 0.5)
    return high, values - BASE * high


def stacked_digits(values):
    high, low = balanced_digits(values)
    return jnp.concatenate([high, low], 0).astype(jnp.bfloat16)


def partner(index, shift, size):
    return index ^ shift if size & (size - 1) == 0 else (index + shift) % size


def shift_of(index, other, size):
    return index ^ other if size & (size - 1) == 0 else (other - index) % size


def gather_pieces(piece, axis):
    size = lax.axis_size(axis)
    return [piece] + [
        lax.ppermute(piece, axis, [(partner(i, shift, size), i) for i in range(size)])
        for shift in range(1, size)
    ]


def scatter_pieces(pieces, axis):
    size = lax.axis_size(axis)
    return [pieces[0]] + [
        lax.ppermute(pieces[shift], axis, [(i, partner(i, shift, size)) for i in range(size)])
        for shift in range(1, size)
    ]


def dot_pairs(left, right):
    return lax.dot_general(left, right, (((1,), (1,)), ((), ())), preferred_element_type=jnp.float32)


def projection_residues(products, span):
    middle = reduce_centered(products[:span, span:]) + reduce_centered(products[span:, :span])
    return reduce_centered(
        15.0 * reduce_centered(products[:span, :span])
        + 256.0 * reduce_centered(middle)
        + reduce_centered(products[span:, span:])
    )


def pack_square(square, width):
    span = square.shape[0]
    rows = span * span // width
    return jnp.concatenate([square[j * rows : (j + 1) * rows] for j in range(width // span)], 1)


def unpack_square(packed, span):
    count = packed.shape[1] // span
    return jnp.concatenate([packed[:, j * span : (j + 1) * span] for j in range(count)], 0)


def build_kernel(group, positions_ref, entries_ref, dense_ref):
    step = pl.program_id(0)
    tile_len = entries_ref.shape[1]

    @pl.when(step == 0)
    def _():
        def clear(block, carry):
            dense_ref[block] = jnp.zeros(dense_ref.shape[1:], dense_ref.dtype)
            return carry

        lax.fori_loop(0, dense_ref.shape[0], clear, 0)

    for index in range(group):
        slot = step * group + index

        @pl.when(slot < positions_ref[2, 0])
        def _():
            values = entries_ref[index]
            values = jnp.where(values > HALF_MODULUS, values - MODULUS, values)
            high, low = balanced_digits(values)
            start = pl.multiple_of(positions_ref[1, slot] * tile_len, tile_len)
            both = jnp.concatenate([high.T, low.T], 1).astype(jnp.bfloat16)
            dense_ref[positions_ref[0, slot], pl.ds(start, tile_len), :] = both


def build_dense(entries, positions, row_blocks, col_blocks):
    slot_count, tile_len, _ = entries.shape
    group = next(size for size in (8, 4, 2, 1) if slot_count % size == 0)
    shape = (row_blocks, col_blocks * tile_len, 2 * tile_len)
    return pl.pallas_call(
        functools.partial(build_kernel, group),
        grid_spec=pltpu.PrefetchScalarGridSpec(
            num_scalar_prefetch=1,
            grid=(slot_count // group,),
            in_specs=[pl.BlockSpec((group, tile_len, tile_len), lambda i, p: (i, 0, 0))],
            out_specs=pl.BlockSpec(shape, lambda i, p: (0, 0, 0)),
        ),
        out_shape=jax.ShapeDtypeStruct(shape, jnp.bfloat16),
        compiler_params=pltpu.CompilerParams(vmem_limit_bytes=VMEM_LIMIT),
        cost_estimate=pl.CostEstimate(
            flops=8 * entries.size, bytes_accessed=16 * entries.size, transcendentals=0
        ),
    )(positions, entries)


def step_kernel(n_row, n_col, span, first, *refs):
    pieces, refs = refs[:n_row], refs[n_row:]
    x_pieces, refs = refs[:n_col], refs[n_col:]
    dense_ref, refs = refs[0], refs[1:]
    outs, refs = refs[:n_col], refs[n_col:]
    if not first:
        total_ref, refs = refs[0], refs[1:]
    held, digits, sems = refs
    row_blocks, depth, width = dense_ref.shape
    tile_len = width // 2
    piece_len = x_pieces[0].shape[1]
    piece_blocks = piece_len // tile_len
    copies = [
        pltpu.make_async_copy(dense_ref.at[b], held.at[b], sems.at[b]) for b in range(row_blocks)
    ]
    for copy in copies:
        copy.start()
    for d, piece in enumerate(pieces):
        vector = reduce_centered(piece[:span, :])
        digits[:, d * piece_len : (d + 1) * piece_len] = stacked_digits(vector)
    if not first:
        packed = pieces[0][span:, :]
        for piece in pieces[1:]:
            packed = packed + piece[span:, :]
        total_ref[...] = unpack_square(reduce_centered(packed), span)
    projected = None
    for e in range(n_col):
        for sub in range(piece_blocks):
            block = e * piece_blocks + sub
            copies[block].wait()
            high = middle = low = 0.0
            for start in range(0, depth, EXACT_DEPTH):
                stop = min(start + EXACT_DEPTH, depth)
                products = jnp.dot(
                    digits[:, start:stop],
                    held[block, start:stop, :],
                    preferred_element_type=jnp.float32,
                )
                products = reduce_centered(products)
                high = high + products[:span, :tile_len]
                middle = middle + products[:span, tile_len:] + products[span:, :tile_len]
                low = low + products[span:, tile_len:]
            outs[e][:span, sub * tile_len : (sub + 1) * tile_len] = reduce_centered(
                15.0 * high + 256.0 * reduce_centered(middle) + low
            )
        x_values = x_pieces[e][...]
        x_values = jnp.where(x_values > HALF_MODULUS, x_values - MODULUS, x_values)
        products = dot_pairs(stacked_digits(x_values), stacked_digits(outs[e][:span, :]))
        if n_col * piece_len > EXACT_DEPTH:
            products = reduce_centered(products)
        projected = products if projected is None else projected + products
    packed = pack_square(projection_residues(projected, span), piece_len)
    for out in outs:
        out[span:, :] = packed


def dense_step(pieces, x_pieces, dense, first):
    n_row, n_col = len(pieces), len(x_pieces)
    span, piece_len = x_pieces[0].shape
    row_blocks, depth, width = dense.shape
    rows = span + span * span // piece_len
    outs = [jax.ShapeDtypeStruct((rows, piece_len), jnp.float32)] * n_col
    if not first:
        outs = outs + [jax.ShapeDtypeStruct((span, span), jnp.float32)]
    vmem = pl.BlockSpec(memory_space=pltpu.VMEM)
    results = pl.pallas_call(
        functools.partial(step_kernel, n_row, n_col, span, first),
        in_specs=[vmem] * (n_row + n_col) + [pl.BlockSpec(memory_space=pl.ANY)],
        out_specs=[vmem] * len(outs),
        out_shape=outs,
        scratch_shapes=[
            pltpu.VMEM(dense.shape, dense.dtype),
            pltpu.VMEM((2 * span, depth), jnp.bfloat16),
            pltpu.SemaphoreType.DMA((row_blocks,)),
        ],
        compiler_params=pltpu.CompilerParams(vmem_limit_bytes=VMEM_LIMIT),
        cost_estimate=pl.CostEstimate(
            flops=4 * span * dense.size, bytes_accessed=2 * dense.size, transcendentals=0
        ),
    )(*pieces, *x_pieces, dense)
    return list(results[:n_col]), (None if first else results[n_col])


def sparse_step(pieces, x_pieces, a_digits, positions, first):
    span, piece_len = x_pieces[0].shape
    slot_count, _, tile_len, _ = a_digits.shape
    n_col = len(x_pieces)
    row_blocks = piece_len // tile_len * n_col
    total = None
    if not first:
        packed = functools.reduce(jnp.add, [piece[span:] for piece in pieces])
        total = unpack_square(reduce_centered(packed), span)
    vector = reduce_centered(jnp.concatenate([piece[:span] for piece in pieces], 1))
    v_digits = stacked_digits(vector).reshape(2 * span, -1, tile_len)
    picked = jnp.take(v_digits, positions[1], axis=1)
    products = jnp.einsum("ntk,tdik->tdni", picked, a_digits, preferred_element_type=jnp.float32)
    products = reduce_centered(products)
    residues = reduce_centered(
        15.0 * products[:, 0, :span]
        + 256.0 * reduce_centered(products[:, 0, span:] + products[:, 1, :span])
        + products[:, 1, span:]
    )
    live = jnp.arange(slot_count, dtype=jnp.int32) < positions[2, 0]
    onehot = positions[0][None, :] == jnp.arange(row_blocks, dtype=jnp.int32)[:, None]
    onehot = (onehot & live[None, :]).astype(jnp.float32)
    summed = jnp.einsum("bt,twi->wbi", onehot, residues, precision=lax.Precision.HIGHEST)
    outs = reduce_centered(summed).reshape(span, n_col, piece_len)
    projected = 0.0
    for e in range(n_col):
        x_values = x_pieces[e]
        x_values = jnp.where(x_values > HALF_MODULUS, x_values - MODULUS, x_values)
        products = dot_pairs(stacked_digits(x_values), stacked_digits(outs[:, e]))
        projected = projected + reduce_centered(products)
    packed = pack_square(projection_residues(projected, span), piece_len)
    return [jnp.concatenate([outs[:, e], packed], 0) for e in range(n_col)], total


def multiply_mod(left, right):
    span = left.shape[0]
    left = stacked_digits(left)
    high, low = (part.astype(jnp.bfloat16) for part in balanced_digits(right))
    by_high = jnp.dot(left, high, preferred_element_type=jnp.float32)
    by_low = jnp.dot(left, low, preferred_element_type=jnp.float32)
    return reduce_centered(
        reduce_centered(15.0 * by_high[:span])
        + 256.0 * reduce_centered(by_low[:span] + by_high[span:])
        + by_low[span:]
    )


def sigma_kernel(count, first_ref, second_ref, *refs):
    thirds, out_ref = refs[:count], refs[count]
    c_1, c_2 = first_ref[...], second_ref[...]
    c_3 = thirds[0][...]
    for piece in thirds[1:]:
        c_3 = c_3 + piece[...]
    c_3 = reduce_centered(c_3)
    e_2 = reduce_centered(c_1 - multiply_mod(c_1, c_2))
    both = reduce_centered(c_1 + e_2)
    start = multiply_mod(e_2, c_1)
    rest = c_1 - multiply_mod(both, c_2)
    e_3 = reduce_centered(multiply_mod(start, c_3) + rest)
    out_ref[0] = canonical(-multiply_mod(e_3, start)) * (1.0 / MODULUS)
    out_ref[1] = canonical(start + multiply_mod(e_3, both)) * (1.0 / MODULUS)
    out_ref[2] = canonical(-both - e_3) * (1.0 / MODULUS)


def sigma_update(c_1, c_2, c_3_pieces):
    span = c_1.shape[0]
    return pl.pallas_call(
        functools.partial(sigma_kernel, len(c_3_pieces)),
        out_shape=jax.ShapeDtypeStruct((STEP_COUNT, span, span), jnp.float32),
    )(c_1, c_2, *c_3_pieces)


def local(tile_entries, tile_rows, tile_cols, tile_count, block_x, block_y):
    entries = tile_entries[0, 0]
    slot_count, tile_len, _ = entries.shape
    span, piece_len = block_y.shape
    piece_blocks = piece_len // tile_len
    n_row, n_col = lax.axis_size("row"), lax.axis_size("col")
    row_blocks, col_blocks = n_col * piece_blocks, n_row * piece_blocks
    rows_here, cols_here = tile_rows[0, 0], tile_cols[0, 0]
    row_shift = shift_of(lax.axis_index("col"), rows_here // piece_blocks, n_col)
    col_shift = shift_of(lax.axis_index("row"), cols_here // piece_blocks, n_row)
    positions = jnp.stack(
        [
            row_shift * piece_blocks + rows_here % piece_blocks,
            col_shift * piece_blocks + cols_here % piece_blocks,
            jnp.full((slot_count,), tile_count[0, 0], jnp.int32),
        ]
    )
    pieces = gather_pieces(block_y, "row")
    x_pieces = gather_pieces(block_x, "col")
    if row_blocks * col_blocks <= DENSE_CELLS * slot_count:
        dense = build_dense(entries, positions, row_blocks, col_blocks)
        multiply = functools.partial(dense_step, dense=dense)
    else:
        centred = jnp.where(entries > HALF_MODULUS, entries - MODULUS, entries)
        a_digits = jnp.stack(balanced_digits(centred), 1).astype(jnp.bfloat16)
        multiply = functools.partial(sparse_step, a_digits=a_digits, positions=positions)
    totals = []
    for step_index in range(STEP_COUNT):
        outs, total = multiply(pieces, x_pieces, first=step_index == 0)
        totals.append(total)
        summed = functools.reduce(jnp.add, scatter_pieces(outs, "col"))
        if step_index < STEP_COUNT - 1:
            pieces = gather_pieces(summed, "row")
    thirds = gather_pieces(unpack_square(summed[span:], span), "row")
    polynomial = sigma_update(totals[1], totals[2], thirds)
    return polynomial, canonical(summed[:span]) * (1.0 / MODULUS)


def solution(mesh):
    placed = (
        P("row", "col", None, None, None),
        P("row", "col", None),
        P("row", "col", None),
        P("row", "col"),
        P(None, ("row", "col")),
        P(None, ("row", "col")),
    )
    return jax.shard_map(
        local, mesh=mesh, in_specs=placed, out_specs=(P(), P(None, ("row", "col"))), check_vma=False
    )
```

time: 194 us -> 106 us (0.55)
  blocking collectives: 71.4 us -> 0 us
  starting transfers between devices: 0.12 us -> 46.6 us
  waiting for transfers between devices: 53.1 us -> 29 us
  other arithmetic: 24.6 us -> 1.48 us
  Pallas kernels: 0 us -> 23.1 us
  matrix products: 19.7 us -> 0 us
  between operations: 15 us -> 1.52 us
  local copies, waits for them, and re-layouts: 9.75 us -> 2.93 us
    reduce_scatter x3 -> x0, waiting for transfers between devices: 53.1 us -> none  [local(): lax.psum_scatter(partial_rows, 'col', scatter_dimension=1, tiled=True)]
    ppermute x0 -> x40, starting transfers between devices: none -> 46.6 us  [the longest x31 33.2 us: gather_pieces(): lax.ppermute(piece, axis, [(partner(i, shift, size), i) for i in range(si...]
    psum x1 -> x0, blocking collectives: 39.6 us -> none  [local(): projections.append(reduce_mod(lax.psum(partial_terms, ('row', 'col'))))]
    all_gather x3 -> x0, blocking collectives: 31.8 us -> none  [local(): gathered = lax.all_gather(vector, 'row', axis=1, tiled=True)]
    ppermute x0 -> x40, waiting for transfers between devices: none -> 29 us  [the longest x9 18.2 us: scatter_pieces(): lax.ppermute(pieces[shift], axis, [(i, partner(i, shift, size)) for i in...]
    pallas_call x0 -> x5, Pallas kernels: none -> 23.1 us  [the longest x3 14.2 us: dense_step(): pl.pallas_call(functools.partial(step_kernel, n_row, n_col, span, first),...]
    dot_general x15 -> x0, matrix products: 19.7 us -> none  [the longest x3 10.6 us: local(): jnp.einsum('ntk,tdik->tdni', picked, a_digits, preferred_element_type=jnp...]
    select_n x9 -> x0, other arithmetic: 13.9 us -> none  [the longest x5 13.2 us: reduce_mod(): return jnp.where(leftover >= MODULUS, leftover - MODULUS, leftover)]
  transfers between devices with their start and end apart: 3 -> 40, of which waited for: 3 -> 18; matrix products, arithmetic and copies ran while one was open for 0% -> 1% of each run, Pallas kernels for 0% -> 6%
where the time goes in v1:
time: 106 us; the launch traced here: 105 us
  starting transfers between devices  46.6 us (44%)
  waiting for transfers between devices  29 us (27%)
  Pallas kernels  23.1 us (22%)
  local copies, waits for them, and re-layouts  2.93 us (3%)
  between operations  1.52 us (1%)
  other arithmetic  1.48 us (1%)
    ppermute x31, starting transfers between devices, gather_pieces(): lax.ppermute(piece, axis, [(partner(i, shift, size), i) for i in range(si...  33.2 us
    ppermute x9, waiting for transfers between devices, scatter_pieces(): lax.ppermute(pieces[shift], axis, [(i, partner(i, shift, size)) for i in...  18.2 us
    pallas_call x3, Pallas kernels, dense_step(): pl.pallas_call(functools.partial(step_kernel, n_row, n_col, span, first),...  14.2 us
    ppermute x9, starting transfers between devices, scatter_pieces(): lax.ppermute(pieces[shift], axis, [(i, partner(i, shift, size)) for i in...  13.3 us
    ppermute x31, waiting for transfers between devices, gather_pieces(): lax.ppermute(piece, axis, [(partner(i, shift, size), i) for i in range(si...  10.8 us
    pallas_call x1, Pallas kernels, build_dense(): pl.pallas_call(functools.partial(build_kernel, group), grid_spec=pltpu.Pr...  6.6 us
    unnamed x26, local copies, waits for them, and re-layouts  2.78 us
    pallas_call x1, Pallas kernels, sigma_update(): pl.pallas_call(functools.partial(sigma_kernel, len(c_3_pieces)), out_shap...  2.27 us
  transfers between devices with their start and end apart: 40, of which 18 were waited for; matrix products, arithmetic and copies ran while one was open for 1% of the time, Pallas kernels for 6%

profile of v1, /device:TPU:0, one launch (start us, length us, event | category | flops | bytes accessed | tf_op | source)
XLA Modules:
  0.0 104.6 jit_solution(14920325370920297333)
XLA Ops:
  0.6 5.1 %collective-permute-start.9 = (f32[64,256]{1,0:T(8,128)}, f32[64,256]{1,0:T(8,128)S(1)}, u32[]{:S(2)}, u32[]{:S(2)}) collective-permute-start(f32[64,256]{1,0:T(8,128)} %refs_8_.5), channel_id=1, source_target_pairs={{3,0},{2,1},{1,2},{0,3},{7,4},{6,5},{5,6},{4,7},{11,8},{10,9},{9,1... | collective-permute-start | bytes 196616 | tf_op jit(solution)/shard_map/ppermute | solution.py:50
  5.7 0.6 collective-permute-start.7
  6.4 2.6 %collective-permute-start.5 = (f32[64,256]{1,0:T(8,128)}, f32[64,256]{1,0:T(8,128)S(1)}, u32[]{:S(2)}, u32[]{:S(2)}) collective-permute-start(f32[64,256]{1,0:T(8,128)} %refs_0_.1), channel_id=1, source_target_pairs={{24,0},{28,4},{16,8},{20,12},{8,16},{12,20},{0,24},{4,28},{25,1},{... | collective-permute-start | bytes 196616 | tf_op jit(solution)/shard_map/ppermute | solution.py:50
  9.0 0.7 fusion.1
  10.9 0.6 collective-permute-done.8.refs_10_
  11.6 0.9 collective-permute-start.2
  12.5 1.4 %collective-permute-start.1 = (f32[64,256]{1,0:T(8,128)}, f32[64,256]{1,0:T(8,128)S(1)}, u32[]{:S(2)}, u32[]{:S(2)}) collective-permute-start(f32[64,256]{1,0:T(8,128)} %refs_0_.1), channel_id=1, source_target_pairs={{8,0},{12,4},{0,8},{4,12},{24,16},{28,20},{16,24},{20,28},{9,1},{1... | collective-permute-start | bytes 196616 | tf_op jit(solution)/shard_map/ppermute | solution.py:50
  13.9 1.7 %collective-permute-start.6 = (f32[64,256]{1,0:T(8,128)}, f32[64,256]{1,0:T(8,128)S(1)}, u32[]{:S(2)}, u32[]{:S(2)}) collective-permute-start(f32[64,256]{1,0:T(8,128)} %refs_0_.1), channel_id=1, source_target_pairs={{28,0},{24,4},{20,8},{16,12},{12,16},{8,20},{4,24},{0,28},{29,1},{... | collective-permute-start | bytes 196616 | tf_op jit(solution)/shard_map/ppermute | solution.py:50
  15.7 2.2 %copy-done = f32[1,1,64,128,128]{4,3,2,1,0:T(8,128)S(1)} copy-done((f32[1,1,64,128,128]{4,3,2,1,0:T(8,128)S(1)}, f32[1,1,64,128,128]{4,3,2,1,0:T(8,128)}, u32[]{:S(2)}) %copy-start) | copy-done | bytes 4194328
  17.9 6.6 %shard_map.77.refs_12_ = bf16[8,2048,256]{2,1,0:T(8,128)(2,1)} custom-call(s32[3,64]{1,0:T(4,128)S(1)} %add_add_fusion.3.positions_ref, f32[64,128,128]{2,1,0:T(8,128)S(1)} %bitcast.31), custom_call_target="tpu_custom_call" | custom-call | flops 8388608 | bytes 16777216 | tf_op jit(solution)/shard_map/pallas_call | solution.py:116
  24.5 4.8 %shard_map.78 = (f32[80,256]{1,0:T(8,128)S(1)}, f32[80,256]{1,0:T(8,128)S(1)}, f32[80,256]{1,0:T(8,128)S(1)}, f32[80,256]{1,0:T(8,128)S(1)}) custom-call(f32[64,256]{1,0:T(8,128)S(1)} %copy-done.2, f32[64,256]{1,0:T(8,128)S(1)} %collective-permute-done.refs_1_, f32[64,256]{1,0:T(8,128)S(1)} %collective-permute-done.1.refs_2_, ...), custom_call_target="tpu_custom_call" | custom-call | flops 1073741824 | bytes 8388608 | tf_op jit(solution)/shard_map/pallas_call | solution.py:197
  29.4 3.5 %collective-permute-start.11 = (f32[80,256]{1,0:T(8,128)S(1)}, f32[80,256]{1,0:T(8,128)S(1)}, u32[]{:S(2)}, u32[]{:S(2)}) collective-permute-start(f32[80,256]{1,0:T(8,128)S(1)} %get-tuple-element.18), channel_id=1, source_target_pairs={{0,2},{1,3},{2,0},{3,1},{4,6},{5,7},{6,4},{7,5},{8,10},{9,11},{10,... | collective-permute-start | bytes 245768 | tf_op jit(solution)/shard_map/ppermute | solution.py:58
  32.9 0.9 collective-permute-start.12
  33.8 1.8 %collective-permute-done.11 = f32[80,256]{1,0:T(8,128)S(1)} collective-permute-done((f32[80,256]{1,0:T(8,128)S(1)}, f32[80,256]{1,0:T(8,128)S(1)}, u32[]{:S(2)}, u32[]{:S(2)}) %collective-permute-start.11) | collective-permute-done | bytes 81952 | tf_op jit(solution)/shard_map/ppermute | solution.py:58
  35.7 4.3 %collective-permute-done.12 = f32[80,256]{1,0:T(8,128)S(1)} collective-permute-done((f32[80,256]{1,0:T(8,128)S(1)}, f32[80,256]{1,0:T(8,128)S(1)}, u32[]{:S(2)}, u32[]{:S(2)}) %collective-permute-start.12) | collective-permute-done | bytes 81952 | tf_op jit(solution)/shard_map/ppermute | solution.py:58
  40.1 3.8 %collective-permute-start.18 = (f32[80,256]{1,0:T(8,128)S(1)}, f32[80,256]{1,0:T(8,128)S(1)}, u32[]{:S(2)}, u32[]{:S(2)}) collective-permute-start(f32[80,256]{1,0:T(8,128)S(1)} %add_add_fusion.2.refs_0_), channel_id=1, source_target_pairs={{24,0},{28,4},{16,8},{20,12},{8,16},{12,20},{0,24},{4,28},{25,1},{... | collective-permute-start | bytes 245768 | tf_op jit(solution)/shard_map/ppermute | solution.py:50
  43.9 1.7 %collective-permute-start.16 = (f32[80,256]{1,0:T(8,128)S(1)}, f32[80,256]{1,0:T(8,128)S(1)}, u32[]{:S(2)}, u32[]{:S(2)}) collective-permute-start(f32[80,256]{1,0:T(8,128)S(1)} %add_add_fusion.2.refs_0_), channel_id=1, source_target_pairs={{16,0},{20,4},{24,8},{28,12},{0,16},{4,20},{8,24},{12,28},{17,1},{... | collective-permute-start | bytes 245768 | tf_op jit(solution)/shard_map/ppermute | solution.py:50
  45.6 0.9 collective-permute-start.15
  46.5 0.9 collective-permute-start.14
  47.4 0.8 collective-permute-start.13
  48.2 1.6 %collective-permute-done.17.refs_5_ = f32[80,256]{1,0:T(8,128)S(1)} collective-permute-done((f32[80,256]{1,0:T(8,128)S(1)}, f32[80,256]{1,0:T(8,128)S(1)}, u32[]{:S(2)}, u32[]{:S(2)}) %collective-permute-start.17) | collective-permute-done | bytes 81952 | tf_op jit(solution)/shard_map/ppermute | solution.py:50
  49.7 1.8 %collective-permute-done.16.refs_4_ = f32[80,256]{1,0:T(8,128)S(1)} collective-permute-done((f32[80,256]{1,0:T(8,128)S(1)}, f32[80,256]{1,0:T(8,128)S(1)}, u32[]{:S(2)}, u32[]{:S(2)}) %collective-permute-start.16) | collective-permute-done | bytes 81952 | tf_op jit(solution)/shard_map/ppermute | solution.py:50
  52.1 4.7 %shard_map.79 = (f32[80,256]{1,0:T(8,128)S(1)}, f32[80,256]{1,0:T(8,128)S(1)}, f32[80,256]{1,0:T(8,128)S(1)}, f32[80,256]{1,0:T(8,128)S(1)}, f32[64,64]{1,0:T(8,128)S(1)}) custom-call(f32[80,256]{1,0:T(8,128)S(1)} %add_add_fusion.2.refs_0_, f32[80,256]{1,0:T(8,128)S(1)} %collective-permute-done.13.refs_1_, f32[80,256]{1,0:T(8,128)S(1)} %collective-permute-done.14.refs_2_, ...), custom_call_target="tpu_custom_call" | custom-call | flops 1073741824 | bytes 8388608 | tf_op jit(solution)/shard_map/pallas_call | solution.py:197
  56.8 0.8 collective-permute-start.20
  57.7 0.8 collective-permute-start.21
  58.5 2.8 %collective-permute-start.22 = (f32[80,256]{1,0:T(8,128)S(1)}, f32[80,256]{1,0:T(8,128)S(1)}, u32[]{:S(2)}, u32[]{:S(2)}) collective-permute-start(f32[80,256]{1,0:T(8,128)S(1)} %get-tuple-element.24), channel_id=1, source_target_pairs={{0,3},{1,2},{2,1},{3,0},{4,7},{5,6},{6,5},{7,4},{8,11},{9,10},{10,... | collective-permute-start | bytes 245768 | tf_op jit(solution)/shard_map/ppermute | solution.py:58
  61.3 1.0 collective-permute-done.20
  62.3 4.6 %collective-permute-done.21 = f32[80,256]{1,0:T(8,128)S(1)} collective-permute-done((f32[80,256]{1,0:T(8,128)S(1)}, f32[80,256]{1,0:T(8,128)S(1)}, u32[]{:S(2)}, u32[]{:S(2)}) %collective-permute-start.21) | collective-permute-done | bytes 81952 | tf_op jit(solution)/shard_map/ppermute | solution.py:58
  67.0 1.2 %collective-permute-start.28 = (f32[80,256]{1,0:T(8,128)S(1)}, f32[80,256]{1,0:T(8,128)S(1)}, u32[]{:S(2)}, u32[]{:S(2)}) collective-permute-start(f32[80,256]{1,0:T(8,128)S(1)} %add_add_fusion.1.refs_0_), channel_id=1, source_target_pairs={{24,0},{28,4},{16,8},{20,12},{8,16},{12,20},{0,24},{4,28},{25,1},{... | collective-permute-start | bytes 245768 | tf_op jit(solution)/shard_map/ppermute | solution.py:50
  68.2 2.5 %collective-permute-start.27 = (f32[80,256]{1,0:T(8,128)S(1)}, f32[80,256]{1,0:T(8,128)S(1)}, u32[]{:S(2)}, u32[]{:S(2)}) collective-permute-start(f32[80,256]{1,0:T(8,128)S(1)} %add_add_fusion.1.refs_0_), channel_id=1, source_target_pairs={{20,0},{16,4},{28,8},{24,12},{4,16},{0,20},{12,24},{8,28},{21,1},{... | collective-permute-start | bytes 245768 | tf_op jit(solution)/shard_map/ppermute | solution.py:50
  70.7 0.7 collective-permute-start.26
  71.4 0.6 collective-permute-done.29.refs_7_
  72.0 1.3 %collective-permute-start.24 = (f32[80,256]{1,0:T(8,128)S(1)}, f32[80,256]{1,0:T(8,128)S(1)}, u32[]{:S(2)}, u32[]{:S(2)}) collective-permute-start(f32[80,256]{1,0:T(8,128)S(1)} %add_add_fusion.1.refs_0_), channel_id=1, source_target_pairs={{8,0},{12,4},{0,8},{4,12},{24,16},{28,20},{16,24},{20,28},{9,1},{1... | collective-permute-start | bytes 245768 | tf_op jit(solution)/shard_map/ppermute | solution.py:50
  73.4 1.7 %collective-permute-done.27.refs_5_ = f32[80,256]{1,0:T(8,128)S(1)} collective-permute-done((f32[80,256]{1,0:T(8,128)S(1)}, f32[80,256]{1,0:T(8,128)S(1)}, u32[]{:S(2)}, u32[]{:S(2)}) %collective-permute-start.27) | collective-permute-done | bytes 81952 | tf_op jit(solution)/shard_map/ppermute | solution.py:50
  75.2 1.9 %collective-permute-done.26.refs_4_ = f32[80,256]{1,0:T(8,128)S(1)} collective-permute-done((f32[80,256]{1,0:T(8,128)S(1)}, f32[80,256]{1,0:T(8,128)S(1)}, u32[]{:S(2)}, u32[]{:S(2)}) %collective-permute-start.26) | collective-permute-done | bytes 81952 | tf_op jit(solution)/shard_map/ppermute | solution.py:50
  77.4 4.7 %shard_map.80 = (f32[80,256]{1,0:T(8,128)S(1)}, f32[80,256]{1,0:T(8,128)S(1)}, f32[80,256]{1,0:T(8,128)S(1)}, f32[80,256]{1,0:T(8,128)S(1)}, f32[64,64]{1,0:T(8,128)S(1)}) custom-call(f32[80,256]{1,0:T(8,128)S(1)} %add_add_fusion.1.refs_0_, f32[80,256]{1,0:T(8,128)S(1)} %collective-permute-done.23.refs_1_, f32[80,256]{1,0:T(8,128)S(1)} %collective-permute-done.24.refs_2_, ...), custom_call_target="tpu_custom_call" | custom-call | flops 1073741824 | bytes 8388608 | tf_op jit(solution)/shard_map/pallas_call | solution.py:197
  82.1 1.5 %collective-permute-start.30 = (f32[80,256]{1,0:T(8,128)S(1)}, f32[80,256]{1,0:T(8,128)S(1)}, u32[]{:S(2)}, u32[]{:S(2)}) collective-permute-start(f32[80,256]{1,0:T(8,128)S(1)} %get-tuple-element.27), channel_id=1, source_target_pairs={{0,1},{1,0},{2,3},{3,2},{4,5},{5,4},{6,7},{7,6},{8,9},{9,8},{10,11... | collective-permute-start | bytes 245768 | tf_op jit(solution)/shard_map/ppermute | solution.py:58
  83.6 0.9 collective-permute-start.31
  84.6 2.0 %collective-permute-start.32 = (f32[80,256]{1,0:T(8,128)S(1)}, f32[80,256]{1,0:T(8,128)S(1)}, u32[]{:S(2)}, u32[]{:S(2)}) collective-permute-start(f32[80,256]{1,0:T(8,128)S(1)} %get-tuple-element.29), channel_id=1, source_target_pairs={{0,3},{1,2},{2,1},{3,0},{4,7},{5,6},{6,5},{7,4},{8,11},{9,10},{10,... | collective-permute-start | bytes 245768 | tf_op jit(solution)/shard_map/ppermute | solution.py:58
  86.7 6.3 %collective-permute-done.31 = f32[80,256]{1,0:T(8,128)S(1)} collective-permute-done((f32[80,256]{1,0:T(8,128)S(1)}, f32[80,256]{1,0:T(8,128)S(1)}, u32[]{:S(2)}, u32[]{:S(2)}) %collective-permute-start.31) | collective-permute-done | bytes 81952 | tf_op jit(solution)/shard_map/ppermute | solution.py:58
  93.2 1.4 %collective-permute-start.38 = (f32[64,64]{1,0:T(8,128)S(1)}, f32[64,64]{1,0:T(8,128)S(1)}, u32[]{:S(2)}, u32[]{:S(2)}) collective-permute-start(f32[64,64]{1,0:T(8,128)S(1)} %pad_maximum_fusion.refs_0_), channel_id=1, source_target_pairs={{24,0},{28,4},{16,8},{20,12},{8,16},{12,20},{0,24},{4,28},{25,1},{... | collective-permute-start | bytes 49160 | tf_op jit(solution)/shard_map/ppermute | solution.py:50
  94.6 2.0 %collective-permute-start.37 = (f32[64,64]{1,0:T(8,128)S(1)}, f32[64,64]{1,0:T(8,128)S(1)}, u32[]{:S(2)}, u32[]{:S(2)}) collective-permute-start(f32[64,64]{1,0:T(8,128)S(1)} %pad_maximum_fusion.refs_0_), channel_id=1, source_target_pairs={{20,0},{16,4},{28,8},{24,12},{4,16},{0,20},{12,24},{8,28},{21,1},{... | collective-permute-start | bytes 49160 | tf_op jit(solution)/shard_map/ppermute | solution.py:50
  96.6 1.0 collective-permute-start.36
  97.6 0.8 collective-permute-start.34
  98.4 1.1 %collective-permute-start.33 = (f32[64,64]{1,0:T(8,128)S(1)}, f32[64,64]{1,0:T(8,128)S(1)}, u32[]{:S(2)}, u32[]{:S(2)}) collective-permute-start(f32[64,64]{1,0:T(8,128)S(1)} %pad_maximum_fusion.refs_0_), channel_id=1, source_target_pairs={{4,0},{0,4},{12,8},{8,12},{20,16},{16,20},{28,24},{24,28},{5,1},{1... | collective-permute-start | bytes 49160 | tf_op jit(solution)/shard_map/ppermute | solution.py:50
  99.5 0.7 fusion
  101.0 0.8 collective-permute-done.34.refs_2_
  102.4 2.3 %shard_map.81 = f32[3,64,64]{2,1,0:T(8,128)} custom-call(f32[64,64]{1,0:T(8,128)} %copy-done.3, f32[64,64]{1,0:T(8,128)} %copy-done.4, f32[64,64]{1,0:T(8,128)} %copy-done.5, f32[64,64]{1,0:T(8,128)} %copy-done.12, f32[64,64]{1,0:T(8,128)} %copy-done.11, f32[64,64]{1,0:T(8,128)} %copy-done.10, f32[64,64]{1,0:T(8,128)} %copy-done.9, f32[64,64]{1,0:T(8,128)} %copy-done.8, ...), custom_call_target="tpu_custom_call" | custom-call | tf_op jit(solution)/shard_map/pallas_call | solution.py:281
  (72 shorter events, 3.7 us)
Async XLA Ops:
  0.6 9.8 %collective-permute-start.9 = (f32[64,256]{1,0:T(8,128)}, f32[64,256]{1,0:T(8,128)S(1)}, u32[]{:S(2)}, u32[]{:S(2)}) collective-permute-start(f32[64,256]{1,0:T(8,128)} %refs_8_.5), channel_id=1, source_target_pairs={{3,0},{2,1},{1,2},{0,3},{7,4},{6,5},{5,6},{4,7},{11,8},{10,9},{9,1... | collective-permute-start | bytes 196616 | tf_op jit(solution)/shard_map/ppermute | solution.py:50
  5.7 5.8 %collective-permute-start.8 = (f32[64,256]{1,0:T(8,128)}, f32[64,256]{1,0:T(8,128)S(1)}, u32[]{:S(2)}, u32[]{:S(2)}) collective-permute-start(f32[64,256]{1,0:T(8,128)} %refs_8_.5), channel_id=1, source_target_pairs={{2,0},{3,1},{0,2},{1,3},{6,4},{7,5},{4,6},{5,7},{10,8},{11,9},{8,1... | collective-permute-start | bytes 196616 | tf_op jit(solution)/shard_map/ppermute | solution.py:50
  5.7 6.8 %collective-permute-start.7 = (f32[64,256]{1,0:T(8,128)}, f32[64,256]{1,0:T(8,128)S(1)}, u32[]{:S(2)}, u32[]{:S(2)}) collective-permute-start(f32[64,256]{1,0:T(8,128)} %refs_8_.5), channel_id=1, source_target_pairs={{1,0},{0,1},{3,2},{2,3},{5,4},{4,5},{7,6},{6,7},{9,8},{8,9},{11,10... | collective-permute-start | bytes 196616 | tf_op jit(solution)/shard_map/ppermute | solution.py:50
  6.4 7.5 %collective-permute-start.5 = (f32[64,256]{1,0:T(8,128)}, f32[64,256]{1,0:T(8,128)S(1)}, u32[]{:S(2)}, u32[]{:S(2)}) collective-permute-start(f32[64,256]{1,0:T(8,128)} %refs_0_.1), channel_id=1, source_target_pairs={{24,0},{28,4},{16,8},{20,12},{8,16},{12,20},{0,24},{4,28},{25,1},{... | collective-permute-start | bytes 196616 | tf_op jit(solution)/shard_map/ppermute | solution.py:50
  9.0 4.9 %collective-permute-start.4 = (f32[64,256]{1,0:T(8,128)}, f32[64,256]{1,0:T(8,128)S(1)}, u32[]{:S(2)}, u32[]{:S(2)}) collective-permute-start(f32[64,256]{1,0:T(8,128)} %refs_0_.1), channel_id=1, source_target_pairs={{20,0},{16,4},{28,8},{24,12},{4,16},{0,20},{12,24},{8,28},{21,1},{... | collective-permute-start | bytes 196616 | tf_op jit(solution)/shard_map/ppermute | solution.py:50
  10.4 14.1 %collective-permute-start.3 = (f32[64,256]{1,0:T(8,128)}, f32[64,256]{1,0:T(8,128)S(1)}, u32[]{:S(2)}, u32[]{:S(2)}) collective-permute-start(f32[64,256]{1,0:T(8,128)} %refs_0_.1), channel_id=1, source_target_pairs={{16,0},{20,4},{24,8},{28,12},{0,16},{4,20},{8,24},{12,28},{17,1},{... | collective-permute-start | bytes 196616 | tf_op jit(solution)/shard_map/ppermute | solution.py:50
  11.6 12.9 %collective-permute-start.2 = (f32[64,256]{1,0:T(8,128)}, f32[64,256]{1,0:T(8,128)S(1)}, u32[]{:S(2)}, u32[]{:S(2)}) collective-permute-start(f32[64,256]{1,0:T(8,128)} %refs_0_.1), channel_id=1, source_target_pairs={{12,0},{8,4},{4,8},{0,12},{28,16},{24,20},{20,24},{16,28},{13,1},{... | collective-permute-start | bytes 196616 | tf_op jit(solution)/shard_map/ppermute | solution.py:50
  12.5 12.0 %collective-permute-start.1 = (f32[64,256]{1,0:T(8,128)}, f32[64,256]{1,0:T(8,128)S(1)}, u32[]{:S(2)}, u32[]{:S(2)}) collective-permute-start(f32[64,256]{1,0:T(8,128)} %refs_0_.1), channel_id=1, source_target_pairs={{8,0},{12,4},{0,8},{4,12},{24,16},{28,20},{16,24},{20,28},{9,1},{1... | collective-permute-start | bytes 196616 | tf_op jit(solution)/shard_map/ppermute | solution.py:50
  13.9 10.6 %collective-permute-start = (f32[64,256]{1,0:T(8,128)}, f32[64,256]{1,0:T(8,128)S(1)}, u32[]{:S(2)}, u32[]{:S(2)}) collective-permute-start(f32[64,256]{1,0:T(8,128)} %refs_0_.1), channel_id=1, source_target_pairs={{4,0},{0,4},{12,8},{8,12},{20,16},{16,20},{28,24},{24,28},{5,1},{1... | collective-permute-start | bytes 196616 | tf_op jit(solution)/shard_map/ppermute | solution.py:50
  13.9 10.6 %collective-permute-start.6 = (f32[64,256]{1,0:T(8,128)}, f32[64,256]{1,0:T(8,128)S(1)}, u32[]{:S(2)}, u32[]{:S(2)}) collective-permute-start(f32[64,256]{1,0:T(8,128)} %refs_0_.1), channel_id=1, source_target_pairs={{28,0},{24,4},{20,8},{16,12},{12,16},{8,20},{4,24},{0,28},{29,1},{... | collective-permute-start | bytes 196616 | tf_op jit(solution)/shard_map/ppermute | solution.py:50
  15.7 2.2 %copy-start = (f32[1,1,64,128,128]{4,3,2,1,0:T(8,128)S(1)}, f32[1,1,64,128,128]{4,3,2,1,0:T(8,128)}, u32[]{:S(2)}) copy-start(f32[1,1,64,128,128]{4,3,2,1,0:T(8,128)} %param.6) | copy-start | bytes 12582916
  17.9 6.6 %copy-start.1 = (f32[64,256]{1,0:T(8,128)S(1)}, f32[64,256]{1,0:T(8,128)}, u32[]{:S(2)}) copy-start(f32[64,256]{1,0:T(8,128)} %refs_8_.5) | copy-start | bytes 196612
  17.9 6.7 %copy-start.2 = (f32[64,256]{1,0:T(8,128)S(1)}, f32[64,256]{1,0:T(8,128)}, u32[]{:S(2)}) copy-start(f32[64,256]{1,0:T(8,128)} %refs_0_.1) | copy-start | bytes 196612
  29.3 4.5 %collective-permute-start.10 = (f32[80,256]{1,0:T(8,128)S(1)}, f32[80,256]{1,0:T(8,128)S(1)}, u32[]{:S(2)}, u32[]{:S(2)}) collective-permute-start(f32[80,256]{1,0:T(8,128)S(1)} %get-tuple-element.17), channel_id=1, source_target_pairs={{0,1},{1,0},{2,3},{3,2},{4,5},{5,4},{6,7},{7,6},{8,9},{9,8},{10,11... | collective-permute-start | bytes 245768 | tf_op jit(solution)/shard_map/ppermute | solution.py:58
  29.4 6.3 %collective-permute-start.11 = (f32[80,256]{1,0:T(8,128)S(1)}, f32[80,256]{1,0:T(8,128)S(1)}, u32[]{:S(2)}, u32[]{:S(2)}) collective-permute-start(f32[80,256]{1,0:T(8,128)S(1)} %get-tuple-element.18), channel_id=1, source_target_pairs={{0,2},{1,3},{2,0},{3,1},{4,6},{5,7},{6,4},{7,5},{8,10},{9,11},{10,... | collective-permute-start | bytes 245768 | tf_op jit(solution)/shard_map/ppermute | solution.py:58
  32.9 7.1 %collective-permute-start.12 = (f32[80,256]{1,0:T(8,128)S(1)}, f32[80,256]{1,0:T(8,128)S(1)}, u32[]{:S(2)}, u32[]{:S(2)}) collective-permute-start(f32[80,256]{1,0:T(8,128)S(1)} %get-tuple-element.19), channel_id=1, source_target_pairs={{0,3},{1,2},{2,1},{3,0},{4,7},{5,6},{6,5},{7,4},{8,11},{9,10},{10,... | collective-permute-start | bytes 245768 | tf_op jit(solution)/shard_map/ppermute | solution.py:58
  40.0 6.5 %collective-permute-start.19 = (f32[80,256]{1,0:T(8,128)S(1)}, f32[80,256]{1,0:T(8,128)S(1)}, u32[]{:S(2)}, u32[]{:S(2)}) collective-permute-start(f32[80,256]{1,0:T(8,128)S(1)} %add_add_fusion.2.refs_0_), channel_id=1, source_target_pairs={{28,0},{24,4},{20,8},{16,12},{12,16},{8,20},{4,24},{0,28},{29,1},{... | collective-permute-start | bytes 245768 | tf_op jit(solution)/shard_map/ppermute | solution.py:50
  40.1 7.3 %collective-permute-start.18 = (f32[80,256]{1,0:T(8,128)S(1)}, f32[80,256]{1,0:T(8,128)S(1)}, u32[]{:S(2)}, u32[]{:S(2)}) collective-permute-start(f32[80,256]{1,0:T(8,128)S(1)} %add_add_fusion.2.refs_0_), channel_id=1, source_target_pairs={{24,0},{28,4},{16,8},{20,12},{8,16},{12,20},{0,24},{4,28},{25,1},{... | collective-permute-start | bytes 245768 | tf_op jit(solution)/shard_map/ppermute | solution.py:50
  43.9 5.8 %collective-permute-start.17 = (f32[80,256]{1,0:T(8,128)S(1)}, f32[80,256]{1,0:T(8,128)S(1)}, u32[]{:S(2)}, u32[]{:S(2)}) collective-permute-start(f32[80,256]{1,0:T(8,128)S(1)} %add_add_fusion.2.refs_0_), channel_id=1, source_target_pairs={{20,0},{16,4},{28,8},{24,12},{4,16},{0,20},{12,24},{8,28},{21,1},{... | collective-permute-start | bytes 245768 | tf_op jit(solution)/shard_map/ppermute | solution.py:50
  43.9 7.6 %collective-permute-start.16 = (f32[80,256]{1,0:T(8,128)S(1)}, f32[80,256]{1,0:T(8,128)S(1)}, u32[]{:S(2)}, u32[]{:S(2)}) collective-permute-start(f32[80,256]{1,0:T(8,128)S(1)} %add_add_fusion.2.refs_0_), channel_id=1, source_target_pairs={{16,0},{20,4},{24,8},{28,12},{0,16},{4,20},{8,24},{12,28},{17,1},{... | collective-permute-start | bytes 245768 | tf_op jit(solution)/shard_map/ppermute | solution.py:50
  45.6 5.9 %collective-permute-start.15 = (f32[80,256]{1,0:T(8,128)S(1)}, f32[80,256]{1,0:T(8,128)S(1)}, u32[]{:S(2)}, u32[]{:S(2)}) collective-permute-start(f32[80,256]{1,0:T(8,128)S(1)} %add_add_fusion.2.refs_0_), channel_id=1, source_target_pairs={{12,0},{8,4},{4,8},{0,12},{28,16},{24,20},{20,24},{16,28},{13,1},{... | collective-permute-start | bytes 245768 | tf_op jit(solution)/shard_map/ppermute | solution.py:50
  46.5 5.6 %collective-permute-start.14 = (f32[80,256]{1,0:T(8,128)S(1)}, f32[80,256]{1,0:T(8,128)S(1)}, u32[]{:S(2)}, u32[]{:S(2)}) collective-permute-start(f32[80,256]{1,0:T(8,128)S(1)} %add_add_fusion.2.refs_0_), channel_id=1, source_target_pairs={{8,0},{12,4},{0,8},{4,12},{24,16},{28,20},{16,24},{20,28},{9,1},{1... | collective-permute-start | bytes 245768 | tf_op jit(solution)/shard_map/ppermute | solution.py:50
  47.4 4.7 %collective-permute-start.13 = (f32[80,256]{1,0:T(8,128)S(1)}, f32[80,256]{1,0:T(8,128)S(1)}, u32[]{:S(2)}, u32[]{:S(2)}) collective-permute-start(f32[80,256]{1,0:T(8,128)S(1)} %add_add_fusion.2.refs_0_), channel_id=1, source_target_pairs={{4,0},{0,4},{12,8},{8,12},{20,16},{16,20},{28,24},{24,28},{5,1},{1... | collective-permute-start | bytes 245768 | tf_op jit(solution)/shard_map/ppermute | solution.py:50
  56.8 36.2 %copy-start.3 = (f32[64,64]{1,0:T(8,128)}, f32[64,64]{1,0:T(8,128)S(1)}, u32[]{:S(2)}) copy-start(f32[64,64]{1,0:T(8,128)S(1)} %get-tuple-element.20.first_ref) | copy-start | bytes 49156
  56.8 5.4 %collective-permute-start.20 = (f32[80,256]{1,0:T(8,128)S(1)}, f32[80,256]{1,0:T(8,128)S(1)}, u32[]{:S(2)}, u32[]{:S(2)}) collective-permute-start(f32[80,256]{1,0:T(8,128)S(1)} %get-tuple-element.22), channel_id=1, source_target_pairs={{0,1},{1,0},{2,3},{3,2},{4,5},{5,4},{6,7},{7,6},{8,9},{9,8},{10,11... | collective-permute-start | bytes 245768 | tf_op jit(solution)/shard_map/ppermute | solution.py:58
  57.7 9.2 %collective-permute-start.21 = (f32[80,256]{1,0:T(8,128)S(1)}, f32[80,256]{1,0:T(8,128)S(1)}, u32[]{:S(2)}, u32[]{:S(2)}) collective-permute-start(f32[80,256]{1,0:T(8,128)S(1)} %get-tuple-element.23), channel_id=1, source_target_pairs={{0,2},{1,3},{2,0},{3,1},{4,6},{5,7},{6,4},{7,5},{8,10},{9,11},{10,... | collective-permute-start | bytes 245768 | tf_op jit(solution)/shard_map/ppermute | solution.py:58
  58.5 8.4 %collective-permute-start.22 = (f32[80,256]{1,0:T(8,128)S(1)}, f32[80,256]{1,0:T(8,128)S(1)}, u32[]{:S(2)}, u32[]{:S(2)}) collective-permute-start(f32[80,256]{1,0:T(8,128)S(1)} %get-tuple-element.24), channel_id=1, source_target_pairs={{0,3},{1,2},{2,1},{3,0},{4,7},{5,6},{6,5},{7,4},{8,11},{9,10},{10,... | collective-permute-start | bytes 245768 | tf_op jit(solution)/shard_map/ppermute | solution.py:58
  66.9 5.1 %collective-permute-start.29 = (f32[80,256]{1,0:T(8,128)S(1)}, f32[80,256]{1,0:T(8,128)S(1)}, u32[]{:S(2)}, u32[]{:S(2)}) collective-permute-start(f32[80,256]{1,0:T(8,128)S(1)} %add_add_fusion.1.refs_0_), channel_id=1, source_target_pairs={{28,0},{24,4},{20,8},{16,12},{12,16},{8,20},{4,24},{0,28},{29,1},{... | collective-permute-start | bytes 245768 | tf_op jit(solution)/shard_map/ppermute | solution.py:50
  67.0 6.4 %collective-permute-start.28 = (f32[80,256]{1,0:T(8,128)S(1)}, f32[80,256]{1,0:T(8,128)S(1)}, u32[]{:S(2)}, u32[]{:S(2)}) collective-permute-start(f32[80,256]{1,0:T(8,128)S(1)} %add_add_fusion.1.refs_0_), channel_id=1, source_target_pairs={{24,0},{28,4},{16,8},{20,12},{8,16},{12,20},{0,24},{4,28},{25,1},{... | collective-permute-start | bytes 245768 | tf_op jit(solution)/shard_map/ppermute | solution.py:50
  68.2 7.0 %collective-permute-start.27 = (f32[80,256]{1,0:T(8,128)S(1)}, f32[80,256]{1,0:T(8,128)S(1)}, u32[]{:S(2)}, u32[]{:S(2)}) collective-permute-start(f32[80,256]{1,0:T(8,128)S(1)} %add_add_fusion.1.refs_0_), channel_id=1, source_target_pairs={{20,0},{16,4},{28,8},{24,12},{4,16},{0,20},{12,24},{8,28},{21,1},{... | collective-permute-start | bytes 245768 | tf_op jit(solution)/shard_map/ppermute | solution.py:50
  70.7 6.4 %collective-permute-start.26 = (f32[80,256]{1,0:T(8,128)S(1)}, f32[80,256]{1,0:T(8,128)S(1)}, u32[]{:S(2)}, u32[]{:S(2)}) collective-permute-start(f32[80,256]{1,0:T(8,128)S(1)} %add_add_fusion.1.refs_0_), channel_id=1, source_target_pairs={{16,0},{20,4},{24,8},{28,12},{0,16},{4,20},{8,24},{12,28},{17,1},{... | collective-permute-start | bytes 245768 | tf_op jit(solution)/shard_map/ppermute | solution.py:50
  71.4 5.6 %collective-permute-start.25 = (f32[80,256]{1,0:T(8,128)S(1)}, f32[80,256]{1,0:T(8,128)S(1)}, u32[]{:S(2)}, u32[]{:S(2)}) collective-permute-start(f32[80,256]{1,0:T(8,128)S(1)} %add_add_fusion.1.refs_0_), channel_id=1, source_target_pairs={{12,0},{8,4},{4,8},{0,12},{28,16},{24,20},{20,24},{16,28},{13,1},{... | collective-permute-start | bytes 245768 | tf_op jit(solution)/shard_map/ppermute | solution.py:50
  72.0 5.3 %collective-permute-start.24 = (f32[80,256]{1,0:T(8,128)S(1)}, f32[80,256]{1,0:T(8,128)S(1)}, u32[]{:S(2)}, u32[]{:S(2)}) collective-permute-start(f32[80,256]{1,0:T(8,128)S(1)} %add_add_fusion.1.refs_0_), channel_id=1, source_target_pairs={{8,0},{12,4},{0,8},{4,12},{24,16},{28,20},{16,24},{20,28},{9,1},{1... | collective-permute-start | bytes 245768 | tf_op jit(solution)/shard_map/ppermute | solution.py:50
  73.4 4.0 %collective-permute-start.23 = (f32[80,256]{1,0:T(8,128)S(1)}, f32[80,256]{1,0:T(8,128)S(1)}, u32[]{:S(2)}, u32[]{:S(2)}) collective-permute-start(f32[80,256]{1,0:T(8,128)S(1)} %add_add_fusion.1.refs_0_), channel_id=1, source_target_pairs={{4,0},{0,4},{12,8},{8,12},{20,16},{16,20},{28,24},{24,28},{5,1},{1... | collective-permute-start | bytes 245768 | tf_op jit(solution)/shard_map/ppermute | solution.py:50
  82.1 11.0 %copy-start.4 = (f32[64,64]{1,0:T(8,128)}, f32[64,64]{1,0:T(8,128)S(1)}, u32[]{:S(2)}) copy-start(f32[64,64]{1,0:T(8,128)S(1)} %get-tuple-element.25.second_ref) | copy-start | bytes 49156
  82.1 4.5 %collective-permute-start.30 = (f32[80,256]{1,0:T(8,128)S(1)}, f32[80,256]{1,0:T(8,128)S(1)}, u32[]{:S(2)}, u32[]{:S(2)}) collective-permute-start(f32[80,256]{1,0:T(8,128)S(1)} %get-tuple-element.27), channel_id=1, source_target_pairs={{0,1},{1,0},{2,3},{3,2},{4,5},{5,4},{6,7},{7,6},{8,9},{9,8},{10,11... | collective-permute-start | bytes 245768 | tf_op jit(solution)/shard_map/ppermute | solution.py:58
  83.6 9.4 %collective-permute-start.31 = (f32[80,256]{1,0:T(8,128)S(1)}, f32[80,256]{1,0:T(8,128)S(1)}, u32[]{:S(2)}, u32[]{:S(2)}) collective-permute-start(f32[80,256]{1,0:T(8,128)S(1)} %get-tuple-element.28), channel_id=1, source_target_pairs={{0,2},{1,3},{2,0},{3,1},{4,6},{5,7},{6,4},{7,5},{8,10},{9,11},{10,... | collective-permute-start | bytes 245768 | tf_op jit(solution)/shard_map/ppermute | solution.py:58
  84.6 8.5 %collective-permute-start.32 = (f32[80,256]{1,0:T(8,128)S(1)}, f32[80,256]{1,0:T(8,128)S(1)}, u32[]{:S(2)}, u32[]{:S(2)}) collective-permute-start(f32[80,256]{1,0:T(8,128)S(1)} %get-tuple-element.29), channel_id=1, source_target_pairs={{0,3},{1,2},{2,1},{3,0},{4,7},{5,6},{6,5},{7,4},{8,11},{9,10},{10,... | collective-permute-start | bytes 245768 | tf_op jit(solution)/shard_map/ppermute | solution.py:58
  93.1 8.6 %copy-start.5 = (f32[64,64]{1,0:T(8,128)}, f32[64,64]{1,0:T(8,128)S(1)}, u32[]{:S(2)}) copy-start(f32[64,64]{1,0:T(8,128)S(1)} %pad_maximum_fusion.refs_0_) | copy-start | bytes 49156
  93.2 4.5 %collective-permute-start.39 = (f32[64,64]{1,0:T(8,128)S(1)}, f32[64,64]{1,0:T(8,128)S(1)}, u32[]{:S(2)}, u32[]{:S(2)}) collective-permute-start(f32[64,64]{1,0:T(8,128)S(1)} %pad_maximum_fusion.refs_0_), channel_id=1, source_target_pairs={{28,0},{24,4},{20,8},{16,12},{12,16},{8,20},{4,24},{0,28},{29,1},{... | collective-permute-start | bytes 49160 | tf_op jit(solution)/shard_map/ppermute | solution.py:50
  93.2 5.2 %collective-permute-start.38 = (f32[64,64]{1,0:T(8,128)S(1)}, f32[64,64]{1,0:T(8,128)S(1)}, u32[]{:S(2)}, u32[]{:S(2)}) collective-permute-start(f32[64,64]{1,0:T(8,128)S(1)} %pad_maximum_fusion.refs_0_), channel_id=1, source_target_pairs={{24,0},{28,4},{16,8},{20,12},{8,16},{12,20},{0,24},{4,28},{25,1},{... | collective-permute-start | bytes 49160 | tf_op jit(solution)/shard_map/ppermute | solution.py:50
  94.6 5.5 %collective-permute-start.37 = (f32[64,64]{1,0:T(8,128)S(1)}, f32[64,64]{1,0:T(8,128)S(1)}, u32[]{:S(2)}, u32[]{:S(2)}) collective-permute-start(f32[64,64]{1,0:T(8,128)S(1)} %pad_maximum_fusion.refs_0_), channel_id=1, source_target_pairs={{20,0},{16,4},{28,8},{24,12},{4,16},{0,20},{12,24},{8,28},{21,1},{... | collective-permute-start | bytes 49160 | tf_op jit(solution)/shard_map/ppermute | solution.py:50
  96.6 3.9 %collective-permute-start.36 = (f32[64,64]{1,0:T(8,128)S(1)}, f32[64,64]{1,0:T(8,128)S(1)}, u32[]{:S(2)}, u32[]{:S(2)}) collective-permute-start(f32[64,64]{1,0:T(8,128)S(1)} %pad_maximum_fusion.refs_0_), channel_id=1, source_target_pairs={{16,0},{20,4},{24,8},{28,12},{0,16},{4,20},{8,24},{12,28},{17,1},{... | collective-permute-start | bytes 49160 | tf_op jit(solution)/shard_map/ppermute | solution.py:50
  97.6 3.3 %collective-permute-start.35 = (f32[64,64]{1,0:T(8,128)S(1)}, f32[64,64]{1,0:T(8,128)S(1)}, u32[]{:S(2)}, u32[]{:S(2)}) collective-permute-start(f32[64,64]{1,0:T(8,128)S(1)} %pad_maximum_fusion.refs_0_), channel_id=1, source_target_pairs={{12,0},{8,4},{4,8},{0,12},{28,16},{24,20},{20,24},{16,28},{13,1},{... | collective-permute-start | bytes 49160 | tf_op jit(solution)/shard_map/ppermute | solution.py:50
  97.6 4.1 %copy-start.6 = (f32[64,64]{1,0:T(8,128)}, f32[64,64]{1,0:T(8,128)S(1)}, u32[]{:S(2)}) copy-start(f32[64,64]{1,0:T(8,128)S(1)} %collective-permute-done.39.refs_7_) | copy-start | bytes 49156
  97.6 4.1 %collective-permute-start.34 = (f32[64,64]{1,0:T(8,128)S(1)}, f32[64,64]{1,0:T(8,128)S(1)}, u32[]{:S(2)}, u32[]{:S(2)}) collective-permute-start(f32[64,64]{1,0:T(8,128)S(1)} %pad_maximum_fusion.refs_0_), channel_id=1, source_target_pairs={{8,0},{12,4},{0,8},{4,12},{24,16},{28,20},{16,24},{20,28},{9,1},{1... | collective-permute-start | bytes 49160 | tf_op jit(solution)/shard_map/ppermute | solution.py:50
  98.4 3.4 %copy-start.7 = (f32[64,64]{1,0:T(8,128)}, f32[64,64]{1,0:T(8,128)S(1)}, u32[]{:S(2)}) copy-start(f32[64,64]{1,0:T(8,128)S(1)} %collective-permute-done.38.refs_6_) | copy-start | bytes 49156
  98.4 3.3 %collective-permute-start.33 = (f32[64,64]{1,0:T(8,128)S(1)}, f32[64,64]{1,0:T(8,128)S(1)}, u32[]{:S(2)}, u32[]{:S(2)}) collective-permute-start(f32[64,64]{1,0:T(8,128)S(1)} %pad_maximum_fusion.refs_0_), channel_id=1, source_target_pairs={{4,0},{0,4},{12,8},{8,12},{20,16},{16,20},{28,24},{24,28},{5,1},{1... | collective-permute-start | bytes 49160 | tf_op jit(solution)/shard_map/ppermute | solution.py:50
  (5 other events, 5.0 us)

commit v2 on v1

--- a/solution.py
+++ b/solution.py
@@ -44,20 +44,26 @@
     return index ^ other if size & (size - 1) == 0 else (other - index) % size
 
 
+def fetch(piece, axis, shift):
+    size = lax.axis_size(axis)
+    return lax.ppermute(piece, axis, [(partner(i, shift, size), i) for i in range(size)])
+
+
 def gather_pieces(piece, axis):
+    return [piece] + [fetch(piece, axis, shift) for shift in range(1, lax.axis_size(axis))]
+
+
+def gather_in_pairs(piece, axis):
     size = lax.axis_size(axis)
-    return [piece] + [
-        lax.ppermute(piece, axis, [(partner(i, shift, size), i) for i in range(size)])
-        for shift in range(1, size)
-    ]
-
-
-def scatter_pieces(pieces, axis):
-    size = lax.axis_size(axis)
-    return [pieces[0]] + [
-        lax.ppermute(pieces[shift], axis, [(i, partner(i, shift, size)) for i in range(size)])
-        for shift in range(1, size)
-    ]
+    if size & (size - 1) or size == 1:
+        pieces = gather_pieces(piece, axis)
+        return [jnp.stack(pieces[:1])] if size == 1 else [jnp.stack(pieces[k::2]) for k in (0, 1)]
+    evens = jnp.stack([piece] + [fetch(piece, axis, shift) for shift in range(2, size, 2)])
+    return [evens, fetch(evens, axis, 1)]
+
+
+def piece_at(pairs, shift):
+    return pairs[shift % len(pairs)][shift // len(pairs)]
 
 
 def dot_pairs(left, right):
@@ -129,11 +135,10 @@
     )(positions, entries)
 
 
-def step_kernel(n_row, n_col, span, first, *refs):
-    pieces, refs = refs[:n_row], refs[n_row:]
+def step_kernel(n_pairs, n_row, n_col, span, first, positions_ref, *refs):
+    pairs, refs = refs[:n_pairs], refs[n_pairs:]
     x_pieces, refs = refs[:n_col], refs[n_col:]
-    dense_ref, refs = refs[0], refs[1:]
-    outs, refs = refs[:n_col], refs[n_col:]
+    dense_ref, out_ref, refs = refs[0], refs[1], refs[2:]
     if not first:
         total_ref, refs = refs[0], refs[1:]
     held, digits, sems = refs
@@ -146,16 +151,16 @@
     ]
     for copy in copies:
         copy.start()
-    for d, piece in enumerate(pieces):
-        vector = reduce_centered(piece[:span, :])
+    for d in range(n_row):
+        vector = reduce_centered(piece_at(pairs, d)[:span])
         digits[:, d * piece_len : (d + 1) * piece_len] = stacked_digits(vector)
     if not first:
-        packed = pieces[0][span:, :]
-        for piece in pieces[1:]:
-            packed = packed + piece[span:, :]
+        packed = sum(jnp.sum(pair[:, span:, :], 0) for pair in pairs)
         total_ref[...] = unpack_square(reduce_centered(packed), span)
     projected = None
     for e in range(n_col):
+        target = positions_ref[3, e]
+        parts = []
         for sub in range(piece_blocks):
             block = e * piece_blocks + sub
             copies[block].wait()
@@ -171,32 +176,34 @@
                 high = high + products[:span, :tile_len]
                 middle = middle + products[:span, tile_len:] + products[span:, :tile_len]
                 low = low + products[span:, tile_len:]
-            outs[e][:span, sub * tile_len : (sub + 1) * tile_len] = reduce_centered(
-                15.0 * high + 256.0 * reduce_centered(middle) + low
-            )
+            parts.append(reduce_centered(15.0 * high + 256.0 * reduce_centered(middle) + low))
+        piece = jnp.concatenate(parts, 1)
+        out_ref[target, :span, :] = piece
         x_values = x_pieces[e][...]
         x_values = jnp.where(x_values > HALF_MODULUS, x_values - MODULUS, x_values)
-        products = dot_pairs(stacked_digits(x_values), stacked_digits(outs[e][:span, :]))
+        products = dot_pairs(stacked_digits(x_values), stacked_digits(piece))
         if n_col * piece_len > EXACT_DEPTH:
             products = reduce_centered(products)
         projected = products if projected is None else projected + products
     packed = pack_square(projection_residues(projected, span), piece_len)
-    for out in outs:
-        out[span:, :] = packed
-
-
-def dense_step(pieces, x_pieces, dense, first):
-    n_row, n_col = len(pieces), len(x_pieces)
+    for e in range(n_col):
+        out_ref[e, span:, :] = packed
+
+
+def dense_step(pairs, x_pieces, positions, dense, first):
+    n_row, n_col = len(pairs) * pairs[0].shape[0], len(x_pieces)
     span, piece_len = x_pieces[0].shape
     row_blocks, depth, width = dense.shape
     rows = span + span * span // piece_len
-    outs = [jax.ShapeDtypeStruct((rows, piece_len), jnp.float32)] * n_col
+    outs = [jax.ShapeDtypeStruct((n_col, rows, piece_len), jnp.float32)]
     if not first:
         outs = outs + [jax.ShapeDtypeStruct((span, span), jnp.float32)]
     vmem = pl.BlockSpec(memory_space=pltpu.VMEM)
     results = pl.pallas_call(
-        functools.partial(step_kernel, n_row, n_col, span, first),
-        in_specs=[vmem] * (n_row + n_col) + [pl.BlockSpec(memory_space=pl.ANY)],
+        functools.partial(step_kernel, len(pairs), n_row, n_col, span, first),
+        in_specs=[pl.BlockSpec(memory_space=pltpu.SMEM)]
+        + [vmem] * (len(pairs) + n_col)
+        + [pl.BlockSpec(memory_space=pl.ANY)],
         out_specs=[vmem] * len(outs),
         out_shape=outs,
         scratch_shapes=[
@@ -208,12 +215,13 @@
         cost_estimate=pl.CostEstimate(
             flops=4 * span * dense.size, bytes_accessed=2 * dense.size, transcendentals=0
         ),
-    )(*pieces, *x_pieces, dense)
-    return list(results[:n_col]), (None if first else results[n_col])
-
-
-def sparse_step(pieces, x_pieces, a_digits, positions, first):
+    )(positions, *pairs, *x_pieces, dense)
+    return results[0], (None if first else results[1])
+
+
+def sparse_step(pairs, x_pieces, positions, a_digits, first):
     span, piece_len = x_pieces[0].shape
+    pieces = [piece_at(pairs, d) for d in range(len(pairs) * pairs[0].shape[0])]
     slot_count, _, tile_len, _ = a_digits.shape
     n_col = len(x_pieces)
     row_blocks = piece_len // tile_len * n_col
@@ -243,7 +251,8 @@
         products = dot_pairs(stacked_digits(x_values), stacked_digits(outs[:, e]))
         projected = projected + reduce_centered(products)
     packed = pack_square(projection_residues(projected, span), piece_len)
-    return [jnp.concatenate([outs[:, e], packed], 0) for e in range(n_col)], total
+    outs = jnp.stack([jnp.concatenate([outs[:, e], packed], 0) for e in range(n_col)])
+    return jnp.zeros_like(outs).at[positions[3, :n_col]].set(outs), total
 
 
 def multiply_mod(left, right):
@@ -262,10 +271,8 @@
 def sigma_kernel(count, first_ref, second_ref, *refs):
     thirds, out_ref = refs[:count], refs[count]
     c_1, c_2 = first_ref[...], second_ref[...]
-    c_3 = thirds[0][...]
-    for piece in thirds[1:]:
-        c_3 = c_3 + piece[...]
-    c_3 = reduce_centered(c_3)
+    packed = sum(jnp.sum(pair[...], 0) for pair in thirds)
+    c_3 = unpack_square(reduce_centered(packed), c_1.shape[0])
     e_2 = reduce_centered(c_1 - multiply_mod(c_1, c_2))
     both = reduce_centered(c_1 + e_2)
     start = multiply_mod(e_2, c_1)
@@ -276,12 +283,12 @@
     out_ref[2] = canonical(-both - e_3) * (1.0 / MODULUS)
 
 
-def sigma_update(c_1, c_2, c_3_pieces):
+def sigma_update(c_1, c_2, c_3_pairs):
     span = c_1.shape[0]
     return pl.pallas_call(
-        functools.partial(sigma_kernel, len(c_3_pieces)),
+        functools.partial(sigma_kernel, len(c_3_pairs)),
         out_shape=jax.ShapeDtypeStruct((STEP_COUNT, span, span), jnp.float32),
-    )(c_1, c_2, *c_3_pieces)
+    )(c_1, c_2, *c_3_pairs)
 
 
 def local(tile_entries, tile_rows, tile_cols, tile_count, block_x, block_y):
@@ -299,25 +306,26 @@
             row_shift * piece_blocks + rows_here % piece_blocks,
             col_shift * piece_blocks + cols_here % piece_blocks,
             jnp.full((slot_count,), tile_count[0, 0], jnp.int32),
+            partner(lax.axis_index("col"), jnp.arange(slot_count, dtype=jnp.int32) % n_col, n_col),
         ]
     )
-    pieces = gather_pieces(block_y, "row")
+    pairs = gather_in_pairs(block_y, "row")
     x_pieces = gather_pieces(block_x, "col")
     if row_blocks * col_blocks <= DENSE_CELLS * slot_count:
         dense = build_dense(entries, positions, row_blocks, col_blocks)
-        multiply = functools.partial(dense_step, dense=dense)
+        multiply = functools.partial(dense_step, positions=positions, dense=dense)
     else:
         centred = jnp.where(entries > HALF_MODULUS, entries - MODULUS, entries)
         a_digits = jnp.stack(balanced_digits(centred), 1).astype(jnp.bfloat16)
-        multiply = functools.partial(sparse_step, a_digits=a_digits, positions=positions)
+        multiply = functools.partial(sparse_step, positions=positions, a_digits=a_digits)
     totals = []
     for step_index in range(STEP_COUNT):
-        outs, total = multiply(pieces, x_pieces, first=step_index == 0)
+        outs, total = multiply(pairs, x_pieces, first=step_index == 0)
         totals.append(total)
-        summed = functools.reduce(jnp.add, scatter_pieces(outs, "col"))
+        summed = jnp.sum(lax.all_to_all(outs, "col", 0, 0), 0)
         if step_index < STEP_COUNT - 1:
-            pieces = gather_pieces(summed, "row")
-    thirds = gather_pieces(unpack_square(summed[span:], span), "row")
+            pairs = gather_in_pairs(summed, "row")
+    thirds = gather_in_pairs(summed[span:], "row")
     polynomial = sigma_update(totals[1], totals[2], thirds)
     return polynomial, canonical(summed[:span]) * (1.0 / MODULUS)
 

time: 106 us -> 113 us (1.066)
  blocking collectives: 0 us -> 42.6 us
  starting transfers between devices: 46.6 us -> 23.4 us
  waiting for transfers between devices: 29 us -> 14 us
  other arithmetic: 1.48 us -> 3.04 us
  local copies, waits for them, and re-layouts: 2.93 us -> 4.1 us
    all_to_all x0 -> x3, blocking collectives: none -> 42.6 us  [local(): summed = jnp.sum(lax.all_to_all(outs, 'col', 0, 0), 0)]
    ppermute x40 -> x19, starting transfers between devices: 46.6 us -> 23.4 us  [fetch(): lax.ppermute(piece, axis, [(partner(i, shift, size), i) for i in range(si...]
    ppermute x40 -> x19, waiting for transfers between devices: 29 us -> 14 us  [fetch(): lax.ppermute(piece, axis, [(partner(i, shift, size), i) for i in range(si...]
    pallas_call x4, Pallas kernels: 16.5 us -> 18.2 us  [the longest x3 15.9 us: dense_step(): pl.pallas_call(functools.partial(step_kernel, len(pairs), n_row, n_col, s...]
    unnamed x26 -> x12, local copies, waits for them, and re-layouts: 2.78 us -> 4.02 us
  transfers between devices with their start and end apart: 40 -> 19, of which waited for: 18 -> 10; matrix products, arithmetic and copies ran while one was open for 1% -> 3% of each run, Pallas kernels for 6% -> 5%
where the time goes in v2:
time: 113 us
  blocking collectives  42.6 us (38%)
  Pallas kernels  24.1 us (21%)
  starting transfers between devices  23.4 us (21%)
  waiting for transfers between devices  14 us (12%)
  local copies, waits for them, and re-layouts  4.1 us (4%)
  other arithmetic  3.04 us (3%)
  between operations  1.45 us (1%)
    all_to_all x3, blocking collectives, local(): summed = jnp.sum(lax.all_to_all(outs, 'col', 0, 0), 0)  42.6 us
    ppermute x19, starting transfers between devices, fetch(): lax.ppermute(piece, axis, [(partner(i, shift, size), i) for i in range(si...  23.4 us
    pallas_call x3, Pallas kernels, dense_step(): pl.pallas_call(functools.partial(step_kernel, len(pairs), n_row, n_col, s...  15.9 us
    ppermute x19, waiting for transfers between devices, fetch(): lax.ppermute(piece, axis, [(partner(i, shift, size), i) for i in range(si...  14 us
    pallas_call x1, Pallas kernels, build_dense(): pl.pallas_call(functools.partial(build_kernel, group), grid_spec=pltpu.Pr...  5.92 us
    unnamed x12, local copies, waits for them, and re-layouts  4.02 us
    pallas_call x1, Pallas kernels, sigma_update(): pl.pallas_call(functools.partial(sigma_kernel, len(c_3_pairs)), out_shape...  2.28 us
  transfers between devices with their start and end apart: 19, of which 10 were waited for; matrix products, arithmetic and copies ran while one was open for 3% of the time, Pallas kernels for 5%

profile of v2, /device:TPU:0, one launch (start us, length us, event | category | flops | bytes accessed | tf_op | source)
XLA Modules:
  0.0 112.7 jit_solution(13147161146345538489)
XLA Ops:
  0.6 0.0 copy-start.1
  0.6 3.0 %collective-permute-start = (f32[64,256]{1,0:T(8,128)}, f32[64,256]{1,0:T(8,128)S(1)}, u32[]{:S(2)}, u32[]{:S(2)}) collective-permute-start(f32[64,256]{1,0:T(8,128)} %param.11), channel_id=1, source_target_pairs={{8,0},{12,4},{0,8},{4,12},{24,16},{28,20},{16,24},{20,28},{9,1},{1... | collective-permute-start | bytes 196616 | tf_op jit(solution)/shard_map/ppermute | solution.py:49
  3.6 1.5 %collective-permute-start.2 = (f32[64,256]{1,0:T(8,128)}, f32[64,256]{1,0:T(8,128)S(1)}, u32[]{:S(2)}, u32[]{:S(2)}) collective-permute-start(f32[64,256]{1,0:T(8,128)} %param.11), channel_id=1, source_target_pairs={{24,0},{28,4},{16,8},{20,12},{8,16},{12,20},{0,24},{4,28},{25,1},{... | collective-permute-start | bytes 196616 | tf_op jit(solution)/shard_map/ppermute | solution.py:49
  5.1 0.1 collective-permute-start.1
  5.2 4.1 %collective-permute-start.6 = (f32[64,256]{1,0:T(8,128)}, f32[64,256]{1,0:T(8,128)S(1)}, u32[]{:S(2)}, u32[]{:S(2)}) collective-permute-start(f32[64,256]{1,0:T(8,128)} %refs_2_.5), channel_id=1, source_target_pairs={{3,0},{2,1},{1,2},{0,3},{7,4},{6,5},{5,6},{4,7},{11,8},{10,9},{9,1... | collective-permute-start | bytes 196616 | tf_op jit(solution)/shard_map/ppermute | solution.py:49
  9.2 0.0 collective-permute-start.5
  9.2 0.7 fusion.1
  9.9 0.0 collective-permute-done
  9.9 0.6 collective-permute-start.4
  10.6 0.9 pad_maximum_fusion.2.refs_0_
  11.4 0.1 collective-permute-start.3
  11.5 0.7 fusion.2
  12.8 0.1 pad.18.clone
  12.9 0.1 pad_add_fusion.positions_ref
  13.0 2.2 %copy-done = f32[1,1,64,128,128]{4,3,2,1,0:T(8,128)S(1)} copy-done((f32[1,1,64,128,128]{4,3,2,1,0:T(8,128)S(1)}, f32[1,1,64,128,128]{4,3,2,1,0:T(8,128)}, u32[]{:S(2)}) %copy-start) | copy-done | bytes 4194328
  15.2 5.9 %shard_map.77.refs_6_ = bf16[8,2048,256]{2,1,0:T(8,128)(2,1)} custom-call(s32[4,64]{1,0:T(4,128)S(1)} %pad_add_fusion.positions_ref, f32[64,128,128]{2,1,0:T(8,128)S(1)} %bitcast.48), custom_call_target="tpu_custom_call" | custom-call | flops 8388608 | bytes 16777216 | tf_op jit(solution)/shard_map/pallas_call | solution.py:122
  21.1 5.3 %shard_map.78 = f32[4,80,256]{2,1,0:T(8,128)S(1)} custom-call(s32[4,64]{1,0:T(4,128)S(1)} %pad_add_fusion.positions_ref, f32[4,64,256]{2,1,0:T(8,128)S(1)} %pad_maximum_fusion.2.refs_0_, f32[4,64,256]{2,1,0:T(8,128)S(1)} %collective-permute-done.3.refs_1_, f32[64,256]{1,0:T(8,128)S(1)} %copy-done.1, f32[64,256]{1,0:T(8,128)S(1)} %collective-permute-done.4.refs_3_, ...), custom_call_target="tpu_custom_call" | custom-call | flops 1073741824 | bytes 8388608 | tf_op jit(solution)/shard_map/pallas_call | solution.py:202
  26.4 15.8 %all_to_all.15 = f32[4,80,256]{2,1,0:T(8,128)S(1)} all-to-all(f32[4,80,256]{2,1,0:T(8,128)S(1)} %shard_map.78), channel_id=1, replica_groups=mesh['row'=8,'col'=4] {'col'}, dimensions={0} | all-to-all | bytes 655360 | tf_op jit(solution)/shard_map/all_to_all | solution.py:325
  42.3 4.2 %collective-permute-start.9 = (f32[80,256]{1,0:T(8,128)S(1)}, f32[80,256]{1,0:T(8,128)S(1)}, u32[]{:S(2)}, u32[]{:S(2)}) collective-permute-start(f32[80,256]{1,0:T(8,128)S(1)} %reduce_sum.27), channel_id=1, source_target_pairs={{24,0},{28,4},{16,8},{20,12},{8,16},{12,20},{0,24},{4,28},{25,1},{... | collective-permute-start | bytes 245768 | tf_op jit(solution)/shard_map/ppermute | solution.py:49
  46.5 2.6 %collective-permute-start.8 = (f32[80,256]{1,0:T(8,128)S(1)}, f32[80,256]{1,0:T(8,128)S(1)}, u32[]{:S(2)}, u32[]{:S(2)}) collective-permute-start(f32[80,256]{1,0:T(8,128)S(1)} %reduce_sum.27), channel_id=1, source_target_pairs={{16,0},{20,4},{24,8},{28,12},{0,16},{4,20},{8,24},{12,28},{17,1},{... | collective-permute-start | bytes 245768 | tf_op jit(solution)/shard_map/ppermute | solution.py:49
  49.1 2.4 %collective-permute-done.8 = f32[80,256]{1,0:T(8,128)S(1)} collective-permute-done((f32[80,256]{1,0:T(8,128)S(1)}, f32[80,256]{1,0:T(8,128)S(1)}, u32[]{:S(2)}, u32[]{:S(2)}) %collective-permute-start.8) | collective-permute-done | bytes 81952 | tf_op jit(solution)/shard_map/ppermute | solution.py:49
  51.5 2.0 %collective-permute-done.7 = f32[80,256]{1,0:T(8,128)S(1)} collective-permute-done((f32[80,256]{1,0:T(8,128)S(1)}, f32[80,256]{1,0:T(8,128)S(1)}, u32[]{:S(2)}, u32[]{:S(2)}) %collective-permute-start.7) | collective-permute-done | bytes 81952 | tf_op jit(solution)/shard_map/ppermute | solution.py:49
  53.6 0.1 collective-permute-start.10
  53.6 1.6 %collective-permute-done.10.refs_1_ = f32[4,80,256]{2,1,0:T(8,128)S(1)} collective-permute-done((f32[4,80,256]{2,1,0:T(8,128)S(1)}, f32[4,80,256]{2,1,0:T(8,128)S(1)}, u32[]{:S(2)}, u32[]{:S(2)}) %collective-permute-start.10) | collective-permute-done | bytes 327712 | tf_op jit(solution)/shard_map/ppermute | solution.py:49
  55.3 5.3 %shard_map.79 = (f32[4,80,256]{2,1,0:T(8,128)S(1)}, f32[64,64]{1,0:T(8,128)S(1)}) custom-call(s32[4,64]{1,0:T(4,128)S(1)} %pad_add_fusion.positions_ref, f32[4,80,256]{2,1,0:T(8,128)S(1)} %pad_maximum_fusion.refs_0_, f32[4,80,256]{2,1,0:T(8,128)S(1)} %collective-permute-done.10.refs_1_, f32[64,256]{1,0:T(8,128)S(1)} %copy-done.1, ...), custom_call_target="tpu_custom_call" | custom-call | flops 1073741824 | bytes 8388608 | tf_op jit(solution)/shard_map/pallas_call | solution.py:202
  60.6 0.6 copy-done.2
  61.2 13.2 %all_to_all.16 = f32[4,80,256]{2,1,0:T(8,128)S(1)} all-to-all(f32[4,80,256]{2,1,0:T(8,128)S(1)} %get-tuple-element.7), channel_id=1, replica_groups=mesh['row'=8,'col'=4] {'col'}, dimensions={0} | all-to-all | bytes 655360 | tf_op jit(solution)/shard_map/all_to_all | solution.py:325
  74.4 1.2 %collective-permute-start.13 = (f32[80,256]{1,0:T(8,128)S(1)}, f32[80,256]{1,0:T(8,128)S(1)}, u32[]{:S(2)}, u32[]{:S(2)}) collective-permute-start(f32[80,256]{1,0:T(8,128)S(1)} %reduce_sum.28), channel_id=1, source_target_pairs={{24,0},{28,4},{16,8},{20,12},{8,16},{12,20},{0,24},{4,28},{25,1},{... | collective-permute-start | bytes 245768 | tf_op jit(solution)/shard_map/ppermute | solution.py:49
  75.6 0.6 collective-permute-start.12
  76.3 1.7 %collective-permute-start.11 = (f32[80,256]{1,0:T(8,128)S(1)}, f32[80,256]{1,0:T(8,128)S(1)}, u32[]{:S(2)}, u32[]{:S(2)}) collective-permute-start(f32[80,256]{1,0:T(8,128)S(1)} %reduce_sum.28), channel_id=1, source_target_pairs={{8,0},{12,4},{0,8},{4,12},{24,16},{28,20},{16,24},{20,28},{9,1},{1... | collective-permute-start | bytes 245768 | tf_op jit(solution)/shard_map/ppermute | solution.py:49
  78.0 1.9 %collective-permute-done.13 = f32[80,256]{1,0:T(8,128)S(1)} collective-permute-done((f32[80,256]{1,0:T(8,128)S(1)}, f32[80,256]{1,0:T(8,128)S(1)}, u32[]{:S(2)}, u32[]{:S(2)}) %collective-permute-start.13) | collective-permute-done | bytes 81952 | tf_op jit(solution)/shard_map/ppermute | solution.py:49
  79.9 0.8 collective-permute-done.12
  80.8 0.1 collective-permute-start.14
  80.8 1.6 %collective-permute-done.14.refs_1_ = f32[4,80,256]{2,1,0:T(8,128)S(1)} collective-permute-done((f32[4,80,256]{2,1,0:T(8,128)S(1)}, f32[4,80,256]{2,1,0:T(8,128)S(1)}, u32[]{:S(2)}, u32[]{:S(2)}) %collective-permute-start.14) | collective-permute-done | bytes 327712 | tf_op jit(solution)/shard_map/ppermute | solution.py:49
  82.5 5.3 %shard_map.80 = (f32[4,80,256]{2,1,0:T(8,128)S(1)}, f32[64,64]{1,0:T(8,128)S(1)}) custom-call(s32[4,64]{1,0:T(4,128)S(1)} %pad_add_fusion.positions_ref, f32[4,80,256]{2,1,0:T(8,128)S(1)} %pad_maximum_fusion.1.refs_0_, f32[4,80,256]{2,1,0:T(8,128)S(1)} %collective-permute-done.14.refs_1_, f32[64,256]{1,0:T(8,128)S(1)} %copy-done.1, ...), custom_call_target="tpu_custom_call" | custom-call | flops 1073741824 | bytes 8388608 | tf_op jit(solution)/shard_map/pallas_call | solution.py:202
  87.8 0.6 copy-done.3
  88.4 13.6 %all_to_all.17 = f32[4,80,256]{2,1,0:T(8,128)S(1)} all-to-all(f32[4,80,256]{2,1,0:T(8,128)S(1)} %get-tuple-element.9), channel_id=1, replica_groups=mesh['row'=8,'col'=4] {'col'}, dimensions={0} | all-to-all | bytes 655360 | tf_op jit(solution)/shard_map/all_to_all | solution.py:325
  102.0 1.1 collective-permute-start.16
  103.1 0.7 collective-permute-start.15
  103.8 1.7 %collective-permute-start.17 = (f32[16,256]{1,0:T(8,128)S(1)}, f32[16,256]{1,0:T(8,128)S(1)}, u32[]{:S(2)}, u32[]{:S(2)}) collective-permute-start(f32[16,256]{1,0:T(8,128)S(1)} %get-tuple-element.11), channel_id=1, source_target_pairs={{24,0},{28,4},{16,8},{20,12},{8,16},{12,20},{0,24},{4,28},{25,1},{... | collective-permute-start | bytes 49160 | tf_op jit(solution)/shard_map/ppermute | solution.py:49
  105.5 0.4 collective-permute-done.16
  105.9 0.9 collective-permute-done.15
  106.8 1.6 %collective-permute-done.17 = f32[16,256]{1,0:T(8,128)S(1)} collective-permute-done((f32[16,256]{1,0:T(8,128)S(1)}, f32[16,256]{1,0:T(8,128)S(1)}, u32[]{:S(2)}, u32[]{:S(2)}) %collective-permute-start.17) | collective-permute-done | bytes 16416 | tf_op jit(solution)/shard_map/ppermute | solution.py:49
  108.5 0.1 collective-permute-start.18
  108.6 0.7 fusion
  109.2 0.6 collective-permute-done.18.refs_1_
  109.8 0.6 copy-done.5
  110.4 2.3 %shard_map.81 = f32[3,64,64]{2,1,0:T(8,128)} custom-call(f32[64,64]{1,0:T(8,128)} %copy-done.2, f32[64,64]{1,0:T(8,128)} %copy-done.3, f32[4,16,256]{2,1,0:T(8,128)} %copy-done.4, f32[4,16,256]{2,1,0:T(8,128)} %copy-done.5), custom_call_target="tpu_custom_call" | custom-call | tf_op jit(solution)/shard_map/pallas_call | solution.py:288
  (23 shorter events, 0.2 us)
Async XLA Ops:
  0.6 20.5 %copy-start.1 = (f32[64,256]{1,0:T(8,128)S(1)}, f32[64,256]{1,0:T(8,128)}, u32[]{:S(2)}) copy-start(f32[64,256]{1,0:T(8,128)} %refs_2_.5) | copy-start | bytes 196612
  0.6 9.3 %collective-permute-start = (f32[64,256]{1,0:T(8,128)}, f32[64,256]{1,0:T(8,128)S(1)}, u32[]{:S(2)}, u32[]{:S(2)}) collective-permute-start(f32[64,256]{1,0:T(8,128)} %param.11), channel_id=1, source_target_pairs={{8,0},{12,4},{0,8},{4,12},{24,16},{28,20},{16,24},{20,28},{9,1},{1... | collective-permute-start | bytes 196616 | tf_op jit(solution)/shard_map/ppermute | solution.py:49
  3.6 6.9 %collective-permute-start.2 = (f32[64,256]{1,0:T(8,128)}, f32[64,256]{1,0:T(8,128)S(1)}, u32[]{:S(2)}, u32[]{:S(2)}) collective-permute-start(f32[64,256]{1,0:T(8,128)} %param.11), channel_id=1, source_target_pairs={{24,0},{28,4},{16,8},{20,12},{8,16},{12,20},{0,24},{4,28},{25,1},{... | collective-permute-start | bytes 196616 | tf_op jit(solution)/shard_map/ppermute | solution.py:49
  5.1 5.4 %collective-permute-start.1 = (f32[64,256]{1,0:T(8,128)}, f32[64,256]{1,0:T(8,128)S(1)}, u32[]{:S(2)}, u32[]{:S(2)}) collective-permute-start(f32[64,256]{1,0:T(8,128)} %param.11), channel_id=1, source_target_pairs={{16,0},{20,4},{24,8},{28,12},{0,16},{4,20},{8,24},{12,28},{17,1},{... | collective-permute-start | bytes 196616 | tf_op jit(solution)/shard_map/ppermute | solution.py:49
  5.2 15.9 %collective-permute-start.6 = (f32[64,256]{1,0:T(8,128)}, f32[64,256]{1,0:T(8,128)S(1)}, u32[]{:S(2)}, u32[]{:S(2)}) collective-permute-start(f32[64,256]{1,0:T(8,128)} %refs_2_.5), channel_id=1, source_target_pairs={{3,0},{2,1},{1,2},{0,3},{7,4},{6,5},{5,6},{4,7},{11,8},{10,9},{9,1... | collective-permute-start | bytes 196616 | tf_op jit(solution)/shard_map/ppermute | solution.py:49
  9.2 11.9 %collective-permute-start.5 = (f32[64,256]{1,0:T(8,128)}, f32[64,256]{1,0:T(8,128)S(1)}, u32[]{:S(2)}, u32[]{:S(2)}) collective-permute-start(f32[64,256]{1,0:T(8,128)} %refs_2_.5), channel_id=1, source_target_pairs={{2,0},{3,1},{0,2},{1,3},{6,4},{7,5},{4,6},{5,7},{10,8},{11,9},{8,1... | collective-permute-start | bytes 196616 | tf_op jit(solution)/shard_map/ppermute | solution.py:49
  9.9 11.2 %collective-permute-start.4 = (f32[64,256]{1,0:T(8,128)}, f32[64,256]{1,0:T(8,128)S(1)}, u32[]{:S(2)}, u32[]{:S(2)}) collective-permute-start(f32[64,256]{1,0:T(8,128)} %refs_2_.5), channel_id=1, source_target_pairs={{1,0},{0,1},{3,2},{2,3},{5,4},{4,5},{7,6},{6,7},{9,8},{8,9},{11,10... | collective-permute-start | bytes 196616 | tf_op jit(solution)/shard_map/ppermute | solution.py:49
  11.4 9.7 %collective-permute-start.3 = (f32[4,64,256]{2,1,0:T(8,128)S(1)}, f32[4,64,256]{2,1,0:T(8,128)S(1)}, u32[]{:S(2)}, u32[]{:S(2)}) collective-permute-start(f32[4,64,256]{2,1,0:T(8,128)S(1)} %pad_maximum_fusion.2.refs_0_), channel_id=1, source_target_pairs={{4,0},{0,4},{12,8},{8,12},{20,16},{16,20},{28,24},{24,28},{5,1},{1... | collective-permute-start | bytes 786440 | tf_op jit(solution)/shard_map/ppermute | solution.py:49
  13.0 2.2 %copy-start = (f32[1,1,64,128,128]{4,3,2,1,0:T(8,128)S(1)}, f32[1,1,64,128,128]{4,3,2,1,0:T(8,128)}, u32[]{:S(2)}) copy-start(f32[1,1,64,128,128]{4,3,2,1,0:T(8,128)} %param.6) | copy-start | bytes 12582916
  42.3 6.8 %collective-permute-start.9 = (f32[80,256]{1,0:T(8,128)S(1)}, f32[80,256]{1,0:T(8,128)S(1)}, u32[]{:S(2)}, u32[]{:S(2)}) collective-permute-start(f32[80,256]{1,0:T(8,128)S(1)} %reduce_sum.27), channel_id=1, source_target_pairs={{24,0},{28,4},{16,8},{20,12},{8,16},{12,20},{0,24},{4,28},{25,1},{... | collective-permute-start | bytes 245768 | tf_op jit(solution)/shard_map/ppermute | solution.py:49
  46.5 5.0 %collective-permute-start.8 = (f32[80,256]{1,0:T(8,128)S(1)}, f32[80,256]{1,0:T(8,128)S(1)}, u32[]{:S(2)}, u32[]{:S(2)}) collective-permute-start(f32[80,256]{1,0:T(8,128)S(1)} %reduce_sum.27), channel_id=1, source_target_pairs={{16,0},{20,4},{24,8},{28,12},{0,16},{4,20},{8,24},{12,28},{17,1},{... | collective-permute-start | bytes 245768 | tf_op jit(solution)/shard_map/ppermute | solution.py:49
  49.1 4.4 %collective-permute-start.7 = (f32[80,256]{1,0:T(8,128)S(1)}, f32[80,256]{1,0:T(8,128)S(1)}, u32[]{:S(2)}, u32[]{:S(2)}) collective-permute-start(f32[80,256]{1,0:T(8,128)S(1)} %reduce_sum.27), channel_id=1, source_target_pairs={{8,0},{12,4},{0,8},{4,12},{24,16},{28,20},{16,24},{20,28},{9,1},{1... | collective-permute-start | bytes 245768 | tf_op jit(solution)/shard_map/ppermute | solution.py:49
  53.6 1.7 %collective-permute-start.10 = (f32[4,80,256]{2,1,0:T(8,128)S(1)}, f32[4,80,256]{2,1,0:T(8,128)S(1)}, u32[]{:S(2)}, u32[]{:S(2)}) collective-permute-start(f32[4,80,256]{2,1,0:T(8,128)S(1)} %pad_maximum_fusion.refs_0_), channel_id=1, source_target_pairs={{4,0},{0,4},{12,8},{8,12},{20,16},{16,20},{28,24},{24,28},{5,1},{1... | collective-permute-start | bytes 983048 | tf_op jit(solution)/shard_map/ppermute | solution.py:49
  60.6 0.6 copy-start.2
  74.4 5.5 %collective-permute-start.13 = (f32[80,256]{1,0:T(8,128)S(1)}, f32[80,256]{1,0:T(8,128)S(1)}, u32[]{:S(2)}, u32[]{:S(2)}) collective-permute-start(f32[80,256]{1,0:T(8,128)S(1)} %reduce_sum.28), channel_id=1, source_target_pairs={{24,0},{28,4},{16,8},{20,12},{8,16},{12,20},{0,24},{4,28},{25,1},{... | collective-permute-start | bytes 245768 | tf_op jit(solution)/shard_map/ppermute | solution.py:49
  75.6 5.1 %collective-permute-start.12 = (f32[80,256]{1,0:T(8,128)S(1)}, f32[80,256]{1,0:T(8,128)S(1)}, u32[]{:S(2)}, u32[]{:S(2)}) collective-permute-start(f32[80,256]{1,0:T(8,128)S(1)} %reduce_sum.28), channel_id=1, source_target_pairs={{16,0},{20,4},{24,8},{28,12},{0,16},{4,20},{8,24},{12,28},{17,1},{... | collective-permute-start | bytes 245768 | tf_op jit(solution)/shard_map/ppermute | solution.py:49
  76.3 4.4 %collective-permute-start.11 = (f32[80,256]{1,0:T(8,128)S(1)}, f32[80,256]{1,0:T(8,128)S(1)}, u32[]{:S(2)}, u32[]{:S(2)}) collective-permute-start(f32[80,256]{1,0:T(8,128)S(1)} %reduce_sum.28), channel_id=1, source_target_pairs={{8,0},{12,4},{0,8},{4,12},{24,16},{28,20},{16,24},{20,28},{9,1},{1... | collective-permute-start | bytes 245768 | tf_op jit(solution)/shard_map/ppermute | solution.py:49
  80.8 1.7 %collective-permute-start.14 = (f32[4,80,256]{2,1,0:T(8,128)S(1)}, f32[4,80,256]{2,1,0:T(8,128)S(1)}, u32[]{:S(2)}, u32[]{:S(2)}) collective-permute-start(f32[4,80,256]{2,1,0:T(8,128)S(1)} %pad_maximum_fusion.1.refs_0_), channel_id=1, source_target_pairs={{4,0},{0,4},{12,8},{8,12},{20,16},{16,20},{28,24},{24,28},{5,1},{1... | collective-permute-start | bytes 983048 | tf_op jit(solution)/shard_map/ppermute | solution.py:49
  87.8 0.6 copy-start.3
  102.0 4.0 %collective-permute-start.16 = (f32[16,256]{1,0:T(8,128)S(1)}, f32[16,256]{1,0:T(8,128)S(1)}, u32[]{:S(2)}, u32[]{:S(2)}) collective-permute-start(f32[16,256]{1,0:T(8,128)S(1)} %get-tuple-element.11), channel_id=1, source_target_pairs={{16,0},{20,4},{24,8},{28,12},{0,16},{4,20},{8,24},{12,28},{17,1},{... | collective-permute-start | bytes 49160 | tf_op jit(solution)/shard_map/ppermute | solution.py:49
  103.1 3.7 %collective-permute-start.15 = (f32[16,256]{1,0:T(8,128)S(1)}, f32[16,256]{1,0:T(8,128)S(1)}, u32[]{:S(2)}, u32[]{:S(2)}) collective-permute-start(f32[16,256]{1,0:T(8,128)S(1)} %get-tuple-element.11), channel_id=1, source_target_pairs={{8,0},{12,4},{0,8},{4,12},{24,16},{28,20},{16,24},{20,28},{9,1},{1... | collective-permute-start | bytes 49160 | tf_op jit(solution)/shard_map/ppermute | solution.py:49
  103.8 4.6 %collective-permute-start.17 = (f32[16,256]{1,0:T(8,128)S(1)}, f32[16,256]{1,0:T(8,128)S(1)}, u32[]{:S(2)}, u32[]{:S(2)}) collective-permute-start(f32[16,256]{1,0:T(8,128)S(1)} %get-tuple-element.11), channel_id=1, source_target_pairs={{24,0},{28,4},{16,8},{20,12},{8,16},{12,20},{0,24},{4,28},{25,1},{... | collective-permute-start | bytes 49160 | tf_op jit(solution)/shard_map/ppermute | solution.py:49
  108.5 1.3 %copy-start.4 = (f32[4,16,256]{2,1,0:T(8,128)}, f32[4,16,256]{2,1,0:T(8,128)S(1)}, u32[]{:S(2)}) copy-start(f32[4,16,256]{2,1,0:T(8,128)S(1)} %pad_maximum_fusion.3.refs_0_) | copy-start | bytes 196612
  108.5 1.3 %collective-permute-start.18 = (f32[4,16,256]{2,1,0:T(8,128)S(1)}, f32[4,16,256]{2,1,0:T(8,128)S(1)}, u32[]{:S(2)}, u32[]{:S(2)}) collective-permute-start(f32[4,16,256]{2,1,0:T(8,128)S(1)} %pad_maximum_fusion.3.refs_0_), channel_id=1, source_target_pairs={{4,0},{0,4},{12,8},{8,12},{20,16},{16,20},{28,24},{24,28},{5,1},{1... | collective-permute-start | bytes 196616 | tf_op jit(solution)/shard_map/ppermute | solution.py:49
  109.8 0.6 copy-start.5

commit v3 on v2

--- a/solution.py
+++ b/solution.py
@@ -14,7 +14,7 @@
 BASE = 256.0
 EXACT_DEPTH = 1024
 DENSE_CELLS = 4
-VMEM_LIMIT = 48 * 1024 * 1024
+VMEM_LIMIT = 20 * 1024 * 1024
 
 
 def reduce_centered(values):
@@ -51,6 +51,15 @@
 
 def gather_pieces(piece, axis):
     return [piece] + [fetch(piece, axis, shift) for shift in range(1, lax.axis_size(axis))]
+
+
+def scatter_pieces(pieces, axis):
+    size = lax.axis_size(axis)
+    came = [
+        lax.ppermute(pieces[shift], axis, [(i, partner(i, shift, size)) for i in range(size)])
+        for shift in reversed(range(1, size))
+    ]
+    return [pieces[0]] + came
 
 
 def gather_in_pairs(piece, axis):
@@ -90,67 +99,80 @@
     return jnp.concatenate([packed[:, j * span : (j + 1) * span] for j in range(count)], 0)
 
 
-def build_kernel(group, positions_ref, entries_ref, dense_ref):
-    step = pl.program_id(0)
-    tile_len = entries_ref.shape[1]
-
-    @pl.when(step == 0)
-    def _():
-        def clear(block, carry):
-            dense_ref[block] = jnp.zeros(dense_ref.shape[1:], dense_ref.dtype)
-            return carry
-
-        lax.fori_loop(0, dense_ref.shape[0], clear, 0)
-
-    for index in range(group):
-        slot = step * group + index
-
-        @pl.when(slot < positions_ref[2, 0])
-        def _():
-            values = entries_ref[index]
-            values = jnp.where(values > HALF_MODULUS, values - MODULUS, values)
-            high, low = balanced_digits(values)
-            start = pl.multiple_of(positions_ref[1, slot] * tile_len, tile_len)
-            both = jnp.concatenate([high.T, low.T], 1).astype(jnp.bfloat16)
-            dense_ref[positions_ref[0, slot], pl.ds(start, tile_len), :] = both
-
-
-def build_dense(entries, positions, row_blocks, col_blocks):
-    slot_count, tile_len, _ = entries.shape
+def build_kernel(sizes, rows_ref, cols_ref, count_ref, entries_ref, dense_ref, held, sems):
+    n_row, n_col, piece_blocks, group = sizes
+    _, _, slot_count, tile_len, _ = entries_ref.shape
+    me_row, me_col = lax.axis_index("row"), lax.axis_index("col")
+
+    def chunk(index):
+        source = entries_ref.at[0, 0, pl.ds(index * group, group)]
+        return pltpu.make_async_copy(source, held.at[pl.ds(index * group, group)], sems.at[index])
+
+    chunk_count = slot_count // group
+    for index in range(chunk_count):
+        chunk(index).start()
+
+    def clear(block, carry):
+        dense_ref[block] = jnp.zeros(dense_ref.shape[1:], dense_ref.dtype)
+        return carry
+
+    lax.fori_loop(0, dense_ref.shape[0], clear, 0)
+
+    def place(slot):
+        row, col = rows_ref[0, 0, slot], cols_ref[0, 0, slot]
+        row_shift = shift_of(me_col, row // piece_blocks, n_col)
+        col_shift = shift_of(me_row, col // piece_blocks, n_row)
+        block = row_shift * piece_blocks + row % piece_blocks
+        start = (col_shift * piece_blocks + col % piece_blocks) * tile_len
+        values = jnp.where(slot < count_ref[0, 0], held[slot], 0.0)
+        values = jnp.where(values > HALF_MODULUS, values - MODULUS, values)
+        high, low = balanced_digits(values)
+        both = jnp.concatenate([high.T, low.T], 1).astype(jnp.bfloat16)
+        dense_ref[block, pl.ds(pl.multiple_of(start, tile_len), tile_len), :] = both
+
+    def step(index, carry):
+        chunk(index).wait()
+        for offset in range(group):
+            place(index * group + offset)
+        return carry
+
+    lax.fori_loop(0, chunk_count, step, 0)
+
+
+def build_dense(tile_entries, tile_rows, tile_cols, tile_count, sizes):
+    n_row, n_col, piece_blocks = sizes
+    _, _, slot_count, tile_len, _ = tile_entries.shape
     group = next(size for size in (8, 4, 2, 1) if slot_count % size == 0)
-    shape = (row_blocks, col_blocks * tile_len, 2 * tile_len)
+    shape = (n_col * piece_blocks, n_row * piece_blocks * tile_len, 2 * tile_len)
+    smem = pl.BlockSpec(memory_space=pltpu.SMEM)
     return pl.pallas_call(
-        functools.partial(build_kernel, group),
-        grid_spec=pltpu.PrefetchScalarGridSpec(
-            num_scalar_prefetch=1,
-            grid=(slot_count // group,),
-            in_specs=[pl.BlockSpec((group, tile_len, tile_len), lambda i, p: (i, 0, 0))],
-            out_specs=pl.BlockSpec(shape, lambda i, p: (0, 0, 0)),
-        ),
-        out_shape=jax.ShapeDtypeStruct(shape, jnp.bfloat16),
+        functools.partial(build_kernel, (*sizes, group)),
+        in_specs=[smem, smem, smem, pl.BlockSpec(memory_space=pltpu.HBM)],
+        out_specs=pl.BlockSpec(memory_space=pltpu.VMEM),
+        out_shape=pltpu.VMEM(shape, jnp.bfloat16),
+        scratch_shapes=[
+            pltpu.VMEM((slot_count, tile_len, tile_len), jnp.float32),
+            pltpu.SemaphoreType.DMA((slot_count // group,)),
+        ],
         compiler_params=pltpu.CompilerParams(vmem_limit_bytes=VMEM_LIMIT),
         cost_estimate=pl.CostEstimate(
-            flops=8 * entries.size, bytes_accessed=16 * entries.size, transcendentals=0
+            flops=8 * tile_entries.size, bytes_accessed=8 * tile_entries.size, transcendentals=0
         ),
-    )(positions, entries)
-
-
-def step_kernel(n_pairs, n_row, n_col, span, first, positions_ref, *refs):
+    )(tile_rows, tile_cols, tile_count, tile_entries)
+
+
+def step_kernel(n_pairs, n_row, n_col, span, first, *refs):
     pairs, refs = refs[:n_pairs], refs[n_pairs:]
     x_pieces, refs = refs[:n_col], refs[n_col:]
-    dense_ref, out_ref, refs = refs[0], refs[1], refs[2:]
+    dense_ref, refs = refs[0], refs[1:]
+    outs, refs = refs[:n_col], refs[n_col:]
     if not first:
         total_ref, refs = refs[0], refs[1:]
-    held, digits, sems = refs
+    digits = refs[0]
     row_blocks, depth, width = dense_ref.shape
     tile_len = width // 2
     piece_len = x_pieces[0].shape[1]
     piece_blocks = piece_len // tile_len
-    copies = [
-        pltpu.make_async_copy(dense_ref.at[b], held.at[b], sems.at[b]) for b in range(row_blocks)
-    ]
-    for copy in copies:
-        copy.start()
     for d in range(n_row):
         vector = reduce_centered(piece_at(pairs, d)[:span])
         digits[:, d * piece_len : (d + 1) * piece_len] = stacked_digits(vector)
@@ -159,17 +181,15 @@
         total_ref[...] = unpack_square(reduce_centered(packed), span)
     projected = None
     for e in range(n_col):
-        target = positions_ref[3, e]
         parts = []
         for sub in range(piece_blocks):
             block = e * piece_blocks + sub
-            copies[block].wait()
             high = middle = low = 0.0
             for start in range(0, depth, EXACT_DEPTH):
                 stop = min(start + EXACT_DEPTH, depth)
                 products = jnp.dot(
                     digits[:, start:stop],
-                    held[block, start:stop, :],
+                    dense_ref[block, start:stop, :],
                     preferred_element_type=jnp.float32,
                 )
                 products = reduce_centered(products)
@@ -178,7 +198,7 @@
                 low = low + products[span:, tile_len:]
             parts.append(reduce_centered(15.0 * high + 256.0 * reduce_centered(middle) + low))
         piece = jnp.concatenate(parts, 1)
-        out_ref[target, :span, :] = piece
+        outs[e][:span, :] = piece
         x_values = x_pieces[e][...]
         x_values = jnp.where(x_values > HALF_MODULUS, x_values - MODULUS, x_values)
         products = dot_pairs(stacked_digits(x_values), stacked_digits(piece))
@@ -186,37 +206,31 @@
             products = reduce_centered(products)
         projected = products if projected is None else projected + products
     packed = pack_square(projection_residues(projected, span), piece_len)
-    for e in range(n_col):
-        out_ref[e, span:, :] = packed
-
-
-def dense_step(pairs, x_pieces, positions, dense, first):
+    for out in outs:
+        out[span:, :] = packed
+
+
+def dense_step(pairs, x_pieces, dense, first):
     n_row, n_col = len(pairs) * pairs[0].shape[0], len(x_pieces)
     span, piece_len = x_pieces[0].shape
     row_blocks, depth, width = dense.shape
     rows = span + span * span // piece_len
-    outs = [jax.ShapeDtypeStruct((n_col, rows, piece_len), jnp.float32)]
+    outs = [pltpu.VMEM((rows, piece_len), jnp.float32)] * n_col
     if not first:
         outs = outs + [jax.ShapeDtypeStruct((span, span), jnp.float32)]
     vmem = pl.BlockSpec(memory_space=pltpu.VMEM)
     results = pl.pallas_call(
         functools.partial(step_kernel, len(pairs), n_row, n_col, span, first),
-        in_specs=[pl.BlockSpec(memory_space=pltpu.SMEM)]
-        + [vmem] * (len(pairs) + n_col)
-        + [pl.BlockSpec(memory_space=pl.ANY)],
+        in_specs=[vmem] * (len(pairs) + n_col + 1),
         out_specs=[vmem] * len(outs),
         out_shape=outs,
-        scratch_shapes=[
-            pltpu.VMEM(dense.shape, dense.dtype),
-            pltpu.VMEM((2 * span, depth), jnp.bfloat16),
-            pltpu.SemaphoreType.DMA((row_blocks,)),
-        ],
+        scratch_shapes=[pltpu.VMEM((2 * span, depth), jnp.bfloat16)],
         compiler_params=pltpu.CompilerParams(vmem_limit_bytes=VMEM_LIMIT),
         cost_estimate=pl.CostEstimate(
             flops=4 * span * dense.size, bytes_accessed=2 * dense.size, transcendentals=0
         ),
-    )(positions, *pairs, *x_pieces, dense)
-    return results[0], (None if first else results[1])
+    )(*(pltpu.with_memory_space_constraint(part, pltpu.VMEM) for part in (*pairs, *x_pieces, dense)))
+    return list(results[:n_col]), (None if first else results[n_col])
 
 
 def sparse_step(pairs, x_pieces, positions, a_digits, first):
@@ -239,7 +253,7 @@
         + 256.0 * reduce_centered(products[:, 0, span:] + products[:, 1, :span])
         + products[:, 1, span:]
     )
-    live = jnp.arange(slot_count, dtype=jnp.int32) < positions[2, 0]
+    live = jnp.arange(slot_count, dtype=jnp.int32) < positions[2]
     onehot = positions[0][None, :] == jnp.arange(row_blocks, dtype=jnp.int32)[:, None]
     onehot = (onehot & live[None, :]).astype(jnp.float32)
     summed = jnp.einsum("bt,twi->wbi", onehot, residues, precision=lax.Precision.HIGHEST)
@@ -251,8 +265,7 @@
         products = dot_pairs(stacked_digits(x_values), stacked_digits(outs[:, e]))
         projected = projected + reduce_centered(products)
     packed = pack_square(projection_residues(projected, span), piece_len)
-    outs = jnp.stack([jnp.concatenate([outs[:, e], packed], 0) for e in range(n_col)])
-    return jnp.zeros_like(outs).at[positions[3, :n_col]].set(outs), total
+    return [jnp.concatenate([outs[:, e], packed], 0) for e in range(n_col)], total
 
 
 def multiply_mod(left, right):
@@ -291,38 +304,39 @@
     )(c_1, c_2, *c_3_pairs)
 
 
+def sparse_tiles(tile_entries, tile_rows, tile_cols, tile_count, sizes):
+    n_row, n_col, piece_blocks = sizes
+    entries, rows, cols = tile_entries[0, 0], tile_rows[0, 0], tile_cols[0, 0]
+    row_shift = shift_of(lax.axis_index("col"), rows // piece_blocks, n_col)
+    col_shift = shift_of(lax.axis_index("row"), cols // piece_blocks, n_row)
+    positions = [
+        row_shift * piece_blocks + rows % piece_blocks,
+        col_shift * piece_blocks + cols % piece_blocks,
+        tile_count[0, 0],
+    ]
+    entries = jnp.where(entries > HALF_MODULUS, entries - MODULUS, entries)
+    return jnp.stack(balanced_digits(entries), 1).astype(jnp.bfloat16), positions
+
+
 def local(tile_entries, tile_rows, tile_cols, tile_count, block_x, block_y):
-    entries = tile_entries[0, 0]
-    slot_count, tile_len, _ = entries.shape
+    _, _, slot_count, tile_len, _ = tile_entries.shape
     span, piece_len = block_y.shape
     piece_blocks = piece_len // tile_len
     n_row, n_col = lax.axis_size("row"), lax.axis_size("col")
-    row_blocks, col_blocks = n_col * piece_blocks, n_row * piece_blocks
-    rows_here, cols_here = tile_rows[0, 0], tile_cols[0, 0]
-    row_shift = shift_of(lax.axis_index("col"), rows_here // piece_blocks, n_col)
-    col_shift = shift_of(lax.axis_index("row"), cols_here // piece_blocks, n_row)
-    positions = jnp.stack(
-        [
-            row_shift * piece_blocks + rows_here % piece_blocks,
-            col_shift * piece_blocks + cols_here % piece_blocks,
-            jnp.full((slot_count,), tile_count[0, 0], jnp.int32),
-            partner(lax.axis_index("col"), jnp.arange(slot_count, dtype=jnp.int32) % n_col, n_col),
-        ]
-    )
+    tiles = (tile_entries, tile_rows, tile_cols, tile_count)
+    sizes = (n_row, n_col, piece_blocks)
     pairs = gather_in_pairs(block_y, "row")
     x_pieces = gather_pieces(block_x, "col")
-    if row_blocks * col_blocks <= DENSE_CELLS * slot_count:
-        dense = build_dense(entries, positions, row_blocks, col_blocks)
-        multiply = functools.partial(dense_step, positions=positions, dense=dense)
+    if n_col * piece_blocks * n_row * piece_blocks <= DENSE_CELLS * slot_count:
+        multiply = functools.partial(dense_step, dense=build_dense(*tiles, sizes))
     else:
-        centred = jnp.where(entries > HALF_MODULUS, entries - MODULUS, entries)
-        a_digits = jnp.stack(balanced_digits(centred), 1).astype(jnp.bfloat16)
+        a_digits, positions = sparse_tiles(*tiles, sizes)
         multiply = functools.partial(sparse_step, positions=positions, a_digits=a_digits)
     totals = []
     for step_index in range(STEP_COUNT):
         outs, total = multiply(pairs, x_pieces, first=step_index == 0)
         totals.append(total)
-        summed = jnp.sum(lax.all_to_all(outs, "col", 0, 0), 0)
+        summed = functools.reduce(jnp.add, scatter_pieces(outs, "col"))
         if step_index < STEP_COUNT - 1:
             pairs = gather_in_pairs(summed, "row")
     thirds = gather_in_pairs(summed[span:], "row")

time: 113 us -> 88.9 us (0.79)
  blocking collectives: 42.6 us -> 0 us
  waiting for transfers between devices: 14 us -> 35.5 us
  Pallas kernels: 24.1 us -> 12.7 us
  starting transfers between devices: 23.4 us -> 33.3 us
  other arithmetic: 3.04 us -> 1.63 us
    all_to_all x3 -> x0, blocking collectives: 42.6 us -> none  [local(): summed = jnp.sum(lax.all_to_all(outs, 'col', 0, 0), 0)]
    ppermute x0 -> x9, waiting for transfers between devices: none -> 16.9 us  [scatter_pieces(): lax.ppermute(pieces[shift], axis, [(i, partner(i, shift, size)) for i in...]
    ppermute x0 -> x9, starting transfers between devices: none -> 13.3 us  [scatter_pieces(): lax.ppermute(pieces[shift], axis, [(i, partner(i, shift, size)) for i in...]
    pallas_call x3, Pallas kernels: 15.9 us -> 6.72 us  [dense_step(): pl.pallas_call(functools.partial(step_kernel, len(pairs), n_row, n_col, s...]
    ppermute x19, waiting for transfers between devices: 14 us -> 18.5 us  [fetch(): lax.ppermute(piece, axis, [(partner(i, shift, size), i) for i in range(si...]
    ppermute x19, starting transfers between devices: 23.4 us -> 19.9 us  [fetch(): lax.ppermute(piece, axis, [(partner(i, shift, size), i) for i in range(si...]
    pallas_call x1, Pallas kernels: 5.92 us -> 3.7 us  [build_dense(): pl.pallas_call(functools.partial(build_kernel, (*sizes, group)), in_specs...]
    add x2 -> x3, other arithmetic: 1.34 us -> 0.06 us  [local(): summed = functools.reduce(jnp.add, scatter_pieces(outs, 'col'))]
  transfers between devices with their start and end apart: 19 -> 28, of which waited for: 10 -> 20; matrix products, arithmetic and copies ran while one was open for 3% -> 1% of each run, Pallas kernels for 5% -> 4%
where the time goes in v3:
time: 88.9 us; the launch traced here: 88.7 us
  waiting for transfers between devices  35.5 us (40%)
  starting transfers between devices  33.3 us (37%)
  Pallas kernels  12.7 us (14%)
  local copies, waits for them, and re-layouts  4.13 us (5%)
  other arithmetic  1.63 us (2%)
  between operations  1.47 us (2%)
    ppermute x19, starting transfers between devices, fetch(): lax.ppermute(piece, axis, [(partner(i, shift, size), i) for i in range(si...  19.9 us
    ppermute x19, waiting for transfers between devices, fetch(): lax.ppermute(piece, axis, [(partner(i, shift, size), i) for i in range(si...  18.5 us
    ppermute x9, waiting for transfers between devices, scatter_pieces(): lax.ppermute(pieces[shift], axis, [(i, partner(i, shift, size)) for i in...  16.9 us
    ppermute x9, starting transfers between devices, scatter_pieces(): lax.ppermute(pieces[shift], axis, [(i, partner(i, shift, size)) for i in...  13.3 us
    pallas_call x3, Pallas kernels, dense_step(): pl.pallas_call(functools.partial(step_kernel, len(pairs), n_row, n_col, s...  6.72 us
    unnamed x16, local copies, waits for them, and re-layouts  4.12 us
    pallas_call x1, Pallas kernels, build_dense(): pl.pallas_call(functools.partial(build_kernel, (*sizes, group)), in_specs...  3.7 us
    pallas_call x1, Pallas kernels, sigma_update(): pl.pallas_call(functools.partial(sigma_kernel, len(c_3_pairs)), out_shape...  2.28 us
  transfers between devices with their start and end apart: 28, of which 20 were waited for; matrix products, arithmetic and copies ran while one was open for 1% of the time, Pallas kernels for 4%

profile of v3, /device:TPU:0, one launch (start us, length us, event | category | flops | bytes accessed | tf_op | source)
XLA Modules:
  0.0 88.7 jit_solution(14620326375107128533)
XLA Ops:
  0.6 3.0 %collective-permute-start = (f32[64,256]{1,0:T(8,128)}, f32[64,256]{1,0:T(8,128)S(1)}, u32[]{:S(2)}, u32[]{:S(2)}) collective-permute-start(f32[64,256]{1,0:T(8,128)} %param.11), channel_id=1, source_target_pairs={{8,0},{12,4},{0,8},{4,12},{24,16},{28,20},{16,24},{20,28},{9,1},{1... | collective-permute-start | bytes 196616 | tf_op jit(solution)/shard_map/ppermute | solution.py:49
  3.6 1.5 %collective-permute-start.2 = (f32[64,256]{1,0:T(8,128)}, f32[64,256]{1,0:T(8,128)S(1)}, u32[]{:S(2)}, u32[]{:S(2)}) collective-permute-start(f32[64,256]{1,0:T(8,128)} %param.11), channel_id=1, source_target_pairs={{24,0},{28,4},{16,8},{20,12},{8,16},{12,20},{0,24},{4,28},{25,1},{... | collective-permute-start | bytes 196616 | tf_op jit(solution)/shard_map/ppermute | solution.py:49
  5.2 1.2 %collective-permute-done = f32[64,256]{1,0:T(8,128)S(1)} collective-permute-done((f32[64,256]{1,0:T(8,128)}, f32[64,256]{1,0:T(8,128)S(1)}, u32[]{:S(2)}, u32[]{:S(2)}) %collective-permute-start) | collective-permute-done | bytes 65568 | tf_op jit(solution)/shard_map/ppermute | solution.py:49
  6.4 2.7 %collective-permute-done.2 = f32[64,256]{1,0:T(8,128)S(1)} collective-permute-done((f32[64,256]{1,0:T(8,128)}, f32[64,256]{1,0:T(8,128)S(1)}, u32[]{:S(2)}, u32[]{:S(2)}) %collective-permute-start.2) | collective-permute-done | bytes 65568 | tf_op jit(solution)/shard_map/ppermute | solution.py:49
  9.1 0.8 collective-permute-done.1
  9.9 0.9 pad_maximum_fusion.2.refs_0_
  10.8 3.7 %collective-permute-start.6 = (f32[64,256]{1,0:T(8,128)}, f32[64,256]{1,0:T(8,128)S(1)}, u32[]{:S(2)}, u32[]{:S(2)}) collective-permute-start(f32[64,256]{1,0:T(8,128)} %refs_2_.5), channel_id=1, source_target_pairs={{3,0},{2,1},{1,2},{0,3},{7,4},{6,5},{5,6},{4,7},{11,8},{10,9},{9,1... | collective-permute-start | bytes 196616 | tf_op jit(solution)/shard_map/ppermute | solution.py:49
  14.5 0.8 collective-permute-start.4
  15.9 2.2 %copy-done = f32[1,1,64,128,128]{4,3,2,1,0:T(8,128)S(1)} copy-done((f32[1,1,64,128,128]{4,3,2,1,0:T(8,128)S(1)}, f32[1,1,64,128,128]{4,3,2,1,0:T(8,128)}, u32[]{:S(2)}) %copy-start) | copy-done | bytes 4194328
  18.1 0.7 copy-done.4
  18.8 0.7 copy-done.5
  19.4 3.7 %shard_map.77.refs_6_ = bf16[8,2048,256]{2,1,0:T(8,128)(2,1)S(1)} custom-call(s32[1,1,64]{2,1,0:T(1,128)S(1)} %copy-done.4, s32[1,1,64]{2,1,0:T(1,128)S(1)} %copy-done.5, s32[1,1]{1,0:T(1,128)S(6)} %copy.8.count_ref, f32[1,1,64,128,128]{4,3,2,1,0:T(8,128)S(1)} %copy-done), custom_call_target="tpu_custom_call" | custom-call | flops 8388608 | bytes 8388608 | tf_op jit(solution)/shard_map/pallas_call | solution.py:148
  23.2 2.2 %shard_map.78 = (f32[80,256]{1,0:T(8,128)S(1)}, f32[80,256]{1,0:T(8,128)S(1)}, f32[80,256]{1,0:T(8,128)S(1)}, f32[80,256]{1,0:T(8,128)S(1)}) custom-call(f32[4,64,256]{2,1,0:T(8,128)S(1)} %pad_maximum_fusion.2.refs_0_, f32[4,64,256]{2,1,0:T(8,128)S(1)} %collective-permute-done.3.refs_1_, f32[64,256]{1,0:T(8,128)S(1)} %copy-done.1, ...), custom_call_target="tpu_custom_call" | custom-call | flops 1073741824 | bytes 8388608 | tf_op jit(solution)/shard_map/pallas_call | solution.py:222
  25.4 3.6 %collective-permute-start.7 = (f32[80,256]{1,0:T(8,128)S(1)}, f32[80,256]{1,0:T(8,128)S(1)}, u32[]{:S(2)}, u32[]{:S(2)}) collective-permute-start(f32[80,256]{1,0:T(8,128)S(1)} %get-tuple-element.17), channel_id=1, source_target_pairs={{0,3},{1,2},{2,1},{3,0},{4,7},{5,6},{6,5},{7,4},{8,11},{9,10},{10,... | collective-permute-start | bytes 245768 | tf_op jit(solution)/shard_map/ppermute | solution.py:59
  29.1 0.8 collective-permute-start.9
  29.8 2.8 %collective-permute-done.7 = f32[80,256]{1,0:T(8,128)S(1)} collective-permute-done((f32[80,256]{1,0:T(8,128)S(1)}, f32[80,256]{1,0:T(8,128)S(1)}, u32[]{:S(2)}, u32[]{:S(2)}) %collective-permute-start.7) | collective-permute-done | bytes 81952 | tf_op jit(solution)/shard_map/ppermute | solution.py:59
  32.6 3.0 %collective-permute-done.8 = f32[80,256]{1,0:T(8,128)S(1)} collective-permute-done((f32[80,256]{1,0:T(8,128)S(1)}, f32[80,256]{1,0:T(8,128)S(1)}, u32[]{:S(2)}, u32[]{:S(2)}) %collective-permute-start.8) | collective-permute-done | bytes 81952 | tf_op jit(solution)/shard_map/ppermute | solution.py:59
  35.7 1.5 %collective-permute-start.12 = (f32[80,256]{1,0:T(8,128)S(1)}, f32[80,256]{1,0:T(8,128)S(1)}, u32[]{:S(2)}, u32[]{:S(2)}) collective-permute-start(f32[80,256]{1,0:T(8,128)S(1)} %add_add_fusion.2), channel_id=1, source_target_pairs={{24,0},{28,4},{16,8},{20,12},{8,16},{12,20},{0,24},{4,28},{25,1},{... | collective-permute-start | bytes 245768 | tf_op jit(solution)/shard_map/ppermute | solution.py:49
  37.2 1.2 %collective-permute-start.11 = (f32[80,256]{1,0:T(8,128)S(1)}, f32[80,256]{1,0:T(8,128)S(1)}, u32[]{:S(2)}, u32[]{:S(2)}) collective-permute-start(f32[80,256]{1,0:T(8,128)S(1)} %add_add_fusion.2), channel_id=1, source_target_pairs={{16,0},{20,4},{24,8},{28,12},{0,16},{4,20},{8,24},{12,28},{17,1},{... | collective-permute-start | bytes 245768 | tf_op jit(solution)/shard_map/ppermute | solution.py:49
  38.5 0.8 collective-permute-start.10
  39.2 2.6 %collective-permute-done.12 = f32[80,256]{1,0:T(8,128)S(1)} collective-permute-done((f32[80,256]{1,0:T(8,128)S(1)}, f32[80,256]{1,0:T(8,128)S(1)}, u32[]{:S(2)}, u32[]{:S(2)}) %collective-permute-start.12) | collective-permute-done | bytes 81952 | tf_op jit(solution)/shard_map/ppermute | solution.py:49
  41.8 0.6 collective-permute-done.11
  43.0 1.6 %collective-permute-done.13.refs_1_ = f32[4,80,256]{2,1,0:T(8,128)S(1)} collective-permute-done((f32[4,80,256]{2,1,0:T(8,128)S(1)}, f32[4,80,256]{2,1,0:T(8,128)S(1)}, u32[]{:S(2)}, u32[]{:S(2)}) %collective-permute-start.13) | collective-permute-done | bytes 327712 | tf_op jit(solution)/shard_map/ppermute | solution.py:49
  44.6 2.2 %shard_map.79 = (f32[80,256]{1,0:T(8,128)S(1)}, f32[80,256]{1,0:T(8,128)S(1)}, f32[80,256]{1,0:T(8,128)S(1)}, f32[80,256]{1,0:T(8,128)S(1)}, f32[64,64]{1,0:T(8,128)S(1)}) custom-call(f32[4,80,256]{2,1,0:T(8,128)S(1)} %pad_maximum_fusion.refs_0_, f32[4,80,256]{2,1,0:T(8,128)S(1)} %collective-permute-done.13.refs_1_, f32[64,256]{1,0:T(8,128)S(1)} %copy-done.1, ...), custom_call_target="tpu_custom_call" | custom-call | flops 1073741824 | bytes 8388608 | tf_op jit(solution)/shard_map/pallas_call | solution.py:222
  46.9 2.6 %collective-permute-start.14 = (f32[80,256]{1,0:T(8,128)S(1)}, f32[80,256]{1,0:T(8,128)S(1)}, u32[]{:S(2)}, u32[]{:S(2)}) collective-permute-start(f32[80,256]{1,0:T(8,128)S(1)} %get-tuple-element.22), channel_id=1, source_target_pairs={{0,3},{1,2},{2,1},{3,0},{4,7},{5,6},{6,5},{7,4},{8,11},{9,10},{10,... | collective-permute-start | bytes 245768 | tf_op jit(solution)/shard_map/ppermute | solution.py:59
  49.5 1.8 %collective-permute-start.16 = (f32[80,256]{1,0:T(8,128)S(1)}, f32[80,256]{1,0:T(8,128)S(1)}, u32[]{:S(2)}, u32[]{:S(2)}) collective-permute-start(f32[80,256]{1,0:T(8,128)S(1)} %get-tuple-element.24), channel_id=1, source_target_pairs={{0,1},{1,0},{2,3},{3,2},{4,5},{5,4},{6,7},{7,6},{8,9},{9,8},{10,11... | collective-permute-start | bytes 245768 | tf_op jit(solution)/shard_map/ppermute | solution.py:59
  51.3 2.8 %collective-permute-done.14 = f32[80,256]{1,0:T(8,128)S(1)} collective-permute-done((f32[80,256]{1,0:T(8,128)S(1)}, f32[80,256]{1,0:T(8,128)S(1)}, u32[]{:S(2)}, u32[]{:S(2)}) %collective-permute-start.14) | collective-permute-done | bytes 81952 | tf_op jit(solution)/shard_map/ppermute | solution.py:59
  54.1 2.9 %collective-permute-done.15 = f32[80,256]{1,0:T(8,128)S(1)} collective-permute-done((f32[80,256]{1,0:T(8,128)S(1)}, f32[80,256]{1,0:T(8,128)S(1)}, u32[]{:S(2)}, u32[]{:S(2)}) %collective-permute-start.15) | collective-permute-done | bytes 81952 | tf_op jit(solution)/shard_map/ppermute | solution.py:59
  57.1 1.2 %collective-permute-start.19 = (f32[80,256]{1,0:T(8,128)S(1)}, f32[80,256]{1,0:T(8,128)S(1)}, u32[]{:S(2)}, u32[]{:S(2)}) collective-permute-start(f32[80,256]{1,0:T(8,128)S(1)} %add_add_fusion.1), channel_id=1, source_target_pairs={{24,0},{28,4},{16,8},{20,12},{8,16},{12,20},{0,24},{4,28},{25,1},{... | collective-permute-start | bytes 245768 | tf_op jit(solution)/shard_map/ppermute | solution.py:49
  58.3 1.1 %collective-permute-start.18 = (f32[80,256]{1,0:T(8,128)S(1)}, f32[80,256]{1,0:T(8,128)S(1)}, u32[]{:S(2)}, u32[]{:S(2)}) collective-permute-start(f32[80,256]{1,0:T(8,128)S(1)} %add_add_fusion.1), channel_id=1, source_target_pairs={{16,0},{20,4},{24,8},{28,12},{0,16},{4,20},{8,24},{12,28},{17,1},{... | collective-permute-start | bytes 245768 | tf_op jit(solution)/shard_map/ppermute | solution.py:49
  59.4 1.2 %collective-permute-start.17 = (f32[80,256]{1,0:T(8,128)S(1)}, f32[80,256]{1,0:T(8,128)S(1)}, u32[]{:S(2)}, u32[]{:S(2)}) collective-permute-start(f32[80,256]{1,0:T(8,128)S(1)} %add_add_fusion.1), channel_id=1, source_target_pairs={{8,0},{12,4},{0,8},{4,12},{24,16},{28,20},{16,24},{20,28},{9,1},{1... | collective-permute-start | bytes 245768 | tf_op jit(solution)/shard_map/ppermute | solution.py:49
  60.6 2.5 %collective-permute-done.19 = f32[80,256]{1,0:T(8,128)S(1)} collective-permute-done((f32[80,256]{1,0:T(8,128)S(1)}, f32[80,256]{1,0:T(8,128)S(1)}, u32[]{:S(2)}, u32[]{:S(2)}) %collective-permute-start.19) | collective-permute-done | bytes 81952 | tf_op jit(solution)/shard_map/ppermute | solution.py:49
  63.1 1.0 %collective-permute-done.18 = f32[80,256]{1,0:T(8,128)S(1)} collective-permute-done((f32[80,256]{1,0:T(8,128)S(1)}, f32[80,256]{1,0:T(8,128)S(1)}, u32[]{:S(2)}, u32[]{:S(2)}) %collective-permute-start.18) | collective-permute-done | bytes 81952 | tf_op jit(solution)/shard_map/ppermute | solution.py:49
  64.2 1.6 %collective-permute-done.20.refs_1_ = f32[4,80,256]{2,1,0:T(8,128)S(1)} collective-permute-done((f32[4,80,256]{2,1,0:T(8,128)S(1)}, f32[4,80,256]{2,1,0:T(8,128)S(1)}, u32[]{:S(2)}, u32[]{:S(2)}) %collective-permute-start.20) | collective-permute-done | bytes 327712 | tf_op jit(solution)/shard_map/ppermute | solution.py:49
  65.8 2.2 %shard_map.80 = (f32[80,256]{1,0:T(8,128)S(1)}, f32[80,256]{1,0:T(8,128)S(1)}, f32[80,256]{1,0:T(8,128)S(1)}, f32[80,256]{1,0:T(8,128)S(1)}, f32[64,64]{1,0:T(8,128)S(1)}) custom-call(f32[4,80,256]{2,1,0:T(8,128)S(1)} %pad_maximum_fusion.1.refs_0_, f32[4,80,256]{2,1,0:T(8,128)S(1)} %collective-permute-done.20.refs_1_, f32[64,256]{1,0:T(8,128)S(1)} %copy-done.1, ...), custom_call_target="tpu_custom_call" | custom-call | flops 1073741824 | bytes 8388608 | tf_op jit(solution)/shard_map/pallas_call | solution.py:222
  68.1 2.4 %collective-permute-start.21 = (f32[80,256]{1,0:T(8,128)S(1)}, f32[80,256]{1,0:T(8,128)S(1)}, u32[]{:S(2)}, u32[]{:S(2)}) collective-permute-start(f32[80,256]{1,0:T(8,128)S(1)} %get-tuple-element.27), channel_id=1, source_target_pairs={{0,3},{1,2},{2,1},{3,0},{4,7},{5,6},{6,5},{7,4},{8,11},{9,10},{10,... | collective-permute-start | bytes 245768 | tf_op jit(solution)/shard_map/ppermute | solution.py:59
  70.4 2.1 %collective-permute-start.23 = (f32[80,256]{1,0:T(8,128)S(1)}, f32[80,256]{1,0:T(8,128)S(1)}, u32[]{:S(2)}, u32[]{:S(2)}) collective-permute-start(f32[80,256]{1,0:T(8,128)S(1)} %get-tuple-element.29), channel_id=1, source_target_pairs={{0,1},{1,0},{2,3},{3,2},{4,5},{5,4},{6,7},{7,6},{8,9},{9,8},{10,11... | collective-permute-start | bytes 245768 | tf_op jit(solution)/shard_map/ppermute | solution.py:59
  72.5 2.8 %collective-permute-done.21 = f32[80,256]{1,0:T(8,128)S(1)} collective-permute-done((f32[80,256]{1,0:T(8,128)S(1)}, f32[80,256]{1,0:T(8,128)S(1)}, u32[]{:S(2)}, u32[]{:S(2)}) %collective-permute-start.21) | collective-permute-done | bytes 81952 | tf_op jit(solution)/shard_map/ppermute | solution.py:59
  75.3 2.6 %collective-permute-done.22 = f32[80,256]{1,0:T(8,128)S(1)} collective-permute-done((f32[80,256]{1,0:T(8,128)S(1)}, f32[80,256]{1,0:T(8,128)S(1)}, u32[]{:S(2)}, u32[]{:S(2)}) %collective-permute-start.22) | collective-permute-done | bytes 81952 | tf_op jit(solution)/shard_map/ppermute | solution.py:59
  78.0 0.9 collective-permute-start.25
  78.8 0.9 %collective-permute-start.24 = (f32[16,256]{1,0:T(8,128)S(1)}, f32[16,256]{1,0:T(8,128)S(1)}, u32[]{:S(2)}, u32[]{:S(2)}) collective-permute-start(f32[16,256]{1,0:T(8,128)S(1)} %get-tuple-element.31), channel_id=1, source_target_pairs={{8,0},{12,4},{0,8},{4,12},{24,16},{28,20},{16,24},{20,28},{9,1},{1... | collective-permute-start | bytes 49160 | tf_op jit(solution)/shard_map/ppermute | solution.py:49
  79.8 1.7 %collective-permute-start.26 = (f32[16,256]{1,0:T(8,128)S(1)}, f32[16,256]{1,0:T(8,128)S(1)}, u32[]{:S(2)}, u32[]{:S(2)}) collective-permute-start(f32[16,256]{1,0:T(8,128)S(1)} %get-tuple-element.31), channel_id=1, source_target_pairs={{24,0},{28,4},{16,8},{20,12},{8,16},{12,20},{0,24},{4,28},{25,1},{... | collective-permute-start | bytes 49160 | tf_op jit(solution)/shard_map/ppermute | solution.py:49
  81.8 0.9 collective-permute-done.24
  82.7 1.8 %collective-permute-done.26 = f32[16,256]{1,0:T(8,128)S(1)} collective-permute-done((f32[16,256]{1,0:T(8,128)S(1)}, f32[16,256]{1,0:T(8,128)S(1)}, u32[]{:S(2)}, u32[]{:S(2)}) %collective-permute-start.26) | collective-permute-done | bytes 16416 | tf_op jit(solution)/shard_map/ppermute | solution.py:49
  84.5 0.7 fusion
  85.2 0.6 collective-permute-done.27.refs_1_
  85.8 0.6 copy-done.7
  86.4 2.3 %shard_map.81 = f32[3,64,64]{2,1,0:T(8,128)} custom-call(f32[64,64]{1,0:T(8,128)} %copy-done.2, f32[64,64]{1,0:T(8,128)} %copy-done.3, f32[4,16,256]{2,1,0:T(8,128)} %copy-done.6, f32[4,16,256]{2,1,0:T(8,128)} %copy-done.7), custom_call_target="tpu_custom_call" | custom-call | tf_op jit(solution)/shard_map/pallas_call | solution.py:301
  (38 shorter events, 1.2 us)
Async XLA Ops:
  0.6 22.5 %copy-start.1 = (f32[64,256]{1,0:T(8,128)S(1)}, f32[64,256]{1,0:T(8,128)}, u32[]{:S(2)}) copy-start(f32[64,256]{1,0:T(8,128)} %refs_2_.5) | copy-start | bytes 196612
  0.6 5.7 %collective-permute-start = (f32[64,256]{1,0:T(8,128)}, f32[64,256]{1,0:T(8,128)S(1)}, u32[]{:S(2)}, u32[]{:S(2)}) collective-permute-start(f32[64,256]{1,0:T(8,128)} %param.11), channel_id=1, source_target_pairs={{8,0},{12,4},{0,8},{4,12},{24,16},{28,20},{16,24},{20,28},{9,1},{1... | collective-permute-start | bytes 196616 | tf_op jit(solution)/shard_map/ppermute | solution.py:49
  3.6 5.4 %collective-permute-start.2 = (f32[64,256]{1,0:T(8,128)}, f32[64,256]{1,0:T(8,128)S(1)}, u32[]{:S(2)}, u32[]{:S(2)}) collective-permute-start(f32[64,256]{1,0:T(8,128)} %param.11), channel_id=1, source_target_pairs={{24,0},{28,4},{16,8},{20,12},{8,16},{12,20},{0,24},{4,28},{25,1},{... | collective-permute-start | bytes 196616 | tf_op jit(solution)/shard_map/ppermute | solution.py:49
  5.1 4.7 %collective-permute-start.1 = (f32[64,256]{1,0:T(8,128)}, f32[64,256]{1,0:T(8,128)S(1)}, u32[]{:S(2)}, u32[]{:S(2)}) collective-permute-start(f32[64,256]{1,0:T(8,128)} %param.11), channel_id=1, source_target_pairs={{16,0},{20,4},{24,8},{28,12},{0,16},{4,20},{8,24},{12,28},{17,1},{... | collective-permute-start | bytes 196616 | tf_op jit(solution)/shard_map/ppermute | solution.py:49
  10.7 12.4 %collective-permute-start.3 = (f32[4,64,256]{2,1,0:T(8,128)S(1)}, f32[4,64,256]{2,1,0:T(8,128)S(1)}, u32[]{:S(2)}, u32[]{:S(2)}) collective-permute-start(f32[4,64,256]{2,1,0:T(8,128)S(1)} %pad_maximum_fusion.2.refs_0_), channel_id=1, source_target_pairs={{4,0},{0,4},{12,8},{8,12},{20,16},{16,20},{28,24},{24,28},{5,1},{1... | collective-permute-start | bytes 786440 | tf_op jit(solution)/shard_map/ppermute | solution.py:49
  10.8 12.3 %collective-permute-start.6 = (f32[64,256]{1,0:T(8,128)}, f32[64,256]{1,0:T(8,128)S(1)}, u32[]{:S(2)}, u32[]{:S(2)}) collective-permute-start(f32[64,256]{1,0:T(8,128)} %refs_2_.5), channel_id=1, source_target_pairs={{3,0},{2,1},{1,2},{0,3},{7,4},{6,5},{5,6},{4,7},{11,8},{10,9},{9,1... | collective-permute-start | bytes 196616 | tf_op jit(solution)/shard_map/ppermute | solution.py:49
  14.5 8.7 %collective-permute-start.5 = (f32[64,256]{1,0:T(8,128)}, f32[64,256]{1,0:T(8,128)S(1)}, u32[]{:S(2)}, u32[]{:S(2)}) collective-permute-start(f32[64,256]{1,0:T(8,128)} %refs_2_.5), channel_id=1, source_target_pairs={{2,0},{3,1},{0,2},{1,3},{6,4},{7,5},{4,6},{5,7},{10,8},{11,9},{8,1... | collective-permute-start | bytes 196616 | tf_op jit(solution)/shard_map/ppermute | solution.py:49
  14.5 8.7 %collective-permute-start.4 = (f32[64,256]{1,0:T(8,128)}, f32[64,256]{1,0:T(8,128)S(1)}, u32[]{:S(2)}, u32[]{:S(2)}) collective-permute-start(f32[64,256]{1,0:T(8,128)} %refs_2_.5), channel_id=1, source_target_pairs={{1,0},{0,1},{3,2},{2,3},{5,4},{4,5},{7,6},{6,7},{9,8},{8,9},{11,10... | collective-permute-start | bytes 196616 | tf_op jit(solution)/shard_map/ppermute | solution.py:49
  15.9 2.2 %copy-start = (f32[1,1,64,128,128]{4,3,2,1,0:T(8,128)S(1)}, f32[1,1,64,128,128]{4,3,2,1,0:T(8,128)}, u32[]{:S(2)}) copy-start(f32[1,1,64,128,128]{4,3,2,1,0:T(8,128)} %entries_ref.1) | copy-start | bytes 12582916
  18.1 0.7 copy-start.4
  18.8 0.7 copy-start.5
  25.4 7.2 %collective-permute-start.7 = (f32[80,256]{1,0:T(8,128)S(1)}, f32[80,256]{1,0:T(8,128)S(1)}, u32[]{:S(2)}, u32[]{:S(2)}) collective-permute-start(f32[80,256]{1,0:T(8,128)S(1)} %get-tuple-element.17), channel_id=1, source_target_pairs={{0,3},{1,2},{2,1},{3,0},{4,7},{5,6},{6,5},{7,4},{8,11},{9,10},{10,... | collective-permute-start | bytes 245768 | tf_op jit(solution)/shard_map/ppermute | solution.py:59
  29.1 6.6 %collective-permute-start.8 = (f32[80,256]{1,0:T(8,128)S(1)}, f32[80,256]{1,0:T(8,128)S(1)}, u32[]{:S(2)}, u32[]{:S(2)}) collective-permute-start(f32[80,256]{1,0:T(8,128)S(1)} %get-tuple-element.18), channel_id=1, source_target_pairs={{0,2},{1,3},{2,0},{3,1},{4,6},{5,7},{6,4},{7,5},{8,10},{9,11},{10,... | collective-permute-start | bytes 245768 | tf_op jit(solution)/shard_map/ppermute | solution.py:59
  29.1 6.6 %collective-permute-start.9 = (f32[80,256]{1,0:T(8,128)S(1)}, f32[80,256]{1,0:T(8,128)S(1)}, u32[]{:S(2)}, u32[]{:S(2)}) collective-permute-start(f32[80,256]{1,0:T(8,128)S(1)} %get-tuple-element.19), channel_id=1, source_target_pairs={{0,1},{1,0},{2,3},{3,2},{4,5},{5,4},{6,7},{7,6},{8,9},{9,8},{10,11... | collective-permute-start | bytes 245768 | tf_op jit(solution)/shard_map/ppermute | solution.py:59
  35.7 6.1 %collective-permute-start.12 = (f32[80,256]{1,0:T(8,128)S(1)}, f32[80,256]{1,0:T(8,128)S(1)}, u32[]{:S(2)}, u32[]{:S(2)}) collective-permute-start(f32[80,256]{1,0:T(8,128)S(1)} %add_add_fusion.2), channel_id=1, source_target_pairs={{24,0},{28,4},{16,8},{20,12},{8,16},{12,20},{0,24},{4,28},{25,1},{... | collective-permute-start | bytes 245768 | tf_op jit(solution)/shard_map/ppermute | solution.py:49
  37.2 5.2 %collective-permute-start.11 = (f32[80,256]{1,0:T(8,128)S(1)}, f32[80,256]{1,0:T(8,128)S(1)}, u32[]{:S(2)}, u32[]{:S(2)}) collective-permute-start(f32[80,256]{1,0:T(8,128)S(1)} %add_add_fusion.2), channel_id=1, source_target_pairs={{16,0},{20,4},{24,8},{28,12},{0,16},{4,20},{8,24},{12,28},{17,1},{... | collective-permute-start | bytes 245768 | tf_op jit(solution)/shard_map/ppermute | solution.py:49
  38.5 4.4 %collective-permute-start.10 = (f32[80,256]{1,0:T(8,128)S(1)}, f32[80,256]{1,0:T(8,128)S(1)}, u32[]{:S(2)}, u32[]{:S(2)}) collective-permute-start(f32[80,256]{1,0:T(8,128)S(1)} %add_add_fusion.2), channel_id=1, source_target_pairs={{8,0},{12,4},{0,8},{4,12},{24,16},{28,20},{16,24},{20,28},{9,1},{1... | collective-permute-start | bytes 245768 | tf_op jit(solution)/shard_map/ppermute | solution.py:49
  42.9 1.7 %collective-permute-start.13 = (f32[4,80,256]{2,1,0:T(8,128)S(1)}, f32[4,80,256]{2,1,0:T(8,128)S(1)}, u32[]{:S(2)}, u32[]{:S(2)}) collective-permute-start(f32[4,80,256]{2,1,0:T(8,128)S(1)} %pad_maximum_fusion.refs_0_), channel_id=1, source_target_pairs={{4,0},{0,4},{12,8},{8,12},{20,16},{16,20},{28,24},{24,28},{5,1},{1... | collective-permute-start | bytes 983048 | tf_op jit(solution)/shard_map/ppermute | solution.py:49
  46.9 17.4 %copy-start.2 = (f32[64,64]{1,0:T(8,128)}, f32[64,64]{1,0:T(8,128)S(1)}, u32[]{:S(2)}) copy-start(f32[64,64]{1,0:T(8,128)S(1)} %get-tuple-element.20.first_ref) | copy-start | bytes 49156
  46.9 7.3 %collective-permute-start.14 = (f32[80,256]{1,0:T(8,128)S(1)}, f32[80,256]{1,0:T(8,128)S(1)}, u32[]{:S(2)}, u32[]{:S(2)}) collective-permute-start(f32[80,256]{1,0:T(8,128)S(1)} %get-tuple-element.22), channel_id=1, source_target_pairs={{0,3},{1,2},{2,1},{3,0},{4,7},{5,6},{6,5},{7,4},{8,11},{9,10},{10,... | collective-permute-start | bytes 245768 | tf_op jit(solution)/shard_map/ppermute | solution.py:59
  49.5 7.6 %collective-permute-start.15 = (f32[80,256]{1,0:T(8,128)S(1)}, f32[80,256]{1,0:T(8,128)S(1)}, u32[]{:S(2)}, u32[]{:S(2)}) collective-permute-start(f32[80,256]{1,0:T(8,128)S(1)} %get-tuple-element.23), channel_id=1, source_target_pairs={{0,2},{1,3},{2,0},{3,1},{4,6},{5,7},{6,4},{7,5},{8,10},{9,11},{10,... | collective-permute-start | bytes 245768 | tf_op jit(solution)/shard_map/ppermute | solution.py:59
  49.5 7.6 %collective-permute-start.16 = (f32[80,256]{1,0:T(8,128)S(1)}, f32[80,256]{1,0:T(8,128)S(1)}, u32[]{:S(2)}, u32[]{:S(2)}) collective-permute-start(f32[80,256]{1,0:T(8,128)S(1)} %get-tuple-element.24), channel_id=1, source_target_pairs={{0,1},{1,0},{2,3},{3,2},{4,5},{5,4},{6,7},{7,6},{8,9},{9,8},{10,11... | collective-permute-start | bytes 245768 | tf_op jit(solution)/shard_map/ppermute | solution.py:59
  57.1 6.1 %collective-permute-start.19 = (f32[80,256]{1,0:T(8,128)S(1)}, f32[80,256]{1,0:T(8,128)S(1)}, u32[]{:S(2)}, u32[]{:S(2)}) collective-permute-start(f32[80,256]{1,0:T(8,128)S(1)} %add_add_fusion.1), channel_id=1, source_target_pairs={{24,0},{28,4},{16,8},{20,12},{8,16},{12,20},{0,24},{4,28},{25,1},{... | collective-permute-start | bytes 245768 | tf_op jit(solution)/shard_map/ppermute | solution.py:49
  58.3 5.8 %collective-permute-start.18 = (f32[80,256]{1,0:T(8,128)S(1)}, f32[80,256]{1,0:T(8,128)S(1)}, u32[]{:S(2)}, u32[]{:S(2)}) collective-permute-start(f32[80,256]{1,0:T(8,128)S(1)} %add_add_fusion.1), channel_id=1, source_target_pairs={{16,0},{20,4},{24,8},{28,12},{0,16},{4,20},{8,24},{12,28},{17,1},{... | collective-permute-start | bytes 245768 | tf_op jit(solution)/shard_map/ppermute | solution.py:49
  59.4 4.7 %collective-permute-start.17 = (f32[80,256]{1,0:T(8,128)S(1)}, f32[80,256]{1,0:T(8,128)S(1)}, u32[]{:S(2)}, u32[]{:S(2)}) collective-permute-start(f32[80,256]{1,0:T(8,128)S(1)} %add_add_fusion.1), channel_id=1, source_target_pairs={{8,0},{12,4},{0,8},{4,12},{24,16},{28,20},{16,24},{20,28},{9,1},{1... | collective-permute-start | bytes 245768 | tf_op jit(solution)/shard_map/ppermute | solution.py:49
  64.1 1.7 %collective-permute-start.20 = (f32[4,80,256]{2,1,0:T(8,128)S(1)}, f32[4,80,256]{2,1,0:T(8,128)S(1)}, u32[]{:S(2)}, u32[]{:S(2)}) collective-permute-start(f32[4,80,256]{2,1,0:T(8,128)S(1)} %pad_maximum_fusion.1.refs_0_), channel_id=1, source_target_pairs={{4,0},{0,4},{12,8},{8,12},{20,16},{16,20},{28,24},{24,28},{5,1},{1... | collective-permute-start | bytes 983048 | tf_op jit(solution)/shard_map/ppermute | solution.py:49
  68.1 9.9 %copy-start.3 = (f32[64,64]{1,0:T(8,128)}, f32[64,64]{1,0:T(8,128)S(1)}, u32[]{:S(2)}) copy-start(f32[64,64]{1,0:T(8,128)S(1)} %get-tuple-element.25.second_ref) | copy-start | bytes 49156
  68.1 7.3 %collective-permute-start.21 = (f32[80,256]{1,0:T(8,128)S(1)}, f32[80,256]{1,0:T(8,128)S(1)}, u32[]{:S(2)}, u32[]{:S(2)}) collective-permute-start(f32[80,256]{1,0:T(8,128)S(1)} %get-tuple-element.27), channel_id=1, source_target_pairs={{0,3},{1,2},{2,1},{3,0},{4,7},{5,6},{6,5},{7,4},{8,11},{9,10},{10,... | collective-permute-start | bytes 245768 | tf_op jit(solution)/shard_map/ppermute | solution.py:59
  70.4 7.5 %collective-permute-start.22 = (f32[80,256]{1,0:T(8,128)S(1)}, f32[80,256]{1,0:T(8,128)S(1)}, u32[]{:S(2)}, u32[]{:S(2)}) collective-permute-start(f32[80,256]{1,0:T(8,128)S(1)} %get-tuple-element.28), channel_id=1, source_target_pairs={{0,2},{1,3},{2,0},{3,1},{4,6},{5,7},{6,4},{7,5},{8,10},{9,11},{10,... | collective-permute-start | bytes 245768 | tf_op jit(solution)/shard_map/ppermute | solution.py:59
  70.4 7.5 %collective-permute-start.23 = (f32[80,256]{1,0:T(8,128)S(1)}, f32[80,256]{1,0:T(8,128)S(1)}, u32[]{:S(2)}, u32[]{:S(2)}) collective-permute-start(f32[80,256]{1,0:T(8,128)S(1)} %get-tuple-element.29), channel_id=1, source_target_pairs={{0,1},{1,0},{2,3},{3,2},{4,5},{5,4},{6,7},{7,6},{8,9},{9,8},{10,11... | collective-permute-start | bytes 245768 | tf_op jit(solution)/shard_map/ppermute | solution.py:59
  78.0 3.8 %collective-permute-start.25 = (f32[16,256]{1,0:T(8,128)S(1)}, f32[16,256]{1,0:T(8,128)S(1)}, u32[]{:S(2)}, u32[]{:S(2)}) collective-permute-start(f32[16,256]{1,0:T(8,128)S(1)} %get-tuple-element.31), channel_id=1, source_target_pairs={{16,0},{20,4},{24,8},{28,12},{0,16},{4,20},{8,24},{12,28},{17,1},{... | collective-permute-start | bytes 49160 | tf_op jit(solution)/shard_map/ppermute | solution.py:49
  78.8 3.8 %collective-permute-start.24 = (f32[16,256]{1,0:T(8,128)S(1)}, f32[16,256]{1,0:T(8,128)S(1)}, u32[]{:S(2)}, u32[]{:S(2)}) collective-permute-start(f32[16,256]{1,0:T(8,128)S(1)} %get-tuple-element.31), channel_id=1, source_target_pairs={{8,0},{12,4},{0,8},{4,12},{24,16},{28,20},{16,24},{20,28},{9,1},{1... | collective-permute-start | bytes 49160 | tf_op jit(solution)/shard_map/ppermute | solution.py:49
  79.8 4.6 %collective-permute-start.26 = (f32[16,256]{1,0:T(8,128)S(1)}, f32[16,256]{1,0:T(8,128)S(1)}, u32[]{:S(2)}, u32[]{:S(2)}) collective-permute-start(f32[16,256]{1,0:T(8,128)S(1)} %get-tuple-element.31), channel_id=1, source_target_pairs={{24,0},{28,4},{16,8},{20,12},{8,16},{12,20},{0,24},{4,28},{25,1},{... | collective-permute-start | bytes 49160 | tf_op jit(solution)/shard_map/ppermute | solution.py:49
  84.4 1.3 %copy-start.6 = (f32[4,16,256]{2,1,0:T(8,128)}, f32[4,16,256]{2,1,0:T(8,128)S(1)}, u32[]{:S(2)}) copy-start(f32[4,16,256]{2,1,0:T(8,128)S(1)} %pad_maximum_fusion.3.refs_0_) | copy-start | bytes 196612
  84.4 1.3 %collective-permute-start.27 = (f32[4,16,256]{2,1,0:T(8,128)S(1)}, f32[4,16,256]{2,1,0:T(8,128)S(1)}, u32[]{:S(2)}, u32[]{:S(2)}) collective-permute-start(f32[4,16,256]{2,1,0:T(8,128)S(1)} %pad_maximum_fusion.3.refs_0_), channel_id=1, source_target_pairs={{4,0},{0,4},{12,8},{8,12},{20,16},{16,20},{28,24},{24,28},{5,1},{1... | collective-permute-start | bytes 196616 | tf_op jit(solution)/shard_map/ppermute | solution.py:49
  85.8 0.6 copy-start.7

commit v4 on v3

--- a/solution.py
+++ b/solution.py
@@ -34,6 +34,10 @@
 def stacked_digits(values):
     high, low = balanced_digits(values)
     return jnp.concatenate([high, low], 0).astype(jnp.bfloat16)
+
+
+def centred_digits(residues):
+    return stacked_digits(jnp.where(residues > HALF_MODULUS, residues - MODULUS, residues))
 
 
 def partner(index, shift, size):
@@ -62,12 +66,18 @@
     return [pieces[0]] + came
 
 
-def gather_in_pairs(piece, axis):
+def zero_after(*arrays):
+    return sum(array[(0,) * array.ndim] for array in arrays) * 0.0
+
+
+def gather_in_pairs(piece, axis, *before):
     size = lax.axis_size(axis)
     if size & (size - 1) or size == 1:
         pieces = gather_pieces(piece, axis)
         return [jnp.stack(pieces[:1])] if size == 1 else [jnp.stack(pieces[k::2]) for k in (0, 1)]
     evens = jnp.stack([piece] + [fetch(piece, axis, shift) for shift in range(2, size, 2)])
+    if before:
+        evens = evens + zero_after(*before)
     return [evens, fetch(evens, axis, 1)]
 
 
@@ -99,7 +109,9 @@
     return jnp.concatenate([packed[:, j * span : (j + 1) * span] for j in range(count)], 0)
 
 
-def build_kernel(sizes, rows_ref, cols_ref, count_ref, entries_ref, dense_ref, held, sems):
+def build_kernel(sizes, *refs):
+    count_ref, entries_ref, dense_ref, token_ref = refs[2:6]
+    rows_ref, cols_ref, held, sems = refs[6:]
     n_row, n_col, piece_blocks, group = sizes
     _, _, slot_count, tile_len, _ = entries_ref.shape
     me_row, me_col = lax.axis_index("row"), lax.axis_index("col")
@@ -109,6 +121,12 @@
         return pltpu.make_async_copy(source, held.at[pl.ds(index * group, group)], sems.at[index])
 
     chunk_count = slot_count // group
+    positions = [
+        pltpu.make_async_copy(refs[index], refs[6 + index], sems.at[chunk_count + index])
+        for index in range(2)
+    ]
+    for copy in positions:
+        copy.start()
     for index in range(chunk_count):
         chunk(index).start()
 
@@ -117,6 +135,8 @@
         return carry
 
     lax.fori_loop(0, dense_ref.shape[0], clear, 0)
+    for copy in positions:
+        copy.wait()
 
     def place(slot):
         row, col = rows_ref[0, 0, slot], cols_ref[0, 0, slot]
@@ -137,6 +157,7 @@
         return carry
 
     lax.fori_loop(0, chunk_count, step, 0)
+    token_ref[...] = jnp.zeros_like(token_ref)
 
 
 def build_dense(tile_entries, tile_rows, tile_cols, tile_count, sizes):
@@ -144,26 +165,32 @@
     _, _, slot_count, tile_len, _ = tile_entries.shape
     group = next(size for size in (8, 4, 2, 1) if slot_count % size == 0)
     shape = (n_col * piece_blocks, n_row * piece_blocks * tile_len, 2 * tile_len)
-    smem = pl.BlockSpec(memory_space=pltpu.SMEM)
+    hbm = pl.BlockSpec(memory_space=pltpu.HBM)
+    rows, cols, entries = (
+        pltpu.with_memory_space_constraint(part, pltpu.HBM)
+        for part in (tile_rows, tile_cols, tile_entries)
+    )
     return pl.pallas_call(
         functools.partial(build_kernel, (*sizes, group)),
-        in_specs=[smem, smem, smem, pl.BlockSpec(memory_space=pltpu.HBM)],
-        out_specs=pl.BlockSpec(memory_space=pltpu.VMEM),
-        out_shape=pltpu.VMEM(shape, jnp.bfloat16),
+        in_specs=[hbm, hbm, pl.BlockSpec(memory_space=pltpu.SMEM), hbm],
+        out_specs=[pl.BlockSpec(memory_space=pltpu.VMEM)] * 2,
+        out_shape=[pltpu.VMEM(shape, jnp.bfloat16), pltpu.VMEM((8, 128), jnp.float32)],
         scratch_shapes=[
+            *(pltpu.SMEM(part.shape, part.dtype) for part in (tile_rows, tile_cols)),
             pltpu.VMEM((slot_count, tile_len, tile_len), jnp.float32),
-            pltpu.SemaphoreType.DMA((slot_count // group,)),
+            pltpu.SemaphoreType.DMA((slot_count // group + 2,)),
         ],
         compiler_params=pltpu.CompilerParams(vmem_limit_bytes=VMEM_LIMIT),
         cost_estimate=pl.CostEstimate(
             flops=8 * tile_entries.size, bytes_accessed=8 * tile_entries.size, transcendentals=0
         ),
-    )(tile_rows, tile_cols, tile_count, tile_entries)
-
-
-def step_kernel(n_pairs, n_row, n_col, span, first, *refs):
+    )(rows, cols, tile_count, entries)
+
+
+def step_kernel(n_pairs, n_row, n_col, span, first, last, *refs):
     pairs, refs = refs[:n_pairs], refs[n_pairs:]
-    x_pieces, refs = refs[:n_col], refs[n_col:]
+    if not last:
+        x_pieces, refs = refs[:n_col], refs[n_col:]
     dense_ref, refs = refs[0], refs[1:]
     outs, refs = refs[:n_col], refs[n_col:]
     if not first:
@@ -171,16 +198,17 @@
     digits = refs[0]
     row_blocks, depth, width = dense_ref.shape
     tile_len = width // 2
-    piece_len = x_pieces[0].shape[1]
+    piece_len = outs[0].shape[1]
     piece_blocks = piece_len // tile_len
+    packed_rows = span * span // piece_len
     for d in range(n_row):
         vector = reduce_centered(piece_at(pairs, d)[:span])
         digits[:, d * piece_len : (d + 1) * piece_len] = stacked_digits(vector)
     if not first:
-        packed = sum(jnp.sum(pair[:, span:, :], 0) for pair in pairs)
+        packed = sum(jnp.sum(pair[:, span : span + packed_rows, :], 0) for pair in pairs)
         total_ref[...] = unpack_square(reduce_centered(packed), span)
     projected = None
-    for e in range(n_col):
+    for e in reversed(range(n_col)):
         parts = []
         for sub in range(piece_blocks):
             block = e * piece_blocks + sub
@@ -199,73 +227,170 @@
             parts.append(reduce_centered(15.0 * high + 256.0 * reduce_centered(middle) + low))
         piece = jnp.concatenate(parts, 1)
         outs[e][:span, :] = piece
-        x_values = x_pieces[e][...]
-        x_values = jnp.where(x_values > HALF_MODULUS, x_values - MODULUS, x_values)
-        products = dot_pairs(stacked_digits(x_values), stacked_digits(piece))
-        if n_col * piece_len > EXACT_DEPTH:
-            products = reduce_centered(products)
-        projected = products if projected is None else projected + products
-    packed = pack_square(projection_residues(projected, span), piece_len)
+        if not last:
+            products = dot_pairs(centred_digits(x_pieces[e][...]), stacked_digits(piece))
+            if n_col * piece_len > EXACT_DEPTH:
+                products = reduce_centered(products)
+            projected = products if projected is None else projected + products
+    if last:
+        packed = sum(jnp.sum(pair[:, span + packed_rows :, :], 0) for pair in pairs)
+    else:
+        packed = pack_square(projection_residues(projected, span), piece_len)
     for out in outs:
         out[span:, :] = packed
 
 
-def dense_step(pairs, x_pieces, dense, first):
+def in_vmem(*arrays):
+    return [pltpu.with_memory_space_constraint(array, pltpu.VMEM) for array in arrays]
+
+
+def dense_step(pairs, x_pieces, dense, first, last):
     n_row, n_col = len(pairs) * pairs[0].shape[0], len(x_pieces)
     span, piece_len = x_pieces[0].shape
-    row_blocks, depth, width = dense.shape
+    _, depth, _ = dense.shape
     rows = span + span * span // piece_len
     outs = [pltpu.VMEM((rows, piece_len), jnp.float32)] * n_col
     if not first:
         outs = outs + [jax.ShapeDtypeStruct((span, span), jnp.float32)]
-    vmem = pl.BlockSpec(memory_space=pltpu.VMEM)
+    operands = in_vmem(*pairs, *([] if last else x_pieces), dense)
     results = pl.pallas_call(
-        functools.partial(step_kernel, len(pairs), n_row, n_col, span, first),
-        in_specs=[vmem] * (len(pairs) + n_col + 1),
-        out_specs=[vmem] * len(outs),
+        functools.partial(step_kernel, len(pairs), n_row, n_col, span, first, last),
+        in_specs=[pl.BlockSpec(memory_space=pltpu.VMEM)] * len(operands),
+        out_specs=[pl.BlockSpec(memory_space=pltpu.VMEM)] * len(outs),
         out_shape=outs,
         scratch_shapes=[pltpu.VMEM((2 * span, depth), jnp.bfloat16)],
         compiler_params=pltpu.CompilerParams(vmem_limit_bytes=VMEM_LIMIT),
         cost_estimate=pl.CostEstimate(
             flops=4 * span * dense.size, bytes_accessed=2 * dense.size, transcendentals=0
         ),
-    )(*(pltpu.with_memory_space_constraint(part, pltpu.VMEM) for part in (*pairs, *x_pieces, dense)))
+    )(*operands)
     return list(results[:n_col]), (None if first else results[n_col])
 
 
-def sparse_step(pairs, x_pieces, positions, a_digits, first):
+def left_kernel(n_col, n_row, *refs):
+    x_pieces, (dense_ref, _, out_ref) = refs[:n_col], refs[n_col:]
+    me_row = lax.axis_index("row")
+    row_blocks, _, width = dense_ref.shape
+    tile_len = width // 2
+    span, piece_len = x_pieces[0].shape
+    piece_blocks = piece_len // tile_len
+    x_digits = [centred_digits(piece[...]) for piece in x_pieces]
+    for d in range(n_row):
+        by_high = by_low = 0.0
+        for block in range(row_blocks):
+            sub = block % piece_blocks
+            left = x_digits[block // piece_blocks][:, sub * tile_len : (sub + 1) * tile_len]
+            right = dense_ref[block, d * piece_len : (d + 1) * piece_len, :]
+            by_high = by_high + dot_pairs(left, right[:, :tile_len])
+            by_low = by_low + dot_pairs(left, right[:, tile_len:])
+            if (block + 1) * tile_len % EXACT_DEPTH == 0:
+                by_high, by_low = reduce_centered(by_high), reduce_centered(by_low)
+        by_high, by_low = reduce_centered(by_high), reduce_centered(by_low)
+        piece = reduce_centered(
+            15.0 * by_high[:span]
+            + 256.0 * reduce_centered(by_low[:span] + by_high[span:])
+            + by_low[span:]
+        )
+        out_ref[partner(me_row, d, n_row)] = piece
+
+
+def dense_left(x_pieces, dense, after, n_row):
+    n_col = len(x_pieces)
+    span, piece_len = x_pieces[0].shape
+    operands = in_vmem(*x_pieces, dense, after)
+    return pl.pallas_call(
+        functools.partial(left_kernel, n_col, n_row),
+        in_specs=[pl.BlockSpec(memory_space=pltpu.VMEM)] * (n_col + 1)
+        + [pl.BlockSpec(memory_space=pl.ANY)],
+        out_specs=pl.BlockSpec(memory_space=pltpu.VMEM),
+        out_shape=jax.ShapeDtypeStruct((n_row, span, piece_len), jnp.float32),
+        compiler_params=pltpu.CompilerParams(vmem_limit_bytes=VMEM_LIMIT),
+        cost_estimate=pl.CostEstimate(
+            flops=4 * span * dense.size, bytes_accessed=2 * dense.size, transcendentals=0
+        ),
+    )(*operands)
+
+
+def append_kernel(w_ref, *refs):
+    pieces, out_ref = refs[:-1], refs[-1]
+    span = w_ref.shape[0]
+    summed = pieces[0][...]
+    for piece in pieces[1:]:
+        summed = summed + piece[...]
+    rows = summed.shape[0]
+    out_ref[:rows, :] = summed
+    products = dot_pairs(
+        stacked_digits(reduce_centered(w_ref[...])),
+        stacked_digits(reduce_centered(summed[:span])),
+    )
+    out_ref[rows:, :] = pack_square(projection_residues(products, span), summed.shape[1])
+
+
+def append_projection(w_piece, pieces):
+    span, piece_len = w_piece.shape
+    rows = pieces[0].shape[0] + span * span // piece_len
+    return pl.pallas_call(
+        append_kernel,
+        out_shape=jax.ShapeDtypeStruct((rows, piece_len), jnp.float32),
+    )(w_piece, *pieces)
+
+
+def sparse_step(pairs, x_pieces, positions, a_digits, first, last):
     span, piece_len = x_pieces[0].shape
     pieces = [piece_at(pairs, d) for d in range(len(pairs) * pairs[0].shape[0])]
-    slot_count, _, tile_len, _ = a_digits.shape
+    tile_len = a_digits.shape[-1]
     n_col = len(x_pieces)
-    row_blocks = piece_len // tile_len * n_col
+    packed_rows = span * span // piece_len
     total = None
     if not first:
-        packed = functools.reduce(jnp.add, [piece[span:] for piece in pieces])
+        packed = functools.reduce(jnp.add, [piece[span : span + packed_rows] for piece in pieces])
         total = unpack_square(reduce_centered(packed), span)
     vector = reduce_centered(jnp.concatenate([piece[:span] for piece in pieces], 1))
+    residues = sparse_residues(vector, positions[1], a_digits, "ntk,tdik->tdni")
+    summed = sparse_sum(residues, positions[0], positions[2], piece_len // tile_len * n_col)
+    outs = reduce_centered(summed).reshape(span, n_col, piece_len)
+    if last:
+        packed = functools.reduce(jnp.add, [piece[span + packed_rows :] for piece in pieces])
+    else:
+        projected = 0.0
+        for e in range(n_col):
+            products = dot_pairs(centred_digits(x_pieces[e]), stacked_digits(outs[:, e]))
+            projected = projected + reduce_centered(products)
+        packed = pack_square(projection_residues(projected, span), piece_len)
+    return [jnp.concatenate([outs[:, e], packed], 0) for e in range(n_col)], total
+
+
+def sparse_residues(vector, places, a_digits, spec):
+    span, tile_len = vector.shape[0], a_digits.shape[-1]
     v_digits = stacked_digits(vector).reshape(2 * span, -1, tile_len)
-    picked = jnp.take(v_digits, positions[1], axis=1)
-    products = jnp.einsum("ntk,tdik->tdni", picked, a_digits, preferred_element_type=jnp.float32)
+    picked = jnp.take(v_digits, places, axis=1)
+    products = jnp.einsum(spec, picked, a_digits, preferred_element_type=jnp.float32)
     products = reduce_centered(products)
-    residues = reduce_centered(
+    return reduce_centered(
         15.0 * products[:, 0, :span]
         + 256.0 * reduce_centered(products[:, 0, span:] + products[:, 1, :span])
         + products[:, 1, span:]
     )
-    live = jnp.arange(slot_count, dtype=jnp.int32) < positions[2]
-    onehot = positions[0][None, :] == jnp.arange(row_blocks, dtype=jnp.int32)[:, None]
+
+
+def sparse_sum(residues, places, count, blocks):
+    live = jnp.arange(places.shape[0], dtype=jnp.int32) < count
+    onehot = places[None, :] == jnp.arange(blocks, dtype=jnp.int32)[:, None]
     onehot = (onehot & live[None, :]).astype(jnp.float32)
-    summed = jnp.einsum("bt,twi->wbi", onehot, residues, precision=lax.Precision.HIGHEST)
-    outs = reduce_centered(summed).reshape(span, n_col, piece_len)
-    projected = 0.0
-    for e in range(n_col):
-        x_values = x_pieces[e]
-        x_values = jnp.where(x_values > HALF_MODULUS, x_values - MODULUS, x_values)
-        products = dot_pairs(stacked_digits(x_values), stacked_digits(outs[:, e]))
-        projected = projected + reduce_centered(products)
-    packed = pack_square(projection_residues(projected, span), piece_len)
-    return [jnp.concatenate([outs[:, e], packed], 0) for e in range(n_col)], total
+    return jnp.einsum("bt,twi->wbi", onehot, residues, precision=lax.Precision.HIGHEST)
+
+
+def sparse_left(x_pieces, after, positions, a_digits, n_row):
+    del after
+    span, piece_len = x_pieces[0].shape
+    tile_len = a_digits.shape[-1]
+    values = jnp.concatenate(x_pieces, 1)
+    values = jnp.where(values > HALF_MODULUS, values - MODULUS, values)
+    residues = sparse_residues(values, positions[0], a_digits, "nti,tdik->tdnk")
+    summed = sparse_sum(residues, positions[1], positions[2], piece_len // tile_len * n_row)
+    pieces = reduce_centered(summed).reshape(span, n_row, piece_len)
+    order = partner(lax.axis_index("row"), jnp.arange(n_row, dtype=jnp.int32), n_row)
+    return jnp.zeros((n_row, span, piece_len)).at[order].set(jnp.moveaxis(pieces, 1, 0))
 
 
 def multiply_mod(left, right):
@@ -281,27 +406,29 @@
     )
 
 
-def sigma_kernel(count, first_ref, second_ref, *refs):
-    thirds, out_ref = refs[:count], refs[count]
+def sigma_start_kernel(first_ref, second_ref, start_ref, both_ref, rest_ref):
     c_1, c_2 = first_ref[...], second_ref[...]
-    packed = sum(jnp.sum(pair[...], 0) for pair in thirds)
-    c_3 = unpack_square(reduce_centered(packed), c_1.shape[0])
     e_2 = reduce_centered(c_1 - multiply_mod(c_1, c_2))
     both = reduce_centered(c_1 + e_2)
-    start = multiply_mod(e_2, c_1)
-    rest = c_1 - multiply_mod(both, c_2)
-    e_3 = reduce_centered(multiply_mod(start, c_3) + rest)
+    start_ref[...] = multiply_mod(e_2, c_1)
+    both_ref[...] = both
+    rest_ref[...] = c_1 - multiply_mod(both, c_2)
+
+
+def sigma_end_kernel(start_ref, both_ref, rest_ref, packed_ref, out_ref):
+    start, both = start_ref[...], both_ref[...]
+    c_3 = unpack_square(reduce_centered(packed_ref[...]), start.shape[0])
+    e_3 = reduce_centered(multiply_mod(start, c_3) + rest_ref[...])
     out_ref[0] = canonical(-multiply_mod(e_3, start)) * (1.0 / MODULUS)
     out_ref[1] = canonical(start + multiply_mod(e_3, both)) * (1.0 / MODULUS)
     out_ref[2] = canonical(-both - e_3) * (1.0 / MODULUS)
 
 
-def sigma_update(c_1, c_2, c_3_pairs):
-    span = c_1.shape[0]
-    return pl.pallas_call(
-        functools.partial(sigma_kernel, len(c_3_pairs)),
-        out_shape=jax.ShapeDtypeStruct((STEP_COUNT, span, span), jnp.float32),
-    )(c_1, c_2, *c_3_pairs)
+def sigma_update(c_1, c_2, packed_3):
+    square = jax.ShapeDtypeStruct(c_1.shape, jnp.float32)
+    known = pl.pallas_call(sigma_start_kernel, out_shape=[square] * 3)(c_1, c_2)
+    shape = jax.ShapeDtypeStruct((STEP_COUNT, *c_1.shape), jnp.float32)
+    return pl.pallas_call(sigma_end_kernel, out_shape=shape)(*known, packed_3)
 
 
 def sparse_tiles(tile_entries, tile_rows, tile_cols, tile_count, sizes):
@@ -325,22 +452,35 @@
     n_row, n_col = lax.axis_size("row"), lax.axis_size("col")
     tiles = (tile_entries, tile_rows, tile_cols, tile_count)
     sizes = (n_row, n_col, piece_blocks)
-    pairs = gather_in_pairs(block_y, "row")
     x_pieces = gather_pieces(block_x, "col")
+    before = list(x_pieces[1:])
     if n_col * piece_blocks * n_row * piece_blocks <= DENSE_CELLS * slot_count:
-        multiply = functools.partial(dense_step, dense=build_dense(*tiles, sizes))
+        dense, token = build_dense(*tiles, sizes)
+        before.append(token)
+        multiply = functools.partial(dense_step, dense=dense)
+        multiply_left = functools.partial(dense_left, dense=dense)
     else:
         a_digits, positions = sparse_tiles(*tiles, sizes)
         multiply = functools.partial(sparse_step, positions=positions, a_digits=a_digits)
+        multiply_left = functools.partial(sparse_left, positions=positions, a_digits=a_digits)
+    pairs = gather_in_pairs(block_y, "row", *before)
     totals = []
     for step_index in range(STEP_COUNT):
-        outs, total = multiply(pairs, x_pieces, first=step_index == 0)
+        first, last = step_index == 0, step_index == STEP_COUNT - 1
+        outs, total = multiply(pairs, x_pieces, first=first, last=last)
         totals.append(total)
-        summed = functools.reduce(jnp.add, scatter_pieces(outs, "col"))
-        if step_index < STEP_COUNT - 1:
+        pieces = scatter_pieces(outs, "col")
+        if step_index == STEP_COUNT - 2:
+            pairs = gather_in_pairs(append_projection(w_piece, pieces), "row")
+            continue
+        summed = functools.reduce(jnp.add, pieces)
+        if first:
+            left = multiply_left(x_pieces, after=outs[0], n_row=n_row)
+            w_piece = lax.psum_scatter(left, "row")
+            summed = summed + zero_after(left)
+        if not last:
             pairs = gather_in_pairs(summed, "row")
-    thirds = gather_in_pairs(summed[span:], "row")
-    polynomial = sigma_update(totals[1], totals[2], thirds)
+    polynomial = sigma_update(totals[1], totals[2], summed[span:])
     return polynomial, canonical(summed[:span]) * (1.0 / MODULUS)
 
 

time: 88.9 us -> 117 us (1.32)
  between operations: 1.47 us -> 18 us
  local copies, waits for them, and re-layouts: 4.13 us -> 14.3 us
  Pallas kernels: 12.7 us -> 18.4 us
  waiting for transfers between devices: 35.5 us -> 31.5 us
  starting transfers between devices: 33.3 us -> 31.5 us
    reduce_scatter x0 -> x1, waiting for transfers between devices: none -> 6.99 us  [local(): w_piece = lax.psum_scatter(left, 'row')]
    pallas_call x1 -> x4, Pallas kernels: 2.28 us -> 9.18 us  [the longest x1 3.46 us: dense_left(): pl.pallas_call(functools.partial(left_kernel, n_col, n_row), in_specs=[pl...]
    ppermute x19 -> x15, waiting for transfers between devices: 18.5 us -> 13 us  [fetch(): lax.ppermute(piece, axis, [(partner(i, shift, size), i) for i in range(si...]
    unnamed x16 -> x22, local copies, waits for them, and re-layouts: 4.12 us -> 9.56 us
    ppermute x9, waiting for transfers between devices: 16.9 us -> 11.5 us  [scatter_pieces(): lax.ppermute(pieces[shift], axis, [(i, partner(i, shift, size)) for i in...]
    slice x0 -> x6, local copies, waits for them, and re-layouts: none -> 4.71 us  [the longest x5 4.11 us: zero_after(): return sum((array[(0,) * array.ndim] for array in arrays)) * 0.0]
    ppermute x19 -> x15, starting transfers between devices: 19.9 us -> 16.5 us  [fetch(): lax.ppermute(piece, axis, [(partner(i, shift, size), i) for i in range(si...]
    ppermute x9, starting transfers between devices: 13.3 us -> 14.9 us  [scatter_pieces(): lax.ppermute(pieces[shift], axis, [(i, partner(i, shift, size)) for i in...]
  transfers between devices with their start and end apart: 28 -> 25, of which waited for: 20 -> 15; matrix products, arithmetic and copies ran while one was open for 1% -> 4% of each run, Pallas kernels for 4% -> 9%
where the time goes in v4:
time: 117 us; the launch traced here: 116 us
  starting transfers between devices  31.5 us (27%)
  waiting for transfers between devices  31.5 us (27%)
  Pallas kernels  18.4 us (16%)
  between operations  18 us (15%)
  local copies, waits for them, and re-layouts  14.3 us (12%)
  other arithmetic  2.5 us (2%)
    ppermute x15, starting transfers between devices, fetch(): lax.ppermute(piece, axis, [(partner(i, shift, size), i) for i in range(si...  16.5 us
    ppermute x9, starting transfers between devices, scatter_pieces(): lax.ppermute(pieces[shift], axis, [(i, partner(i, shift, size)) for i in...  14.9 us
    ppermute x15, waiting for transfers between devices, fetch(): lax.ppermute(piece, axis, [(partner(i, shift, size), i) for i in range(si...  13 us
    ppermute x9, waiting for transfers between devices, scatter_pieces(): lax.ppermute(pieces[shift], axis, [(i, partner(i, shift, size)) for i in...  11.5 us
    unnamed x22, local copies, waits for them, and re-layouts  9.56 us
    reduce_scatter x1, waiting for transfers between devices, local(): w_piece = lax.psum_scatter(left, 'row')  6.99 us
    pallas_call x3, Pallas kernels, dense_step(): pl.pallas_call(functools.partial(step_kernel, len(pairs), n_row, n_col, s...  5.87 us
    slice x5, local copies, waits for them, and re-layouts, zero_after(): return sum((array[(0,) * array.ndim] for array in arrays)) * 0.0  4.11 us
  transfers between devices with their start and end apart: 25, of which 15 were waited for; matrix products, arithmetic and copies ran while one was open for 4% of the time, Pallas kernels for 9%

profile of v4, /device:TPU:0, one launch (start us, length us, event | category | flops | bytes accessed | tf_op | source)
XLA Modules:
  0.0 116.2 jit_solution(10212533340926131655)
XLA Ops:
  7.2 4.1 %collective-permute-start.4 = (f32[64,256]{1,0:T(8,128)}, f32[64,256]{1,0:T(8,128)S(1)}, u32[]{:S(2)}, u32[]{:S(2)}) collective-permute-start(f32[64,256]{1,0:T(8,128)} %refs_2_.4), channel_id=1, source_target_pairs={{2,0},{3,1},{0,2},{1,3},{6,4},{7,5},{4,6},{5,7},{10,8},{11,9},{8,1... | collective-permute-start | bytes 196616 | tf_op jit(solution)/shard_map/ppermute | solution.py:53
  11.3 1.6 %collective-permute-start.3 = (f32[64,256]{1,0:T(8,128)}, f32[64,256]{1,0:T(8,128)S(1)}, u32[]{:S(2)}, u32[]{:S(2)}) collective-permute-start(f32[64,256]{1,0:T(8,128)} %refs_2_.4), channel_id=1, source_target_pairs={{1,0},{0,1},{3,2},{2,3},{5,4},{4,5},{7,6},{6,7},{9,8},{8,9},{11,10... | collective-permute-start | bytes 196616 | tf_op jit(solution)/shard_map/ppermute | solution.py:53
  12.9 1.7 %collective-permute-start = (f32[64,256]{1,0:T(8,128)}, f32[64,256]{1,0:T(8,128)S(1)}, u32[]{:S(2)}, u32[]{:S(2)}) collective-permute-start(f32[64,256]{1,0:T(8,128)} %param.11), channel_id=1, source_target_pairs={{8,0},{12,4},{0,8},{4,12},{24,16},{28,20},{16,24},{20,28},{9,1},{1... | collective-permute-start | bytes 196616 | tf_op jit(solution)/shard_map/ppermute | solution.py:53
  14.6 1.5 %collective-permute-start.2 = (f32[64,256]{1,0:T(8,128)}, f32[64,256]{1,0:T(8,128)S(1)}, u32[]{:S(2)}, u32[]{:S(2)}) collective-permute-start(f32[64,256]{1,0:T(8,128)} %param.11), channel_id=1, source_target_pairs={{24,0},{28,4},{16,8},{20,12},{8,16},{12,20},{0,24},{4,28},{25,1},{... | collective-permute-start | bytes 196616 | tf_op jit(solution)/shard_map/ppermute | solution.py:53
  17.1 3.4 %shard_map.77 = (bf16[8,2048,256]{2,1,0:T(8,128)(2,1)S(1)}, f32[8,128]{1,0:T(8,128)S(1)}) custom-call(s32[1,1,64]{2,1,0:T(1,128)} %refs_0_.2, s32[1,1,64]{2,1,0:T(1,128)} %refs_1_.1, s32[1,1]{1,0:T(1,128)S(6)} %copy.8.refs_2_, f32[1,1,64,128,128]{4,3,2,1,0:T(8,128)} %refs_3_.1), custom_call_target="tpu_custom_call" | custom-call | flops 8388608 | bytes 8388608 | tf_op jit(solution)/shard_map/pallas_call | solution.py:173
  20.5 0.6 slice.24
  21.1 0.9 slice.29
  21.9 1.0 slice.28
  26.0 0.9 maximum_add_fusion.refs_0_
  27.0 1.5 %collective-permute-done.6.refs_1_ = f32[4,64,256]{2,1,0:T(8,128)S(1)} collective-permute-done((f32[4,64,256]{2,1,0:T(8,128)S(1)}, f32[4,64,256]{2,1,0:T(8,128)S(1)}, u32[]{:S(2)}, u32[]{:S(2)}) %collective-permute-start.6) | collective-permute-done | bytes 262176 | tf_op jit(solution)/shard_map/ppermute | solution.py:53
  28.5 0.8 copy-done.3
  29.3 2.2 %shard_map.78 = (f32[80,256]{1,0:T(8,128)S(1)}, f32[80,256]{1,0:T(8,128)S(1)}, f32[80,256]{1,0:T(8,128)S(1)}, f32[80,256]{1,0:T(8,128)S(1)}) custom-call(f32[4,64,256]{2,1,0:T(8,128)S(1)} %maximum_add_fusion.refs_0_, f32[4,64,256]{2,1,0:T(8,128)S(1)} %collective-permute-done.6.refs_1_, f32[64,256]{1,0:T(8,128)S(1)} %copy-done.3, ...), custom_call_target="tpu_custom_call" | custom-call | flops 1073741824 | bytes 8388608 | tf_op jit(solution)/shard_map/pallas_call | solution.py:256
  31.6 5.5 %collective-permute-start.7 = (f32[80,256]{1,0:T(8,128)S(1)}, f32[80,256]{1,0:T(8,128)S(1)}, u32[]{:S(2)}, u32[]{:S(2)}) collective-permute-start(f32[80,256]{1,0:T(8,128)S(1)} %get-tuple-element.24), channel_id=1, source_target_pairs={{0,3},{1,2},{2,1},{3,0},{4,7},{5,6},{6,5},{7,4},{8,11},{9,10},{10,... | collective-permute-start | bytes 245768 | tf_op jit(solution)/shard_map/ppermute | solution.py:63
  37.1 0.6 collective-permute-start.9
  37.7 3.5 %shard_map.79 = f32[8,64,256]{2,1,0:T(8,128)} custom-call(f32[64,256]{1,0:T(8,128)S(1)} %copy-done.4, f32[64,256]{1,0:T(8,128)S(1)} %collective-permute-done.3.refs_3_.refs_1_, f32[64,256]{1,0:T(8,128)S(1)} %collective-permute-done.4.refs_4_.refs_2_, f32[64,256]{1,0:T(8,128)S(1)} %collective-permute-done.5.refs_5_.refs_3_, ...), custom_call_target="tpu_custom_call" | custom-call | flops 1073741824 | bytes 8388608 | tf_op jit(solution)/shard_map/pallas_call | solution.py:301
  41.2 1.2 %slice.31 = f32[1,1,1]{2,1,0:T(1,128)} slice(f32[8,64,256]{2,1,0:T(8,128)} %shard_map.79), slice={[0:1], [0:1], [0:1]} | slice | bytes 8 | tf_op jit(solution)/shard_map/slice | solution.py:70
  43.4 1.5 %collective-permute-start.12 = (f32[80,256]{1,0:T(8,128)S(1)}, f32[80,256]{1,0:T(8,128)S(1)}, u32[]{:S(2)}, u32[]{:S(2)}) collective-permute-start(f32[80,256]{1,0:T(8,128)S(1)} %add_add_fusion.1), channel_id=1, source_target_pairs={{24,0},{28,4},{16,8},{20,12},{8,16},{12,20},{0,24},{4,28},{25,1},{... | collective-permute-start | bytes 245768 | tf_op jit(solution)/shard_map/ppermute | solution.py:53
  44.9 1.5 %collective-permute-start.11 = (f32[80,256]{1,0:T(8,128)S(1)}, f32[80,256]{1,0:T(8,128)S(1)}, u32[]{:S(2)}, u32[]{:S(2)}) collective-permute-start(f32[80,256]{1,0:T(8,128)S(1)} %add_add_fusion.1), channel_id=1, source_target_pairs={{16,0},{20,4},{24,8},{28,12},{0,16},{4,20},{8,24},{12,28},{17,1},{... | collective-permute-start | bytes 245768 | tf_op jit(solution)/shard_map/ppermute | solution.py:53
  47.0 2.4 %collective-permute-done.12 = f32[80,256]{1,0:T(8,128)S(1)} collective-permute-done((f32[80,256]{1,0:T(8,128)S(1)}, f32[80,256]{1,0:T(8,128)S(1)}, u32[]{:S(2)}, u32[]{:S(2)}) %collective-permute-start.12) | collective-permute-done | bytes 81952 | tf_op jit(solution)/shard_map/ppermute | solution.py:53
  49.4 1.1 collective-permute-done.11
  51.0 1.6 %collective-permute-done.13.refs_1_ = f32[4,80,256]{2,1,0:T(8,128)S(1)} collective-permute-done((f32[4,80,256]{2,1,0:T(8,128)S(1)}, f32[4,80,256]{2,1,0:T(8,128)S(1)}, u32[]{:S(2)}, u32[]{:S(2)}) %collective-permute-start.13) | collective-permute-done | bytes 327712 | tf_op jit(solution)/shard_map/ppermute | solution.py:53
  52.6 3.5 %copy-done.1 = bf16[8,2048,256]{2,1,0:T(8,128)(2,1)S(1)} copy-done((bf16[8,2048,256]{2,1,0:T(8,128)(2,1)S(1)}, bf16[8,2048,256]{2,1,0:T(8,128)(2,1)}, u32[]{:S(2)}) %copy-start.1) | copy-done | bytes 8388632
  56.1 2.2 %shard_map.80 = (f32[80,256]{1,0:T(8,128)S(1)}, f32[80,256]{1,0:T(8,128)S(1)}, f32[80,256]{1,0:T(8,128)S(1)}, f32[80,256]{1,0:T(8,128)S(1)}, f32[64,64]{1,0:T(8,128)S(1)}) custom-call(f32[4,80,256]{2,1,0:T(8,128)S(1)} %pad_maximum_fusion.1.refs_0_, f32[4,80,256]{2,1,0:T(8,128)S(1)} %collective-permute-done.13.refs_1_, f32[64,256]{1,0:T(8,128)S(1)} %copy-done.4, ...), custom_call_target="tpu_custom_call" | custom-call | flops 1073741824 | bytes 8388608 | tf_op jit(solution)/shard_map/pallas_call | solution.py:256
  58.3 0.6 copy-done.5
  59.0 0.6 copy-done.6
  59.6 3.4 %collective-permute-start.14 = (f32[80,256]{1,0:T(8,128)S(1)}, f32[80,256]{1,0:T(8,128)S(1)}, u32[]{:S(2)}, u32[]{:S(2)}) collective-permute-start(f32[80,256]{1,0:T(8,128)S(1)} %get-tuple-element.29), channel_id=1, source_target_pairs={{0,3},{1,2},{2,1},{3,0},{4,7},{5,6},{6,5},{7,4},{8,11},{9,10},{10,... | collective-permute-start | bytes 245768 | tf_op jit(solution)/shard_map/ppermute | solution.py:63
  63.0 1.0 collective-permute-start.16
  64.0 2.8 %collective-permute-done.14.refs_1_ = f32[80,256]{1,0:T(8,128)S(1)} collective-permute-done((f32[80,256]{1,0:T(8,128)S(1)}, f32[80,256]{1,0:T(8,128)S(1)}, u32[]{:S(2)}, u32[]{:S(2)}) %collective-permute-start.14) | collective-permute-done | bytes 81952 | tf_op jit(solution)/shard_map/ppermute | solution.py:63
  66.8 3.7 %collective-permute-done.15.refs_2_ = f32[80,256]{1,0:T(8,128)S(1)} collective-permute-done((f32[80,256]{1,0:T(8,128)S(1)}, f32[80,256]{1,0:T(8,128)S(1)}, u32[]{:S(2)}, u32[]{:S(2)}) %collective-permute-start.15) | collective-permute-done | bytes 81952 | tf_op jit(solution)/shard_map/ppermute | solution.py:63
  70.5 7.0 %reduce-scatter.2.cloned.1.call-done = f32[1,64,256]{2,1,0:T(8,128)} async-done(((f32[8,64,256]{2,1,0:T(8,128)}), f32[1,64,256]{2,1,0:T(8,128)}) %reduce-scatter.2.cloned.1.call-update) | async-done | bytes 65552 | tf_op jit(solution)/shard_map/reduce_scatter | solution.py:479
  77.5 2.1 %shard_map.81 = f32[96,256]{1,0:T(8,128)} custom-call(f32[64,256]{1,0:T(8,128)} %bitcast.24, f32[80,256]{1,0:T(8,128)} %copy-done.5, f32[80,256]{1,0:T(8,128)} %copy-done.8, f32[80,256]{1,0:T(8,128)} %copy-done.9, f32[80,256]{1,0:T(8,128)} %copy-done.10), custom_call_target="tpu_custom_call" | custom-call | tf_op jit(solution)/shard_map/pallas_call | solution.py:332
  79.5 1.4 %collective-permute-start.19 = (f32[96,256]{1,0:T(8,128)}, f32[96,256]{1,0:T(8,128)S(1)}, u32[]{:S(2)}, u32[]{:S(2)}) collective-permute-start(f32[96,256]{1,0:T(8,128)} %shard_map.81), channel_id=1, source_target_pairs={{24,0},{28,4},{16,8},{20,12},{8,16},{12,20},{0,24},{4,28},{25,1},{... | collective-permute-start | bytes 294920 | tf_op jit(solution)/shard_map/ppermute | solution.py:53
  81.0 1.4 %collective-permute-start.18 = (f32[96,256]{1,0:T(8,128)}, f32[96,256]{1,0:T(8,128)S(1)}, u32[]{:S(2)}, u32[]{:S(2)}) collective-permute-start(f32[96,256]{1,0:T(8,128)} %shard_map.81), channel_id=1, source_target_pairs={{16,0},{20,4},{24,8},{28,12},{0,16},{4,20},{8,24},{12,28},{17,1},{... | collective-permute-start | bytes 294920 | tf_op jit(solution)/shard_map/ppermute | solution.py:53
  82.4 0.6 collective-permute-start.17
  83.0 3.2 %collective-permute-done.19 = f32[96,256]{1,0:T(8,128)S(1)} collective-permute-done((f32[96,256]{1,0:T(8,128)}, f32[96,256]{1,0:T(8,128)S(1)}, u32[]{:S(2)}, u32[]{:S(2)}) %collective-permute-start.19) | collective-permute-done | bytes 98336 | tf_op jit(solution)/shard_map/ppermute | solution.py:53
  87.2 0.9 pad_maximum_fusion.refs_0_
  88.2 1.7 %collective-permute-done.20.refs_1_ = f32[4,96,256]{2,1,0:T(8,128)S(1)} collective-permute-done((f32[4,96,256]{2,1,0:T(8,128)S(1)}, f32[4,96,256]{2,1,0:T(8,128)S(1)}, u32[]{:S(2)}, u32[]{:S(2)}) %collective-permute-start.20) | collective-permute-done | bytes 393248 | tf_op jit(solution)/shard_map/ppermute | solution.py:53
  89.9 3.4 %copy-done.2 = bf16[8,2048,256]{2,1,0:T(8,128)(2,1)S(1)} copy-done((bf16[8,2048,256]{2,1,0:T(8,128)(2,1)S(1)}, bf16[8,2048,256]{2,1,0:T(8,128)(2,1)}, u32[]{:S(2)}) %copy-start.2) | copy-done | bytes 8388632
  93.3 1.4 %shard_map.82 = (f32[80,256]{1,0:T(8,128)S(1)}, f32[80,256]{1,0:T(8,128)S(1)}, f32[80,256]{1,0:T(8,128)S(1)}, f32[80,256]{1,0:T(8,128)S(1)}, f32[64,64]{1,0:T(8,128)S(1)}) custom-call(f32[4,96,256]{2,1,0:T(8,128)S(1)} %pad_maximum_fusion.refs_0_, f32[4,96,256]{2,1,0:T(8,128)S(1)} %collective-permute-done.20.refs_1_, bf16[8,2048,256]{2,1,0:T(8,128)(2,1)S(1)} %copy-done.2), custom_call_target="tpu_custom_call" | custom-call | flops 1073741824 | bytes 8388608 | tf_op jit(solution)/shard_map/pallas_call | solution.py:256
  94.8 0.6 copy-done.7
  95.4 3.4 %collective-permute-start.21 = (f32[80,256]{1,0:T(8,128)S(1)}, f32[80,256]{1,0:T(8,128)S(1)}, u32[]{:S(2)}, u32[]{:S(2)}) collective-permute-start(f32[80,256]{1,0:T(8,128)S(1)} %get-tuple-element.37), channel_id=1, source_target_pairs={{0,3},{1,2},{2,1},{3,0},{4,7},{5,6},{6,5},{7,4},{8,11},{9,10},{10,... | collective-permute-start | bytes 245768 | tf_op jit(solution)/shard_map/ppermute | solution.py:63
  98.8 0.9 collective-permute-start.23
  99.8 1.8 %shard_map.83 = (f32[64,64]{1,0:T(8,128)}, f32[64,64]{1,0:T(8,128)}, f32[64,64]{1,0:T(8,128)}) custom-call(f32[64,64]{1,0:T(8,128)} %copy-done.6, f32[64,64]{1,0:T(8,128)} %copy-done.7), custom_call_target="tpu_custom_call" | custom-call | tf_op jit(solution)/shard_map/pallas_call | solution.py:429
  101.5 0.8 collective-permute-done.21
  102.3 3.9 %collective-permute-done.22 = f32[80,256]{1,0:T(8,128)S(1)} collective-permute-done((f32[80,256]{1,0:T(8,128)S(1)}, f32[80,256]{1,0:T(8,128)S(1)}, u32[]{:S(2)}, u32[]{:S(2)}) %collective-permute-start.22) | collective-permute-done | bytes 81952 | tf_op jit(solution)/shard_map/ppermute | solution.py:63
  106.2 0.6 slice.32.packed_ref
  106.8 0.7 fusion
  107.4 1.9 %shard_map.84 = f32[3,64,64]{2,1,0:T(8,128)} custom-call(f32[64,64]{1,0:T(8,128)} %get-tuple-element.33.start_ref, f32[64,64]{1,0:T(8,128)} %get-tuple-element.34.both_ref, f32[64,64]{1,0:T(8,128)} %get-tuple-element.35.rest_ref, f32[16,256]{1,0:T(8,128)} %slice.32.packed_ref), custom_call_target="tpu_custom_call" | custom-call | tf_op jit(solution)/shard_map/pallas_call | solution.py:431
  (45 shorter events, 3.6 us)
Async XLA Ops:
  7.2 30.5 %copy-start.4 = (f32[64,256]{1,0:T(8,128)S(1)}, f32[64,256]{1,0:T(8,128)}, u32[]{:S(2)}) copy-start(f32[64,256]{1,0:T(8,128)} %refs_2_.4) | copy-start | bytes 196612
  7.2 70.3 %reduce-scatter.2.cloned.1.call-start = ((), (), s32[]{:S(2)}) async-start(), calls=%async_computation.1 | async-start | bytes 589824 | tf_op jit(solution)/shard_map/reduce_scatter | solution.py:479
  7.2 8.9 %collective-permute-start.4 = (f32[64,256]{1,0:T(8,128)}, f32[64,256]{1,0:T(8,128)S(1)}, u32[]{:S(2)}, u32[]{:S(2)}) collective-permute-start(f32[64,256]{1,0:T(8,128)} %refs_2_.4), channel_id=1, source_target_pairs={{2,0},{3,1},{0,2},{1,3},{6,4},{7,5},{4,6},{5,7},{10,8},{11,9},{8,1... | collective-permute-start | bytes 196616 | tf_op jit(solution)/shard_map/ppermute | solution.py:53
  11.3 10.6 %collective-permute-start.3 = (f32[64,256]{1,0:T(8,128)}, f32[64,256]{1,0:T(8,128)S(1)}, u32[]{:S(2)}, u32[]{:S(2)}) collective-permute-start(f32[64,256]{1,0:T(8,128)} %refs_2_.4), channel_id=1, source_target_pairs={{1,0},{0,1},{3,2},{2,3},{5,4},{4,5},{7,6},{6,7},{9,8},{8,9},{11,10... | collective-permute-start | bytes 196616 | tf_op jit(solution)/shard_map/ppermute | solution.py:53
  12.9 11.4 %collective-permute-start.5 = (f32[64,256]{1,0:T(8,128)}, f32[64,256]{1,0:T(8,128)S(1)}, u32[]{:S(2)}, u32[]{:S(2)}) collective-permute-start(f32[64,256]{1,0:T(8,128)} %refs_2_.4), channel_id=1, source_target_pairs={{3,0},{2,1},{1,2},{0,3},{7,4},{6,5},{5,6},{4,7},{11,8},{10,9},{9,1... | collective-permute-start | bytes 196616 | tf_op jit(solution)/shard_map/ppermute | solution.py:53
  12.9 13.1 %collective-permute-start = (f32[64,256]{1,0:T(8,128)}, f32[64,256]{1,0:T(8,128)S(1)}, u32[]{:S(2)}, u32[]{:S(2)}) collective-permute-start(f32[64,256]{1,0:T(8,128)} %param.11), channel_id=1, source_target_pairs={{8,0},{12,4},{0,8},{4,12},{24,16},{28,20},{16,24},{20,28},{9,1},{1... | collective-permute-start | bytes 196616 | tf_op jit(solution)/shard_map/ppermute | solution.py:53
  14.6 11.4 %collective-permute-start.2 = (f32[64,256]{1,0:T(8,128)}, f32[64,256]{1,0:T(8,128)S(1)}, u32[]{:S(2)}, u32[]{:S(2)}) collective-permute-start(f32[64,256]{1,0:T(8,128)} %param.11), channel_id=1, source_target_pairs={{24,0},{28,4},{16,8},{20,12},{8,16},{12,20},{0,24},{4,28},{25,1},{... | collective-permute-start | bytes 196616 | tf_op jit(solution)/shard_map/ppermute | solution.py:53
  16.1 9.9 %collective-permute-start.1 = (f32[64,256]{1,0:T(8,128)}, f32[64,256]{1,0:T(8,128)S(1)}, u32[]{:S(2)}, u32[]{:S(2)}) collective-permute-start(f32[64,256]{1,0:T(8,128)} %param.11), channel_id=1, source_target_pairs={{16,0},{20,4},{24,8},{28,12},{0,16},{4,20},{8,24},{12,28},{17,1},{... | collective-permute-start | bytes 196616 | tf_op jit(solution)/shard_map/ppermute | solution.py:53
  20.5 17.2 %copy-start = (bf16[8,2048,256]{2,1,0:T(8,128)(2,1)}, bf16[8,2048,256]{2,1,0:T(8,128)(2,1)S(1)}, u32[]{:S(2)}) copy-start(bf16[8,2048,256]{2,1,0:T(8,128)(2,1)S(1)} %get-tuple-element.22.refs_6_.refs_4_.refs_2_) | copy-start | bytes 25165828
  26.9 1.6 %collective-permute-start.6 = (f32[4,64,256]{2,1,0:T(8,128)S(1)}, f32[4,64,256]{2,1,0:T(8,128)S(1)}, u32[]{:S(2)}, u32[]{:S(2)}) collective-permute-start(f32[4,64,256]{2,1,0:T(8,128)S(1)} %maximum_add_fusion.refs_0_), channel_id=1, source_target_pairs={{4,0},{0,4},{12,8},{8,12},{20,16},{16,20},{28,24},{24,28},{5,1},{1... | collective-permute-start | bytes 786440 | tf_op jit(solution)/shard_map/ppermute | solution.py:53
  28.5 0.8 copy-start.3
  31.6 11.5 %collective-permute-start.7 = (f32[80,256]{1,0:T(8,128)S(1)}, f32[80,256]{1,0:T(8,128)S(1)}, u32[]{:S(2)}, u32[]{:S(2)}) collective-permute-start(f32[80,256]{1,0:T(8,128)S(1)} %get-tuple-element.24), channel_id=1, source_target_pairs={{0,3},{1,2},{2,1},{3,0},{4,7},{5,6},{6,5},{7,4},{8,11},{9,10},{10,... | collective-permute-start | bytes 245768 | tf_op jit(solution)/shard_map/ppermute | solution.py:63
  37.1 6.4 %collective-permute-start.8 = (f32[80,256]{1,0:T(8,128)S(1)}, f32[80,256]{1,0:T(8,128)S(1)}, u32[]{:S(2)}, u32[]{:S(2)}) collective-permute-start(f32[80,256]{1,0:T(8,128)S(1)} %get-tuple-element.25), channel_id=1, source_target_pairs={{0,2},{1,3},{2,0},{3,1},{4,6},{5,7},{6,4},{7,5},{8,10},{9,11},{10,... | collective-permute-start | bytes 245768 | tf_op jit(solution)/shard_map/ppermute | solution.py:63
  37.1 6.4 %collective-permute-start.9 = (f32[80,256]{1,0:T(8,128)S(1)}, f32[80,256]{1,0:T(8,128)S(1)}, u32[]{:S(2)}, u32[]{:S(2)}) collective-permute-start(f32[80,256]{1,0:T(8,128)S(1)} %get-tuple-element.26), channel_id=1, source_target_pairs={{0,1},{1,0},{2,3},{3,2},{4,5},{5,4},{6,7},{7,6},{8,9},{9,8},{10,11... | collective-permute-start | bytes 245768 | tf_op jit(solution)/shard_map/ppermute | solution.py:63
  43.4 5.9 %collective-permute-start.12 = (f32[80,256]{1,0:T(8,128)S(1)}, f32[80,256]{1,0:T(8,128)S(1)}, u32[]{:S(2)}, u32[]{:S(2)}) collective-permute-start(f32[80,256]{1,0:T(8,128)S(1)} %add_add_fusion.1), channel_id=1, source_target_pairs={{24,0},{28,4},{16,8},{20,12},{8,16},{12,20},{0,24},{4,28},{25,1},{... | collective-permute-start | bytes 245768 | tf_op jit(solution)/shard_map/ppermute | solution.py:53
  44.9 5.5 %collective-permute-start.11 = (f32[80,256]{1,0:T(8,128)S(1)}, f32[80,256]{1,0:T(8,128)S(1)}, u32[]{:S(2)}, u32[]{:S(2)}) collective-permute-start(f32[80,256]{1,0:T(8,128)S(1)} %add_add_fusion.1), channel_id=1, source_target_pairs={{16,0},{20,4},{24,8},{28,12},{0,16},{4,20},{8,24},{12,28},{17,1},{... | collective-permute-start | bytes 245768 | tf_op jit(solution)/shard_map/ppermute | solution.py:53
  46.5 4.4 %collective-permute-start.10 = (f32[80,256]{1,0:T(8,128)S(1)}, f32[80,256]{1,0:T(8,128)S(1)}, u32[]{:S(2)}, u32[]{:S(2)}) collective-permute-start(f32[80,256]{1,0:T(8,128)S(1)} %add_add_fusion.1), channel_id=1, source_target_pairs={{8,0},{12,4},{0,8},{4,12},{24,16},{28,20},{16,24},{20,28},{9,1},{1... | collective-permute-start | bytes 245768 | tf_op jit(solution)/shard_map/ppermute | solution.py:53
  50.9 1.7 %collective-permute-start.13 = (f32[4,80,256]{2,1,0:T(8,128)S(1)}, f32[4,80,256]{2,1,0:T(8,128)S(1)}, u32[]{:S(2)}, u32[]{:S(2)}) collective-permute-start(f32[4,80,256]{2,1,0:T(8,128)S(1)} %pad_maximum_fusion.1.refs_0_), channel_id=1, source_target_pairs={{4,0},{0,4},{12,8},{8,12},{20,16},{16,20},{28,24},{24,28},{5,1},{1... | collective-permute-start | bytes 983048 | tf_op jit(solution)/shard_map/ppermute | solution.py:53
  52.6 3.5 %copy-start.1 = (bf16[8,2048,256]{2,1,0:T(8,128)(2,1)S(1)}, bf16[8,2048,256]{2,1,0:T(8,128)(2,1)}, u32[]{:S(2)}) copy-start(bf16[8,2048,256]{2,1,0:T(8,128)(2,1)} %copy-done) | copy-start | bytes 25165828
  58.3 0.6 copy-start.5
  59.0 0.6 copy-start.6
  59.6 7.2 %collective-permute-start.14 = (f32[80,256]{1,0:T(8,128)S(1)}, f32[80,256]{1,0:T(8,128)S(1)}, u32[]{:S(2)}, u32[]{:S(2)}) collective-permute-start(f32[80,256]{1,0:T(8,128)S(1)} %get-tuple-element.29), channel_id=1, source_target_pairs={{0,3},{1,2},{2,1},{3,0},{4,7},{5,6},{6,5},{7,4},{8,11},{9,10},{10,... | collective-permute-start | bytes 245768 | tf_op jit(solution)/shard_map/ppermute | solution.py:63
  63.0 7.5 %collective-permute-start.15 = (f32[80,256]{1,0:T(8,128)S(1)}, f32[80,256]{1,0:T(8,128)S(1)}, u32[]{:S(2)}, u32[]{:S(2)}) collective-permute-start(f32[80,256]{1,0:T(8,128)S(1)} %get-tuple-element.30), channel_id=1, source_target_pairs={{0,2},{1,3},{2,0},{3,1},{4,6},{5,7},{6,4},{7,5},{8,10},{9,11},{10,... | collective-permute-start | bytes 245768 | tf_op jit(solution)/shard_map/ppermute | solution.py:63
  63.0 7.5 %collective-permute-start.16 = (f32[80,256]{1,0:T(8,128)S(1)}, f32[80,256]{1,0:T(8,128)S(1)}, u32[]{:S(2)}, u32[]{:S(2)}) collective-permute-start(f32[80,256]{1,0:T(8,128)S(1)} %get-tuple-element.31), channel_id=1, source_target_pairs={{0,1},{1,0},{2,3},{3,2},{4,5},{5,4},{6,7},{7,6},{8,9},{9,8},{10,11... | collective-permute-start | bytes 245768 | tf_op jit(solution)/shard_map/ppermute | solution.py:63
  66.8 10.7 %copy-start.8 = (f32[80,256]{1,0:T(8,128)}, f32[80,256]{1,0:T(8,128)S(1)}, u32[]{:S(2)}) copy-start(f32[80,256]{1,0:T(8,128)S(1)} %collective-permute-done.14.refs_1_) | copy-start | bytes 245764
  70.4 7.0 %copy-start.9 = (f32[80,256]{1,0:T(8,128)}, f32[80,256]{1,0:T(8,128)S(1)}, u32[]{:S(2)}) copy-start(f32[80,256]{1,0:T(8,128)S(1)} %collective-permute-done.15.refs_2_) | copy-start | bytes 245764
  70.5 7.0 %copy-start.10 = (f32[80,256]{1,0:T(8,128)}, f32[80,256]{1,0:T(8,128)S(1)}, u32[]{:S(2)}) copy-start(f32[80,256]{1,0:T(8,128)S(1)} %collective-permute-done.16.refs_3_) | copy-start | bytes 245764
  79.5 6.7 %collective-permute-start.19 = (f32[96,256]{1,0:T(8,128)}, f32[96,256]{1,0:T(8,128)S(1)}, u32[]{:S(2)}, u32[]{:S(2)}) collective-permute-start(f32[96,256]{1,0:T(8,128)} %shard_map.81), channel_id=1, source_target_pairs={{24,0},{28,4},{16,8},{20,12},{8,16},{12,20},{0,24},{4,28},{25,1},{... | collective-permute-start | bytes 294920 | tf_op jit(solution)/shard_map/ppermute | solution.py:53
  81.0 5.8 %collective-permute-start.18 = (f32[96,256]{1,0:T(8,128)}, f32[96,256]{1,0:T(8,128)S(1)}, u32[]{:S(2)}, u32[]{:S(2)}) collective-permute-start(f32[96,256]{1,0:T(8,128)} %shard_map.81), channel_id=1, source_target_pairs={{16,0},{20,4},{24,8},{28,12},{0,16},{4,20},{8,24},{12,28},{17,1},{... | collective-permute-start | bytes 294920 | tf_op jit(solution)/shard_map/ppermute | solution.py:53
  82.4 4.8 %collective-permute-start.17 = (f32[96,256]{1,0:T(8,128)}, f32[96,256]{1,0:T(8,128)S(1)}, u32[]{:S(2)}, u32[]{:S(2)}) collective-permute-start(f32[96,256]{1,0:T(8,128)} %shard_map.81), channel_id=1, source_target_pairs={{8,0},{12,4},{0,8},{4,12},{24,16},{28,20},{16,24},{20,28},{9,1},{1... | collective-permute-start | bytes 294920 | tf_op jit(solution)/shard_map/ppermute | solution.py:53
  88.2 1.8 %collective-permute-start.20 = (f32[4,96,256]{2,1,0:T(8,128)S(1)}, f32[4,96,256]{2,1,0:T(8,128)S(1)}, u32[]{:S(2)}, u32[]{:S(2)}) collective-permute-start(f32[4,96,256]{2,1,0:T(8,128)S(1)} %pad_maximum_fusion.refs_0_), channel_id=1, source_target_pairs={{4,0},{0,4},{12,8},{8,12},{20,16},{16,20},{28,24},{24,28},{5,1},{1... | collective-permute-start | bytes 1179656 | tf_op jit(solution)/shard_map/ppermute | solution.py:53
  89.9 3.4 %copy-start.2 = (bf16[8,2048,256]{2,1,0:T(8,128)(2,1)S(1)}, bf16[8,2048,256]{2,1,0:T(8,128)(2,1)}, u32[]{:S(2)}) copy-start(bf16[8,2048,256]{2,1,0:T(8,128)(2,1)} %copy-done) | copy-start | bytes 25165828
  94.7 0.6 copy-start.7
  95.4 6.9 %collective-permute-start.21 = (f32[80,256]{1,0:T(8,128)S(1)}, f32[80,256]{1,0:T(8,128)S(1)}, u32[]{:S(2)}, u32[]{:S(2)}) collective-permute-start(f32[80,256]{1,0:T(8,128)S(1)} %get-tuple-element.37), channel_id=1, source_target_pairs={{0,3},{1,2},{2,1},{3,0},{4,7},{5,6},{6,5},{7,4},{8,11},{9,10},{10,... | collective-permute-start | bytes 245768 | tf_op jit(solution)/shard_map/ppermute | solution.py:63
  98.8 7.4 %collective-permute-start.22 = (f32[80,256]{1,0:T(8,128)S(1)}, f32[80,256]{1,0:T(8,128)S(1)}, u32[]{:S(2)}, u32[]{:S(2)}) collective-permute-start(f32[80,256]{1,0:T(8,128)S(1)} %get-tuple-element.38), channel_id=1, source_target_pairs={{0,2},{1,3},{2,0},{3,1},{4,6},{5,7},{6,4},{7,5},{8,10},{9,11},{10,... | collective-permute-start | bytes 245768 | tf_op jit(solution)/shard_map/ppermute | solution.py:63
  98.8 7.4 %collective-permute-start.23 = (f32[80,256]{1,0:T(8,128)S(1)}, f32[80,256]{1,0:T(8,128)S(1)}, u32[]{:S(2)}, u32[]{:S(2)}) collective-permute-start(f32[80,256]{1,0:T(8,128)S(1)} %get-tuple-element.39), channel_id=1, source_target_pairs={{0,1},{1,0},{2,3},{3,2},{4,5},{5,4},{6,7},{7,6},{8,9},{9,8},{10,11... | collective-permute-start | bytes 245768 | tf_op jit(solution)/shard_map/ppermute | solution.py:63
Sparse Core Ops, SparseCore 0:
  42.5 34.8 reduce-scatter.1

commit v5 on v4

--- a/solution.py
+++ b/solution.py
@@ -14,7 +14,8 @@
 BASE = 256.0
 EXACT_DEPTH = 1024
 DENSE_CELLS = 4
-VMEM_LIMIT = 20 * 1024 * 1024
+VMEM_LIMIT = 16 * 1024 * 1024
+SMALL_LIMIT = 4 * 1024 * 1024
 
 
 def reduce_centered(values):
@@ -66,19 +67,42 @@
     return [pieces[0]] + came
 
 
-def zero_after(*arrays):
-    return sum(array[(0,) * array.ndim] for array in arrays) * 0.0
-
-
-def gather_in_pairs(piece, axis, *before):
+def stack_kernel(count, *refs):
+    out_ref = refs[-1]
+    for index in range(count):
+        out_ref[index] = refs[index][...]
+
+
+def stack_after(pieces, before):
+    return pl.pallas_call(
+        functools.partial(stack_kernel, len(pieces)),
+        in_specs=[pl.BlockSpec(memory_space=pltpu.VMEM)] * len(pieces)
+        + [pl.BlockSpec(memory_space=pl.ANY)] * len(before),
+        out_specs=pl.BlockSpec(memory_space=pltpu.VMEM),
+        out_shape=pltpu.VMEM((len(pieces), *pieces[0].shape), pieces[0].dtype),
+        compiler_params=pltpu.CompilerParams(vmem_limit_bytes=SMALL_LIMIT),
+    )(*in_vmem(*pieces), *before)
+
+
+def gather_in_pairs(piece, axis, before=()):
     size = lax.axis_size(axis)
     if size & (size - 1) or size == 1:
         pieces = gather_pieces(piece, axis)
         return [jnp.stack(pieces[:1])] if size == 1 else [jnp.stack(pieces[k::2]) for k in (0, 1)]
-    evens = jnp.stack([piece] + [fetch(piece, axis, shift) for shift in range(2, size, 2)])
-    if before:
-        evens = evens + zero_after(*before)
+    evens = [piece] + [fetch(piece, axis, shift) for shift in range(2, size, 2)]
+    evens = stack_after(evens, before) if before else jnp.stack(evens)
     return [evens, fetch(evens, axis, 1)]
+
+
+def reduce_pieces(evens, odds, axis):
+    came = None
+    if odds is not None:
+        came = fetch(odds, axis, 1)
+        evens = [even + came[index] for index, even in enumerate(evens)]
+    parts = [evens[0]]
+    for index in reversed(range(1, len(evens))):
+        parts.append(fetch(evens[index], axis, 2 * index))
+    return parts, came
 
 
 def piece_at(pairs, shift):
@@ -187,11 +211,11 @@
     )(rows, cols, tile_count, entries)
 
 
-def step_kernel(n_pairs, n_row, n_col, span, first, last, *refs):
+def step_kernel(n_pairs, n_row, n_col, span, first, last, n_before, *refs):
     pairs, refs = refs[:n_pairs], refs[n_pairs:]
     if not last:
         x_pieces, refs = refs[:n_col], refs[n_col:]
-    dense_ref, refs = refs[0], refs[1:]
+    dense_ref, refs = refs[0], refs[1 + n_before :]
     outs, refs = refs[:n_col], refs[n_col:]
     if not first:
         total_ref, refs = refs[0], refs[1:]
@@ -244,7 +268,7 @@
     return [pltpu.with_memory_space_constraint(array, pltpu.VMEM) for array in arrays]
 
 
-def dense_step(pairs, x_pieces, dense, first, last):
+def dense_step(pairs, x_pieces, dense, first, last, before=()):
     n_row, n_col = len(pairs) * pairs[0].shape[0], len(x_pieces)
     span, piece_len = x_pieces[0].shape
     _, depth, _ = dense.shape
@@ -254,8 +278,9 @@
         outs = outs + [jax.ShapeDtypeStruct((span, span), jnp.float32)]
     operands = in_vmem(*pairs, *([] if last else x_pieces), dense)
     results = pl.pallas_call(
-        functools.partial(step_kernel, len(pairs), n_row, n_col, span, first, last),
-        in_specs=[pl.BlockSpec(memory_space=pltpu.VMEM)] * len(operands),
+        functools.partial(step_kernel, len(pairs), n_row, n_col, span, first, last, len(before)),
+        in_specs=[pl.BlockSpec(memory_space=pltpu.VMEM)] * len(operands)
+        + [pl.BlockSpec(memory_space=pl.ANY)] * len(before),
         out_specs=[pl.BlockSpec(memory_space=pltpu.VMEM)] * len(outs),
         out_shape=outs,
         scratch_shapes=[pltpu.VMEM((2 * span, depth), jnp.bfloat16)],
@@ -263,13 +288,14 @@
         cost_estimate=pl.CostEstimate(
             flops=4 * span * dense.size, bytes_accessed=2 * dense.size, transcendentals=0
         ),
-    )(*operands)
+    )(*operands, *before)
     return list(results[:n_col]), (None if first else results[n_col])
 
 
 def left_kernel(n_col, n_row, *refs):
-    x_pieces, (dense_ref, _, out_ref) = refs[:n_col], refs[n_col:]
-    me_row = lax.axis_index("row")
+    x_pieces, dense_ref, refs = refs[:n_col], refs[n_col], refs[n_col + 2 :]
+    n_evens = (n_row + 1) // 2
+    evens, odds = refs[:n_evens], refs[n_evens:]
     row_blocks, _, width = dense_ref.shape
     tile_len = width // 2
     span, piece_len = x_pieces[0].shape
@@ -291,51 +317,61 @@
             + 256.0 * reduce_centered(by_low[:span] + by_high[span:])
             + by_low[span:]
         )
-        out_ref[partner(me_row, d, n_row)] = piece
+        if d % 2 == 0:
+            evens[d // 2][...] = piece
+        else:
+            odds[0][d // 2] = piece
 
 
 def dense_left(x_pieces, dense, after, n_row):
     n_col = len(x_pieces)
     span, piece_len = x_pieces[0].shape
-    operands = in_vmem(*x_pieces, dense, after)
-    return pl.pallas_call(
+    n_evens = (n_row + 1) // 2
+    outs = [pltpu.VMEM((span, piece_len), jnp.float32)] * n_evens
+    if n_row > 1:
+        outs = outs + [pltpu.VMEM((n_row // 2, span, piece_len), jnp.float32)]
+    results = pl.pallas_call(
         functools.partial(left_kernel, n_col, n_row),
         in_specs=[pl.BlockSpec(memory_space=pltpu.VMEM)] * (n_col + 1)
         + [pl.BlockSpec(memory_space=pl.ANY)],
-        out_specs=pl.BlockSpec(memory_space=pltpu.VMEM),
-        out_shape=jax.ShapeDtypeStruct((n_row, span, piece_len), jnp.float32),
+        out_specs=[pl.BlockSpec(memory_space=pltpu.VMEM)] * len(outs),
+        out_shape=outs,
         compiler_params=pltpu.CompilerParams(vmem_limit_bytes=VMEM_LIMIT),
         cost_estimate=pl.CostEstimate(
             flops=4 * span * dense.size, bytes_accessed=2 * dense.size, transcendentals=0
         ),
-    )(*operands)
-
-
-def append_kernel(w_ref, *refs):
-    pieces, out_ref = refs[:-1], refs[-1]
-    span = w_ref.shape[0]
-    summed = pieces[0][...]
-    for piece in pieces[1:]:
-        summed = summed + piece[...]
+    )(*in_vmem(*x_pieces, dense), after)
+    return list(results[:n_evens]), (results[n_evens] if n_row > 1 else None)
+
+
+def append_kernel(n_parts, *refs):
+    w_parts, pieces, out_ref = refs[:n_parts], refs[n_parts:-1], refs[-1]
+    span = w_parts[0].shape[0]
+    w_piece = functools.reduce(jnp.add, [part[...] for part in w_parts])
+    summed = functools.reduce(jnp.add, [piece[...] for piece in pieces])
     rows = summed.shape[0]
     out_ref[:rows, :] = summed
     products = dot_pairs(
-        stacked_digits(reduce_centered(w_ref[...])),
-        stacked_digits(reduce_centered(summed[:span])),
+        stacked_digits(reduce_centered(w_piece)), stacked_digits(reduce_centered(summed[:span]))
     )
     out_ref[rows:, :] = pack_square(projection_residues(products, span), summed.shape[1])
 
 
-def append_projection(w_piece, pieces):
-    span, piece_len = w_piece.shape
+def append_projection(w_parts, pieces):
+    span, piece_len = w_parts[0].shape
     rows = pieces[0].shape[0] + span * span // piece_len
+    operands = in_vmem(*w_parts, *pieces)
     return pl.pallas_call(
-        append_kernel,
-        out_shape=jax.ShapeDtypeStruct((rows, piece_len), jnp.float32),
-    )(w_piece, *pieces)
-
-
-def sparse_step(pairs, x_pieces, positions, a_digits, first, last):
+        functools.partial(append_kernel, len(w_parts)),
+        in_specs=[pl.BlockSpec(memory_space=pltpu.VMEM)] * len(operands),
+        out_specs=pl.BlockSpec(memory_space=pltpu.VMEM),
+        out_shape=pltpu.VMEM((rows, piece_len), jnp.float32),
+        compiler_params=pltpu.CompilerParams(vmem_limit_bytes=SMALL_LIMIT),
+    )(*operands)
+
+
+def sparse_step(pairs, x_pieces, positions, a_digits, first, last, before=()):
+    del before
     span, piece_len = x_pieces[0].shape
     pieces = [piece_at(pairs, d) for d in range(len(pairs) * pairs[0].shape[0])]
     tile_len = a_digits.shape[-1]
@@ -389,8 +425,8 @@
     residues = sparse_residues(values, positions[0], a_digits, "nti,tdik->tdnk")
     summed = sparse_sum(residues, positions[1], positions[2], piece_len // tile_len * n_row)
     pieces = reduce_centered(summed).reshape(span, n_row, piece_len)
-    order = partner(lax.axis_index("row"), jnp.arange(n_row, dtype=jnp.int32), n_row)
-    return jnp.zeros((n_row, span, piece_len)).at[order].set(jnp.moveaxis(pieces, 1, 0))
+    odds = jnp.moveaxis(pieces[:, 1::2], 1, 0) if n_row > 1 else None
+    return [pieces[:, d] for d in range(0, n_row, 2)], odds
 
 
 def multiply_mod(left, right):
@@ -426,9 +462,10 @@
 
 def sigma_update(c_1, c_2, packed_3):
     square = jax.ShapeDtypeStruct(c_1.shape, jnp.float32)
-    known = pl.pallas_call(sigma_start_kernel, out_shape=[square] * 3)(c_1, c_2)
+    params = pltpu.CompilerParams(vmem_limit_bytes=SMALL_LIMIT)
+    known = pl.pallas_call(sigma_start_kernel, out_shape=[square] * 3, compiler_params=params)(c_1, c_2)
     shape = jax.ShapeDtypeStruct((STEP_COUNT, *c_1.shape), jnp.float32)
-    return pl.pallas_call(sigma_end_kernel, out_shape=shape)(*known, packed_3)
+    return pl.pallas_call(sigma_end_kernel, out_shape=shape, compiler_params=params)(*known, packed_3)
 
 
 def sparse_tiles(tile_entries, tile_rows, tile_cols, tile_count, sizes):
@@ -463,21 +500,22 @@
         a_digits, positions = sparse_tiles(*tiles, sizes)
         multiply = functools.partial(sparse_step, positions=positions, a_digits=a_digits)
         multiply_left = functools.partial(sparse_left, positions=positions, a_digits=a_digits)
-    pairs = gather_in_pairs(block_y, "row", *before)
-    totals = []
+    pairs = gather_in_pairs(block_y, "row", before)
+    totals, before = [], []
     for step_index in range(STEP_COUNT):
         first, last = step_index == 0, step_index == STEP_COUNT - 1
-        outs, total = multiply(pairs, x_pieces, first=first, last=last)
+        outs, total = multiply(pairs, x_pieces, first=first, last=last, before=before)
         totals.append(total)
         pieces = scatter_pieces(outs, "col")
         if step_index == STEP_COUNT - 2:
-            pairs = gather_in_pairs(append_projection(w_piece, pieces), "row")
+            pairs = gather_in_pairs(append_projection(w_parts, pieces), "row")
             continue
         summed = functools.reduce(jnp.add, pieces)
+        before = []
         if first:
-            left = multiply_left(x_pieces, after=outs[0], n_row=n_row)
-            w_piece = lax.psum_scatter(left, "row")
-            summed = summed + zero_after(left)
+            evens, odds = multiply_left(x_pieces, after=outs[0], n_row=n_row)
+            w_parts, came = reduce_pieces(evens, odds, "row")
+            before = [came if odds is not None else evens[0]]
         if not last:
             pairs = gather_in_pairs(summed, "row")
     polynomial = sigma_update(totals[1], totals[2], summed[span:])

time: 117 us -> 75.2 us (0.64)
  between operations: 18 us -> 1.44 us
  local copies, waits for them, and re-layouts: 14.3 us -> 1.69 us
  waiting for transfers between devices: 31.5 us -> 23.4 us
  Pallas kernels: 18.4 us -> 13.7 us
  starting transfers between devices: 31.5 us -> 33.9 us
  other arithmetic: 2.5 us -> 0.78 us
    unnamed x22 -> x6, local copies, waits for them, and re-layouts: 9.56 us -> 1.69 us
    reduce_scatter x1 -> x0, waiting for transfers between devices: 6.99 us -> none  [local(): w_piece = lax.psum_scatter(left, 'row')]
    slice x5 -> x0, local copies, waits for them, and re-layouts: 4.11 us -> none  [zero_after(): return sum((array[(0,) * array.ndim] for array in arrays)) * 0.0]
    ppermute x15 -> x19, starting transfers between devices: 16.5 us -> 20.6 us  [fetch(): lax.ppermute(piece, axis, [(partner(i, shift, size), i) for i in range(si...]
    pallas_call x3 -> x4, Pallas kernels: 5.71 us -> 1.86 us  [the longest x1 1.09 us: sigma_update(): pl.pallas_call(sigma_end_kernel, out_shape=shape, compiler_params=params)]
    ppermute x9, starting transfers between devices: 14.9 us -> 13.3 us  [scatter_pieces(): lax.ppermute(pieces[shift], axis, [(i, partner(i, shift, size)) for i in...]
    ppermute x15 -> x19, waiting for transfers between devices: 13 us -> 12.9 us  [fetch(): lax.ppermute(piece, axis, [(partner(i, shift, size), i) for i in range(si...]
  transfers between devices with their start and end apart: 25 -> 28, of which waited for: 15 -> 14; matrix products, arithmetic and copies ran while one was open for 4% -> 0% of each run, Pallas kernels for 9% -> 11%
where the time goes in v5:
time: 75.2 us; the launch traced here: 74.9 us
  starting transfers between devices  33.9 us (45%)
  waiting for transfers between devices  23.4 us (31%)
  Pallas kernels  13.7 us (18%)
  local copies, waits for them, and re-layouts  1.69 us (2%)
  between operations  1.44 us (2%)
  other arithmetic  0.78 us (1%)
    ppermute x19, starting transfers between devices, fetch(): lax.ppermute(piece, axis, [(partner(i, shift, size), i) for i in range(si...  20.6 us
    ppermute x9, starting transfers between devices, scatter_pieces(): lax.ppermute(pieces[shift], axis, [(i, partner(i, shift, size)) for i in...  13.3 us
    ppermute x19, waiting for transfers between devices, fetch(): lax.ppermute(piece, axis, [(partner(i, shift, size), i) for i in range(si...  12.9 us
    ppermute x9, waiting for transfers between devices, scatter_pieces(): lax.ppermute(pieces[shift], axis, [(i, partner(i, shift, size)) for i in...  10.5 us
    pallas_call x3, Pallas kernels, dense_step(): pl.pallas_call(functools.partial(step_kernel, len(pairs), n_row, n_col, s...  5.87 us
    pallas_call x1, Pallas kernels, build_dense(): pl.pallas_call(functools.partial(build_kernel, (*sizes, group)), in_specs...  3.37 us
    pallas_call x1, Pallas kernels, dense_left(): pl.pallas_call(functools.partial(left_kernel, n_col, n_row), in_specs=[pl...  2.61 us
    unnamed x6, local copies, waits for them, and re-layouts  1.69 us
  transfers between devices with their start and end apart: 28, of which 14 were waited for; matrix products, arithmetic and copies ran while one was open for 0% of the time, Pallas kernels for 11%

profile of v5, /device:TPU:0, one launch (start us, length us, event | category | flops | bytes accessed | tf_op | source)
XLA Modules:
  0.0 74.9 jit_solution(3965416665805416899)
XLA Ops:
  0.6 3.0 %collective-permute-start.1 = (f32[64,256]{1,0:T(8,128)}, f32[64,256]{1,0:T(8,128)S(1)}, u32[]{:S(2)}, u32[]{:S(2)}) collective-permute-start(f32[64,256]{1,0:T(8,128)} %refs_0_.4), channel_id=1, source_target_pairs={{16,0},{20,4},{24,8},{28,12},{0,16},{4,20},{8,24},{12,28},{17,1},{... | collective-permute-start | bytes 196616 | tf_op jit(solution)/shard_map/ppermute | solution.py:54
  3.7 1.5 %collective-permute-start = (f32[64,256]{1,0:T(8,128)}, f32[64,256]{1,0:T(8,128)S(1)}, u32[]{:S(2)}, u32[]{:S(2)}) collective-permute-start(f32[64,256]{1,0:T(8,128)} %refs_0_.4), channel_id=1, source_target_pairs={{8,0},{12,4},{0,8},{4,12},{24,16},{28,20},{16,24},{20,28},{9,1},{1... | collective-permute-start | bytes 196616 | tf_op jit(solution)/shard_map/ppermute | solution.py:54
  5.2 4.0 %collective-permute-start.5 = (f32[64,256]{1,0:T(8,128)}, f32[64,256]{1,0:T(8,128)S(1)}, u32[]{:S(2)}, u32[]{:S(2)}) collective-permute-start(f32[64,256]{1,0:T(8,128)} %refs_2_.4), channel_id=1, source_target_pairs={{3,0},{2,1},{1,2},{0,3},{7,4},{6,5},{5,6},{4,7},{11,8},{10,9},{9,1... | collective-permute-start | bytes 196616 | tf_op jit(solution)/shard_map/ppermute | solution.py:54
  9.3 0.6 collective-permute-start.3
  10.5 3.4 %shard_map.77 = (bf16[8,2048,256]{2,1,0:T(8,128)(2,1)S(1)}, f32[8,128]{1,0:T(8,128)S(1)}) custom-call(s32[1,1,64]{2,1,0:T(1,128)} %refs_0_.3, s32[1,1,64]{2,1,0:T(1,128)} %refs_1_.1, s32[1,1]{1,0:T(1,128)S(6)} %copy.8.refs_2_, f32[1,1,64,128,128]{4,3,2,1,0:T(8,128)} %refs_3_.1), custom_call_target="tpu_custom_call" | custom-call | flops 8388608 | bytes 8388608 | tf_op jit(solution)/shard_map/pallas_call | solution.py:197
  13.9 0.9 %collective-permute-done.4.refs_5_.refs_4_.refs_2_ = f32[64,256]{1,0:T(8,128)S(1)} collective-permute-done((f32[64,256]{1,0:T(8,128)}, f32[64,256]{1,0:T(8,128)S(1)}, u32[]{:S(2)}, u32[]{:S(2)}) %collective-permute-start.4) | collective-permute-done | bytes 65568 | tf_op jit(solution)/shard_map/ppermute | solution.py:54
  14.8 0.8 %copy-done.2 = f32[64,256]{1,0:T(8,128)S(1)} copy-done((f32[64,256]{1,0:T(8,128)S(1)}, f32[64,256]{1,0:T(8,128)}, u32[]{:S(2)}) %copy-start.2) | copy-done | bytes 65560
  15.7 0.1 collective-permute-start.6
  15.8 1.5 %collective-permute-done.6.refs_1_ = f32[4,64,256]{2,1,0:T(8,128)S(1)} collective-permute-done((f32[4,64,256]{2,1,0:T(8,128)S(1)}, f32[4,64,256]{2,1,0:T(8,128)S(1)}, u32[]{:S(2)}, u32[]{:S(2)}) %collective-permute-start.6) | collective-permute-done | bytes 262176 | tf_op jit(solution)/shard_map/ppermute | solution.py:54
  17.3 0.8 %copy-done = f32[64,256]{1,0:T(8,128)S(1)} copy-done((f32[64,256]{1,0:T(8,128)S(1)}, f32[64,256]{1,0:T(8,128)}, u32[]{:S(2)}) %copy-start) | copy-done | bytes 65560
  18.1 2.2 %shard_map.79 = (f32[80,256]{1,0:T(8,128)S(1)}, f32[80,256]{1,0:T(8,128)S(1)}, f32[80,256]{1,0:T(8,128)S(1)}, f32[80,256]{1,0:T(8,128)S(1)}) custom-call(f32[4,64,256]{2,1,0:T(8,128)S(1)} %shard_map.78.refs_0_, f32[4,64,256]{2,1,0:T(8,128)S(1)} %collective-permute-done.6.refs_1_, f32[64,256]{1,0:T(8,128)S(1)} %copy-done, ...), custom_call_target="tpu_custom_call" | custom-call | flops 1073741824 | bytes 8388608 | tf_op jit(solution)/shard_map/pallas_call | solution.py:280
  20.4 2.9 %collective-permute-start.7 = (f32[80,256]{1,0:T(8,128)S(1)}, f32[80,256]{1,0:T(8,128)S(1)}, u32[]{:S(2)}, u32[]{:S(2)}) collective-permute-start(f32[80,256]{1,0:T(8,128)S(1)} %get-tuple-element.29), channel_id=1, source_target_pairs={{0,3},{1,2},{2,1},{3,0},{4,7},{5,6},{6,5},{7,4},{8,11},{9,10},{10,... | collective-permute-start | bytes 245768 | tf_op jit(solution)/shard_map/ppermute | solution.py:64
  23.3 1.5 %collective-permute-start.9 = (f32[80,256]{1,0:T(8,128)S(1)}, f32[80,256]{1,0:T(8,128)S(1)}, u32[]{:S(2)}, u32[]{:S(2)}) collective-permute-start(f32[80,256]{1,0:T(8,128)S(1)} %get-tuple-element.31), channel_id=1, source_target_pairs={{0,1},{1,0},{2,3},{3,2},{4,5},{5,4},{6,7},{7,6},{8,9},{9,8},{10,11... | collective-permute-start | bytes 245768 | tf_op jit(solution)/shard_map/ppermute | solution.py:64
  24.8 2.8 %collective-permute-done.7 = f32[80,256]{1,0:T(8,128)S(1)} collective-permute-done((f32[80,256]{1,0:T(8,128)S(1)}, f32[80,256]{1,0:T(8,128)S(1)}, u32[]{:S(2)}, u32[]{:S(2)}) %collective-permute-start.7) | collective-permute-done | bytes 81952 | tf_op jit(solution)/shard_map/ppermute | solution.py:64
  27.6 2.7 %collective-permute-done.8 = f32[80,256]{1,0:T(8,128)S(1)} collective-permute-done((f32[80,256]{1,0:T(8,128)S(1)}, f32[80,256]{1,0:T(8,128)S(1)}, u32[]{:S(2)}, u32[]{:S(2)}) %collective-permute-start.8) | collective-permute-done | bytes 81952 | tf_op jit(solution)/shard_map/ppermute | solution.py:64
  30.3 2.5 %collective-permute-start.12 = (f32[80,256]{1,0:T(8,128)S(1)}, f32[80,256]{1,0:T(8,128)S(1)}, u32[]{:S(2)}, u32[]{:S(2)}) collective-permute-start(f32[80,256]{1,0:T(8,128)S(1)} %add_add_fusion.1), channel_id=1, source_target_pairs={{24,0},{28,4},{16,8},{20,12},{8,16},{12,20},{0,24},{4,28},{25,1},{... | collective-permute-start | bytes 245768 | tf_op jit(solution)/shard_map/ppermute | solution.py:54
  32.8 0.5 collective-permute-start.11
  33.3 0.5 collective-permute-start.10
  33.8 2.6 %shard_map.80 = (f32[64,256]{1,0:T(8,128)S(1)}, f32[64,256]{1,0:T(8,128)S(1)}, f32[64,256]{1,0:T(8,128)S(1)}, f32[64,256]{1,0:T(8,128)S(1)}, f32[4,64,256]{2,1,0:T(8,128)S(1)}) custom-call(f32[64,256]{1,0:T(8,128)S(1)} %copy-done.1, f32[64,256]{1,0:T(8,128)S(1)} %collective-permute-done.3.refs_4_.refs_3_.refs_1_, ...), custom_call_target="tpu_custom_call" | custom-call | flops 1073741824 | bytes 8388608 | tf_op jit(solution)/shard_map/pallas_call | solution.py:333
  36.4 0.1 collective-permute-start.14
  36.5 0.9 %collective-permute-done.11 = f32[80,256]{1,0:T(8,128)S(1)} collective-permute-done((f32[80,256]{1,0:T(8,128)S(1)}, f32[80,256]{1,0:T(8,128)S(1)}, u32[]{:S(2)}, u32[]{:S(2)}) %collective-permute-start.11) | collective-permute-done | bytes 81952 | tf_op jit(solution)/shard_map/ppermute | solution.py:54
  37.4 0.3 collective-permute-done.10
  37.8 0.1 collective-permute-start.13
  37.8 0.2 collective-permute-done.14.refs_7_.refs_3_
  38.1 1.5 %collective-permute-start.17 = (f32[64,256]{1,0:T(8,128)S(1)}, f32[64,256]{1,0:T(8,128)S(1)}, u32[]{:S(2)}, u32[]{:S(2)}) collective-permute-start(f32[64,256]{1,0:T(8,128)S(1)} %get-tuple-element.50), channel_id=1, source_target_pairs={{8,0},{12,4},{0,8},{4,12},{24,16},{28,20},{16,24},{20,28},{9,1},{1... | collective-permute-start | bytes 196616 | tf_op jit(solution)/shard_map/ppermute | solution.py:54
  39.6 2.2 %shard_map.81 = (f32[80,256]{1,0:T(8,128)S(1)}, f32[80,256]{1,0:T(8,128)S(1)}, f32[80,256]{1,0:T(8,128)S(1)}, f32[80,256]{1,0:T(8,128)S(1)}, f32[64,64]{1,0:T(8,128)S(1)}) custom-call(f32[4,80,256]{2,1,0:T(8,128)S(1)} %pad_maximum_fusion.1.refs_0_, f32[4,80,256]{2,1,0:T(8,128)S(1)} %collective-permute-done.13.refs_1_, f32[64,256]{1,0:T(8,128)S(1)} %copy-done.1, ...), custom_call_target="tpu_custom_call" | custom-call | flops 1073741824 | bytes 8388608 | tf_op jit(solution)/shard_map/pallas_call | solution.py:280
  41.9 2.7 %collective-permute-start.18 = (f32[80,256]{1,0:T(8,128)S(1)}, f32[80,256]{1,0:T(8,128)S(1)}, u32[]{:S(2)}, u32[]{:S(2)}) collective-permute-start(f32[80,256]{1,0:T(8,128)S(1)} %get-tuple-element.39), channel_id=1, source_target_pairs={{0,3},{1,2},{2,1},{3,0},{4,7},{5,6},{6,5},{7,4},{8,11},{9,10},{10,... | collective-permute-start | bytes 245768 | tf_op jit(solution)/shard_map/ppermute | solution.py:64
  44.6 1.7 %collective-permute-start.20 = (f32[80,256]{1,0:T(8,128)S(1)}, f32[80,256]{1,0:T(8,128)S(1)}, u32[]{:S(2)}, u32[]{:S(2)}) collective-permute-start(f32[80,256]{1,0:T(8,128)S(1)} %get-tuple-element.41), channel_id=1, source_target_pairs={{0,1},{1,0},{2,3},{3,2},{4,5},{5,4},{6,7},{7,6},{8,9},{9,8},{10,11... | collective-permute-start | bytes 245768 | tf_op jit(solution)/shard_map/ppermute | solution.py:64
  46.3 1.5 %collective-permute-start.16 = (f32[64,256]{1,0:T(8,128)S(1)}, f32[64,256]{1,0:T(8,128)S(1)}, u32[]{:S(2)}, u32[]{:S(2)}) collective-permute-start(f32[64,256]{1,0:T(8,128)S(1)} %get-tuple-element.51), channel_id=1, source_target_pairs={{16,0},{20,4},{24,8},{28,12},{0,16},{4,20},{8,24},{12,28},{17,1},{... | collective-permute-start | bytes 196616 | tf_op jit(solution)/shard_map/ppermute | solution.py:54
  47.8 1.0 %collective-permute-start.15 = (f32[64,256]{1,0:T(8,128)S(1)}, f32[64,256]{1,0:T(8,128)S(1)}, u32[]{:S(2)}, u32[]{:S(2)}) collective-permute-start(f32[64,256]{1,0:T(8,128)S(1)} %get-tuple-element.52), channel_id=1, source_target_pairs={{24,0},{28,4},{16,8},{20,12},{8,16},{12,20},{0,24},{4,28},{25,1},{... | collective-permute-start | bytes 196616 | tf_op jit(solution)/shard_map/ppermute | solution.py:54
  48.8 2.5 %collective-permute-done.16.refs_2_ = f32[64,256]{1,0:T(8,128)S(1)} collective-permute-done((f32[64,256]{1,0:T(8,128)S(1)}, f32[64,256]{1,0:T(8,128)S(1)}, u32[]{:S(2)}, u32[]{:S(2)}) %collective-permute-start.16) | collective-permute-done | bytes 65568 | tf_op jit(solution)/shard_map/ppermute | solution.py:54
  51.3 1.7 %collective-permute-done.15.refs_1_ = f32[64,256]{1,0:T(8,128)S(1)} collective-permute-done((f32[64,256]{1,0:T(8,128)S(1)}, f32[64,256]{1,0:T(8,128)S(1)}, u32[]{:S(2)}, u32[]{:S(2)}) %collective-permute-start.15) | collective-permute-done | bytes 65568 | tf_op jit(solution)/shard_map/ppermute | solution.py:54
  53.0 0.4 shard_map.82
  53.4 1.0 %collective-permute-start.23 = (f32[96,256]{1,0:T(8,128)S(1)}, f32[96,256]{1,0:T(8,128)S(1)}, u32[]{:S(2)}, u32[]{:S(2)}) collective-permute-start(f32[96,256]{1,0:T(8,128)S(1)} %shard_map.82), channel_id=1, source_target_pairs={{24,0},{28,4},{16,8},{20,12},{8,16},{12,20},{0,24},{4,28},{25,1},{... | collective-permute-start | bytes 294920 | tf_op jit(solution)/shard_map/ppermute | solution.py:54
  54.4 1.0 %collective-permute-start.22 = (f32[96,256]{1,0:T(8,128)S(1)}, f32[96,256]{1,0:T(8,128)S(1)}, u32[]{:S(2)}, u32[]{:S(2)}) collective-permute-start(f32[96,256]{1,0:T(8,128)S(1)} %shard_map.82), channel_id=1, source_target_pairs={{16,0},{20,4},{24,8},{28,12},{0,16},{4,20},{8,24},{12,28},{17,1},{... | collective-permute-start | bytes 294920 | tf_op jit(solution)/shard_map/ppermute | solution.py:54
  55.4 1.5 %collective-permute-start.21 = (f32[96,256]{1,0:T(8,128)S(1)}, f32[96,256]{1,0:T(8,128)S(1)}, u32[]{:S(2)}, u32[]{:S(2)}) collective-permute-start(f32[96,256]{1,0:T(8,128)S(1)} %shard_map.82), channel_id=1, source_target_pairs={{8,0},{12,4},{0,8},{4,12},{24,16},{28,20},{16,24},{20,28},{9,1},{1... | collective-permute-start | bytes 294920 | tf_op jit(solution)/shard_map/ppermute | solution.py:54
  56.9 2.6 %collective-permute-done.23 = f32[96,256]{1,0:T(8,128)S(1)} collective-permute-done((f32[96,256]{1,0:T(8,128)S(1)}, f32[96,256]{1,0:T(8,128)S(1)}, u32[]{:S(2)}, u32[]{:S(2)}) %collective-permute-start.23) | collective-permute-done | bytes 98336 | tf_op jit(solution)/shard_map/ppermute | solution.py:54
  59.6 0.5 collective-permute-done.22
  60.1 0.1 collective-permute-start.24
  60.2 1.7 %collective-permute-done.24.refs_1_ = f32[4,96,256]{2,1,0:T(8,128)S(1)} collective-permute-done((f32[4,96,256]{2,1,0:T(8,128)S(1)}, f32[4,96,256]{2,1,0:T(8,128)S(1)}, u32[]{:S(2)}, u32[]{:S(2)}) %collective-permute-start.24) | collective-permute-done | bytes 393248 | tf_op jit(solution)/shard_map/ppermute | solution.py:54
  61.9 1.4 %shard_map.83 = (f32[80,256]{1,0:T(8,128)S(1)}, f32[80,256]{1,0:T(8,128)S(1)}, f32[80,256]{1,0:T(8,128)S(1)}, f32[80,256]{1,0:T(8,128)S(1)}, f32[64,64]{1,0:T(8,128)S(1)}) custom-call(f32[4,96,256]{2,1,0:T(8,128)S(1)} %pad_maximum_fusion.refs_0_, f32[4,96,256]{2,1,0:T(8,128)S(1)} %collective-permute-done.24.refs_1_, ...), custom_call_target="tpu_custom_call" | custom-call | flops 1073741824 | bytes 8388608 | tf_op jit(solution)/shard_map/pallas_call | solution.py:280
  63.3 2.7 %collective-permute-start.25 = (f32[80,256]{1,0:T(8,128)S(1)}, f32[80,256]{1,0:T(8,128)S(1)}, u32[]{:S(2)}, u32[]{:S(2)}) collective-permute-start(f32[80,256]{1,0:T(8,128)S(1)} %get-tuple-element.47), channel_id=1, source_target_pairs={{0,3},{1,2},{2,1},{3,0},{4,7},{5,6},{6,5},{7,4},{8,11},{9,10},{10,... | collective-permute-start | bytes 245768 | tf_op jit(solution)/shard_map/ppermute | solution.py:64
  66.0 1.7 %collective-permute-start.27 = (f32[80,256]{1,0:T(8,128)S(1)}, f32[80,256]{1,0:T(8,128)S(1)}, u32[]{:S(2)}, u32[]{:S(2)}) collective-permute-start(f32[80,256]{1,0:T(8,128)S(1)} %get-tuple-element.49), channel_id=1, source_target_pairs={{0,1},{1,0},{2,3},{3,2},{4,5},{5,4},{6,7},{7,6},{8,9},{9,8},{10,11... | collective-permute-start | bytes 245768 | tf_op jit(solution)/shard_map/ppermute | solution.py:64
  67.7 0.3 shard_map.84
  68.1 2.4 %collective-permute-done.25 = f32[80,256]{1,0:T(8,128)S(1)} collective-permute-done((f32[80,256]{1,0:T(8,128)S(1)}, f32[80,256]{1,0:T(8,128)S(1)}, u32[]{:S(2)}, u32[]{:S(2)}) %collective-permute-start.25) | collective-permute-done | bytes 81952 | tf_op jit(solution)/shard_map/ppermute | solution.py:64
  70.5 2.6 %collective-permute-done.26 = f32[80,256]{1,0:T(8,128)S(1)} collective-permute-done((f32[80,256]{1,0:T(8,128)S(1)}, f32[80,256]{1,0:T(8,128)S(1)}, u32[]{:S(2)}, u32[]{:S(2)}) %collective-permute-start.26) | collective-permute-done | bytes 81952 | tf_op jit(solution)/shard_map/ppermute | solution.py:64
  73.2 0.7 fusion
  73.8 1.1 %shard_map.85 = f32[3,64,64]{2,1,0:T(8,128)} custom-call(f32[64,64]{1,0:T(8,128)S(1)} %get-tuple-element.43.start_ref, f32[64,64]{1,0:T(8,128)S(1)} %get-tuple-element.44.both_ref, f32[64,64]{1,0:T(8,128)S(1)} %get-tuple-element.45.rest_ref, f32[16,256]{1,0:T(8,128)S(1)} %slice.28.packed_ref), custom_call_target="tpu_custom_call" | custom-call | tf_op jit(solution)/shard_map/pallas_call | solution.py:468
  (30 shorter events, 0.3 us)
Async XLA Ops:
  0.6 33.2 %copy-start.1 = (f32[64,256]{1,0:T(8,128)S(1)}, f32[64,256]{1,0:T(8,128)}, u32[]{:S(2)}) copy-start(f32[64,256]{1,0:T(8,128)} %refs_2_.4) | copy-start | bytes 196612
  0.6 8.6 %collective-permute-start.1 = (f32[64,256]{1,0:T(8,128)}, f32[64,256]{1,0:T(8,128)S(1)}, u32[]{:S(2)}, u32[]{:S(2)}) collective-permute-start(f32[64,256]{1,0:T(8,128)} %refs_0_.4), channel_id=1, source_target_pairs={{16,0},{20,4},{24,8},{28,12},{0,16},{4,20},{8,24},{12,28},{17,1},{... | collective-permute-start | bytes 196616 | tf_op jit(solution)/shard_map/ppermute | solution.py:54
  3.7 10.2 %collective-permute-start = (f32[64,256]{1,0:T(8,128)}, f32[64,256]{1,0:T(8,128)S(1)}, u32[]{:S(2)}, u32[]{:S(2)}) collective-permute-start(f32[64,256]{1,0:T(8,128)} %refs_0_.4), channel_id=1, source_target_pairs={{8,0},{12,4},{0,8},{4,12},{24,16},{28,20},{16,24},{20,28},{9,1},{1... | collective-permute-start | bytes 196616 | tf_op jit(solution)/shard_map/ppermute | solution.py:54
  5.2 8.7 %collective-permute-start.2 = (f32[64,256]{1,0:T(8,128)}, f32[64,256]{1,0:T(8,128)S(1)}, u32[]{:S(2)}, u32[]{:S(2)}) collective-permute-start(f32[64,256]{1,0:T(8,128)} %refs_0_.4), channel_id=1, source_target_pairs={{24,0},{28,4},{16,8},{20,12},{8,16},{12,20},{0,24},{4,28},{25,1},{... | collective-permute-start | bytes 196616 | tf_op jit(solution)/shard_map/ppermute | solution.py:54
  5.2 8.7 %collective-permute-start.5 = (f32[64,256]{1,0:T(8,128)}, f32[64,256]{1,0:T(8,128)S(1)}, u32[]{:S(2)}, u32[]{:S(2)}) collective-permute-start(f32[64,256]{1,0:T(8,128)} %refs_2_.4), channel_id=1, source_target_pairs={{3,0},{2,1},{1,2},{0,3},{7,4},{6,5},{5,6},{4,7},{11,8},{10,9},{9,1... | collective-permute-start | bytes 196616 | tf_op jit(solution)/shard_map/ppermute | solution.py:54
  9.2 5.6 %collective-permute-start.4 = (f32[64,256]{1,0:T(8,128)}, f32[64,256]{1,0:T(8,128)S(1)}, u32[]{:S(2)}, u32[]{:S(2)}) collective-permute-start(f32[64,256]{1,0:T(8,128)} %refs_2_.4), channel_id=1, source_target_pairs={{2,0},{3,1},{0,2},{1,3},{6,4},{7,5},{4,6},{5,7},{10,8},{11,9},{8,1... | collective-permute-start | bytes 196616 | tf_op jit(solution)/shard_map/ppermute | solution.py:54
  9.3 5.6 %collective-permute-start.3 = (f32[64,256]{1,0:T(8,128)}, f32[64,256]{1,0:T(8,128)S(1)}, u32[]{:S(2)}, u32[]{:S(2)}) collective-permute-start(f32[64,256]{1,0:T(8,128)} %refs_2_.4), channel_id=1, source_target_pairs={{1,0},{0,1},{3,2},{2,3},{5,4},{4,5},{7,6},{6,7},{9,8},{8,9},{11,10... | collective-permute-start | bytes 196616 | tf_op jit(solution)/shard_map/ppermute | solution.py:54
  14.8 0.8 %copy-start.2 = (f32[64,256]{1,0:T(8,128)S(1)}, f32[64,256]{1,0:T(8,128)}, u32[]{:S(2)}) copy-start(f32[64,256]{1,0:T(8,128)} %refs_0_.4) | copy-start | bytes 196612
  15.7 1.6 %collective-permute-start.6 = (f32[4,64,256]{2,1,0:T(8,128)S(1)}, f32[4,64,256]{2,1,0:T(8,128)S(1)}, u32[]{:S(2)}, u32[]{:S(2)}) collective-permute-start(f32[4,64,256]{2,1,0:T(8,128)S(1)} %shard_map.78.refs_0_), channel_id=1, source_target_pairs={{4,0},{0,4},{12,8},{8,12},{20,16},{16,20},{28,24},{24,28},{5,1},{1... | collective-permute-start | bytes 786440 | tf_op jit(solution)/shard_map/ppermute | solution.py:54
  17.3 0.8 %copy-start = (f32[64,256]{1,0:T(8,128)S(1)}, f32[64,256]{1,0:T(8,128)}, u32[]{:S(2)}) copy-start(f32[64,256]{1,0:T(8,128)} %refs_2_.4) | copy-start | bytes 196612
  20.4 7.2 %collective-permute-start.7 = (f32[80,256]{1,0:T(8,128)S(1)}, f32[80,256]{1,0:T(8,128)S(1)}, u32[]{:S(2)}, u32[]{:S(2)}) collective-permute-start(f32[80,256]{1,0:T(8,128)S(1)} %get-tuple-element.29), channel_id=1, source_target_pairs={{0,3},{1,2},{2,1},{3,0},{4,7},{5,6},{6,5},{7,4},{8,11},{9,10},{10,... | collective-permute-start | bytes 245768 | tf_op jit(solution)/shard_map/ppermute | solution.py:64
  23.3 6.9 %collective-permute-start.8 = (f32[80,256]{1,0:T(8,128)S(1)}, f32[80,256]{1,0:T(8,128)S(1)}, u32[]{:S(2)}, u32[]{:S(2)}) collective-permute-start(f32[80,256]{1,0:T(8,128)S(1)} %get-tuple-element.30), channel_id=1, source_target_pairs={{0,2},{1,3},{2,0},{3,1},{4,6},{5,7},{6,4},{7,5},{8,10},{9,11},{10,... | collective-permute-start | bytes 245768 | tf_op jit(solution)/shard_map/ppermute | solution.py:64
  23.3 6.9 %collective-permute-start.9 = (f32[80,256]{1,0:T(8,128)S(1)}, f32[80,256]{1,0:T(8,128)S(1)}, u32[]{:S(2)}, u32[]{:S(2)}) collective-permute-start(f32[80,256]{1,0:T(8,128)S(1)} %get-tuple-element.31), channel_id=1, source_target_pairs={{0,1},{1,0},{2,3},{3,2},{4,5},{5,4},{6,7},{7,6},{8,9},{9,8},{10,11... | collective-permute-start | bytes 245768 | tf_op jit(solution)/shard_map/ppermute | solution.py:64
  30.3 6.3 %collective-permute-start.12 = (f32[80,256]{1,0:T(8,128)S(1)}, f32[80,256]{1,0:T(8,128)S(1)}, u32[]{:S(2)}, u32[]{:S(2)}) collective-permute-start(f32[80,256]{1,0:T(8,128)S(1)} %add_add_fusion.1), channel_id=1, source_target_pairs={{24,0},{28,4},{16,8},{20,12},{8,16},{12,20},{0,24},{4,28},{25,1},{... | collective-permute-start | bytes 245768 | tf_op jit(solution)/shard_map/ppermute | solution.py:54
  32.8 4.6 %collective-permute-start.11 = (f32[80,256]{1,0:T(8,128)S(1)}, f32[80,256]{1,0:T(8,128)S(1)}, u32[]{:S(2)}, u32[]{:S(2)}) collective-permute-start(f32[80,256]{1,0:T(8,128)S(1)} %add_add_fusion.1), channel_id=1, source_target_pairs={{16,0},{20,4},{24,8},{28,12},{0,16},{4,20},{8,24},{12,28},{17,1},{... | collective-permute-start | bytes 245768 | tf_op jit(solution)/shard_map/ppermute | solution.py:54
  33.3 4.4 %collective-permute-start.10 = (f32[80,256]{1,0:T(8,128)S(1)}, f32[80,256]{1,0:T(8,128)S(1)}, u32[]{:S(2)}, u32[]{:S(2)}) collective-permute-start(f32[80,256]{1,0:T(8,128)S(1)} %add_add_fusion.1), channel_id=1, source_target_pairs={{8,0},{12,4},{0,8},{4,12},{24,16},{28,20},{16,24},{20,28},{9,1},{1... | collective-permute-start | bytes 245768 | tf_op jit(solution)/shard_map/ppermute | solution.py:54
  36.4 1.6 %collective-permute-start.14 = (f32[4,64,256]{2,1,0:T(8,128)S(1)}, f32[4,64,256]{2,1,0:T(8,128)S(1)}, u32[]{:S(2)}, u32[]{:S(2)}) collective-permute-start(f32[4,64,256]{2,1,0:T(8,128)S(1)} %get-tuple-element.32), channel_id=1, source_target_pairs={{4,0},{0,4},{12,8},{8,12},{20,16},{16,20},{28,24},{24,28},{5,1},{1... | collective-permute-start | bytes 786440 | tf_op jit(solution)/shard_map/ppermute | solution.py:54
  37.8 1.9 %collective-permute-start.13 = (f32[4,80,256]{2,1,0:T(8,128)S(1)}, f32[4,80,256]{2,1,0:T(8,128)S(1)}, u32[]{:S(2)}, u32[]{:S(2)}) collective-permute-start(f32[4,80,256]{2,1,0:T(8,128)S(1)} %pad_maximum_fusion.1.refs_0_), channel_id=1, source_target_pairs={{4,0},{0,4},{12,8},{8,12},{20,16},{16,20},{28,24},{24,28},{5,1},{1... | collective-permute-start | bytes 983048 | tf_op jit(solution)/shard_map/ppermute | solution.py:54
  38.1 9.8 %collective-permute-start.17 = (f32[64,256]{1,0:T(8,128)S(1)}, f32[64,256]{1,0:T(8,128)S(1)}, u32[]{:S(2)}, u32[]{:S(2)}) collective-permute-start(f32[64,256]{1,0:T(8,128)S(1)} %get-tuple-element.50), channel_id=1, source_target_pairs={{8,0},{12,4},{0,8},{4,12},{24,16},{28,20},{16,24},{20,28},{9,1},{1... | collective-permute-start | bytes 196616 | tf_op jit(solution)/shard_map/ppermute | solution.py:54
  41.9 11.1 %collective-permute-start.18 = (f32[80,256]{1,0:T(8,128)S(1)}, f32[80,256]{1,0:T(8,128)S(1)}, u32[]{:S(2)}, u32[]{:S(2)}) collective-permute-start(f32[80,256]{1,0:T(8,128)S(1)} %get-tuple-element.39), channel_id=1, source_target_pairs={{0,3},{1,2},{2,1},{3,0},{4,7},{5,6},{6,5},{7,4},{8,11},{9,10},{10,... | collective-permute-start | bytes 245768 | tf_op jit(solution)/shard_map/ppermute | solution.py:64
  44.6 8.4 %collective-permute-start.19 = (f32[80,256]{1,0:T(8,128)S(1)}, f32[80,256]{1,0:T(8,128)S(1)}, u32[]{:S(2)}, u32[]{:S(2)}) collective-permute-start(f32[80,256]{1,0:T(8,128)S(1)} %get-tuple-element.40), channel_id=1, source_target_pairs={{0,2},{1,3},{2,0},{3,1},{4,6},{5,7},{6,4},{7,5},{8,10},{9,11},{10,... | collective-permute-start | bytes 245768 | tf_op jit(solution)/shard_map/ppermute | solution.py:64
  44.6 8.4 %collective-permute-start.20 = (f32[80,256]{1,0:T(8,128)S(1)}, f32[80,256]{1,0:T(8,128)S(1)}, u32[]{:S(2)}, u32[]{:S(2)}) collective-permute-start(f32[80,256]{1,0:T(8,128)S(1)} %get-tuple-element.41), channel_id=1, source_target_pairs={{0,1},{1,0},{2,3},{3,2},{4,5},{5,4},{6,7},{7,6},{8,9},{9,8},{10,11... | collective-permute-start | bytes 245768 | tf_op jit(solution)/shard_map/ppermute | solution.py:64
  46.3 5.0 %collective-permute-start.16 = (f32[64,256]{1,0:T(8,128)S(1)}, f32[64,256]{1,0:T(8,128)S(1)}, u32[]{:S(2)}, u32[]{:S(2)}) collective-permute-start(f32[64,256]{1,0:T(8,128)S(1)} %get-tuple-element.51), channel_id=1, source_target_pairs={{16,0},{20,4},{24,8},{28,12},{0,16},{4,20},{8,24},{12,28},{17,1},{... | collective-permute-start | bytes 196616 | tf_op jit(solution)/shard_map/ppermute | solution.py:54
  47.8 5.2 %collective-permute-start.15 = (f32[64,256]{1,0:T(8,128)S(1)}, f32[64,256]{1,0:T(8,128)S(1)}, u32[]{:S(2)}, u32[]{:S(2)}) collective-permute-start(f32[64,256]{1,0:T(8,128)S(1)} %get-tuple-element.52), channel_id=1, source_target_pairs={{24,0},{28,4},{16,8},{20,12},{8,16},{12,20},{0,24},{4,28},{25,1},{... | collective-permute-start | bytes 196616 | tf_op jit(solution)/shard_map/ppermute | solution.py:54
  53.4 6.1 %collective-permute-start.23 = (f32[96,256]{1,0:T(8,128)S(1)}, f32[96,256]{1,0:T(8,128)S(1)}, u32[]{:S(2)}, u32[]{:S(2)}) collective-permute-start(f32[96,256]{1,0:T(8,128)S(1)} %shard_map.82), channel_id=1, source_target_pairs={{24,0},{28,4},{16,8},{20,12},{8,16},{12,20},{0,24},{4,28},{25,1},{... | collective-permute-start | bytes 294920 | tf_op jit(solution)/shard_map/ppermute | solution.py:54
  54.4 5.6 %collective-permute-start.22 = (f32[96,256]{1,0:T(8,128)S(1)}, f32[96,256]{1,0:T(8,128)S(1)}, u32[]{:S(2)}, u32[]{:S(2)}) collective-permute-start(f32[96,256]{1,0:T(8,128)S(1)} %shard_map.82), channel_id=1, source_target_pairs={{16,0},{20,4},{24,8},{28,12},{0,16},{4,20},{8,24},{12,28},{17,1},{... | collective-permute-start | bytes 294920 | tf_op jit(solution)/shard_map/ppermute | solution.py:54
  55.4 4.6 %collective-permute-start.21 = (f32[96,256]{1,0:T(8,128)S(1)}, f32[96,256]{1,0:T(8,128)S(1)}, u32[]{:S(2)}, u32[]{:S(2)}) collective-permute-start(f32[96,256]{1,0:T(8,128)S(1)} %shard_map.82), channel_id=1, source_target_pairs={{8,0},{12,4},{0,8},{4,12},{24,16},{28,20},{16,24},{20,28},{9,1},{1... | collective-permute-start | bytes 294920 | tf_op jit(solution)/shard_map/ppermute | solution.py:54
  60.1 1.8 %collective-permute-start.24 = (f32[4,96,256]{2,1,0:T(8,128)S(1)}, f32[4,96,256]{2,1,0:T(8,128)S(1)}, u32[]{:S(2)}, u32[]{:S(2)}) collective-permute-start(f32[4,96,256]{2,1,0:T(8,128)S(1)} %pad_maximum_fusion.refs_0_), channel_id=1, source_target_pairs={{4,0},{0,4},{12,8},{8,12},{20,16},{16,20},{28,24},{24,28},{5,1},{1... | collective-permute-start | bytes 1179656 | tf_op jit(solution)/shard_map/ppermute | solution.py:54
  63.3 7.2 %collective-permute-start.25 = (f32[80,256]{1,0:T(8,128)S(1)}, f32[80,256]{1,0:T(8,128)S(1)}, u32[]{:S(2)}, u32[]{:S(2)}) collective-permute-start(f32[80,256]{1,0:T(8,128)S(1)} %get-tuple-element.47), channel_id=1, source_target_pairs={{0,3},{1,2},{2,1},{3,0},{4,7},{5,6},{6,5},{7,4},{8,11},{9,10},{10,... | collective-permute-start | bytes 245768 | tf_op jit(solution)/shard_map/ppermute | solution.py:64
  66.0 7.2 %collective-permute-start.26 = (f32[80,256]{1,0:T(8,128)S(1)}, f32[80,256]{1,0:T(8,128)S(1)}, u32[]{:S(2)}, u32[]{:S(2)}) collective-permute-start(f32[80,256]{1,0:T(8,128)S(1)} %get-tuple-element.48), channel_id=1, source_target_pairs={{0,2},{1,3},{2,0},{3,1},{4,6},{5,7},{6,4},{7,5},{8,10},{9,11},{10,... | collective-permute-start | bytes 245768 | tf_op jit(solution)/shard_map/ppermute | solution.py:64
  66.0 7.2 %collective-permute-start.27 = (f32[80,256]{1,0:T(8,128)S(1)}, f32[80,256]{1,0:T(8,128)S(1)}, u32[]{:S(2)}, u32[]{:S(2)}) collective-permute-start(f32[80,256]{1,0:T(8,128)S(1)} %get-tuple-element.49), channel_id=1, source_target_pairs={{0,1},{1,0},{2,3},{3,2},{4,5},{5,4},{6,7},{7,6},{8,9},{9,8},{10,11... | collective-permute-start | bytes 245768 | tf_op jit(solution)/shard_map/ppermute | solution.py:64

commit v6 on v3

v6 whole, which is shorter than its diff:
```python
import functools

import jax
import jax.numpy as jnp
from jax import lax
from jax.experimental import pallas as pl
from jax.experimental.pallas import tpu as pltpu
from jax.sharding import PartitionSpec as P

STEP_COUNT = 3

MODULUS = 65521.0
HALF_MODULUS = 32760.0
BASE = 256.0
EXACT_DEPTH = 1024
DENSE_CELLS = 4
VMEM_LIMIT = 16 * 1024 * 1024
SMALL_LIMIT = 4 * 1024 * 1024


def reduce_centered(values):
    return values - MODULUS * jnp.floor(values * (1.0 / MODULUS) + 0.5)


def canonical(values):
    reduced = reduce_centered(values)
    return jnp.where(reduced < 0, reduced + MODULUS, reduced)


def balanced_digits(values):
    high = jnp.floor(values * (1.0 / BASE) + 0.5)
    return high, values - BASE * high


def stacked_digits(values):
    high, low = balanced_digits(values)
    return jnp.concatenate([high, low], 0).astype(jnp.bfloat16)


def centred_digits(residues):
    return stacked_digits(jnp.where(residues > HALF_MODULUS, residues - MODULUS, residues))


def partner(index, shift, size):
    return index ^ shift if size & (size - 1) == 0 else (index + shift) % size


def shift_of(index, other, size):
    return index ^ other if size & (size - 1) == 0 else (other - index) % size


def fetch(piece, axis, shift):
    size = lax.axis_size(axis)
    return lax.ppermute(piece, axis, [(partner(i, shift, size), i) for i in range(size)])


def scatter_pieces(pieces, axis):
    size = lax.axis_size(axis)
    came = [
        lax.ppermute(pieces[shift], axis, [(i, partner(i, shift, size)) for i in range(size)])
        for shift in reversed(range(1, size))
    ]
    return [pieces[0]] + came


def call(kernel, operands, outs, before=(), scratch=(), limit=SMALL_LIMIT, flops=0):
    def body(*refs):
        kernel(*refs[: len(operands)], *refs[len(operands) + len(before) :])

    vmem = pl.BlockSpec(memory_space=pltpu.VMEM)
    return pl.pallas_call(
        body,
        in_specs=[vmem] * len(operands) + [pl.BlockSpec(memory_space=pl.ANY)] * len(before),
        out_specs=[vmem] * len(outs),
        out_shape=outs,
        scratch_shapes=list(scratch),
        compiler_params=pltpu.CompilerParams(vmem_limit_bytes=limit),
        cost_estimate=pl.CostEstimate(flops=flops, bytes_accessed=0, transcendentals=0),
    )(*(pltpu.with_memory_space_constraint(part, pltpu.VMEM) for part in operands), *before)


def held(*shape):
    return pltpu.VMEM(shape, jnp.float32)


def stack_after(pieces, before=()):
    def kernel(*refs):
        for index, ref in enumerate(refs[:-1]):
            refs[-1][index] = ref[...]

    return call(kernel, pieces, [held(len(pieces), *pieces[0].shape)], before)[0]


def sum_after(pieces, before=()):
    def kernel(*refs):
        refs[-1][...] = functools.reduce(jnp.add, [ref[...] for ref in refs[:-1]])

    return call(kernel, pieces, [held(*pieces[0].shape)], before)[0]


def fetch_evens(piece, axis):
    return [fetch(piece, axis, shift) for shift in range(2, lax.axis_size(axis), 2)]


def gather_evens(piece, axis):
    return stack_after([piece] + fetch_evens(piece, axis))


def gather_odds(evens, axis):
    size = lax.axis_size(axis)
    assert size > 1 and size & (size - 1) == 0
    return fetch(evens, axis, 1)


def dot_pairs(left, right):
    return lax.dot_general(left, right, (((1,), (1,)), ((), ())), preferred_element_type=jnp.float32)


def combine(high, middle, low):
    return reduce_centered(15.0 * high + 256.0 * reduce_centered(middle) + low)


def pack_square(square, width):
    span = square.shape[0]
    rows = span * span // width
    return jnp.concatenate([square[j * rows : (j + 1) * rows] for j in range(width // span)], 1)


def unpack_square(packed, span):
    count = packed.shape[1] // span
    return jnp.concatenate([packed[:, j * span : (j + 1) * span] for j in range(count)], 0)


def build_kernel(sizes, *refs):
    count_ref, entries_ref, x_ref, y_ref, dense_ref, x_out, y_out, token_ref = refs[2:10]
    rows_ref, cols_ref, tiles, sems = refs[10:]
    n_row, n_col, piece_blocks, group = sizes
    _, _, slot_count, tile_len, _ = entries_ref.shape
    me_row, me_col = lax.axis_index("row"), lax.axis_index("col")
    chunk_count = slot_count // group

    def chunk(index):
        source = entries_ref.at[0, 0, pl.ds(index * group, group)]
        return pltpu.make_async_copy(source, tiles.at[pl.ds(index * group, group)], sems.at[index])

    small = [(refs[0], rows_ref), (refs[1], cols_ref), (y_ref, y_out), (x_ref, x_out)]
    small = [
        pltpu.make_async_copy(source, target, sems.at[chunk_count + index])
        for index, (source, target) in enumerate(small)
    ]
    for copy in small[:2]:
        copy.start()
    for index in range(chunk_count):
        chunk(index).start()
    for copy in small[2:]:
        copy.start()

    def clear(block, carry):
        dense_ref[block] = jnp.zeros(dense_ref.shape[1:], dense_ref.dtype)
        return carry

    lax.fori_loop(0, dense_ref.shape[0], clear, 0)
    for copy in small[:2]:
        copy.wait()

    def place(slot):
        row, col = rows_ref[0, 0, slot], cols_ref[0, 0, slot]
        row_shift = shift_of(me_col, row // piece_blocks, n_col)
        col_shift = shift_of(me_row, col // piece_blocks, n_row)
        col_place = col_shift % 2 * (n_row // 2) + col_shift // 2
        block = row_shift * piece_blocks + row % piece_blocks
        start = (col_place * piece_blocks + col % piece_blocks) * tile_len
        values = jnp.where(slot < count_ref[0, 0], tiles[slot], 0.0)
        values = jnp.where(values > HALF_MODULUS, values - MODULUS, values).T
        both = jnp.concatenate(balanced_digits(values), 1).astype(jnp.bfloat16)
        dense_ref[block, pl.ds(pl.multiple_of(start, tile_len), tile_len), :] = both

    def step(index, carry):
        chunk(index).wait()
        for offset in range(group):
            place(index * group + offset)
        return carry

    lax.fori_loop(0, chunk_count, step, 0)
    for copy in small[2:]:
        copy.wait()
    token_ref[...] = jnp.zeros_like(token_ref)


def build_dense(tiles, block_x, block_y, sizes):
    tile_rows, tile_cols, tile_count, tile_entries = tiles
    n_row, n_col, piece_blocks = sizes
    _, _, slot_count, tile_len, _ = tile_entries.shape
    group = next(size for size in (8, 4, 2, 1) if slot_count % size == 0)
    shape = (n_col * piece_blocks, n_row * piece_blocks * tile_len, 2 * tile_len)
    hbm = pl.BlockSpec(memory_space=pltpu.HBM)
    rows, cols, entries, x_piece, y_piece = (
        pltpu.with_memory_space_constraint(part, pltpu.HBM)
        for part in (tile_rows, tile_cols, tile_entries, block_x, block_y)
    )
    return pl.pallas_call(
        functools.partial(build_kernel, (*sizes, group)),
        in_specs=[hbm, hbm, pl.BlockSpec(memory_space=pltpu.SMEM), hbm, hbm, hbm],
        out_specs=[pl.BlockSpec(memory_space=pltpu.VMEM)] * 4,
        out_shape=[
            pltpu.VMEM(shape, jnp.bfloat16),
            held(*block_x.shape),
            held(*block_y.shape),
            held(8, 128),
        ],
        scratch_shapes=[
            *(pltpu.SMEM(part.shape, part.dtype) for part in (tile_rows, tile_cols)),
            pltpu.VMEM((slot_count, tile_len, tile_len), jnp.float32),
            pltpu.SemaphoreType.DMA((slot_count // group + 4,)),
        ],
        compiler_params=pltpu.CompilerParams(vmem_limit_bytes=VMEM_LIMIT),
        cost_estimate=pl.CostEstimate(
            flops=8 * tile_entries.size, bytes_accessed=8 * tile_entries.size, transcendentals=0
        ),
    )(rows, cols, tile_count, entries, x_piece, y_piece)


def half_products(half, span, pieces_ref, dense_ref, digits, block):
    _, depth, width = dense_ref.shape
    tile_len, half_depth = width // 2, depth // 2
    high = middle = low = 0.0
    for start in range(0, half_depth, EXACT_DEPTH):
        stop = min(start + EXACT_DEPTH, half_depth)
        products = jnp.dot(
            digits[:, start:stop],
            dense_ref[block, half * half_depth + start : half * half_depth + stop, :],
            preferred_element_type=jnp.float32,
        )
        products = reduce_centered(products)
        high = high + products[:span, :tile_len]
        middle = middle + products[:span, tile_len:] + products[span:, :tile_len]
        low = low + products[span:, tile_len:]
    return high, middle, low


def fill_digits(span, pieces_ref, digits):
    piece_len = pieces_ref.shape[2]
    for d in range(pieces_ref.shape[0]):
        vector = reduce_centered(pieces_ref[d, :span, :])
        digits[:, d * piece_len : (d + 1) * piece_len] = stacked_digits(vector)


def first_half_kernel(span, pieces_ref, dense_ref, sums_ref, digits):
    fill_digits(span, pieces_ref, digits)
    tile_len = dense_ref.shape[2] // 2
    for block in range(dense_ref.shape[0]):
        parts = half_products(0, span, pieces_ref, dense_ref, digits, block)
        for index, part in enumerate(parts):
            sums_ref[index, :, block * tile_len : (block + 1) * tile_len] = part


def second_half_kernel(span, n_col, pieces_ref, evens_ref, sums_ref, dense_ref, *refs):
    outs, refs = refs[:n_col], refs[n_col:]
    digits = refs[-1]
    fill_digits(span, pieces_ref, digits)
    row_blocks, _, width = dense_ref.shape
    tile_len = width // 2
    piece_blocks = row_blocks // n_col
    for e in reversed(range(n_col)):
        for sub in range(piece_blocks):
            block = e * piece_blocks + sub
            parts = half_products(1, span, pieces_ref, dense_ref, digits, block)
            parts = (
                part + sums_ref[index, :, block * tile_len : (block + 1) * tile_len]
                for index, part in enumerate(parts)
            )
            outs[e][:span, sub * tile_len : (sub + 1) * tile_len] = combine(*parts)
    if len(refs) > 1:
        packed = jnp.sum(pieces_ref[:, span:, :], 0) + jnp.sum(evens_ref[:, span:, :], 0)
        tail = outs[0].shape[0] - span
        for out in outs:
            out[span:, :] = packed[:tail]
        refs[0][...] = packed[tail:]


def dense_first(evens, span, dense):
    row_blocks, depth, width = dense.shape
    return call(
        functools.partial(first_half_kernel, span),
        [evens, dense],
        [held(3, span, row_blocks * width // 2)],
        scratch=[pltpu.VMEM((2 * span, depth // 2), jnp.bfloat16)],
        limit=VMEM_LIMIT,
        flops=2 * span * dense.size,
    )[0]


def dense_second(odds, evens, sums, span, n_col, tail, dense, before):
    _, depth, _ = dense.shape
    piece_len = odds.shape[2]
    outs = [held(span + tail, piece_len)] * n_col
    if tail:
        outs = outs + [held(odds.shape[1] - span - tail, piece_len)]
    results = call(
        functools.partial(second_half_kernel, span, n_col),
        [odds, evens, sums, dense],
        outs,
        before,
        scratch=[pltpu.VMEM((2 * span, depth // 2), jnp.bfloat16)],
        limit=VMEM_LIMIT,
        flops=2 * span * dense.size,
    )
    return list(results[:n_col]), (results[n_col] if tail else None)


def left_kernel(n_row, x_evens, x_odds, dense_ref, *refs):
    evens, odds_ref = refs[:-1], refs[-1]
    row_blocks, _, width = dense_ref.shape
    tile_len = width // 2
    _, span, piece_len = x_evens.shape
    piece_blocks = piece_len // tile_len
    x_digits = [
        centred_digits((x_odds if e % 2 else x_evens)[e // 2])
        for e in range(row_blocks // piece_blocks)
    ]
    for place in range(n_row):
        by_high = by_low = high_part = low_part = 0.0
        for block in range(row_blocks):
            sub = block % piece_blocks
            left = x_digits[block // piece_blocks][:, sub * tile_len : (sub + 1) * tile_len]
            right = dense_ref[block, place * piece_len : (place + 1) * piece_len, :]
            high_part = high_part + dot_pairs(left, right[:, :tile_len])
            low_part = low_part + dot_pairs(left, right[:, tile_len:])
            if (block + 1) * tile_len % EXACT_DEPTH == 0 or block == row_blocks - 1:
                by_high = by_high + reduce_centered(high_part)
                by_low = by_low + reduce_centered(low_part)
                high_part = low_part = 0.0
        piece = combine(by_high[:span], by_low[:span] + by_high[span:], by_low[span:])
        if place < n_row // 2:
            evens[place][...] = piece
        else:
            odds_ref[place - n_row // 2] = piece


def dense_left(x_pairs, n_row, dense, before):
    _, span, piece_len = x_pairs[0].shape
    results = call(
        functools.partial(left_kernel, n_row),
        [*x_pairs, dense],
        [held(span, piece_len)] * (n_row // 2) + [held(n_row // 2, span, piece_len)],
        before,
        limit=VMEM_LIMIT,
        flops=4 * span * dense.size,
    )
    return list(results[:-1]), results[-1]


def sparse_tiles(tiles, sizes):
    tile_rows, tile_cols, tile_count, tile_entries = tiles
    n_row, n_col, piece_blocks = sizes
    entries, rows, cols = tile_entries[0, 0], tile_rows[0, 0], tile_cols[0, 0]
    row_shift = shift_of(lax.axis_index("col"), rows // piece_blocks, n_col)
    col_shift = shift_of(lax.axis_index("row"), cols // piece_blocks, n_row)
    col_place = col_shift % 2 * (n_row // 2) + col_shift // 2
    positions = (
        row_shift * piece_blocks + rows % piece_blocks,
        col_place * piece_blocks + cols % piece_blocks,
        tile_count[0, 0],
    )
    entries = jnp.where(entries > HALF_MODULUS, entries - MODULUS, entries)
    return positions, jnp.stack(balanced_digits(entries), 1).astype(jnp.bfloat16)


def sparse_product(vector, spec, places, targets, count, blocks, a_digits):
    span, tile_len = vector.shape[0], a_digits.shape[-1]
    v_digits = stacked_digits(vector).reshape(2 * span, -1, tile_len)
    picked = jnp.take(v_digits, places, axis=1)
    products = jnp.einsum(spec, picked, a_digits, preferred_element_type=jnp.float32)
    products = reduce_centered(products)
    residues = combine(
        products[:, 0, :span],
        products[:, 0, span:] + products[:, 1, :span],
        products[:, 1, span:],
    )
    live = jnp.arange(targets.shape[0], dtype=jnp.int32) < count
    onehot = targets[None, :] == jnp.arange(blocks, dtype=jnp.int32)[:, None]
    onehot = (onehot & live[None, :]).astype(jnp.float32)
    summed = jnp.einsum("bt,twi->wbi", onehot, residues, precision=lax.Precision.HIGHEST)
    return reduce_centered(summed).reshape(span, blocks * tile_len)


def sparse_second(odds, evens, span, n_col, tail, positions, a_digits):
    rows, cols, count = positions
    pieces = [*evens, *odds]
    piece_len = pieces[0].shape[1]
    blocks = n_col * piece_len // a_digits.shape[-1]
    vector = reduce_centered(jnp.concatenate([piece[:span] for piece in pieces], 1))
    product = sparse_product(vector, "ntk,tdik->tdni", cols, rows, count, blocks, a_digits)
    outs = [product[:, e * piece_len : (e + 1) * piece_len] for e in range(n_col)]
    if not tail:
        return outs, None
    packed = functools.reduce(jnp.add, [piece[span:] for piece in pieces])
    return [jnp.concatenate([out, packed[:tail]], 0) for out in outs], packed[tail:]


def sparse_left(x_pairs, n_row, positions, a_digits):
    rows, cols, count = positions
    n_col = 2 * x_pairs[0].shape[0]
    x_pieces = [x_pairs[e % 2][e // 2] for e in range(n_col)]
    piece_len = x_pieces[0].shape[1]
    values = jnp.concatenate(x_pieces, 1)
    values = jnp.where(values > HALF_MODULUS, values - MODULUS, values)
    blocks = n_row * piece_len // a_digits.shape[-1]
    product = sparse_product(values, "nti,tdik->tdnk", rows, cols, count, blocks, a_digits)
    pieces = [product[:, d * piece_len : (d + 1) * piece_len] for d in range(n_row)]
    return pieces[: n_row // 2], jnp.stack(pieces[n_row // 2 :])


def add_came(evens, odds_came, before):
    def kernel(*refs):
        for index in range(len(evens)):
            refs[len(evens) + 1 + index][...] = refs[index][...] + refs[len(evens)][index]

    return list(call(kernel, [*evens, odds_came], [held(*evens[0].shape)] * len(evens), before))


def append_projections(w_parts, pieces, earlier):
    span, piece_len = pieces[0].shape
    rows = span * span // piece_len
    count = len(earlier) + 1

    def kernel(*refs):
        w_refs, refs = refs[: len(w_parts)], refs[len(w_parts) :]
        piece_refs, refs = refs[: len(pieces)], refs[len(pieces) :]
        out_ref = refs[-1]
        summed = functools.reduce(jnp.add, [ref[...] for ref in piece_refs])
        out_ref[:span, :] = summed
        w_piece = functools.reduce(jnp.add, [ref[...] for ref in w_refs])
        w_digits = stacked_digits(reduce_centered(w_piece))
        for index, vector in enumerate([summed] + [ref[...] for ref in refs[:-1]]):
            products = dot_pairs(w_digits, stacked_digits(reduce_centered(vector)))
            square = combine(
                reduce_centered(products[:span, :span]),
                reduce_centered(products[:span, span:]) + reduce_centered(products[span:, :span]),
                reduce_centered(products[span:, span:]),
            )
            start = span + index * rows
            out_ref[start : start + rows, :] = pack_square(square, piece_len)

    outs = [held(span + count * rows, piece_len)]
    return call(kernel, [*w_parts, *pieces, *earlier], outs)[0]


def multiply_mod(left, right):
    span = left.shape[0]
    left = stacked_digits(left)
    high, low = (part.astype(jnp.bfloat16) for part in balanced_digits(right))
    by_high = jnp.dot(left, high, preferred_element_type=jnp.float32)
    by_low = jnp.dot(left, low, preferred_element_type=jnp.float32)
    return combine(
        reduce_centered(by_high[:span]), by_low[:span] + by_high[span:], by_low[span:]
    )


def sigma_start(packed, span):
    def kernel(packed_ref, start_ref, both_ref, rest_ref):
        rows = packed_ref.shape[0] // 2
        c_1 = unpack_square(reduce_centered(packed_ref[:rows, :]), span)
        c_2 = unpack_square(reduce_centered(packed_ref[rows:, :]), span)
        e_2 = reduce_centered(c_1 - multiply_mod(c_1, c_2))
        both = reduce_centered(c_1 + e_2)
        start_ref[...] = multiply_mod(e_2, c_1)
        both_ref[...] = both
        rest_ref[...] = c_1 - multiply_mod(both, c_2)

    return call(kernel, [packed], [held(span, span)] * 3)


def finish(pieces, known, span):
    def kernel(*refs):
        piece_refs, (start_ref, both_ref, rest_ref, poly_ref, vector_ref) = refs[:-5], refs[-5:]
        summed = functools.reduce(jnp.add, [ref[...] for ref in piece_refs])
        vector_ref[...] = canonical(summed[:span]) * (1.0 / MODULUS)
        start, both = start_ref[...], both_ref[...]
        c_3 = unpack_square(reduce_centered(summed[span:]), span)
        e_3 = reduce_centered(multiply_mod(start, c_3) + rest_ref[...])
        poly_ref[0] = canonical(-multiply_mod(e_3, start)) * (1.0 / MODULUS)
        poly_ref[1] = canonical(start + multiply_mod(e_3, both)) * (1.0 / MODULUS)
        poly_ref[2] = canonical(-both - e_3) * (1.0 / MODULUS)

    outs = [
        jax.ShapeDtypeStruct((STEP_COUNT, span, span), jnp.float32),
        jax.ShapeDtypeStruct((span, pieces[0].shape[1]), jnp.float32),
    ]
    return tuple(call(kernel, [*pieces, *known], outs))


def local(tile_entries, tile_rows, tile_cols, tile_count, block_x, block_y):
    _, _, slot_count, tile_len, _ = tile_entries.shape
    span, piece_len = block_y.shape
    piece_blocks = piece_len // tile_len
    n_row, n_col = lax.axis_size("row"), lax.axis_size("col")
    packed_rows = span * span // piece_len
    tiles = (tile_rows, tile_cols, tile_count, tile_entries)
    sizes = (n_row, n_col, piece_blocks)
    is_dense = n_col * piece_blocks * n_row * piece_blocks <= DENSE_CELLS * slot_count
    if is_dense:
        dense, x_own, y_own, token = build_dense(tiles, block_x, block_y, sizes)
        before = [token]
    else:
        positions, a_digits = sparse_tiles(tiles, sizes)
        x_own, y_own, before = block_x, block_y, []

    def multiply(evens, tail=0, before=()):
        odds = gather_odds(evens, "row")
        if is_dense:
            sums = dense_first(evens, span, dense)
            return dense_second(odds, evens, sums, span, n_col, tail, dense, before)
        return sparse_second(odds, evens, span, n_col, tail, positions, a_digits)

    x_came = fetch_evens(block_x, "col")
    evens = stack_after([y_own] + fetch_evens(block_y, "row"), [*before, *x_came])
    x_evens = stack_after([x_own] + x_came)
    outs, _ = multiply(evens, before=[x_evens])
    x_pairs = [x_evens, gather_odds(x_evens, "col")]
    if is_dense:
        w_evens, w_odds = dense_left(x_pairs, n_row, dense, [outs[0]])
    else:
        w_evens, w_odds = sparse_left(x_pairs, n_row, positions, a_digits)
    vector_1 = sum_after(scatter_pieces(outs, "col"), [w_odds])
    w_came = fetch(w_odds, "row", 1)
    evens = gather_evens(vector_1, "row")
    outs, _ = multiply(evens, before=[w_came])
    pieces = scatter_pieces(outs, "col")
    w_evens = add_came(w_evens, w_came, [outs[0]])
    w_parts = [w_evens[0]] + [
        fetch(w_evens[index], "row", 2 * index) for index in reversed(range(1, n_row // 2))
    ]
    vector_2 = append_projections(w_parts, pieces, [y_own, vector_1])
    evens = gather_evens(vector_2, "row")
    outs, packed = multiply(evens, packed_rows)
    pieces = scatter_pieces(outs, "col")
    shift = 1
    while shift < n_col:
        packed = packed + fetch(packed, "col", shift)
        shift *= 2
    return finish(pieces, sigma_start(packed, span), span)


def solution(mesh):
    placed = (
        P("row", "col", None, None, None),
        P("row", "col", None),
        P("row", "col", None),
        P("row", "col"),
        P(None, ("row", "col")),
        P(None, ("row", "col")),
    )
    return jax.shard_map(
        local, mesh=mesh, in_specs=placed, out_specs=(P(), P(None, ("row", "col"))), check_vma=False
    )
```

time: 88.9 us -> 73.1 us (0.82)
  waiting for transfers between devices: 35.5 us -> 24.9 us
  local copies, waits for them, and re-layouts: 4.13 us -> 0 us
  other arithmetic: 1.63 us -> 0.01 us
    ppermute x9, waiting for transfers between devices: 16.9 us -> 2.83 us  [scatter_pieces(): lax.ppermute(pieces[shift], axis, [(i, partner(i, shift, size)) for i in...]
    unnamed x16 -> x0, local copies, waits for them, and re-layouts: 4.12 us -> none
    ppermute x19 -> x20, waiting for transfers between devices: 18.5 us -> 22.1 us  [fetch(): lax.ppermute(piece, axis, [(partner(i, shift, size), i) for i in range(si...]
    another operation x4 -> x0, other arithmetic: 0.91 us -> none  [gather_in_pairs(): jnp.stack([piece] + [fetch(piece, axis, shift) for shift in range(2, size...]
    ppermute x19 -> x20, starting transfers between devices: 19.9 us -> 20.5 us  [fetch(): lax.ppermute(piece, axis, [(partner(i, shift, size), i) for i in range(si...]
    pallas_call x4 -> x16, Pallas kernels: 9 us -> 9.18 us  [call(): pl.pallas_call(body, in_specs=[vmem] * len(operands) + [pl.BlockSpec(memo...]
  transfers between devices with their start and end apart: 28 -> 29, of which waited for: 20 -> 16; matrix products, arithmetic and copies ran while one was open for 1% -> 0% of each run, Pallas kernels for 4% -> 13%
where the time goes in v6:
time: 73.1 us; the launch traced here: 72.9 us
  starting transfers between devices  33.8 us (46%)
  waiting for transfers between devices  24.9 us (34%)
  Pallas kernels  12.7 us (17%)
  between operations  1.5 us (2%)
    ppermute x20, waiting for transfers between devices, fetch(): lax.ppermute(piece, axis, [(partner(i, shift, size), i) for i in range(si...  22.1 us
    ppermute x20, starting transfers between devices, fetch(): lax.ppermute(piece, axis, [(partner(i, shift, size), i) for i in range(si...  20.5 us
    ppermute x9, starting transfers between devices, scatter_pieces(): lax.ppermute(pieces[shift], axis, [(i, partner(i, shift, size)) for i in...  13.4 us
    pallas_call x16, Pallas kernels, call(): pl.pallas_call(body, in_specs=[vmem] * len(operands) + [pl.BlockSpec(memo...  9.18 us
    pallas_call x1, Pallas kernels, build_dense(): pl.pallas_call(functools.partial(build_kernel, (*sizes, group)), in_specs...  3.49 us
    ppermute x9, waiting for transfers between devices, scatter_pieces(): lax.ppermute(pieces[shift], axis, [(i, partner(i, shift, size)) for i in...  2.83 us
  transfers between devices with their start and end apart: 29, of which 16 were waited for; matrix products, arithmetic and copies ran while one was open for 0% of the time, Pallas kernels for 13%

profile of v6, /device:TPU:0, one launch (start us, length us, event | category | flops | bytes accessed | tf_op | source)
XLA Modules:
  0.0 72.9 jit_solution(10433716658846717449)
XLA Ops:
  0.6 4.1 %collective-permute-start = (f32[64,256]{1,0:T(8,128)}, f32[64,256]{1,0:T(8,128)S(1)}, u32[]{:S(2)}, u32[]{:S(2)}) collective-permute-start(f32[64,256]{1,0:T(8,128)} %refs_4_.1), channel_id=1, source_target_pairs={{2,0},{3,1},{0,2},{1,3},{6,4},{7,5},{4,6},{5,7},{10,8},{11,9},{8,1... | collective-permute-start | bytes 196616 | tf_op jit(solution)/shard_map/ppermute | solution.py:54
  4.7 1.5 %collective-permute-start.2 = (f32[64,256]{1,0:T(8,128)}, f32[64,256]{1,0:T(8,128)S(1)}, u32[]{:S(2)}, u32[]{:S(2)}) collective-permute-start(f32[64,256]{1,0:T(8,128)} %refs_5_.1), channel_id=1, source_target_pairs={{8,0},{12,4},{0,8},{4,12},{24,16},{28,20},{16,24},{20,28},{9,1},{1... | collective-permute-start | bytes 196616 | tf_op jit(solution)/shard_map/ppermute | solution.py:54
  6.2 1.5 %collective-permute-start.4 = (f32[64,256]{1,0:T(8,128)}, f32[64,256]{1,0:T(8,128)S(1)}, u32[]{:S(2)}, u32[]{:S(2)}) collective-permute-start(f32[64,256]{1,0:T(8,128)} %refs_5_.1), channel_id=1, source_target_pairs={{24,0},{28,4},{16,8},{20,12},{8,16},{12,20},{0,24},{4,28},{25,1},{... | collective-permute-start | bytes 196616 | tf_op jit(solution)/shard_map/ppermute | solution.py:54
  7.7 0.5 collective-permute-start.3
  8.9 3.5 %shard_map.77 = (bf16[8,2048,256]{2,1,0:T(8,128)(2,1)S(1)}, f32[64,256]{1,0:T(8,128)S(1)}, f32[64,256]{1,0:T(8,128)S(1)}, f32[8,128]{1,0:T(8,128)S(1)}) custom-call(s32[1,1,64]{2,1,0:T(1,128)} %refs_0_.1, s32[1,1,64]{2,1,0:T(1,128)} %refs_1_.1, s32[1,1]{1,0:T(1,128)S(6)} %copy.8.refs_2_, f32[1,1,64,128,128]{4,3,2,1,0:T(8,128)} %refs_3_.1, ...), custom_call_target="tpu_custom_call" | custom-call | flops 8388608 | bytes 8388608 | tf_op jit(solution)/shard_map/pallas_call | solution.py:201
  12.5 1.6 %collective-permute-start.1 = (f32[2,64,256]{2,1,0:T(8,128)S(1)}, f32[2,64,256]{2,1,0:T(8,128)S(1)}, u32[]{:S(2)}, u32[]{:S(2)}) collective-permute-start(f32[2,64,256]{2,1,0:T(8,128)S(1)} %shard_map.78.refs_4_.refs_0_), channel_id=1, source_target_pairs={{1,0},{0,1},{3,2},{2,3},{5,4},{4,5},{7,6},{6,7},{9,8},{8,9},{11,10... | collective-permute-start | bytes 393224 | tf_op jit(solution)/shard_map/ppermute | solution.py:54
  14.2 0.8 %shard_map.80.refs_2_ = f32[3,64,1024]{2,1,0:T(8,128)S(1)} custom-call(f32[4,64,256]{2,1,0:T(8,128)S(1)} %shard_map.79.refs_0_.refs_1_, bf16[8,2048,256]{2,1,0:T(8,128)(2,1)S(1)} %get-tuple-element.32.refs_1_.refs_3_.refs_2_), custom_call_target="tpu_custom_call" | custom-call | flops 536870912 | tf_op jit(solution)/shard_map/pallas_call | solution.py:71
  15.0 0.8 %shard_map.81 = (f32[64,256]{1,0:T(8,128)S(1)}, f32[64,256]{1,0:T(8,128)S(1)}, f32[64,256]{1,0:T(8,128)S(1)}, f32[64,256]{1,0:T(8,128)S(1)}) custom-call(f32[4,64,256]{2,1,0:T(8,128)S(1)} %collective-permute-done.5.refs_0_, f32[4,64,256]{2,1,0:T(8,128)S(1)} %shard_map.79.refs_0_.refs_1_, f32[3,64,1024]{2,1,0:T(8,128)S(1)} %shard_map.80.refs_2_, ...), custom_call_target="tpu_custom_call" | custom-call | flops 536870912 | tf_op jit(solution)/shard_map/pallas_call | solution.py:71
  15.8 0.5 collective-permute-start.7
  16.3 1.7 %collective-permute-start.8 = (f32[64,256]{1,0:T(8,128)S(1)}, f32[64,256]{1,0:T(8,128)S(1)}, u32[]{:S(2)}, u32[]{:S(2)}) collective-permute-start(f32[64,256]{1,0:T(8,128)S(1)} %get-tuple-element.42), channel_id=1, source_target_pairs={{0,2},{1,3},{2,0},{3,1},{4,6},{5,7},{6,4},{7,5},{8,10},{9,11},{10,... | collective-permute-start | bytes 196616 | tf_op jit(solution)/shard_map/ppermute | solution.py:60
  18.0 2.3 %collective-permute-start.9 = (f32[64,256]{1,0:T(8,128)S(1)}, f32[64,256]{1,0:T(8,128)S(1)}, u32[]{:S(2)}, u32[]{:S(2)}) collective-permute-start(f32[64,256]{1,0:T(8,128)S(1)} %get-tuple-element.43), channel_id=1, source_target_pairs={{0,1},{1,0},{2,3},{3,2},{4,5},{5,4},{6,7},{7,6},{8,9},{9,8},{10,11... | collective-permute-start | bytes 196616 | tf_op jit(solution)/shard_map/ppermute | solution.py:60
  20.2 2.4 %shard_map.82 = (f32[64,256]{1,0:T(8,128)S(1)}, f32[64,256]{1,0:T(8,128)S(1)}, f32[64,256]{1,0:T(8,128)S(1)}, f32[64,256]{1,0:T(8,128)S(1)}, f32[4,64,256]{2,1,0:T(8,128)S(1)}) custom-call(f32[2,64,256]{2,1,0:T(8,128)S(1)} %shard_map.78.refs_4_.refs_0_, f32[2,64,256]{2,1,0:T(8,128)S(1)} %collective-permute-done.1.refs_1_, ...), custom_call_target="tpu_custom_call" | custom-call | flops 1073741824 | tf_op jit(solution)/shard_map/pallas_call | solution.py:71
  22.6 1.8 %collective-permute-done.8.refs_2_ = f32[64,256]{1,0:T(8,128)S(1)} collective-permute-done((f32[64,256]{1,0:T(8,128)S(1)}, f32[64,256]{1,0:T(8,128)S(1)}, u32[]{:S(2)}, u32[]{:S(2)}) %collective-permute-start.8) | collective-permute-done | bytes 65568 | tf_op jit(solution)/shard_map/ppermute | solution.py:60
  24.4 2.5 %collective-permute-start.12 = (f32[64,256]{1,0:T(8,128)S(1)}, f32[64,256]{1,0:T(8,128)S(1)}, u32[]{:S(2)}, u32[]{:S(2)}) collective-permute-start(f32[64,256]{1,0:T(8,128)S(1)} %shard_map.83.refs_0_.refs_9_), channel_id=1, source_target_pairs={{24,0},{28,4},{16,8},{20,12},{8,16},{12,20},{0,24},{4,28},{25,1},{... | collective-permute-start | bytes 196616 | tf_op jit(solution)/shard_map/ppermute | solution.py:54
  26.9 0.5 collective-permute-start.11
  27.5 0.5 collective-permute-start.10
  28.0 1.8 %collective-permute-done.12.refs_3_ = f32[64,256]{1,0:T(8,128)S(1)} collective-permute-done((f32[64,256]{1,0:T(8,128)S(1)}, f32[64,256]{1,0:T(8,128)S(1)}, u32[]{:S(2)}, u32[]{:S(2)}) %collective-permute-start.12) | collective-permute-done | bytes 65568 | tf_op jit(solution)/shard_map/ppermute | solution.py:54
  29.8 1.4 %collective-permute-done.11.refs_2_ = f32[64,256]{1,0:T(8,128)S(1)} collective-permute-done((f32[64,256]{1,0:T(8,128)S(1)}, f32[64,256]{1,0:T(8,128)S(1)}, u32[]{:S(2)}, u32[]{:S(2)}) %collective-permute-start.11) | collective-permute-done | bytes 65568 | tf_op jit(solution)/shard_map/ppermute | solution.py:54
  31.2 0.5 collective-permute-done.10.refs_1_
  31.8 0.8 %shard_map.85.refs_2_ = f32[3,64,1024]{2,1,0:T(8,128)S(1)} custom-call(f32[4,64,256]{2,1,0:T(8,128)S(1)} %shard_map.84.refs_0_.refs_1_, bf16[8,2048,256]{2,1,0:T(8,128)(2,1)S(1)} %get-tuple-element.32.refs_1_.refs_3_.refs_2_), custom_call_target="tpu_custom_call" | custom-call | flops 536870912 | tf_op jit(solution)/shard_map/pallas_call | solution.py:71
  32.6 0.8 %collective-permute-done.13.refs_0_ = f32[4,64,256]{2,1,0:T(8,128)S(1)} collective-permute-done((f32[4,64,256]{2,1,0:T(8,128)S(1)}, f32[4,64,256]{2,1,0:T(8,128)S(1)}, u32[]{:S(2)}, u32[]{:S(2)}) %collective-permute-start.13) | collective-permute-done | bytes 262176 | tf_op jit(solution)/shard_map/ppermute | solution.py:54
  33.3 0.8 %shard_map.86 = (f32[64,256]{1,0:T(8,128)S(1)}, f32[64,256]{1,0:T(8,128)S(1)}, f32[64,256]{1,0:T(8,128)S(1)}, f32[64,256]{1,0:T(8,128)S(1)}) custom-call(f32[4,64,256]{2,1,0:T(8,128)S(1)} %collective-permute-done.13.refs_0_, f32[4,64,256]{2,1,0:T(8,128)S(1)} %shard_map.84.refs_0_.refs_1_, f32[3,64,1024]{2,1,0:T(8,128)S(1)} %shard_map.85.refs_2_, ...), custom_call_target="tpu_custom_call" | custom-call | flops 536870912 | tf_op jit(solution)/shard_map/pallas_call | solution.py:71
  34.1 1.7 %collective-permute-start.17 = (f32[64,256]{1,0:T(8,128)S(1)}, f32[64,256]{1,0:T(8,128)S(1)}, u32[]{:S(2)}, u32[]{:S(2)}) collective-permute-start(f32[64,256]{1,0:T(8,128)S(1)} %get-tuple-element.49), channel_id=1, source_target_pairs={{0,3},{1,2},{2,1},{3,0},{4,7},{5,6},{6,5},{7,4},{8,11},{9,10},{10,... | collective-permute-start | bytes 196616 | tf_op jit(solution)/shard_map/ppermute | solution.py:60
  35.9 2.7 %collective-permute-start.19 = (f32[64,256]{1,0:T(8,128)S(1)}, f32[64,256]{1,0:T(8,128)S(1)}, u32[]{:S(2)}, u32[]{:S(2)}) collective-permute-start(f32[64,256]{1,0:T(8,128)S(1)} %get-tuple-element.51), channel_id=1, source_target_pairs={{0,1},{1,0},{2,3},{3,2},{4,5},{5,4},{6,7},{7,6},{8,9},{9,8},{10,11... | collective-permute-start | bytes 196616 | tf_op jit(solution)/shard_map/ppermute | solution.py:60
  38.6 1.6 %collective-permute-start.14 = (f32[64,256]{1,0:T(8,128)S(1)}, f32[64,256]{1,0:T(8,128)S(1)}, u32[]{:S(2)}, u32[]{:S(2)}) collective-permute-start(f32[64,256]{1,0:T(8,128)S(1)} %get-tuple-element.46), channel_id=1, source_target_pairs={{24,0},{28,4},{16,8},{20,12},{8,16},{12,20},{0,24},{4,28},{25,1},{... | collective-permute-start | bytes 196616 | tf_op jit(solution)/shard_map/ppermute | solution.py:54
  40.2 0.5 collective-permute-start.15
  40.7 0.3 collective-permute-done.17.refs_5_
  41.0 1.2 %collective-permute-start.16 = (f32[64,256]{1,0:T(8,128)S(1)}, f32[64,256]{1,0:T(8,128)S(1)}, u32[]{:S(2)}, u32[]{:S(2)}) collective-permute-start(f32[64,256]{1,0:T(8,128)S(1)} %get-tuple-element.48), channel_id=1, source_target_pairs={{8,0},{12,4},{0,8},{4,12},{24,16},{28,20},{16,24},{20,28},{9,1},{1... | collective-permute-start | bytes 196616 | tf_op jit(solution)/shard_map/ppermute | solution.py:54
  42.2 0.8 %collective-permute-done.18.refs_6_ = f32[64,256]{1,0:T(8,128)S(1)} collective-permute-done((f32[64,256]{1,0:T(8,128)S(1)}, f32[64,256]{1,0:T(8,128)S(1)}, u32[]{:S(2)}, u32[]{:S(2)}) %collective-permute-start.18) | collective-permute-done | bytes 65568 | tf_op jit(solution)/shard_map/ppermute | solution.py:60
  43.0 1.5 %collective-permute-done.14.refs_1_ = f32[64,256]{1,0:T(8,128)S(1)} collective-permute-done((f32[64,256]{1,0:T(8,128)S(1)}, f32[64,256]{1,0:T(8,128)S(1)}, u32[]{:S(2)}, u32[]{:S(2)}) %collective-permute-start.14) | collective-permute-done | bytes 65568 | tf_op jit(solution)/shard_map/ppermute | solution.py:54
  44.5 0.4 collective-permute-done.15.refs_2_
  44.9 0.4 collective-permute-done.16.refs_3_
  45.2 0.5 shard_map.88.refs_0_
  45.7 2.3 %collective-permute-start.22 = (f32[112,256]{1,0:T(8,128)S(1)}, f32[112,256]{1,0:T(8,128)S(1)}, u32[]{:S(2)}, u32[]{:S(2)}) collective-permute-start(f32[112,256]{1,0:T(8,128)S(1)} %shard_map.88.refs_0_), channel_id=1, source_target_pairs={{24,0},{28,4},{16,8},{20,12},{8,16},{12,20},{0,24},{4,28},{25,1},{... | collective-permute-start | bytes 344072 | tf_op jit(solution)/shard_map/ppermute | solution.py:54
  48.0 0.5 collective-permute-start.21
  48.5 0.8 %collective-permute-start.20 = (f32[112,256]{1,0:T(8,128)S(1)}, f32[112,256]{1,0:T(8,128)S(1)}, u32[]{:S(2)}, u32[]{:S(2)}) collective-permute-start(f32[112,256]{1,0:T(8,128)S(1)} %shard_map.88.refs_0_), channel_id=1, source_target_pairs={{8,0},{12,4},{0,8},{4,12},{24,16},{28,20},{16,24},{20,28},{9,1},{1... | collective-permute-start | bytes 344072 | tf_op jit(solution)/shard_map/ppermute | solution.py:54
  49.3 2.6 %collective-permute-done.22.refs_3_ = f32[112,256]{1,0:T(8,128)S(1)} collective-permute-done((f32[112,256]{1,0:T(8,128)S(1)}, f32[112,256]{1,0:T(8,128)S(1)}, u32[]{:S(2)}, u32[]{:S(2)}) %collective-permute-start.22) | collective-permute-done | bytes 114720 | tf_op jit(solution)/shard_map/ppermute | solution.py:54
  51.8 1.2 %collective-permute-done.21.refs_2_ = f32[112,256]{1,0:T(8,128)S(1)} collective-permute-done((f32[112,256]{1,0:T(8,128)S(1)}, f32[112,256]{1,0:T(8,128)S(1)}, u32[]{:S(2)}, u32[]{:S(2)}) %collective-permute-start.21) | collective-permute-done | bytes 114720 | tf_op jit(solution)/shard_map/ppermute | solution.py:54
  53.4 0.8 %shard_map.90.refs_2_ = f32[3,64,1024]{2,1,0:T(8,128)S(1)} custom-call(f32[4,112,256]{2,1,0:T(8,128)S(1)} %shard_map.89.refs_0_.refs_1_, bf16[8,2048,256]{2,1,0:T(8,128)(2,1)S(1)} %get-tuple-element.32.refs_1_.refs_3_.refs_2_), custom_call_target="tpu_custom_call" | custom-call | flops 536870912 | tf_op jit(solution)/shard_map/pallas_call | solution.py:71
  54.1 1.0 %collective-permute-done.23.refs_0_ = f32[4,112,256]{2,1,0:T(8,128)S(1)} collective-permute-done((f32[4,112,256]{2,1,0:T(8,128)S(1)}, f32[4,112,256]{2,1,0:T(8,128)S(1)}, u32[]{:S(2)}, u32[]{:S(2)}) %collective-permute-start.23) | collective-permute-done | bytes 458784 | tf_op jit(solution)/shard_map/ppermute | solution.py:54
  55.2 0.8 %shard_map.91 = (f32[80,256]{1,0:T(8,128)S(1)}, f32[80,256]{1,0:T(8,128)S(1)}, f32[80,256]{1,0:T(8,128)S(1)}, f32[80,256]{1,0:T(8,128)S(1)}, f32[32,256]{1,0:T(8,128)S(1)}) custom-call(f32[4,112,256]{2,1,0:T(8,128)S(1)} %collective-permute-done.23.refs_0_, f32[4,112,256]{2,1,0:T(8,128)S(1)} %shard_map.89.refs_0_.refs_1_, ...), custom_call_target="tpu_custom_call" | custom-call | flops 536870912 | tf_op jit(solution)/shard_map/pallas_call | solution.py:71
  56.0 1.7 %collective-permute-start.24 = (f32[80,256]{1,0:T(8,128)S(1)}, f32[80,256]{1,0:T(8,128)S(1)}, u32[]{:S(2)}, u32[]{:S(2)}) collective-permute-start(f32[80,256]{1,0:T(8,128)S(1)} %get-tuple-element.53), channel_id=1, source_target_pairs={{0,3},{1,2},{2,1},{3,0},{4,7},{5,6},{6,5},{7,4},{8,11},{9,10},{10,... | collective-permute-start | bytes 245768 | tf_op jit(solution)/shard_map/ppermute | solution.py:60
  57.7 2.7 %collective-permute-start.26 = (f32[80,256]{1,0:T(8,128)S(1)}, f32[80,256]{1,0:T(8,128)S(1)}, u32[]{:S(2)}, u32[]{:S(2)}) collective-permute-start(f32[80,256]{1,0:T(8,128)S(1)} %get-tuple-element.55), channel_id=1, source_target_pairs={{0,1},{1,0},{2,3},{3,2},{4,5},{5,4},{6,7},{7,6},{8,9},{9,8},{10,11... | collective-permute-start | bytes 245768 | tf_op jit(solution)/shard_map/ppermute | solution.py:60
  60.5 6.1 %collective-permute-done.27 = f32[32,256]{1,0:T(8,128)S(1)} collective-permute-done((f32[32,256]{1,0:T(8,128)S(1)}, f32[32,256]{1,0:T(8,128)S(1)}, u32[]{:S(2)}, u32[]{:S(2)}) %collective-permute-start.27) | collective-permute-done | bytes 32800 | tf_op jit(solution)/shard_map/ppermute | solution.py:54
  66.5 0.6 collective-permute-start.28
  67.2 4.2 %collective-permute-done.28 = f32[32,256]{1,0:T(8,128)S(1)} collective-permute-done((f32[32,256]{1,0:T(8,128)S(1)}, f32[32,256]{1,0:T(8,128)S(1)}, u32[]{:S(2)}, u32[]{:S(2)}) %collective-permute-start.28) | collective-permute-done | bytes 32800 | tf_op jit(solution)/shard_map/ppermute | solution.py:54
  71.4 0.4 shard_map.92
  71.8 1.1 %shard_map.93 = (f32[3,64,64]{2,1,0:T(8,128)}, f32[64,256]{1,0:T(8,128)}) custom-call(f32[80,256]{1,0:T(8,128)S(1)} %get-tuple-element.52.refs_0_, f32[80,256]{1,0:T(8,128)S(1)} %collective-permute-done.24.refs_1_, f32[80,256]{1,0:T(8,128)S(1)} %collective-permute-done.25.refs_2_, f32[80,256]{1,0:T(8,128)S(1)} %collective-permute-done.26.refs_3_, ...), custom_call_target="tpu_custom_call" | custom-call | tf_op jit(solution)/shard_map/pallas_call | solution.py:71
  (29 shorter events, 0.7 us)
Async XLA Ops:
  0.6 11.7 %collective-permute-start = (f32[64,256]{1,0:T(8,128)}, f32[64,256]{1,0:T(8,128)S(1)}, u32[]{:S(2)}, u32[]{:S(2)}) collective-permute-start(f32[64,256]{1,0:T(8,128)} %refs_4_.1), channel_id=1, source_target_pairs={{2,0},{3,1},{0,2},{1,3},{6,4},{7,5},{4,6},{5,7},{10,8},{11,9},{8,1... | collective-permute-start | bytes 196616 | tf_op jit(solution)/shard_map/ppermute | solution.py:54
  4.7 7.7 %collective-permute-start.2 = (f32[64,256]{1,0:T(8,128)}, f32[64,256]{1,0:T(8,128)S(1)}, u32[]{:S(2)}, u32[]{:S(2)}) collective-permute-start(f32[64,256]{1,0:T(8,128)} %refs_5_.1), channel_id=1, source_target_pairs={{8,0},{12,4},{0,8},{4,12},{24,16},{28,20},{16,24},{20,28},{9,1},{1... | collective-permute-start | bytes 196616 | tf_op jit(solution)/shard_map/ppermute | solution.py:54
  6.2 6.2 %collective-permute-start.4 = (f32[64,256]{1,0:T(8,128)}, f32[64,256]{1,0:T(8,128)S(1)}, u32[]{:S(2)}, u32[]{:S(2)}) collective-permute-start(f32[64,256]{1,0:T(8,128)} %refs_5_.1), channel_id=1, source_target_pairs={{24,0},{28,4},{16,8},{20,12},{8,16},{12,20},{0,24},{4,28},{25,1},{... | collective-permute-start | bytes 196616 | tf_op jit(solution)/shard_map/ppermute | solution.py:54
  7.7 4.7 %collective-permute-start.3 = (f32[64,256]{1,0:T(8,128)}, f32[64,256]{1,0:T(8,128)S(1)}, u32[]{:S(2)}, u32[]{:S(2)}) collective-permute-start(f32[64,256]{1,0:T(8,128)} %refs_5_.1), channel_id=1, source_target_pairs={{16,0},{20,4},{24,8},{28,12},{0,16},{4,20},{8,24},{12,28},{17,1},{... | collective-permute-start | bytes 196616 | tf_op jit(solution)/shard_map/ppermute | solution.py:54
  12.4 2.5 %collective-permute-start.5 = (f32[4,64,256]{2,1,0:T(8,128)S(1)}, f32[4,64,256]{2,1,0:T(8,128)S(1)}, u32[]{:S(2)}, u32[]{:S(2)}) collective-permute-start(f32[4,64,256]{2,1,0:T(8,128)S(1)} %shard_map.79.refs_0_.refs_1_), channel_id=1, source_target_pairs={{4,0},{0,4},{12,8},{8,12},{20,16},{16,20},{28,24},{24,28},{5,1},{1... | collective-permute-start | bytes 786440 | tf_op jit(solution)/shard_map/ppermute | solution.py:54
  12.5 7.7 %collective-permute-start.1 = (f32[2,64,256]{2,1,0:T(8,128)S(1)}, f32[2,64,256]{2,1,0:T(8,128)S(1)}, u32[]{:S(2)}, u32[]{:S(2)}) collective-permute-start(f32[2,64,256]{2,1,0:T(8,128)S(1)} %shard_map.78.refs_4_.refs_0_), channel_id=1, source_target_pairs={{1,0},{0,1},{3,2},{2,3},{5,4},{4,5},{7,6},{6,7},{9,8},{8,9},{11,10... | collective-permute-start | bytes 393224 | tf_op jit(solution)/shard_map/ppermute | solution.py:54
  15.8 6.9 %collective-permute-start.7 = (f32[64,256]{1,0:T(8,128)S(1)}, f32[64,256]{1,0:T(8,128)S(1)}, u32[]{:S(2)}, u32[]{:S(2)}) collective-permute-start(f32[64,256]{1,0:T(8,128)S(1)} %get-tuple-element.41), channel_id=1, source_target_pairs={{0,3},{1,2},{2,1},{3,0},{4,7},{5,6},{6,5},{7,4},{8,11},{9,10},{10,... | collective-permute-start | bytes 196616 | tf_op jit(solution)/shard_map/ppermute | solution.py:60
  16.3 8.1 %collective-permute-start.8 = (f32[64,256]{1,0:T(8,128)S(1)}, f32[64,256]{1,0:T(8,128)S(1)}, u32[]{:S(2)}, u32[]{:S(2)}) collective-permute-start(f32[64,256]{1,0:T(8,128)S(1)} %get-tuple-element.42), channel_id=1, source_target_pairs={{0,2},{1,3},{2,0},{3,1},{4,6},{5,7},{6,4},{7,5},{8,10},{9,11},{10,... | collective-permute-start | bytes 196616 | tf_op jit(solution)/shard_map/ppermute | solution.py:60
  18.0 6.5 %collective-permute-start.9 = (f32[64,256]{1,0:T(8,128)S(1)}, f32[64,256]{1,0:T(8,128)S(1)}, u32[]{:S(2)}, u32[]{:S(2)}) collective-permute-start(f32[64,256]{1,0:T(8,128)S(1)} %get-tuple-element.43), channel_id=1, source_target_pairs={{0,1},{1,0},{2,3},{3,2},{4,5},{5,4},{6,7},{7,6},{8,9},{9,8},{10,11... | collective-permute-start | bytes 196616 | tf_op jit(solution)/shard_map/ppermute | solution.py:60
  24.4 5.3 %collective-permute-start.12 = (f32[64,256]{1,0:T(8,128)S(1)}, f32[64,256]{1,0:T(8,128)S(1)}, u32[]{:S(2)}, u32[]{:S(2)}) collective-permute-start(f32[64,256]{1,0:T(8,128)S(1)} %shard_map.83.refs_0_.refs_9_), channel_id=1, source_target_pairs={{24,0},{28,4},{16,8},{20,12},{8,16},{12,20},{0,24},{4,28},{25,1},{... | collective-permute-start | bytes 196616 | tf_op jit(solution)/shard_map/ppermute | solution.py:54
  26.9 4.3 %collective-permute-start.11 = (f32[64,256]{1,0:T(8,128)S(1)}, f32[64,256]{1,0:T(8,128)S(1)}, u32[]{:S(2)}, u32[]{:S(2)}) collective-permute-start(f32[64,256]{1,0:T(8,128)S(1)} %shard_map.83.refs_0_.refs_9_), channel_id=1, source_target_pairs={{16,0},{20,4},{24,8},{28,12},{0,16},{4,20},{8,24},{12,28},{17,1},{... | collective-permute-start | bytes 196616 | tf_op jit(solution)/shard_map/ppermute | solution.py:54
  27.5 4.3 %collective-permute-start.10 = (f32[64,256]{1,0:T(8,128)S(1)}, f32[64,256]{1,0:T(8,128)S(1)}, u32[]{:S(2)}, u32[]{:S(2)}) collective-permute-start(f32[64,256]{1,0:T(8,128)S(1)} %shard_map.83.refs_0_.refs_9_), channel_id=1, source_target_pairs={{8,0},{12,4},{0,8},{4,12},{24,16},{28,20},{16,24},{20,28},{9,1},{1... | collective-permute-start | bytes 196616 | tf_op jit(solution)/shard_map/ppermute | solution.py:54
  28.0 4.6 %collective-permute-start.6 = (f32[4,64,256]{2,1,0:T(8,128)S(1)}, f32[4,64,256]{2,1,0:T(8,128)S(1)}, u32[]{:S(2)}, u32[]{:S(2)}) collective-permute-start(f32[4,64,256]{2,1,0:T(8,128)S(1)} %get-tuple-element.40.refs_4_), channel_id=1, source_target_pairs={{4,0},{0,4},{12,8},{8,12},{20,16},{16,20},{28,24},{24,28},{5,1},{1... | collective-permute-start | bytes 786440 | tf_op jit(solution)/shard_map/ppermute | solution.py:54
  31.7 1.6 %collective-permute-start.13 = (f32[4,64,256]{2,1,0:T(8,128)S(1)}, f32[4,64,256]{2,1,0:T(8,128)S(1)}, u32[]{:S(2)}, u32[]{:S(2)}) collective-permute-start(f32[4,64,256]{2,1,0:T(8,128)S(1)} %shard_map.84.refs_0_.refs_1_), channel_id=1, source_target_pairs={{4,0},{0,4},{12,8},{8,12},{20,16},{16,20},{28,24},{24,28},{5,1},{1... | collective-permute-start | bytes 786440 | tf_op jit(solution)/shard_map/ppermute | solution.py:54
  34.1 6.8 %collective-permute-start.17 = (f32[64,256]{1,0:T(8,128)S(1)}, f32[64,256]{1,0:T(8,128)S(1)}, u32[]{:S(2)}, u32[]{:S(2)}) collective-permute-start(f32[64,256]{1,0:T(8,128)S(1)} %get-tuple-element.49), channel_id=1, source_target_pairs={{0,3},{1,2},{2,1},{3,0},{4,7},{5,6},{6,5},{7,4},{8,11},{9,10},{10,... | collective-permute-start | bytes 196616 | tf_op jit(solution)/shard_map/ppermute | solution.py:60
  35.9 7.1 %collective-permute-start.18 = (f32[64,256]{1,0:T(8,128)S(1)}, f32[64,256]{1,0:T(8,128)S(1)}, u32[]{:S(2)}, u32[]{:S(2)}) collective-permute-start(f32[64,256]{1,0:T(8,128)S(1)} %get-tuple-element.50), channel_id=1, source_target_pairs={{0,2},{1,3},{2,0},{3,1},{4,6},{5,7},{6,4},{7,5},{8,10},{9,11},{10,... | collective-permute-start | bytes 196616 | tf_op jit(solution)/shard_map/ppermute | solution.py:60
  35.9 7.1 %collective-permute-start.19 = (f32[64,256]{1,0:T(8,128)S(1)}, f32[64,256]{1,0:T(8,128)S(1)}, u32[]{:S(2)}, u32[]{:S(2)}) collective-permute-start(f32[64,256]{1,0:T(8,128)S(1)} %get-tuple-element.51), channel_id=1, source_target_pairs={{0,1},{1,0},{2,3},{3,2},{4,5},{5,4},{6,7},{7,6},{8,9},{9,8},{10,11... | collective-permute-start | bytes 196616 | tf_op jit(solution)/shard_map/ppermute | solution.py:60
  38.6 5.9 %collective-permute-start.14 = (f32[64,256]{1,0:T(8,128)S(1)}, f32[64,256]{1,0:T(8,128)S(1)}, u32[]{:S(2)}, u32[]{:S(2)}) collective-permute-start(f32[64,256]{1,0:T(8,128)S(1)} %get-tuple-element.46), channel_id=1, source_target_pairs={{24,0},{28,4},{16,8},{20,12},{8,16},{12,20},{0,24},{4,28},{25,1},{... | collective-permute-start | bytes 196616 | tf_op jit(solution)/shard_map/ppermute | solution.py:54
  40.2 4.7 %collective-permute-start.15 = (f32[64,256]{1,0:T(8,128)S(1)}, f32[64,256]{1,0:T(8,128)S(1)}, u32[]{:S(2)}, u32[]{:S(2)}) collective-permute-start(f32[64,256]{1,0:T(8,128)S(1)} %get-tuple-element.47), channel_id=1, source_target_pairs={{16,0},{20,4},{24,8},{28,12},{0,16},{4,20},{8,24},{12,28},{17,1},{... | collective-permute-start | bytes 196616 | tf_op jit(solution)/shard_map/ppermute | solution.py:54
  41.0 4.3 %collective-permute-start.16 = (f32[64,256]{1,0:T(8,128)S(1)}, f32[64,256]{1,0:T(8,128)S(1)}, u32[]{:S(2)}, u32[]{:S(2)}) collective-permute-start(f32[64,256]{1,0:T(8,128)S(1)} %get-tuple-element.48), channel_id=1, source_target_pairs={{8,0},{12,4},{0,8},{4,12},{24,16},{28,20},{16,24},{20,28},{9,1},{1... | collective-permute-start | bytes 196616 | tf_op jit(solution)/shard_map/ppermute | solution.py:54
  45.7 6.1 %collective-permute-start.22 = (f32[112,256]{1,0:T(8,128)S(1)}, f32[112,256]{1,0:T(8,128)S(1)}, u32[]{:S(2)}, u32[]{:S(2)}) collective-permute-start(f32[112,256]{1,0:T(8,128)S(1)} %shard_map.88.refs_0_), channel_id=1, source_target_pairs={{24,0},{28,4},{16,8},{20,12},{8,16},{12,20},{0,24},{4,28},{25,1},{... | collective-permute-start | bytes 344072 | tf_op jit(solution)/shard_map/ppermute | solution.py:54
  48.0 5.1 %collective-permute-start.21 = (f32[112,256]{1,0:T(8,128)S(1)}, f32[112,256]{1,0:T(8,128)S(1)}, u32[]{:S(2)}, u32[]{:S(2)}) collective-permute-start(f32[112,256]{1,0:T(8,128)S(1)} %shard_map.88.refs_0_), channel_id=1, source_target_pairs={{16,0},{20,4},{24,8},{28,12},{0,16},{4,20},{8,24},{12,28},{17,1},{... | collective-permute-start | bytes 344072 | tf_op jit(solution)/shard_map/ppermute | solution.py:54
  48.5 4.8 %collective-permute-start.20 = (f32[112,256]{1,0:T(8,128)S(1)}, f32[112,256]{1,0:T(8,128)S(1)}, u32[]{:S(2)}, u32[]{:S(2)}) collective-permute-start(f32[112,256]{1,0:T(8,128)S(1)} %shard_map.88.refs_0_), channel_id=1, source_target_pairs={{8,0},{12,4},{0,8},{4,12},{24,16},{28,20},{16,24},{20,28},{9,1},{1... | collective-permute-start | bytes 344072 | tf_op jit(solution)/shard_map/ppermute | solution.py:54
  53.3 1.9 %collective-permute-start.23 = (f32[4,112,256]{2,1,0:T(8,128)S(1)}, f32[4,112,256]{2,1,0:T(8,128)S(1)}, u32[]{:S(2)}, u32[]{:S(2)}) collective-permute-start(f32[4,112,256]{2,1,0:T(8,128)S(1)} %shard_map.89.refs_0_.refs_1_), channel_id=1, source_target_pairs={{4,0},{0,4},{12,8},{8,12},{20,16},{16,20},{28,24},{24,28},{5,1},{1... | collective-permute-start | bytes 1376264 | tf_op jit(solution)/shard_map/ppermute | solution.py:54
  56.0 15.8 %collective-permute-start.24 = (f32[80,256]{1,0:T(8,128)S(1)}, f32[80,256]{1,0:T(8,128)S(1)}, u32[]{:S(2)}, u32[]{:S(2)}) collective-permute-start(f32[80,256]{1,0:T(8,128)S(1)} %get-tuple-element.53), channel_id=1, source_target_pairs={{0,3},{1,2},{2,1},{3,0},{4,7},{5,6},{6,5},{7,4},{8,11},{9,10},{10,... | collective-permute-start | bytes 245768 | tf_op jit(solution)/shard_map/ppermute | solution.py:60
  57.7 14.1 %collective-permute-start.25 = (f32[80,256]{1,0:T(8,128)S(1)}, f32[80,256]{1,0:T(8,128)S(1)}, u32[]{:S(2)}, u32[]{:S(2)}) collective-permute-start(f32[80,256]{1,0:T(8,128)S(1)} %get-tuple-element.54), channel_id=1, source_target_pairs={{0,2},{1,3},{2,0},{3,1},{4,6},{5,7},{6,4},{7,5},{8,10},{9,11},{10,... | collective-permute-start | bytes 245768 | tf_op jit(solution)/shard_map/ppermute | solution.py:60
  57.7 14.1 %collective-permute-start.26 = (f32[80,256]{1,0:T(8,128)S(1)}, f32[80,256]{1,0:T(8,128)S(1)}, u32[]{:S(2)}, u32[]{:S(2)}) collective-permute-start(f32[80,256]{1,0:T(8,128)S(1)} %get-tuple-element.55), channel_id=1, source_target_pairs={{0,1},{1,0},{2,3},{3,2},{4,5},{5,4},{6,7},{7,6},{8,9},{9,8},{10,11... | collective-permute-start | bytes 245768 | tf_op jit(solution)/shard_map/ppermute | solution.py:60
  60.4 6.1 %collective-permute-start.27 = (f32[32,256]{1,0:T(8,128)S(1)}, f32[32,256]{1,0:T(8,128)S(1)}, u32[]{:S(2)}, u32[]{:S(2)}) collective-permute-start(f32[32,256]{1,0:T(8,128)S(1)} %get-tuple-element.56), channel_id=1, source_target_pairs={{1,0},{0,1},{3,2},{2,3},{5,4},{4,5},{7,6},{6,7},{9,8},{8,9},{11,10... | collective-permute-start | bytes 98312 | tf_op jit(solution)/shard_map/ppermute | solution.py:54
  66.5 4.8 %collective-permute-start.28 = (f32[32,256]{1,0:T(8,128)S(1)}, f32[32,256]{1,0:T(8,128)S(1)}, u32[]{:S(2)}, u32[]{:S(2)}) collective-permute-start(f32[32,256]{1,0:T(8,128)S(1)} %add.6), channel_id=1, source_target_pairs={{2,0},{3,1},{0,2},{1,3},{6,4},{7,5},{4,6},{5,7},{10,8},{11,9},{8,1... | collective-permute-start | bytes 98312 | tf_op jit(solution)/shard_map/ppermute | solution.py:54

commit v7 on v6

--- a/solution.py
+++ b/solution.py
@@ -102,8 +102,8 @@
     return [fetch(piece, axis, shift) for shift in range(2, lax.axis_size(axis), 2)]
 
 
-def gather_evens(piece, axis):
-    return stack_after([piece] + fetch_evens(piece, axis))
+def gather_evens(piece, axis, before=()):
+    return stack_after([piece] + fetch_evens(piece, axis), before)
 
 
 def gather_odds(evens, axis):
@@ -132,8 +132,8 @@
 
 
 def build_kernel(sizes, *refs):
-    count_ref, entries_ref, x_ref, y_ref, dense_ref, x_out, y_out, token_ref = refs[2:10]
-    rows_ref, cols_ref, tiles, sems = refs[10:]
+    entries_ref, x_ref, y_ref, dense_ref, x_out, y_out, token_ref = refs[3:10]
+    rows_ref, cols_ref, count_ref, tiles, sems = refs[10:]
     n_row, n_col, piece_blocks, group = sizes
     _, _, slot_count, tile_len, _ = entries_ref.shape
     me_row, me_col = lax.axis_index("row"), lax.axis_index("col")
@@ -143,16 +143,16 @@
         source = entries_ref.at[0, 0, pl.ds(index * group, group)]
         return pltpu.make_async_copy(source, tiles.at[pl.ds(index * group, group)], sems.at[index])
 
-    small = [(refs[0], rows_ref), (refs[1], cols_ref), (y_ref, y_out), (x_ref, x_out)]
+    small = [*zip(refs[:3], refs[10:13]), (y_ref, y_out), (x_ref, x_out)]
     small = [
         pltpu.make_async_copy(source, target, sems.at[chunk_count + index])
         for index, (source, target) in enumerate(small)
     ]
-    for copy in small[:2]:
+    for copy in small[:3]:
         copy.start()
     for index in range(chunk_count):
         chunk(index).start()
-    for copy in small[2:]:
+    for copy in small[3:]:
         copy.start()
 
     def clear(block, carry):
@@ -160,7 +160,7 @@
         return carry
 
     lax.fori_loop(0, dense_ref.shape[0], clear, 0)
-    for copy in small[:2]:
+    for copy in small[:3]:
         copy.wait()
 
     def place(slot):
@@ -182,7 +182,7 @@
         return carry
 
     lax.fori_loop(0, chunk_count, step, 0)
-    for copy in small[2:]:
+    for copy in small[3:]:
         copy.wait()
     token_ref[...] = jnp.zeros_like(token_ref)
 
@@ -200,7 +200,7 @@
     )
     return pl.pallas_call(
         functools.partial(build_kernel, (*sizes, group)),
-        in_specs=[hbm, hbm, pl.BlockSpec(memory_space=pltpu.SMEM), hbm, hbm, hbm],
+        in_specs=[hbm, hbm, pl.BlockSpec(memory_space=pl.ANY), hbm, hbm, hbm],
         out_specs=[pl.BlockSpec(memory_space=pltpu.VMEM)] * 4,
         out_shape=[
             pltpu.VMEM(shape, jnp.bfloat16),
@@ -209,9 +209,9 @@
             held(8, 128),
         ],
         scratch_shapes=[
-            *(pltpu.SMEM(part.shape, part.dtype) for part in (tile_rows, tile_cols)),
+            *(pltpu.SMEM(part.shape, part.dtype) for part in (tile_rows, tile_cols, tile_count)),
             pltpu.VMEM((slot_count, tile_len, tile_len), jnp.float32),
-            pltpu.SemaphoreType.DMA((slot_count // group + 4,)),
+            pltpu.SemaphoreType.DMA((slot_count // group + 5,)),
         ],
         compiler_params=pltpu.CompilerParams(vmem_limit_bytes=VMEM_LIMIT),
         cost_estimate=pl.CostEstimate(
@@ -254,9 +254,9 @@
             sums_ref[index, :, block * tile_len : (block + 1) * tile_len] = part
 
 
-def second_half_kernel(span, n_col, pieces_ref, evens_ref, sums_ref, dense_ref, *refs):
-    outs, refs = refs[:n_col], refs[n_col:]
-    digits = refs[-1]
+def second_half_kernel(span, pieces_ref, evens_ref, sums_ref, dense_ref, *refs):
+    outs, digits = refs[:-1], refs[-1]
+    n_col = len(outs)
     fill_digits(span, pieces_ref, digits)
     row_blocks, _, width = dense_ref.shape
     tile_len = width // 2
@@ -270,12 +270,10 @@
                 for index, part in enumerate(parts)
             )
             outs[e][:span, sub * tile_len : (sub + 1) * tile_len] = combine(*parts)
-    if len(refs) > 1:
+    if outs[0].shape[0] > span:
         packed = jnp.sum(pieces_ref[:, span:, :], 0) + jnp.sum(evens_ref[:, span:, :], 0)
-        tail = outs[0].shape[0] - span
         for out in outs:
-            out[span:, :] = packed[:tail]
-        refs[0][...] = packed[tail:]
+            out[span:, :] = packed
 
 
 def dense_first(evens, span, dense):
@@ -290,22 +288,20 @@
     )[0]
 
 
-def dense_second(odds, evens, sums, span, n_col, tail, dense, before):
+def dense_second(odds, evens, sums, span, n_col, dense, before):
     _, depth, _ = dense.shape
-    piece_len = odds.shape[2]
-    outs = [held(span + tail, piece_len)] * n_col
-    if tail:
-        outs = outs + [held(odds.shape[1] - span - tail, piece_len)]
-    results = call(
-        functools.partial(second_half_kernel, span, n_col),
-        [odds, evens, sums, dense],
-        outs,
-        before,
-        scratch=[pltpu.VMEM((2 * span, depth // 2), jnp.bfloat16)],
-        limit=VMEM_LIMIT,
-        flops=2 * span * dense.size,
-    )
-    return list(results[:n_col]), (results[n_col] if tail else None)
+    _, rows, piece_len = odds.shape
+    return list(
+        call(
+            functools.partial(second_half_kernel, span),
+            [odds, evens, sums, dense],
+            [held(rows, piece_len)] * n_col,
+            before,
+            scratch=[pltpu.VMEM((2 * span, depth // 2), jnp.bfloat16)],
+            limit=VMEM_LIMIT,
+            flops=2 * span * dense.size,
+        )
+    )
 
 
 def left_kernel(n_row, x_evens, x_odds, dense_ref, *refs):
@@ -384,18 +380,16 @@
     return reduce_centered(summed).reshape(span, blocks * tile_len)
 
 
-def sparse_second(odds, evens, span, n_col, tail, positions, a_digits):
+def sparse_second(odds, evens, span, n_col, positions, a_digits):
     rows, cols, count = positions
     pieces = [*evens, *odds]
     piece_len = pieces[0].shape[1]
     blocks = n_col * piece_len // a_digits.shape[-1]
     vector = reduce_centered(jnp.concatenate([piece[:span] for piece in pieces], 1))
     product = sparse_product(vector, "ntk,tdik->tdni", cols, rows, count, blocks, a_digits)
+    packed = functools.reduce(jnp.add, [piece[span:] for piece in pieces])
     outs = [product[:, e * piece_len : (e + 1) * piece_len] for e in range(n_col)]
-    if not tail:
-        return outs, None
-    packed = functools.reduce(jnp.add, [piece[span:] for piece in pieces])
-    return [jnp.concatenate([out, packed[:tail]], 0) for out in outs], packed[tail:]
+    return [jnp.concatenate([out, packed], 0) for out in outs]
 
 
 def sparse_left(x_pairs, n_row, positions, a_digits):
@@ -411,39 +405,47 @@
     return pieces[: n_row // 2], jnp.stack(pieces[n_row // 2 :])
 
 
-def add_came(evens, odds_came, before):
-    def kernel(*refs):
-        for index in range(len(evens)):
-            refs[len(evens) + 1 + index][...] = refs[index][...] + refs[len(evens)][index]
-
-    return list(call(kernel, [*evens, odds_came], [held(*evens[0].shape)] * len(evens), before))
+def add_came(evens, odds_came, index, before=()):
+    def kernel(even_ref, came_ref, out_ref):
+        out_ref[...] = even_ref[...] + came_ref[index]
+
+    return call(kernel, [evens[index], odds_came], [held(*evens[index].shape)], before)[0]
+
+
+def sum_over(packed, axis, shift=1):
+    while shift < lax.axis_size(axis):
+        packed = packed + fetch(packed, axis, shift)
+        shift *= 2
+    return packed
 
 
 def append_projections(w_parts, pieces, earlier):
     span, piece_len = pieces[0].shape
     rows = span * span // piece_len
-    count = len(earlier) + 1
 
     def kernel(*refs):
         w_refs, refs = refs[: len(w_parts)], refs[len(w_parts) :]
         piece_refs, refs = refs[: len(pieces)], refs[len(pieces) :]
-        out_ref = refs[-1]
+        earlier_refs, (out_ref, terms_ref) = refs[:-2], refs[-2:]
         summed = functools.reduce(jnp.add, [ref[...] for ref in piece_refs])
         out_ref[:span, :] = summed
         w_piece = functools.reduce(jnp.add, [ref[...] for ref in w_refs])
         w_digits = stacked_digits(reduce_centered(w_piece))
-        for index, vector in enumerate([summed] + [ref[...] for ref in refs[:-1]]):
+        for index, vector in enumerate([summed] + [ref[...] for ref in earlier_refs]):
             products = dot_pairs(w_digits, stacked_digits(reduce_centered(vector)))
             square = combine(
                 reduce_centered(products[:span, :span]),
                 reduce_centered(products[:span, span:]) + reduce_centered(products[span:, :span]),
                 reduce_centered(products[span:, span:]),
             )
-            start = span + index * rows
-            out_ref[start : start + rows, :] = pack_square(square, piece_len)
-
-    outs = [held(span + count * rows, piece_len)]
-    return call(kernel, [*w_parts, *pieces, *earlier], outs)[0]
+            square = pack_square(square, piece_len)
+            if index == 0:
+                out_ref[span:, :] = square
+            else:
+                terms_ref[(index - 1) * rows : index * rows, :] = square
+
+    outs = [held(span + rows, piece_len), held(len(earlier) * rows, piece_len)]
+    return call(kernel, [*w_parts, *pieces, *earlier], outs)
 
 
 def multiply_mod(left, right):
@@ -506,17 +508,21 @@
         positions, a_digits = sparse_tiles(tiles, sizes)
         x_own, y_own, before = block_x, block_y, []
 
-    def multiply(evens, tail=0, before=()):
-        odds = gather_odds(evens, "row")
+    def multiply_evens(evens):
+        return dense_first(evens, span, dense) if is_dense else evens
+
+    def multiply_odds(odds, evens, sums, before):
         if is_dense:
-            sums = dense_first(evens, span, dense)
-            return dense_second(odds, evens, sums, span, n_col, tail, dense, before)
-        return sparse_second(odds, evens, span, n_col, tail, positions, a_digits)
+            return dense_second(odds, evens, sums, span, n_col, dense, before)
+        return sparse_second(odds, evens, span, n_col, positions, a_digits)
+
+    def multiply(evens, before):
+        return multiply_odds(gather_odds(evens, "row"), evens, multiply_evens(evens), before)
 
     x_came = fetch_evens(block_x, "col")
     evens = stack_after([y_own] + fetch_evens(block_y, "row"), [*before, *x_came])
     x_evens = stack_after([x_own] + x_came)
-    outs, _ = multiply(evens, before=[x_evens])
+    outs = multiply(evens, [x_evens])
     x_pairs = [x_evens, gather_odds(x_evens, "col")]
     if is_dense:
         w_evens, w_odds = dense_left(x_pairs, n_row, dense, [outs[0]])
@@ -524,22 +530,26 @@
         w_evens, w_odds = sparse_left(x_pairs, n_row, positions, a_digits)
     vector_1 = sum_after(scatter_pieces(outs, "col"), [w_odds])
     w_came = fetch(w_odds, "row", 1)
-    evens = gather_evens(vector_1, "row")
-    outs, _ = multiply(evens, before=[w_came])
+    outs = multiply(gather_evens(vector_1, "row"), [w_came])
     pieces = scatter_pieces(outs, "col")
-    w_evens = add_came(w_evens, w_came, [outs[0]])
-    w_parts = [w_evens[0]] + [
-        fetch(w_evens[index], "row", 2 * index) for index in reversed(range(1, n_row // 2))
+    w_last = n_row // 2 - 1
+    w_parts = [
+        add_came(w_evens, w_came, index, [] if index == w_last else [outs[0]])
+        for index in range(n_row // 2)
     ]
-    vector_2 = append_projections(w_parts, pieces, [y_own, vector_1])
-    evens = gather_evens(vector_2, "row")
-    outs, packed = multiply(evens, packed_rows)
-    pieces = scatter_pieces(outs, "col")
-    shift = 1
-    while shift < n_col:
-        packed = packed + fetch(packed, "col", shift)
-        shift *= 2
-    return finish(pieces, sigma_start(packed, span), span)
+    w_parts = w_parts[:1] + [
+        fetch(w_parts[index], "row", 2 * index) for index in reversed(range(1, n_row // 2))
+    ]
+    vector_2, terms = append_projections(w_parts, pieces, [y_own, vector_1])
+    terms = terms + fetch(terms, "col", 1)
+    evens = gather_evens(vector_2, "row", [terms])
+    odds, sums = gather_odds(evens, "row"), multiply_evens(evens)
+    if n_col > 2:
+        terms = sum_after([terms, fetch(terms, "col", 2)], [sums])
+    terms = sum_over(terms, "col", 4)
+    outs = multiply_odds(odds, evens, sums, [terms])
+    terms = sum_over(sum_after([terms], [outs[0]]), "row")
+    return finish(scatter_pieces(outs, "col"), sigma_start(terms, span), span)
 
 
 def solution(mesh):

time: 73.1 us -> 72.7 us (level)
  waiting for transfers between devices: 24.9 us -> 21.6 us
  starting transfers between devices: 33.8 us -> 36.7 us
    ppermute x20 -> x23, waiting for transfers between devices: 22.1 us -> 17.5 us  [fetch(): lax.ppermute(piece, axis, [(partner(i, shift, size), i) for i in range(si...]
    ppermute x20 -> x23, starting transfers between devices: 20.5 us -> 23.3 us  [fetch(): lax.ppermute(piece, axis, [(partner(i, shift, size), i) for i in range(si...]
    ppermute x9, waiting for transfers between devices: 2.83 us -> 4.06 us  [scatter_pieces(): lax.ppermute(pieces[shift], axis, [(i, partner(i, shift, size)) for i in...]
    pallas_call x16 -> x21, Pallas kernels: 9.18 us -> 9.19 us  [call(): pl.pallas_call(body, in_specs=[vmem] * len(operands) + [pl.BlockSpec(memo...]
  transfers between devices with their start and end apart: 29 -> 32, of which waited for: 16 -> 11; matrix products, arithmetic and copies ran while one was open for 0% -> 0% of each run, Pallas kernels for 13% -> 14%
where the time goes in v7:
time: 72.7 us; the launch traced here: 72.5 us
  starting transfers between devices  36.7 us (50%)
  waiting for transfers between devices  21.6 us (30%)
  Pallas kernels  12.7 us (17%)
  between operations  1.58 us (2%)
    ppermute x23, starting transfers between devices, fetch(): lax.ppermute(piece, axis, [(partner(i, shift, size), i) for i in range(si...  23.3 us
    ppermute x23, waiting for transfers between devices, fetch(): lax.ppermute(piece, axis, [(partner(i, shift, size), i) for i in range(si...  17.5 us
    ppermute x9, starting transfers between devices, scatter_pieces(): lax.ppermute(pieces[shift], axis, [(i, partner(i, shift, size)) for i in...  13.4 us
    pallas_call x21, Pallas kernels, call(): pl.pallas_call(body, in_specs=[vmem] * len(operands) + [pl.BlockSpec(memo...  9.19 us
    ppermute x9, waiting for transfers between devices, scatter_pieces(): lax.ppermute(pieces[shift], axis, [(i, partner(i, shift, size)) for i in...  4.06 us
    pallas_call x1, Pallas kernels, build_dense(): pl.pallas_call(functools.partial(build_kernel, (*sizes, group)), in_specs...  3.5 us
  transfers between devices with their start and end apart: 32, of which 11 were waited for; matrix products, arithmetic and copies ran while one was open for 0% of the time, Pallas kernels for 14%

profile of v7, /device:TPU:0, one launch (start us, length us, event | category | flops | bytes accessed | tf_op | source)
XLA Modules:
  0.0 72.5 jit_solution(3482275648691536374)
XLA Ops:
  0.6 4.1 %collective-permute-start = (f32[64,256]{1,0:T(8,128)}, f32[64,256]{1,0:T(8,128)S(1)}, u32[]{:S(2)}, u32[]{:S(2)}) collective-permute-start(f32[64,256]{1,0:T(8,128)} %refs_4_.1), channel_id=1, source_target_pairs={{2,0},{3,1},{0,2},{1,3},{6,4},{7,5},{4,6},{5,7},{10,8},{11,9},{8,1... | collective-permute-start | bytes 196616 | tf_op jit(solution)/shard_map/ppermute | solution.py:54
  4.7 1.5 %collective-permute-start.2 = (f32[64,256]{1,0:T(8,128)}, f32[64,256]{1,0:T(8,128)S(1)}, u32[]{:S(2)}, u32[]{:S(2)}) collective-permute-start(f32[64,256]{1,0:T(8,128)} %refs_5_.1), channel_id=1, source_target_pairs={{8,0},{12,4},{0,8},{4,12},{24,16},{28,20},{16,24},{20,28},{9,1},{1... | collective-permute-start | bytes 196616 | tf_op jit(solution)/shard_map/ppermute | solution.py:54
  6.2 1.5 %collective-permute-start.4 = (f32[64,256]{1,0:T(8,128)}, f32[64,256]{1,0:T(8,128)S(1)}, u32[]{:S(2)}, u32[]{:S(2)}) collective-permute-start(f32[64,256]{1,0:T(8,128)} %refs_5_.1), channel_id=1, source_target_pairs={{24,0},{28,4},{16,8},{20,12},{8,16},{12,20},{0,24},{4,28},{25,1},{... | collective-permute-start | bytes 196616 | tf_op jit(solution)/shard_map/ppermute | solution.py:54
  7.7 0.5 collective-permute-start.3
  8.9 3.5 %shard_map.77 = (bf16[8,2048,256]{2,1,0:T(8,128)(2,1)S(1)}, f32[64,256]{1,0:T(8,128)S(1)}, f32[64,256]{1,0:T(8,128)S(1)}, f32[8,128]{1,0:T(8,128)S(1)}) custom-call(s32[1,1,64]{2,1,0:T(1,128)} %refs_0_.1, s32[1,1,64]{2,1,0:T(1,128)} %refs_1_.1, s32[1,1]{1,0:T(1,128)S(6)} %copy.8.refs_2_, f32[1,1,64,128,128]{4,3,2,1,0:T(8,128)} %refs_3_.1, ...), custom_call_target="tpu_custom_call" | custom-call | flops 8388608 | bytes 8388608 | tf_op jit(solution)/shard_map/pallas_call | solution.py:201
  12.5 0.1 collective-permute-start.5
  12.6 1.6 %collective-permute-start.1 = (f32[2,64,256]{2,1,0:T(8,128)S(1)}, f32[2,64,256]{2,1,0:T(8,128)S(1)}, u32[]{:S(2)}, u32[]{:S(2)}) collective-permute-start(f32[2,64,256]{2,1,0:T(8,128)S(1)} %shard_map.78.refs_4_.refs_0_), channel_id=1, source_target_pairs={{1,0},{0,1},{3,2},{2,3},{5,4},{4,5},{7,6},{6,7},{9,8},{8,9},{11,10... | collective-permute-start | bytes 393224 | tf_op jit(solution)/shard_map/ppermute | solution.py:54
  14.2 0.7 %shard_map.80.refs_2_ = f32[3,64,1024]{2,1,0:T(8,128)S(1)} custom-call(f32[4,64,256]{2,1,0:T(8,128)S(1)} %shard_map.79.refs_0_.refs_1_, bf16[8,2048,256]{2,1,0:T(8,128)(2,1)S(1)} %get-tuple-element.29.refs_1_.refs_3_.refs_2_), custom_call_target="tpu_custom_call" | custom-call | flops 536870912 | tf_op jit(solution)/shard_map/pallas_call | solution.py:71
  15.0 0.8 %shard_map.81 = (f32[64,256]{1,0:T(8,128)S(1)}, f32[64,256]{1,0:T(8,128)S(1)}, f32[64,256]{1,0:T(8,128)S(1)}, f32[64,256]{1,0:T(8,128)S(1)}) custom-call(f32[4,64,256]{2,1,0:T(8,128)S(1)} %collective-permute-done.5.refs_0_, f32[4,64,256]{2,1,0:T(8,128)S(1)} %shard_map.79.refs_0_.refs_1_, f32[3,64,1024]{2,1,0:T(8,128)S(1)} %shard_map.80.refs_2_, ...), custom_call_target="tpu_custom_call" | custom-call | flops 536870912 | tf_op jit(solution)/shard_map/pallas_call | solution.py:71
  15.8 0.5 collective-permute-start.7
  16.3 1.7 %collective-permute-start.8 = (f32[64,256]{1,0:T(8,128)S(1)}, f32[64,256]{1,0:T(8,128)S(1)}, u32[]{:S(2)}, u32[]{:S(2)}) collective-permute-start(f32[64,256]{1,0:T(8,128)S(1)} %get-tuple-element.36), channel_id=1, source_target_pairs={{0,2},{1,3},{2,0},{3,1},{4,6},{5,7},{6,4},{7,5},{8,10},{9,11},{10,... | collective-permute-start | bytes 196616 | tf_op jit(solution)/shard_map/ppermute | solution.py:60
  18.0 2.3 %collective-permute-start.9 = (f32[64,256]{1,0:T(8,128)S(1)}, f32[64,256]{1,0:T(8,128)S(1)}, u32[]{:S(2)}, u32[]{:S(2)}) collective-permute-start(f32[64,256]{1,0:T(8,128)S(1)} %get-tuple-element.37), channel_id=1, source_target_pairs={{0,1},{1,0},{2,3},{3,2},{4,5},{5,4},{6,7},{7,6},{8,9},{9,8},{10,11... | collective-permute-start | bytes 196616 | tf_op jit(solution)/shard_map/ppermute | solution.py:60
  20.2 2.4 %shard_map.82 = (f32[64,256]{1,0:T(8,128)S(1)}, f32[64,256]{1,0:T(8,128)S(1)}, f32[64,256]{1,0:T(8,128)S(1)}, f32[64,256]{1,0:T(8,128)S(1)}, f32[4,64,256]{2,1,0:T(8,128)S(1)}) custom-call(f32[2,64,256]{2,1,0:T(8,128)S(1)} %shard_map.78.refs_4_.refs_0_, f32[2,64,256]{2,1,0:T(8,128)S(1)} %collective-permute-done.1.refs_1_, ...), custom_call_target="tpu_custom_call" | custom-call | flops 1073741824 | tf_op jit(solution)/shard_map/pallas_call | solution.py:71
  22.6 1.8 %collective-permute-done.8.refs_2_ = f32[64,256]{1,0:T(8,128)S(1)} collective-permute-done((f32[64,256]{1,0:T(8,128)S(1)}, f32[64,256]{1,0:T(8,128)S(1)}, u32[]{:S(2)}, u32[]{:S(2)}) %collective-permute-start.8) | collective-permute-done | bytes 65568 | tf_op jit(solution)/shard_map/ppermute | solution.py:60
  24.4 2.5 %collective-permute-start.12 = (f32[64,256]{1,0:T(8,128)S(1)}, f32[64,256]{1,0:T(8,128)S(1)}, u32[]{:S(2)}, u32[]{:S(2)}) collective-permute-start(f32[64,256]{1,0:T(8,128)S(1)} %shard_map.83.refs_0_.refs_9_), channel_id=1, source_target_pairs={{24,0},{28,4},{16,8},{20,12},{8,16},{12,20},{0,24},{4,28},{25,1},{... | collective-permute-start | bytes 196616 | tf_op jit(solution)/shard_map/ppermute | solution.py:54
  27.0 0.5 collective-permute-start.11
  27.5 0.5 collective-permute-start.10
  28.0 1.8 %collective-permute-done.12.refs_3_ = f32[64,256]{1,0:T(8,128)S(1)} collective-permute-done((f32[64,256]{1,0:T(8,128)S(1)}, f32[64,256]{1,0:T(8,128)S(1)}, u32[]{:S(2)}, u32[]{:S(2)}) %collective-permute-start.12) | collective-permute-done | bytes 65568 | tf_op jit(solution)/shard_map/ppermute | solution.py:54
  29.8 1.4 %collective-permute-done.11.refs_2_ = f32[64,256]{1,0:T(8,128)S(1)} collective-permute-done((f32[64,256]{1,0:T(8,128)S(1)}, f32[64,256]{1,0:T(8,128)S(1)}, u32[]{:S(2)}, u32[]{:S(2)}) %collective-permute-start.11) | collective-permute-done | bytes 65568 | tf_op jit(solution)/shard_map/ppermute | solution.py:54
  31.2 0.5 collective-permute-done.10.refs_1_
  31.7 0.1 collective-permute-start.13
  31.9 1.6 %collective-permute-start.14 = (f32[64,256]{1,0:T(8,128)S(1)}, f32[64,256]{1,0:T(8,128)S(1)}, u32[]{:S(2)}, u32[]{:S(2)}) collective-permute-start(f32[64,256]{1,0:T(8,128)S(1)} %shard_map.88), channel_id=1, source_target_pairs={{24,0},{28,4},{16,8},{20,12},{8,16},{12,20},{0,24},{4,28},{25,1},{... | collective-permute-start | bytes 196616 | tf_op jit(solution)/shard_map/ppermute | solution.py:54
  33.4 0.7 %shard_map.85.refs_2_ = f32[3,64,1024]{2,1,0:T(8,128)S(1)} custom-call(f32[4,64,256]{2,1,0:T(8,128)S(1)} %shard_map.84.refs_0_.refs_1_, bf16[8,2048,256]{2,1,0:T(8,128)(2,1)S(1)} %get-tuple-element.29.refs_1_.refs_3_.refs_2_), custom_call_target="tpu_custom_call" | custom-call | flops 536870912 | tf_op jit(solution)/shard_map/pallas_call | solution.py:71
  34.2 0.8 %shard_map.86 = (f32[64,256]{1,0:T(8,128)S(1)}, f32[64,256]{1,0:T(8,128)S(1)}, f32[64,256]{1,0:T(8,128)S(1)}, f32[64,256]{1,0:T(8,128)S(1)}) custom-call(f32[4,64,256]{2,1,0:T(8,128)S(1)} %collective-permute-done.13.refs_0_, f32[4,64,256]{2,1,0:T(8,128)S(1)} %shard_map.84.refs_0_.refs_1_, f32[3,64,1024]{2,1,0:T(8,128)S(1)} %shard_map.85.refs_2_, ...), custom_call_target="tpu_custom_call" | custom-call | flops 536870912 | tf_op jit(solution)/shard_map/pallas_call | solution.py:71
  35.0 1.8 %collective-permute-start.17 = (f32[64,256]{1,0:T(8,128)S(1)}, f32[64,256]{1,0:T(8,128)S(1)}, u32[]{:S(2)}, u32[]{:S(2)}) collective-permute-start(f32[64,256]{1,0:T(8,128)S(1)} %get-tuple-element.42), channel_id=1, source_target_pairs={{0,3},{1,2},{2,1},{3,0},{4,7},{5,6},{6,5},{7,4},{8,11},{9,10},{10,... | collective-permute-start | bytes 196616 | tf_op jit(solution)/shard_map/ppermute | solution.py:60
  36.7 2.7 %collective-permute-start.19 = (f32[64,256]{1,0:T(8,128)S(1)}, f32[64,256]{1,0:T(8,128)S(1)}, u32[]{:S(2)}, u32[]{:S(2)}) collective-permute-start(f32[64,256]{1,0:T(8,128)S(1)} %get-tuple-element.44), channel_id=1, source_target_pairs={{0,1},{1,0},{2,3},{3,2},{4,5},{5,4},{6,7},{7,6},{8,9},{9,8},{10,11... | collective-permute-start | bytes 196616 | tf_op jit(solution)/shard_map/ppermute | solution.py:60
  39.5 0.8 %collective-permute-start.15 = (f32[64,256]{1,0:T(8,128)S(1)}, f32[64,256]{1,0:T(8,128)S(1)}, u32[]{:S(2)}, u32[]{:S(2)}) collective-permute-start(f32[64,256]{1,0:T(8,128)S(1)} %shard_map.89), channel_id=1, source_target_pairs={{16,0},{20,4},{24,8},{28,12},{0,16},{4,20},{8,24},{12,28},{17,1},{... | collective-permute-start | bytes 196616 | tf_op jit(solution)/shard_map/ppermute | solution.py:54
  40.2 1.4 %collective-permute-start.16 = (f32[64,256]{1,0:T(8,128)S(1)}, f32[64,256]{1,0:T(8,128)S(1)}, u32[]{:S(2)}, u32[]{:S(2)}) collective-permute-start(f32[64,256]{1,0:T(8,128)S(1)} %shard_map.90), channel_id=1, source_target_pairs={{8,0},{12,4},{0,8},{4,12},{24,16},{28,20},{16,24},{20,28},{9,1},{1... | collective-permute-start | bytes 196616 | tf_op jit(solution)/shard_map/ppermute | solution.py:54
  41.6 0.2 collective-permute-done.17.refs_5_
  41.9 2.0 %collective-permute-done.18.refs_6_ = f32[64,256]{1,0:T(8,128)S(1)} collective-permute-done((f32[64,256]{1,0:T(8,128)S(1)}, f32[64,256]{1,0:T(8,128)S(1)}, u32[]{:S(2)}, u32[]{:S(2)}) %collective-permute-start.18) | collective-permute-done | bytes 65568 | tf_op jit(solution)/shard_map/ppermute | solution.py:60
  43.9 0.7 collective-permute-done.16.refs_3_
  44.6 0.5 shard_map.91
  45.0 2.3 %collective-permute-start.22 = (f32[80,256]{1,0:T(8,128)S(1)}, f32[80,256]{1,0:T(8,128)S(1)}, u32[]{:S(2)}, u32[]{:S(2)}) collective-permute-start(f32[80,256]{1,0:T(8,128)S(1)} %get-tuple-element.45.refs_0_), channel_id=1, source_target_pairs={{24,0},{28,4},{16,8},{20,12},{8,16},{12,20},{0,24},{4,28},{25,1},{... | collective-permute-start | bytes 245768 | tf_op jit(solution)/shard_map/ppermute | solution.py:54
  47.4 0.5 collective-permute-start.21
  47.9 0.7 collective-permute-start.20
  48.6 3.9 %collective-permute-done.23 = f32[32,256]{1,0:T(8,128)S(1)} collective-permute-done((f32[32,256]{1,0:T(8,128)S(1)}, f32[32,256]{1,0:T(8,128)S(1)}, u32[]{:S(2)}, u32[]{:S(2)}) %collective-permute-start.23) | collective-permute-done | bytes 32800 | tf_op jit(solution)/shard_map/ppermute | solution.py:54
  52.7 0.3 collective-permute-start.25
  52.9 0.7 %shard_map.93.refs_2_ = f32[3,64,1024]{2,1,0:T(8,128)S(1)} custom-call(f32[4,80,256]{2,1,0:T(8,128)S(1)} %shard_map.92.refs_0_.refs_1_, bf16[8,2048,256]{2,1,0:T(8,128)(2,1)S(1)} %get-tuple-element.29.refs_1_.refs_3_.refs_2_), custom_call_target="tpu_custom_call" | custom-call | flops 536870912 | tf_op jit(solution)/shard_map/pallas_call | solution.py:71
  53.7 4.0 %collective-permute-done.25.refs_1_ = f32[32,256]{1,0:T(8,128)S(1)} collective-permute-done((f32[32,256]{1,0:T(8,128)S(1)}, f32[32,256]{1,0:T(8,128)S(1)}, u32[]{:S(2)}, u32[]{:S(2)}) %collective-permute-start.25) | collective-permute-done | bytes 32800 | tf_op jit(solution)/shard_map/ppermute | solution.py:54
  57.7 0.8 %shard_map.95 = (f32[80,256]{1,0:T(8,128)S(1)}, f32[80,256]{1,0:T(8,128)S(1)}, f32[80,256]{1,0:T(8,128)S(1)}, f32[80,256]{1,0:T(8,128)S(1)}) custom-call(f32[4,80,256]{2,1,0:T(8,128)S(1)} %collective-permute-done.24.refs_0_, f32[4,80,256]{2,1,0:T(8,128)S(1)} %shard_map.92.refs_0_.refs_1_, f32[3,64,1024]{2,1,0:T(8,128)S(1)} %shard_map.93.refs_2_, ...), custom_call_target="tpu_custom_call" | custom-call | flops 536870912 | tf_op jit(solution)/shard_map/pallas_call | solution.py:71
  58.6 1.7 %collective-permute-start.26 = (f32[80,256]{1,0:T(8,128)S(1)}, f32[80,256]{1,0:T(8,128)S(1)}, u32[]{:S(2)}, u32[]{:S(2)}) collective-permute-start(f32[80,256]{1,0:T(8,128)S(1)} %get-tuple-element.48), channel_id=1, source_target_pairs={{0,3},{1,2},{2,1},{3,0},{4,7},{5,6},{6,5},{7,4},{8,11},{9,10},{10,... | collective-permute-start | bytes 245768 | tf_op jit(solution)/shard_map/ppermute | solution.py:60
  60.3 2.7 %collective-permute-start.28 = (f32[80,256]{1,0:T(8,128)S(1)}, f32[80,256]{1,0:T(8,128)S(1)}, u32[]{:S(2)}, u32[]{:S(2)}) collective-permute-start(f32[80,256]{1,0:T(8,128)S(1)} %get-tuple-element.50), channel_id=1, source_target_pairs={{0,1},{1,0},{2,3},{3,2},{4,5},{5,4},{6,7},{7,6},{8,9},{9,8},{10,11... | collective-permute-start | bytes 245768 | tf_op jit(solution)/shard_map/ppermute | solution.py:60
  63.0 1.4 %collective-permute-start.30 = (f32[32,256]{1,0:T(8,128)S(1)}, f32[32,256]{1,0:T(8,128)S(1)}, u32[]{:S(2)}, u32[]{:S(2)}) collective-permute-start(f32[32,256]{1,0:T(8,128)S(1)} %add.13), channel_id=1, source_target_pairs={{8,0},{12,4},{0,8},{4,12},{24,16},{28,20},{16,24},{20,28},{9,1},{1... | collective-permute-start | bytes 98312 | tf_op jit(solution)/shard_map/ppermute | solution.py:54
  64.4 2.6 %collective-permute-done.30 = f32[32,256]{1,0:T(8,128)S(1)} collective-permute-done((f32[32,256]{1,0:T(8,128)S(1)}, f32[32,256]{1,0:T(8,128)S(1)}, u32[]{:S(2)}, u32[]{:S(2)}) %collective-permute-start.30) | collective-permute-done | bytes 32800 | tf_op jit(solution)/shard_map/ppermute | solution.py:54
  67.0 1.3 %collective-permute-start.31 = (f32[32,256]{1,0:T(8,128)S(1)}, f32[32,256]{1,0:T(8,128)S(1)}, u32[]{:S(2)}, u32[]{:S(2)}) collective-permute-start(f32[32,256]{1,0:T(8,128)S(1)} %add.14), channel_id=1, source_target_pairs={{16,0},{20,4},{24,8},{28,12},{0,16},{4,20},{8,24},{12,28},{17,1},{... | collective-permute-start | bytes 98312 | tf_op jit(solution)/shard_map/ppermute | solution.py:54
  68.4 2.6 %collective-permute-done.31 = f32[32,256]{1,0:T(8,128)S(1)} collective-permute-done((f32[32,256]{1,0:T(8,128)S(1)}, f32[32,256]{1,0:T(8,128)S(1)}, u32[]{:S(2)}, u32[]{:S(2)}) %collective-permute-start.31) | collective-permute-done | bytes 32800 | tf_op jit(solution)/shard_map/ppermute | solution.py:54
  71.0 0.4 shard_map.97
  71.4 1.1 %shard_map.98 = (f32[3,64,64]{2,1,0:T(8,128)}, f32[64,256]{1,0:T(8,128)}) custom-call(f32[80,256]{1,0:T(8,128)S(1)} %get-tuple-element.47.refs_1_.refs_0_, f32[80,256]{1,0:T(8,128)S(1)} %collective-permute-done.26.refs_1_, f32[80,256]{1,0:T(8,128)S(1)} %collective-permute-done.27.refs_2_, f32[80,256]{1,0:T(8,128)S(1)} %collective-permute-done.28.refs_3_, ...), custom_call_target="tpu_custom_call" | custom-call | tf_op jit(solution)/shard_map/pallas_call | solution.py:71
  (42 shorter events, 0.4 us)
Async XLA Ops:
  0.6 11.8 %collective-permute-start = (f32[64,256]{1,0:T(8,128)}, f32[64,256]{1,0:T(8,128)S(1)}, u32[]{:S(2)}, u32[]{:S(2)}) collective-permute-start(f32[64,256]{1,0:T(8,128)} %refs_4_.1), channel_id=1, source_target_pairs={{2,0},{3,1},{0,2},{1,3},{6,4},{7,5},{4,6},{5,7},{10,8},{11,9},{8,1... | collective-permute-start | bytes 196616 | tf_op jit(solution)/shard_map/ppermute | solution.py:54
  4.7 7.7 %collective-permute-start.2 = (f32[64,256]{1,0:T(8,128)}, f32[64,256]{1,0:T(8,128)S(1)}, u32[]{:S(2)}, u32[]{:S(2)}) collective-permute-start(f32[64,256]{1,0:T(8,128)} %refs_5_.1), channel_id=1, source_target_pairs={{8,0},{12,4},{0,8},{4,12},{24,16},{28,20},{16,24},{20,28},{9,1},{1... | collective-permute-start | bytes 196616 | tf_op jit(solution)/shard_map/ppermute | solution.py:54
  6.2 6.2 %collective-permute-start.4 = (f32[64,256]{1,0:T(8,128)}, f32[64,256]{1,0:T(8,128)S(1)}, u32[]{:S(2)}, u32[]{:S(2)}) collective-permute-start(f32[64,256]{1,0:T(8,128)} %refs_5_.1), channel_id=1, source_target_pairs={{24,0},{28,4},{16,8},{20,12},{8,16},{12,20},{0,24},{4,28},{25,1},{... | collective-permute-start | bytes 196616 | tf_op jit(solution)/shard_map/ppermute | solution.py:54
  7.7 4.7 %collective-permute-start.3 = (f32[64,256]{1,0:T(8,128)}, f32[64,256]{1,0:T(8,128)S(1)}, u32[]{:S(2)}, u32[]{:S(2)}) collective-permute-start(f32[64,256]{1,0:T(8,128)} %refs_5_.1), channel_id=1, source_target_pairs={{16,0},{20,4},{24,8},{28,12},{0,16},{4,20},{8,24},{12,28},{17,1},{... | collective-permute-start | bytes 196616 | tf_op jit(solution)/shard_map/ppermute | solution.py:54
  12.5 2.5 %collective-permute-start.5 = (f32[4,64,256]{2,1,0:T(8,128)S(1)}, f32[4,64,256]{2,1,0:T(8,128)S(1)}, u32[]{:S(2)}, u32[]{:S(2)}) collective-permute-start(f32[4,64,256]{2,1,0:T(8,128)S(1)} %shard_map.79.refs_0_.refs_1_), channel_id=1, source_target_pairs={{4,0},{0,4},{12,8},{8,12},{20,16},{16,20},{28,24},{24,28},{5,1},{1... | collective-permute-start | bytes 786440 | tf_op jit(solution)/shard_map/ppermute | solution.py:54
  12.6 7.7 %collective-permute-start.1 = (f32[2,64,256]{2,1,0:T(8,128)S(1)}, f32[2,64,256]{2,1,0:T(8,128)S(1)}, u32[]{:S(2)}, u32[]{:S(2)}) collective-permute-start(f32[2,64,256]{2,1,0:T(8,128)S(1)} %shard_map.78.refs_4_.refs_0_), channel_id=1, source_target_pairs={{1,0},{0,1},{3,2},{2,3},{5,4},{4,5},{7,6},{6,7},{9,8},{8,9},{11,10... | collective-permute-start | bytes 393224 | tf_op jit(solution)/shard_map/ppermute | solution.py:54
  15.8 6.9 %collective-permute-start.7 = (f32[64,256]{1,0:T(8,128)S(1)}, f32[64,256]{1,0:T(8,128)S(1)}, u32[]{:S(2)}, u32[]{:S(2)}) collective-permute-start(f32[64,256]{1,0:T(8,128)S(1)} %get-tuple-element.35), channel_id=1, source_target_pairs={{0,3},{1,2},{2,1},{3,0},{4,7},{5,6},{6,5},{7,4},{8,11},{9,10},{10,... | collective-permute-start | bytes 196616 | tf_op jit(solution)/shard_map/ppermute | solution.py:60
  16.3 8.1 %collective-permute-start.8 = (f32[64,256]{1,0:T(8,128)S(1)}, f32[64,256]{1,0:T(8,128)S(1)}, u32[]{:S(2)}, u32[]{:S(2)}) collective-permute-start(f32[64,256]{1,0:T(8,128)S(1)} %get-tuple-element.36), channel_id=1, source_target_pairs={{0,2},{1,3},{2,0},{3,1},{4,6},{5,7},{6,4},{7,5},{8,10},{9,11},{10,... | collective-permute-start | bytes 196616 | tf_op jit(solution)/shard_map/ppermute | solution.py:60
  18.0 6.5 %collective-permute-start.9 = (f32[64,256]{1,0:T(8,128)S(1)}, f32[64,256]{1,0:T(8,128)S(1)}, u32[]{:S(2)}, u32[]{:S(2)}) collective-permute-start(f32[64,256]{1,0:T(8,128)S(1)} %get-tuple-element.37), channel_id=1, source_target_pairs={{0,1},{1,0},{2,3},{3,2},{4,5},{5,4},{6,7},{7,6},{8,9},{9,8},{10,11... | collective-permute-start | bytes 196616 | tf_op jit(solution)/shard_map/ppermute | solution.py:60
  24.4 5.3 %collective-permute-start.12 = (f32[64,256]{1,0:T(8,128)S(1)}, f32[64,256]{1,0:T(8,128)S(1)}, u32[]{:S(2)}, u32[]{:S(2)}) collective-permute-start(f32[64,256]{1,0:T(8,128)S(1)} %shard_map.83.refs_0_.refs_9_), channel_id=1, source_target_pairs={{24,0},{28,4},{16,8},{20,12},{8,16},{12,20},{0,24},{4,28},{25,1},{... | collective-permute-start | bytes 196616 | tf_op jit(solution)/shard_map/ppermute | solution.py:54
  27.0 4.3 %collective-permute-start.11 = (f32[64,256]{1,0:T(8,128)S(1)}, f32[64,256]{1,0:T(8,128)S(1)}, u32[]{:S(2)}, u32[]{:S(2)}) collective-permute-start(f32[64,256]{1,0:T(8,128)S(1)} %shard_map.83.refs_0_.refs_9_), channel_id=1, source_target_pairs={{16,0},{20,4},{24,8},{28,12},{0,16},{4,20},{8,24},{12,28},{17,1},{... | collective-permute-start | bytes 196616 | tf_op jit(solution)/shard_map/ppermute | solution.py:54
  27.5 4.3 %collective-permute-start.10 = (f32[64,256]{1,0:T(8,128)S(1)}, f32[64,256]{1,0:T(8,128)S(1)}, u32[]{:S(2)}, u32[]{:S(2)}) collective-permute-start(f32[64,256]{1,0:T(8,128)S(1)} %shard_map.83.refs_0_.refs_9_), channel_id=1, source_target_pairs={{8,0},{12,4},{0,8},{4,12},{24,16},{28,20},{16,24},{20,28},{9,1},{1... | collective-permute-start | bytes 196616 | tf_op jit(solution)/shard_map/ppermute | solution.py:54
  28.0 3.8 %collective-permute-start.6 = (f32[4,64,256]{2,1,0:T(8,128)S(1)}, f32[4,64,256]{2,1,0:T(8,128)S(1)}, u32[]{:S(2)}, u32[]{:S(2)}) collective-permute-start(f32[4,64,256]{2,1,0:T(8,128)S(1)} %get-tuple-element.34.refs_4_), channel_id=1, source_target_pairs={{4,0},{0,4},{12,8},{8,12},{20,16},{16,20},{28,24},{24,28},{5,1},{1... | collective-permute-start | bytes 786440 | tf_op jit(solution)/shard_map/ppermute | solution.py:54
  31.7 2.4 %collective-permute-start.13 = (f32[4,64,256]{2,1,0:T(8,128)S(1)}, f32[4,64,256]{2,1,0:T(8,128)S(1)}, u32[]{:S(2)}, u32[]{:S(2)}) collective-permute-start(f32[4,64,256]{2,1,0:T(8,128)S(1)} %shard_map.84.refs_0_.refs_1_), channel_id=1, source_target_pairs={{4,0},{0,4},{12,8},{8,12},{20,16},{16,20},{28,24},{24,28},{5,1},{1... | collective-permute-start | bytes 786440 | tf_op jit(solution)/shard_map/ppermute | solution.py:54
  31.9 8.4 %collective-permute-start.14 = (f32[64,256]{1,0:T(8,128)S(1)}, f32[64,256]{1,0:T(8,128)S(1)}, u32[]{:S(2)}, u32[]{:S(2)}) collective-permute-start(f32[64,256]{1,0:T(8,128)S(1)} %shard_map.88), channel_id=1, source_target_pairs={{24,0},{28,4},{16,8},{20,12},{8,16},{12,20},{0,24},{4,28},{25,1},{... | collective-permute-start | bytes 196616 | tf_op jit(solution)/shard_map/ppermute | solution.py:54
  35.0 6.9 %collective-permute-start.17 = (f32[64,256]{1,0:T(8,128)S(1)}, f32[64,256]{1,0:T(8,128)S(1)}, u32[]{:S(2)}, u32[]{:S(2)}) collective-permute-start(f32[64,256]{1,0:T(8,128)S(1)} %get-tuple-element.42), channel_id=1, source_target_pairs={{0,3},{1,2},{2,1},{3,0},{4,7},{5,6},{6,5},{7,4},{8,11},{9,10},{10,... | collective-permute-start | bytes 196616 | tf_op jit(solution)/shard_map/ppermute | solution.py:60
  36.7 7.1 %collective-permute-start.18 = (f32[64,256]{1,0:T(8,128)S(1)}, f32[64,256]{1,0:T(8,128)S(1)}, u32[]{:S(2)}, u32[]{:S(2)}) collective-permute-start(f32[64,256]{1,0:T(8,128)S(1)} %get-tuple-element.43), channel_id=1, source_target_pairs={{0,2},{1,3},{2,0},{3,1},{4,6},{5,7},{6,4},{7,5},{8,10},{9,11},{10,... | collective-permute-start | bytes 196616 | tf_op jit(solution)/shard_map/ppermute | solution.py:60
  36.7 7.1 %collective-permute-start.19 = (f32[64,256]{1,0:T(8,128)S(1)}, f32[64,256]{1,0:T(8,128)S(1)}, u32[]{:S(2)}, u32[]{:S(2)}) collective-permute-start(f32[64,256]{1,0:T(8,128)S(1)} %get-tuple-element.44), channel_id=1, source_target_pairs={{0,1},{1,0},{2,3},{3,2},{4,5},{5,4},{6,7},{7,6},{8,9},{9,8},{10,11... | collective-permute-start | bytes 196616 | tf_op jit(solution)/shard_map/ppermute | solution.py:60
  39.5 4.4 %collective-permute-start.15 = (f32[64,256]{1,0:T(8,128)S(1)}, f32[64,256]{1,0:T(8,128)S(1)}, u32[]{:S(2)}, u32[]{:S(2)}) collective-permute-start(f32[64,256]{1,0:T(8,128)S(1)} %shard_map.89), channel_id=1, source_target_pairs={{16,0},{20,4},{24,8},{28,12},{0,16},{4,20},{8,24},{12,28},{17,1},{... | collective-permute-start | bytes 196616 | tf_op jit(solution)/shard_map/ppermute | solution.py:54
  40.2 4.3 %collective-permute-start.16 = (f32[64,256]{1,0:T(8,128)S(1)}, f32[64,256]{1,0:T(8,128)S(1)}, u32[]{:S(2)}, u32[]{:S(2)}) collective-permute-start(f32[64,256]{1,0:T(8,128)S(1)} %shard_map.90), channel_id=1, source_target_pairs={{8,0},{12,4},{0,8},{4,12},{24,16},{28,20},{16,24},{20,28},{9,1},{1... | collective-permute-start | bytes 196616 | tf_op jit(solution)/shard_map/ppermute | solution.py:54
  45.0 7.5 %collective-permute-start.22 = (f32[80,256]{1,0:T(8,128)S(1)}, f32[80,256]{1,0:T(8,128)S(1)}, u32[]{:S(2)}, u32[]{:S(2)}) collective-permute-start(f32[80,256]{1,0:T(8,128)S(1)} %get-tuple-element.45.refs_0_), channel_id=1, source_target_pairs={{24,0},{28,4},{16,8},{20,12},{8,16},{12,20},{0,24},{4,28},{25,1},{... | collective-permute-start | bytes 245768 | tf_op jit(solution)/shard_map/ppermute | solution.py:54
  47.4 5.2 %collective-permute-start.21 = (f32[80,256]{1,0:T(8,128)S(1)}, f32[80,256]{1,0:T(8,128)S(1)}, u32[]{:S(2)}, u32[]{:S(2)}) collective-permute-start(f32[80,256]{1,0:T(8,128)S(1)} %get-tuple-element.45.refs_0_), channel_id=1, source_target_pairs={{16,0},{20,4},{24,8},{28,12},{0,16},{4,20},{8,24},{12,28},{17,1},{... | collective-permute-start | bytes 245768 | tf_op jit(solution)/shard_map/ppermute | solution.py:54
  47.9 4.7 %collective-permute-start.20 = (f32[80,256]{1,0:T(8,128)S(1)}, f32[80,256]{1,0:T(8,128)S(1)}, u32[]{:S(2)}, u32[]{:S(2)}) collective-permute-start(f32[80,256]{1,0:T(8,128)S(1)} %get-tuple-element.45.refs_0_), channel_id=1, source_target_pairs={{8,0},{12,4},{0,8},{4,12},{24,16},{28,20},{16,24},{20,28},{9,1},{1... | collective-permute-start | bytes 245768 | tf_op jit(solution)/shard_map/ppermute | solution.py:54
  48.6 3.9 %collective-permute-start.23 = (f32[32,256]{1,0:T(8,128)S(1)}, f32[32,256]{1,0:T(8,128)S(1)}, u32[]{:S(2)}, u32[]{:S(2)}) collective-permute-start(f32[32,256]{1,0:T(8,128)S(1)} %get-tuple-element.46), channel_id=1, source_target_pairs={{1,0},{0,1},{3,2},{2,3},{5,4},{4,5},{7,6},{6,7},{9,8},{8,9},{11,10... | collective-permute-start | bytes 98312 | tf_op jit(solution)/shard_map/ppermute | solution.py:54
  52.6 5.1 %collective-permute-start.24 = (f32[4,80,256]{2,1,0:T(8,128)S(1)}, f32[4,80,256]{2,1,0:T(8,128)S(1)}, u32[]{:S(2)}, u32[]{:S(2)}) collective-permute-start(f32[4,80,256]{2,1,0:T(8,128)S(1)} %shard_map.92.refs_0_.refs_1_), channel_id=1, source_target_pairs={{4,0},{0,4},{12,8},{8,12},{20,16},{16,20},{28,24},{24,28},{5,1},{1... | collective-permute-start | bytes 983048 | tf_op jit(solution)/shard_map/ppermute | solution.py:54
  52.7 5.0 %collective-permute-start.25 = (f32[32,256]{1,0:T(8,128)S(1)}, f32[32,256]{1,0:T(8,128)S(1)}, u32[]{:S(2)}, u32[]{:S(2)}) collective-permute-start(f32[32,256]{1,0:T(8,128)S(1)} %add.12.refs_4_.refs_0_), channel_id=1, source_target_pairs={{2,0},{3,1},{0,2},{1,3},{6,4},{7,5},{4,6},{5,7},{10,8},{11,9},{8,1... | collective-permute-start | bytes 98312 | tf_op jit(solution)/shard_map/ppermute | solution.py:54
  58.5 4.5 %collective-permute-start.29 = (f32[32,256]{1,0:T(8,128)S(1)}, f32[32,256]{1,0:T(8,128)S(1)}, u32[]{:S(2)}, u32[]{:S(2)}) collective-permute-start(f32[32,256]{1,0:T(8,128)S(1)} %shard_map.96), channel_id=1, source_target_pairs={{4,0},{0,4},{12,8},{8,12},{20,16},{16,20},{28,24},{24,28},{5,1},{1... | collective-permute-start | bytes 98312 | tf_op jit(solution)/shard_map/ppermute | solution.py:54
  58.6 12.8 %collective-permute-start.26 = (f32[80,256]{1,0:T(8,128)S(1)}, f32[80,256]{1,0:T(8,128)S(1)}, u32[]{:S(2)}, u32[]{:S(2)}) collective-permute-start(f32[80,256]{1,0:T(8,128)S(1)} %get-tuple-element.48), channel_id=1, source_target_pairs={{0,3},{1,2},{2,1},{3,0},{4,7},{5,6},{6,5},{7,4},{8,11},{9,10},{10,... | collective-permute-start | bytes 245768 | tf_op jit(solution)/shard_map/ppermute | solution.py:60
  60.3 11.1 %collective-permute-start.27 = (f32[80,256]{1,0:T(8,128)S(1)}, f32[80,256]{1,0:T(8,128)S(1)}, u32[]{:S(2)}, u32[]{:S(2)}) collective-permute-start(f32[80,256]{1,0:T(8,128)S(1)} %get-tuple-element.49), channel_id=1, source_target_pairs={{0,2},{1,3},{2,0},{3,1},{4,6},{5,7},{6,4},{7,5},{8,10},{9,11},{10,... | collective-permute-start | bytes 245768 | tf_op jit(solution)/shard_map/ppermute | solution.py:60
  60.3 11.1 %collective-permute-start.28 = (f32[80,256]{1,0:T(8,128)S(1)}, f32[80,256]{1,0:T(8,128)S(1)}, u32[]{:S(2)}, u32[]{:S(2)}) collective-permute-start(f32[80,256]{1,0:T(8,128)S(1)} %get-tuple-element.50), channel_id=1, source_target_pairs={{0,1},{1,0},{2,3},{3,2},{4,5},{5,4},{6,7},{7,6},{8,9},{9,8},{10,11... | collective-permute-start | bytes 245768 | tf_op jit(solution)/shard_map/ppermute | solution.py:60
  63.0 4.0 %collective-permute-start.30 = (f32[32,256]{1,0:T(8,128)S(1)}, f32[32,256]{1,0:T(8,128)S(1)}, u32[]{:S(2)}, u32[]{:S(2)}) collective-permute-start(f32[32,256]{1,0:T(8,128)S(1)} %add.13), channel_id=1, source_target_pairs={{8,0},{12,4},{0,8},{4,12},{24,16},{28,20},{16,24},{20,28},{9,1},{1... | collective-permute-start | bytes 98312 | tf_op jit(solution)/shard_map/ppermute | solution.py:54
  67.0 3.9 %collective-permute-start.31 = (f32[32,256]{1,0:T(8,128)S(1)}, f32[32,256]{1,0:T(8,128)S(1)}, u32[]{:S(2)}, u32[]{:S(2)}) collective-permute-start(f32[32,256]{1,0:T(8,128)S(1)} %add.14), channel_id=1, source_target_pairs={{16,0},{20,4},{24,8},{28,12},{0,16},{4,20},{8,24},{12,28},{17,1},{... | collective-permute-start | bytes 98312 | tf_op jit(solution)/shard_map/ppermute | solution.py:54

commit v8 on v7

--- a/solution.py
+++ b/solution.py
@@ -254,6 +254,11 @@
             sums_ref[index, :, block * tile_len : (block + 1) * tile_len] = part
 
 
+def half_of_core(packed):
+    rows = packed.shape[0] // 2
+    return jnp.where(lax.axis_index("row") % 2 == 0, packed[:rows], packed[rows:])
+
+
 def second_half_kernel(span, pieces_ref, evens_ref, sums_ref, dense_ref, *refs):
     outs, digits = refs[:-1], refs[-1]
     n_col = len(outs)
@@ -272,6 +277,7 @@
             outs[e][:span, sub * tile_len : (sub + 1) * tile_len] = combine(*parts)
     if outs[0].shape[0] > span:
         packed = jnp.sum(pieces_ref[:, span:, :], 0) + jnp.sum(evens_ref[:, span:, :], 0)
+        packed = half_of_core(packed)
         for out in outs:
             out[span:, :] = packed
 
@@ -295,7 +301,7 @@
         call(
             functools.partial(second_half_kernel, span),
             [odds, evens, sums, dense],
-            [held(rows, piece_len)] * n_col,
+            [held(span + (rows - span) // 2, piece_len)] * n_col,
             before,
             scratch=[pltpu.VMEM((2 * span, depth // 2), jnp.bfloat16)],
             limit=VMEM_LIMIT,
@@ -387,7 +393,7 @@
     blocks = n_col * piece_len // a_digits.shape[-1]
     vector = reduce_centered(jnp.concatenate([piece[:span] for piece in pieces], 1))
     product = sparse_product(vector, "ntk,tdik->tdni", cols, rows, count, blocks, a_digits)
-    packed = functools.reduce(jnp.add, [piece[span:] for piece in pieces])
+    packed = half_of_core(functools.reduce(jnp.add, [piece[span:] for piece in pieces]))
     outs = [product[:, e * piece_len : (e + 1) * piece_len] for e in range(n_col)]
     return [jnp.concatenate([out, packed], 0) for out in outs]
 
@@ -412,13 +418,6 @@
     return call(kernel, [evens[index], odds_came], [held(*evens[index].shape)], before)[0]
 
 
-def sum_over(packed, axis, shift=1):
-    while shift < lax.axis_size(axis):
-        packed = packed + fetch(packed, axis, shift)
-        shift *= 2
-    return packed
-
-
 def append_projections(w_parts, pieces, earlier):
     span, piece_len = pieces[0].shape
     rows = span * span // piece_len
@@ -426,7 +425,7 @@
     def kernel(*refs):
         w_refs, refs = refs[: len(w_parts)], refs[len(w_parts) :]
         piece_refs, refs = refs[: len(pieces)], refs[len(pieces) :]
-        earlier_refs, (out_ref, terms_ref) = refs[:-2], refs[-2:]
+        earlier_refs, out_ref = refs[:-1], refs[-1]
         summed = functools.reduce(jnp.add, [ref[...] for ref in piece_refs])
         out_ref[:span, :] = summed
         w_piece = functools.reduce(jnp.add, [ref[...] for ref in w_refs])
@@ -438,14 +437,11 @@
                 reduce_centered(products[:span, span:]) + reduce_centered(products[span:, :span]),
                 reduce_centered(products[span:, span:]),
             )
-            square = pack_square(square, piece_len)
-            if index == 0:
-                out_ref[span:, :] = square
-            else:
-                terms_ref[(index - 1) * rows : index * rows, :] = square
-
-    outs = [held(span + rows, piece_len), held(len(earlier) * rows, piece_len)]
-    return call(kernel, [*w_parts, *pieces, *earlier], outs)
+            start = span + index * rows
+            out_ref[start : start + rows, :] = pack_square(square, piece_len)
+
+    outs = [held(span + (len(earlier) + 1) * rows, piece_len)]
+    return call(kernel, [*w_parts, *pieces, *earlier], outs)[0]
 
 
 def multiply_mod(left, right):
@@ -459,37 +455,27 @@
     )
 
 
-def sigma_start(packed, span):
-    def kernel(packed_ref, start_ref, both_ref, rest_ref):
-        rows = packed_ref.shape[0] // 2
-        c_1 = unpack_square(reduce_centered(packed_ref[:rows, :]), span)
-        c_2 = unpack_square(reduce_centered(packed_ref[rows:, :]), span)
+def sigma_update(mine, other, span):
+    rows = span * span // mine.shape[1]
+
+    def kernel(mine_ref, other_ref, out_ref):
+        first = lax.axis_index("row") % 2 == 0
+        mine, other = reduce_centered(mine_ref[...]), reduce_centered(other_ref[...])
+        packed = jnp.concatenate([jnp.where(first, mine, other), jnp.where(first, other, mine)], 0)
+        c_3, c_1, c_2 = (
+            unpack_square(packed[index * rows : (index + 1) * rows], span) for index in range(3)
+        )
         e_2 = reduce_centered(c_1 - multiply_mod(c_1, c_2))
         both = reduce_centered(c_1 + e_2)
-        start_ref[...] = multiply_mod(e_2, c_1)
-        both_ref[...] = both
-        rest_ref[...] = c_1 - multiply_mod(both, c_2)
-
-    return call(kernel, [packed], [held(span, span)] * 3)
-
-
-def finish(pieces, known, span):
-    def kernel(*refs):
-        piece_refs, (start_ref, both_ref, rest_ref, poly_ref, vector_ref) = refs[:-5], refs[-5:]
-        summed = functools.reduce(jnp.add, [ref[...] for ref in piece_refs])
-        vector_ref[...] = canonical(summed[:span]) * (1.0 / MODULUS)
-        start, both = start_ref[...], both_ref[...]
-        c_3 = unpack_square(reduce_centered(summed[span:]), span)
-        e_3 = reduce_centered(multiply_mod(start, c_3) + rest_ref[...])
-        poly_ref[0] = canonical(-multiply_mod(e_3, start)) * (1.0 / MODULUS)
-        poly_ref[1] = canonical(start + multiply_mod(e_3, both)) * (1.0 / MODULUS)
-        poly_ref[2] = canonical(-both - e_3) * (1.0 / MODULUS)
-
-    outs = [
-        jax.ShapeDtypeStruct((STEP_COUNT, span, span), jnp.float32),
-        jax.ShapeDtypeStruct((span, pieces[0].shape[1]), jnp.float32),
-    ]
-    return tuple(call(kernel, [*pieces, *known], outs))
+        start = multiply_mod(e_2, c_1)
+        rest = c_1 - multiply_mod(both, c_2)
+        e_3 = reduce_centered(multiply_mod(start, c_3) + rest)
+        out_ref[0] = canonical(-multiply_mod(e_3, start)) * (1.0 / MODULUS)
+        out_ref[1] = canonical(start + multiply_mod(e_3, both)) * (1.0 / MODULUS)
+        out_ref[2] = canonical(-both - e_3) * (1.0 / MODULUS)
+
+    outs = [jax.ShapeDtypeStruct((STEP_COUNT, span, span), jnp.float32)]
+    return call(kernel, [mine, other], outs)[0]
 
 
 def local(tile_entries, tile_rows, tile_cols, tile_count, block_x, block_y):
@@ -540,16 +526,12 @@
     w_parts = w_parts[:1] + [
         fetch(w_parts[index], "row", 2 * index) for index in reversed(range(1, n_row // 2))
     ]
-    vector_2, terms = append_projections(w_parts, pieces, [y_own, vector_1])
-    terms = terms + fetch(terms, "col", 1)
-    evens = gather_evens(vector_2, "row", [terms])
-    odds, sums = gather_odds(evens, "row"), multiply_evens(evens)
-    if n_col > 2:
-        terms = sum_after([terms, fetch(terms, "col", 2)], [sums])
-    terms = sum_over(terms, "col", 4)
-    outs = multiply_odds(odds, evens, sums, [terms])
-    terms = sum_over(sum_after([terms], [outs[0]]), "row")
-    return finish(scatter_pieces(outs, "col"), sigma_start(terms, span), span)
+    vector_2 = append_projections(w_parts, pieces, [y_own, vector_1])
+    outs = multiply(gather_evens(vector_2, "row"), [])
+    pieces = scatter_pieces(outs, "col")
+    terms = functools.reduce(jnp.add, [piece[span:] for piece in pieces])
+    vector_3 = functools.reduce(jnp.add, [piece[:span] for piece in pieces])
+    return sigma_update(terms, fetch(terms, "row", 1), span), canonical(vector_3) * (1.0 / MODULUS)
 
 
 def solution(mesh):

time: 72.7 us -> 69.1 us (0.950)
  starting transfers between devices: 36.7 us -> 33.7 us
  waiting for transfers between devices: 21.6 us -> 20.5 us
    ppermute x23 -> x19, waiting for transfers between devices: 17.5 us -> 10.5 us  [fetch(): lax.ppermute(piece, axis, [(partner(i, shift, size), i) for i in range(si...]
    ppermute x9, waiting for transfers between devices: 4.06 us -> 9.98 us  [scatter_pieces(): lax.ppermute(pieces[shift], axis, [(i, partner(i, shift, size)) for i in...]
    ppermute x23 -> x19, starting transfers between devices: 23.3 us -> 20.3 us  [fetch(): lax.ppermute(piece, axis, [(partner(i, shift, size), i) for i in range(si...]
    pallas_call x21 -> x18, Pallas kernels: 9.19 us -> 9.09 us  [call(): pl.pallas_call(body, in_specs=[vmem] * len(operands) + [pl.BlockSpec(memo...]
  transfers between devices with their start and end apart: 32 -> 28, of which waited for: 11 -> 14; matrix products, arithmetic and copies ran while one was open for 0% -> 1% of each run, Pallas kernels for 14% -> 14%
where the time goes in v8:
time: 69.1 us; the launch traced here: 68.9 us
  starting transfers between devices  33.7 us (49%)
  waiting for transfers between devices  20.5 us (30%)
  Pallas kernels  12.6 us (18%)
  between operations  1.5 us (2%)
    ppermute x19, starting transfers between devices, fetch(): lax.ppermute(piece, axis, [(partner(i, shift, size), i) for i in range(si...  20.3 us
    ppermute x9, starting transfers between devices, scatter_pieces(): lax.ppermute(pieces[shift], axis, [(i, partner(i, shift, size)) for i in...  13.4 us
    ppermute x19, waiting for transfers between devices, fetch(): lax.ppermute(piece, axis, [(partner(i, shift, size), i) for i in range(si...  10.5 us
    ppermute x9, waiting for transfers between devices, scatter_pieces(): lax.ppermute(pieces[shift], axis, [(i, partner(i, shift, size)) for i in...  9.98 us
    pallas_call x18, Pallas kernels, call(): pl.pallas_call(body, in_specs=[vmem] * len(operands) + [pl.BlockSpec(memo...  9.09 us
    pallas_call x1, Pallas kernels, build_dense(): pl.pallas_call(functools.partial(build_kernel, (*sizes, group)), in_specs...  3.5 us
  transfers between devices with their start and end apart: 28, of which 14 were waited for; matrix products, arithmetic and copies ran while one was open for 1% of the time, Pallas kernels for 14%

profile of v8, /device:TPU:0, one launch (start us, length us, event | category | flops | bytes accessed | tf_op | source)
XLA Modules:
  0.0 68.9 jit_solution(17625288199319838741)
XLA Ops:
  0.6 4.1 %collective-permute-start = (f32[64,256]{1,0:T(8,128)}, f32[64,256]{1,0:T(8,128)S(1)}, u32[]{:S(2)}, u32[]{:S(2)}) collective-permute-start(f32[64,256]{1,0:T(8,128)} %refs_4_.1), channel_id=1, source_target_pairs={{2,0},{3,1},{0,2},{1,3},{6,4},{7,5},{4,6},{5,7},{10,8},{11,9},{8,1... | collective-permute-start | bytes 196616 | tf_op jit(solution)/shard_map/ppermute | solution.py:54
  4.7 1.5 %collective-permute-start.2 = (f32[64,256]{1,0:T(8,128)}, f32[64,256]{1,0:T(8,128)S(1)}, u32[]{:S(2)}, u32[]{:S(2)}) collective-permute-start(f32[64,256]{1,0:T(8,128)} %refs_5_.1), channel_id=1, source_target_pairs={{8,0},{12,4},{0,8},{4,12},{24,16},{28,20},{16,24},{20,28},{9,1},{1... | collective-permute-start | bytes 196616 | tf_op jit(solution)/shard_map/ppermute | solution.py:54
  6.2 1.5 %collective-permute-start.4 = (f32[64,256]{1,0:T(8,128)}, f32[64,256]{1,0:T(8,128)S(1)}, u32[]{:S(2)}, u32[]{:S(2)}) collective-permute-start(f32[64,256]{1,0:T(8,128)} %refs_5_.1), channel_id=1, source_target_pairs={{24,0},{28,4},{16,8},{20,12},{8,16},{12,20},{0,24},{4,28},{25,1},{... | collective-permute-start | bytes 196616 | tf_op jit(solution)/shard_map/ppermute | solution.py:54
  7.7 0.5 collective-permute-start.3
  8.9 3.5 %shard_map.77 = (bf16[8,2048,256]{2,1,0:T(8,128)(2,1)S(1)}, f32[64,256]{1,0:T(8,128)S(1)}, f32[64,256]{1,0:T(8,128)S(1)}, f32[8,128]{1,0:T(8,128)S(1)}) custom-call(s32[1,1,64]{2,1,0:T(1,128)} %refs_0_.1, s32[1,1,64]{2,1,0:T(1,128)} %refs_1_.1, s32[1,1]{1,0:T(1,128)S(6)} %copy.8.refs_2_, f32[1,1,64,128,128]{4,3,2,1,0:T(8,128)} %refs_3_.1, ...), custom_call_target="tpu_custom_call" | custom-call | flops 8388608 | bytes 8388608 | tf_op jit(solution)/shard_map/pallas_call | solution.py:201
  12.5 0.1 collective-permute-start.5
  12.6 1.6 %collective-permute-start.1 = (f32[2,64,256]{2,1,0:T(8,128)S(1)}, f32[2,64,256]{2,1,0:T(8,128)S(1)}, u32[]{:S(2)}, u32[]{:S(2)}) collective-permute-start(f32[2,64,256]{2,1,0:T(8,128)S(1)} %shard_map.78.refs_4_.refs_0_), channel_id=1, source_target_pairs={{1,0},{0,1},{3,2},{2,3},{5,4},{4,5},{7,6},{6,7},{9,8},{8,9},{11,10... | collective-permute-start | bytes 393224 | tf_op jit(solution)/shard_map/ppermute | solution.py:54
  14.2 0.7 %shard_map.80.refs_2_ = f32[3,64,1024]{2,1,0:T(8,128)S(1)} custom-call(f32[4,64,256]{2,1,0:T(8,128)S(1)} %shard_map.79.refs_0_.refs_1_, bf16[8,2048,256]{2,1,0:T(8,128)(2,1)S(1)} %get-tuple-element.24.refs_1_.refs_3_.refs_2_), custom_call_target="tpu_custom_call" | custom-call | flops 536870912 | tf_op jit(solution)/shard_map/pallas_call | solution.py:71
  15.0 0.8 %shard_map.81 = (f32[64,256]{1,0:T(8,128)S(1)}, f32[64,256]{1,0:T(8,128)S(1)}, f32[64,256]{1,0:T(8,128)S(1)}, f32[64,256]{1,0:T(8,128)S(1)}) custom-call(f32[4,64,256]{2,1,0:T(8,128)S(1)} %collective-permute-done.5.refs_0_, f32[4,64,256]{2,1,0:T(8,128)S(1)} %shard_map.79.refs_0_.refs_1_, f32[3,64,1024]{2,1,0:T(8,128)S(1)} %shard_map.80.refs_2_, ...), custom_call_target="tpu_custom_call" | custom-call | flops 536870912 | tf_op jit(solution)/shard_map/pallas_call | solution.py:71
  15.8 0.5 collective-permute-start.7
  16.3 1.7 %collective-permute-start.8 = (f32[64,256]{1,0:T(8,128)S(1)}, f32[64,256]{1,0:T(8,128)S(1)}, u32[]{:S(2)}, u32[]{:S(2)}) collective-permute-start(f32[64,256]{1,0:T(8,128)S(1)} %get-tuple-element.31), channel_id=1, source_target_pairs={{0,2},{1,3},{2,0},{3,1},{4,6},{5,7},{6,4},{7,5},{8,10},{9,11},{10,... | collective-permute-start | bytes 196616 | tf_op jit(solution)/shard_map/ppermute | solution.py:60
  18.0 2.3 %collective-permute-start.9 = (f32[64,256]{1,0:T(8,128)S(1)}, f32[64,256]{1,0:T(8,128)S(1)}, u32[]{:S(2)}, u32[]{:S(2)}) collective-permute-start(f32[64,256]{1,0:T(8,128)S(1)} %get-tuple-element.32), channel_id=1, source_target_pairs={{0,1},{1,0},{2,3},{3,2},{4,5},{5,4},{6,7},{7,6},{8,9},{9,8},{10,11... | collective-permute-start | bytes 196616 | tf_op jit(solution)/shard_map/ppermute | solution.py:60
  20.2 2.4 %shard_map.82 = (f32[64,256]{1,0:T(8,128)S(1)}, f32[64,256]{1,0:T(8,128)S(1)}, f32[64,256]{1,0:T(8,128)S(1)}, f32[64,256]{1,0:T(8,128)S(1)}, f32[4,64,256]{2,1,0:T(8,128)S(1)}) custom-call(f32[2,64,256]{2,1,0:T(8,128)S(1)} %shard_map.78.refs_4_.refs_0_, f32[2,64,256]{2,1,0:T(8,128)S(1)} %collective-permute-done.1.refs_1_, ...), custom_call_target="tpu_custom_call" | custom-call | flops 1073741824 | tf_op jit(solution)/shard_map/pallas_call | solution.py:71
  22.6 1.8 %collective-permute-done.8.refs_2_ = f32[64,256]{1,0:T(8,128)S(1)} collective-permute-done((f32[64,256]{1,0:T(8,128)S(1)}, f32[64,256]{1,0:T(8,128)S(1)}, u32[]{:S(2)}, u32[]{:S(2)}) %collective-permute-start.8) | collective-permute-done | bytes 65568 | tf_op jit(solution)/shard_map/ppermute | solution.py:60
  24.4 2.5 %collective-permute-start.12 = (f32[64,256]{1,0:T(8,128)S(1)}, f32[64,256]{1,0:T(8,128)S(1)}, u32[]{:S(2)}, u32[]{:S(2)}) collective-permute-start(f32[64,256]{1,0:T(8,128)S(1)} %shard_map.83.refs_0_.refs_9_), channel_id=1, source_target_pairs={{24,0},{28,4},{16,8},{20,12},{8,16},{12,20},{0,24},{4,28},{25,1},{... | collective-permute-start | bytes 196616 | tf_op jit(solution)/shard_map/ppermute | solution.py:54
  27.0 0.5 collective-permute-start.11
  27.5 0.5 collective-permute-start.10
  28.0 1.8 %collective-permute-done.12.refs_3_ = f32[64,256]{1,0:T(8,128)S(1)} collective-permute-done((f32[64,256]{1,0:T(8,128)S(1)}, f32[64,256]{1,0:T(8,128)S(1)}, u32[]{:S(2)}, u32[]{:S(2)}) %collective-permute-start.12) | collective-permute-done | bytes 65568 | tf_op jit(solution)/shard_map/ppermute | solution.py:54
  29.8 1.4 %collective-permute-done.11.refs_2_ = f32[64,256]{1,0:T(8,128)S(1)} collective-permute-done((f32[64,256]{1,0:T(8,128)S(1)}, f32[64,256]{1,0:T(8,128)S(1)}, u32[]{:S(2)}, u32[]{:S(2)}) %collective-permute-start.11) | collective-permute-done | bytes 65568 | tf_op jit(solution)/shard_map/ppermute | solution.py:54
  31.2 0.5 collective-permute-done.10.refs_1_
  31.9 1.6 %collective-permute-start.14 = (f32[64,256]{1,0:T(8,128)S(1)}, f32[64,256]{1,0:T(8,128)S(1)}, u32[]{:S(2)}, u32[]{:S(2)}) collective-permute-start(f32[64,256]{1,0:T(8,128)S(1)} %shard_map.88), channel_id=1, source_target_pairs={{24,0},{28,4},{16,8},{20,12},{8,16},{12,20},{0,24},{4,28},{25,1},{... | collective-permute-start | bytes 196616 | tf_op jit(solution)/shard_map/ppermute | solution.py:54
  33.4 0.7 %shard_map.85.refs_2_ = f32[3,64,1024]{2,1,0:T(8,128)S(1)} custom-call(f32[4,64,256]{2,1,0:T(8,128)S(1)} %shard_map.84.refs_0_.refs_1_, bf16[8,2048,256]{2,1,0:T(8,128)(2,1)S(1)} %get-tuple-element.24.refs_1_.refs_3_.refs_2_), custom_call_target="tpu_custom_call" | custom-call | flops 536870912 | tf_op jit(solution)/shard_map/pallas_call | solution.py:71
  34.2 0.8 %shard_map.86 = (f32[64,256]{1,0:T(8,128)S(1)}, f32[64,256]{1,0:T(8,128)S(1)}, f32[64,256]{1,0:T(8,128)S(1)}, f32[64,256]{1,0:T(8,128)S(1)}) custom-call(f32[4,64,256]{2,1,0:T(8,128)S(1)} %collective-permute-done.13.refs_0_, f32[4,64,256]{2,1,0:T(8,128)S(1)} %shard_map.84.refs_0_.refs_1_, f32[3,64,1024]{2,1,0:T(8,128)S(1)} %shard_map.85.refs_2_, ...), custom_call_target="tpu_custom_call" | custom-call | flops 536870912 | tf_op jit(solution)/shard_map/pallas_call | solution.py:71
  35.0 1.8 %collective-permute-start.17 = (f32[64,256]{1,0:T(8,128)S(1)}, f32[64,256]{1,0:T(8,128)S(1)}, u32[]{:S(2)}, u32[]{:S(2)}) collective-permute-start(f32[64,256]{1,0:T(8,128)S(1)} %get-tuple-element.37), channel_id=1, source_target_pairs={{0,3},{1,2},{2,1},{3,0},{4,7},{5,6},{6,5},{7,4},{8,11},{9,10},{10,... | collective-permute-start | bytes 196616 | tf_op jit(solution)/shard_map/ppermute | solution.py:60
  36.7 2.7 %collective-permute-start.19 = (f32[64,256]{1,0:T(8,128)S(1)}, f32[64,256]{1,0:T(8,128)S(1)}, u32[]{:S(2)}, u32[]{:S(2)}) collective-permute-start(f32[64,256]{1,0:T(8,128)S(1)} %get-tuple-element.39), channel_id=1, source_target_pairs={{0,1},{1,0},{2,3},{3,2},{4,5},{5,4},{6,7},{7,6},{8,9},{9,8},{10,11... | collective-permute-start | bytes 196616 | tf_op jit(solution)/shard_map/ppermute | solution.py:60
  39.5 0.8 %collective-permute-start.15 = (f32[64,256]{1,0:T(8,128)S(1)}, f32[64,256]{1,0:T(8,128)S(1)}, u32[]{:S(2)}, u32[]{:S(2)}) collective-permute-start(f32[64,256]{1,0:T(8,128)S(1)} %shard_map.89), channel_id=1, source_target_pairs={{16,0},{20,4},{24,8},{28,12},{0,16},{4,20},{8,24},{12,28},{17,1},{... | collective-permute-start | bytes 196616 | tf_op jit(solution)/shard_map/ppermute | solution.py:54
  40.2 1.4 %collective-permute-start.16 = (f32[64,256]{1,0:T(8,128)S(1)}, f32[64,256]{1,0:T(8,128)S(1)}, u32[]{:S(2)}, u32[]{:S(2)}) collective-permute-start(f32[64,256]{1,0:T(8,128)S(1)} %shard_map.90), channel_id=1, source_target_pairs={{8,0},{12,4},{0,8},{4,12},{24,16},{28,20},{16,24},{20,28},{9,1},{1... | collective-permute-start | bytes 196616 | tf_op jit(solution)/shard_map/ppermute | solution.py:54
  41.6 0.2 collective-permute-done.17.refs_5_
  41.9 2.0 %collective-permute-done.18.refs_6_ = f32[64,256]{1,0:T(8,128)S(1)} collective-permute-done((f32[64,256]{1,0:T(8,128)S(1)}, f32[64,256]{1,0:T(8,128)S(1)}, u32[]{:S(2)}, u32[]{:S(2)}) %collective-permute-start.18) | collective-permute-done | bytes 65568 | tf_op jit(solution)/shard_map/ppermute | solution.py:60
  43.9 0.7 %collective-permute-done.16.refs_3_ = f32[64,256]{1,0:T(8,128)S(1)} collective-permute-done((f32[64,256]{1,0:T(8,128)S(1)}, f32[64,256]{1,0:T(8,128)S(1)}, u32[]{:S(2)}, u32[]{:S(2)}) %collective-permute-start.16) | collective-permute-done | bytes 65568 | tf_op jit(solution)/shard_map/ppermute | solution.py:54
  44.6 0.5 shard_map.91.refs_0_
  45.0 2.3 %collective-permute-start.22 = (f32[112,256]{1,0:T(8,128)S(1)}, f32[112,256]{1,0:T(8,128)S(1)}, u32[]{:S(2)}, u32[]{:S(2)}) collective-permute-start(f32[112,256]{1,0:T(8,128)S(1)} %shard_map.91.refs_0_), channel_id=1, source_target_pairs={{24,0},{28,4},{16,8},{20,12},{8,16},{12,20},{0,24},{4,28},{25,1},{... | collective-permute-start | bytes 344072 | tf_op jit(solution)/shard_map/ppermute | solution.py:54
  47.4 0.5 collective-permute-start.21
  47.9 0.7 %collective-permute-start.20 = (f32[112,256]{1,0:T(8,128)S(1)}, f32[112,256]{1,0:T(8,128)S(1)}, u32[]{:S(2)}, u32[]{:S(2)}) collective-permute-start(f32[112,256]{1,0:T(8,128)S(1)} %shard_map.91.refs_0_), channel_id=1, source_target_pairs={{8,0},{12,4},{0,8},{4,12},{24,16},{28,20},{16,24},{20,28},{9,1},{1... | collective-permute-start | bytes 344072 | tf_op jit(solution)/shard_map/ppermute | solution.py:54
  48.6 3.3 %collective-permute-done.22.refs_3_ = f32[112,256]{1,0:T(8,128)S(1)} collective-permute-done((f32[112,256]{1,0:T(8,128)S(1)}, f32[112,256]{1,0:T(8,128)S(1)}, u32[]{:S(2)}, u32[]{:S(2)}) %collective-permute-start.22) | collective-permute-done | bytes 114720 | tf_op jit(solution)/shard_map/ppermute | solution.py:54
  51.9 1.0 %collective-permute-done.21.refs_2_ = f32[112,256]{1,0:T(8,128)S(1)} collective-permute-done((f32[112,256]{1,0:T(8,128)S(1)}, f32[112,256]{1,0:T(8,128)S(1)}, u32[]{:S(2)}, u32[]{:S(2)}) %collective-permute-start.21) | collective-permute-done | bytes 114720 | tf_op jit(solution)/shard_map/ppermute | solution.py:54
  52.8 0.3 collective-permute-done.20.refs_1_
  53.2 0.7 %shard_map.93.refs_2_ = f32[3,64,1024]{2,1,0:T(8,128)S(1)} custom-call(f32[4,112,256]{2,1,0:T(8,128)S(1)} %shard_map.92.refs_0_.refs_1_, bf16[8,2048,256]{2,1,0:T(8,128)(2,1)S(1)} %get-tuple-element.24.refs_1_.refs_3_.refs_2_), custom_call_target="tpu_custom_call" | custom-call | flops 536870912 | tf_op jit(solution)/shard_map/pallas_call | solution.py:71
  54.0 1.0 %collective-permute-done.23.refs_0_ = f32[4,112,256]{2,1,0:T(8,128)S(1)} collective-permute-done((f32[4,112,256]{2,1,0:T(8,128)S(1)}, f32[4,112,256]{2,1,0:T(8,128)S(1)}, u32[]{:S(2)}, u32[]{:S(2)}) %collective-permute-start.23) | collective-permute-done | bytes 458784 | tf_op jit(solution)/shard_map/ppermute | solution.py:54
  55.0 0.8 %shard_map.94 = (f32[88,256]{1,0:T(8,128)S(1)}, f32[88,256]{1,0:T(8,128)S(1)}, f32[88,256]{1,0:T(8,128)S(1)}, f32[88,256]{1,0:T(8,128)S(1)}) custom-call(f32[4,112,256]{2,1,0:T(8,128)S(1)} %collective-permute-done.23.refs_0_, f32[4,112,256]{2,1,0:T(8,128)S(1)} %shard_map.92.refs_0_.refs_1_, f32[3,64,1024]{2,1,0:T(8,128)S(1)} %shard_map.93.refs_2_, ...), custom_call_target="tpu_custom_call" | custom-call | flops 536870912 | tf_op jit(solution)/shard_map/pallas_call | solution.py:71
  55.8 1.8 %collective-permute-start.24 = (f32[88,256]{1,0:T(8,128)S(1)}, f32[88,256]{1,0:T(8,128)S(1)}, u32[]{:S(2)}, u32[]{:S(2)}) collective-permute-start(f32[88,256]{1,0:T(8,128)S(1)} %get-tuple-element.41), channel_id=1, source_target_pairs={{0,3},{1,2},{2,1},{3,0},{4,7},{5,6},{6,5},{7,4},{8,11},{9,10},{10,... | collective-permute-start | bytes 270344 | tf_op jit(solution)/shard_map/ppermute | solution.py:60
  57.6 2.7 %collective-permute-start.26 = (f32[88,256]{1,0:T(8,128)S(1)}, f32[88,256]{1,0:T(8,128)S(1)}, u32[]{:S(2)}, u32[]{:S(2)}) collective-permute-start(f32[88,256]{1,0:T(8,128)S(1)} %get-tuple-element.43), channel_id=1, source_target_pairs={{0,1},{1,0},{2,3},{3,2},{4,5},{5,4},{6,7},{7,6},{8,9},{9,8},{10,11... | collective-permute-start | bytes 270344 | tf_op jit(solution)/shard_map/ppermute | solution.py:60
  60.3 3.0 %collective-permute-done.24 = f32[88,256]{1,0:T(8,128)S(1)} collective-permute-done((f32[88,256]{1,0:T(8,128)S(1)}, f32[88,256]{1,0:T(8,128)S(1)}, u32[]{:S(2)}, u32[]{:S(2)}) %collective-permute-start.24) | collective-permute-done | bytes 90144 | tf_op jit(solution)/shard_map/ppermute | solution.py:60
  63.3 3.0 %collective-permute-done.25 = f32[88,256]{1,0:T(8,128)S(1)} collective-permute-done((f32[88,256]{1,0:T(8,128)S(1)}, f32[88,256]{1,0:T(8,128)S(1)}, u32[]{:S(2)}, u32[]{:S(2)}) %collective-permute-start.25) | collective-permute-done | bytes 90144 | tf_op jit(solution)/shard_map/ppermute | solution.py:60
  66.2 0.1 collective-permute-start.27
  66.3 0.7 fusion
  67.0 0.5 collective-permute-done.27.refs_1_
  67.5 1.4 %shard_map.95 = f32[3,64,64]{2,1,0:T(8,128)} custom-call(f32[24,256]{1,0:T(8,128)S(1)} %slice_add_fusion.3.refs_0_, f32[24,256]{1,0:T(8,128)S(1)} %collective-permute-done.27.refs_1_), custom_call_target="tpu_custom_call" | custom-call | tf_op jit(solution)/shard_map/pallas_call | solution.py:71
  (29 shorter events, 0.4 us)
Async XLA Ops:
  0.6 11.8 %collective-permute-start = (f32[64,256]{1,0:T(8,128)}, f32[64,256]{1,0:T(8,128)S(1)}, u32[]{:S(2)}, u32[]{:S(2)}) collective-permute-start(f32[64,256]{1,0:T(8,128)} %refs_4_.1), channel_id=1, source_target_pairs={{2,0},{3,1},{0,2},{1,3},{6,4},{7,5},{4,6},{5,7},{10,8},{11,9},{8,1... | collective-permute-start | bytes 196616 | tf_op jit(solution)/shard_map/ppermute | solution.py:54
  4.7 7.7 %collective-permute-start.2 = (f32[64,256]{1,0:T(8,128)}, f32[64,256]{1,0:T(8,128)S(1)}, u32[]{:S(2)}, u32[]{:S(2)}) collective-permute-start(f32[64,256]{1,0:T(8,128)} %refs_5_.1), channel_id=1, source_target_pairs={{8,0},{12,4},{0,8},{4,12},{24,16},{28,20},{16,24},{20,28},{9,1},{1... | collective-permute-start | bytes 196616 | tf_op jit(solution)/shard_map/ppermute | solution.py:54
  6.2 6.2 %collective-permute-start.4 = (f32[64,256]{1,0:T(8,128)}, f32[64,256]{1,0:T(8,128)S(1)}, u32[]{:S(2)}, u32[]{:S(2)}) collective-permute-start(f32[64,256]{1,0:T(8,128)} %refs_5_.1), channel_id=1, source_target_pairs={{24,0},{28,4},{16,8},{20,12},{8,16},{12,20},{0,24},{4,28},{25,1},{... | collective-permute-start | bytes 196616 | tf_op jit(solution)/shard_map/ppermute | solution.py:54
  7.7 4.7 %collective-permute-start.3 = (f32[64,256]{1,0:T(8,128)}, f32[64,256]{1,0:T(8,128)S(1)}, u32[]{:S(2)}, u32[]{:S(2)}) collective-permute-start(f32[64,256]{1,0:T(8,128)} %refs_5_.1), channel_id=1, source_target_pairs={{16,0},{20,4},{24,8},{28,12},{0,16},{4,20},{8,24},{12,28},{17,1},{... | collective-permute-start | bytes 196616 | tf_op jit(solution)/shard_map/ppermute | solution.py:54
  12.5 2.5 %collective-permute-start.5 = (f32[4,64,256]{2,1,0:T(8,128)S(1)}, f32[4,64,256]{2,1,0:T(8,128)S(1)}, u32[]{:S(2)}, u32[]{:S(2)}) collective-permute-start(f32[4,64,256]{2,1,0:T(8,128)S(1)} %shard_map.79.refs_0_.refs_1_), channel_id=1, source_target_pairs={{4,0},{0,4},{12,8},{8,12},{20,16},{16,20},{28,24},{24,28},{5,1},{1... | collective-permute-start | bytes 786440 | tf_op jit(solution)/shard_map/ppermute | solution.py:54
  12.6 7.7 %collective-permute-start.1 = (f32[2,64,256]{2,1,0:T(8,128)S(1)}, f32[2,64,256]{2,1,0:T(8,128)S(1)}, u32[]{:S(2)}, u32[]{:S(2)}) collective-permute-start(f32[2,64,256]{2,1,0:T(8,128)S(1)} %shard_map.78.refs_4_.refs_0_), channel_id=1, source_target_pairs={{1,0},{0,1},{3,2},{2,3},{5,4},{4,5},{7,6},{6,7},{9,8},{8,9},{11,10... | collective-permute-start | bytes 393224 | tf_op jit(solution)/shard_map/ppermute | solution.py:54
  15.8 6.9 %collective-permute-start.7 = (f32[64,256]{1,0:T(8,128)S(1)}, f32[64,256]{1,0:T(8,128)S(1)}, u32[]{:S(2)}, u32[]{:S(2)}) collective-permute-start(f32[64,256]{1,0:T(8,128)S(1)} %get-tuple-element.30), channel_id=1, source_target_pairs={{0,3},{1,2},{2,1},{3,0},{4,7},{5,6},{6,5},{7,4},{8,11},{9,10},{10,... | collective-permute-start | bytes 196616 | tf_op jit(solution)/shard_map/ppermute | solution.py:60
  16.3 8.1 %collective-permute-start.8 = (f32[64,256]{1,0:T(8,128)S(1)}, f32[64,256]{1,0:T(8,128)S(1)}, u32[]{:S(2)}, u32[]{:S(2)}) collective-permute-start(f32[64,256]{1,0:T(8,128)S(1)} %get-tuple-element.31), channel_id=1, source_target_pairs={{0,2},{1,3},{2,0},{3,1},{4,6},{5,7},{6,4},{7,5},{8,10},{9,11},{10,... | collective-permute-start | bytes 196616 | tf_op jit(solution)/shard_map/ppermute | solution.py:60
  18.0 6.5 %collective-permute-start.9 = (f32[64,256]{1,0:T(8,128)S(1)}, f32[64,256]{1,0:T(8,128)S(1)}, u32[]{:S(2)}, u32[]{:S(2)}) collective-permute-start(f32[64,256]{1,0:T(8,128)S(1)} %get-tuple-element.32), channel_id=1, source_target_pairs={{0,1},{1,0},{2,3},{3,2},{4,5},{5,4},{6,7},{7,6},{8,9},{9,8},{10,11... | collective-permute-start | bytes 196616 | tf_op jit(solution)/shard_map/ppermute | solution.py:60
  24.4 5.3 %collective-permute-start.12 = (f32[64,256]{1,0:T(8,128)S(1)}, f32[64,256]{1,0:T(8,128)S(1)}, u32[]{:S(2)}, u32[]{:S(2)}) collective-permute-start(f32[64,256]{1,0:T(8,128)S(1)} %shard_map.83.refs_0_.refs_9_), channel_id=1, source_target_pairs={{24,0},{28,4},{16,8},{20,12},{8,16},{12,20},{0,24},{4,28},{25,1},{... | collective-permute-start | bytes 196616 | tf_op jit(solution)/shard_map/ppermute | solution.py:54
  27.0 4.3 %collective-permute-start.11 = (f32[64,256]{1,0:T(8,128)S(1)}, f32[64,256]{1,0:T(8,128)S(1)}, u32[]{:S(2)}, u32[]{:S(2)}) collective-permute-start(f32[64,256]{1,0:T(8,128)S(1)} %shard_map.83.refs_0_.refs_9_), channel_id=1, source_target_pairs={{16,0},{20,4},{24,8},{28,12},{0,16},{4,20},{8,24},{12,28},{17,1},{... | collective-permute-start | bytes 196616 | tf_op jit(solution)/shard_map/ppermute | solution.py:54
  27.5 4.3 %collective-permute-start.10 = (f32[64,256]{1,0:T(8,128)S(1)}, f32[64,256]{1,0:T(8,128)S(1)}, u32[]{:S(2)}, u32[]{:S(2)}) collective-permute-start(f32[64,256]{1,0:T(8,128)S(1)} %shard_map.83.refs_0_.refs_9_), channel_id=1, source_target_pairs={{8,0},{12,4},{0,8},{4,12},{24,16},{28,20},{16,24},{20,28},{9,1},{1... | collective-permute-start | bytes 196616 | tf_op jit(solution)/shard_map/ppermute | solution.py:54
  28.0 3.8 %collective-permute-start.6 = (f32[4,64,256]{2,1,0:T(8,128)S(1)}, f32[4,64,256]{2,1,0:T(8,128)S(1)}, u32[]{:S(2)}, u32[]{:S(2)}) collective-permute-start(f32[4,64,256]{2,1,0:T(8,128)S(1)} %get-tuple-element.29.refs_4_), channel_id=1, source_target_pairs={{4,0},{0,4},{12,8},{8,12},{20,16},{16,20},{28,24},{24,28},{5,1},{1... | collective-permute-start | bytes 786440 | tf_op jit(solution)/shard_map/ppermute | solution.py:54
  31.7 2.4 %collective-permute-start.13 = (f32[4,64,256]{2,1,0:T(8,128)S(1)}, f32[4,64,256]{2,1,0:T(8,128)S(1)}, u32[]{:S(2)}, u32[]{:S(2)}) collective-permute-start(f32[4,64,256]{2,1,0:T(8,128)S(1)} %shard_map.84.refs_0_.refs_1_), channel_id=1, source_target_pairs={{4,0},{0,4},{12,8},{8,12},{20,16},{16,20},{28,24},{24,28},{5,1},{1... | collective-permute-start | bytes 786440 | tf_op jit(solution)/shard_map/ppermute | solution.py:54
  31.9 8.4 %collective-permute-start.14 = (f32[64,256]{1,0:T(8,128)S(1)}, f32[64,256]{1,0:T(8,128)S(1)}, u32[]{:S(2)}, u32[]{:S(2)}) collective-permute-start(f32[64,256]{1,0:T(8,128)S(1)} %shard_map.88), channel_id=1, source_target_pairs={{24,0},{28,4},{16,8},{20,12},{8,16},{12,20},{0,24},{4,28},{25,1},{... | collective-permute-start | bytes 196616 | tf_op jit(solution)/shard_map/ppermute | solution.py:54
  35.0 6.9 %collective-permute-start.17 = (f32[64,256]{1,0:T(8,128)S(1)}, f32[64,256]{1,0:T(8,128)S(1)}, u32[]{:S(2)}, u32[]{:S(2)}) collective-permute-start(f32[64,256]{1,0:T(8,128)S(1)} %get-tuple-element.37), channel_id=1, source_target_pairs={{0,3},{1,2},{2,1},{3,0},{4,7},{5,6},{6,5},{7,4},{8,11},{9,10},{10,... | collective-permute-start | bytes 196616 | tf_op jit(solution)/shard_map/ppermute | solution.py:60
  36.7 7.1 %collective-permute-start.18 = (f32[64,256]{1,0:T(8,128)S(1)}, f32[64,256]{1,0:T(8,128)S(1)}, u32[]{:S(2)}, u32[]{:S(2)}) collective-permute-start(f32[64,256]{1,0:T(8,128)S(1)} %get-tuple-element.38), channel_id=1, source_target_pairs={{0,2},{1,3},{2,0},{3,1},{4,6},{5,7},{6,4},{7,5},{8,10},{9,11},{10,... | collective-permute-start | bytes 196616 | tf_op jit(solution)/shard_map/ppermute | solution.py:60
  36.7 7.1 %collective-permute-start.19 = (f32[64,256]{1,0:T(8,128)S(1)}, f32[64,256]{1,0:T(8,128)S(1)}, u32[]{:S(2)}, u32[]{:S(2)}) collective-permute-start(f32[64,256]{1,0:T(8,128)S(1)} %get-tuple-element.39), channel_id=1, source_target_pairs={{0,1},{1,0},{2,3},{3,2},{4,5},{5,4},{6,7},{7,6},{8,9},{9,8},{10,11... | collective-permute-start | bytes 196616 | tf_op jit(solution)/shard_map/ppermute | solution.py:60
  39.5 4.4 %collective-permute-start.15 = (f32[64,256]{1,0:T(8,128)S(1)}, f32[64,256]{1,0:T(8,128)S(1)}, u32[]{:S(2)}, u32[]{:S(2)}) collective-permute-start(f32[64,256]{1,0:T(8,128)S(1)} %shard_map.89), channel_id=1, source_target_pairs={{16,0},{20,4},{24,8},{28,12},{0,16},{4,20},{8,24},{12,28},{17,1},{... | collective-permute-start | bytes 196616 | tf_op jit(solution)/shard_map/ppermute | solution.py:54
  40.2 4.3 %collective-permute-start.16 = (f32[64,256]{1,0:T(8,128)S(1)}, f32[64,256]{1,0:T(8,128)S(1)}, u32[]{:S(2)}, u32[]{:S(2)}) collective-permute-start(f32[64,256]{1,0:T(8,128)S(1)} %shard_map.90), channel_id=1, source_target_pairs={{8,0},{12,4},{0,8},{4,12},{24,16},{28,20},{16,24},{20,28},{9,1},{1... | collective-permute-start | bytes 196616 | tf_op jit(solution)/shard_map/ppermute | solution.py:54
  45.0 6.8 %collective-permute-start.22 = (f32[112,256]{1,0:T(8,128)S(1)}, f32[112,256]{1,0:T(8,128)S(1)}, u32[]{:S(2)}, u32[]{:S(2)}) collective-permute-start(f32[112,256]{1,0:T(8,128)S(1)} %shard_map.91.refs_0_), channel_id=1, source_target_pairs={{24,0},{28,4},{16,8},{20,12},{8,16},{12,20},{0,24},{4,28},{25,1},{... | collective-permute-start | bytes 344072 | tf_op jit(solution)/shard_map/ppermute | solution.py:54
  47.4 5.5 %collective-permute-start.21 = (f32[112,256]{1,0:T(8,128)S(1)}, f32[112,256]{1,0:T(8,128)S(1)}, u32[]{:S(2)}, u32[]{:S(2)}) collective-permute-start(f32[112,256]{1,0:T(8,128)S(1)} %shard_map.91.refs_0_), channel_id=1, source_target_pairs={{16,0},{20,4},{24,8},{28,12},{0,16},{4,20},{8,24},{12,28},{17,1},{... | collective-permute-start | bytes 344072 | tf_op jit(solution)/shard_map/ppermute | solution.py:54
  47.9 5.2 %collective-permute-start.20 = (f32[112,256]{1,0:T(8,128)S(1)}, f32[112,256]{1,0:T(8,128)S(1)}, u32[]{:S(2)}, u32[]{:S(2)}) collective-permute-start(f32[112,256]{1,0:T(8,128)S(1)} %shard_map.91.refs_0_), channel_id=1, source_target_pairs={{8,0},{12,4},{0,8},{4,12},{24,16},{28,20},{16,24},{20,28},{9,1},{1... | collective-permute-start | bytes 344072 | tf_op jit(solution)/shard_map/ppermute | solution.py:54
  53.1 1.9 %collective-permute-start.23 = (f32[4,112,256]{2,1,0:T(8,128)S(1)}, f32[4,112,256]{2,1,0:T(8,128)S(1)}, u32[]{:S(2)}, u32[]{:S(2)}) collective-permute-start(f32[4,112,256]{2,1,0:T(8,128)S(1)} %shard_map.92.refs_0_.refs_1_), channel_id=1, source_target_pairs={{4,0},{0,4},{12,8},{8,12},{20,16},{16,20},{28,24},{24,28},{5,1},{1... | collective-permute-start | bytes 1376264 | tf_op jit(solution)/shard_map/ppermute | solution.py:54
  55.8 7.4 %collective-permute-start.24 = (f32[88,256]{1,0:T(8,128)S(1)}, f32[88,256]{1,0:T(8,128)S(1)}, u32[]{:S(2)}, u32[]{:S(2)}) collective-permute-start(f32[88,256]{1,0:T(8,128)S(1)} %get-tuple-element.41), channel_id=1, source_target_pairs={{0,3},{1,2},{2,1},{3,0},{4,7},{5,6},{6,5},{7,4},{8,11},{9,10},{10,... | collective-permute-start | bytes 270344 | tf_op jit(solution)/shard_map/ppermute | solution.py:60
  57.6 8.6 %collective-permute-start.25 = (f32[88,256]{1,0:T(8,128)S(1)}, f32[88,256]{1,0:T(8,128)S(1)}, u32[]{:S(2)}, u32[]{:S(2)}) collective-permute-start(f32[88,256]{1,0:T(8,128)S(1)} %get-tuple-element.42), channel_id=1, source_target_pairs={{0,2},{1,3},{2,0},{3,1},{4,6},{5,7},{6,4},{7,5},{8,10},{9,11},{10,... | collective-permute-start | bytes 270344 | tf_op jit(solution)/shard_map/ppermute | solution.py:60
  57.6 8.6 %collective-permute-start.26 = (f32[88,256]{1,0:T(8,128)S(1)}, f32[88,256]{1,0:T(8,128)S(1)}, u32[]{:S(2)}, u32[]{:S(2)}) collective-permute-start(f32[88,256]{1,0:T(8,128)S(1)} %get-tuple-element.43), channel_id=1, source_target_pairs={{0,1},{1,0},{2,3},{3,2},{4,5},{5,4},{6,7},{7,6},{8,9},{9,8},{10,11... | collective-permute-start | bytes 270344 | tf_op jit(solution)/shard_map/ppermute | solution.py:60
  66.2 1.3 %collective-permute-start.27 = (f32[24,256]{1,0:T(8,128)S(1)}, f32[24,256]{1,0:T(8,128)S(1)}, u32[]{:S(2)}, u32[]{:S(2)}) collective-permute-start(f32[24,256]{1,0:T(8,128)S(1)} %slice_add_fusion.3.refs_0_), channel_id=1, source_target_pairs={{4,0},{0,4},{12,8},{8,12},{20,16},{16,20},{28,24},{24,28},{5,1},{1... | collective-permute-start | bytes 73736 | tf_op jit(solution)/shard_map/ppermute | solution.py:54

commit v9 on v8

--- a/solution.py
+++ b/solution.py
@@ -310,8 +310,7 @@
     )
 
 
-def left_kernel(n_row, x_evens, x_odds, dense_ref, *refs):
-    evens, odds_ref = refs[:-1], refs[-1]
+def left_kernel(n_row, x_evens, x_odds, dense_ref, evens_ref, odds_ref):
     row_blocks, _, width = dense_ref.shape
     tile_len = width // 2
     _, span, piece_len = x_evens.shape
@@ -334,22 +333,21 @@
                 high_part = low_part = 0.0
         piece = combine(by_high[:span], by_low[:span] + by_high[span:], by_low[span:])
         if place < n_row // 2:
-            evens[place][...] = piece
+            evens_ref[place] = piece
         else:
             odds_ref[place - n_row // 2] = piece
 
 
 def dense_left(x_pairs, n_row, dense, before):
     _, span, piece_len = x_pairs[0].shape
-    results = call(
+    return call(
         functools.partial(left_kernel, n_row),
         [*x_pairs, dense],
-        [held(span, piece_len)] * (n_row // 2) + [held(n_row // 2, span, piece_len)],
+        [held(n_row // 2, span, piece_len)] * 2,
         before,
         limit=VMEM_LIMIT,
         flops=4 * span * dense.size,
     )
-    return list(results[:-1]), results[-1]
 
 
 def sparse_tiles(tiles, sizes):
@@ -408,14 +406,15 @@
     blocks = n_row * piece_len // a_digits.shape[-1]
     product = sparse_product(values, "nti,tdik->tdnk", rows, cols, count, blocks, a_digits)
     pieces = [product[:, d * piece_len : (d + 1) * piece_len] for d in range(n_row)]
-    return pieces[: n_row // 2], jnp.stack(pieces[n_row // 2 :])
-
-
-def add_came(evens, odds_came, index, before=()):
-    def kernel(even_ref, came_ref, out_ref):
-        out_ref[...] = even_ref[...] + came_ref[index]
-
-    return call(kernel, [evens[index], odds_came], [held(*evens[index].shape)], before)[0]
+    return jnp.stack(pieces[: n_row // 2]), jnp.stack(pieces[n_row // 2 :])
+
+
+def add_and_part(kept, came, before=()):
+    def kernel(kept_ref, came_ref, evens_ref, odds_ref):
+        for index in range(kept.shape[0]):
+            (odds_ref if index % 2 else evens_ref)[index // 2] = kept_ref[index] + came_ref[index]
+
+    return call(kernel, [kept, came], [held(kept.shape[0] // 2, *kept.shape[1:])] * 2, before)
 
 
 def append_projections(w_parts, pieces, earlier):
@@ -423,9 +422,9 @@
     rows = span * span // piece_len
 
     def kernel(*refs):
-        w_refs, refs = refs[: len(w_parts)], refs[len(w_parts) :]
         piece_refs, refs = refs[: len(pieces)], refs[len(pieces) :]
-        earlier_refs, out_ref = refs[:-1], refs[-1]
+        earlier_refs, refs = refs[: len(earlier)], refs[len(earlier) :]
+        w_refs, out_ref = refs[:-1], refs[-1]
         summed = functools.reduce(jnp.add, [ref[...] for ref in piece_refs])
         out_ref[:span, :] = summed
         w_piece = functools.reduce(jnp.add, [ref[...] for ref in w_refs])
@@ -441,7 +440,7 @@
             out_ref[start : start + rows, :] = pack_square(square, piece_len)
 
     outs = [held(span + (len(earlier) + 1) * rows, piece_len)]
-    return call(kernel, [*w_parts, *pieces, *earlier], outs)[0]
+    return call(kernel, [*pieces, *earlier, *w_parts], outs)[0]
 
 
 def multiply_mod(left, right):
@@ -505,8 +504,9 @@
     def multiply(evens, before):
         return multiply_odds(gather_odds(evens, "row"), evens, multiply_evens(evens), before)
 
+    y_came = fetch_evens(block_y, "row")
     x_came = fetch_evens(block_x, "col")
-    evens = stack_after([y_own] + fetch_evens(block_y, "row"), [*before, *x_came])
+    evens = stack_after([y_own] + y_came, [*before, *x_came])
     x_evens = stack_after([x_own] + x_came)
     outs = multiply(evens, [x_evens])
     x_pairs = [x_evens, gather_odds(x_evens, "col")]
@@ -518,15 +518,12 @@
     w_came = fetch(w_odds, "row", 1)
     outs = multiply(gather_evens(vector_1, "row"), [w_came])
     pieces = scatter_pieces(outs, "col")
-    w_last = n_row // 2 - 1
-    w_parts = [
-        add_came(w_evens, w_came, index, [] if index == w_last else [outs[0]])
-        for index in range(n_row // 2)
-    ]
-    w_parts = w_parts[:1] + [
-        fetch(w_parts[index], "row", 2 * index) for index in reversed(range(1, n_row // 2))
-    ]
-    vector_2 = append_projections(w_parts, pieces, [y_own, vector_1])
+    w_kept, shift, before = w_evens, 2, []
+    while shift < n_row:
+        w_kept, w_sent = add_and_part(w_kept, w_came, before)
+        w_came = fetch(w_sent, "row", shift)
+        shift, before = 2 * shift, [outs[0]]
+    vector_2 = append_projections([w_kept[0], w_came[0]], pieces, [y_own, vector_1])
     outs = multiply(gather_evens(vector_2, "row"), [])
     pieces = scatter_pieces(outs, "col")
     terms = functools.reduce(jnp.add, [piece[span:] for piece in pieces])

time: 69.1 us -> 68 us (0.984)
  starting transfers between devices: 33.7 us -> 32.2 us
    ppermute x19 -> x18, starting transfers between devices: 20.3 us -> 18.9 us  [fetch(): lax.ppermute(piece, axis, [(partner(i, shift, size), i) for i in range(si...]
    ppermute x19 -> x18, waiting for transfers between devices: 10.5 us -> 10.4 us  [fetch(): lax.ppermute(piece, axis, [(partner(i, shift, size), i) for i in range(si...]
    pallas_call x18 -> x16, Pallas kernels: 9.09 us -> 9.1 us  [call(): pl.pallas_call(body, in_specs=[vmem] * len(operands) + [pl.BlockSpec(memo...]
  transfers between devices with their start and end apart: 28 -> 27, of which waited for: 14 -> 14; matrix products, arithmetic and copies ran while one was open for 1% -> 1% of each run, Pallas kernels for 14% -> 14%
where the time goes in v9:
time: 68 us; the launch traced here: 67.8 us
  starting transfers between devices  32.2 us (47%)
  waiting for transfers between devices  20.8 us (31%)
  Pallas kernels  12.6 us (19%)
  between operations  1.49 us (2%)
  other arithmetic  0.68 us (1%)
    ppermute x18, starting transfers between devices, fetch(): lax.ppermute(piece, axis, [(partner(i, shift, size), i) for i in range(si...  18.9 us
    ppermute x9, starting transfers between devices, scatter_pieces(): lax.ppermute(pieces[shift], axis, [(i, partner(i, shift, size)) for i in...  13.4 us
    ppermute x18, waiting for transfers between devices, fetch(): lax.ppermute(piece, axis, [(partner(i, shift, size), i) for i in range(si...  10.4 us
    ppermute x9, waiting for transfers between devices, scatter_pieces(): lax.ppermute(pieces[shift], axis, [(i, partner(i, shift, size)) for i in...  10.4 us
    pallas_call x16, Pallas kernels, call(): pl.pallas_call(body, in_specs=[vmem] * len(operands) + [pl.BlockSpec(memo...  9.1 us
    pallas_call x1, Pallas kernels, build_dense(): pl.pallas_call(functools.partial(build_kernel, (*sizes, group)), in_specs...  3.5 us
  transfers between devices with their start and end apart: 27, of which 14 were waited for; matrix products, arithmetic and copies ran while one was open for 1% of the time, Pallas kernels for 14%

profile of v9, /device:TPU:0, one launch (start us, length us, event | category | flops | bytes accessed | tf_op | source)
XLA Modules:
  0.0 67.8 jit_solution(10754603425683029689)
XLA Ops:
  0.6 4.1 %collective-permute-start.3 = (f32[64,256]{1,0:T(8,128)}, f32[64,256]{1,0:T(8,128)S(1)}, u32[]{:S(2)}, u32[]{:S(2)}) collective-permute-start(f32[64,256]{1,0:T(8,128)} %refs_4_.1), channel_id=1, source_target_pairs={{2,0},{3,1},{0,2},{1,3},{6,4},{7,5},{4,6},{5,7},{10,8},{11,9},{8,1... | collective-permute-start | bytes 196616 | tf_op jit(solution)/shard_map/ppermute | solution.py:54
  4.7 1.5 %collective-permute-start = (f32[64,256]{1,0:T(8,128)}, f32[64,256]{1,0:T(8,128)S(1)}, u32[]{:S(2)}, u32[]{:S(2)}) collective-permute-start(f32[64,256]{1,0:T(8,128)} %refs_5_.1), channel_id=1, source_target_pairs={{8,0},{12,4},{0,8},{4,12},{24,16},{28,20},{16,24},{20,28},{9,1},{1... | collective-permute-start | bytes 196616 | tf_op jit(solution)/shard_map/ppermute | solution.py:54
  6.2 1.5 %collective-permute-start.2 = (f32[64,256]{1,0:T(8,128)}, f32[64,256]{1,0:T(8,128)S(1)}, u32[]{:S(2)}, u32[]{:S(2)}) collective-permute-start(f32[64,256]{1,0:T(8,128)} %refs_5_.1), channel_id=1, source_target_pairs={{24,0},{28,4},{16,8},{20,12},{8,16},{12,20},{0,24},{4,28},{25,1},{... | collective-permute-start | bytes 196616 | tf_op jit(solution)/shard_map/ppermute | solution.py:54
  7.7 0.5 collective-permute-start.1
  8.9 3.5 %shard_map.77 = (bf16[8,2048,256]{2,1,0:T(8,128)(2,1)S(1)}, f32[64,256]{1,0:T(8,128)S(1)}, f32[64,256]{1,0:T(8,128)S(1)}, f32[8,128]{1,0:T(8,128)S(1)}) custom-call(s32[1,1,64]{2,1,0:T(1,128)} %refs_0_.1, s32[1,1,64]{2,1,0:T(1,128)} %refs_1_.1, s32[1,1]{1,0:T(1,128)S(6)} %copy.8.refs_2_, f32[1,1,64,128,128]{4,3,2,1,0:T(8,128)} %refs_3_.1, ...), custom_call_target="tpu_custom_call" | custom-call | flops 8388608 | bytes 8388608 | tf_op jit(solution)/shard_map/pallas_call | solution.py:201
  12.5 0.1 collective-permute-start.4
  12.6 1.6 %collective-permute-start.8 = (f32[2,64,256]{2,1,0:T(8,128)S(1)}, f32[2,64,256]{2,1,0:T(8,128)S(1)}, u32[]{:S(2)}, u32[]{:S(2)}) collective-permute-start(f32[2,64,256]{2,1,0:T(8,128)S(1)} %shard_map.80.refs_4_.refs_0_), channel_id=1, source_target_pairs={{1,0},{0,1},{3,2},{2,3},{5,4},{4,5},{7,6},{6,7},{9,8},{8,9},{11,10... | collective-permute-start | bytes 393224 | tf_op jit(solution)/shard_map/ppermute | solution.py:54
  14.2 0.7 %shard_map.79.refs_2_ = f32[3,64,1024]{2,1,0:T(8,128)S(1)} custom-call(f32[4,64,256]{2,1,0:T(8,128)S(1)} %shard_map.78.refs_0_.refs_1_, bf16[8,2048,256]{2,1,0:T(8,128)(2,1)S(1)} %get-tuple-element.26.refs_1_.refs_3_.refs_2_), custom_call_target="tpu_custom_call" | custom-call | flops 536870912 | tf_op jit(solution)/shard_map/pallas_call | solution.py:71
  15.0 0.8 %shard_map.81 = (f32[64,256]{1,0:T(8,128)S(1)}, f32[64,256]{1,0:T(8,128)S(1)}, f32[64,256]{1,0:T(8,128)S(1)}, f32[64,256]{1,0:T(8,128)S(1)}) custom-call(f32[4,64,256]{2,1,0:T(8,128)S(1)} %collective-permute-done.4.refs_0_, f32[4,64,256]{2,1,0:T(8,128)S(1)} %shard_map.78.refs_0_.refs_1_, f32[3,64,1024]{2,1,0:T(8,128)S(1)} %shard_map.79.refs_2_, ...), custom_call_target="tpu_custom_call" | custom-call | flops 536870912 | tf_op jit(solution)/shard_map/pallas_call | solution.py:71
  15.8 0.5 collective-permute-start.5
  16.3 1.7 %collective-permute-start.6 = (f32[64,256]{1,0:T(8,128)S(1)}, f32[64,256]{1,0:T(8,128)S(1)}, u32[]{:S(2)}, u32[]{:S(2)}) collective-permute-start(f32[64,256]{1,0:T(8,128)S(1)} %get-tuple-element.30), channel_id=1, source_target_pairs={{0,2},{1,3},{2,0},{3,1},{4,6},{5,7},{6,4},{7,5},{8,10},{9,11},{10,... | collective-permute-start | bytes 196616 | tf_op jit(solution)/shard_map/ppermute | solution.py:60
  18.0 2.3 %collective-permute-start.7 = (f32[64,256]{1,0:T(8,128)S(1)}, f32[64,256]{1,0:T(8,128)S(1)}, u32[]{:S(2)}, u32[]{:S(2)}) collective-permute-start(f32[64,256]{1,0:T(8,128)S(1)} %get-tuple-element.31), channel_id=1, source_target_pairs={{0,1},{1,0},{2,3},{3,2},{4,5},{5,4},{6,7},{7,6},{8,9},{9,8},{10,11... | collective-permute-start | bytes 196616 | tf_op jit(solution)/shard_map/ppermute | solution.py:60
  20.2 2.4 %shard_map.82 = (f32[4,64,256]{2,1,0:T(8,128)S(1)}, f32[4,64,256]{2,1,0:T(8,128)S(1)}) custom-call(f32[2,64,256]{2,1,0:T(8,128)S(1)} %shard_map.80.refs_4_.refs_0_, f32[2,64,256]{2,1,0:T(8,128)S(1)} %collective-permute-done.8.refs_1_, bf16[8,2048,256]{2,1,0:T(8,128)(2,1)S(1)} %get-tuple-element.26.refs_1_.refs_3_.refs_2_, ...), custom_call_target="tpu_custom_call" | custom-call | flops 1073741824 | tf_op jit(solution)/shard_map/pallas_call | solution.py:71
  22.6 0.1 collective-permute-start.13
  22.7 1.7 %collective-permute-done.6.refs_2_ = f32[64,256]{1,0:T(8,128)S(1)} collective-permute-done((f32[64,256]{1,0:T(8,128)S(1)}, f32[64,256]{1,0:T(8,128)S(1)}, u32[]{:S(2)}, u32[]{:S(2)}) %collective-permute-start.6) | collective-permute-done | bytes 65568 | tf_op jit(solution)/shard_map/ppermute | solution.py:60
  24.4 2.5 %collective-permute-start.11 = (f32[64,256]{1,0:T(8,128)S(1)}, f32[64,256]{1,0:T(8,128)S(1)}, u32[]{:S(2)}, u32[]{:S(2)}) collective-permute-start(f32[64,256]{1,0:T(8,128)S(1)} %shard_map.83.refs_0_.refs_5_), channel_id=1, source_target_pairs={{24,0},{28,4},{16,8},{20,12},{8,16},{12,20},{0,24},{4,28},{25,1},{... | collective-permute-start | bytes 196616 | tf_op jit(solution)/shard_map/ppermute | solution.py:54
  27.0 0.5 collective-permute-start.10
  27.5 0.5 collective-permute-start.9
  28.0 1.8 %collective-permute-done.11.refs_3_ = f32[64,256]{1,0:T(8,128)S(1)} collective-permute-done((f32[64,256]{1,0:T(8,128)S(1)}, f32[64,256]{1,0:T(8,128)S(1)}, u32[]{:S(2)}, u32[]{:S(2)}) %collective-permute-start.11) | collective-permute-done | bytes 65568 | tf_op jit(solution)/shard_map/ppermute | solution.py:54
  29.8 1.4 %collective-permute-done.10.refs_2_ = f32[64,256]{1,0:T(8,128)S(1)} collective-permute-done((f32[64,256]{1,0:T(8,128)S(1)}, f32[64,256]{1,0:T(8,128)S(1)}, u32[]{:S(2)}, u32[]{:S(2)}) %collective-permute-start.10) | collective-permute-done | bytes 65568 | tf_op jit(solution)/shard_map/ppermute | solution.py:54
  31.2 0.5 collective-permute-done.9.refs_1_
  31.7 0.1 collective-permute-start.12
  31.9 0.6 collective-permute-start.17
  32.5 0.8 %shard_map.85.refs_2_ = f32[3,64,1024]{2,1,0:T(8,128)S(1)} custom-call(f32[4,64,256]{2,1,0:T(8,128)S(1)} %shard_map.84.refs_0_.refs_1_, bf16[8,2048,256]{2,1,0:T(8,128)(2,1)S(1)} %get-tuple-element.26.refs_1_.refs_3_.refs_2_), custom_call_target="tpu_custom_call" | custom-call | flops 536870912 | tf_op jit(solution)/shard_map/pallas_call | solution.py:71
  33.2 0.1 collective-permute-done.12.refs_0_
  33.3 0.8 %shard_map.86 = (f32[64,256]{1,0:T(8,128)S(1)}, f32[64,256]{1,0:T(8,128)S(1)}, f32[64,256]{1,0:T(8,128)S(1)}, f32[64,256]{1,0:T(8,128)S(1)}) custom-call(f32[4,64,256]{2,1,0:T(8,128)S(1)} %collective-permute-done.12.refs_0_, f32[4,64,256]{2,1,0:T(8,128)S(1)} %shard_map.84.refs_0_.refs_1_, f32[3,64,1024]{2,1,0:T(8,128)S(1)} %shard_map.85.refs_2_, ...), custom_call_target="tpu_custom_call" | custom-call | flops 536870912 | tf_op jit(solution)/shard_map/pallas_call | solution.py:71
  34.2 1.8 %collective-permute-start.14 = (f32[64,256]{1,0:T(8,128)S(1)}, f32[64,256]{1,0:T(8,128)S(1)}, u32[]{:S(2)}, u32[]{:S(2)}) collective-permute-start(f32[64,256]{1,0:T(8,128)S(1)} %get-tuple-element.34), channel_id=1, source_target_pairs={{0,3},{1,2},{2,1},{3,0},{4,7},{5,6},{6,5},{7,4},{8,11},{9,10},{10,... | collective-permute-start | bytes 196616 | tf_op jit(solution)/shard_map/ppermute | solution.py:60
  35.9 2.7 %collective-permute-start.16 = (f32[64,256]{1,0:T(8,128)S(1)}, f32[64,256]{1,0:T(8,128)S(1)}, u32[]{:S(2)}, u32[]{:S(2)}) collective-permute-start(f32[64,256]{1,0:T(8,128)S(1)} %get-tuple-element.36), channel_id=1, source_target_pairs={{0,1},{1,0},{2,3},{3,2},{4,5},{5,4},{6,7},{7,6},{8,9},{9,8},{10,11... | collective-permute-start | bytes 196616 | tf_op jit(solution)/shard_map/ppermute | solution.py:60
  38.6 1.6 %collective-permute-start.18 = (f32[1,64,256]{2,1,0:T(8,128)S(1)}, f32[1,64,256]{2,1,0:T(8,128)S(1)}, u32[]{:S(2)}, u32[]{:S(2)}) collective-permute-start(f32[1,64,256]{2,1,0:T(8,128)S(1)} %get-tuple-element.41), channel_id=1, source_target_pairs={{16,0},{20,4},{24,8},{28,12},{0,16},{4,20},{8,24},{12,28},{17,1},{... | collective-permute-start | bytes 196616 | tf_op jit(solution)/shard_map/ppermute | solution.py:54
  40.2 0.8 %collective-permute-done.14.refs_1_ = f32[64,256]{1,0:T(8,128)S(1)} collective-permute-done((f32[64,256]{1,0:T(8,128)S(1)}, f32[64,256]{1,0:T(8,128)S(1)}, u32[]{:S(2)}, u32[]{:S(2)}) %collective-permute-start.14) | collective-permute-done | bytes 65568 | tf_op jit(solution)/shard_map/ppermute | solution.py:60
  41.0 2.0 %collective-permute-done.15.refs_2_ = f32[64,256]{1,0:T(8,128)S(1)} collective-permute-done((f32[64,256]{1,0:T(8,128)S(1)}, f32[64,256]{1,0:T(8,128)S(1)}, u32[]{:S(2)}, u32[]{:S(2)}) %collective-permute-start.15) | collective-permute-done | bytes 65568 | tf_op jit(solution)/shard_map/ppermute | solution.py:60
  43.0 0.5 shard_map.89.refs_0_
  43.5 2.5 %collective-permute-start.21 = (f32[112,256]{1,0:T(8,128)S(1)}, f32[112,256]{1,0:T(8,128)S(1)}, u32[]{:S(2)}, u32[]{:S(2)}) collective-permute-start(f32[112,256]{1,0:T(8,128)S(1)} %shard_map.89.refs_0_), channel_id=1, source_target_pairs={{24,0},{28,4},{16,8},{20,12},{8,16},{12,20},{0,24},{4,28},{25,1},{... | collective-permute-start | bytes 344072 | tf_op jit(solution)/shard_map/ppermute | solution.py:54
  45.9 0.5 collective-permute-start.20
  46.4 0.6 collective-permute-start.19
  47.0 2.6 %collective-permute-done.21.refs_3_ = f32[112,256]{1,0:T(8,128)S(1)} collective-permute-done((f32[112,256]{1,0:T(8,128)S(1)}, f32[112,256]{1,0:T(8,128)S(1)}, u32[]{:S(2)}, u32[]{:S(2)}) %collective-permute-start.21) | collective-permute-done | bytes 114720 | tf_op jit(solution)/shard_map/ppermute | solution.py:54
  49.6 2.4 %collective-permute-done.20.refs_2_ = f32[112,256]{1,0:T(8,128)S(1)} collective-permute-done((f32[112,256]{1,0:T(8,128)S(1)}, f32[112,256]{1,0:T(8,128)S(1)}, u32[]{:S(2)}, u32[]{:S(2)}) %collective-permute-start.20) | collective-permute-done | bytes 114720 | tf_op jit(solution)/shard_map/ppermute | solution.py:54
  52.1 0.8 %shard_map.91.refs_2_ = f32[3,64,1024]{2,1,0:T(8,128)S(1)} custom-call(f32[4,112,256]{2,1,0:T(8,128)S(1)} %shard_map.90.refs_0_.refs_1_, bf16[8,2048,256]{2,1,0:T(8,128)(2,1)S(1)} %get-tuple-element.26.refs_1_.refs_3_.refs_2_), custom_call_target="tpu_custom_call" | custom-call | flops 536870912 | tf_op jit(solution)/shard_map/pallas_call | solution.py:71
  52.9 1.0 %collective-permute-done.22.refs_0_ = f32[4,112,256]{2,1,0:T(8,128)S(1)} collective-permute-done((f32[4,112,256]{2,1,0:T(8,128)S(1)}, f32[4,112,256]{2,1,0:T(8,128)S(1)}, u32[]{:S(2)}, u32[]{:S(2)}) %collective-permute-start.22) | collective-permute-done | bytes 458784 | tf_op jit(solution)/shard_map/ppermute | solution.py:54
  53.9 0.8 %shard_map.92 = (f32[88,256]{1,0:T(8,128)S(1)}, f32[88,256]{1,0:T(8,128)S(1)}, f32[88,256]{1,0:T(8,128)S(1)}, f32[88,256]{1,0:T(8,128)S(1)}) custom-call(f32[4,112,256]{2,1,0:T(8,128)S(1)} %collective-permute-done.22.refs_0_, f32[4,112,256]{2,1,0:T(8,128)S(1)} %shard_map.90.refs_0_.refs_1_, f32[3,64,1024]{2,1,0:T(8,128)S(1)} %shard_map.91.refs_2_, ...), custom_call_target="tpu_custom_call" | custom-call | flops 536870912 | tf_op jit(solution)/shard_map/pallas_call | solution.py:71
  54.7 1.8 %collective-permute-start.23 = (f32[88,256]{1,0:T(8,128)S(1)}, f32[88,256]{1,0:T(8,128)S(1)}, u32[]{:S(2)}, u32[]{:S(2)}) collective-permute-start(f32[88,256]{1,0:T(8,128)S(1)} %get-tuple-element.43), channel_id=1, source_target_pairs={{0,3},{1,2},{2,1},{3,0},{4,7},{5,6},{6,5},{7,4},{8,11},{9,10},{10,... | collective-permute-start | bytes 270344 | tf_op jit(solution)/shard_map/ppermute | solution.py:60
  56.5 2.7 %collective-permute-start.25 = (f32[88,256]{1,0:T(8,128)S(1)}, f32[88,256]{1,0:T(8,128)S(1)}, u32[]{:S(2)}, u32[]{:S(2)}) collective-permute-start(f32[88,256]{1,0:T(8,128)S(1)} %get-tuple-element.45), channel_id=1, source_target_pairs={{0,1},{1,0},{2,3},{3,2},{4,5},{5,4},{6,7},{7,6},{8,9},{9,8},{10,11... | collective-permute-start | bytes 270344 | tf_op jit(solution)/shard_map/ppermute | solution.py:60
  59.2 3.0 %collective-permute-done.23 = f32[88,256]{1,0:T(8,128)S(1)} collective-permute-done((f32[88,256]{1,0:T(8,128)S(1)}, f32[88,256]{1,0:T(8,128)S(1)}, u32[]{:S(2)}, u32[]{:S(2)}) %collective-permute-start.23) | collective-permute-done | bytes 90144 | tf_op jit(solution)/shard_map/ppermute | solution.py:60
  62.1 3.0 %collective-permute-done.24 = f32[88,256]{1,0:T(8,128)S(1)} collective-permute-done((f32[88,256]{1,0:T(8,128)S(1)}, f32[88,256]{1,0:T(8,128)S(1)}, u32[]{:S(2)}, u32[]{:S(2)}) %collective-permute-start.24) | collective-permute-done | bytes 90144 | tf_op jit(solution)/shard_map/ppermute | solution.py:60
  65.1 0.1 collective-permute-start.26
  65.2 0.7 fusion
  65.9 0.5 collective-permute-done.26.refs_1_
  66.4 1.4 %shard_map.93 = f32[3,64,64]{2,1,0:T(8,128)} custom-call(f32[24,256]{1,0:T(8,128)S(1)} %slice_add_fusion.3.refs_0_, f32[24,256]{1,0:T(8,128)S(1)} %collective-permute-done.26.refs_1_), custom_call_target="tpu_custom_call" | custom-call | tf_op jit(solution)/shard_map/pallas_call | solution.py:71
  (25 shorter events, 0.3 us)
Async XLA Ops:
  0.6 11.8 %collective-permute-start.3 = (f32[64,256]{1,0:T(8,128)}, f32[64,256]{1,0:T(8,128)S(1)}, u32[]{:S(2)}, u32[]{:S(2)}) collective-permute-start(f32[64,256]{1,0:T(8,128)} %refs_4_.1), channel_id=1, source_target_pairs={{2,0},{3,1},{0,2},{1,3},{6,4},{7,5},{4,6},{5,7},{10,8},{11,9},{8,1... | collective-permute-start | bytes 196616 | tf_op jit(solution)/shard_map/ppermute | solution.py:54
  4.7 7.7 %collective-permute-start = (f32[64,256]{1,0:T(8,128)}, f32[64,256]{1,0:T(8,128)S(1)}, u32[]{:S(2)}, u32[]{:S(2)}) collective-permute-start(f32[64,256]{1,0:T(8,128)} %refs_5_.1), channel_id=1, source_target_pairs={{8,0},{12,4},{0,8},{4,12},{24,16},{28,20},{16,24},{20,28},{9,1},{1... | collective-permute-start | bytes 196616 | tf_op jit(solution)/shard_map/ppermute | solution.py:54
  6.2 6.2 %collective-permute-start.2 = (f32[64,256]{1,0:T(8,128)}, f32[64,256]{1,0:T(8,128)S(1)}, u32[]{:S(2)}, u32[]{:S(2)}) collective-permute-start(f32[64,256]{1,0:T(8,128)} %refs_5_.1), channel_id=1, source_target_pairs={{24,0},{28,4},{16,8},{20,12},{8,16},{12,20},{0,24},{4,28},{25,1},{... | collective-permute-start | bytes 196616 | tf_op jit(solution)/shard_map/ppermute | solution.py:54
  7.7 4.7 %collective-permute-start.1 = (f32[64,256]{1,0:T(8,128)}, f32[64,256]{1,0:T(8,128)S(1)}, u32[]{:S(2)}, u32[]{:S(2)}) collective-permute-start(f32[64,256]{1,0:T(8,128)} %refs_5_.1), channel_id=1, source_target_pairs={{16,0},{20,4},{24,8},{28,12},{0,16},{4,20},{8,24},{12,28},{17,1},{... | collective-permute-start | bytes 196616 | tf_op jit(solution)/shard_map/ppermute | solution.py:54
  12.5 2.5 %collective-permute-start.4 = (f32[4,64,256]{2,1,0:T(8,128)S(1)}, f32[4,64,256]{2,1,0:T(8,128)S(1)}, u32[]{:S(2)}, u32[]{:S(2)}) collective-permute-start(f32[4,64,256]{2,1,0:T(8,128)S(1)} %shard_map.78.refs_0_.refs_1_), channel_id=1, source_target_pairs={{4,0},{0,4},{12,8},{8,12},{20,16},{16,20},{28,24},{24,28},{5,1},{1... | collective-permute-start | bytes 786440 | tf_op jit(solution)/shard_map/ppermute | solution.py:54
  12.6 7.7 %collective-permute-start.8 = (f32[2,64,256]{2,1,0:T(8,128)S(1)}, f32[2,64,256]{2,1,0:T(8,128)S(1)}, u32[]{:S(2)}, u32[]{:S(2)}) collective-permute-start(f32[2,64,256]{2,1,0:T(8,128)S(1)} %shard_map.80.refs_4_.refs_0_), channel_id=1, source_target_pairs={{1,0},{0,1},{3,2},{2,3},{5,4},{4,5},{7,6},{6,7},{9,8},{8,9},{11,10... | collective-permute-start | bytes 393224 | tf_op jit(solution)/shard_map/ppermute | solution.py:54
  15.8 6.9 %collective-permute-start.5 = (f32[64,256]{1,0:T(8,128)S(1)}, f32[64,256]{1,0:T(8,128)S(1)}, u32[]{:S(2)}, u32[]{:S(2)}) collective-permute-start(f32[64,256]{1,0:T(8,128)S(1)} %get-tuple-element.29), channel_id=1, source_target_pairs={{0,3},{1,2},{2,1},{3,0},{4,7},{5,6},{6,5},{7,4},{8,11},{9,10},{10,... | collective-permute-start | bytes 196616 | tf_op jit(solution)/shard_map/ppermute | solution.py:60
  16.3 8.1 %collective-permute-start.6 = (f32[64,256]{1,0:T(8,128)S(1)}, f32[64,256]{1,0:T(8,128)S(1)}, u32[]{:S(2)}, u32[]{:S(2)}) collective-permute-start(f32[64,256]{1,0:T(8,128)S(1)} %get-tuple-element.30), channel_id=1, source_target_pairs={{0,2},{1,3},{2,0},{3,1},{4,6},{5,7},{6,4},{7,5},{8,10},{9,11},{10,... | collective-permute-start | bytes 196616 | tf_op jit(solution)/shard_map/ppermute | solution.py:60
  18.0 6.5 %collective-permute-start.7 = (f32[64,256]{1,0:T(8,128)S(1)}, f32[64,256]{1,0:T(8,128)S(1)}, u32[]{:S(2)}, u32[]{:S(2)}) collective-permute-start(f32[64,256]{1,0:T(8,128)S(1)} %get-tuple-element.31), channel_id=1, source_target_pairs={{0,1},{1,0},{2,3},{3,2},{4,5},{5,4},{6,7},{7,6},{8,9},{9,8},{10,11... | collective-permute-start | bytes 196616 | tf_op jit(solution)/shard_map/ppermute | solution.py:60
  22.6 9.2 %collective-permute-start.13 = (f32[4,64,256]{2,1,0:T(8,128)S(1)}, f32[4,64,256]{2,1,0:T(8,128)S(1)}, u32[]{:S(2)}, u32[]{:S(2)}) collective-permute-start(f32[4,64,256]{2,1,0:T(8,128)S(1)} %get-tuple-element.32.refs_4_), channel_id=1, source_target_pairs={{4,0},{0,4},{12,8},{8,12},{20,16},{16,20},{28,24},{24,28},{5,1},{1... | collective-permute-start | bytes 786440 | tf_op jit(solution)/shard_map/ppermute | solution.py:54
  24.4 5.3 %collective-permute-start.11 = (f32[64,256]{1,0:T(8,128)S(1)}, f32[64,256]{1,0:T(8,128)S(1)}, u32[]{:S(2)}, u32[]{:S(2)}) collective-permute-start(f32[64,256]{1,0:T(8,128)S(1)} %shard_map.83.refs_0_.refs_5_), channel_id=1, source_target_pairs={{24,0},{28,4},{16,8},{20,12},{8,16},{12,20},{0,24},{4,28},{25,1},{... | collective-permute-start | bytes 196616 | tf_op jit(solution)/shard_map/ppermute | solution.py:54
  27.0 4.3 %collective-permute-start.10 = (f32[64,256]{1,0:T(8,128)S(1)}, f32[64,256]{1,0:T(8,128)S(1)}, u32[]{:S(2)}, u32[]{:S(2)}) collective-permute-start(f32[64,256]{1,0:T(8,128)S(1)} %shard_map.83.refs_0_.refs_5_), channel_id=1, source_target_pairs={{16,0},{20,4},{24,8},{28,12},{0,16},{4,20},{8,24},{12,28},{17,1},{... | collective-permute-start | bytes 196616 | tf_op jit(solution)/shard_map/ppermute | solution.py:54
  27.5 4.3 %collective-permute-start.9 = (f32[64,256]{1,0:T(8,128)S(1)}, f32[64,256]{1,0:T(8,128)S(1)}, u32[]{:S(2)}, u32[]{:S(2)}) collective-permute-start(f32[64,256]{1,0:T(8,128)S(1)} %shard_map.83.refs_0_.refs_5_), channel_id=1, source_target_pairs={{8,0},{12,4},{0,8},{4,12},{24,16},{28,20},{16,24},{20,28},{9,1},{1... | collective-permute-start | bytes 196616 | tf_op jit(solution)/shard_map/ppermute | solution.py:54
  31.7 1.6 %collective-permute-start.12 = (f32[4,64,256]{2,1,0:T(8,128)S(1)}, f32[4,64,256]{2,1,0:T(8,128)S(1)}, u32[]{:S(2)}, u32[]{:S(2)}) collective-permute-start(f32[4,64,256]{2,1,0:T(8,128)S(1)} %shard_map.84.refs_0_.refs_1_), channel_id=1, source_target_pairs={{4,0},{0,4},{12,8},{8,12},{20,16},{16,20},{28,24},{24,28},{5,1},{1... | collective-permute-start | bytes 786440 | tf_op jit(solution)/shard_map/ppermute | solution.py:54
  31.9 6.7 %collective-permute-start.17 = (f32[2,64,256]{2,1,0:T(8,128)S(1)}, f32[2,64,256]{2,1,0:T(8,128)S(1)}, u32[]{:S(2)}, u32[]{:S(2)}) collective-permute-start(f32[2,64,256]{2,1,0:T(8,128)S(1)} %get-tuple-element.39), channel_id=1, source_target_pairs={{8,0},{12,4},{0,8},{4,12},{24,16},{28,20},{16,24},{20,28},{9,1},{1... | collective-permute-start | bytes 393224 | tf_op jit(solution)/shard_map/ppermute | solution.py:54
  34.2 6.8 %collective-permute-start.14 = (f32[64,256]{1,0:T(8,128)S(1)}, f32[64,256]{1,0:T(8,128)S(1)}, u32[]{:S(2)}, u32[]{:S(2)}) collective-permute-start(f32[64,256]{1,0:T(8,128)S(1)} %get-tuple-element.34), channel_id=1, source_target_pairs={{0,3},{1,2},{2,1},{3,0},{4,7},{5,6},{6,5},{7,4},{8,11},{9,10},{10,... | collective-permute-start | bytes 196616 | tf_op jit(solution)/shard_map/ppermute | solution.py:60
  35.9 7.0 %collective-permute-start.15 = (f32[64,256]{1,0:T(8,128)S(1)}, f32[64,256]{1,0:T(8,128)S(1)}, u32[]{:S(2)}, u32[]{:S(2)}) collective-permute-start(f32[64,256]{1,0:T(8,128)S(1)} %get-tuple-element.35), channel_id=1, source_target_pairs={{0,2},{1,3},{2,0},{3,1},{4,6},{5,7},{6,4},{7,5},{8,10},{9,11},{10,... | collective-permute-start | bytes 196616 | tf_op jit(solution)/shard_map/ppermute | solution.py:60
  35.9 7.0 %collective-permute-start.16 = (f32[64,256]{1,0:T(8,128)S(1)}, f32[64,256]{1,0:T(8,128)S(1)}, u32[]{:S(2)}, u32[]{:S(2)}) collective-permute-start(f32[64,256]{1,0:T(8,128)S(1)} %get-tuple-element.36), channel_id=1, source_target_pairs={{0,1},{1,0},{2,3},{3,2},{4,5},{5,4},{6,7},{7,6},{8,9},{9,8},{10,11... | collective-permute-start | bytes 196616 | tf_op jit(solution)/shard_map/ppermute | solution.py:60
  38.6 4.3 %collective-permute-start.18 = (f32[1,64,256]{2,1,0:T(8,128)S(1)}, f32[1,64,256]{2,1,0:T(8,128)S(1)}, u32[]{:S(2)}, u32[]{:S(2)}) collective-permute-start(f32[1,64,256]{2,1,0:T(8,128)S(1)} %get-tuple-element.41), channel_id=1, source_target_pairs={{16,0},{20,4},{24,8},{28,12},{0,16},{4,20},{8,24},{12,28},{17,1},{... | collective-permute-start | bytes 196616 | tf_op jit(solution)/shard_map/ppermute | solution.py:54
  43.5 6.1 %collective-permute-start.21 = (f32[112,256]{1,0:T(8,128)S(1)}, f32[112,256]{1,0:T(8,128)S(1)}, u32[]{:S(2)}, u32[]{:S(2)}) collective-permute-start(f32[112,256]{1,0:T(8,128)S(1)} %shard_map.89.refs_0_), channel_id=1, source_target_pairs={{24,0},{28,4},{16,8},{20,12},{8,16},{12,20},{0,24},{4,28},{25,1},{... | collective-permute-start | bytes 344072 | tf_op jit(solution)/shard_map/ppermute | solution.py:54
  45.9 6.0 %collective-permute-start.20 = (f32[112,256]{1,0:T(8,128)S(1)}, f32[112,256]{1,0:T(8,128)S(1)}, u32[]{:S(2)}, u32[]{:S(2)}) collective-permute-start(f32[112,256]{1,0:T(8,128)S(1)} %shard_map.89.refs_0_), channel_id=1, source_target_pairs={{16,0},{20,4},{24,8},{28,12},{0,16},{4,20},{8,24},{12,28},{17,1},{... | collective-permute-start | bytes 344072 | tf_op jit(solution)/shard_map/ppermute | solution.py:54
  46.4 5.6 %collective-permute-start.19 = (f32[112,256]{1,0:T(8,128)S(1)}, f32[112,256]{1,0:T(8,128)S(1)}, u32[]{:S(2)}, u32[]{:S(2)}) collective-permute-start(f32[112,256]{1,0:T(8,128)S(1)} %shard_map.89.refs_0_), channel_id=1, source_target_pairs={{8,0},{12,4},{0,8},{4,12},{24,16},{28,20},{16,24},{20,28},{9,1},{1... | collective-permute-start | bytes 344072 | tf_op jit(solution)/shard_map/ppermute | solution.py:54
  52.0 1.9 %collective-permute-start.22 = (f32[4,112,256]{2,1,0:T(8,128)S(1)}, f32[4,112,256]{2,1,0:T(8,128)S(1)}, u32[]{:S(2)}, u32[]{:S(2)}) collective-permute-start(f32[4,112,256]{2,1,0:T(8,128)S(1)} %shard_map.90.refs_0_.refs_1_), channel_id=1, source_target_pairs={{4,0},{0,4},{12,8},{8,12},{20,16},{16,20},{28,24},{24,28},{5,1},{1... | collective-permute-start | bytes 1376264 | tf_op jit(solution)/shard_map/ppermute | solution.py:54
  54.7 7.4 %collective-permute-start.23 = (f32[88,256]{1,0:T(8,128)S(1)}, f32[88,256]{1,0:T(8,128)S(1)}, u32[]{:S(2)}, u32[]{:S(2)}) collective-permute-start(f32[88,256]{1,0:T(8,128)S(1)} %get-tuple-element.43), channel_id=1, source_target_pairs={{0,3},{1,2},{2,1},{3,0},{4,7},{5,6},{6,5},{7,4},{8,11},{9,10},{10,... | collective-permute-start | bytes 270344 | tf_op jit(solution)/shard_map/ppermute | solution.py:60
  56.5 8.6 %collective-permute-start.24 = (f32[88,256]{1,0:T(8,128)S(1)}, f32[88,256]{1,0:T(8,128)S(1)}, u32[]{:S(2)}, u32[]{:S(2)}) collective-permute-start(f32[88,256]{1,0:T(8,128)S(1)} %get-tuple-element.44), channel_id=1, source_target_pairs={{0,2},{1,3},{2,0},{3,1},{4,6},{5,7},{6,4},{7,5},{8,10},{9,11},{10,... | collective-permute-start | bytes 270344 | tf_op jit(solution)/shard_map/ppermute | solution.py:60
  56.5 8.6 %collective-permute-start.25 = (f32[88,256]{1,0:T(8,128)S(1)}, f32[88,256]{1,0:T(8,128)S(1)}, u32[]{:S(2)}, u32[]{:S(2)}) collective-permute-start(f32[88,256]{1,0:T(8,128)S(1)} %get-tuple-element.45), channel_id=1, source_target_pairs={{0,1},{1,0},{2,3},{3,2},{4,5},{5,4},{6,7},{7,6},{8,9},{9,8},{10,11... | collective-permute-start | bytes 270344 | tf_op jit(solution)/shard_map/ppermute | solution.py:60
  65.1 1.3 %collective-permute-start.26 = (f32[24,256]{1,0:T(8,128)S(1)}, f32[24,256]{1,0:T(8,128)S(1)}, u32[]{:S(2)}, u32[]{:S(2)}) collective-permute-start(f32[24,256]{1,0:T(8,128)S(1)} %slice_add_fusion.3.refs_0_), channel_id=1, source_target_pairs={{4,0},{0,4},{12,8},{8,12},{20,16},{16,20},{28,24},{24,28},{5,1},{1... | collective-permute-start | bytes 73736 | tf_op jit(solution)/shard_map/ppermute | solution.py:54

commit v10 on v9

--- a/solution.py
+++ b/solution.py
@@ -259,14 +259,12 @@
     return jnp.where(lax.axis_index("row") % 2 == 0, packed[:rows], packed[rows:])
 
 
-def second_half_kernel(span, pieces_ref, evens_ref, sums_ref, dense_ref, *refs):
-    outs, digits = refs[:-1], refs[-1]
-    n_col = len(outs)
+def second_half_kernel(span, shifts, pieces_ref, evens_ref, sums_ref, dense_ref, *refs):
+    outs, digits = dict(zip(shifts, refs[:-1])), refs[-1]
     fill_digits(span, pieces_ref, digits)
-    row_blocks, _, width = dense_ref.shape
-    tile_len = width // 2
-    piece_blocks = row_blocks // n_col
-    for e in reversed(range(n_col)):
+    tile_len = dense_ref.shape[2] // 2
+    piece_blocks = pieces_ref.shape[2] // tile_len
+    for e in shifts:
         for sub in range(piece_blocks):
             block = e * piece_blocks + sub
             parts = half_products(1, span, pieces_ref, dense_ref, digits, block)
@@ -275,10 +273,10 @@
                 for index, part in enumerate(parts)
             )
             outs[e][:span, sub * tile_len : (sub + 1) * tile_len] = combine(*parts)
-    if outs[0].shape[0] > span:
+    if pieces_ref.shape[1] > span:
         packed = jnp.sum(pieces_ref[:, span:, :], 0) + jnp.sum(evens_ref[:, span:, :], 0)
         packed = half_of_core(packed)
-        for out in outs:
+        for out in outs.values():
             out[span:, :] = packed
 
 
@@ -297,17 +295,20 @@
 def dense_second(odds, evens, sums, span, n_col, dense, before):
     _, depth, _ = dense.shape
     _, rows, piece_len = odds.shape
-    return list(
-        call(
-            functools.partial(second_half_kernel, span),
+    outs = {}
+    for shifts in (range(n_col // 2, n_col), range(n_col // 2)):
+        shifts = [*reversed(shifts)]
+        parts = call(
+            functools.partial(second_half_kernel, span, shifts),
             [odds, evens, sums, dense],
-            [held(span + (rows - span) // 2, piece_len)] * n_col,
+            [held(span + (rows - span) // 2, piece_len)] * len(shifts),
             before,
             scratch=[pltpu.VMEM((2 * span, depth // 2), jnp.bfloat16)],
             limit=VMEM_LIMIT,
-            flops=2 * span * dense.size,
+            flops=span * dense.size,
         )
-    )
+        outs.update(zip(shifts, parts))
+    return [outs[e] for e in range(n_col)]
 
 
 def left_kernel(n_row, x_evens, x_odds, dense_ref, evens_ref, odds_ref):

time: 68 us -> 68.2 us (level)
  starting transfers between devices: 32.2 us -> 31.1 us
  Pallas kernels: 12.6 us -> 13.3 us
  waiting for transfers between devices: 20.8 us -> 21.5 us
    ppermute x9, starting transfers between devices: 13.4 us -> 12.2 us  [scatter_pieces(): lax.ppermute(pieces[shift], axis, [(i, partner(i, shift, size)) for i in...]
    ppermute x18, waiting for transfers between devices: 10.4 us -> 11.4 us  [fetch(): lax.ppermute(piece, axis, [(partner(i, shift, size), i) for i in range(si...]
    pallas_call x16 -> x19, Pallas kernels: 9.1 us -> 9.75 us  [call(): pl.pallas_call(body, in_specs=[vmem] * len(operands) + [pl.BlockSpec(memo...]
  transfers between devices with their start and end apart: 27 -> 27, of which waited for: 14 -> 15; matrix products, arithmetic and copies ran while one was open for 1% -> 1% of each run, Pallas kernels for 14% -> 16%
where the time goes in v10:
time: 68.2 us; the launch traced here: 68.1 us
  starting transfers between devices  31.1 us (46%)
  waiting for transfers between devices  21.5 us (32%)
  Pallas kernels  13.3 us (20%)
  between operations  1.51 us (2%)
    ppermute x18, starting transfers between devices, fetch(): lax.ppermute(piece, axis, [(partner(i, shift, size), i) for i in range(si...  18.9 us
    ppermute x9, starting transfers between devices, scatter_pieces(): lax.ppermute(pieces[shift], axis, [(i, partner(i, shift, size)) for i in...  12.2 us
    ppermute x18, waiting for transfers between devices, fetch(): lax.ppermute(piece, axis, [(partner(i, shift, size), i) for i in range(si...  11.4 us
    ppermute x9, waiting for transfers between devices, scatter_pieces(): lax.ppermute(pieces[shift], axis, [(i, partner(i, shift, size)) for i in...  10.1 us
    pallas_call x19, Pallas kernels, call(): pl.pallas_call(body, in_specs=[vmem] * len(operands) + [pl.BlockSpec(memo...  9.75 us
    pallas_call x1, Pallas kernels, build_dense(): pl.pallas_call(functools.partial(build_kernel, (*sizes, group)), in_specs...  3.5 us
  transfers between devices with their start and end apart: 27, of which 15 were waited for; matrix products, arithmetic and copies ran while one was open for 1% of the time, Pallas kernels for 16%

profile of v10, /device:TPU:0, one launch (start us, length us, event | category | flops | bytes accessed | tf_op | source)
XLA Modules:
  0.0 68.1 jit_solution(14666076648167422606)
XLA Ops:
  0.6 4.1 %collective-permute-start.3 = (f32[64,256]{1,0:T(8,128)}, f32[64,256]{1,0:T(8,128)S(1)}, u32[]{:S(2)}, u32[]{:S(2)}) collective-permute-start(f32[64,256]{1,0:T(8,128)} %refs_4_.1), channel_id=1, source_target_pairs={{2,0},{3,1},{0,2},{1,3},{6,4},{7,5},{4,6},{5,7},{10,8},{11,9},{8,1... | collective-permute-start | bytes 196616 | tf_op jit(solution)/shard_map/ppermute | solution.py:54
  4.7 1.5 %collective-permute-start = (f32[64,256]{1,0:T(8,128)}, f32[64,256]{1,0:T(8,128)S(1)}, u32[]{:S(2)}, u32[]{:S(2)}) collective-permute-start(f32[64,256]{1,0:T(8,128)} %refs_5_.1), channel_id=1, source_target_pairs={{8,0},{12,4},{0,8},{4,12},{24,16},{28,20},{16,24},{20,28},{9,1},{1... | collective-permute-start | bytes 196616 | tf_op jit(solution)/shard_map/ppermute | solution.py:54
  6.2 1.5 %collective-permute-start.2 = (f32[64,256]{1,0:T(8,128)}, f32[64,256]{1,0:T(8,128)S(1)}, u32[]{:S(2)}, u32[]{:S(2)}) collective-permute-start(f32[64,256]{1,0:T(8,128)} %refs_5_.1), channel_id=1, source_target_pairs={{24,0},{28,4},{16,8},{20,12},{8,16},{12,20},{0,24},{4,28},{25,1},{... | collective-permute-start | bytes 196616 | tf_op jit(solution)/shard_map/ppermute | solution.py:54
  7.7 0.5 collective-permute-start.1
  8.9 3.5 %shard_map.77 = (bf16[8,2048,256]{2,1,0:T(8,128)(2,1)S(1)}, f32[64,256]{1,0:T(8,128)S(1)}, f32[64,256]{1,0:T(8,128)S(1)}, f32[8,128]{1,0:T(8,128)S(1)}) custom-call(s32[1,1,64]{2,1,0:T(1,128)} %refs_0_.1, s32[1,1,64]{2,1,0:T(1,128)} %refs_1_.1, s32[1,1]{1,0:T(1,128)S(6)} %copy.8.refs_2_, f32[1,1,64,128,128]{4,3,2,1,0:T(8,128)} %refs_3_.1, ...), custom_call_target="tpu_custom_call" | custom-call | flops 8388608 | bytes 8388608 | tf_op jit(solution)/shard_map/pallas_call | solution.py:201
  12.6 1.6 %collective-permute-start.8 = (f32[2,64,256]{2,1,0:T(8,128)S(1)}, f32[2,64,256]{2,1,0:T(8,128)S(1)}, u32[]{:S(2)}, u32[]{:S(2)}) collective-permute-start(f32[2,64,256]{2,1,0:T(8,128)S(1)} %shard_map.80.refs_4_.refs_0_), channel_id=1, source_target_pairs={{1,0},{0,1},{3,2},{2,3},{5,4},{4,5},{7,6},{6,7},{9,8},{8,9},{11,10... | collective-permute-start | bytes 393224 | tf_op jit(solution)/shard_map/ppermute | solution.py:54
  14.2 0.7 %shard_map.79.refs_2_ = f32[3,64,1024]{2,1,0:T(8,128)S(1)} custom-call(f32[4,64,256]{2,1,0:T(8,128)S(1)} %shard_map.78.refs_0_.refs_1_, bf16[8,2048,256]{2,1,0:T(8,128)(2,1)S(1)} %get-tuple-element.26.refs_1_.refs_3_.refs_2_), custom_call_target="tpu_custom_call" | custom-call | flops 536870912 | tf_op jit(solution)/shard_map/pallas_call | solution.py:71
  15.0 0.5 shard_map.82
  15.5 0.5 collective-permute-start.5
  16.0 1.7 %collective-permute-start.6 = (f32[64,256]{1,0:T(8,128)S(1)}, f32[64,256]{1,0:T(8,128)S(1)}, u32[]{:S(2)}, u32[]{:S(2)}) collective-permute-start(f32[64,256]{1,0:T(8,128)S(1)} %get-tuple-element.30), channel_id=1, source_target_pairs={{0,2},{1,3},{2,0},{3,1},{4,6},{5,7},{6,4},{7,5},{8,10},{9,11},{10,... | collective-permute-start | bytes 196616 | tf_op jit(solution)/shard_map/ppermute | solution.py:60
  17.7 0.5 shard_map.81
  18.2 2.3 %collective-permute-start.7 = (f32[64,256]{1,0:T(8,128)S(1)}, f32[64,256]{1,0:T(8,128)S(1)}, u32[]{:S(2)}, u32[]{:S(2)}) collective-permute-start(f32[64,256]{1,0:T(8,128)S(1)} %get-tuple-element.31), channel_id=1, source_target_pairs={{0,1},{1,0},{2,3},{3,2},{4,5},{5,4},{6,7},{7,6},{8,9},{9,8},{10,11... | collective-permute-start | bytes 196616 | tf_op jit(solution)/shard_map/ppermute | solution.py:60
  20.5 2.4 %shard_map.83 = (f32[4,64,256]{2,1,0:T(8,128)S(1)}, f32[4,64,256]{2,1,0:T(8,128)S(1)}) custom-call(f32[2,64,256]{2,1,0:T(8,128)S(1)} %shard_map.80.refs_4_.refs_0_, f32[2,64,256]{2,1,0:T(8,128)S(1)} %collective-permute-done.8.refs_1_, bf16[8,2048,256]{2,1,0:T(8,128)(2,1)S(1)} %get-tuple-element.26.refs_1_.refs_3_.refs_2_, ...), custom_call_target="tpu_custom_call" | custom-call | flops 1073741824 | tf_op jit(solution)/shard_map/pallas_call | solution.py:71
  23.0 1.1 %collective-permute-done.6.refs_2_ = f32[64,256]{1,0:T(8,128)S(1)} collective-permute-done((f32[64,256]{1,0:T(8,128)S(1)}, f32[64,256]{1,0:T(8,128)S(1)}, u32[]{:S(2)}, u32[]{:S(2)}) %collective-permute-start.6) | collective-permute-done | bytes 65568 | tf_op jit(solution)/shard_map/ppermute | solution.py:60
  24.1 2.5 %collective-permute-start.11 = (f32[64,256]{1,0:T(8,128)S(1)}, f32[64,256]{1,0:T(8,128)S(1)}, u32[]{:S(2)}, u32[]{:S(2)}) collective-permute-start(f32[64,256]{1,0:T(8,128)S(1)} %shard_map.84.refs_0_.refs_5_), channel_id=1, source_target_pairs={{24,0},{28,4},{16,8},{20,12},{8,16},{12,20},{0,24},{4,28},{25,1},{... | collective-permute-start | bytes 196616 | tf_op jit(solution)/shard_map/ppermute | solution.py:54
  26.7 0.5 collective-permute-start.10
  27.2 0.5 collective-permute-start.9
  27.7 1.8 %collective-permute-done.11.refs_3_ = f32[64,256]{1,0:T(8,128)S(1)} collective-permute-done((f32[64,256]{1,0:T(8,128)S(1)}, f32[64,256]{1,0:T(8,128)S(1)}, u32[]{:S(2)}, u32[]{:S(2)}) %collective-permute-start.11) | collective-permute-done | bytes 65568 | tf_op jit(solution)/shard_map/ppermute | solution.py:54
  29.5 1.4 %collective-permute-done.10.refs_2_ = f32[64,256]{1,0:T(8,128)S(1)} collective-permute-done((f32[64,256]{1,0:T(8,128)S(1)}, f32[64,256]{1,0:T(8,128)S(1)}, u32[]{:S(2)}, u32[]{:S(2)}) %collective-permute-start.10) | collective-permute-done | bytes 65568 | tf_op jit(solution)/shard_map/ppermute | solution.py:54
  30.9 0.5 collective-permute-done.9.refs_1_
  31.6 0.6 collective-permute-start.17
  32.2 0.7 %shard_map.86.refs_2_ = f32[3,64,1024]{2,1,0:T(8,128)S(1)} custom-call(f32[4,64,256]{2,1,0:T(8,128)S(1)} %shard_map.85.refs_0_.refs_1_, bf16[8,2048,256]{2,1,0:T(8,128)(2,1)S(1)} %get-tuple-element.26.refs_1_.refs_3_.refs_2_), custom_call_target="tpu_custom_call" | custom-call | flops 536870912 | tf_op jit(solution)/shard_map/pallas_call | solution.py:71
  33.1 0.5 shard_map.88
  33.6 2.0 %collective-permute-start.14 = (f32[64,256]{1,0:T(8,128)S(1)}, f32[64,256]{1,0:T(8,128)S(1)}, u32[]{:S(2)}, u32[]{:S(2)}) collective-permute-start(f32[64,256]{1,0:T(8,128)S(1)} %get-tuple-element.34), channel_id=1, source_target_pairs={{0,3},{1,2},{2,1},{3,0},{4,7},{5,6},{6,5},{7,4},{8,11},{9,10},{10,... | collective-permute-start | bytes 196616 | tf_op jit(solution)/shard_map/ppermute | solution.py:60
  35.7 0.5 shard_map.87
  36.3 1.3 %collective-permute-done.17.refs_1_ = f32[2,64,256]{2,1,0:T(8,128)S(1)} collective-permute-done((f32[2,64,256]{2,1,0:T(8,128)S(1)}, f32[2,64,256]{2,1,0:T(8,128)S(1)}, u32[]{:S(2)}, u32[]{:S(2)}) %collective-permute-start.17) | collective-permute-done | bytes 131104 | tf_op jit(solution)/shard_map/ppermute | solution.py:54
  37.6 1.6 %collective-permute-start.18 = (f32[1,64,256]{2,1,0:T(8,128)S(1)}, f32[1,64,256]{2,1,0:T(8,128)S(1)}, u32[]{:S(2)}, u32[]{:S(2)}) collective-permute-start(f32[1,64,256]{2,1,0:T(8,128)S(1)} %get-tuple-element.41), channel_id=1, source_target_pairs={{16,0},{20,4},{24,8},{28,12},{0,16},{4,20},{8,24},{12,28},{17,1},{... | collective-permute-start | bytes 196616 | tf_op jit(solution)/shard_map/ppermute | solution.py:54
  39.1 1.0 %collective-permute-start.16 = (f32[64,256]{1,0:T(8,128)S(1)}, f32[64,256]{1,0:T(8,128)S(1)}, u32[]{:S(2)}, u32[]{:S(2)}) collective-permute-start(f32[64,256]{1,0:T(8,128)S(1)} %get-tuple-element.36), channel_id=1, source_target_pairs={{0,1},{1,0},{2,3},{3,2},{4,5},{5,4},{6,7},{7,6},{8,9},{9,8},{10,11... | collective-permute-start | bytes 196616 | tf_op jit(solution)/shard_map/ppermute | solution.py:60
  40.2 0.2 collective-permute-done.14.refs_1_
  40.4 2.1 %collective-permute-done.15.refs_2_ = f32[64,256]{1,0:T(8,128)S(1)} collective-permute-done((f32[64,256]{1,0:T(8,128)S(1)}, f32[64,256]{1,0:T(8,128)S(1)}, u32[]{:S(2)}, u32[]{:S(2)}) %collective-permute-start.15) | collective-permute-done | bytes 65568 | tf_op jit(solution)/shard_map/ppermute | solution.py:60
  42.5 1.3 %collective-permute-done.16.refs_3_ = f32[64,256]{1,0:T(8,128)S(1)} collective-permute-done((f32[64,256]{1,0:T(8,128)S(1)}, f32[64,256]{1,0:T(8,128)S(1)}, u32[]{:S(2)}, u32[]{:S(2)}) %collective-permute-start.16) | collective-permute-done | bytes 65568 | tf_op jit(solution)/shard_map/ppermute | solution.py:60
  43.8 0.5 shard_map.91.refs_0_
  44.3 1.5 %collective-permute-start.21 = (f32[112,256]{1,0:T(8,128)S(1)}, f32[112,256]{1,0:T(8,128)S(1)}, u32[]{:S(2)}, u32[]{:S(2)}) collective-permute-start(f32[112,256]{1,0:T(8,128)S(1)} %shard_map.91.refs_0_), channel_id=1, source_target_pairs={{24,0},{28,4},{16,8},{20,12},{8,16},{12,20},{0,24},{4,28},{25,1},{... | collective-permute-start | bytes 344072 | tf_op jit(solution)/shard_map/ppermute | solution.py:54
  45.7 0.8 %collective-permute-start.20 = (f32[112,256]{1,0:T(8,128)S(1)}, f32[112,256]{1,0:T(8,128)S(1)}, u32[]{:S(2)}, u32[]{:S(2)}) collective-permute-start(f32[112,256]{1,0:T(8,128)S(1)} %shard_map.91.refs_0_), channel_id=1, source_target_pairs={{16,0},{20,4},{24,8},{28,12},{0,16},{4,20},{8,24},{12,28},{17,1},{... | collective-permute-start | bytes 344072 | tf_op jit(solution)/shard_map/ppermute | solution.py:54
  46.5 1.3 %collective-permute-start.19 = (f32[112,256]{1,0:T(8,128)S(1)}, f32[112,256]{1,0:T(8,128)S(1)}, u32[]{:S(2)}, u32[]{:S(2)}) collective-permute-start(f32[112,256]{1,0:T(8,128)S(1)} %shard_map.91.refs_0_), channel_id=1, source_target_pairs={{8,0},{12,4},{0,8},{4,12},{24,16},{28,20},{16,24},{20,28},{9,1},{1... | collective-permute-start | bytes 344072 | tf_op jit(solution)/shard_map/ppermute | solution.py:54
  47.8 3.4 %collective-permute-done.21.refs_3_ = f32[112,256]{1,0:T(8,128)S(1)} collective-permute-done((f32[112,256]{1,0:T(8,128)S(1)}, f32[112,256]{1,0:T(8,128)S(1)}, u32[]{:S(2)}, u32[]{:S(2)}) %collective-permute-start.21) | collective-permute-done | bytes 114720 | tf_op jit(solution)/shard_map/ppermute | solution.py:54
  51.2 1.3 %collective-permute-done.20.refs_2_ = f32[112,256]{1,0:T(8,128)S(1)} collective-permute-done((f32[112,256]{1,0:T(8,128)S(1)}, f32[112,256]{1,0:T(8,128)S(1)}, u32[]{:S(2)}, u32[]{:S(2)}) %collective-permute-start.20) | collective-permute-done | bytes 114720 | tf_op jit(solution)/shard_map/ppermute | solution.py:54
  52.6 0.8 %shard_map.93.refs_2_ = f32[3,64,1024]{2,1,0:T(8,128)S(1)} custom-call(f32[4,112,256]{2,1,0:T(8,128)S(1)} %shard_map.92.refs_0_.refs_1_, bf16[8,2048,256]{2,1,0:T(8,128)(2,1)S(1)} %get-tuple-element.26.refs_1_.refs_3_.refs_2_), custom_call_target="tpu_custom_call" | custom-call | flops 536870912 | tf_op jit(solution)/shard_map/pallas_call | solution.py:71
  53.4 1.0 %collective-permute-done.22.refs_0_ = f32[4,112,256]{2,1,0:T(8,128)S(1)} collective-permute-done((f32[4,112,256]{2,1,0:T(8,128)S(1)}, f32[4,112,256]{2,1,0:T(8,128)S(1)}, u32[]{:S(2)}, u32[]{:S(2)}) %collective-permute-start.22) | collective-permute-done | bytes 458784 | tf_op jit(solution)/shard_map/ppermute | solution.py:54
  54.4 0.5 shard_map.95
  55.0 2.2 %collective-permute-start.23 = (f32[88,256]{1,0:T(8,128)S(1)}, f32[88,256]{1,0:T(8,128)S(1)}, u32[]{:S(2)}, u32[]{:S(2)}) collective-permute-start(f32[88,256]{1,0:T(8,128)S(1)} %get-tuple-element.43), channel_id=1, source_target_pairs={{0,3},{1,2},{2,1},{3,0},{4,7},{5,6},{6,5},{7,4},{8,11},{9,10},{10,... | collective-permute-start | bytes 270344 | tf_op jit(solution)/shard_map/ppermute | solution.py:60
  57.1 0.5 shard_map.94
  57.6 2.4 %collective-permute-start.25 = (f32[88,256]{1,0:T(8,128)S(1)}, f32[88,256]{1,0:T(8,128)S(1)}, u32[]{:S(2)}, u32[]{:S(2)}) collective-permute-start(f32[88,256]{1,0:T(8,128)S(1)} %get-tuple-element.45), channel_id=1, source_target_pairs={{0,1},{1,0},{2,3},{3,2},{4,5},{5,4},{6,7},{7,6},{8,9},{9,8},{10,11... | collective-permute-start | bytes 270344 | tf_op jit(solution)/shard_map/ppermute | solution.py:60
  60.0 2.4 %collective-permute-done.23 = f32[88,256]{1,0:T(8,128)S(1)} collective-permute-done((f32[88,256]{1,0:T(8,128)S(1)}, f32[88,256]{1,0:T(8,128)S(1)}, u32[]{:S(2)}, u32[]{:S(2)}) %collective-permute-start.23) | collective-permute-done | bytes 90144 | tf_op jit(solution)/shard_map/ppermute | solution.py:60
  62.4 3.0 %collective-permute-done.24 = f32[88,256]{1,0:T(8,128)S(1)} collective-permute-done((f32[88,256]{1,0:T(8,128)S(1)}, f32[88,256]{1,0:T(8,128)S(1)}, u32[]{:S(2)}, u32[]{:S(2)}) %collective-permute-start.24) | collective-permute-done | bytes 90144 | tf_op jit(solution)/shard_map/ppermute | solution.py:60
  65.4 0.7 fusion
  66.1 0.5 collective-permute-done.26.refs_1_
  66.6 1.4 %shard_map.96 = f32[3,64,64]{2,1,0:T(8,128)} custom-call(f32[24,256]{1,0:T(8,128)S(1)} %slice_add_fusion.3.refs_0_, f32[24,256]{1,0:T(8,128)S(1)} %collective-permute-done.26.refs_1_), custom_call_target="tpu_custom_call" | custom-call | tf_op jit(solution)/shard_map/pallas_call | solution.py:71
  (28 shorter events, 0.8 us)
Async XLA Ops:
  0.6 11.8 %collective-permute-start.3 = (f32[64,256]{1,0:T(8,128)}, f32[64,256]{1,0:T(8,128)S(1)}, u32[]{:S(2)}, u32[]{:S(2)}) collective-permute-start(f32[64,256]{1,0:T(8,128)} %refs_4_.1), channel_id=1, source_target_pairs={{2,0},{3,1},{0,2},{1,3},{6,4},{7,5},{4,6},{5,7},{10,8},{11,9},{8,1... | collective-permute-start | bytes 196616 | tf_op jit(solution)/shard_map/ppermute | solution.py:54
  4.7 7.7 %collective-permute-start = (f32[64,256]{1,0:T(8,128)}, f32[64,256]{1,0:T(8,128)S(1)}, u32[]{:S(2)}, u32[]{:S(2)}) collective-permute-start(f32[64,256]{1,0:T(8,128)} %refs_5_.1), channel_id=1, source_target_pairs={{8,0},{12,4},{0,8},{4,12},{24,16},{28,20},{16,24},{20,28},{9,1},{1... | collective-permute-start | bytes 196616 | tf_op jit(solution)/shard_map/ppermute | solution.py:54
  6.2 6.2 %collective-permute-start.2 = (f32[64,256]{1,0:T(8,128)}, f32[64,256]{1,0:T(8,128)S(1)}, u32[]{:S(2)}, u32[]{:S(2)}) collective-permute-start(f32[64,256]{1,0:T(8,128)} %refs_5_.1), channel_id=1, source_target_pairs={{24,0},{28,4},{16,8},{20,12},{8,16},{12,20},{0,24},{4,28},{25,1},{... | collective-permute-start | bytes 196616 | tf_op jit(solution)/shard_map/ppermute | solution.py:54
  7.7 4.7 %collective-permute-start.1 = (f32[64,256]{1,0:T(8,128)}, f32[64,256]{1,0:T(8,128)S(1)}, u32[]{:S(2)}, u32[]{:S(2)}) collective-permute-start(f32[64,256]{1,0:T(8,128)} %refs_5_.1), channel_id=1, source_target_pairs={{16,0},{20,4},{24,8},{28,12},{0,16},{4,20},{8,24},{12,28},{17,1},{... | collective-permute-start | bytes 196616 | tf_op jit(solution)/shard_map/ppermute | solution.py:54
  12.5 2.5 %collective-permute-start.4 = (f32[4,64,256]{2,1,0:T(8,128)S(1)}, f32[4,64,256]{2,1,0:T(8,128)S(1)}, u32[]{:S(2)}, u32[]{:S(2)}) collective-permute-start(f32[4,64,256]{2,1,0:T(8,128)S(1)} %shard_map.78.refs_0_.refs_1_), channel_id=1, source_target_pairs={{4,0},{0,4},{12,8},{8,12},{20,16},{16,20},{28,24},{24,28},{5,1},{1... | collective-permute-start | bytes 786440 | tf_op jit(solution)/shard_map/ppermute | solution.py:54
  12.6 8.0 %collective-permute-start.8 = (f32[2,64,256]{2,1,0:T(8,128)S(1)}, f32[2,64,256]{2,1,0:T(8,128)S(1)}, u32[]{:S(2)}, u32[]{:S(2)}) collective-permute-start(f32[2,64,256]{2,1,0:T(8,128)S(1)} %shard_map.80.refs_4_.refs_0_), channel_id=1, source_target_pairs={{1,0},{0,1},{3,2},{2,3},{5,4},{4,5},{7,6},{6,7},{9,8},{8,9},{11,10... | collective-permute-start | bytes 393224 | tf_op jit(solution)/shard_map/ppermute | solution.py:54
  15.5 7.5 %collective-permute-start.5 = (f32[64,256]{1,0:T(8,128)S(1)}, f32[64,256]{1,0:T(8,128)S(1)}, u32[]{:S(2)}, u32[]{:S(2)}) collective-permute-start(f32[64,256]{1,0:T(8,128)S(1)} %get-tuple-element.29), channel_id=1, source_target_pairs={{0,3},{1,2},{2,1},{3,0},{4,7},{5,6},{6,5},{7,4},{8,11},{9,10},{10,... | collective-permute-start | bytes 196616 | tf_op jit(solution)/shard_map/ppermute | solution.py:60
  16.0 8.1 %collective-permute-start.6 = (f32[64,256]{1,0:T(8,128)S(1)}, f32[64,256]{1,0:T(8,128)S(1)}, u32[]{:S(2)}, u32[]{:S(2)}) collective-permute-start(f32[64,256]{1,0:T(8,128)S(1)} %get-tuple-element.30), channel_id=1, source_target_pairs={{0,2},{1,3},{2,0},{3,1},{4,6},{5,7},{6,4},{7,5},{8,10},{9,11},{10,... | collective-permute-start | bytes 196616 | tf_op jit(solution)/shard_map/ppermute | solution.py:60
  18.2 5.9 %collective-permute-start.7 = (f32[64,256]{1,0:T(8,128)S(1)}, f32[64,256]{1,0:T(8,128)S(1)}, u32[]{:S(2)}, u32[]{:S(2)}) collective-permute-start(f32[64,256]{1,0:T(8,128)S(1)} %get-tuple-element.31), channel_id=1, source_target_pairs={{0,1},{1,0},{2,3},{3,2},{4,5},{5,4},{6,7},{7,6},{8,9},{9,8},{10,11... | collective-permute-start | bytes 196616 | tf_op jit(solution)/shard_map/ppermute | solution.py:60
  22.9 8.6 %collective-permute-start.13 = (f32[4,64,256]{2,1,0:T(8,128)S(1)}, f32[4,64,256]{2,1,0:T(8,128)S(1)}, u32[]{:S(2)}, u32[]{:S(2)}) collective-permute-start(f32[4,64,256]{2,1,0:T(8,128)S(1)} %get-tuple-element.32.refs_4_), channel_id=1, source_target_pairs={{4,0},{0,4},{12,8},{8,12},{20,16},{16,20},{28,24},{24,28},{5,1},{1... | collective-permute-start | bytes 786440 | tf_op jit(solution)/shard_map/ppermute | solution.py:54
  24.1 5.3 %collective-permute-start.11 = (f32[64,256]{1,0:T(8,128)S(1)}, f32[64,256]{1,0:T(8,128)S(1)}, u32[]{:S(2)}, u32[]{:S(2)}) collective-permute-start(f32[64,256]{1,0:T(8,128)S(1)} %shard_map.84.refs_0_.refs_5_), channel_id=1, source_target_pairs={{24,0},{28,4},{16,8},{20,12},{8,16},{12,20},{0,24},{4,28},{25,1},{... | collective-permute-start | bytes 196616 | tf_op jit(solution)/shard_map/ppermute | solution.py:54
  26.7 4.3 %collective-permute-start.10 = (f32[64,256]{1,0:T(8,128)S(1)}, f32[64,256]{1,0:T(8,128)S(1)}, u32[]{:S(2)}, u32[]{:S(2)}) collective-permute-start(f32[64,256]{1,0:T(8,128)S(1)} %shard_map.84.refs_0_.refs_5_), channel_id=1, source_target_pairs={{16,0},{20,4},{24,8},{28,12},{0,16},{4,20},{8,24},{12,28},{17,1},{... | collective-permute-start | bytes 196616 | tf_op jit(solution)/shard_map/ppermute | solution.py:54
  27.2 4.3 %collective-permute-start.9 = (f32[64,256]{1,0:T(8,128)S(1)}, f32[64,256]{1,0:T(8,128)S(1)}, u32[]{:S(2)}, u32[]{:S(2)}) collective-permute-start(f32[64,256]{1,0:T(8,128)S(1)} %shard_map.84.refs_0_.refs_5_), channel_id=1, source_target_pairs={{8,0},{12,4},{0,8},{4,12},{24,16},{28,20},{16,24},{20,28},{9,1},{1... | collective-permute-start | bytes 196616 | tf_op jit(solution)/shard_map/ppermute | solution.py:54
  31.5 1.6 %collective-permute-start.12 = (f32[4,64,256]{2,1,0:T(8,128)S(1)}, f32[4,64,256]{2,1,0:T(8,128)S(1)}, u32[]{:S(2)}, u32[]{:S(2)}) collective-permute-start(f32[4,64,256]{2,1,0:T(8,128)S(1)} %shard_map.85.refs_0_.refs_1_), channel_id=1, source_target_pairs={{4,0},{0,4},{12,8},{8,12},{20,16},{16,20},{28,24},{24,28},{5,1},{1... | collective-permute-start | bytes 786440 | tf_op jit(solution)/shard_map/ppermute | solution.py:54
  31.6 6.0 %collective-permute-start.17 = (f32[2,64,256]{2,1,0:T(8,128)S(1)}, f32[2,64,256]{2,1,0:T(8,128)S(1)}, u32[]{:S(2)}, u32[]{:S(2)}) collective-permute-start(f32[2,64,256]{2,1,0:T(8,128)S(1)} %get-tuple-element.39), channel_id=1, source_target_pairs={{8,0},{12,4},{0,8},{4,12},{24,16},{28,20},{16,24},{20,28},{9,1},{1... | collective-permute-start | bytes 393224 | tf_op jit(solution)/shard_map/ppermute | solution.py:54
  33.6 6.8 %collective-permute-start.14 = (f32[64,256]{1,0:T(8,128)S(1)}, f32[64,256]{1,0:T(8,128)S(1)}, u32[]{:S(2)}, u32[]{:S(2)}) collective-permute-start(f32[64,256]{1,0:T(8,128)S(1)} %get-tuple-element.34), channel_id=1, source_target_pairs={{0,3},{1,2},{2,1},{3,0},{4,7},{5,6},{6,5},{7,4},{8,11},{9,10},{10,... | collective-permute-start | bytes 196616 | tf_op jit(solution)/shard_map/ppermute | solution.py:60
  35.6 6.9 %collective-permute-start.15 = (f32[64,256]{1,0:T(8,128)S(1)}, f32[64,256]{1,0:T(8,128)S(1)}, u32[]{:S(2)}, u32[]{:S(2)}) collective-permute-start(f32[64,256]{1,0:T(8,128)S(1)} %get-tuple-element.35), channel_id=1, source_target_pairs={{0,2},{1,3},{2,0},{3,1},{4,6},{5,7},{6,4},{7,5},{8,10},{9,11},{10,... | collective-permute-start | bytes 196616 | tf_op jit(solution)/shard_map/ppermute | solution.py:60
  37.6 4.9 %collective-permute-start.18 = (f32[1,64,256]{2,1,0:T(8,128)S(1)}, f32[1,64,256]{2,1,0:T(8,128)S(1)}, u32[]{:S(2)}, u32[]{:S(2)}) collective-permute-start(f32[1,64,256]{2,1,0:T(8,128)S(1)} %get-tuple-element.41), channel_id=1, source_target_pairs={{16,0},{20,4},{24,8},{28,12},{0,16},{4,20},{8,24},{12,28},{17,1},{... | collective-permute-start | bytes 196616 | tf_op jit(solution)/shard_map/ppermute | solution.py:54
  39.1 4.6 %collective-permute-start.16 = (f32[64,256]{1,0:T(8,128)S(1)}, f32[64,256]{1,0:T(8,128)S(1)}, u32[]{:S(2)}, u32[]{:S(2)}) collective-permute-start(f32[64,256]{1,0:T(8,128)S(1)} %get-tuple-element.36), channel_id=1, source_target_pairs={{0,1},{1,0},{2,3},{3,2},{4,5},{5,4},{6,7},{7,6},{8,9},{9,8},{10,11... | collective-permute-start | bytes 196616 | tf_op jit(solution)/shard_map/ppermute | solution.py:60
  44.3 7.0 %collective-permute-start.21 = (f32[112,256]{1,0:T(8,128)S(1)}, f32[112,256]{1,0:T(8,128)S(1)}, u32[]{:S(2)}, u32[]{:S(2)}) collective-permute-start(f32[112,256]{1,0:T(8,128)S(1)} %shard_map.91.refs_0_), channel_id=1, source_target_pairs={{24,0},{28,4},{16,8},{20,12},{8,16},{12,20},{0,24},{4,28},{25,1},{... | collective-permute-start | bytes 344072 | tf_op jit(solution)/shard_map/ppermute | solution.py:54
  45.7 6.8 %collective-permute-start.20 = (f32[112,256]{1,0:T(8,128)S(1)}, f32[112,256]{1,0:T(8,128)S(1)}, u32[]{:S(2)}, u32[]{:S(2)}) collective-permute-start(f32[112,256]{1,0:T(8,128)S(1)} %shard_map.91.refs_0_), channel_id=1, source_target_pairs={{16,0},{20,4},{24,8},{28,12},{0,16},{4,20},{8,24},{12,28},{17,1},{... | collective-permute-start | bytes 344072 | tf_op jit(solution)/shard_map/ppermute | solution.py:54
  46.5 6.0 %collective-permute-start.19 = (f32[112,256]{1,0:T(8,128)S(1)}, f32[112,256]{1,0:T(8,128)S(1)}, u32[]{:S(2)}, u32[]{:S(2)}) collective-permute-start(f32[112,256]{1,0:T(8,128)S(1)} %shard_map.91.refs_0_), channel_id=1, source_target_pairs={{8,0},{12,4},{0,8},{4,12},{24,16},{28,20},{16,24},{20,28},{9,1},{1... | collective-permute-start | bytes 344072 | tf_op jit(solution)/shard_map/ppermute | solution.py:54
  52.6 1.9 %collective-permute-start.22 = (f32[4,112,256]{2,1,0:T(8,128)S(1)}, f32[4,112,256]{2,1,0:T(8,128)S(1)}, u32[]{:S(2)}, u32[]{:S(2)}) collective-permute-start(f32[4,112,256]{2,1,0:T(8,128)S(1)} %shard_map.92.refs_0_.refs_1_), channel_id=1, source_target_pairs={{4,0},{0,4},{12,8},{8,12},{20,16},{16,20},{28,24},{24,28},{5,1},{1... | collective-permute-start | bytes 1376264 | tf_op jit(solution)/shard_map/ppermute | solution.py:54
  55.0 7.4 %collective-permute-start.23 = (f32[88,256]{1,0:T(8,128)S(1)}, f32[88,256]{1,0:T(8,128)S(1)}, u32[]{:S(2)}, u32[]{:S(2)}) collective-permute-start(f32[88,256]{1,0:T(8,128)S(1)} %get-tuple-element.43), channel_id=1, source_target_pairs={{0,3},{1,2},{2,1},{3,0},{4,7},{5,6},{6,5},{7,4},{8,11},{9,10},{10,... | collective-permute-start | bytes 270344 | tf_op jit(solution)/shard_map/ppermute | solution.py:60
  57.1 8.2 %collective-permute-start.24 = (f32[88,256]{1,0:T(8,128)S(1)}, f32[88,256]{1,0:T(8,128)S(1)}, u32[]{:S(2)}, u32[]{:S(2)}) collective-permute-start(f32[88,256]{1,0:T(8,128)S(1)} %get-tuple-element.44), channel_id=1, source_target_pairs={{0,2},{1,3},{2,0},{3,1},{4,6},{5,7},{6,4},{7,5},{8,10},{9,11},{10,... | collective-permute-start | bytes 270344 | tf_op jit(solution)/shard_map/ppermute | solution.py:60
  57.6 7.7 %collective-permute-start.25 = (f32[88,256]{1,0:T(8,128)S(1)}, f32[88,256]{1,0:T(8,128)S(1)}, u32[]{:S(2)}, u32[]{:S(2)}) collective-permute-start(f32[88,256]{1,0:T(8,128)S(1)} %get-tuple-element.45), channel_id=1, source_target_pairs={{0,1},{1,0},{2,3},{3,2},{4,5},{5,4},{6,7},{7,6},{8,9},{9,8},{10,11... | collective-permute-start | bytes 270344 | tf_op jit(solution)/shard_map/ppermute | solution.py:60
  65.4 1.3 %collective-permute-start.26 = (f32[24,256]{1,0:T(8,128)S(1)}, f32[24,256]{1,0:T(8,128)S(1)}, u32[]{:S(2)}, u32[]{:S(2)}) collective-permute-start(f32[24,256]{1,0:T(8,128)S(1)} %slice_add_fusion.3.refs_0_), channel_id=1, source_target_pairs={{4,0},{0,4},{12,8},{8,12},{20,16},{16,20},{28,24},{24,28},{5,1},{1... | collective-permute-start | bytes 73736 | tf_op jit(solution)/shard_map/ppermute | solution.py:54

commit v11 on v9

--- a/solution.py
+++ b/solution.py
@@ -56,9 +56,10 @@
 
 def scatter_pieces(pieces, axis):
     size = lax.axis_size(axis)
+    order = sorted(range(1, size), key=lambda shift: (shift < size // 2, shift))
     came = [
         lax.ppermute(pieces[shift], axis, [(i, partner(i, shift, size)) for i in range(size)])
-        for shift in reversed(range(1, size))
+        for shift in order
     ]
     return [pieces[0]] + came
 

time: 68 us -> 68.5 us (level)
  waiting for transfers between devices: 20.8 us -> 24.1 us
  starting transfers between devices: 32.2 us -> 29.5 us
    ppermute x9, waiting for transfers between devices: 10.4 us -> 13.8 us  [scatter_pieces(): lax.ppermute(pieces[shift], axis, [(i, partner(i, shift, size)) for i in...]
    ppermute x9, starting transfers between devices: 13.4 us -> 10.7 us  [scatter_pieces(): lax.ppermute(pieces[shift], axis, [(i, partner(i, shift, size)) for i in...]
  transfers between devices with their start and end apart: 27 -> 27, of which waited for: 14 -> 16; matrix products, arithmetic and copies ran while one was open for 1% -> 1% of each run, Pallas kernels for 14% -> 14%
where the time goes in v11:
time: 68.5 us; the launch traced here: 68.4 us
  starting transfers between devices  29.5 us (43%)
  waiting for transfers between devices  24.1 us (35%)
  Pallas kernels  12.6 us (18%)
  between operations  1.49 us (2%)
    ppermute x18, starting transfers between devices, fetch(): lax.ppermute(piece, axis, [(partner(i, shift, size), i) for i in range(si...  18.9 us
    ppermute x9, waiting for transfers between devices, scatter_pieces(): lax.ppermute(pieces[shift], axis, [(i, partner(i, shift, size)) for i in...  13.8 us
    ppermute x9, starting transfers between devices, scatter_pieces(): lax.ppermute(pieces[shift], axis, [(i, partner(i, shift, size)) for i in...  10.7 us
    ppermute x18, waiting for transfers between devices, fetch(): lax.ppermute(piece, axis, [(partner(i, shift, size), i) for i in range(si...  10.2 us
    pallas_call x16, Pallas kernels, call(): pl.pallas_call(body, in_specs=[vmem] * len(operands) + [pl.BlockSpec(memo...  9.1 us
    pallas_call x1, Pallas kernels, build_dense(): pl.pallas_call(functools.partial(build_kernel, (*sizes, group)), in_specs...  3.5 us
  transfers between devices with their start and end apart: 27, of which 16 were waited for; matrix products, arithmetic and copies ran while one was open for 1% of the time, Pallas kernels for 14%

profile of v11, /device:TPU:0, one launch (start us, length us, event | category | flops | bytes accessed | tf_op | source)
XLA Modules:
  0.0 68.4 jit_solution(3978309738141192638)
XLA Ops:
  0.6 4.1 %collective-permute-start.3 = (f32[64,256]{1,0:T(8,128)}, f32[64,256]{1,0:T(8,128)S(1)}, u32[]{:S(2)}, u32[]{:S(2)}) collective-permute-start(f32[64,256]{1,0:T(8,128)} %refs_4_.1), channel_id=1, source_target_pairs={{2,0},{3,1},{0,2},{1,3},{6,4},{7,5},{4,6},{5,7},{10,8},{11,9},{8,1... | collective-permute-start | bytes 196616 | tf_op jit(solution)/shard_map/ppermute | solution.py:54
  4.7 1.5 %collective-permute-start = (f32[64,256]{1,0:T(8,128)}, f32[64,256]{1,0:T(8,128)S(1)}, u32[]{:S(2)}, u32[]{:S(2)}) collective-permute-start(f32[64,256]{1,0:T(8,128)} %refs_5_.1), channel_id=1, source_target_pairs={{8,0},{12,4},{0,8},{4,12},{24,16},{28,20},{16,24},{20,28},{9,1},{1... | collective-permute-start | bytes 196616 | tf_op jit(solution)/shard_map/ppermute | solution.py:54
  6.2 1.5 %collective-permute-start.2 = (f32[64,256]{1,0:T(8,128)}, f32[64,256]{1,0:T(8,128)S(1)}, u32[]{:S(2)}, u32[]{:S(2)}) collective-permute-start(f32[64,256]{1,0:T(8,128)} %refs_5_.1), channel_id=1, source_target_pairs={{24,0},{28,4},{16,8},{20,12},{8,16},{12,20},{0,24},{4,28},{25,1},{... | collective-permute-start | bytes 196616 | tf_op jit(solution)/shard_map/ppermute | solution.py:54
  7.7 0.5 collective-permute-start.1
  8.9 3.5 %shard_map.77 = (bf16[8,2048,256]{2,1,0:T(8,128)(2,1)S(1)}, f32[64,256]{1,0:T(8,128)S(1)}, f32[64,256]{1,0:T(8,128)S(1)}, f32[8,128]{1,0:T(8,128)S(1)}) custom-call(s32[1,1,64]{2,1,0:T(1,128)} %refs_0_.1, s32[1,1,64]{2,1,0:T(1,128)} %refs_1_.1, s32[1,1]{1,0:T(1,128)S(6)} %copy.8.refs_2_, f32[1,1,64,128,128]{4,3,2,1,0:T(8,128)} %refs_3_.1, ...), custom_call_target="tpu_custom_call" | custom-call | flops 8388608 | bytes 8388608 | tf_op jit(solution)/shard_map/pallas_call | solution.py:202
  12.6 1.6 %collective-permute-start.8 = (f32[2,64,256]{2,1,0:T(8,128)S(1)}, f32[2,64,256]{2,1,0:T(8,128)S(1)}, u32[]{:S(2)}, u32[]{:S(2)}) collective-permute-start(f32[2,64,256]{2,1,0:T(8,128)S(1)} %shard_map.80.refs_4_.refs_0_), channel_id=1, source_target_pairs={{1,0},{0,1},{3,2},{2,3},{5,4},{4,5},{7,6},{6,7},{9,8},{8,9},{11,10... | collective-permute-start | bytes 393224 | tf_op jit(solution)/shard_map/ppermute | solution.py:54
  14.2 0.7 %shard_map.79.refs_2_ = f32[3,64,1024]{2,1,0:T(8,128)S(1)} custom-call(f32[4,64,256]{2,1,0:T(8,128)S(1)} %shard_map.78.refs_0_.refs_1_, bf16[8,2048,256]{2,1,0:T(8,128)(2,1)S(1)} %get-tuple-element.26.refs_1_.refs_3_.refs_2_), custom_call_target="tpu_custom_call" | custom-call | flops 536870912 | tf_op jit(solution)/shard_map/pallas_call | solution.py:72
  15.0 0.8 %shard_map.81 = (f32[64,256]{1,0:T(8,128)S(1)}, f32[64,256]{1,0:T(8,128)S(1)}, f32[64,256]{1,0:T(8,128)S(1)}, f32[64,256]{1,0:T(8,128)S(1)}) custom-call(f32[4,64,256]{2,1,0:T(8,128)S(1)} %collective-permute-done.4.refs_0_, f32[4,64,256]{2,1,0:T(8,128)S(1)} %shard_map.78.refs_0_.refs_1_, f32[3,64,1024]{2,1,0:T(8,128)S(1)} %shard_map.79.refs_2_, ...), custom_call_target="tpu_custom_call" | custom-call | flops 536870912 | tf_op jit(solution)/shard_map/pallas_call | solution.py:72
  15.8 0.4 collective-permute-start.5
  16.2 2.7 %collective-permute-start.6 = (f32[64,256]{1,0:T(8,128)S(1)}, f32[64,256]{1,0:T(8,128)S(1)}, u32[]{:S(2)}, u32[]{:S(2)}) collective-permute-start(f32[64,256]{1,0:T(8,128)S(1)} %get-tuple-element.30), channel_id=1, source_target_pairs={{0,3},{1,2},{2,1},{3,0},{4,7},{5,6},{6,5},{7,4},{8,11},{9,10},{10,... | collective-permute-start | bytes 196616 | tf_op jit(solution)/shard_map/ppermute | solution.py:61
  18.9 0.5 collective-permute-start.7
  19.3 2.4 %shard_map.82 = (f32[4,64,256]{2,1,0:T(8,128)S(1)}, f32[4,64,256]{2,1,0:T(8,128)S(1)}) custom-call(f32[2,64,256]{2,1,0:T(8,128)S(1)} %shard_map.80.refs_4_.refs_0_, f32[2,64,256]{2,1,0:T(8,128)S(1)} %collective-permute-done.8.refs_1_, bf16[8,2048,256]{2,1,0:T(8,128)(2,1)S(1)} %get-tuple-element.26.refs_1_.refs_3_.refs_2_, ...), custom_call_target="tpu_custom_call" | custom-call | flops 1073741824 | tf_op jit(solution)/shard_map/pallas_call | solution.py:72
  21.8 2.1 %collective-permute-done.5.refs_1_ = f32[64,256]{1,0:T(8,128)S(1)} collective-permute-done((f32[64,256]{1,0:T(8,128)S(1)}, f32[64,256]{1,0:T(8,128)S(1)}, u32[]{:S(2)}, u32[]{:S(2)}) %collective-permute-start.5) | collective-permute-done | bytes 65568 | tf_op jit(solution)/shard_map/ppermute | solution.py:61
  23.9 0.9 %collective-permute-done.7.refs_3_ = f32[64,256]{1,0:T(8,128)S(1)} collective-permute-done((f32[64,256]{1,0:T(8,128)S(1)}, f32[64,256]{1,0:T(8,128)S(1)}, u32[]{:S(2)}, u32[]{:S(2)}) %collective-permute-start.7) | collective-permute-done | bytes 65568 | tf_op jit(solution)/shard_map/ppermute | solution.py:61
  24.8 2.5 %collective-permute-start.11 = (f32[64,256]{1,0:T(8,128)S(1)}, f32[64,256]{1,0:T(8,128)S(1)}, u32[]{:S(2)}, u32[]{:S(2)}) collective-permute-start(f32[64,256]{1,0:T(8,128)S(1)} %shard_map.83.refs_0_.refs_5_), channel_id=1, source_target_pairs={{24,0},{28,4},{16,8},{20,12},{8,16},{12,20},{0,24},{4,28},{25,1},{... | collective-permute-start | bytes 196616 | tf_op jit(solution)/shard_map/ppermute | solution.py:54
  27.4 0.5 collective-permute-start.10
  27.9 0.5 collective-permute-start.9
  28.4 1.8 %collective-permute-done.11.refs_3_ = f32[64,256]{1,0:T(8,128)S(1)} collective-permute-done((f32[64,256]{1,0:T(8,128)S(1)}, f32[64,256]{1,0:T(8,128)S(1)}, u32[]{:S(2)}, u32[]{:S(2)}) %collective-permute-start.11) | collective-permute-done | bytes 65568 | tf_op jit(solution)/shard_map/ppermute | solution.py:54
  30.2 1.4 %collective-permute-done.10.refs_2_ = f32[64,256]{1,0:T(8,128)S(1)} collective-permute-done((f32[64,256]{1,0:T(8,128)S(1)}, f32[64,256]{1,0:T(8,128)S(1)}, u32[]{:S(2)}, u32[]{:S(2)}) %collective-permute-start.10) | collective-permute-done | bytes 65568 | tf_op jit(solution)/shard_map/ppermute | solution.py:54
  31.6 0.5 collective-permute-done.9.refs_1_
  32.3 0.6 collective-permute-start.17
  32.9 0.7 %shard_map.85.refs_2_ = f32[3,64,1024]{2,1,0:T(8,128)S(1)} custom-call(f32[4,64,256]{2,1,0:T(8,128)S(1)} %shard_map.84.refs_0_.refs_1_, bf16[8,2048,256]{2,1,0:T(8,128)(2,1)S(1)} %get-tuple-element.26.refs_1_.refs_3_.refs_2_), custom_call_target="tpu_custom_call" | custom-call | flops 536870912 | tf_op jit(solution)/shard_map/pallas_call | solution.py:72
  33.6 0.1 collective-permute-done.12.refs_0_
  33.8 0.8 %shard_map.86 = (f32[64,256]{1,0:T(8,128)S(1)}, f32[64,256]{1,0:T(8,128)S(1)}, f32[64,256]{1,0:T(8,128)S(1)}, f32[64,256]{1,0:T(8,128)S(1)}) custom-call(f32[4,64,256]{2,1,0:T(8,128)S(1)} %collective-permute-done.12.refs_0_, f32[4,64,256]{2,1,0:T(8,128)S(1)} %shard_map.84.refs_0_.refs_1_, f32[3,64,1024]{2,1,0:T(8,128)S(1)} %shard_map.85.refs_2_, ...), custom_call_target="tpu_custom_call" | custom-call | flops 536870912 | tf_op jit(solution)/shard_map/pallas_call | solution.py:72
  34.6 0.4 collective-permute-start.14
  34.9 3.0 %collective-permute-start.15 = (f32[64,256]{1,0:T(8,128)S(1)}, f32[64,256]{1,0:T(8,128)S(1)}, u32[]{:S(2)}, u32[]{:S(2)}) collective-permute-start(f32[64,256]{1,0:T(8,128)S(1)} %get-tuple-element.35), channel_id=1, source_target_pairs={{0,3},{1,2},{2,1},{3,0},{4,7},{5,6},{6,5},{7,4},{8,11},{9,10},{10,... | collective-permute-start | bytes 196616 | tf_op jit(solution)/shard_map/ppermute | solution.py:61
  37.9 0.2 collective-permute-start.16
  38.3 1.6 %collective-permute-start.18 = (f32[1,64,256]{2,1,0:T(8,128)S(1)}, f32[1,64,256]{2,1,0:T(8,128)S(1)}, u32[]{:S(2)}, u32[]{:S(2)}) collective-permute-start(f32[1,64,256]{2,1,0:T(8,128)S(1)} %get-tuple-element.41), channel_id=1, source_target_pairs={{16,0},{20,4},{24,8},{28,12},{0,16},{4,20},{8,24},{12,28},{17,1},{... | collective-permute-start | bytes 196616 | tf_op jit(solution)/shard_map/ppermute | solution.py:54
  39.8 3.1 %collective-permute-done.14.refs_1_ = f32[64,256]{1,0:T(8,128)S(1)} collective-permute-done((f32[64,256]{1,0:T(8,128)S(1)}, f32[64,256]{1,0:T(8,128)S(1)}, u32[]{:S(2)}, u32[]{:S(2)}) %collective-permute-start.14) | collective-permute-done | bytes 65568 | tf_op jit(solution)/shard_map/ppermute | solution.py:61
  43.0 0.5 collective-permute-done.16.refs_3_
  43.5 0.5 shard_map.89.refs_0_
  44.0 2.5 %collective-permute-start.21 = (f32[112,256]{1,0:T(8,128)S(1)}, f32[112,256]{1,0:T(8,128)S(1)}, u32[]{:S(2)}, u32[]{:S(2)}) collective-permute-start(f32[112,256]{1,0:T(8,128)S(1)} %shard_map.89.refs_0_), channel_id=1, source_target_pairs={{24,0},{28,4},{16,8},{20,12},{8,16},{12,20},{0,24},{4,28},{25,1},{... | collective-permute-start | bytes 344072 | tf_op jit(solution)/shard_map/ppermute | solution.py:54
  46.4 0.5 collective-permute-start.20
  47.0 0.6 collective-permute-start.19
  47.5 2.5 %collective-permute-done.21.refs_3_ = f32[112,256]{1,0:T(8,128)S(1)} collective-permute-done((f32[112,256]{1,0:T(8,128)S(1)}, f32[112,256]{1,0:T(8,128)S(1)}, u32[]{:S(2)}, u32[]{:S(2)}) %collective-permute-start.21) | collective-permute-done | bytes 114720 | tf_op jit(solution)/shard_map/ppermute | solution.py:54
  50.0 2.1 %collective-permute-done.20.refs_2_ = f32[112,256]{1,0:T(8,128)S(1)} collective-permute-done((f32[112,256]{1,0:T(8,128)S(1)}, f32[112,256]{1,0:T(8,128)S(1)}, u32[]{:S(2)}, u32[]{:S(2)}) %collective-permute-start.20) | collective-permute-done | bytes 114720 | tf_op jit(solution)/shard_map/ppermute | solution.py:54
  52.0 0.2 collective-permute-done.19.refs_1_
  52.3 0.7 %shard_map.91.refs_2_ = f32[3,64,1024]{2,1,0:T(8,128)S(1)} custom-call(f32[4,112,256]{2,1,0:T(8,128)S(1)} %shard_map.90.refs_0_.refs_1_, bf16[8,2048,256]{2,1,0:T(8,128)(2,1)S(1)} %get-tuple-element.26.refs_1_.refs_3_.refs_2_), custom_call_target="tpu_custom_call" | custom-call | flops 536870912 | tf_op jit(solution)/shard_map/pallas_call | solution.py:72
  53.1 1.0 %collective-permute-done.22.refs_0_ = f32[4,112,256]{2,1,0:T(8,128)S(1)} collective-permute-done((f32[4,112,256]{2,1,0:T(8,128)S(1)}, f32[4,112,256]{2,1,0:T(8,128)S(1)}, u32[]{:S(2)}, u32[]{:S(2)}) %collective-permute-start.22) | collective-permute-done | bytes 458784 | tf_op jit(solution)/shard_map/ppermute | solution.py:54
  54.1 0.8 %shard_map.92 = (f32[88,256]{1,0:T(8,128)S(1)}, f32[88,256]{1,0:T(8,128)S(1)}, f32[88,256]{1,0:T(8,128)S(1)}, f32[88,256]{1,0:T(8,128)S(1)}) custom-call(f32[4,112,256]{2,1,0:T(8,128)S(1)} %collective-permute-done.22.refs_0_, f32[4,112,256]{2,1,0:T(8,128)S(1)} %shard_map.90.refs_0_.refs_1_, f32[3,64,1024]{2,1,0:T(8,128)S(1)} %shard_map.91.refs_2_, ...), custom_call_target="tpu_custom_call" | custom-call | flops 536870912 | tf_op jit(solution)/shard_map/pallas_call | solution.py:72
  54.9 0.2 collective-permute-start.23
  55.1 3.2 %collective-permute-start.24 = (f32[88,256]{1,0:T(8,128)S(1)}, f32[88,256]{1,0:T(8,128)S(1)}, u32[]{:S(2)}, u32[]{:S(2)}) collective-permute-start(f32[88,256]{1,0:T(8,128)S(1)} %get-tuple-element.44), channel_id=1, source_target_pairs={{0,3},{1,2},{2,1},{3,0},{4,7},{5,6},{6,5},{7,4},{8,11},{9,10},{10,... | collective-permute-start | bytes 270344 | tf_op jit(solution)/shard_map/ppermute | solution.py:61
  58.4 0.1 collective-permute-start.25
  58.5 6.5 %collective-permute-done.23 = f32[88,256]{1,0:T(8,128)S(1)} collective-permute-done((f32[88,256]{1,0:T(8,128)S(1)}, f32[88,256]{1,0:T(8,128)S(1)}, u32[]{:S(2)}, u32[]{:S(2)}) %collective-permute-start.23) | collective-permute-done | bytes 90144 | tf_op jit(solution)/shard_map/ppermute | solution.py:61
  65.0 0.7 %collective-permute-done.25 = f32[88,256]{1,0:T(8,128)S(1)} collective-permute-done((f32[88,256]{1,0:T(8,128)S(1)}, f32[88,256]{1,0:T(8,128)S(1)}, u32[]{:S(2)}, u32[]{:S(2)}) %collective-permute-start.25) | collective-permute-done | bytes 90144 | tf_op jit(solution)/shard_map/ppermute | solution.py:61
  65.7 0.7 fusion
  66.4 0.5 collective-permute-done.26.refs_1_
  66.9 1.4 %shard_map.93 = f32[3,64,64]{2,1,0:T(8,128)} custom-call(f32[24,256]{1,0:T(8,128)S(1)} %slice_add_fusion.3.refs_0_, f32[24,256]{1,0:T(8,128)S(1)} %collective-permute-done.26.refs_1_), custom_call_target="tpu_custom_call" | custom-call | tf_op jit(solution)/shard_map/pallas_call | solution.py:72
  (25 shorter events, 0.7 us)
Async XLA Ops:
  0.6 11.8 %collective-permute-start.3 = (f32[64,256]{1,0:T(8,128)}, f32[64,256]{1,0:T(8,128)S(1)}, u32[]{:S(2)}, u32[]{:S(2)}) collective-permute-start(f32[64,256]{1,0:T(8,128)} %refs_4_.1), channel_id=1, source_target_pairs={{2,0},{3,1},{0,2},{1,3},{6,4},{7,5},{4,6},{5,7},{10,8},{11,9},{8,1... | collective-permute-start | bytes 196616 | tf_op jit(solution)/shard_map/ppermute | solution.py:54
  4.7 7.7 %collective-permute-start = (f32[64,256]{1,0:T(8,128)}, f32[64,256]{1,0:T(8,128)S(1)}, u32[]{:S(2)}, u32[]{:S(2)}) collective-permute-start(f32[64,256]{1,0:T(8,128)} %refs_5_.1), channel_id=1, source_target_pairs={{8,0},{12,4},{0,8},{4,12},{24,16},{28,20},{16,24},{20,28},{9,1},{1... | collective-permute-start | bytes 196616 | tf_op jit(solution)/shard_map/ppermute | solution.py:54
  6.2 6.2 %collective-permute-start.2 = (f32[64,256]{1,0:T(8,128)}, f32[64,256]{1,0:T(8,128)S(1)}, u32[]{:S(2)}, u32[]{:S(2)}) collective-permute-start(f32[64,256]{1,0:T(8,128)} %refs_5_.1), channel_id=1, source_target_pairs={{24,0},{28,4},{16,8},{20,12},{8,16},{12,20},{0,24},{4,28},{25,1},{... | collective-permute-start | bytes 196616 | tf_op jit(solution)/shard_map/ppermute | solution.py:54
  7.7 4.7 %collective-permute-start.1 = (f32[64,256]{1,0:T(8,128)}, f32[64,256]{1,0:T(8,128)S(1)}, u32[]{:S(2)}, u32[]{:S(2)}) collective-permute-start(f32[64,256]{1,0:T(8,128)} %refs_5_.1), channel_id=1, source_target_pairs={{16,0},{20,4},{24,8},{28,12},{0,16},{4,20},{8,24},{12,28},{17,1},{... | collective-permute-start | bytes 196616 | tf_op jit(solution)/shard_map/ppermute | solution.py:54
  12.5 2.5 %collective-permute-start.4 = (f32[4,64,256]{2,1,0:T(8,128)S(1)}, f32[4,64,256]{2,1,0:T(8,128)S(1)}, u32[]{:S(2)}, u32[]{:S(2)}) collective-permute-start(f32[4,64,256]{2,1,0:T(8,128)S(1)} %shard_map.78.refs_0_.refs_1_), channel_id=1, source_target_pairs={{4,0},{0,4},{12,8},{8,12},{20,16},{16,20},{28,24},{24,28},{5,1},{1... | collective-permute-start | bytes 786440 | tf_op jit(solution)/shard_map/ppermute | solution.py:54
  12.6 6.8 %collective-permute-start.8 = (f32[2,64,256]{2,1,0:T(8,128)S(1)}, f32[2,64,256]{2,1,0:T(8,128)S(1)}, u32[]{:S(2)}, u32[]{:S(2)}) collective-permute-start(f32[2,64,256]{2,1,0:T(8,128)S(1)} %shard_map.80.refs_4_.refs_0_), channel_id=1, source_target_pairs={{1,0},{0,1},{3,2},{2,3},{5,4},{4,5},{7,6},{6,7},{9,8},{8,9},{11,10... | collective-permute-start | bytes 393224 | tf_op jit(solution)/shard_map/ppermute | solution.py:54
  15.8 8.2 %collective-permute-start.5 = (f32[64,256]{1,0:T(8,128)S(1)}, f32[64,256]{1,0:T(8,128)S(1)}, u32[]{:S(2)}, u32[]{:S(2)}) collective-permute-start(f32[64,256]{1,0:T(8,128)S(1)} %get-tuple-element.29), channel_id=1, source_target_pairs={{0,2},{1,3},{2,0},{3,1},{4,6},{5,7},{6,4},{7,5},{8,10},{9,11},{10,... | collective-permute-start | bytes 196616 | tf_op jit(solution)/shard_map/ppermute | solution.py:61
  16.2 7.8 %collective-permute-start.6 = (f32[64,256]{1,0:T(8,128)S(1)}, f32[64,256]{1,0:T(8,128)S(1)}, u32[]{:S(2)}, u32[]{:S(2)}) collective-permute-start(f32[64,256]{1,0:T(8,128)S(1)} %get-tuple-element.30), channel_id=1, source_target_pairs={{0,3},{1,2},{2,1},{3,0},{4,7},{5,6},{6,5},{7,4},{8,11},{9,10},{10,... | collective-permute-start | bytes 196616 | tf_op jit(solution)/shard_map/ppermute | solution.py:61
  18.9 6.0 %collective-permute-start.7 = (f32[64,256]{1,0:T(8,128)S(1)}, f32[64,256]{1,0:T(8,128)S(1)}, u32[]{:S(2)}, u32[]{:S(2)}) collective-permute-start(f32[64,256]{1,0:T(8,128)S(1)} %get-tuple-element.31), channel_id=1, source_target_pairs={{0,1},{1,0},{2,3},{3,2},{4,5},{5,4},{6,7},{7,6},{8,9},{9,8},{10,11... | collective-permute-start | bytes 196616 | tf_op jit(solution)/shard_map/ppermute | solution.py:61
  21.7 10.5 %collective-permute-start.13 = (f32[4,64,256]{2,1,0:T(8,128)S(1)}, f32[4,64,256]{2,1,0:T(8,128)S(1)}, u32[]{:S(2)}, u32[]{:S(2)}) collective-permute-start(f32[4,64,256]{2,1,0:T(8,128)S(1)} %get-tuple-element.32.refs_4_), channel_id=1, source_target_pairs={{4,0},{0,4},{12,8},{8,12},{20,16},{16,20},{28,24},{24,28},{5,1},{1... | collective-permute-start | bytes 786440 | tf_op jit(solution)/shard_map/ppermute | solution.py:54
  24.8 5.3 %collective-permute-start.11 = (f32[64,256]{1,0:T(8,128)S(1)}, f32[64,256]{1,0:T(8,128)S(1)}, u32[]{:S(2)}, u32[]{:S(2)}) collective-permute-start(f32[64,256]{1,0:T(8,128)S(1)} %shard_map.83.refs_0_.refs_5_), channel_id=1, source_target_pairs={{24,0},{28,4},{16,8},{20,12},{8,16},{12,20},{0,24},{4,28},{25,1},{... | collective-permute-start | bytes 196616 | tf_op jit(solution)/shard_map/ppermute | solution.py:54
  27.4 4.3 %collective-permute-start.10 = (f32[64,256]{1,0:T(8,128)S(1)}, f32[64,256]{1,0:T(8,128)S(1)}, u32[]{:S(2)}, u32[]{:S(2)}) collective-permute-start(f32[64,256]{1,0:T(8,128)S(1)} %shard_map.83.refs_0_.refs_5_), channel_id=1, source_target_pairs={{16,0},{20,4},{24,8},{28,12},{0,16},{4,20},{8,24},{12,28},{17,1},{... | collective-permute-start | bytes 196616 | tf_op jit(solution)/shard_map/ppermute | solution.py:54
  27.9 4.3 %collective-permute-start.9 = (f32[64,256]{1,0:T(8,128)S(1)}, f32[64,256]{1,0:T(8,128)S(1)}, u32[]{:S(2)}, u32[]{:S(2)}) collective-permute-start(f32[64,256]{1,0:T(8,128)S(1)} %shard_map.83.refs_0_.refs_5_), channel_id=1, source_target_pairs={{8,0},{12,4},{0,8},{4,12},{24,16},{28,20},{16,24},{20,28},{9,1},{1... | collective-permute-start | bytes 196616 | tf_op jit(solution)/shard_map/ppermute | solution.py:54
  32.2 1.6 %collective-permute-start.12 = (f32[4,64,256]{2,1,0:T(8,128)S(1)}, f32[4,64,256]{2,1,0:T(8,128)S(1)}, u32[]{:S(2)}, u32[]{:S(2)}) collective-permute-start(f32[4,64,256]{2,1,0:T(8,128)S(1)} %shard_map.84.refs_0_.refs_1_), channel_id=1, source_target_pairs={{4,0},{0,4},{12,8},{8,12},{20,16},{16,20},{28,24},{24,28},{5,1},{1... | collective-permute-start | bytes 786440 | tf_op jit(solution)/shard_map/ppermute | solution.py:54
  32.3 6.0 %collective-permute-start.17 = (f32[2,64,256]{2,1,0:T(8,128)S(1)}, f32[2,64,256]{2,1,0:T(8,128)S(1)}, u32[]{:S(2)}, u32[]{:S(2)}) collective-permute-start(f32[2,64,256]{2,1,0:T(8,128)S(1)} %get-tuple-element.39), channel_id=1, source_target_pairs={{8,0},{12,4},{0,8},{4,12},{24,16},{28,20},{16,24},{20,28},{9,1},{1... | collective-permute-start | bytes 393224 | tf_op jit(solution)/shard_map/ppermute | solution.py:54
  34.6 8.4 %collective-permute-start.14 = (f32[64,256]{1,0:T(8,128)S(1)}, f32[64,256]{1,0:T(8,128)S(1)}, u32[]{:S(2)}, u32[]{:S(2)}) collective-permute-start(f32[64,256]{1,0:T(8,128)S(1)} %get-tuple-element.34), channel_id=1, source_target_pairs={{0,2},{1,3},{2,0},{3,1},{4,6},{5,7},{6,4},{7,5},{8,10},{9,11},{10,... | collective-permute-start | bytes 196616 | tf_op jit(solution)/shard_map/ppermute | solution.py:61
  34.9 8.0 %collective-permute-start.15 = (f32[64,256]{1,0:T(8,128)S(1)}, f32[64,256]{1,0:T(8,128)S(1)}, u32[]{:S(2)}, u32[]{:S(2)}) collective-permute-start(f32[64,256]{1,0:T(8,128)S(1)} %get-tuple-element.35), channel_id=1, source_target_pairs={{0,3},{1,2},{2,1},{3,0},{4,7},{5,6},{6,5},{7,4},{8,11},{9,10},{10,... | collective-permute-start | bytes 196616 | tf_op jit(solution)/shard_map/ppermute | solution.py:61
  37.9 5.5 %collective-permute-start.16 = (f32[64,256]{1,0:T(8,128)S(1)}, f32[64,256]{1,0:T(8,128)S(1)}, u32[]{:S(2)}, u32[]{:S(2)}) collective-permute-start(f32[64,256]{1,0:T(8,128)S(1)} %get-tuple-element.36), channel_id=1, source_target_pairs={{0,1},{1,0},{2,3},{3,2},{4,5},{5,4},{6,7},{7,6},{8,9},{9,8},{10,11... | collective-permute-start | bytes 196616 | tf_op jit(solution)/shard_map/ppermute | solution.py:61
  38.3 5.2 %collective-permute-start.18 = (f32[1,64,256]{2,1,0:T(8,128)S(1)}, f32[1,64,256]{2,1,0:T(8,128)S(1)}, u32[]{:S(2)}, u32[]{:S(2)}) collective-permute-start(f32[1,64,256]{2,1,0:T(8,128)S(1)} %get-tuple-element.41), channel_id=1, source_target_pairs={{16,0},{20,4},{24,8},{28,12},{0,16},{4,20},{8,24},{12,28},{17,1},{... | collective-permute-start | bytes 196616 | tf_op jit(solution)/shard_map/ppermute | solution.py:54
  44.0 6.0 %collective-permute-start.21 = (f32[112,256]{1,0:T(8,128)S(1)}, f32[112,256]{1,0:T(8,128)S(1)}, u32[]{:S(2)}, u32[]{:S(2)}) collective-permute-start(f32[112,256]{1,0:T(8,128)S(1)} %shard_map.89.refs_0_), channel_id=1, source_target_pairs={{24,0},{28,4},{16,8},{20,12},{8,16},{12,20},{0,24},{4,28},{25,1},{... | collective-permute-start | bytes 344072 | tf_op jit(solution)/shard_map/ppermute | solution.py:54
  46.4 5.6 %collective-permute-start.20 = (f32[112,256]{1,0:T(8,128)S(1)}, f32[112,256]{1,0:T(8,128)S(1)}, u32[]{:S(2)}, u32[]{:S(2)}) collective-permute-start(f32[112,256]{1,0:T(8,128)S(1)} %shard_map.89.refs_0_), channel_id=1, source_target_pairs={{16,0},{20,4},{24,8},{28,12},{0,16},{4,20},{8,24},{12,28},{17,1},{... | collective-permute-start | bytes 344072 | tf_op jit(solution)/shard_map/ppermute | solution.py:54
  47.0 5.2 %collective-permute-start.19 = (f32[112,256]{1,0:T(8,128)S(1)}, f32[112,256]{1,0:T(8,128)S(1)}, u32[]{:S(2)}, u32[]{:S(2)}) collective-permute-start(f32[112,256]{1,0:T(8,128)S(1)} %shard_map.89.refs_0_), channel_id=1, source_target_pairs={{8,0},{12,4},{0,8},{4,12},{24,16},{28,20},{16,24},{20,28},{9,1},{1... | collective-permute-start | bytes 344072 | tf_op jit(solution)/shard_map/ppermute | solution.py:54
  52.2 1.9 %collective-permute-start.22 = (f32[4,112,256]{2,1,0:T(8,128)S(1)}, f32[4,112,256]{2,1,0:T(8,128)S(1)}, u32[]{:S(2)}, u32[]{:S(2)}) collective-permute-start(f32[4,112,256]{2,1,0:T(8,128)S(1)} %shard_map.90.refs_0_.refs_1_), channel_id=1, source_target_pairs={{4,0},{0,4},{12,8},{8,12},{20,16},{16,20},{28,24},{24,28},{5,1},{1... | collective-permute-start | bytes 1376264 | tf_op jit(solution)/shard_map/ppermute | solution.py:54
  54.9 10.0 %collective-permute-start.23 = (f32[88,256]{1,0:T(8,128)S(1)}, f32[88,256]{1,0:T(8,128)S(1)}, u32[]{:S(2)}, u32[]{:S(2)}) collective-permute-start(f32[88,256]{1,0:T(8,128)S(1)} %get-tuple-element.43), channel_id=1, source_target_pairs={{0,2},{1,3},{2,0},{3,1},{4,6},{5,7},{6,4},{7,5},{8,10},{9,11},{10,... | collective-permute-start | bytes 270344 | tf_op jit(solution)/shard_map/ppermute | solution.py:61
  55.1 9.8 %collective-permute-start.24 = (f32[88,256]{1,0:T(8,128)S(1)}, f32[88,256]{1,0:T(8,128)S(1)}, u32[]{:S(2)}, u32[]{:S(2)}) collective-permute-start(f32[88,256]{1,0:T(8,128)S(1)} %get-tuple-element.44), channel_id=1, source_target_pairs={{0,3},{1,2},{2,1},{3,0},{4,7},{5,6},{6,5},{7,4},{8,11},{9,10},{10,... | collective-permute-start | bytes 270344 | tf_op jit(solution)/shard_map/ppermute | solution.py:61
  58.4 7.3 %collective-permute-start.25 = (f32[88,256]{1,0:T(8,128)S(1)}, f32[88,256]{1,0:T(8,128)S(1)}, u32[]{:S(2)}, u32[]{:S(2)}) collective-permute-start(f32[88,256]{1,0:T(8,128)S(1)} %get-tuple-element.45), channel_id=1, source_target_pairs={{0,1},{1,0},{2,3},{3,2},{4,5},{5,4},{6,7},{7,6},{8,9},{9,8},{10,11... | collective-permute-start | bytes 270344 | tf_op jit(solution)/shard_map/ppermute | solution.py:61
  65.7 1.3 %collective-permute-start.26 = (f32[24,256]{1,0:T(8,128)S(1)}, f32[24,256]{1,0:T(8,128)S(1)}, u32[]{:S(2)}, u32[]{:S(2)}) collective-permute-start(f32[24,256]{1,0:T(8,128)S(1)} %slice_add_fusion.3.refs_0_), channel_id=1, source_target_pairs={{4,0},{0,4},{12,8},{8,12},{20,16},{16,20},{28,24},{24,28},{5,1},{1... | collective-permute-start | bytes 73736 | tf_op jit(solution)/shard_map/ppermute | solution.py:54

commit v12 on v9

--- a/solution.py
+++ b/solution.py
@@ -150,8 +150,15 @@
     ]
     for copy in small[:3]:
         copy.start()
+    for copy in small[:3]:
+        copy.wait()
+    used_count = (count_ref[0, 0] + group - 1) // group
     for index in range(chunk_count):
-        chunk(index).start()
+
+        @pl.when(index < used_count)
+        def _():
+            chunk(index).start(priority=index % 2)
+
     for copy in small[3:]:
         copy.start()
 
@@ -160,8 +167,6 @@
         return carry
 
     lax.fori_loop(0, dense_ref.shape[0], clear, 0)
-    for copy in small[:3]:
-        copy.wait()
 
     def place(slot):
         row, col = rows_ref[0, 0, slot], cols_ref[0, 0, slot]
@@ -181,7 +186,7 @@
             place(index * group + offset)
         return carry
 
-    lax.fori_loop(0, chunk_count, step, 0)
+    lax.fori_loop(0, used_count, step, 0)
     for copy in small[3:]:
         copy.wait()
     token_ref[...] = jnp.zeros_like(token_ref)
@@ -191,7 +196,7 @@
     tile_rows, tile_cols, tile_count, tile_entries = tiles
     n_row, n_col, piece_blocks = sizes
     _, _, slot_count, tile_len, _ = tile_entries.shape
-    group = next(size for size in (8, 4, 2, 1) if slot_count % size == 0)
+    group = next(size for size in (4, 2, 1) if slot_count % size == 0)
     shape = (n_col * piece_blocks, n_row * piece_blocks * tile_len, 2 * tile_len)
     hbm = pl.BlockSpec(memory_space=pltpu.HBM)
     rows, cols, entries, x_piece, y_piece = (

time: 68 us -> 69.1 us (1.016)
  transfers between devices with their start and end apart: 27 -> 27, of which waited for: 14 -> 12; matrix products, arithmetic and copies ran while one was open for 1% -> 1% of each run, Pallas kernels for 14% -> 15%
where the time goes in v12:
time: 69.1 us; the launch traced here: 69 us
  starting transfers between devices  32.8 us (47%)
  waiting for transfers between devices  21 us (30%)
  Pallas kernels  13.1 us (19%)
  between operations  1.5 us (2%)
    ppermute x18, starting transfers between devices, fetch(): lax.ppermute(piece, axis, [(partner(i, shift, size), i) for i in range(si...  19.5 us
    ppermute x9, starting transfers between devices, scatter_pieces(): lax.ppermute(pieces[shift], axis, [(i, partner(i, shift, size)) for i in...  13.4 us
    ppermute x18, waiting for transfers between devices, fetch(): lax.ppermute(piece, axis, [(partner(i, shift, size), i) for i in range(si...  10.6 us
    ppermute x9, waiting for transfers between devices, scatter_pieces(): lax.ppermute(pieces[shift], axis, [(i, partner(i, shift, size)) for i in...  10.3 us
    pallas_call x16, Pallas kernels, call(): pl.pallas_call(body, in_specs=[vmem] * len(operands) + [pl.BlockSpec(memo...  9.11 us
    pallas_call x1, Pallas kernels, build_dense(): pl.pallas_call(functools.partial(build_kernel, (*sizes, group)), in_specs...  3.97 us
  transfers between devices with their start and end apart: 27, of which 12 were waited for; matrix products, arithmetic and copies ran while one was open for 1% of the time, Pallas kernels for 15%

profile of v12, /device:TPU:0, one launch (start us, length us, event | category | flops | bytes accessed | tf_op | source)
XLA Modules:
  0.0 69.0 jit_solution(14957086790212784430)
XLA Ops:
  0.6 4.1 %collective-permute-start.3 = (f32[64,256]{1,0:T(8,128)}, f32[64,256]{1,0:T(8,128)S(1)}, u32[]{:S(2)}, u32[]{:S(2)}) collective-permute-start(f32[64,256]{1,0:T(8,128)} %refs_4_.1), channel_id=1, source_target_pairs={{2,0},{3,1},{0,2},{1,3},{6,4},{7,5},{4,6},{5,7},{10,8},{11,9},{8,1... | collective-permute-start | bytes 196616 | tf_op jit(solution)/shard_map/ppermute | solution.py:54
  4.7 1.5 %collective-permute-start = (f32[64,256]{1,0:T(8,128)}, f32[64,256]{1,0:T(8,128)S(1)}, u32[]{:S(2)}, u32[]{:S(2)}) collective-permute-start(f32[64,256]{1,0:T(8,128)} %refs_5_.1), channel_id=1, source_target_pairs={{8,0},{12,4},{0,8},{4,12},{24,16},{28,20},{16,24},{20,28},{9,1},{1... | collective-permute-start | bytes 196616 | tf_op jit(solution)/shard_map/ppermute | solution.py:54
  6.2 1.5 %collective-permute-start.2 = (f32[64,256]{1,0:T(8,128)}, f32[64,256]{1,0:T(8,128)S(1)}, u32[]{:S(2)}, u32[]{:S(2)}) collective-permute-start(f32[64,256]{1,0:T(8,128)} %refs_5_.1), channel_id=1, source_target_pairs={{24,0},{28,4},{16,8},{20,12},{8,16},{12,20},{0,24},{4,28},{25,1},{... | collective-permute-start | bytes 196616 | tf_op jit(solution)/shard_map/ppermute | solution.py:54
  7.7 0.5 collective-permute-start.1
  8.9 4.0 %shard_map.77 = (bf16[8,2048,256]{2,1,0:T(8,128)(2,1)S(1)}, f32[64,256]{1,0:T(8,128)S(1)}, f32[64,256]{1,0:T(8,128)S(1)}, f32[8,128]{1,0:T(8,128)S(1)}) custom-call(s32[1,1,64]{2,1,0:T(1,128)} %refs_0_.1, s32[1,1,64]{2,1,0:T(1,128)} %refs_1_.1, s32[1,1]{1,0:T(1,128)S(6)} %copy.8.refs_2_, f32[1,1,64,128,128]{4,3,2,1,0:T(8,128)} %refs_3_.1, ...), custom_call_target="tpu_custom_call" | custom-call | flops 8388608 | bytes 8388608 | tf_op jit(solution)/shard_map/pallas_call | solution.py:206
  12.9 0.0 collective-permute-done.3.refs_5_.refs_1_
  12.9 0.1 collective-permute-start.4
  13.0 1.0 %collective-permute-start.8 = (f32[2,64,256]{2,1,0:T(8,128)S(1)}, f32[2,64,256]{2,1,0:T(8,128)S(1)}, u32[]{:S(2)}, u32[]{:S(2)}) collective-permute-start(f32[2,64,256]{2,1,0:T(8,128)S(1)} %shard_map.80.refs_4_.refs_0_), channel_id=1, source_target_pairs={{1,0},{0,1},{3,2},{2,3},{5,4},{4,5},{7,6},{6,7},{9,8},{8,9},{11,10... | collective-permute-start | bytes 393224 | tf_op jit(solution)/shard_map/ppermute | solution.py:54
  14.1 0.7 %shard_map.79.refs_2_ = f32[3,64,1024]{2,1,0:T(8,128)S(1)} custom-call(f32[4,64,256]{2,1,0:T(8,128)S(1)} %shard_map.78.refs_0_.refs_1_, bf16[8,2048,256]{2,1,0:T(8,128)(2,1)S(1)} %get-tuple-element.26.refs_1_.refs_3_.refs_2_), custom_call_target="tpu_custom_call" | custom-call | flops 536870912 | tf_op jit(solution)/shard_map/pallas_call | solution.py:71
  14.8 0.8 %shard_map.81 = (f32[64,256]{1,0:T(8,128)S(1)}, f32[64,256]{1,0:T(8,128)S(1)}, f32[64,256]{1,0:T(8,128)S(1)}, f32[64,256]{1,0:T(8,128)S(1)}) custom-call(f32[4,64,256]{2,1,0:T(8,128)S(1)} %collective-permute-done.4.refs_0_, f32[4,64,256]{2,1,0:T(8,128)S(1)} %shard_map.78.refs_0_.refs_1_, f32[3,64,1024]{2,1,0:T(8,128)S(1)} %shard_map.79.refs_2_, ...), custom_call_target="tpu_custom_call" | custom-call | flops 536870912 | tf_op jit(solution)/shard_map/pallas_call | solution.py:71
  15.6 0.5 collective-permute-start.5
  16.1 2.1 %collective-permute-start.6 = (f32[64,256]{1,0:T(8,128)S(1)}, f32[64,256]{1,0:T(8,128)S(1)}, u32[]{:S(2)}, u32[]{:S(2)}) collective-permute-start(f32[64,256]{1,0:T(8,128)S(1)} %get-tuple-element.30), channel_id=1, source_target_pairs={{0,2},{1,3},{2,0},{3,1},{4,6},{5,7},{6,4},{7,5},{8,10},{9,11},{10,... | collective-permute-start | bytes 196616 | tf_op jit(solution)/shard_map/ppermute | solution.py:60
  18.2 1.9 %collective-permute-start.7 = (f32[64,256]{1,0:T(8,128)S(1)}, f32[64,256]{1,0:T(8,128)S(1)}, u32[]{:S(2)}, u32[]{:S(2)}) collective-permute-start(f32[64,256]{1,0:T(8,128)S(1)} %get-tuple-element.31), channel_id=1, source_target_pairs={{0,1},{1,0},{2,3},{3,2},{4,5},{5,4},{6,7},{7,6},{8,9},{9,8},{10,11... | collective-permute-start | bytes 196616 | tf_op jit(solution)/shard_map/ppermute | solution.py:60
  20.1 2.4 %shard_map.82 = (f32[4,64,256]{2,1,0:T(8,128)S(1)}, f32[4,64,256]{2,1,0:T(8,128)S(1)}) custom-call(f32[2,64,256]{2,1,0:T(8,128)S(1)} %shard_map.80.refs_4_.refs_0_, f32[2,64,256]{2,1,0:T(8,128)S(1)} %collective-permute-done.8.refs_1_, bf16[8,2048,256]{2,1,0:T(8,128)(2,1)S(1)} %get-tuple-element.26.refs_1_.refs_3_.refs_2_, ...), custom_call_target="tpu_custom_call" | custom-call | flops 1073741824 | tf_op jit(solution)/shard_map/pallas_call | solution.py:71
  22.5 0.1 collective-permute-start.13
  22.6 2.0 %collective-permute-done.6.refs_2_ = f32[64,256]{1,0:T(8,128)S(1)} collective-permute-done((f32[64,256]{1,0:T(8,128)S(1)}, f32[64,256]{1,0:T(8,128)S(1)}, u32[]{:S(2)}, u32[]{:S(2)}) %collective-permute-start.6) | collective-permute-done | bytes 65568 | tf_op jit(solution)/shard_map/ppermute | solution.py:60
  24.6 3.5 %collective-permute-start.11 = (f32[64,256]{1,0:T(8,128)S(1)}, f32[64,256]{1,0:T(8,128)S(1)}, u32[]{:S(2)}, u32[]{:S(2)}) collective-permute-start(f32[64,256]{1,0:T(8,128)S(1)} %shard_map.83.refs_0_.refs_5_), channel_id=1, source_target_pairs={{24,0},{28,4},{16,8},{20,12},{8,16},{12,20},{0,24},{4,28},{25,1},{... | collective-permute-start | bytes 196616 | tf_op jit(solution)/shard_map/ppermute | solution.py:54
  28.1 0.6 collective-permute-start.9
  28.8 1.7 %collective-permute-done.11.refs_3_ = f32[64,256]{1,0:T(8,128)S(1)} collective-permute-done((f32[64,256]{1,0:T(8,128)S(1)}, f32[64,256]{1,0:T(8,128)S(1)}, u32[]{:S(2)}, u32[]{:S(2)}) %collective-permute-start.11) | collective-permute-done | bytes 65568 | tf_op jit(solution)/shard_map/ppermute | solution.py:54
  30.5 1.9 %collective-permute-done.10.refs_2_ = f32[64,256]{1,0:T(8,128)S(1)} collective-permute-done((f32[64,256]{1,0:T(8,128)S(1)}, f32[64,256]{1,0:T(8,128)S(1)}, u32[]{:S(2)}, u32[]{:S(2)}) %collective-permute-start.10) | collective-permute-done | bytes 65568 | tf_op jit(solution)/shard_map/ppermute | solution.py:54
  32.4 0.1 collective-permute-start.12
  32.5 0.8 %collective-permute-start.17 = (f32[2,64,256]{2,1,0:T(8,128)S(1)}, f32[2,64,256]{2,1,0:T(8,128)S(1)}, u32[]{:S(2)}, u32[]{:S(2)}) collective-permute-start(f32[2,64,256]{2,1,0:T(8,128)S(1)} %get-tuple-element.39), channel_id=1, source_target_pairs={{8,0},{12,4},{0,8},{4,12},{24,16},{28,20},{16,24},{20,28},{9,1},{1... | collective-permute-start | bytes 393224 | tf_op jit(solution)/shard_map/ppermute | solution.py:54
  33.3 0.8 %shard_map.85.refs_2_ = f32[3,64,1024]{2,1,0:T(8,128)S(1)} custom-call(f32[4,64,256]{2,1,0:T(8,128)S(1)} %shard_map.84.refs_0_.refs_1_, bf16[8,2048,256]{2,1,0:T(8,128)(2,1)S(1)} %get-tuple-element.26.refs_1_.refs_3_.refs_2_), custom_call_target="tpu_custom_call" | custom-call | flops 536870912 | tf_op jit(solution)/shard_map/pallas_call | solution.py:71
  34.1 0.8 %shard_map.86 = (f32[64,256]{1,0:T(8,128)S(1)}, f32[64,256]{1,0:T(8,128)S(1)}, f32[64,256]{1,0:T(8,128)S(1)}, f32[64,256]{1,0:T(8,128)S(1)}) custom-call(f32[4,64,256]{2,1,0:T(8,128)S(1)} %collective-permute-done.12.refs_0_, f32[4,64,256]{2,1,0:T(8,128)S(1)} %shard_map.84.refs_0_.refs_1_, f32[3,64,1024]{2,1,0:T(8,128)S(1)} %shard_map.85.refs_2_, ...), custom_call_target="tpu_custom_call" | custom-call | flops 536870912 | tf_op jit(solution)/shard_map/pallas_call | solution.py:71
  34.9 1.4 %collective-permute-start.14 = (f32[64,256]{1,0:T(8,128)S(1)}, f32[64,256]{1,0:T(8,128)S(1)}, u32[]{:S(2)}, u32[]{:S(2)}) collective-permute-start(f32[64,256]{1,0:T(8,128)S(1)} %get-tuple-element.34), channel_id=1, source_target_pairs={{0,3},{1,2},{2,1},{3,0},{4,7},{5,6},{6,5},{7,4},{8,11},{9,10},{10,... | collective-permute-start | bytes 196616 | tf_op jit(solution)/shard_map/ppermute | solution.py:60
  36.3 3.1 %collective-permute-start.16 = (f32[64,256]{1,0:T(8,128)S(1)}, f32[64,256]{1,0:T(8,128)S(1)}, u32[]{:S(2)}, u32[]{:S(2)}) collective-permute-start(f32[64,256]{1,0:T(8,128)S(1)} %get-tuple-element.36), channel_id=1, source_target_pairs={{0,1},{1,0},{2,3},{3,2},{4,5},{5,4},{6,7},{7,6},{8,9},{9,8},{10,11... | collective-permute-start | bytes 196616 | tf_op jit(solution)/shard_map/ppermute | solution.py:60
  39.4 2.0 %collective-permute-start.18 = (f32[1,64,256]{2,1,0:T(8,128)S(1)}, f32[1,64,256]{2,1,0:T(8,128)S(1)}, u32[]{:S(2)}, u32[]{:S(2)}) collective-permute-start(f32[1,64,256]{2,1,0:T(8,128)S(1)} %get-tuple-element.41), channel_id=1, source_target_pairs={{16,0},{20,4},{24,8},{28,12},{0,16},{4,20},{8,24},{12,28},{17,1},{... | collective-permute-start | bytes 196616 | tf_op jit(solution)/shard_map/ppermute | solution.py:54
  41.4 0.4 collective-permute-done.14.refs_1_
  41.7 2.0 %collective-permute-done.15.refs_2_ = f32[64,256]{1,0:T(8,128)S(1)} collective-permute-done((f32[64,256]{1,0:T(8,128)S(1)}, f32[64,256]{1,0:T(8,128)S(1)}, u32[]{:S(2)}, u32[]{:S(2)}) %collective-permute-start.15) | collective-permute-done | bytes 65568 | tf_op jit(solution)/shard_map/ppermute | solution.py:60
  43.8 0.5 shard_map.89.refs_0_
  44.2 2.8 %collective-permute-start.21 = (f32[112,256]{1,0:T(8,128)S(1)}, f32[112,256]{1,0:T(8,128)S(1)}, u32[]{:S(2)}, u32[]{:S(2)}) collective-permute-start(f32[112,256]{1,0:T(8,128)S(1)} %shard_map.89.refs_0_), channel_id=1, source_target_pairs={{24,0},{28,4},{16,8},{20,12},{8,16},{12,20},{0,24},{4,28},{25,1},{... | collective-permute-start | bytes 344072 | tf_op jit(solution)/shard_map/ppermute | solution.py:54
  47.1 0.0 collective-permute-start.20
  47.1 0.7 %collective-permute-start.19 = (f32[112,256]{1,0:T(8,128)S(1)}, f32[112,256]{1,0:T(8,128)S(1)}, u32[]{:S(2)}, u32[]{:S(2)}) collective-permute-start(f32[112,256]{1,0:T(8,128)S(1)} %shard_map.89.refs_0_), channel_id=1, source_target_pairs={{8,0},{12,4},{0,8},{4,12},{24,16},{28,20},{16,24},{20,28},{9,1},{1... | collective-permute-start | bytes 344072 | tf_op jit(solution)/shard_map/ppermute | solution.py:54
  47.8 2.9 %collective-permute-done.21.refs_3_ = f32[112,256]{1,0:T(8,128)S(1)} collective-permute-done((f32[112,256]{1,0:T(8,128)S(1)}, f32[112,256]{1,0:T(8,128)S(1)}, u32[]{:S(2)}, u32[]{:S(2)}) %collective-permute-start.21) | collective-permute-done | bytes 114720 | tf_op jit(solution)/shard_map/ppermute | solution.py:54
  50.7 2.2 %collective-permute-done.20.refs_2_ = f32[112,256]{1,0:T(8,128)S(1)} collective-permute-done((f32[112,256]{1,0:T(8,128)S(1)}, f32[112,256]{1,0:T(8,128)S(1)}, u32[]{:S(2)}, u32[]{:S(2)}) %collective-permute-start.20) | collective-permute-done | bytes 114720 | tf_op jit(solution)/shard_map/ppermute | solution.py:54
  52.9 0.3 collective-permute-done.19.refs_1_
  53.2 0.1 collective-permute-start.22
  53.3 0.8 %shard_map.91.refs_2_ = f32[3,64,1024]{2,1,0:T(8,128)S(1)} custom-call(f32[4,112,256]{2,1,0:T(8,128)S(1)} %shard_map.90.refs_0_.refs_1_, bf16[8,2048,256]{2,1,0:T(8,128)(2,1)S(1)} %get-tuple-element.26.refs_1_.refs_3_.refs_2_), custom_call_target="tpu_custom_call" | custom-call | flops 536870912 | tf_op jit(solution)/shard_map/pallas_call | solution.py:71
  54.1 1.0 %collective-permute-done.22.refs_0_ = f32[4,112,256]{2,1,0:T(8,128)S(1)} collective-permute-done((f32[4,112,256]{2,1,0:T(8,128)S(1)}, f32[4,112,256]{2,1,0:T(8,128)S(1)}, u32[]{:S(2)}, u32[]{:S(2)}) %collective-permute-start.22) | collective-permute-done | bytes 458784 | tf_op jit(solution)/shard_map/ppermute | solution.py:54
  55.1 0.8 %shard_map.92 = (f32[88,256]{1,0:T(8,128)S(1)}, f32[88,256]{1,0:T(8,128)S(1)}, f32[88,256]{1,0:T(8,128)S(1)}, f32[88,256]{1,0:T(8,128)S(1)}) custom-call(f32[4,112,256]{2,1,0:T(8,128)S(1)} %collective-permute-done.22.refs_0_, f32[4,112,256]{2,1,0:T(8,128)S(1)} %shard_map.90.refs_0_.refs_1_, f32[3,64,1024]{2,1,0:T(8,128)S(1)} %shard_map.91.refs_2_, ...), custom_call_target="tpu_custom_call" | custom-call | flops 536870912 | tf_op jit(solution)/shard_map/pallas_call | solution.py:71
  55.9 1.2 %collective-permute-start.23 = (f32[88,256]{1,0:T(8,128)S(1)}, f32[88,256]{1,0:T(8,128)S(1)}, u32[]{:S(2)}, u32[]{:S(2)}) collective-permute-start(f32[88,256]{1,0:T(8,128)S(1)} %get-tuple-element.43), channel_id=1, source_target_pairs={{0,3},{1,2},{2,1},{3,0},{4,7},{5,6},{6,5},{7,4},{8,11},{9,10},{10,... | collective-permute-start | bytes 270344 | tf_op jit(solution)/shard_map/ppermute | solution.py:60
  57.2 3.2 %collective-permute-start.25 = (f32[88,256]{1,0:T(8,128)S(1)}, f32[88,256]{1,0:T(8,128)S(1)}, u32[]{:S(2)}, u32[]{:S(2)}) collective-permute-start(f32[88,256]{1,0:T(8,128)S(1)} %get-tuple-element.45), channel_id=1, source_target_pairs={{0,1},{1,0},{2,3},{3,2},{4,5},{5,4},{6,7},{7,6},{8,9},{9,8},{10,11... | collective-permute-start | bytes 270344 | tf_op jit(solution)/shard_map/ppermute | solution.py:60
  60.4 3.0 %collective-permute-done.23 = f32[88,256]{1,0:T(8,128)S(1)} collective-permute-done((f32[88,256]{1,0:T(8,128)S(1)}, f32[88,256]{1,0:T(8,128)S(1)}, u32[]{:S(2)}, u32[]{:S(2)}) %collective-permute-start.23) | collective-permute-done | bytes 90144 | tf_op jit(solution)/shard_map/ppermute | solution.py:60
  63.4 3.0 %collective-permute-done.24 = f32[88,256]{1,0:T(8,128)S(1)} collective-permute-done((f32[88,256]{1,0:T(8,128)S(1)}, f32[88,256]{1,0:T(8,128)S(1)}, u32[]{:S(2)}, u32[]{:S(2)}) %collective-permute-start.24) | collective-permute-done | bytes 90144 | tf_op jit(solution)/shard_map/ppermute | solution.py:60
  66.3 0.1 collective-permute-start.26
  66.4 0.7 fusion
  67.1 0.5 collective-permute-done.26.refs_1_
  67.6 1.4 %shard_map.93 = f32[3,64,64]{2,1,0:T(8,128)} custom-call(f32[24,256]{1,0:T(8,128)S(1)} %slice_add_fusion.3.refs_0_, f32[24,256]{1,0:T(8,128)S(1)} %collective-permute-done.26.refs_1_), custom_call_target="tpu_custom_call" | custom-call | tf_op jit(solution)/shard_map/pallas_call | solution.py:71
  (25 shorter events, 0.2 us)
Async XLA Ops:
  0.6 12.2 %collective-permute-start.3 = (f32[64,256]{1,0:T(8,128)}, f32[64,256]{1,0:T(8,128)S(1)}, u32[]{:S(2)}, u32[]{:S(2)}) collective-permute-start(f32[64,256]{1,0:T(8,128)} %refs_4_.1), channel_id=1, source_target_pairs={{2,0},{3,1},{0,2},{1,3},{6,4},{7,5},{4,6},{5,7},{10,8},{11,9},{8,1... | collective-permute-start | bytes 196616 | tf_op jit(solution)/shard_map/ppermute | solution.py:54
  4.7 8.1 %collective-permute-start = (f32[64,256]{1,0:T(8,128)}, f32[64,256]{1,0:T(8,128)S(1)}, u32[]{:S(2)}, u32[]{:S(2)}) collective-permute-start(f32[64,256]{1,0:T(8,128)} %refs_5_.1), channel_id=1, source_target_pairs={{8,0},{12,4},{0,8},{4,12},{24,16},{28,20},{16,24},{20,28},{9,1},{1... | collective-permute-start | bytes 196616 | tf_op jit(solution)/shard_map/ppermute | solution.py:54
  6.2 6.7 %collective-permute-start.2 = (f32[64,256]{1,0:T(8,128)}, f32[64,256]{1,0:T(8,128)S(1)}, u32[]{:S(2)}, u32[]{:S(2)}) collective-permute-start(f32[64,256]{1,0:T(8,128)} %refs_5_.1), channel_id=1, source_target_pairs={{24,0},{28,4},{16,8},{20,12},{8,16},{12,20},{0,24},{4,28},{25,1},{... | collective-permute-start | bytes 196616 | tf_op jit(solution)/shard_map/ppermute | solution.py:54
  7.7 5.2 %collective-permute-start.1 = (f32[64,256]{1,0:T(8,128)}, f32[64,256]{1,0:T(8,128)S(1)}, u32[]{:S(2)}, u32[]{:S(2)}) collective-permute-start(f32[64,256]{1,0:T(8,128)} %refs_5_.1), channel_id=1, source_target_pairs={{16,0},{20,4},{24,8},{28,12},{0,16},{4,20},{8,24},{12,28},{17,1},{... | collective-permute-start | bytes 196616 | tf_op jit(solution)/shard_map/ppermute | solution.py:54
  12.9 1.9 %collective-permute-start.4 = (f32[4,64,256]{2,1,0:T(8,128)S(1)}, f32[4,64,256]{2,1,0:T(8,128)S(1)}, u32[]{:S(2)}, u32[]{:S(2)}) collective-permute-start(f32[4,64,256]{2,1,0:T(8,128)S(1)} %shard_map.78.refs_0_.refs_1_), channel_id=1, source_target_pairs={{4,0},{0,4},{12,8},{8,12},{20,16},{16,20},{28,24},{24,28},{5,1},{1... | collective-permute-start | bytes 786440 | tf_op jit(solution)/shard_map/ppermute | solution.py:54
  13.0 7.1 %collective-permute-start.8 = (f32[2,64,256]{2,1,0:T(8,128)S(1)}, f32[2,64,256]{2,1,0:T(8,128)S(1)}, u32[]{:S(2)}, u32[]{:S(2)}) collective-permute-start(f32[2,64,256]{2,1,0:T(8,128)S(1)} %shard_map.80.refs_4_.refs_0_), channel_id=1, source_target_pairs={{1,0},{0,1},{3,2},{2,3},{5,4},{4,5},{7,6},{6,7},{9,8},{8,9},{11,10... | collective-permute-start | bytes 393224 | tf_op jit(solution)/shard_map/ppermute | solution.py:54
  15.6 6.9 %collective-permute-start.5 = (f32[64,256]{1,0:T(8,128)S(1)}, f32[64,256]{1,0:T(8,128)S(1)}, u32[]{:S(2)}, u32[]{:S(2)}) collective-permute-start(f32[64,256]{1,0:T(8,128)S(1)} %get-tuple-element.29), channel_id=1, source_target_pairs={{0,3},{1,2},{2,1},{3,0},{4,7},{5,6},{6,5},{7,4},{8,11},{9,10},{10,... | collective-permute-start | bytes 196616 | tf_op jit(solution)/shard_map/ppermute | solution.py:60
  16.1 8.5 %collective-permute-start.6 = (f32[64,256]{1,0:T(8,128)S(1)}, f32[64,256]{1,0:T(8,128)S(1)}, u32[]{:S(2)}, u32[]{:S(2)}) collective-permute-start(f32[64,256]{1,0:T(8,128)S(1)} %get-tuple-element.30), channel_id=1, source_target_pairs={{0,2},{1,3},{2,0},{3,1},{4,6},{5,7},{6,4},{7,5},{8,10},{9,11},{10,... | collective-permute-start | bytes 196616 | tf_op jit(solution)/shard_map/ppermute | solution.py:60
  18.2 6.4 %collective-permute-start.7 = (f32[64,256]{1,0:T(8,128)S(1)}, f32[64,256]{1,0:T(8,128)S(1)}, u32[]{:S(2)}, u32[]{:S(2)}) collective-permute-start(f32[64,256]{1,0:T(8,128)S(1)} %get-tuple-element.31), channel_id=1, source_target_pairs={{0,1},{1,0},{2,3},{3,2},{4,5},{5,4},{6,7},{7,6},{8,9},{9,8},{10,11... | collective-permute-start | bytes 196616 | tf_op jit(solution)/shard_map/ppermute | solution.py:60
  22.5 10.0 %collective-permute-start.13 = (f32[4,64,256]{2,1,0:T(8,128)S(1)}, f32[4,64,256]{2,1,0:T(8,128)S(1)}, u32[]{:S(2)}, u32[]{:S(2)}) collective-permute-start(f32[4,64,256]{2,1,0:T(8,128)S(1)} %get-tuple-element.32.refs_4_), channel_id=1, source_target_pairs={{4,0},{0,4},{12,8},{8,12},{20,16},{16,20},{28,24},{24,28},{5,1},{1... | collective-permute-start | bytes 786440 | tf_op jit(solution)/shard_map/ppermute | solution.py:54
  24.6 5.8 %collective-permute-start.11 = (f32[64,256]{1,0:T(8,128)S(1)}, f32[64,256]{1,0:T(8,128)S(1)}, u32[]{:S(2)}, u32[]{:S(2)}) collective-permute-start(f32[64,256]{1,0:T(8,128)S(1)} %shard_map.83.refs_0_.refs_5_), channel_id=1, source_target_pairs={{24,0},{28,4},{16,8},{20,12},{8,16},{12,20},{0,24},{4,28},{25,1},{... | collective-permute-start | bytes 196616 | tf_op jit(solution)/shard_map/ppermute | solution.py:54
  28.1 4.3 %collective-permute-start.10 = (f32[64,256]{1,0:T(8,128)S(1)}, f32[64,256]{1,0:T(8,128)S(1)}, u32[]{:S(2)}, u32[]{:S(2)}) collective-permute-start(f32[64,256]{1,0:T(8,128)S(1)} %shard_map.83.refs_0_.refs_5_), channel_id=1, source_target_pairs={{16,0},{20,4},{24,8},{28,12},{0,16},{4,20},{8,24},{12,28},{17,1},{... | collective-permute-start | bytes 196616 | tf_op jit(solution)/shard_map/ppermute | solution.py:54
  28.1 4.3 %collective-permute-start.9 = (f32[64,256]{1,0:T(8,128)S(1)}, f32[64,256]{1,0:T(8,128)S(1)}, u32[]{:S(2)}, u32[]{:S(2)}) collective-permute-start(f32[64,256]{1,0:T(8,128)S(1)} %shard_map.83.refs_0_.refs_5_), channel_id=1, source_target_pairs={{8,0},{12,4},{0,8},{4,12},{24,16},{28,20},{16,24},{20,28},{9,1},{1... | collective-permute-start | bytes 196616 | tf_op jit(solution)/shard_map/ppermute | solution.py:54
  32.4 1.7 %collective-permute-start.12 = (f32[4,64,256]{2,1,0:T(8,128)S(1)}, f32[4,64,256]{2,1,0:T(8,128)S(1)}, u32[]{:S(2)}, u32[]{:S(2)}) collective-permute-start(f32[4,64,256]{2,1,0:T(8,128)S(1)} %shard_map.84.refs_0_.refs_1_), channel_id=1, source_target_pairs={{4,0},{0,4},{12,8},{8,12},{20,16},{16,20},{28,24},{24,28},{5,1},{1... | collective-permute-start | bytes 786440 | tf_op jit(solution)/shard_map/ppermute | solution.py:54
  32.5 6.8 %collective-permute-start.17 = (f32[2,64,256]{2,1,0:T(8,128)S(1)}, f32[2,64,256]{2,1,0:T(8,128)S(1)}, u32[]{:S(2)}, u32[]{:S(2)}) collective-permute-start(f32[2,64,256]{2,1,0:T(8,128)S(1)} %get-tuple-element.39), channel_id=1, source_target_pairs={{8,0},{12,4},{0,8},{4,12},{24,16},{28,20},{16,24},{20,28},{9,1},{1... | collective-permute-start | bytes 393224 | tf_op jit(solution)/shard_map/ppermute | solution.py:54
  34.9 6.9 %collective-permute-start.14 = (f32[64,256]{1,0:T(8,128)S(1)}, f32[64,256]{1,0:T(8,128)S(1)}, u32[]{:S(2)}, u32[]{:S(2)}) collective-permute-start(f32[64,256]{1,0:T(8,128)S(1)} %get-tuple-element.34), channel_id=1, source_target_pairs={{0,3},{1,2},{2,1},{3,0},{4,7},{5,6},{6,5},{7,4},{8,11},{9,10},{10,... | collective-permute-start | bytes 196616 | tf_op jit(solution)/shard_map/ppermute | solution.py:60
  36.3 7.5 %collective-permute-start.15 = (f32[64,256]{1,0:T(8,128)S(1)}, f32[64,256]{1,0:T(8,128)S(1)}, u32[]{:S(2)}, u32[]{:S(2)}) collective-permute-start(f32[64,256]{1,0:T(8,128)S(1)} %get-tuple-element.35), channel_id=1, source_target_pairs={{0,2},{1,3},{2,0},{3,1},{4,6},{5,7},{6,4},{7,5},{8,10},{9,11},{10,... | collective-permute-start | bytes 196616 | tf_op jit(solution)/shard_map/ppermute | solution.py:60
  36.3 7.5 %collective-permute-start.16 = (f32[64,256]{1,0:T(8,128)S(1)}, f32[64,256]{1,0:T(8,128)S(1)}, u32[]{:S(2)}, u32[]{:S(2)}) collective-permute-start(f32[64,256]{1,0:T(8,128)S(1)} %get-tuple-element.36), channel_id=1, source_target_pairs={{0,1},{1,0},{2,3},{3,2},{4,5},{5,4},{6,7},{7,6},{8,9},{9,8},{10,11... | collective-permute-start | bytes 196616 | tf_op jit(solution)/shard_map/ppermute | solution.py:60
  39.4 4.4 %collective-permute-start.18 = (f32[1,64,256]{2,1,0:T(8,128)S(1)}, f32[1,64,256]{2,1,0:T(8,128)S(1)}, u32[]{:S(2)}, u32[]{:S(2)}) collective-permute-start(f32[1,64,256]{2,1,0:T(8,128)S(1)} %get-tuple-element.41), channel_id=1, source_target_pairs={{16,0},{20,4},{24,8},{28,12},{0,16},{4,20},{8,24},{12,28},{17,1},{... | collective-permute-start | bytes 196616 | tf_op jit(solution)/shard_map/ppermute | solution.py:54
  44.2 6.4 %collective-permute-start.21 = (f32[112,256]{1,0:T(8,128)S(1)}, f32[112,256]{1,0:T(8,128)S(1)}, u32[]{:S(2)}, u32[]{:S(2)}) collective-permute-start(f32[112,256]{1,0:T(8,128)S(1)} %shard_map.89.refs_0_), channel_id=1, source_target_pairs={{24,0},{28,4},{16,8},{20,12},{8,16},{12,20},{0,24},{4,28},{25,1},{... | collective-permute-start | bytes 344072 | tf_op jit(solution)/shard_map/ppermute | solution.py:54
  47.1 5.8 %collective-permute-start.20 = (f32[112,256]{1,0:T(8,128)S(1)}, f32[112,256]{1,0:T(8,128)S(1)}, u32[]{:S(2)}, u32[]{:S(2)}) collective-permute-start(f32[112,256]{1,0:T(8,128)S(1)} %shard_map.89.refs_0_), channel_id=1, source_target_pairs={{16,0},{20,4},{24,8},{28,12},{0,16},{4,20},{8,24},{12,28},{17,1},{... | collective-permute-start | bytes 344072 | tf_op jit(solution)/shard_map/ppermute | solution.py:54
  47.1 6.1 %collective-permute-start.19 = (f32[112,256]{1,0:T(8,128)S(1)}, f32[112,256]{1,0:T(8,128)S(1)}, u32[]{:S(2)}, u32[]{:S(2)}) collective-permute-start(f32[112,256]{1,0:T(8,128)S(1)} %shard_map.89.refs_0_), channel_id=1, source_target_pairs={{8,0},{12,4},{0,8},{4,12},{24,16},{28,20},{16,24},{20,28},{9,1},{1... | collective-permute-start | bytes 344072 | tf_op jit(solution)/shard_map/ppermute | solution.py:54
  53.2 1.9 %collective-permute-start.22 = (f32[4,112,256]{2,1,0:T(8,128)S(1)}, f32[4,112,256]{2,1,0:T(8,128)S(1)}, u32[]{:S(2)}, u32[]{:S(2)}) collective-permute-start(f32[4,112,256]{2,1,0:T(8,128)S(1)} %shard_map.90.refs_0_.refs_1_), channel_id=1, source_target_pairs={{4,0},{0,4},{12,8},{8,12},{20,16},{16,20},{28,24},{24,28},{5,1},{1... | collective-permute-start | bytes 1376264 | tf_op jit(solution)/shard_map/ppermute | solution.py:54
  55.9 7.4 %collective-permute-start.23 = (f32[88,256]{1,0:T(8,128)S(1)}, f32[88,256]{1,0:T(8,128)S(1)}, u32[]{:S(2)}, u32[]{:S(2)}) collective-permute-start(f32[88,256]{1,0:T(8,128)S(1)} %get-tuple-element.43), channel_id=1, source_target_pairs={{0,3},{1,2},{2,1},{3,0},{4,7},{5,6},{6,5},{7,4},{8,11},{9,10},{10,... | collective-permute-start | bytes 270344 | tf_op jit(solution)/shard_map/ppermute | solution.py:60
  57.2 9.1 %collective-permute-start.24 = (f32[88,256]{1,0:T(8,128)S(1)}, f32[88,256]{1,0:T(8,128)S(1)}, u32[]{:S(2)}, u32[]{:S(2)}) collective-permute-start(f32[88,256]{1,0:T(8,128)S(1)} %get-tuple-element.44), channel_id=1, source_target_pairs={{0,2},{1,3},{2,0},{3,1},{4,6},{5,7},{6,4},{7,5},{8,10},{9,11},{10,... | collective-permute-start | bytes 270344 | tf_op jit(solution)/shard_map/ppermute | solution.py:60
  57.2 9.1 %collective-permute-start.25 = (f32[88,256]{1,0:T(8,128)S(1)}, f32[88,256]{1,0:T(8,128)S(1)}, u32[]{:S(2)}, u32[]{:S(2)}) collective-permute-start(f32[88,256]{1,0:T(8,128)S(1)} %get-tuple-element.45), channel_id=1, source_target_pairs={{0,1},{1,0},{2,3},{3,2},{4,5},{5,4},{6,7},{7,6},{8,9},{9,8},{10,11... | collective-permute-start | bytes 270344 | tf_op jit(solution)/shard_map/ppermute | solution.py:60
  66.3 1.3 %collective-permute-start.26 = (f32[24,256]{1,0:T(8,128)S(1)}, f32[24,256]{1,0:T(8,128)S(1)}, u32[]{:S(2)}, u32[]{:S(2)}) collective-permute-start(f32[24,256]{1,0:T(8,128)S(1)} %slice_add_fusion.3.refs_0_), channel_id=1, source_target_pairs={{4,0},{0,4},{12,8},{8,12},{20,16},{16,20},{28,24},{24,28},{5,1},{1... | collective-permute-start | bytes 73736 | tf_op jit(solution)/shard_map/ppermute | solution.py:54

commit v13 on v12

--- a/solution.py
+++ b/solution.py
@@ -196,7 +196,7 @@
     tile_rows, tile_cols, tile_count, tile_entries = tiles
     n_row, n_col, piece_blocks = sizes
     _, _, slot_count, tile_len, _ = tile_entries.shape
-    group = next(size for size in (4, 2, 1) if slot_count % size == 0)
+    group = next(size for size in (16, 8, 4, 2, 1) if slot_count % size == 0)
     shape = (n_col * piece_blocks, n_row * piece_blocks * tile_len, 2 * tile_len)
     hbm = pl.BlockSpec(memory_space=pltpu.HBM)
     rows, cols, entries, x_piece, y_piece = (

time: 69.1 us -> 67.9 us (0.983)
  starting transfers between devices: 32.8 us -> 31.6 us
    ppermute x18, starting transfers between devices: 19.5 us -> 18.3 us  [fetch(): lax.ppermute(piece, axis, [(partner(i, shift, size), i) for i in range(si...]
    ppermute x9, waiting for transfers between devices: 10.3 us -> 11.1 us  [scatter_pieces(): lax.ppermute(pieces[shift], axis, [(i, partner(i, shift, size)) for i in...]
where the time goes in v13:
time: 67.9 us; the launch traced here: 67.7 us
  starting transfers between devices  31.6 us (47%)
  waiting for transfers between devices  21.1 us (31%)
  Pallas kernels  12.8 us (19%)
  between operations  1.5 us (2%)
  other arithmetic  0.68 us (1%)
    ppermute x18, starting transfers between devices, fetch(): lax.ppermute(piece, axis, [(partner(i, shift, size), i) for i in range(si...  18.3 us
    ppermute x9, starting transfers between devices, scatter_pieces(): lax.ppermute(pieces[shift], axis, [(i, partner(i, shift, size)) for i in...  13.4 us
    ppermute x9, waiting for transfers between devices, scatter_pieces(): lax.ppermute(pieces[shift], axis, [(i, partner(i, shift, size)) for i in...  11.1 us
    ppermute x18, waiting for transfers between devices, fetch(): lax.ppermute(piece, axis, [(partner(i, shift, size), i) for i in range(si...  10 us
    pallas_call x16, Pallas kernels, call(): pl.pallas_call(body, in_specs=[vmem] * len(operands) + [pl.BlockSpec(memo...  9.1 us
    pallas_call x1, Pallas kernels, build_dense(): pl.pallas_call(functools.partial(build_kernel, (*sizes, group)), in_specs...  3.71 us
  transfers between devices with their start and end apart: 27, of which 12 were waited for; matrix products, arithmetic and copies ran while one was open for 1% of the time, Pallas kernels for 15%

profile of v13, /device:TPU:0, one launch (start us, length us, event | category | flops | bytes accessed | tf_op | source)
XLA Modules:
  0.0 67.7 jit_solution(5390934549994251472)
XLA Ops:
  0.6 4.1 %collective-permute-start.3 = (f32[64,256]{1,0:T(8,128)}, f32[64,256]{1,0:T(8,128)S(1)}, u32[]{:S(2)}, u32[]{:S(2)}) collective-permute-start(f32[64,256]{1,0:T(8,128)} %refs_4_.1), channel_id=1, source_target_pairs={{2,0},{3,1},{0,2},{1,3},{6,4},{7,5},{4,6},{5,7},{10,8},{11,9},{8,1... | collective-permute-start | bytes 196616 | tf_op jit(solution)/shard_map/ppermute | solution.py:54
  4.7 1.5 %collective-permute-start = (f32[64,256]{1,0:T(8,128)}, f32[64,256]{1,0:T(8,128)S(1)}, u32[]{:S(2)}, u32[]{:S(2)}) collective-permute-start(f32[64,256]{1,0:T(8,128)} %refs_5_.1), channel_id=1, source_target_pairs={{8,0},{12,4},{0,8},{4,12},{24,16},{28,20},{16,24},{20,28},{9,1},{1... | collective-permute-start | bytes 196616 | tf_op jit(solution)/shard_map/ppermute | solution.py:54
  6.2 1.5 %collective-permute-start.2 = (f32[64,256]{1,0:T(8,128)}, f32[64,256]{1,0:T(8,128)S(1)}, u32[]{:S(2)}, u32[]{:S(2)}) collective-permute-start(f32[64,256]{1,0:T(8,128)} %refs_5_.1), channel_id=1, source_target_pairs={{24,0},{28,4},{16,8},{20,12},{8,16},{12,20},{0,24},{4,28},{25,1},{... | collective-permute-start | bytes 196616 | tf_op jit(solution)/shard_map/ppermute | solution.py:54
  7.7 0.5 collective-permute-start.1
  8.9 3.7 %shard_map.77 = (bf16[8,2048,256]{2,1,0:T(8,128)(2,1)S(1)}, f32[64,256]{1,0:T(8,128)S(1)}, f32[64,256]{1,0:T(8,128)S(1)}, f32[8,128]{1,0:T(8,128)S(1)}) custom-call(s32[1,1,64]{2,1,0:T(1,128)} %refs_0_.1, s32[1,1,64]{2,1,0:T(1,128)} %refs_1_.1, s32[1,1]{1,0:T(1,128)S(6)} %copy.8.refs_2_, f32[1,1,64,128,128]{4,3,2,1,0:T(8,128)} %refs_3_.1, ...), custom_call_target="tpu_custom_call" | custom-call | flops 8388608 | bytes 8388608 | tf_op jit(solution)/shard_map/pallas_call | solution.py:206
  12.7 0.1 collective-permute-start.4
  12.8 1.3 %collective-permute-start.8 = (f32[2,64,256]{2,1,0:T(8,128)S(1)}, f32[2,64,256]{2,1,0:T(8,128)S(1)}, u32[]{:S(2)}, u32[]{:S(2)}) collective-permute-start(f32[2,64,256]{2,1,0:T(8,128)S(1)} %shard_map.80.refs_4_.refs_0_), channel_id=1, source_target_pairs={{1,0},{0,1},{3,2},{2,3},{5,4},{4,5},{7,6},{6,7},{9,8},{8,9},{11,10... | collective-permute-start | bytes 393224 | tf_op jit(solution)/shard_map/ppermute | solution.py:54
  14.1 0.7 %shard_map.79.refs_2_ = f32[3,64,1024]{2,1,0:T(8,128)S(1)} custom-call(f32[4,64,256]{2,1,0:T(8,128)S(1)} %shard_map.78.refs_0_.refs_1_, bf16[8,2048,256]{2,1,0:T(8,128)(2,1)S(1)} %get-tuple-element.26.refs_1_.refs_3_.refs_2_), custom_call_target="tpu_custom_call" | custom-call | flops 536870912 | tf_op jit(solution)/shard_map/pallas_call | solution.py:71
  14.8 0.8 %shard_map.81 = (f32[64,256]{1,0:T(8,128)S(1)}, f32[64,256]{1,0:T(8,128)S(1)}, f32[64,256]{1,0:T(8,128)S(1)}, f32[64,256]{1,0:T(8,128)S(1)}) custom-call(f32[4,64,256]{2,1,0:T(8,128)S(1)} %collective-permute-done.4.refs_0_, f32[4,64,256]{2,1,0:T(8,128)S(1)} %shard_map.78.refs_0_.refs_1_, f32[3,64,1024]{2,1,0:T(8,128)S(1)} %shard_map.79.refs_2_, ...), custom_call_target="tpu_custom_call" | custom-call | flops 536870912 | tf_op jit(solution)/shard_map/pallas_call | solution.py:71
  15.6 0.5 collective-permute-start.5
  16.1 1.8 %collective-permute-start.6 = (f32[64,256]{1,0:T(8,128)S(1)}, f32[64,256]{1,0:T(8,128)S(1)}, u32[]{:S(2)}, u32[]{:S(2)}) collective-permute-start(f32[64,256]{1,0:T(8,128)S(1)} %get-tuple-element.30), channel_id=1, source_target_pairs={{0,2},{1,3},{2,0},{3,1},{4,6},{5,7},{6,4},{7,5},{8,10},{9,11},{10,... | collective-permute-start | bytes 196616 | tf_op jit(solution)/shard_map/ppermute | solution.py:60
  17.9 2.1 %collective-permute-start.7 = (f32[64,256]{1,0:T(8,128)S(1)}, f32[64,256]{1,0:T(8,128)S(1)}, u32[]{:S(2)}, u32[]{:S(2)}) collective-permute-start(f32[64,256]{1,0:T(8,128)S(1)} %get-tuple-element.31), channel_id=1, source_target_pairs={{0,1},{1,0},{2,3},{3,2},{4,5},{5,4},{6,7},{7,6},{8,9},{9,8},{10,11... | collective-permute-start | bytes 196616 | tf_op jit(solution)/shard_map/ppermute | solution.py:60
  20.1 2.4 %shard_map.82 = (f32[4,64,256]{2,1,0:T(8,128)S(1)}, f32[4,64,256]{2,1,0:T(8,128)S(1)}) custom-call(f32[2,64,256]{2,1,0:T(8,128)S(1)} %shard_map.80.refs_4_.refs_0_, f32[2,64,256]{2,1,0:T(8,128)S(1)} %collective-permute-done.8.refs_1_, bf16[8,2048,256]{2,1,0:T(8,128)(2,1)S(1)} %get-tuple-element.26.refs_1_.refs_3_.refs_2_, ...), custom_call_target="tpu_custom_call" | custom-call | flops 1073741824 | tf_op jit(solution)/shard_map/pallas_call | solution.py:71
  22.5 0.1 collective-permute-start.13
  22.6 1.8 %collective-permute-done.6.refs_2_ = f32[64,256]{1,0:T(8,128)S(1)} collective-permute-done((f32[64,256]{1,0:T(8,128)S(1)}, f32[64,256]{1,0:T(8,128)S(1)}, u32[]{:S(2)}, u32[]{:S(2)}) %collective-permute-start.6) | collective-permute-done | bytes 65568 | tf_op jit(solution)/shard_map/ppermute | solution.py:60
  24.4 1.8 %collective-permute-start.11 = (f32[64,256]{1,0:T(8,128)S(1)}, f32[64,256]{1,0:T(8,128)S(1)}, u32[]{:S(2)}, u32[]{:S(2)}) collective-permute-start(f32[64,256]{1,0:T(8,128)S(1)} %shard_map.83.refs_0_.refs_5_), channel_id=1, source_target_pairs={{24,0},{28,4},{16,8},{20,12},{8,16},{12,20},{0,24},{4,28},{25,1},{... | collective-permute-start | bytes 196616 | tf_op jit(solution)/shard_map/ppermute | solution.py:54
  26.3 0.9 %collective-permute-start.10 = (f32[64,256]{1,0:T(8,128)S(1)}, f32[64,256]{1,0:T(8,128)S(1)}, u32[]{:S(2)}, u32[]{:S(2)}) collective-permute-start(f32[64,256]{1,0:T(8,128)S(1)} %shard_map.83.refs_0_.refs_5_), channel_id=1, source_target_pairs={{16,0},{20,4},{24,8},{28,12},{0,16},{4,20},{8,24},{12,28},{17,1},{... | collective-permute-start | bytes 196616 | tf_op jit(solution)/shard_map/ppermute | solution.py:54
  27.2 0.8 %collective-permute-start.9 = (f32[64,256]{1,0:T(8,128)S(1)}, f32[64,256]{1,0:T(8,128)S(1)}, u32[]{:S(2)}, u32[]{:S(2)}) collective-permute-start(f32[64,256]{1,0:T(8,128)S(1)} %shard_map.83.refs_0_.refs_5_), channel_id=1, source_target_pairs={{8,0},{12,4},{0,8},{4,12},{24,16},{28,20},{16,24},{20,28},{9,1},{1... | collective-permute-start | bytes 196616 | tf_op jit(solution)/shard_map/ppermute | solution.py:54
  28.0 1.8 %collective-permute-done.11.refs_3_ = f32[64,256]{1,0:T(8,128)S(1)} collective-permute-done((f32[64,256]{1,0:T(8,128)S(1)}, f32[64,256]{1,0:T(8,128)S(1)}, u32[]{:S(2)}, u32[]{:S(2)}) %collective-permute-start.11) | collective-permute-done | bytes 65568 | tf_op jit(solution)/shard_map/ppermute | solution.py:54
  29.8 1.0 %collective-permute-done.10.refs_2_ = f32[64,256]{1,0:T(8,128)S(1)} collective-permute-done((f32[64,256]{1,0:T(8,128)S(1)}, f32[64,256]{1,0:T(8,128)S(1)}, u32[]{:S(2)}, u32[]{:S(2)}) %collective-permute-start.10) | collective-permute-done | bytes 65568 | tf_op jit(solution)/shard_map/ppermute | solution.py:54
  30.8 0.7 %collective-permute-done.9.refs_1_ = f32[64,256]{1,0:T(8,128)S(1)} collective-permute-done((f32[64,256]{1,0:T(8,128)S(1)}, f32[64,256]{1,0:T(8,128)S(1)}, u32[]{:S(2)}, u32[]{:S(2)}) %collective-permute-start.9) | collective-permute-done | bytes 65568 | tf_op jit(solution)/shard_map/ppermute | solution.py:54
  31.5 0.1 collective-permute-start.12
  31.6 0.8 %collective-permute-start.17 = (f32[2,64,256]{2,1,0:T(8,128)S(1)}, f32[2,64,256]{2,1,0:T(8,128)S(1)}, u32[]{:S(2)}, u32[]{:S(2)}) collective-permute-start(f32[2,64,256]{2,1,0:T(8,128)S(1)} %get-tuple-element.39), channel_id=1, source_target_pairs={{8,0},{12,4},{0,8},{4,12},{24,16},{28,20},{16,24},{20,28},{9,1},{1... | collective-permute-start | bytes 393224 | tf_op jit(solution)/shard_map/ppermute | solution.py:54
  32.5 0.7 %shard_map.85.refs_2_ = f32[3,64,1024]{2,1,0:T(8,128)S(1)} custom-call(f32[4,64,256]{2,1,0:T(8,128)S(1)} %shard_map.84.refs_0_.refs_1_, bf16[8,2048,256]{2,1,0:T(8,128)(2,1)S(1)} %get-tuple-element.26.refs_1_.refs_3_.refs_2_), custom_call_target="tpu_custom_call" | custom-call | flops 536870912 | tf_op jit(solution)/shard_map/pallas_call | solution.py:71
  33.2 0.8 %shard_map.86 = (f32[64,256]{1,0:T(8,128)S(1)}, f32[64,256]{1,0:T(8,128)S(1)}, f32[64,256]{1,0:T(8,128)S(1)}, f32[64,256]{1,0:T(8,128)S(1)}) custom-call(f32[4,64,256]{2,1,0:T(8,128)S(1)} %collective-permute-done.12.refs_0_, f32[4,64,256]{2,1,0:T(8,128)S(1)} %shard_map.84.refs_0_.refs_1_, f32[3,64,1024]{2,1,0:T(8,128)S(1)} %shard_map.85.refs_2_, ...), custom_call_target="tpu_custom_call" | custom-call | flops 536870912 | tf_op jit(solution)/shard_map/pallas_call | solution.py:71
  34.0 1.6 %collective-permute-start.14 = (f32[64,256]{1,0:T(8,128)S(1)}, f32[64,256]{1,0:T(8,128)S(1)}, u32[]{:S(2)}, u32[]{:S(2)}) collective-permute-start(f32[64,256]{1,0:T(8,128)S(1)} %get-tuple-element.34), channel_id=1, source_target_pairs={{0,3},{1,2},{2,1},{3,0},{4,7},{5,6},{6,5},{7,4},{8,11},{9,10},{10,... | collective-permute-start | bytes 196616 | tf_op jit(solution)/shard_map/ppermute | solution.py:60
  35.7 2.8 %collective-permute-start.16 = (f32[64,256]{1,0:T(8,128)S(1)}, f32[64,256]{1,0:T(8,128)S(1)}, u32[]{:S(2)}, u32[]{:S(2)}) collective-permute-start(f32[64,256]{1,0:T(8,128)S(1)} %get-tuple-element.36), channel_id=1, source_target_pairs={{0,1},{1,0},{2,3},{3,2},{4,5},{5,4},{6,7},{7,6},{8,9},{9,8},{10,11... | collective-permute-start | bytes 196616 | tf_op jit(solution)/shard_map/ppermute | solution.py:60
  38.5 1.0 %collective-permute-start.18 = (f32[1,64,256]{2,1,0:T(8,128)S(1)}, f32[1,64,256]{2,1,0:T(8,128)S(1)}, u32[]{:S(2)}, u32[]{:S(2)}) collective-permute-start(f32[1,64,256]{2,1,0:T(8,128)S(1)} %get-tuple-element.41), channel_id=1, source_target_pairs={{16,0},{20,4},{24,8},{28,12},{0,16},{4,20},{8,24},{12,28},{17,1},{... | collective-permute-start | bytes 196616 | tf_op jit(solution)/shard_map/ppermute | solution.py:54
  39.6 1.3 %collective-permute-done.14.refs_1_ = f32[64,256]{1,0:T(8,128)S(1)} collective-permute-done((f32[64,256]{1,0:T(8,128)S(1)}, f32[64,256]{1,0:T(8,128)S(1)}, u32[]{:S(2)}, u32[]{:S(2)}) %collective-permute-start.14) | collective-permute-done | bytes 65568 | tf_op jit(solution)/shard_map/ppermute | solution.py:60
  40.9 2.0 %collective-permute-done.15.refs_2_ = f32[64,256]{1,0:T(8,128)S(1)} collective-permute-done((f32[64,256]{1,0:T(8,128)S(1)}, f32[64,256]{1,0:T(8,128)S(1)}, u32[]{:S(2)}, u32[]{:S(2)}) %collective-permute-start.15) | collective-permute-done | bytes 65568 | tf_op jit(solution)/shard_map/ppermute | solution.py:60
  42.9 0.5 shard_map.89.refs_0_
  43.4 1.8 %collective-permute-start.21 = (f32[112,256]{1,0:T(8,128)S(1)}, f32[112,256]{1,0:T(8,128)S(1)}, u32[]{:S(2)}, u32[]{:S(2)}) collective-permute-start(f32[112,256]{1,0:T(8,128)S(1)} %shard_map.89.refs_0_), channel_id=1, source_target_pairs={{24,0},{28,4},{16,8},{20,12},{8,16},{12,20},{0,24},{4,28},{25,1},{... | collective-permute-start | bytes 344072 | tf_op jit(solution)/shard_map/ppermute | solution.py:54
  45.2 0.9 %collective-permute-start.20 = (f32[112,256]{1,0:T(8,128)S(1)}, f32[112,256]{1,0:T(8,128)S(1)}, u32[]{:S(2)}, u32[]{:S(2)}) collective-permute-start(f32[112,256]{1,0:T(8,128)S(1)} %shard_map.89.refs_0_), channel_id=1, source_target_pairs={{16,0},{20,4},{24,8},{28,12},{0,16},{4,20},{8,24},{12,28},{17,1},{... | collective-permute-start | bytes 344072 | tf_op jit(solution)/shard_map/ppermute | solution.py:54
  46.2 0.8 %collective-permute-start.19 = (f32[112,256]{1,0:T(8,128)S(1)}, f32[112,256]{1,0:T(8,128)S(1)}, u32[]{:S(2)}, u32[]{:S(2)}) collective-permute-start(f32[112,256]{1,0:T(8,128)S(1)} %shard_map.89.refs_0_), channel_id=1, source_target_pairs={{8,0},{12,4},{0,8},{4,12},{24,16},{28,20},{16,24},{20,28},{9,1},{1... | collective-permute-start | bytes 344072 | tf_op jit(solution)/shard_map/ppermute | solution.py:54
  47.0 3.2 %collective-permute-done.21.refs_3_ = f32[112,256]{1,0:T(8,128)S(1)} collective-permute-done((f32[112,256]{1,0:T(8,128)S(1)}, f32[112,256]{1,0:T(8,128)S(1)}, u32[]{:S(2)}, u32[]{:S(2)}) %collective-permute-start.21) | collective-permute-done | bytes 114720 | tf_op jit(solution)/shard_map/ppermute | solution.py:54
  50.1 1.8 %collective-permute-done.20.refs_2_ = f32[112,256]{1,0:T(8,128)S(1)} collective-permute-done((f32[112,256]{1,0:T(8,128)S(1)}, f32[112,256]{1,0:T(8,128)S(1)}, u32[]{:S(2)}, u32[]{:S(2)}) %collective-permute-start.20) | collective-permute-done | bytes 114720 | tf_op jit(solution)/shard_map/ppermute | solution.py:54
  51.9 0.1 collective-permute-start.22
  52.0 0.7 %shard_map.91.refs_2_ = f32[3,64,1024]{2,1,0:T(8,128)S(1)} custom-call(f32[4,112,256]{2,1,0:T(8,128)S(1)} %shard_map.90.refs_0_.refs_1_, bf16[8,2048,256]{2,1,0:T(8,128)(2,1)S(1)} %get-tuple-element.26.refs_1_.refs_3_.refs_2_), custom_call_target="tpu_custom_call" | custom-call | flops 536870912 | tf_op jit(solution)/shard_map/pallas_call | solution.py:71
  52.8 1.0 %collective-permute-done.22.refs_0_ = f32[4,112,256]{2,1,0:T(8,128)S(1)} collective-permute-done((f32[4,112,256]{2,1,0:T(8,128)S(1)}, f32[4,112,256]{2,1,0:T(8,128)S(1)}, u32[]{:S(2)}, u32[]{:S(2)}) %collective-permute-start.22) | collective-permute-done | bytes 458784 | tf_op jit(solution)/shard_map/ppermute | solution.py:54
  53.8 0.8 %shard_map.92 = (f32[88,256]{1,0:T(8,128)S(1)}, f32[88,256]{1,0:T(8,128)S(1)}, f32[88,256]{1,0:T(8,128)S(1)}, f32[88,256]{1,0:T(8,128)S(1)}) custom-call(f32[4,112,256]{2,1,0:T(8,128)S(1)} %collective-permute-done.22.refs_0_, f32[4,112,256]{2,1,0:T(8,128)S(1)} %shard_map.90.refs_0_.refs_1_, f32[3,64,1024]{2,1,0:T(8,128)S(1)} %shard_map.91.refs_2_, ...), custom_call_target="tpu_custom_call" | custom-call | flops 536870912 | tf_op jit(solution)/shard_map/pallas_call | solution.py:71
  54.6 1.6 %collective-permute-start.23 = (f32[88,256]{1,0:T(8,128)S(1)}, f32[88,256]{1,0:T(8,128)S(1)}, u32[]{:S(2)}, u32[]{:S(2)}) collective-permute-start(f32[88,256]{1,0:T(8,128)S(1)} %get-tuple-element.43), channel_id=1, source_target_pairs={{0,3},{1,2},{2,1},{3,0},{4,7},{5,6},{6,5},{7,4},{8,11},{9,10},{10,... | collective-permute-start | bytes 270344 | tf_op jit(solution)/shard_map/ppermute | solution.py:60
  56.2 2.8 %collective-permute-start.25 = (f32[88,256]{1,0:T(8,128)S(1)}, f32[88,256]{1,0:T(8,128)S(1)}, u32[]{:S(2)}, u32[]{:S(2)}) collective-permute-start(f32[88,256]{1,0:T(8,128)S(1)} %get-tuple-element.45), channel_id=1, source_target_pairs={{0,1},{1,0},{2,3},{3,2},{4,5},{5,4},{6,7},{7,6},{8,9},{9,8},{10,11... | collective-permute-start | bytes 270344 | tf_op jit(solution)/shard_map/ppermute | solution.py:60
  59.1 3.0 %collective-permute-done.23 = f32[88,256]{1,0:T(8,128)S(1)} collective-permute-done((f32[88,256]{1,0:T(8,128)S(1)}, f32[88,256]{1,0:T(8,128)S(1)}, u32[]{:S(2)}, u32[]{:S(2)}) %collective-permute-start.23) | collective-permute-done | bytes 90144 | tf_op jit(solution)/shard_map/ppermute | solution.py:60
  62.0 3.0 %collective-permute-done.24 = f32[88,256]{1,0:T(8,128)S(1)} collective-permute-done((f32[88,256]{1,0:T(8,128)S(1)}, f32[88,256]{1,0:T(8,128)S(1)}, u32[]{:S(2)}, u32[]{:S(2)}) %collective-permute-start.24) | collective-permute-done | bytes 90144 | tf_op jit(solution)/shard_map/ppermute | solution.py:60
  65.0 0.1 collective-permute-start.26
  65.1 0.7 fusion
  65.8 0.5 collective-permute-done.26.refs_1_
  66.3 1.4 %shard_map.93 = f32[3,64,64]{2,1,0:T(8,128)} custom-call(f32[24,256]{1,0:T(8,128)S(1)} %slice_add_fusion.3.refs_0_, f32[24,256]{1,0:T(8,128)S(1)} %collective-permute-done.26.refs_1_), custom_call_target="tpu_custom_call" | custom-call | tf_op jit(solution)/shard_map/pallas_call | solution.py:71
  (25 shorter events, 0.2 us)
Async XLA Ops:
  0.6 12.0 %collective-permute-start.3 = (f32[64,256]{1,0:T(8,128)}, f32[64,256]{1,0:T(8,128)S(1)}, u32[]{:S(2)}, u32[]{:S(2)}) collective-permute-start(f32[64,256]{1,0:T(8,128)} %refs_4_.1), channel_id=1, source_target_pairs={{2,0},{3,1},{0,2},{1,3},{6,4},{7,5},{4,6},{5,7},{10,8},{11,9},{8,1... | collective-permute-start | bytes 196616 | tf_op jit(solution)/shard_map/ppermute | solution.py:54
  4.7 7.9 %collective-permute-start = (f32[64,256]{1,0:T(8,128)}, f32[64,256]{1,0:T(8,128)S(1)}, u32[]{:S(2)}, u32[]{:S(2)}) collective-permute-start(f32[64,256]{1,0:T(8,128)} %refs_5_.1), channel_id=1, source_target_pairs={{8,0},{12,4},{0,8},{4,12},{24,16},{28,20},{16,24},{20,28},{9,1},{1... | collective-permute-start | bytes 196616 | tf_op jit(solution)/shard_map/ppermute | solution.py:54
  6.2 6.4 %collective-permute-start.2 = (f32[64,256]{1,0:T(8,128)}, f32[64,256]{1,0:T(8,128)S(1)}, u32[]{:S(2)}, u32[]{:S(2)}) collective-permute-start(f32[64,256]{1,0:T(8,128)} %refs_5_.1), channel_id=1, source_target_pairs={{24,0},{28,4},{16,8},{20,12},{8,16},{12,20},{0,24},{4,28},{25,1},{... | collective-permute-start | bytes 196616 | tf_op jit(solution)/shard_map/ppermute | solution.py:54
  7.7 4.9 %collective-permute-start.1 = (f32[64,256]{1,0:T(8,128)}, f32[64,256]{1,0:T(8,128)S(1)}, u32[]{:S(2)}, u32[]{:S(2)}) collective-permute-start(f32[64,256]{1,0:T(8,128)} %refs_5_.1), channel_id=1, source_target_pairs={{16,0},{20,4},{24,8},{28,12},{0,16},{4,20},{8,24},{12,28},{17,1},{... | collective-permute-start | bytes 196616 | tf_op jit(solution)/shard_map/ppermute | solution.py:54
  12.7 2.2 %collective-permute-start.4 = (f32[4,64,256]{2,1,0:T(8,128)S(1)}, f32[4,64,256]{2,1,0:T(8,128)S(1)}, u32[]{:S(2)}, u32[]{:S(2)}) collective-permute-start(f32[4,64,256]{2,1,0:T(8,128)S(1)} %shard_map.78.refs_0_.refs_1_), channel_id=1, source_target_pairs={{4,0},{0,4},{12,8},{8,12},{20,16},{16,20},{28,24},{24,28},{5,1},{1... | collective-permute-start | bytes 786440 | tf_op jit(solution)/shard_map/ppermute | solution.py:54
  12.8 7.3 %collective-permute-start.8 = (f32[2,64,256]{2,1,0:T(8,128)S(1)}, f32[2,64,256]{2,1,0:T(8,128)S(1)}, u32[]{:S(2)}, u32[]{:S(2)}) collective-permute-start(f32[2,64,256]{2,1,0:T(8,128)S(1)} %shard_map.80.refs_4_.refs_0_), channel_id=1, source_target_pairs={{1,0},{0,1},{3,2},{2,3},{5,4},{4,5},{7,6},{6,7},{9,8},{8,9},{11,10... | collective-permute-start | bytes 393224 | tf_op jit(solution)/shard_map/ppermute | solution.py:54
  15.6 6.9 %collective-permute-start.5 = (f32[64,256]{1,0:T(8,128)S(1)}, f32[64,256]{1,0:T(8,128)S(1)}, u32[]{:S(2)}, u32[]{:S(2)}) collective-permute-start(f32[64,256]{1,0:T(8,128)S(1)} %get-tuple-element.29), channel_id=1, source_target_pairs={{0,3},{1,2},{2,1},{3,0},{4,7},{5,6},{6,5},{7,4},{8,11},{9,10},{10,... | collective-permute-start | bytes 196616 | tf_op jit(solution)/shard_map/ppermute | solution.py:60
  16.1 8.3 %collective-permute-start.6 = (f32[64,256]{1,0:T(8,128)S(1)}, f32[64,256]{1,0:T(8,128)S(1)}, u32[]{:S(2)}, u32[]{:S(2)}) collective-permute-start(f32[64,256]{1,0:T(8,128)S(1)} %get-tuple-element.30), channel_id=1, source_target_pairs={{0,2},{1,3},{2,0},{3,1},{4,6},{5,7},{6,4},{7,5},{8,10},{9,11},{10,... | collective-permute-start | bytes 196616 | tf_op jit(solution)/shard_map/ppermute | solution.py:60
  17.9 6.5 %collective-permute-start.7 = (f32[64,256]{1,0:T(8,128)S(1)}, f32[64,256]{1,0:T(8,128)S(1)}, u32[]{:S(2)}, u32[]{:S(2)}) collective-permute-start(f32[64,256]{1,0:T(8,128)S(1)} %get-tuple-element.31), channel_id=1, source_target_pairs={{0,1},{1,0},{2,3},{3,2},{4,5},{5,4},{6,7},{7,6},{8,9},{9,8},{10,11... | collective-permute-start | bytes 196616 | tf_op jit(solution)/shard_map/ppermute | solution.py:60
  22.5 9.1 %collective-permute-start.13 = (f32[4,64,256]{2,1,0:T(8,128)S(1)}, f32[4,64,256]{2,1,0:T(8,128)S(1)}, u32[]{:S(2)}, u32[]{:S(2)}) collective-permute-start(f32[4,64,256]{2,1,0:T(8,128)S(1)} %get-tuple-element.32.refs_4_), channel_id=1, source_target_pairs={{4,0},{0,4},{12,8},{8,12},{20,16},{16,20},{28,24},{24,28},{5,1},{1... | collective-permute-start | bytes 786440 | tf_op jit(solution)/shard_map/ppermute | solution.py:54
  24.4 5.3 %collective-permute-start.11 = (f32[64,256]{1,0:T(8,128)S(1)}, f32[64,256]{1,0:T(8,128)S(1)}, u32[]{:S(2)}, u32[]{:S(2)}) collective-permute-start(f32[64,256]{1,0:T(8,128)S(1)} %shard_map.83.refs_0_.refs_5_), channel_id=1, source_target_pairs={{24,0},{28,4},{16,8},{20,12},{8,16},{12,20},{0,24},{4,28},{25,1},{... | collective-permute-start | bytes 196616 | tf_op jit(solution)/shard_map/ppermute | solution.py:54
  26.3 4.5 %collective-permute-start.10 = (f32[64,256]{1,0:T(8,128)S(1)}, f32[64,256]{1,0:T(8,128)S(1)}, u32[]{:S(2)}, u32[]{:S(2)}) collective-permute-start(f32[64,256]{1,0:T(8,128)S(1)} %shard_map.83.refs_0_.refs_5_), channel_id=1, source_target_pairs={{16,0},{20,4},{24,8},{28,12},{0,16},{4,20},{8,24},{12,28},{17,1},{... | collective-permute-start | bytes 196616 | tf_op jit(solution)/shard_map/ppermute | solution.py:54
  27.2 4.3 %collective-permute-start.9 = (f32[64,256]{1,0:T(8,128)S(1)}, f32[64,256]{1,0:T(8,128)S(1)}, u32[]{:S(2)}, u32[]{:S(2)}) collective-permute-start(f32[64,256]{1,0:T(8,128)S(1)} %shard_map.83.refs_0_.refs_5_), channel_id=1, source_target_pairs={{8,0},{12,4},{0,8},{4,12},{24,16},{28,20},{16,24},{20,28},{9,1},{1... | collective-permute-start | bytes 196616 | tf_op jit(solution)/shard_map/ppermute | solution.py:54
  31.5 1.7 %collective-permute-start.12 = (f32[4,64,256]{2,1,0:T(8,128)S(1)}, f32[4,64,256]{2,1,0:T(8,128)S(1)}, u32[]{:S(2)}, u32[]{:S(2)}) collective-permute-start(f32[4,64,256]{2,1,0:T(8,128)S(1)} %shard_map.84.refs_0_.refs_1_), channel_id=1, source_target_pairs={{4,0},{0,4},{12,8},{8,12},{20,16},{16,20},{28,24},{24,28},{5,1},{1... | collective-permute-start | bytes 786440 | tf_op jit(solution)/shard_map/ppermute | solution.py:54
  31.6 6.9 %collective-permute-start.17 = (f32[2,64,256]{2,1,0:T(8,128)S(1)}, f32[2,64,256]{2,1,0:T(8,128)S(1)}, u32[]{:S(2)}, u32[]{:S(2)}) collective-permute-start(f32[2,64,256]{2,1,0:T(8,128)S(1)} %get-tuple-element.39), channel_id=1, source_target_pairs={{8,0},{12,4},{0,8},{4,12},{24,16},{28,20},{16,24},{20,28},{9,1},{1... | collective-permute-start | bytes 393224 | tf_op jit(solution)/shard_map/ppermute | solution.py:54
  34.0 6.9 %collective-permute-start.14 = (f32[64,256]{1,0:T(8,128)S(1)}, f32[64,256]{1,0:T(8,128)S(1)}, u32[]{:S(2)}, u32[]{:S(2)}) collective-permute-start(f32[64,256]{1,0:T(8,128)S(1)} %get-tuple-element.34), channel_id=1, source_target_pairs={{0,3},{1,2},{2,1},{3,0},{4,7},{5,6},{6,5},{7,4},{8,11},{9,10},{10,... | collective-permute-start | bytes 196616 | tf_op jit(solution)/shard_map/ppermute | solution.py:60
  35.7 7.2 %collective-permute-start.15 = (f32[64,256]{1,0:T(8,128)S(1)}, f32[64,256]{1,0:T(8,128)S(1)}, u32[]{:S(2)}, u32[]{:S(2)}) collective-permute-start(f32[64,256]{1,0:T(8,128)S(1)} %get-tuple-element.35), channel_id=1, source_target_pairs={{0,2},{1,3},{2,0},{3,1},{4,6},{5,7},{6,4},{7,5},{8,10},{9,11},{10,... | collective-permute-start | bytes 196616 | tf_op jit(solution)/shard_map/ppermute | solution.py:60
  35.7 7.2 %collective-permute-start.16 = (f32[64,256]{1,0:T(8,128)S(1)}, f32[64,256]{1,0:T(8,128)S(1)}, u32[]{:S(2)}, u32[]{:S(2)}) collective-permute-start(f32[64,256]{1,0:T(8,128)S(1)} %get-tuple-element.36), channel_id=1, source_target_pairs={{0,1},{1,0},{2,3},{3,2},{4,5},{5,4},{6,7},{7,6},{8,9},{9,8},{10,11... | collective-permute-start | bytes 196616 | tf_op jit(solution)/shard_map/ppermute | solution.py:60
  38.5 4.4 %collective-permute-start.18 = (f32[1,64,256]{2,1,0:T(8,128)S(1)}, f32[1,64,256]{2,1,0:T(8,128)S(1)}, u32[]{:S(2)}, u32[]{:S(2)}) collective-permute-start(f32[1,64,256]{2,1,0:T(8,128)S(1)} %get-tuple-element.41), channel_id=1, source_target_pairs={{16,0},{20,4},{24,8},{28,12},{0,16},{4,20},{8,24},{12,28},{17,1},{... | collective-permute-start | bytes 196616 | tf_op jit(solution)/shard_map/ppermute | solution.py:54
  43.4 6.7 %collective-permute-start.21 = (f32[112,256]{1,0:T(8,128)S(1)}, f32[112,256]{1,0:T(8,128)S(1)}, u32[]{:S(2)}, u32[]{:S(2)}) collective-permute-start(f32[112,256]{1,0:T(8,128)S(1)} %shard_map.89.refs_0_), channel_id=1, source_target_pairs={{24,0},{28,4},{16,8},{20,12},{8,16},{12,20},{0,24},{4,28},{25,1},{... | collective-permute-start | bytes 344072 | tf_op jit(solution)/shard_map/ppermute | solution.py:54
  45.2 6.6 %collective-permute-start.20 = (f32[112,256]{1,0:T(8,128)S(1)}, f32[112,256]{1,0:T(8,128)S(1)}, u32[]{:S(2)}, u32[]{:S(2)}) collective-permute-start(f32[112,256]{1,0:T(8,128)S(1)} %shard_map.89.refs_0_), channel_id=1, source_target_pairs={{16,0},{20,4},{24,8},{28,12},{0,16},{4,20},{8,24},{12,28},{17,1},{... | collective-permute-start | bytes 344072 | tf_op jit(solution)/shard_map/ppermute | solution.py:54
  46.2 5.7 %collective-permute-start.19 = (f32[112,256]{1,0:T(8,128)S(1)}, f32[112,256]{1,0:T(8,128)S(1)}, u32[]{:S(2)}, u32[]{:S(2)}) collective-permute-start(f32[112,256]{1,0:T(8,128)S(1)} %shard_map.89.refs_0_), channel_id=1, source_target_pairs={{8,0},{12,4},{0,8},{4,12},{24,16},{28,20},{16,24},{20,28},{9,1},{1... | collective-permute-start | bytes 344072 | tf_op jit(solution)/shard_map/ppermute | solution.py:54
  51.9 1.9 %collective-permute-start.22 = (f32[4,112,256]{2,1,0:T(8,128)S(1)}, f32[4,112,256]{2,1,0:T(8,128)S(1)}, u32[]{:S(2)}, u32[]{:S(2)}) collective-permute-start(f32[4,112,256]{2,1,0:T(8,128)S(1)} %shard_map.90.refs_0_.refs_1_), channel_id=1, source_target_pairs={{4,0},{0,4},{12,8},{8,12},{20,16},{16,20},{28,24},{24,28},{5,1},{1... | collective-permute-start | bytes 1376264 | tf_op jit(solution)/shard_map/ppermute | solution.py:54
  54.6 7.4 %collective-permute-start.23 = (f32[88,256]{1,0:T(8,128)S(1)}, f32[88,256]{1,0:T(8,128)S(1)}, u32[]{:S(2)}, u32[]{:S(2)}) collective-permute-start(f32[88,256]{1,0:T(8,128)S(1)} %get-tuple-element.43), channel_id=1, source_target_pairs={{0,3},{1,2},{2,1},{3,0},{4,7},{5,6},{6,5},{7,4},{8,11},{9,10},{10,... | collective-permute-start | bytes 270344 | tf_op jit(solution)/shard_map/ppermute | solution.py:60
  56.2 8.8 %collective-permute-start.24 = (f32[88,256]{1,0:T(8,128)S(1)}, f32[88,256]{1,0:T(8,128)S(1)}, u32[]{:S(2)}, u32[]{:S(2)}) collective-permute-start(f32[88,256]{1,0:T(8,128)S(1)} %get-tuple-element.44), channel_id=1, source_target_pairs={{0,2},{1,3},{2,0},{3,1},{4,6},{5,7},{6,4},{7,5},{8,10},{9,11},{10,... | collective-permute-start | bytes 270344 | tf_op jit(solution)/shard_map/ppermute | solution.py:60
  56.2 8.8 %collective-permute-start.25 = (f32[88,256]{1,0:T(8,128)S(1)}, f32[88,256]{1,0:T(8,128)S(1)}, u32[]{:S(2)}, u32[]{:S(2)}) collective-permute-start(f32[88,256]{1,0:T(8,128)S(1)} %get-tuple-element.45), channel_id=1, source_target_pairs={{0,1},{1,0},{2,3},{3,2},{4,5},{5,4},{6,7},{7,6},{8,9},{9,8},{10,11... | collective-permute-start | bytes 270344 | tf_op jit(solution)/shard_map/ppermute | solution.py:60
  65.0 1.3 %collective-permute-start.26 = (f32[24,256]{1,0:T(8,128)S(1)}, f32[24,256]{1,0:T(8,128)S(1)}, u32[]{:S(2)}, u32[]{:S(2)}) collective-permute-start(f32[24,256]{1,0:T(8,128)S(1)} %slice_add_fusion.3.refs_0_), channel_id=1, source_target_pairs={{4,0},{0,4},{12,8},{8,12},{20,16},{16,20},{28,24},{24,28},{5,1},{1... | collective-permute-start | bytes 73736 | tf_op jit(solution)/shard_map/ppermute | solution.py:54

commit v14 on v9

--- a/solution.py
+++ b/solution.py
@@ -150,18 +150,28 @@
     ]
     for copy in small[:3]:
         copy.start()
-    for index in range(chunk_count):
+    sure_count = min(2, chunk_count)
+    for index in range(sure_count):
         chunk(index).start()
-    for copy in small[3:]:
-        copy.start()
 
     def clear(block, carry):
         dense_ref[block] = jnp.zeros(dense_ref.shape[1:], dense_ref.dtype)
         return carry
 
-    lax.fori_loop(0, dense_ref.shape[0], clear, 0)
+    half = dense_ref.shape[0] // 2
+    lax.fori_loop(0, half, clear, 0)
     for copy in small[:3]:
         copy.wait()
+    used_count = jnp.maximum((count_ref[0, 0] + group - 1) // group, sure_count)
+    for index in range(sure_count, chunk_count):
+
+        @pl.when(index < used_count)
+        def _():
+            chunk(index).start()
+
+    for copy in small[3:]:
+        copy.start()
+    lax.fori_loop(half, dense_ref.shape[0], clear, 0)
 
     def place(slot):
         row, col = rows_ref[0, 0, slot], cols_ref[0, 0, slot]
@@ -181,7 +191,7 @@
             place(index * group + offset)
         return carry
 
-    lax.fori_loop(0, chunk_count, step, 0)
+    lax.fori_loop(0, used_count, step, 0)
     for copy in small[3:]:
         copy.wait()
     token_ref[...] = jnp.zeros_like(token_ref)

time: 68 us -> 67.8 us (level)
  Pallas kernels: 12.6 us -> 11.3 us
  waiting for transfers between devices: 20.8 us -> 21.9 us
    pallas_call x1, Pallas kernels: 3.5 us -> 2.22 us  [build_dense(): pl.pallas_call(functools.partial(build_kernel, (*sizes, group)), in_specs...]
    ppermute x18, waiting for transfers between devices: 10.4 us -> 11.3 us  [fetch(): lax.ppermute(piece, axis, [(partner(i, shift, size), i) for i in range(si...]
  transfers between devices with their start and end apart: 27 -> 27, of which waited for: 14 -> 14; matrix products, arithmetic and copies ran while one was open for 1% -> 1% of each run, Pallas kernels for 14% -> 13%
where the time goes in v14:
time: 67.8 us; the launch traced here: 67.6 us
  starting transfers between devices  32.2 us (47%)
  waiting for transfers between devices  21.9 us (32%)
  Pallas kernels  11.3 us (17%)
  between operations  1.47 us (2%)
  other arithmetic  0.68 us (1%)
    ppermute x18, starting transfers between devices, fetch(): lax.ppermute(piece, axis, [(partner(i, shift, size), i) for i in range(si...  18.8 us
    ppermute x9, starting transfers between devices, scatter_pieces(): lax.ppermute(pieces[shift], axis, [(i, partner(i, shift, size)) for i in...  13.4 us
    ppermute x18, waiting for transfers between devices, fetch(): lax.ppermute(piece, axis, [(partner(i, shift, size), i) for i in range(si...  11.3 us
    ppermute x9, waiting for transfers between devices, scatter_pieces(): lax.ppermute(pieces[shift], axis, [(i, partner(i, shift, size)) for i in...  10.6 us
    pallas_call x16, Pallas kernels, call(): pl.pallas_call(body, in_specs=[vmem] * len(operands) + [pl.BlockSpec(memo...  9.1 us
    pallas_call x1, Pallas kernels, build_dense(): pl.pallas_call(functools.partial(build_kernel, (*sizes, group)), in_specs...  2.22 us
  transfers between devices with their start and end apart: 27, of which 14 were waited for; matrix products, arithmetic and copies ran while one was open for 1% of the time, Pallas kernels for 13%

profile of v14, /device:TPU:0, one launch (start us, length us, event | category | flops | bytes accessed | tf_op | source)
XLA Modules:
  0.0 67.6 jit_solution(12714936793006407503)
XLA Ops:
  0.6 4.1 %collective-permute-start.3 = (f32[64,256]{1,0:T(8,128)}, f32[64,256]{1,0:T(8,128)S(1)}, u32[]{:S(2)}, u32[]{:S(2)}) collective-permute-start(f32[64,256]{1,0:T(8,128)} %refs_4_.1), channel_id=1, source_target_pairs={{2,0},{3,1},{0,2},{1,3},{6,4},{7,5},{4,6},{5,7},{10,8},{11,9},{8,1... | collective-permute-start | bytes 196616 | tf_op jit(solution)/shard_map/ppermute | solution.py:54
  4.7 1.5 %collective-permute-start = (f32[64,256]{1,0:T(8,128)}, f32[64,256]{1,0:T(8,128)S(1)}, u32[]{:S(2)}, u32[]{:S(2)}) collective-permute-start(f32[64,256]{1,0:T(8,128)} %refs_5_.1), channel_id=1, source_target_pairs={{8,0},{12,4},{0,8},{4,12},{24,16},{28,20},{16,24},{20,28},{9,1},{1... | collective-permute-start | bytes 196616 | tf_op jit(solution)/shard_map/ppermute | solution.py:54
  6.2 1.5 %collective-permute-start.2 = (f32[64,256]{1,0:T(8,128)}, f32[64,256]{1,0:T(8,128)S(1)}, u32[]{:S(2)}, u32[]{:S(2)}) collective-permute-start(f32[64,256]{1,0:T(8,128)} %refs_5_.1), channel_id=1, source_target_pairs={{24,0},{28,4},{16,8},{20,12},{8,16},{12,20},{0,24},{4,28},{25,1},{... | collective-permute-start | bytes 196616 | tf_op jit(solution)/shard_map/ppermute | solution.py:54
  7.7 0.5 collective-permute-start.1
  8.9 2.2 %shard_map.77 = (bf16[8,2048,256]{2,1,0:T(8,128)(2,1)S(1)}, f32[64,256]{1,0:T(8,128)S(1)}, f32[64,256]{1,0:T(8,128)S(1)}, f32[8,128]{1,0:T(8,128)S(1)}) custom-call(s32[1,1,64]{2,1,0:T(1,128)} %refs_0_.1, s32[1,1,64]{2,1,0:T(1,128)} %refs_1_.1, s32[1,1]{1,0:T(1,128)S(6)} %copy.8.refs_2_, f32[1,1,64,128,128]{4,3,2,1,0:T(8,128)} %refs_3_.1, ...), custom_call_target="tpu_custom_call" | custom-call | flops 8388608 | bytes 8388608 | tf_op jit(solution)/shard_map/pallas_call | solution.py:211
  11.1 0.5 collective-permute-done.2.refs_3_
  11.6 0.7 %collective-permute-done.1.refs_2_ = f32[64,256]{1,0:T(8,128)S(1)} collective-permute-done((f32[64,256]{1,0:T(8,128)}, f32[64,256]{1,0:T(8,128)S(1)}, u32[]{:S(2)}, u32[]{:S(2)}) %collective-permute-start.1) | collective-permute-done | bytes 65568 | tf_op jit(solution)/shard_map/ppermute | solution.py:54
  12.4 1.6 %collective-permute-start.8 = (f32[2,64,256]{2,1,0:T(8,128)S(1)}, f32[2,64,256]{2,1,0:T(8,128)S(1)}, u32[]{:S(2)}, u32[]{:S(2)}) collective-permute-start(f32[2,64,256]{2,1,0:T(8,128)S(1)} %shard_map.80.refs_4_.refs_0_), channel_id=1, source_target_pairs={{1,0},{0,1},{3,2},{2,3},{5,4},{4,5},{7,6},{6,7},{9,8},{8,9},{11,10... | collective-permute-start | bytes 393224 | tf_op jit(solution)/shard_map/ppermute | solution.py:54
  14.1 0.7 %shard_map.79.refs_2_ = f32[3,64,1024]{2,1,0:T(8,128)S(1)} custom-call(f32[4,64,256]{2,1,0:T(8,128)S(1)} %shard_map.78.refs_0_.refs_1_, bf16[8,2048,256]{2,1,0:T(8,128)(2,1)S(1)} %get-tuple-element.26.refs_1_.refs_3_.refs_2_), custom_call_target="tpu_custom_call" | custom-call | flops 536870912 | tf_op jit(solution)/shard_map/pallas_call | solution.py:71
  14.8 0.8 %shard_map.81 = (f32[64,256]{1,0:T(8,128)S(1)}, f32[64,256]{1,0:T(8,128)S(1)}, f32[64,256]{1,0:T(8,128)S(1)}, f32[64,256]{1,0:T(8,128)S(1)}) custom-call(f32[4,64,256]{2,1,0:T(8,128)S(1)} %collective-permute-done.4.refs_0_, f32[4,64,256]{2,1,0:T(8,128)S(1)} %shard_map.78.refs_0_.refs_1_, f32[3,64,1024]{2,1,0:T(8,128)S(1)} %shard_map.79.refs_2_, ...), custom_call_target="tpu_custom_call" | custom-call | flops 536870912 | tf_op jit(solution)/shard_map/pallas_call | solution.py:71
  15.6 0.5 collective-permute-start.5
  16.1 1.7 %collective-permute-start.6 = (f32[64,256]{1,0:T(8,128)S(1)}, f32[64,256]{1,0:T(8,128)S(1)}, u32[]{:S(2)}, u32[]{:S(2)}) collective-permute-start(f32[64,256]{1,0:T(8,128)S(1)} %get-tuple-element.30), channel_id=1, source_target_pairs={{0,2},{1,3},{2,0},{3,1},{4,6},{5,7},{6,4},{7,5},{8,10},{9,11},{10,... | collective-permute-start | bytes 196616 | tf_op jit(solution)/shard_map/ppermute | solution.py:60
  17.8 2.3 %collective-permute-start.7 = (f32[64,256]{1,0:T(8,128)S(1)}, f32[64,256]{1,0:T(8,128)S(1)}, u32[]{:S(2)}, u32[]{:S(2)}) collective-permute-start(f32[64,256]{1,0:T(8,128)S(1)} %get-tuple-element.31), channel_id=1, source_target_pairs={{0,1},{1,0},{2,3},{3,2},{4,5},{5,4},{6,7},{7,6},{8,9},{9,8},{10,11... | collective-permute-start | bytes 196616 | tf_op jit(solution)/shard_map/ppermute | solution.py:60
  20.1 2.4 %shard_map.82 = (f32[4,64,256]{2,1,0:T(8,128)S(1)}, f32[4,64,256]{2,1,0:T(8,128)S(1)}) custom-call(f32[2,64,256]{2,1,0:T(8,128)S(1)} %shard_map.80.refs_4_.refs_0_, f32[2,64,256]{2,1,0:T(8,128)S(1)} %collective-permute-done.8.refs_1_, bf16[8,2048,256]{2,1,0:T(8,128)(2,1)S(1)} %get-tuple-element.26.refs_1_.refs_3_.refs_2_, ...), custom_call_target="tpu_custom_call" | custom-call | flops 1073741824 | tf_op jit(solution)/shard_map/pallas_call | solution.py:71
  22.6 1.7 %collective-permute-done.6.refs_2_ = f32[64,256]{1,0:T(8,128)S(1)} collective-permute-done((f32[64,256]{1,0:T(8,128)S(1)}, f32[64,256]{1,0:T(8,128)S(1)}, u32[]{:S(2)}, u32[]{:S(2)}) %collective-permute-start.6) | collective-permute-done | bytes 65568 | tf_op jit(solution)/shard_map/ppermute | solution.py:60
  24.3 2.2 %collective-permute-start.11 = (f32[64,256]{1,0:T(8,128)S(1)}, f32[64,256]{1,0:T(8,128)S(1)}, u32[]{:S(2)}, u32[]{:S(2)}) collective-permute-start(f32[64,256]{1,0:T(8,128)S(1)} %shard_map.83.refs_0_.refs_5_), channel_id=1, source_target_pairs={{24,0},{28,4},{16,8},{20,12},{8,16},{12,20},{0,24},{4,28},{25,1},{... | collective-permute-start | bytes 196616 | tf_op jit(solution)/shard_map/ppermute | solution.py:54
  26.6 0.7 collective-permute-start.10
  27.2 0.6 collective-permute-start.9
  27.9 1.9 %collective-permute-done.11.refs_3_ = f32[64,256]{1,0:T(8,128)S(1)} collective-permute-done((f32[64,256]{1,0:T(8,128)S(1)}, f32[64,256]{1,0:T(8,128)S(1)}, u32[]{:S(2)}, u32[]{:S(2)}) %collective-permute-start.11) | collective-permute-done | bytes 65568 | tf_op jit(solution)/shard_map/ppermute | solution.py:54
  29.8 1.1 %collective-permute-done.10.refs_2_ = f32[64,256]{1,0:T(8,128)S(1)} collective-permute-done((f32[64,256]{1,0:T(8,128)S(1)}, f32[64,256]{1,0:T(8,128)S(1)}, u32[]{:S(2)}, u32[]{:S(2)}) %collective-permute-start.10) | collective-permute-done | bytes 65568 | tf_op jit(solution)/shard_map/ppermute | solution.py:54
  30.8 0.7 collective-permute-done.9.refs_1_
  31.5 0.1 collective-permute-start.12
  31.6 0.7 %collective-permute-start.17 = (f32[2,64,256]{2,1,0:T(8,128)S(1)}, f32[2,64,256]{2,1,0:T(8,128)S(1)}, u32[]{:S(2)}, u32[]{:S(2)}) collective-permute-start(f32[2,64,256]{2,1,0:T(8,128)S(1)} %get-tuple-element.39), channel_id=1, source_target_pairs={{8,0},{12,4},{0,8},{4,12},{24,16},{28,20},{16,24},{20,28},{9,1},{1... | collective-permute-start | bytes 393224 | tf_op jit(solution)/shard_map/ppermute | solution.py:54
  32.3 0.7 %shard_map.85.refs_2_ = f32[3,64,1024]{2,1,0:T(8,128)S(1)} custom-call(f32[4,64,256]{2,1,0:T(8,128)S(1)} %shard_map.84.refs_0_.refs_1_, bf16[8,2048,256]{2,1,0:T(8,128)(2,1)S(1)} %get-tuple-element.26.refs_1_.refs_3_.refs_2_), custom_call_target="tpu_custom_call" | custom-call | flops 536870912 | tf_op jit(solution)/shard_map/pallas_call | solution.py:71
  33.1 0.8 %shard_map.86 = (f32[64,256]{1,0:T(8,128)S(1)}, f32[64,256]{1,0:T(8,128)S(1)}, f32[64,256]{1,0:T(8,128)S(1)}, f32[64,256]{1,0:T(8,128)S(1)}) custom-call(f32[4,64,256]{2,1,0:T(8,128)S(1)} %collective-permute-done.12.refs_0_, f32[4,64,256]{2,1,0:T(8,128)S(1)} %shard_map.84.refs_0_.refs_1_, f32[3,64,1024]{2,1,0:T(8,128)S(1)} %shard_map.85.refs_2_, ...), custom_call_target="tpu_custom_call" | custom-call | flops 536870912 | tf_op jit(solution)/shard_map/pallas_call | solution.py:71
  33.9 1.8 %collective-permute-start.14 = (f32[64,256]{1,0:T(8,128)S(1)}, f32[64,256]{1,0:T(8,128)S(1)}, u32[]{:S(2)}, u32[]{:S(2)}) collective-permute-start(f32[64,256]{1,0:T(8,128)S(1)} %get-tuple-element.34), channel_id=1, source_target_pairs={{0,3},{1,2},{2,1},{3,0},{4,7},{5,6},{6,5},{7,4},{8,11},{9,10},{10,... | collective-permute-start | bytes 196616 | tf_op jit(solution)/shard_map/ppermute | solution.py:60
  35.7 2.7 %collective-permute-start.16 = (f32[64,256]{1,0:T(8,128)S(1)}, f32[64,256]{1,0:T(8,128)S(1)}, u32[]{:S(2)}, u32[]{:S(2)}) collective-permute-start(f32[64,256]{1,0:T(8,128)S(1)} %get-tuple-element.36), channel_id=1, source_target_pairs={{0,1},{1,0},{2,3},{3,2},{4,5},{5,4},{6,7},{7,6},{8,9},{9,8},{10,11... | collective-permute-start | bytes 196616 | tf_op jit(solution)/shard_map/ppermute | solution.py:60
  38.4 1.4 %collective-permute-start.18 = (f32[1,64,256]{2,1,0:T(8,128)S(1)}, f32[1,64,256]{2,1,0:T(8,128)S(1)}, u32[]{:S(2)}, u32[]{:S(2)}) collective-permute-start(f32[1,64,256]{2,1,0:T(8,128)S(1)} %get-tuple-element.41), channel_id=1, source_target_pairs={{16,0},{20,4},{24,8},{28,12},{0,16},{4,20},{8,24},{12,28},{17,1},{... | collective-permute-start | bytes 196616 | tf_op jit(solution)/shard_map/ppermute | solution.py:54
  39.8 1.0 %collective-permute-done.14.refs_1_ = f32[64,256]{1,0:T(8,128)S(1)} collective-permute-done((f32[64,256]{1,0:T(8,128)S(1)}, f32[64,256]{1,0:T(8,128)S(1)}, u32[]{:S(2)}, u32[]{:S(2)}) %collective-permute-start.14) | collective-permute-done | bytes 65568 | tf_op jit(solution)/shard_map/ppermute | solution.py:60
  40.8 2.0 %collective-permute-done.15.refs_2_ = f32[64,256]{1,0:T(8,128)S(1)} collective-permute-done((f32[64,256]{1,0:T(8,128)S(1)}, f32[64,256]{1,0:T(8,128)S(1)}, u32[]{:S(2)}, u32[]{:S(2)}) %collective-permute-start.15) | collective-permute-done | bytes 65568 | tf_op jit(solution)/shard_map/ppermute | solution.py:60
  42.8 0.5 shard_map.89.refs_0_
  43.3 2.2 %collective-permute-start.21 = (f32[112,256]{1,0:T(8,128)S(1)}, f32[112,256]{1,0:T(8,128)S(1)}, u32[]{:S(2)}, u32[]{:S(2)}) collective-permute-start(f32[112,256]{1,0:T(8,128)S(1)} %shard_map.89.refs_0_), channel_id=1, source_target_pairs={{24,0},{28,4},{16,8},{20,12},{8,16},{12,20},{0,24},{4,28},{25,1},{... | collective-permute-start | bytes 344072 | tf_op jit(solution)/shard_map/ppermute | solution.py:54
  45.5 0.7 collective-permute-start.20
  46.2 0.6 collective-permute-start.19
  46.8 2.7 %collective-permute-done.21.refs_3_ = f32[112,256]{1,0:T(8,128)S(1)} collective-permute-done((f32[112,256]{1,0:T(8,128)S(1)}, f32[112,256]{1,0:T(8,128)S(1)}, u32[]{:S(2)}, u32[]{:S(2)}) %collective-permute-start.21) | collective-permute-done | bytes 114720 | tf_op jit(solution)/shard_map/ppermute | solution.py:54
  49.5 2.2 %collective-permute-done.20.refs_2_ = f32[112,256]{1,0:T(8,128)S(1)} collective-permute-done((f32[112,256]{1,0:T(8,128)S(1)}, f32[112,256]{1,0:T(8,128)S(1)}, u32[]{:S(2)}, u32[]{:S(2)}) %collective-permute-start.20) | collective-permute-done | bytes 114720 | tf_op jit(solution)/shard_map/ppermute | solution.py:54
  51.8 0.1 collective-permute-start.22
  51.9 0.7 %shard_map.91.refs_2_ = f32[3,64,1024]{2,1,0:T(8,128)S(1)} custom-call(f32[4,112,256]{2,1,0:T(8,128)S(1)} %shard_map.90.refs_0_.refs_1_, bf16[8,2048,256]{2,1,0:T(8,128)(2,1)S(1)} %get-tuple-element.26.refs_1_.refs_3_.refs_2_), custom_call_target="tpu_custom_call" | custom-call | flops 536870912 | tf_op jit(solution)/shard_map/pallas_call | solution.py:71
  52.6 1.0 %collective-permute-done.22.refs_0_ = f32[4,112,256]{2,1,0:T(8,128)S(1)} collective-permute-done((f32[4,112,256]{2,1,0:T(8,128)S(1)}, f32[4,112,256]{2,1,0:T(8,128)S(1)}, u32[]{:S(2)}, u32[]{:S(2)}) %collective-permute-start.22) | collective-permute-done | bytes 458784 | tf_op jit(solution)/shard_map/ppermute | solution.py:54
  53.7 0.8 %shard_map.92 = (f32[88,256]{1,0:T(8,128)S(1)}, f32[88,256]{1,0:T(8,128)S(1)}, f32[88,256]{1,0:T(8,128)S(1)}, f32[88,256]{1,0:T(8,128)S(1)}) custom-call(f32[4,112,256]{2,1,0:T(8,128)S(1)} %collective-permute-done.22.refs_0_, f32[4,112,256]{2,1,0:T(8,128)S(1)} %shard_map.90.refs_0_.refs_1_, f32[3,64,1024]{2,1,0:T(8,128)S(1)} %shard_map.91.refs_2_, ...), custom_call_target="tpu_custom_call" | custom-call | flops 536870912 | tf_op jit(solution)/shard_map/pallas_call | solution.py:71
  54.5 1.8 %collective-permute-start.23 = (f32[88,256]{1,0:T(8,128)S(1)}, f32[88,256]{1,0:T(8,128)S(1)}, u32[]{:S(2)}, u32[]{:S(2)}) collective-permute-start(f32[88,256]{1,0:T(8,128)S(1)} %get-tuple-element.43), channel_id=1, source_target_pairs={{0,3},{1,2},{2,1},{3,0},{4,7},{5,6},{6,5},{7,4},{8,11},{9,10},{10,... | collective-permute-start | bytes 270344 | tf_op jit(solution)/shard_map/ppermute | solution.py:60
  56.2 2.7 %collective-permute-start.25 = (f32[88,256]{1,0:T(8,128)S(1)}, f32[88,256]{1,0:T(8,128)S(1)}, u32[]{:S(2)}, u32[]{:S(2)}) collective-permute-start(f32[88,256]{1,0:T(8,128)S(1)} %get-tuple-element.45), channel_id=1, source_target_pairs={{0,1},{1,0},{2,3},{3,2},{4,5},{5,4},{6,7},{7,6},{8,9},{9,8},{10,11... | collective-permute-start | bytes 270344 | tf_op jit(solution)/shard_map/ppermute | solution.py:60
  58.9 3.0 %collective-permute-done.23 = f32[88,256]{1,0:T(8,128)S(1)} collective-permute-done((f32[88,256]{1,0:T(8,128)S(1)}, f32[88,256]{1,0:T(8,128)S(1)}, u32[]{:S(2)}, u32[]{:S(2)}) %collective-permute-start.23) | collective-permute-done | bytes 90144 | tf_op jit(solution)/shard_map/ppermute | solution.py:60
  61.9 3.0 %collective-permute-done.24 = f32[88,256]{1,0:T(8,128)S(1)} collective-permute-done((f32[88,256]{1,0:T(8,128)S(1)}, f32[88,256]{1,0:T(8,128)S(1)}, u32[]{:S(2)}, u32[]{:S(2)}) %collective-permute-start.24) | collective-permute-done | bytes 90144 | tf_op jit(solution)/shard_map/ppermute | solution.py:60
  64.9 0.1 collective-permute-start.26
  65.0 0.7 fusion
  65.6 0.5 collective-permute-done.26.refs_1_
  66.2 1.4 %shard_map.93 = f32[3,64,64]{2,1,0:T(8,128)} custom-call(f32[24,256]{1,0:T(8,128)S(1)} %slice_add_fusion.3.refs_0_, f32[24,256]{1,0:T(8,128)S(1)} %collective-permute-done.26.refs_1_), custom_call_target="tpu_custom_call" | custom-call | tf_op jit(solution)/shard_map/pallas_call | solution.py:71
  (25 shorter events, 0.3 us)
Async XLA Ops:
  0.6 10.5 %collective-permute-start.3 = (f32[64,256]{1,0:T(8,128)}, f32[64,256]{1,0:T(8,128)S(1)}, u32[]{:S(2)}, u32[]{:S(2)}) collective-permute-start(f32[64,256]{1,0:T(8,128)} %refs_4_.1), channel_id=1, source_target_pairs={{2,0},{3,1},{0,2},{1,3},{6,4},{7,5},{4,6},{5,7},{10,8},{11,9},{8,1... | collective-permute-start | bytes 196616 | tf_op jit(solution)/shard_map/ppermute | solution.py:54
  4.7 6.4 %collective-permute-start = (f32[64,256]{1,0:T(8,128)}, f32[64,256]{1,0:T(8,128)S(1)}, u32[]{:S(2)}, u32[]{:S(2)}) collective-permute-start(f32[64,256]{1,0:T(8,128)} %refs_5_.1), channel_id=1, source_target_pairs={{8,0},{12,4},{0,8},{4,12},{24,16},{28,20},{16,24},{20,28},{9,1},{1... | collective-permute-start | bytes 196616 | tf_op jit(solution)/shard_map/ppermute | solution.py:54
  6.2 5.4 %collective-permute-start.2 = (f32[64,256]{1,0:T(8,128)}, f32[64,256]{1,0:T(8,128)S(1)}, u32[]{:S(2)}, u32[]{:S(2)}) collective-permute-start(f32[64,256]{1,0:T(8,128)} %refs_5_.1), channel_id=1, source_target_pairs={{24,0},{28,4},{16,8},{20,12},{8,16},{12,20},{0,24},{4,28},{25,1},{... | collective-permute-start | bytes 196616 | tf_op jit(solution)/shard_map/ppermute | solution.py:54
  7.7 4.6 %collective-permute-start.1 = (f32[64,256]{1,0:T(8,128)}, f32[64,256]{1,0:T(8,128)S(1)}, u32[]{:S(2)}, u32[]{:S(2)}) collective-permute-start(f32[64,256]{1,0:T(8,128)} %refs_5_.1), channel_id=1, source_target_pairs={{16,0},{20,4},{24,8},{28,12},{0,16},{4,20},{8,24},{12,28},{17,1},{... | collective-permute-start | bytes 196616 | tf_op jit(solution)/shard_map/ppermute | solution.py:54
  12.3 2.5 %collective-permute-start.4 = (f32[4,64,256]{2,1,0:T(8,128)S(1)}, f32[4,64,256]{2,1,0:T(8,128)S(1)}, u32[]{:S(2)}, u32[]{:S(2)}) collective-permute-start(f32[4,64,256]{2,1,0:T(8,128)S(1)} %shard_map.78.refs_0_.refs_1_), channel_id=1, source_target_pairs={{4,0},{0,4},{12,8},{8,12},{20,16},{16,20},{28,24},{24,28},{5,1},{1... | collective-permute-start | bytes 786440 | tf_op jit(solution)/shard_map/ppermute | solution.py:54
  12.4 7.7 %collective-permute-start.8 = (f32[2,64,256]{2,1,0:T(8,128)S(1)}, f32[2,64,256]{2,1,0:T(8,128)S(1)}, u32[]{:S(2)}, u32[]{:S(2)}) collective-permute-start(f32[2,64,256]{2,1,0:T(8,128)S(1)} %shard_map.80.refs_4_.refs_0_), channel_id=1, source_target_pairs={{1,0},{0,1},{3,2},{2,3},{5,4},{4,5},{7,6},{6,7},{9,8},{8,9},{11,10... | collective-permute-start | bytes 393224 | tf_op jit(solution)/shard_map/ppermute | solution.py:54
  15.6 6.9 %collective-permute-start.5 = (f32[64,256]{1,0:T(8,128)S(1)}, f32[64,256]{1,0:T(8,128)S(1)}, u32[]{:S(2)}, u32[]{:S(2)}) collective-permute-start(f32[64,256]{1,0:T(8,128)S(1)} %get-tuple-element.29), channel_id=1, source_target_pairs={{0,3},{1,2},{2,1},{3,0},{4,7},{5,6},{6,5},{7,4},{8,11},{9,10},{10,... | collective-permute-start | bytes 196616 | tf_op jit(solution)/shard_map/ppermute | solution.py:60
  16.1 8.1 %collective-permute-start.6 = (f32[64,256]{1,0:T(8,128)S(1)}, f32[64,256]{1,0:T(8,128)S(1)}, u32[]{:S(2)}, u32[]{:S(2)}) collective-permute-start(f32[64,256]{1,0:T(8,128)S(1)} %get-tuple-element.30), channel_id=1, source_target_pairs={{0,2},{1,3},{2,0},{3,1},{4,6},{5,7},{6,4},{7,5},{8,10},{9,11},{10,... | collective-permute-start | bytes 196616 | tf_op jit(solution)/shard_map/ppermute | solution.py:60
  17.8 6.5 %collective-permute-start.7 = (f32[64,256]{1,0:T(8,128)S(1)}, f32[64,256]{1,0:T(8,128)S(1)}, u32[]{:S(2)}, u32[]{:S(2)}) collective-permute-start(f32[64,256]{1,0:T(8,128)S(1)} %get-tuple-element.31), channel_id=1, source_target_pairs={{0,1},{1,0},{2,3},{3,2},{4,5},{5,4},{6,7},{7,6},{8,9},{9,8},{10,11... | collective-permute-start | bytes 196616 | tf_op jit(solution)/shard_map/ppermute | solution.py:60
  22.5 9.1 %collective-permute-start.13 = (f32[4,64,256]{2,1,0:T(8,128)S(1)}, f32[4,64,256]{2,1,0:T(8,128)S(1)}, u32[]{:S(2)}, u32[]{:S(2)}) collective-permute-start(f32[4,64,256]{2,1,0:T(8,128)S(1)} %get-tuple-element.32.refs_4_), channel_id=1, source_target_pairs={{4,0},{0,4},{12,8},{8,12},{20,16},{16,20},{28,24},{24,28},{5,1},{1... | collective-permute-start | bytes 786440 | tf_op jit(solution)/shard_map/ppermute | solution.py:54
  24.3 5.4 %collective-permute-start.11 = (f32[64,256]{1,0:T(8,128)S(1)}, f32[64,256]{1,0:T(8,128)S(1)}, u32[]{:S(2)}, u32[]{:S(2)}) collective-permute-start(f32[64,256]{1,0:T(8,128)S(1)} %shard_map.83.refs_0_.refs_5_), channel_id=1, source_target_pairs={{24,0},{28,4},{16,8},{20,12},{8,16},{12,20},{0,24},{4,28},{25,1},{... | collective-permute-start | bytes 196616 | tf_op jit(solution)/shard_map/ppermute | solution.py:54
  26.6 4.3 %collective-permute-start.10 = (f32[64,256]{1,0:T(8,128)S(1)}, f32[64,256]{1,0:T(8,128)S(1)}, u32[]{:S(2)}, u32[]{:S(2)}) collective-permute-start(f32[64,256]{1,0:T(8,128)S(1)} %shard_map.83.refs_0_.refs_5_), channel_id=1, source_target_pairs={{16,0},{20,4},{24,8},{28,12},{0,16},{4,20},{8,24},{12,28},{17,1},{... | collective-permute-start | bytes 196616 | tf_op jit(solution)/shard_map/ppermute | solution.py:54
  27.2 4.3 %collective-permute-start.9 = (f32[64,256]{1,0:T(8,128)S(1)}, f32[64,256]{1,0:T(8,128)S(1)}, u32[]{:S(2)}, u32[]{:S(2)}) collective-permute-start(f32[64,256]{1,0:T(8,128)S(1)} %shard_map.83.refs_0_.refs_5_), channel_id=1, source_target_pairs={{8,0},{12,4},{0,8},{4,12},{24,16},{28,20},{16,24},{20,28},{9,1},{1... | collective-permute-start | bytes 196616 | tf_op jit(solution)/shard_map/ppermute | solution.py:54
  31.5 1.6 %collective-permute-start.12 = (f32[4,64,256]{2,1,0:T(8,128)S(1)}, f32[4,64,256]{2,1,0:T(8,128)S(1)}, u32[]{:S(2)}, u32[]{:S(2)}) collective-permute-start(f32[4,64,256]{2,1,0:T(8,128)S(1)} %shard_map.84.refs_0_.refs_1_), channel_id=1, source_target_pairs={{4,0},{0,4},{12,8},{8,12},{20,16},{16,20},{28,24},{24,28},{5,1},{1... | collective-permute-start | bytes 786440 | tf_op jit(solution)/shard_map/ppermute | solution.py:54
  31.6 6.7 %collective-permute-start.17 = (f32[2,64,256]{2,1,0:T(8,128)S(1)}, f32[2,64,256]{2,1,0:T(8,128)S(1)}, u32[]{:S(2)}, u32[]{:S(2)}) collective-permute-start(f32[2,64,256]{2,1,0:T(8,128)S(1)} %get-tuple-element.39), channel_id=1, source_target_pairs={{8,0},{12,4},{0,8},{4,12},{24,16},{28,20},{16,24},{20,28},{9,1},{1... | collective-permute-start | bytes 393224 | tf_op jit(solution)/shard_map/ppermute | solution.py:54
  33.9 6.9 %collective-permute-start.14 = (f32[64,256]{1,0:T(8,128)S(1)}, f32[64,256]{1,0:T(8,128)S(1)}, u32[]{:S(2)}, u32[]{:S(2)}) collective-permute-start(f32[64,256]{1,0:T(8,128)S(1)} %get-tuple-element.34), channel_id=1, source_target_pairs={{0,3},{1,2},{2,1},{3,0},{4,7},{5,6},{6,5},{7,4},{8,11},{9,10},{10,... | collective-permute-start | bytes 196616 | tf_op jit(solution)/shard_map/ppermute | solution.py:60
  35.7 7.1 %collective-permute-start.15 = (f32[64,256]{1,0:T(8,128)S(1)}, f32[64,256]{1,0:T(8,128)S(1)}, u32[]{:S(2)}, u32[]{:S(2)}) collective-permute-start(f32[64,256]{1,0:T(8,128)S(1)} %get-tuple-element.35), channel_id=1, source_target_pairs={{0,2},{1,3},{2,0},{3,1},{4,6},{5,7},{6,4},{7,5},{8,10},{9,11},{10,... | collective-permute-start | bytes 196616 | tf_op jit(solution)/shard_map/ppermute | solution.py:60
  35.7 7.1 %collective-permute-start.16 = (f32[64,256]{1,0:T(8,128)S(1)}, f32[64,256]{1,0:T(8,128)S(1)}, u32[]{:S(2)}, u32[]{:S(2)}) collective-permute-start(f32[64,256]{1,0:T(8,128)S(1)} %get-tuple-element.36), channel_id=1, source_target_pairs={{0,1},{1,0},{2,3},{3,2},{4,5},{5,4},{6,7},{7,6},{8,9},{9,8},{10,11... | collective-permute-start | bytes 196616 | tf_op jit(solution)/shard_map/ppermute | solution.py:60
  38.4 4.4 %collective-permute-start.18 = (f32[1,64,256]{2,1,0:T(8,128)S(1)}, f32[1,64,256]{2,1,0:T(8,128)S(1)}, u32[]{:S(2)}, u32[]{:S(2)}) collective-permute-start(f32[1,64,256]{2,1,0:T(8,128)S(1)} %get-tuple-element.41), channel_id=1, source_target_pairs={{16,0},{20,4},{24,8},{28,12},{0,16},{4,20},{8,24},{12,28},{17,1},{... | collective-permute-start | bytes 196616 | tf_op jit(solution)/shard_map/ppermute | solution.py:54
  43.3 6.3 %collective-permute-start.21 = (f32[112,256]{1,0:T(8,128)S(1)}, f32[112,256]{1,0:T(8,128)S(1)}, u32[]{:S(2)}, u32[]{:S(2)}) collective-permute-start(f32[112,256]{1,0:T(8,128)S(1)} %shard_map.89.refs_0_), channel_id=1, source_target_pairs={{24,0},{28,4},{16,8},{20,12},{8,16},{12,20},{0,24},{4,28},{25,1},{... | collective-permute-start | bytes 344072 | tf_op jit(solution)/shard_map/ppermute | solution.py:54
  45.5 6.2 %collective-permute-start.20 = (f32[112,256]{1,0:T(8,128)S(1)}, f32[112,256]{1,0:T(8,128)S(1)}, u32[]{:S(2)}, u32[]{:S(2)}) collective-permute-start(f32[112,256]{1,0:T(8,128)S(1)} %shard_map.89.refs_0_), channel_id=1, source_target_pairs={{16,0},{20,4},{24,8},{28,12},{0,16},{4,20},{8,24},{12,28},{17,1},{... | collective-permute-start | bytes 344072 | tf_op jit(solution)/shard_map/ppermute | solution.py:54
  46.2 5.6 %collective-permute-start.19 = (f32[112,256]{1,0:T(8,128)S(1)}, f32[112,256]{1,0:T(8,128)S(1)}, u32[]{:S(2)}, u32[]{:S(2)}) collective-permute-start(f32[112,256]{1,0:T(8,128)S(1)} %shard_map.89.refs_0_), channel_id=1, source_target_pairs={{8,0},{12,4},{0,8},{4,12},{24,16},{28,20},{16,24},{20,28},{9,1},{1... | collective-permute-start | bytes 344072 | tf_op jit(solution)/shard_map/ppermute | solution.py:54
  51.8 1.9 %collective-permute-start.22 = (f32[4,112,256]{2,1,0:T(8,128)S(1)}, f32[4,112,256]{2,1,0:T(8,128)S(1)}, u32[]{:S(2)}, u32[]{:S(2)}) collective-permute-start(f32[4,112,256]{2,1,0:T(8,128)S(1)} %shard_map.90.refs_0_.refs_1_), channel_id=1, source_target_pairs={{4,0},{0,4},{12,8},{8,12},{20,16},{16,20},{28,24},{24,28},{5,1},{1... | collective-permute-start | bytes 1376264 | tf_op jit(solution)/shard_map/ppermute | solution.py:54
  54.5 7.4 %collective-permute-start.23 = (f32[88,256]{1,0:T(8,128)S(1)}, f32[88,256]{1,0:T(8,128)S(1)}, u32[]{:S(2)}, u32[]{:S(2)}) collective-permute-start(f32[88,256]{1,0:T(8,128)S(1)} %get-tuple-element.43), channel_id=1, source_target_pairs={{0,3},{1,2},{2,1},{3,0},{4,7},{5,6},{6,5},{7,4},{8,11},{9,10},{10,... | collective-permute-start | bytes 270344 | tf_op jit(solution)/shard_map/ppermute | solution.py:60
  56.2 8.6 %collective-permute-start.24 = (f32[88,256]{1,0:T(8,128)S(1)}, f32[88,256]{1,0:T(8,128)S(1)}, u32[]{:S(2)}, u32[]{:S(2)}) collective-permute-start(f32[88,256]{1,0:T(8,128)S(1)} %get-tuple-element.44), channel_id=1, source_target_pairs={{0,2},{1,3},{2,0},{3,1},{4,6},{5,7},{6,4},{7,5},{8,10},{9,11},{10,... | collective-permute-start | bytes 270344 | tf_op jit(solution)/shard_map/ppermute | solution.py:60
  56.2 8.6 %collective-permute-start.25 = (f32[88,256]{1,0:T(8,128)S(1)}, f32[88,256]{1,0:T(8,128)S(1)}, u32[]{:S(2)}, u32[]{:S(2)}) collective-permute-start(f32[88,256]{1,0:T(8,128)S(1)} %get-tuple-element.45), channel_id=1, source_target_pairs={{0,1},{1,0},{2,3},{3,2},{4,5},{5,4},{6,7},{7,6},{8,9},{9,8},{10,11... | collective-permute-start | bytes 270344 | tf_op jit(solution)/shard_map/ppermute | solution.py:60
  64.9 1.3 %collective-permute-start.26 = (f32[24,256]{1,0:T(8,128)S(1)}, f32[24,256]{1,0:T(8,128)S(1)}, u32[]{:S(2)}, u32[]{:S(2)}) collective-permute-start(f32[24,256]{1,0:T(8,128)S(1)} %slice_add_fusion.3.refs_0_), channel_id=1, source_target_pairs={{4,0},{0,4},{12,8},{8,12},{20,16},{16,20},{28,24},{24,28},{5,1},{1... | collective-permute-start | bytes 73736 | tf_op jit(solution)/shard_map/ppermute | solution.py:54

commit v15 on v14

--- a/solution.py
+++ b/solution.py
@@ -102,13 +102,9 @@
     return [fetch(piece, axis, shift) for shift in range(2, lax.axis_size(axis), 2)]
 
 
-def gather_evens(piece, axis, before=()):
-    return stack_after([piece] + fetch_evens(piece, axis), before)
-
-
-def gather_odds(evens, axis):
+def fetch_odds(evens, axis):
     size = lax.axis_size(axis)
-    assert size > 1 and size & (size - 1) == 0
+    assert size > 2 and size & (size - 1) == 0
     return fetch(evens, axis, 1)
 
 
@@ -230,15 +226,14 @@
     )(rows, cols, tile_count, entries, x_piece, y_piece)
 
 
-def half_products(half, span, pieces_ref, dense_ref, digits, block):
-    _, depth, width = dense_ref.shape
-    tile_len, half_depth = width // 2, depth // 2
+def part_products(start, span, dense_ref, digits, block):
+    tile_len = dense_ref.shape[2] // 2
     high = middle = low = 0.0
-    for start in range(0, half_depth, EXACT_DEPTH):
-        stop = min(start + EXACT_DEPTH, half_depth)
+    for begin in range(0, digits.shape[1], EXACT_DEPTH):
+        end = min(begin + EXACT_DEPTH, digits.shape[1])
         products = jnp.dot(
-            digits[:, start:stop],
-            dense_ref[block, half * half_depth + start : half * half_depth + stop, :],
+            digits[:, begin:end],
+            dense_ref[block, start + begin : start + end, :],
             preferred_element_type=jnp.float32,
         )
         products = reduce_centered(products)
@@ -248,18 +243,19 @@
     return high, middle, low
 
 
-def fill_digits(span, pieces_ref, digits):
-    piece_len = pieces_ref.shape[2]
-    for d in range(pieces_ref.shape[0]):
-        vector = reduce_centered(pieces_ref[d, :span, :])
+def fill_digits(span, pieces, digits):
+    for d, piece in enumerate(pieces):
+        piece_len = piece.shape[1]
+        vector = reduce_centered(piece[:span])
         digits[:, d * piece_len : (d + 1) * piece_len] = stacked_digits(vector)
 
 
-def first_half_kernel(span, pieces_ref, dense_ref, sums_ref, digits):
-    fill_digits(span, pieces_ref, digits)
+def first_part_kernel(span, own_ref, evens_ref, odd_ref, dense_ref, sums_ref, digits):
+    evens = [evens_ref[index] for index in range(evens_ref.shape[0])]
+    fill_digits(span, [own_ref[...], *evens, odd_ref[...]], digits)
     tile_len = dense_ref.shape[2] // 2
     for block in range(dense_ref.shape[0]):
-        parts = half_products(0, span, pieces_ref, dense_ref, digits, block)
+        parts = part_products(0, span, dense_ref, digits, block)
         for index, part in enumerate(parts):
             sums_ref[index, :, block * tile_len : (block + 1) * tile_len] = part
 
@@ -269,51 +265,52 @@
     return jnp.where(lax.axis_index("row") % 2 == 0, packed[:rows], packed[rows:])
 
 
-def second_half_kernel(span, pieces_ref, evens_ref, sums_ref, dense_ref, *refs):
+def second_part_kernel(span, odds_ref, own_ref, evens_ref, odd_ref, sums_ref, dense_ref, *refs):
     outs, digits = refs[:-1], refs[-1]
     n_col = len(outs)
-    fill_digits(span, pieces_ref, digits)
-    row_blocks, _, width = dense_ref.shape
+    fill_digits(span, [odds_ref[index] for index in range(odds_ref.shape[0])], digits)
+    row_blocks, depth, width = dense_ref.shape
     tile_len = width // 2
     piece_blocks = row_blocks // n_col
     for e in reversed(range(n_col)):
         for sub in range(piece_blocks):
             block = e * piece_blocks + sub
-            parts = half_products(1, span, pieces_ref, dense_ref, digits, block)
+            parts = part_products(depth - digits.shape[1], span, dense_ref, digits, block)
             parts = (
                 part + sums_ref[index, :, block * tile_len : (block + 1) * tile_len]
                 for index, part in enumerate(parts)
             )
             outs[e][:span, sub * tile_len : (sub + 1) * tile_len] = combine(*parts)
     if outs[0].shape[0] > span:
-        packed = jnp.sum(pieces_ref[:, span:, :], 0) + jnp.sum(evens_ref[:, span:, :], 0)
+        packed = own_ref[span:, :] + odd_ref[span:, :]
+        packed = packed + jnp.sum(evens_ref[:, span:, :], 0) + jnp.sum(odds_ref[:, span:, :], 0)
         packed = half_of_core(packed)
         for out in outs:
             out[span:, :] = packed
 
 
-def dense_first(evens, span, dense):
-    row_blocks, depth, width = dense.shape
+def dense_first(known, span, dense):
+    row_blocks, _, width = dense.shape
+    columns = (known[1].shape[0] + 2) * known[0].shape[1]
     return call(
-        functools.partial(first_half_kernel, span),
-        [evens, dense],
+        functools.partial(first_part_kernel, span),
+        [*known, dense],
         [held(3, span, row_blocks * width // 2)],
-        scratch=[pltpu.VMEM((2 * span, depth // 2), jnp.bfloat16)],
+        scratch=[pltpu.VMEM((2 * span, columns), jnp.bfloat16)],
         limit=VMEM_LIMIT,
         flops=2 * span * dense.size,
     )[0]
 
 
-def dense_second(odds, evens, sums, span, n_col, dense, before):
-    _, depth, _ = dense.shape
+def dense_second(odds, known, sums, span, n_col, dense, before):
     _, rows, piece_len = odds.shape
     return list(
         call(
-            functools.partial(second_half_kernel, span),
-            [odds, evens, sums, dense],
+            functools.partial(second_part_kernel, span),
+            [odds, *known, sums, dense],
             [held(span + (rows - span) // 2, piece_len)] * n_col,
             before,
-            scratch=[pltpu.VMEM((2 * span, depth // 2), jnp.bfloat16)],
+            scratch=[pltpu.VMEM((2 * span, odds.shape[0] * piece_len), jnp.bfloat16)],
             limit=VMEM_LIMIT,
             flops=2 * span * dense.size,
         )
@@ -394,9 +391,10 @@
     return reduce_centered(summed).reshape(span, blocks * tile_len)
 
 
-def sparse_second(odds, evens, span, n_col, positions, a_digits):
+def sparse_second(odds, known, span, n_col, positions, a_digits):
     rows, cols, count = positions
-    pieces = [*evens, *odds]
+    own, evens, odd = known
+    pieces = [own, *evens, odd, *odds]
     piece_len = pieces[0].shape[1]
     blocks = n_col * piece_len // a_digits.shape[-1]
     vector = reduce_centered(jnp.concatenate([piece[:span] for piece in pieces], 1))
@@ -503,30 +501,28 @@
         positions, a_digits = sparse_tiles(tiles, sizes)
         x_own, y_own, before = block_x, block_y, []
 
-    def multiply_evens(evens):
-        return dense_first(evens, span, dense) if is_dense else evens
-
-    def multiply_odds(odds, evens, sums, before):
+    def multiply(own, piece, before=(), stack_before=()):
+        evens = fetch_evens(piece, "row")
+        odd = fetch(piece, "row", 1)
+        evens = stack_after(evens, [odd, *stack_before])
+        odds = fetch_odds(evens, "row")
+        known = [own, evens, odd]
         if is_dense:
-            return dense_second(odds, evens, sums, span, n_col, dense, before)
-        return sparse_second(odds, evens, span, n_col, positions, a_digits)
-
-    def multiply(evens, before):
-        return multiply_odds(gather_odds(evens, "row"), evens, multiply_evens(evens), before)
-
-    y_came = fetch_evens(block_y, "row")
+            sums = dense_first(known, span, dense)
+            return dense_second(odds, known, sums, span, n_col, dense, before)
+        return sparse_second(odds, known, span, n_col, positions, a_digits)
+
     x_came = fetch_evens(block_x, "col")
-    evens = stack_after([y_own] + y_came, [*before, *x_came])
     x_evens = stack_after([x_own] + x_came)
-    outs = multiply(evens, [x_evens])
-    x_pairs = [x_evens, gather_odds(x_evens, "col")]
+    outs = multiply(y_own, block_y, [x_evens], [*before, *x_came])
+    x_pairs = [x_evens, fetch_odds(x_evens, "col")]
     if is_dense:
         w_evens, w_odds = dense_left(x_pairs, n_row, dense, [outs[0]])
     else:
         w_evens, w_odds = sparse_left(x_pairs, n_row, positions, a_digits)
     vector_1 = sum_after(scatter_pieces(outs, "col"), [w_odds])
-    w_came = fetch(w_odds, "row", 1)
-    outs = multiply(gather_evens(vector_1, "row"), [w_came])
+    w_came = fetch(sum_after([w_odds], [vector_1]), "row", 1)
+    outs = multiply(vector_1, vector_1, [w_came])
     pieces = scatter_pieces(outs, "col")
     w_kept, shift, before = w_evens, 2, []
     while shift < n_row:
@@ -534,7 +530,7 @@
         w_came = fetch(w_sent, "row", shift)
         shift, before = 2 * shift, [outs[0]]
     vector_2 = append_projections([w_kept[0], w_came[0]], pieces, [y_own, vector_1])
-    outs = multiply(gather_evens(vector_2, "row"), [])
+    outs = multiply(vector_2, vector_2)
     pieces = scatter_pieces(outs, "col")
     terms = functools.reduce(jnp.add, [piece[span:] for piece in pieces])
     vector_3 = functools.reduce(jnp.add, [piece[:span] for piece in pieces])

time: 67.8 us -> 68.8 us (1.015)
  starting transfers between devices: 32.2 us -> 34 us
    ppermute x18 -> x21, starting transfers between devices: 18.8 us -> 20.6 us  [fetch(): lax.ppermute(piece, axis, [(partner(i, shift, size), i) for i in range(si...]
    ppermute x18 -> x21, waiting for transfers between devices: 11.3 us -> 11.1 us  [fetch(): lax.ppermute(piece, axis, [(partner(i, shift, size), i) for i in range(si...]
    pallas_call x16 -> x17, Pallas kernels: 9.1 us -> 9.23 us  [call(): pl.pallas_call(body, in_specs=[vmem] * len(operands) + [pl.BlockSpec(memo...]
  transfers between devices with their start and end apart: 27 -> 30, of which waited for: 14 -> 15; matrix products, arithmetic and copies ran while one was open for 1% -> 1% of each run, Pallas kernels for 13% -> 12%
where the time goes in v15:
time: 68.8 us; the launch traced here: 68.4 us
  starting transfers between devices  34 us (49%)
  waiting for transfers between devices  21.3 us (31%)
  Pallas kernels  11 us (16%)
  between operations  1.49 us (2%)
    ppermute x21, starting transfers between devices, fetch(): lax.ppermute(piece, axis, [(partner(i, shift, size), i) for i in range(si...  20.6 us
    ppermute x9, starting transfers between devices, scatter_pieces(): lax.ppermute(pieces[shift], axis, [(i, partner(i, shift, size)) for i in...  13.4 us
    ppermute x21, waiting for transfers between devices, fetch(): lax.ppermute(piece, axis, [(partner(i, shift, size), i) for i in range(si...  11.1 us
    ppermute x9, waiting for transfers between devices, scatter_pieces(): lax.ppermute(pieces[shift], axis, [(i, partner(i, shift, size)) for i in...  10.2 us
    pallas_call x17, Pallas kernels, call(): pl.pallas_call(body, in_specs=[vmem] * len(operands) + [pl.BlockSpec(memo...  9.23 us
    pallas_call x1, Pallas kernels, build_dense(): pl.pallas_call(functools.partial(build_kernel, (*sizes, group)), in_specs...  1.76 us
  transfers between devices with their start and end apart: 30, of which 15 were waited for; matrix products, arithmetic and copies ran while one was open for 1% of the time, Pallas kernels for 12%

profile of v15, /device:TPU:0, one launch (start us, length us, event | category | flops | bytes accessed | tf_op | source)
XLA Modules:
  0.0 68.4 jit_solution(12034922038473061687)
XLA Ops:
  0.6 4.1 %collective-permute-start.4 = (f32[64,256]{1,0:T(8,128)}, f32[64,256]{1,0:T(8,128)S(1)}, u32[]{:S(2)}, u32[]{:S(2)}) collective-permute-start(f32[64,256]{1,0:T(8,128)} %refs_4_.1), channel_id=1, source_target_pairs={{2,0},{3,1},{0,2},{1,3},{6,4},{7,5},{4,6},{5,7},{10,8},{11,9},{8,1... | collective-permute-start | bytes 196616 | tf_op jit(solution)/shard_map/ppermute | solution.py:54
  4.7 2.4 %collective-permute-start.2 = (f32[64,256]{1,0:T(8,128)}, f32[64,256]{1,0:T(8,128)S(1)}, u32[]{:S(2)}, u32[]{:S(2)}) collective-permute-start(f32[64,256]{1,0:T(8,128)} %refs_5_.1), channel_id=1, source_target_pairs={{24,0},{28,4},{16,8},{20,12},{8,16},{12,20},{0,24},{4,28},{25,1},{... | collective-permute-start | bytes 196616 | tf_op jit(solution)/shard_map/ppermute | solution.py:54
  7.2 0.5 collective-permute-start.1
  7.7 0.5 collective-permute-start
  8.9 1.8 %shard_map.77 = (bf16[8,2048,256]{2,1,0:T(8,128)(2,1)S(1)}, f32[64,256]{1,0:T(8,128)S(1)}, f32[64,256]{1,0:T(8,128)S(1)}, f32[8,128]{1,0:T(8,128)S(1)}) custom-call(s32[1,1,64]{2,1,0:T(1,128)} %refs_0_.1, s32[1,1,64]{2,1,0:T(1,128)} %refs_1_.1, s32[1,1]{1,0:T(1,128)S(6)} %copy.8.refs_2_, f32[1,1,64,128,128]{4,3,2,1,0:T(8,128)} %refs_3_.1, ...), custom_call_target="tpu_custom_call" | custom-call | flops 8388608 | bytes 8388608 | tf_op jit(solution)/shard_map/pallas_call | solution.py:207
  10.7 1.0 %collective-permute-done.1.refs_1_ = f32[64,256]{1,0:T(8,128)S(1)} collective-permute-done((f32[64,256]{1,0:T(8,128)}, f32[64,256]{1,0:T(8,128)S(1)}, u32[]{:S(2)}, u32[]{:S(2)}) %collective-permute-start.1) | collective-permute-done | bytes 65568 | tf_op jit(solution)/shard_map/ppermute | solution.py:54
  11.7 0.5 collective-permute-done.refs_0_
  12.3 2.3 %collective-permute-start.9 = (f32[2,64,256]{2,1,0:T(8,128)S(1)}, f32[2,64,256]{2,1,0:T(8,128)S(1)}, u32[]{:S(2)}, u32[]{:S(2)}) collective-permute-start(f32[2,64,256]{2,1,0:T(8,128)S(1)} %shard_map.80.refs_6_.refs_0_), channel_id=1, source_target_pairs={{1,0},{0,1},{3,2},{2,3},{5,4},{4,5},{7,6},{6,7},{9,8},{8,9},{11,10... | collective-permute-start | bytes 393224 | tf_op jit(solution)/shard_map/ppermute | solution.py:54
  14.6 0.9 %shard_map.79.refs_4_ = f32[3,64,1024]{2,1,0:T(8,128)S(1)} custom-call(f32[64,256]{1,0:T(8,128)S(1)} %get-tuple-element.25.refs_0_.refs_1_.refs_4_, f32[3,64,256]{2,1,0:T(8,128)S(1)} %shard_map.78.refs_1_.refs_2_, f32[64,256]{1,0:T(8,128)S(1)} %collective-permute-done.3.refs_3_.refs_2_, bf16[8,2048,256]{2,1,0:T(8,128)(2,1)S(1)} %get-tuple-element.26.refs_3_.refs_5_.refs_2_), custom_call_target="tpu_custom_call" | custom-call | flops 536870912 | tf_op jit(solution)/shard_map/pallas_call | solution.py:71
  15.5 0.7 shard_map.81
  16.3 1.5 %collective-permute-start.7 = (f32[64,256]{1,0:T(8,128)S(1)}, f32[64,256]{1,0:T(8,128)S(1)}, u32[]{:S(2)}, u32[]{:S(2)}) collective-permute-start(f32[64,256]{1,0:T(8,128)S(1)} %get-tuple-element.30), channel_id=1, source_target_pairs={{0,2},{1,3},{2,0},{3,1},{4,6},{5,7},{6,4},{7,5},{8,10},{9,11},{10,... | collective-permute-start | bytes 196616 | tf_op jit(solution)/shard_map/ppermute | solution.py:60
  17.8 2.9 %collective-permute-start.8 = (f32[64,256]{1,0:T(8,128)S(1)}, f32[64,256]{1,0:T(8,128)S(1)}, u32[]{:S(2)}, u32[]{:S(2)}) collective-permute-start(f32[64,256]{1,0:T(8,128)S(1)} %get-tuple-element.31), channel_id=1, source_target_pairs={{0,1},{1,0},{2,3},{3,2},{4,5},{5,4},{6,7},{7,6},{8,9},{9,8},{10,11... | collective-permute-start | bytes 196616 | tf_op jit(solution)/shard_map/ppermute | solution.py:60
  20.7 2.4 %shard_map.82 = (f32[4,64,256]{2,1,0:T(8,128)S(1)}, f32[4,64,256]{2,1,0:T(8,128)S(1)}) custom-call(f32[2,64,256]{2,1,0:T(8,128)S(1)} %shard_map.80.refs_6_.refs_0_, f32[2,64,256]{2,1,0:T(8,128)S(1)} %collective-permute-done.9.refs_1_, bf16[8,2048,256]{2,1,0:T(8,128)(2,1)S(1)} %get-tuple-element.26.refs_3_.refs_5_.refs_2_, ...), custom_call_target="tpu_custom_call" | custom-call | flops 1073741824 | tf_op jit(solution)/shard_map/pallas_call | solution.py:71
  23.1 1.2 %collective-permute-done.7.refs_2_ = f32[64,256]{1,0:T(8,128)S(1)} collective-permute-done((f32[64,256]{1,0:T(8,128)S(1)}, f32[64,256]{1,0:T(8,128)S(1)}, u32[]{:S(2)}, u32[]{:S(2)}) %collective-permute-start.7) | collective-permute-done | bytes 65568 | tf_op jit(solution)/shard_map/ppermute | solution.py:60
  24.5 0.5 collective-permute-start.13
  25.0 1.3 %collective-permute-start.12 = (f32[64,256]{1,0:T(8,128)S(1)}, f32[64,256]{1,0:T(8,128)S(1)}, u32[]{:S(2)}, u32[]{:S(2)}) collective-permute-start(f32[64,256]{1,0:T(8,128)S(1)} %shard_map.83.refs_0_.refs_1_.refs_5_), channel_id=1, source_target_pairs={{24,0},{28,4},{16,8},{20,12},{8,16},{12,20},{0,24},{4,28},{25,1},{... | collective-permute-start | bytes 196616 | tf_op jit(solution)/shard_map/ppermute | solution.py:54
  26.3 0.9 %collective-permute-start.11 = (f32[64,256]{1,0:T(8,128)S(1)}, f32[64,256]{1,0:T(8,128)S(1)}, u32[]{:S(2)}, u32[]{:S(2)}) collective-permute-start(f32[64,256]{1,0:T(8,128)S(1)} %shard_map.83.refs_0_.refs_1_.refs_5_), channel_id=1, source_target_pairs={{16,0},{20,4},{24,8},{28,12},{0,16},{4,20},{8,24},{12,28},{17,1},{... | collective-permute-start | bytes 196616 | tf_op jit(solution)/shard_map/ppermute | solution.py:54
  27.2 1.2 %collective-permute-start.10 = (f32[64,256]{1,0:T(8,128)S(1)}, f32[64,256]{1,0:T(8,128)S(1)}, u32[]{:S(2)}, u32[]{:S(2)}) collective-permute-start(f32[64,256]{1,0:T(8,128)S(1)} %shard_map.83.refs_0_.refs_1_.refs_5_), channel_id=1, source_target_pairs={{8,0},{12,4},{0,8},{4,12},{24,16},{28,20},{16,24},{20,28},{9,1},{1... | collective-permute-start | bytes 196616 | tf_op jit(solution)/shard_map/ppermute | solution.py:54
  28.4 2.0 %collective-permute-done.12.refs_2_ = f32[64,256]{1,0:T(8,128)S(1)} collective-permute-done((f32[64,256]{1,0:T(8,128)S(1)}, f32[64,256]{1,0:T(8,128)S(1)}, u32[]{:S(2)}, u32[]{:S(2)}) %collective-permute-start.12) | collective-permute-done | bytes 65568 | tf_op jit(solution)/shard_map/ppermute | solution.py:54
  30.5 0.9 %collective-permute-done.11.refs_1_ = f32[64,256]{1,0:T(8,128)S(1)} collective-permute-done((f32[64,256]{1,0:T(8,128)S(1)}, f32[64,256]{1,0:T(8,128)S(1)}, u32[]{:S(2)}, u32[]{:S(2)}) %collective-permute-start.11) | collective-permute-done | bytes 65568 | tf_op jit(solution)/shard_map/ppermute | solution.py:54
  31.3 0.1 collective-permute-done.10.refs_0_
  31.6 1.3 %collective-permute-start.19 = (f32[2,64,256]{2,1,0:T(8,128)S(1)}, f32[2,64,256]{2,1,0:T(8,128)S(1)}, u32[]{:S(2)}, u32[]{:S(2)}) collective-permute-start(f32[2,64,256]{2,1,0:T(8,128)S(1)} %get-tuple-element.39), channel_id=1, source_target_pairs={{8,0},{12,4},{0,8},{4,12},{24,16},{28,20},{16,24},{20,28},{9,1},{1... | collective-permute-start | bytes 393224 | tf_op jit(solution)/shard_map/ppermute | solution.py:54
  32.9 0.9 %shard_map.85.refs_4_ = f32[3,64,1024]{2,1,0:T(8,128)S(1)} custom-call(f32[64,256]{1,0:T(8,128)S(1)} %shard_map.83.refs_0_.refs_1_.refs_5_, f32[3,64,256]{2,1,0:T(8,128)S(1)} %shard_map.84.refs_1_.refs_2_, f32[64,256]{1,0:T(8,128)S(1)} %collective-permute-done.13.refs_3_.refs_2_, bf16[8,2048,256]{2,1,0:T(8,128)(2,1)S(1)} %get-tuple-element.26.refs_3_.refs_5_.refs_2_), custom_call_target="tpu_custom_call" | custom-call | flops 536870912 | tf_op jit(solution)/shard_map/pallas_call | solution.py:71
  33.9 0.7 shard_map.87
  34.5 1.8 %collective-permute-start.16 = (f32[64,256]{1,0:T(8,128)S(1)}, f32[64,256]{1,0:T(8,128)S(1)}, u32[]{:S(2)}, u32[]{:S(2)}) collective-permute-start(f32[64,256]{1,0:T(8,128)S(1)} %get-tuple-element.34), channel_id=1, source_target_pairs={{0,3},{1,2},{2,1},{3,0},{4,7},{5,6},{6,5},{7,4},{8,11},{9,10},{10,... | collective-permute-start | bytes 196616 | tf_op jit(solution)/shard_map/ppermute | solution.py:60
  36.3 0.4 collective-permute-start.17
  36.7 2.3 %collective-permute-start.18 = (f32[64,256]{1,0:T(8,128)S(1)}, f32[64,256]{1,0:T(8,128)S(1)}, u32[]{:S(2)}, u32[]{:S(2)}) collective-permute-start(f32[64,256]{1,0:T(8,128)S(1)} %get-tuple-element.36), channel_id=1, source_target_pairs={{0,1},{1,0},{2,3},{3,2},{4,5},{5,4},{6,7},{7,6},{8,9},{9,8},{10,11... | collective-permute-start | bytes 196616 | tf_op jit(solution)/shard_map/ppermute | solution.py:60
  39.0 1.4 %collective-permute-start.20 = (f32[1,64,256]{2,1,0:T(8,128)S(1)}, f32[1,64,256]{2,1,0:T(8,128)S(1)}, u32[]{:S(2)}, u32[]{:S(2)}) collective-permute-start(f32[1,64,256]{2,1,0:T(8,128)S(1)} %get-tuple-element.41), channel_id=1, source_target_pairs={{16,0},{20,4},{24,8},{28,12},{0,16},{4,20},{8,24},{12,28},{17,1},{... | collective-permute-start | bytes 196616 | tf_op jit(solution)/shard_map/ppermute | solution.py:54
  40.4 1.0 %collective-permute-done.16.refs_1_ = f32[64,256]{1,0:T(8,128)S(1)} collective-permute-done((f32[64,256]{1,0:T(8,128)S(1)}, f32[64,256]{1,0:T(8,128)S(1)}, u32[]{:S(2)}, u32[]{:S(2)}) %collective-permute-start.16) | collective-permute-done | bytes 65568 | tf_op jit(solution)/shard_map/ppermute | solution.py:60
  41.4 2.0 %collective-permute-done.17.refs_2_ = f32[64,256]{1,0:T(8,128)S(1)} collective-permute-done((f32[64,256]{1,0:T(8,128)S(1)}, f32[64,256]{1,0:T(8,128)S(1)}, u32[]{:S(2)}, u32[]{:S(2)}) %collective-permute-start.17) | collective-permute-done | bytes 65568 | tf_op jit(solution)/shard_map/ppermute | solution.py:60
  43.4 0.5 shard_map.90.refs_0_.refs_1_
  44.0 1.4 %collective-permute-start.23 = (f32[112,256]{1,0:T(8,128)S(1)}, f32[112,256]{1,0:T(8,128)S(1)}, u32[]{:S(2)}, u32[]{:S(2)}) collective-permute-start(f32[112,256]{1,0:T(8,128)S(1)} %shard_map.90.refs_0_.refs_1_), channel_id=1, source_target_pairs={{24,0},{28,4},{16,8},{20,12},{8,16},{12,20},{0,24},{4,28},{25,1},{... | collective-permute-start | bytes 344072 | tf_op jit(solution)/shard_map/ppermute | solution.py:54
  45.4 0.9 %collective-permute-start.22 = (f32[112,256]{1,0:T(8,128)S(1)}, f32[112,256]{1,0:T(8,128)S(1)}, u32[]{:S(2)}, u32[]{:S(2)}) collective-permute-start(f32[112,256]{1,0:T(8,128)S(1)} %shard_map.90.refs_0_.refs_1_), channel_id=1, source_target_pairs={{16,0},{20,4},{24,8},{28,12},{0,16},{4,20},{8,24},{12,28},{17,1},{... | collective-permute-start | bytes 344072 | tf_op jit(solution)/shard_map/ppermute | solution.py:54
  46.3 1.2 %collective-permute-start.21 = (f32[112,256]{1,0:T(8,128)S(1)}, f32[112,256]{1,0:T(8,128)S(1)}, u32[]{:S(2)}, u32[]{:S(2)}) collective-permute-start(f32[112,256]{1,0:T(8,128)S(1)} %shard_map.90.refs_0_.refs_1_), channel_id=1, source_target_pairs={{8,0},{12,4},{0,8},{4,12},{24,16},{28,20},{16,24},{20,28},{9,1},{1... | collective-permute-start | bytes 344072 | tf_op jit(solution)/shard_map/ppermute | solution.py:54
  47.5 3.4 %collective-permute-done.23.refs_2_ = f32[112,256]{1,0:T(8,128)S(1)} collective-permute-done((f32[112,256]{1,0:T(8,128)S(1)}, f32[112,256]{1,0:T(8,128)S(1)}, u32[]{:S(2)}, u32[]{:S(2)}) %collective-permute-start.23) | collective-permute-done | bytes 114720 | tf_op jit(solution)/shard_map/ppermute | solution.py:54
  50.9 2.0 %collective-permute-done.22.refs_1_ = f32[112,256]{1,0:T(8,128)S(1)} collective-permute-done((f32[112,256]{1,0:T(8,128)S(1)}, f32[112,256]{1,0:T(8,128)S(1)}, u32[]{:S(2)}, u32[]{:S(2)}) %collective-permute-start.22) | collective-permute-done | bytes 114720 | tf_op jit(solution)/shard_map/ppermute | solution.py:54
  52.9 0.1 collective-permute-start.25
  53.0 0.9 %shard_map.92.refs_4_ = f32[3,64,1024]{2,1,0:T(8,128)S(1)} custom-call(f32[112,256]{1,0:T(8,128)S(1)} %shard_map.90.refs_0_.refs_1_, f32[3,112,256]{2,1,0:T(8,128)S(1)} %shard_map.91.refs_1_.refs_2_, f32[112,256]{1,0:T(8,128)S(1)} %collective-permute-done.24.refs_3_.refs_2_, bf16[8,2048,256]{2,1,0:T(8,128)(2,1)S(1)} %get-tuple-element.26.refs_3_.refs_5_.refs_2_), custom_call_target="tpu_custom_call" | custom-call | flops 536870912 | tf_op jit(solution)/shard_map/pallas_call | solution.py:71
  54.0 0.7 collective-permute-done.25.refs_0_
  54.6 0.7 shard_map.93
  55.3 2.0 %collective-permute-start.26 = (f32[88,256]{1,0:T(8,128)S(1)}, f32[88,256]{1,0:T(8,128)S(1)}, u32[]{:S(2)}, u32[]{:S(2)}) collective-permute-start(f32[88,256]{1,0:T(8,128)S(1)} %get-tuple-element.43), channel_id=1, source_target_pairs={{0,3},{1,2},{2,1},{3,0},{4,7},{5,6},{6,5},{7,4},{8,11},{9,10},{10,... | collective-permute-start | bytes 270344 | tf_op jit(solution)/shard_map/ppermute | solution.py:60
  57.4 2.4 %collective-permute-start.28 = (f32[88,256]{1,0:T(8,128)S(1)}, f32[88,256]{1,0:T(8,128)S(1)}, u32[]{:S(2)}, u32[]{:S(2)}) collective-permute-start(f32[88,256]{1,0:T(8,128)S(1)} %get-tuple-element.45), channel_id=1, source_target_pairs={{0,1},{1,0},{2,3},{3,2},{4,5},{5,4},{6,7},{7,6},{8,9},{9,8},{10,11... | collective-permute-start | bytes 270344 | tf_op jit(solution)/shard_map/ppermute | solution.py:60
  59.8 3.0 %collective-permute-done.26 = f32[88,256]{1,0:T(8,128)S(1)} collective-permute-done((f32[88,256]{1,0:T(8,128)S(1)}, f32[88,256]{1,0:T(8,128)S(1)}, u32[]{:S(2)}, u32[]{:S(2)}) %collective-permute-start.26) | collective-permute-done | bytes 90144 | tf_op jit(solution)/shard_map/ppermute | solution.py:60
  62.7 3.0 %collective-permute-done.27 = f32[88,256]{1,0:T(8,128)S(1)} collective-permute-done((f32[88,256]{1,0:T(8,128)S(1)}, f32[88,256]{1,0:T(8,128)S(1)}, u32[]{:S(2)}, u32[]{:S(2)}) %collective-permute-start.27) | collective-permute-done | bytes 90144 | tf_op jit(solution)/shard_map/ppermute | solution.py:60
  65.7 0.1 collective-permute-start.29
  65.8 0.7 fusion
  66.5 0.5 collective-permute-done.29.refs_1_
  67.0 1.4 %shard_map.94 = f32[3,64,64]{2,1,0:T(8,128)} custom-call(f32[24,256]{1,0:T(8,128)S(1)} %slice_add_fusion.3.refs_0_, f32[24,256]{1,0:T(8,128)S(1)} %collective-permute-done.29.refs_1_), custom_call_target="tpu_custom_call" | custom-call | tf_op jit(solution)/shard_map/pallas_call | solution.py:71
  (32 shorter events, 0.6 us)
Async XLA Ops:
  0.6 10.0 %collective-permute-start.4 = (f32[64,256]{1,0:T(8,128)}, f32[64,256]{1,0:T(8,128)S(1)}, u32[]{:S(2)}, u32[]{:S(2)}) collective-permute-start(f32[64,256]{1,0:T(8,128)} %refs_4_.1), channel_id=1, source_target_pairs={{2,0},{3,1},{0,2},{1,3},{6,4},{7,5},{4,6},{5,7},{10,8},{11,9},{8,1... | collective-permute-start | bytes 196616 | tf_op jit(solution)/shard_map/ppermute | solution.py:54
  4.7 5.9 %collective-permute-start.2 = (f32[64,256]{1,0:T(8,128)}, f32[64,256]{1,0:T(8,128)S(1)}, u32[]{:S(2)}, u32[]{:S(2)}) collective-permute-start(f32[64,256]{1,0:T(8,128)} %refs_5_.1), channel_id=1, source_target_pairs={{24,0},{28,4},{16,8},{20,12},{8,16},{12,20},{0,24},{4,28},{25,1},{... | collective-permute-start | bytes 196616 | tf_op jit(solution)/shard_map/ppermute | solution.py:54
  7.2 4.5 %collective-permute-start.1 = (f32[64,256]{1,0:T(8,128)}, f32[64,256]{1,0:T(8,128)S(1)}, u32[]{:S(2)}, u32[]{:S(2)}) collective-permute-start(f32[64,256]{1,0:T(8,128)} %refs_5_.1), channel_id=1, source_target_pairs={{16,0},{20,4},{24,8},{28,12},{0,16},{4,20},{8,24},{12,28},{17,1},{... | collective-permute-start | bytes 196616 | tf_op jit(solution)/shard_map/ppermute | solution.py:54
  7.7 4.5 %collective-permute-start = (f32[64,256]{1,0:T(8,128)}, f32[64,256]{1,0:T(8,128)S(1)}, u32[]{:S(2)}, u32[]{:S(2)}) collective-permute-start(f32[64,256]{1,0:T(8,128)} %refs_5_.1), channel_id=1, source_target_pairs={{8,0},{12,4},{0,8},{4,12},{24,16},{28,20},{16,24},{20,28},{9,1},{1... | collective-permute-start | bytes 196616 | tf_op jit(solution)/shard_map/ppermute | solution.py:54
  8.2 3.9 %collective-permute-start.3 = (f32[64,256]{1,0:T(8,128)}, f32[64,256]{1,0:T(8,128)S(1)}, u32[]{:S(2)}, u32[]{:S(2)}) collective-permute-start(f32[64,256]{1,0:T(8,128)} %refs_5_.1), channel_id=1, source_target_pairs={{4,0},{0,4},{12,8},{8,12},{20,16},{16,20},{28,24},{24,28},{5,1},{1... | collective-permute-start | bytes 196616 | tf_op jit(solution)/shard_map/ppermute | solution.py:54
  12.2 3.3 %collective-permute-start.5 = (f32[3,64,256]{2,1,0:T(8,128)S(1)}, f32[3,64,256]{2,1,0:T(8,128)S(1)}, u32[]{:S(2)}, u32[]{:S(2)}) collective-permute-start(f32[3,64,256]{2,1,0:T(8,128)S(1)} %shard_map.78.refs_1_.refs_2_), channel_id=1, source_target_pairs={{4,0},{0,4},{12,8},{8,12},{20,16},{16,20},{28,24},{24,28},{5,1},{1... | collective-permute-start | bytes 589832 | tf_op jit(solution)/shard_map/ppermute | solution.py:54
  12.3 8.4 %collective-permute-start.9 = (f32[2,64,256]{2,1,0:T(8,128)S(1)}, f32[2,64,256]{2,1,0:T(8,128)S(1)}, u32[]{:S(2)}, u32[]{:S(2)}) collective-permute-start(f32[2,64,256]{2,1,0:T(8,128)S(1)} %shard_map.80.refs_6_.refs_0_), channel_id=1, source_target_pairs={{1,0},{0,1},{3,2},{2,3},{5,4},{4,5},{7,6},{6,7},{9,8},{8,9},{11,10... | collective-permute-start | bytes 393224 | tf_op jit(solution)/shard_map/ppermute | solution.py:54
  16.2 6.9 %collective-permute-start.6 = (f32[64,256]{1,0:T(8,128)S(1)}, f32[64,256]{1,0:T(8,128)S(1)}, u32[]{:S(2)}, u32[]{:S(2)}) collective-permute-start(f32[64,256]{1,0:T(8,128)S(1)} %get-tuple-element.29), channel_id=1, source_target_pairs={{0,3},{1,2},{2,1},{3,0},{4,7},{5,6},{6,5},{7,4},{8,11},{9,10},{10,... | collective-permute-start | bytes 196616 | tf_op jit(solution)/shard_map/ppermute | solution.py:60
  16.3 8.0 %collective-permute-start.7 = (f32[64,256]{1,0:T(8,128)S(1)}, f32[64,256]{1,0:T(8,128)S(1)}, u32[]{:S(2)}, u32[]{:S(2)}) collective-permute-start(f32[64,256]{1,0:T(8,128)S(1)} %get-tuple-element.30), channel_id=1, source_target_pairs={{0,2},{1,3},{2,0},{3,1},{4,6},{5,7},{6,4},{7,5},{8,10},{9,11},{10,... | collective-permute-start | bytes 196616 | tf_op jit(solution)/shard_map/ppermute | solution.py:60
  17.8 6.5 %collective-permute-start.8 = (f32[64,256]{1,0:T(8,128)S(1)}, f32[64,256]{1,0:T(8,128)S(1)}, u32[]{:S(2)}, u32[]{:S(2)}) collective-permute-start(f32[64,256]{1,0:T(8,128)S(1)} %get-tuple-element.31), channel_id=1, source_target_pairs={{0,1},{1,0},{2,3},{3,2},{4,5},{5,4},{6,7},{7,6},{8,9},{9,8},{10,11... | collective-permute-start | bytes 196616 | tf_op jit(solution)/shard_map/ppermute | solution.py:60
  24.4 7.2 %collective-permute-start.15 = (f32[4,64,256]{2,1,0:T(8,128)S(1)}, f32[4,64,256]{2,1,0:T(8,128)S(1)}, u32[]{:S(2)}, u32[]{:S(2)}) collective-permute-start(f32[4,64,256]{2,1,0:T(8,128)S(1)} %shard_map.86), channel_id=1, source_target_pairs={{4,0},{0,4},{12,8},{8,12},{20,16},{16,20},{28,24},{24,28},{5,1},{1... | collective-permute-start | bytes 786440 | tf_op jit(solution)/shard_map/ppermute | solution.py:54
  24.5 4.0 %collective-permute-start.13 = (f32[64,256]{1,0:T(8,128)S(1)}, f32[64,256]{1,0:T(8,128)S(1)}, u32[]{:S(2)}, u32[]{:S(2)}) collective-permute-start(f32[64,256]{1,0:T(8,128)S(1)} %shard_map.83.refs_0_.refs_1_.refs_5_), channel_id=1, source_target_pairs={{4,0},{0,4},{12,8},{8,12},{20,16},{16,20},{28,24},{24,28},{5,1},{1... | collective-permute-start | bytes 196616 | tf_op jit(solution)/shard_map/ppermute | solution.py:54
  25.0 5.5 %collective-permute-start.12 = (f32[64,256]{1,0:T(8,128)S(1)}, f32[64,256]{1,0:T(8,128)S(1)}, u32[]{:S(2)}, u32[]{:S(2)}) collective-permute-start(f32[64,256]{1,0:T(8,128)S(1)} %shard_map.83.refs_0_.refs_1_.refs_5_), channel_id=1, source_target_pairs={{24,0},{28,4},{16,8},{20,12},{8,16},{12,20},{0,24},{4,28},{25,1},{... | collective-permute-start | bytes 196616 | tf_op jit(solution)/shard_map/ppermute | solution.py:54
  26.3 5.1 %collective-permute-start.11 = (f32[64,256]{1,0:T(8,128)S(1)}, f32[64,256]{1,0:T(8,128)S(1)}, u32[]{:S(2)}, u32[]{:S(2)}) collective-permute-start(f32[64,256]{1,0:T(8,128)S(1)} %shard_map.83.refs_0_.refs_1_.refs_5_), channel_id=1, source_target_pairs={{16,0},{20,4},{24,8},{28,12},{0,16},{4,20},{8,24},{12,28},{17,1},{... | collective-permute-start | bytes 196616 | tf_op jit(solution)/shard_map/ppermute | solution.py:54
  27.2 4.3 %collective-permute-start.10 = (f32[64,256]{1,0:T(8,128)S(1)}, f32[64,256]{1,0:T(8,128)S(1)}, u32[]{:S(2)}, u32[]{:S(2)}) collective-permute-start(f32[64,256]{1,0:T(8,128)S(1)} %shard_map.83.refs_0_.refs_1_.refs_5_), channel_id=1, source_target_pairs={{8,0},{12,4},{0,8},{4,12},{24,16},{28,20},{16,24},{20,28},{9,1},{1... | collective-permute-start | bytes 196616 | tf_op jit(solution)/shard_map/ppermute | solution.py:54
  31.5 2.4 %collective-permute-start.14 = (f32[3,64,256]{2,1,0:T(8,128)S(1)}, f32[3,64,256]{2,1,0:T(8,128)S(1)}, u32[]{:S(2)}, u32[]{:S(2)}) collective-permute-start(f32[3,64,256]{2,1,0:T(8,128)S(1)} %shard_map.84.refs_1_.refs_2_), channel_id=1, source_target_pairs={{4,0},{0,4},{12,8},{8,12},{20,16},{16,20},{28,24},{24,28},{5,1},{1... | collective-permute-start | bytes 589832 | tf_op jit(solution)/shard_map/ppermute | solution.py:54
  31.6 7.4 %collective-permute-start.19 = (f32[2,64,256]{2,1,0:T(8,128)S(1)}, f32[2,64,256]{2,1,0:T(8,128)S(1)}, u32[]{:S(2)}, u32[]{:S(2)}) collective-permute-start(f32[2,64,256]{2,1,0:T(8,128)S(1)} %get-tuple-element.39), channel_id=1, source_target_pairs={{8,0},{12,4},{0,8},{4,12},{24,16},{28,20},{16,24},{20,28},{9,1},{1... | collective-permute-start | bytes 393224 | tf_op jit(solution)/shard_map/ppermute | solution.py:54
  34.5 6.9 %collective-permute-start.16 = (f32[64,256]{1,0:T(8,128)S(1)}, f32[64,256]{1,0:T(8,128)S(1)}, u32[]{:S(2)}, u32[]{:S(2)}) collective-permute-start(f32[64,256]{1,0:T(8,128)S(1)} %get-tuple-element.34), channel_id=1, source_target_pairs={{0,3},{1,2},{2,1},{3,0},{4,7},{5,6},{6,5},{7,4},{8,11},{9,10},{10,... | collective-permute-start | bytes 196616 | tf_op jit(solution)/shard_map/ppermute | solution.py:60
  36.3 7.1 %collective-permute-start.17 = (f32[64,256]{1,0:T(8,128)S(1)}, f32[64,256]{1,0:T(8,128)S(1)}, u32[]{:S(2)}, u32[]{:S(2)}) collective-permute-start(f32[64,256]{1,0:T(8,128)S(1)} %get-tuple-element.35), channel_id=1, source_target_pairs={{0,2},{1,3},{2,0},{3,1},{4,6},{5,7},{6,4},{7,5},{8,10},{9,11},{10,... | collective-permute-start | bytes 196616 | tf_op jit(solution)/shard_map/ppermute | solution.py:60
  36.7 6.8 %collective-permute-start.18 = (f32[64,256]{1,0:T(8,128)S(1)}, f32[64,256]{1,0:T(8,128)S(1)}, u32[]{:S(2)}, u32[]{:S(2)}) collective-permute-start(f32[64,256]{1,0:T(8,128)S(1)} %get-tuple-element.36), channel_id=1, source_target_pairs={{0,1},{1,0},{2,3},{3,2},{4,5},{5,4},{6,7},{7,6},{8,9},{9,8},{10,11... | collective-permute-start | bytes 196616 | tf_op jit(solution)/shard_map/ppermute | solution.py:60
  39.0 4.4 %collective-permute-start.20 = (f32[1,64,256]{2,1,0:T(8,128)S(1)}, f32[1,64,256]{2,1,0:T(8,128)S(1)}, u32[]{:S(2)}, u32[]{:S(2)}) collective-permute-start(f32[1,64,256]{2,1,0:T(8,128)S(1)} %get-tuple-element.41), channel_id=1, source_target_pairs={{16,0},{20,4},{24,8},{28,12},{0,16},{4,20},{8,24},{12,28},{17,1},{... | collective-permute-start | bytes 196616 | tf_op jit(solution)/shard_map/ppermute | solution.py:54
  43.9 3.6 %collective-permute-start.24 = (f32[112,256]{1,0:T(8,128)S(1)}, f32[112,256]{1,0:T(8,128)S(1)}, u32[]{:S(2)}, u32[]{:S(2)}) collective-permute-start(f32[112,256]{1,0:T(8,128)S(1)} %shard_map.90.refs_0_.refs_1_), channel_id=1, source_target_pairs={{4,0},{0,4},{12,8},{8,12},{20,16},{16,20},{28,24},{24,28},{5,1},{1... | collective-permute-start | bytes 344072 | tf_op jit(solution)/shard_map/ppermute | solution.py:54
  44.0 7.0 %collective-permute-start.23 = (f32[112,256]{1,0:T(8,128)S(1)}, f32[112,256]{1,0:T(8,128)S(1)}, u32[]{:S(2)}, u32[]{:S(2)}) collective-permute-start(f32[112,256]{1,0:T(8,128)S(1)} %shard_map.90.refs_0_.refs_1_), channel_id=1, source_target_pairs={{24,0},{28,4},{16,8},{20,12},{8,16},{12,20},{0,24},{4,28},{25,1},{... | collective-permute-start | bytes 344072 | tf_op jit(solution)/shard_map/ppermute | solution.py:54
  45.4 7.5 %collective-permute-start.22 = (f32[112,256]{1,0:T(8,128)S(1)}, f32[112,256]{1,0:T(8,128)S(1)}, u32[]{:S(2)}, u32[]{:S(2)}) collective-permute-start(f32[112,256]{1,0:T(8,128)S(1)} %shard_map.90.refs_0_.refs_1_), channel_id=1, source_target_pairs={{16,0},{20,4},{24,8},{28,12},{0,16},{4,20},{8,24},{12,28},{17,1},{... | collective-permute-start | bytes 344072 | tf_op jit(solution)/shard_map/ppermute | solution.py:54
  46.3 6.6 %collective-permute-start.21 = (f32[112,256]{1,0:T(8,128)S(1)}, f32[112,256]{1,0:T(8,128)S(1)}, u32[]{:S(2)}, u32[]{:S(2)}) collective-permute-start(f32[112,256]{1,0:T(8,128)S(1)} %shard_map.90.refs_0_.refs_1_), channel_id=1, source_target_pairs={{8,0},{12,4},{0,8},{4,12},{24,16},{28,20},{16,24},{20,28},{9,1},{1... | collective-permute-start | bytes 344072 | tf_op jit(solution)/shard_map/ppermute | solution.py:54
  52.9 1.7 %collective-permute-start.25 = (f32[3,112,256]{2,1,0:T(8,128)S(1)}, f32[3,112,256]{2,1,0:T(8,128)S(1)}, u32[]{:S(2)}, u32[]{:S(2)}) collective-permute-start(f32[3,112,256]{2,1,0:T(8,128)S(1)} %shard_map.91.refs_1_.refs_2_), channel_id=1, source_target_pairs={{4,0},{0,4},{12,8},{8,12},{20,16},{16,20},{28,24},{24,28},{5,1},{1... | collective-permute-start | bytes 1032200 | tf_op jit(solution)/shard_map/ppermute | solution.py:54
  55.3 7.4 %collective-permute-start.26 = (f32[88,256]{1,0:T(8,128)S(1)}, f32[88,256]{1,0:T(8,128)S(1)}, u32[]{:S(2)}, u32[]{:S(2)}) collective-permute-start(f32[88,256]{1,0:T(8,128)S(1)} %get-tuple-element.43), channel_id=1, source_target_pairs={{0,3},{1,2},{2,1},{3,0},{4,7},{5,6},{6,5},{7,4},{8,11},{9,10},{10,... | collective-permute-start | bytes 270344 | tf_op jit(solution)/shard_map/ppermute | solution.py:60
  57.4 8.3 %collective-permute-start.27 = (f32[88,256]{1,0:T(8,128)S(1)}, f32[88,256]{1,0:T(8,128)S(1)}, u32[]{:S(2)}, u32[]{:S(2)}) collective-permute-start(f32[88,256]{1,0:T(8,128)S(1)} %get-tuple-element.44), channel_id=1, source_target_pairs={{0,2},{1,3},{2,0},{3,1},{4,6},{5,7},{6,4},{7,5},{8,10},{9,11},{10,... | collective-permute-start | bytes 270344 | tf_op jit(solution)/shard_map/ppermute | solution.py:60
  57.4 8.3 %collective-permute-start.28 = (f32[88,256]{1,0:T(8,128)S(1)}, f32[88,256]{1,0:T(8,128)S(1)}, u32[]{:S(2)}, u32[]{:S(2)}) collective-permute-start(f32[88,256]{1,0:T(8,128)S(1)} %get-tuple-element.45), channel_id=1, source_target_pairs={{0,1},{1,0},{2,3},{3,2},{4,5},{5,4},{6,7},{7,6},{8,9},{9,8},{10,11... | collective-permute-start | bytes 270344 | tf_op jit(solution)/shard_map/ppermute | solution.py:60
  65.7 1.3 %collective-permute-start.29 = (f32[24,256]{1,0:T(8,128)S(1)}, f32[24,256]{1,0:T(8,128)S(1)}, u32[]{:S(2)}, u32[]{:S(2)}) collective-permute-start(f32[24,256]{1,0:T(8,128)S(1)} %slice_add_fusion.3.refs_0_), channel_id=1, source_target_pairs={{4,0},{0,4},{12,8},{8,12},{20,16},{16,20},{28,24},{24,28},{5,1},{1... | collective-permute-start | bytes 73736 | tf_op jit(solution)/shard_map/ppermute | solution.py:54

commit v16 on v14

--- a/solution.py
+++ b/solution.py
@@ -269,9 +269,8 @@
     return jnp.where(lax.axis_index("row") % 2 == 0, packed[:rows], packed[rows:])
 
 
-def second_half_kernel(span, pieces_ref, evens_ref, sums_ref, dense_ref, *refs):
-    outs, digits = refs[:-1], refs[-1]
-    n_col = len(outs)
+def second_half_kernel(span, n_col, pieces_ref, evens_ref, sums_ref, dense_ref, *refs):
+    tails, outs, digits = refs[: -n_col - 1], refs[-n_col - 1 : -1], refs[-1]
     fill_digits(span, pieces_ref, digits)
     row_blocks, _, width = dense_ref.shape
     tile_len = width // 2
@@ -287,7 +286,7 @@
             outs[e][:span, sub * tile_len : (sub + 1) * tile_len] = combine(*parts)
     if outs[0].shape[0] > span:
         packed = jnp.sum(pieces_ref[:, span:, :], 0) + jnp.sum(evens_ref[:, span:, :], 0)
-        packed = half_of_core(packed)
+        packed = half_of_core(jnp.concatenate([packed, *(tail[...] for tail in tails)], 0))
         for out in outs:
             out[span:, :] = packed
 
@@ -304,13 +303,14 @@
     )[0]
 
 
-def dense_second(odds, evens, sums, span, n_col, dense, before):
+def dense_second(odds, evens, sums, span, n_col, tails, dense, before):
     _, depth, _ = dense.shape
     _, rows, piece_len = odds.shape
+    rows = rows + sum(tail.shape[0] for tail in tails)
     return list(
         call(
-            functools.partial(second_half_kernel, span),
-            [odds, evens, sums, dense],
+            functools.partial(second_half_kernel, span, n_col),
+            [odds, evens, sums, dense, *tails],
             [held(span + (rows - span) // 2, piece_len)] * n_col,
             before,
             scratch=[pltpu.VMEM((2 * span, depth // 2), jnp.bfloat16)],
@@ -320,7 +320,19 @@
     )
 
 
-def left_kernel(n_row, x_evens, x_odds, dense_ref, evens_ref, odds_ref):
+def project(terms):
+    products = functools.reduce(jnp.add, [dot_pairs(left, right) for left, right in terms])
+    span = products.shape[0] // 2
+    square = combine(
+        reduce_centered(products[:span, :span]),
+        reduce_centered(products[:span, span:]) + reduce_centered(products[span:, :span]),
+        reduce_centered(products[span:, span:]),
+    )
+    return pack_square(square, terms[0][0].shape[1])
+
+
+def left_kernel(n_row, x_evens, x_odds, dense_ref, *refs):
+    rows_refs, (evens_ref, odds_ref, term_ref) = refs[:-3], refs[-3:]
     row_blocks, _, width = dense_ref.shape
     tile_len = width // 2
     _, span, piece_len = x_evens.shape
@@ -329,6 +341,9 @@
         centred_digits((x_odds if e % 2 else x_evens)[e // 2])
         for e in range(row_blocks // piece_blocks)
     ]
+    term = project([(x, stacked_digits(ref[...])) for x, ref in zip(x_digits, rows_refs)])
+    term_ref[...] = term
+    part_rows = term.shape[0] // odds_ref.shape[0]
     for place in range(n_row):
         by_high = by_low = high_part = low_part = 0.0
         for block in range(row_blocks):
@@ -345,16 +360,22 @@
         if place < n_row // 2:
             evens_ref[place] = piece
         else:
-            odds_ref[place - n_row // 2] = piece
-
-
-def dense_left(x_pairs, n_row, dense, before):
+            index = place - n_row // 2
+            odds_ref[index, :span, :] = piece
+            odds_ref[index, span:, :] = term[index * part_rows : (index + 1) * part_rows]
+
+
+def dense_left(x_pairs, outs, n_row, dense):
     _, span, piece_len = x_pairs[0].shape
+    count, rows = n_row // 2, span * span // piece_len
     return call(
         functools.partial(left_kernel, n_row),
-        [*x_pairs, dense],
-        [held(n_row // 2, span, piece_len)] * 2,
-        before,
+        [*x_pairs, dense, *outs],
+        [
+            held(count, span, piece_len),
+            held(count, span + rows // count, piece_len),
+            held(rows, piece_len),
+        ],
         limit=VMEM_LIMIT,
         flops=4 * span * dense.size,
     )
@@ -394,19 +415,20 @@
     return reduce_centered(summed).reshape(span, blocks * tile_len)
 
 
-def sparse_second(odds, evens, span, n_col, positions, a_digits):
+def sparse_second(odds, evens, span, n_col, tails, positions, a_digits):
     rows, cols, count = positions
     pieces = [*evens, *odds]
     piece_len = pieces[0].shape[1]
     blocks = n_col * piece_len // a_digits.shape[-1]
     vector = reduce_centered(jnp.concatenate([piece[:span] for piece in pieces], 1))
     product = sparse_product(vector, "ntk,tdik->tdni", cols, rows, count, blocks, a_digits)
-    packed = half_of_core(functools.reduce(jnp.add, [piece[span:] for piece in pieces]))
+    packed = functools.reduce(jnp.add, [piece[span:] for piece in pieces])
+    packed = half_of_core(jnp.concatenate([packed, *tails], 0))
     outs = [product[:, e * piece_len : (e + 1) * piece_len] for e in range(n_col)]
     return [jnp.concatenate([out, packed], 0) for out in outs]
 
 
-def sparse_left(x_pairs, n_row, positions, a_digits):
+def sparse_left(x_pairs, outs, n_row, positions, a_digits):
     rows, cols, count = positions
     n_col = 2 * x_pairs[0].shape[0]
     x_pieces = [x_pairs[e % 2][e // 2] for e in range(n_col)]
@@ -416,41 +438,59 @@
     blocks = n_row * piece_len // a_digits.shape[-1]
     product = sparse_product(values, "nti,tdik->tdnk", rows, cols, count, blocks, a_digits)
     pieces = [product[:, d * piece_len : (d + 1) * piece_len] for d in range(n_row)]
-    return jnp.stack(pieces[: n_row // 2]), jnp.stack(pieces[n_row // 2 :])
-
-
-def add_and_part(kept, came, before=()):
-    def kernel(kept_ref, came_ref, evens_ref, odds_ref):
-        for index in range(kept.shape[0]):
-            (odds_ref if index % 2 else evens_ref)[index // 2] = kept_ref[index] + came_ref[index]
-
-    return call(kernel, [kept, came], [held(kept.shape[0] // 2, *kept.shape[1:])] * 2, before)
-
-
-def append_projections(w_parts, pieces, earlier):
+    term = 0.0
+    for x_piece, rows_piece in zip(x_pieces, outs):
+        term = term + project([(centred_digits(x_piece), stacked_digits(rows_piece))])
+    odds = jnp.stack(pieces[n_row // 2 :])
+    below = term.reshape(odds.shape[0], -1, piece_len)
+    return jnp.stack(pieces[: n_row // 2]), jnp.concatenate([odds, below], 1), term
+
+
+def add_and_part(kept, came, term, before=()):
+    count, span, piece_len = kept.shape
+    half, rows = count // 2, term.shape[0]
+    part = rows // half if half > 1 else 0
+
+    def kernel(kept_ref, came_ref, term_ref, evens_ref, odds_ref, out_ref):
+        below = [came_ref[index, span:, :] for index in range(count)]
+        total = term_ref[...] + jnp.concatenate(below, 0)
+        out_ref[...] = total
+        for index in range(count):
+            piece = kept_ref[index] + came_ref[index, :span, :]
+            if index % 2 == 0:
+                evens_ref[index // 2] = piece
+            else:
+                odds_ref[index // 2, :span, :] = piece
+        if part:
+            for index in range(half):
+                odds_ref[index, span:, :] = total[index * part : (index + 1) * part]
+
+    outs = [
+        held(half, span, piece_len),
+        held(half, span + part, piece_len),
+        held(rows, piece_len),
+    ]
+    return call(kernel, [kept, came, term], outs, before)
+
+
+def append_projections(kept, came, term, term_came, pieces, vector_1):
     span, piece_len = pieces[0].shape
-    rows = span * span // piece_len
+    rows = term.shape[0]
 
     def kernel(*refs):
         piece_refs, refs = refs[: len(pieces)], refs[len(pieces) :]
-        earlier_refs, refs = refs[: len(earlier)], refs[len(earlier) :]
-        w_refs, out_ref = refs[:-1], refs[-1]
+        vector_ref, kept_ref, came_ref, term_ref, term_came_ref, out_ref, first_ref = refs
         summed = functools.reduce(jnp.add, [ref[...] for ref in piece_refs])
         out_ref[:span, :] = summed
-        w_piece = functools.reduce(jnp.add, [ref[...] for ref in w_refs])
-        w_digits = stacked_digits(reduce_centered(w_piece))
-        for index, vector in enumerate([summed] + [ref[...] for ref in earlier_refs]):
-            products = dot_pairs(w_digits, stacked_digits(reduce_centered(vector)))
-            square = combine(
-                reduce_centered(products[:span, :span]),
-                reduce_centered(products[:span, span:]) + reduce_centered(products[span:, :span]),
-                reduce_centered(products[span:, span:]),
-            )
+        w_digits = stacked_digits(reduce_centered(kept_ref[0] + came_ref[0]))
+        first_ref[...] = term_ref[...] + term_came_ref[...]
+        for index, vector in enumerate([summed, vector_ref[...]]):
             start = span + index * rows
-            out_ref[start : start + rows, :] = pack_square(square, piece_len)
-
-    outs = [held(span + (len(earlier) + 1) * rows, piece_len)]
-    return call(kernel, [*pieces, *earlier, *w_parts], outs)[0]
+            digits = stacked_digits(reduce_centered(vector))
+            out_ref[start : start + rows, :] = project([(w_digits, digits)])
+
+    outs = [held(span + 2 * rows, piece_len), held(rows, piece_len)]
+    return call(kernel, [*pieces, vector_1, kept, came, term, term_came], outs)
 
 
 def multiply_mod(left, right):
@@ -471,7 +511,7 @@
         first = lax.axis_index("row") % 2 == 0
         mine, other = reduce_centered(mine_ref[...]), reduce_centered(other_ref[...])
         packed = jnp.concatenate([jnp.where(first, mine, other), jnp.where(first, other, mine)], 0)
-        c_3, c_1, c_2 = (
+        c_3, c_2, c_1 = (
             unpack_square(packed[index * rows : (index + 1) * rows], span) for index in range(3)
         )
         e_2 = reduce_centered(c_1 - multiply_mod(c_1, c_2))
@@ -506,13 +546,11 @@
     def multiply_evens(evens):
         return dense_first(evens, span, dense) if is_dense else evens
 
-    def multiply_odds(odds, evens, sums, before):
+    def multiply(evens, before=(), tails=()):
+        odds, sums = gather_odds(evens, "row"), multiply_evens(evens)
         if is_dense:
-            return dense_second(odds, evens, sums, span, n_col, dense, before)
-        return sparse_second(odds, evens, span, n_col, positions, a_digits)
-
-    def multiply(evens, before):
-        return multiply_odds(gather_odds(evens, "row"), evens, multiply_evens(evens), before)
+            return dense_second(odds, evens, sums, span, n_col, tails, dense, before)
+        return sparse_second(odds, evens, span, n_col, tails, positions, a_digits)
 
     y_came = fetch_evens(block_y, "row")
     x_came = fetch_evens(block_x, "col")
@@ -521,20 +559,21 @@
     outs = multiply(evens, [x_evens])
     x_pairs = [x_evens, gather_odds(x_evens, "col")]
     if is_dense:
-        w_evens, w_odds = dense_left(x_pairs, n_row, dense, [outs[0]])
+        w_kept, w_odds, term = dense_left(x_pairs, outs, n_row, dense)
     else:
-        w_evens, w_odds = sparse_left(x_pairs, n_row, positions, a_digits)
+        w_kept, w_odds, term = sparse_left(x_pairs, outs, n_row, positions, a_digits)
     vector_1 = sum_after(scatter_pieces(outs, "col"), [w_odds])
     w_came = fetch(w_odds, "row", 1)
     outs = multiply(gather_evens(vector_1, "row"), [w_came])
     pieces = scatter_pieces(outs, "col")
-    w_kept, shift, before = w_evens, 2, []
+    shift, before = 2, []
     while shift < n_row:
-        w_kept, w_sent = add_and_part(w_kept, w_came, before)
+        w_kept, w_sent, term = add_and_part(w_kept, w_came, term, before)
         w_came = fetch(w_sent, "row", shift)
         shift, before = 2 * shift, [outs[0]]
-    vector_2 = append_projections([w_kept[0], w_came[0]], pieces, [y_own, vector_1])
-    outs = multiply(gather_evens(vector_2, "row"), [])
+    term_came = fetch(term, "row", n_row // 2)
+    vector_2, first = append_projections(w_kept, w_came, term, term_came, pieces, vector_1)
+    outs = multiply(gather_evens(vector_2, "row"), tails=[first])
     pieces = scatter_pieces(outs, "col")
     terms = functools.reduce(jnp.add, [piece[span:] for piece in pieces])
     vector_3 = functools.reduce(jnp.add, [piece[:span] for piece in pieces])

time: 67.8 us -> 67 us (0.988)
  waiting for transfers between devices: 21.9 us -> 20.6 us
  starting transfers between devices: 32.2 us -> 32.9 us
    ppermute x9, waiting for transfers between devices: 10.6 us -> 7.34 us  [scatter_pieces(): lax.ppermute(pieces[shift], axis, [(i, partner(i, shift, size)) for i in...]
    ppermute x18 -> x19, waiting for transfers between devices: 11.3 us -> 13.3 us  [fetch(): lax.ppermute(piece, axis, [(partner(i, shift, size), i) for i in range(si...]
    ppermute x18 -> x19, starting transfers between devices: 18.8 us -> 19.5 us  [fetch(): lax.ppermute(piece, axis, [(partner(i, shift, size), i) for i in range(si...]
  transfers between devices with their start and end apart: 27 -> 28, of which waited for: 14 -> 13; matrix products, arithmetic and copies ran while one was open for 1% -> 1% of each run, Pallas kernels for 13% -> 13%
where the time goes in v16:
time: 67 us; the launch traced here: 66.8 us
  starting transfers between devices  32.9 us (49%)
  waiting for transfers between devices  20.6 us (31%)
  Pallas kernels  11.1 us (17%)
  between operations  1.5 us (2%)
  other arithmetic  0.68 us (1%)
    ppermute x19, starting transfers between devices, fetch(): lax.ppermute(piece, axis, [(partner(i, shift, size), i) for i in range(si...  19.5 us
    ppermute x9, starting transfers between devices, scatter_pieces(): lax.ppermute(pieces[shift], axis, [(i, partner(i, shift, size)) for i in...  13.4 us
    ppermute x19, waiting for transfers between devices, fetch(): lax.ppermute(piece, axis, [(partner(i, shift, size), i) for i in range(si...  13.3 us
    pallas_call x16, Pallas kernels, call(): pl.pallas_call(body, in_specs=[vmem] * len(operands) + [pl.BlockSpec(memo...  9.37 us
    ppermute x9, waiting for transfers between devices, scatter_pieces(): lax.ppermute(pieces[shift], axis, [(i, partner(i, shift, size)) for i in...  7.34 us
    pallas_call x1, Pallas kernels, build_dense(): pl.pallas_call(functools.partial(build_kernel, (*sizes, group)), in_specs...  1.76 us
  transfers between devices with their start and end apart: 28, of which 13 were waited for; matrix products, arithmetic and copies ran while one was open for 1% of the time, Pallas kernels for 13%

profile of v16, /device:TPU:0, one launch (start us, length us, event | category | flops | bytes accessed | tf_op | source)
XLA Modules:
  0.0 66.8 jit_solution(15987861521844846438)
XLA Ops:
  0.6 4.1 %collective-permute-start.3 = (f32[64,256]{1,0:T(8,128)}, f32[64,256]{1,0:T(8,128)S(1)}, u32[]{:S(2)}, u32[]{:S(2)}) collective-permute-start(f32[64,256]{1,0:T(8,128)} %refs_4_.1), channel_id=1, source_target_pairs={{2,0},{3,1},{0,2},{1,3},{6,4},{7,5},{4,6},{5,7},{10,8},{11,9},{8,1... | collective-permute-start | bytes 196616 | tf_op jit(solution)/shard_map/ppermute | solution.py:54
  4.7 1.5 %collective-permute-start = (f32[64,256]{1,0:T(8,128)}, f32[64,256]{1,0:T(8,128)S(1)}, u32[]{:S(2)}, u32[]{:S(2)}) collective-permute-start(f32[64,256]{1,0:T(8,128)} %refs_5_.1), channel_id=1, source_target_pairs={{8,0},{12,4},{0,8},{4,12},{24,16},{28,20},{16,24},{20,28},{9,1},{1... | collective-permute-start | bytes 196616 | tf_op jit(solution)/shard_map/ppermute | solution.py:54
  6.2 1.5 %collective-permute-start.2 = (f32[64,256]{1,0:T(8,128)}, f32[64,256]{1,0:T(8,128)S(1)}, u32[]{:S(2)}, u32[]{:S(2)}) collective-permute-start(f32[64,256]{1,0:T(8,128)} %refs_5_.1), channel_id=1, source_target_pairs={{24,0},{28,4},{16,8},{20,12},{8,16},{12,20},{0,24},{4,28},{25,1},{... | collective-permute-start | bytes 196616 | tf_op jit(solution)/shard_map/ppermute | solution.py:54
  7.7 0.5 collective-permute-start.1
  8.9 1.8 %shard_map.77 = (bf16[8,2048,256]{2,1,0:T(8,128)(2,1)S(1)}, f32[64,256]{1,0:T(8,128)S(1)}, f32[64,256]{1,0:T(8,128)S(1)}, f32[8,128]{1,0:T(8,128)S(1)}) custom-call(s32[1,1,64]{2,1,0:T(1,128)} %refs_0_.1, s32[1,1,64]{2,1,0:T(1,128)} %refs_1_.1, s32[1,1]{1,0:T(1,128)S(6)} %copy.8.refs_2_, f32[1,1,64,128,128]{4,3,2,1,0:T(8,128)} %refs_3_.1, ...), custom_call_target="tpu_custom_call" | custom-call | flops 8388608 | bytes 8388608 | tf_op jit(solution)/shard_map/pallas_call | solution.py:211
  10.7 1.0 %collective-permute-done.2.refs_3_ = f32[64,256]{1,0:T(8,128)S(1)} collective-permute-done((f32[64,256]{1,0:T(8,128)}, f32[64,256]{1,0:T(8,128)S(1)}, u32[]{:S(2)}, u32[]{:S(2)}) %collective-permute-start.2) | collective-permute-done | bytes 65568 | tf_op jit(solution)/shard_map/ppermute | solution.py:54
  11.6 0.7 %collective-permute-done.1.refs_2_ = f32[64,256]{1,0:T(8,128)S(1)} collective-permute-done((f32[64,256]{1,0:T(8,128)}, f32[64,256]{1,0:T(8,128)S(1)}, u32[]{:S(2)}, u32[]{:S(2)}) %collective-permute-start.1) | collective-permute-done | bytes 65568 | tf_op jit(solution)/shard_map/ppermute | solution.py:54
  12.4 1.6 %collective-permute-start.8 = (f32[2,64,256]{2,1,0:T(8,128)S(1)}, f32[2,64,256]{2,1,0:T(8,128)S(1)}, u32[]{:S(2)}, u32[]{:S(2)}) collective-permute-start(f32[2,64,256]{2,1,0:T(8,128)S(1)} %shard_map.80.refs_4_.refs_0_), channel_id=1, source_target_pairs={{1,0},{0,1},{3,2},{2,3},{5,4},{4,5},{7,6},{6,7},{9,8},{8,9},{11,10... | collective-permute-start | bytes 393224 | tf_op jit(solution)/shard_map/ppermute | solution.py:54
  14.1 0.7 %shard_map.79.refs_2_ = f32[3,64,1024]{2,1,0:T(8,128)S(1)} custom-call(f32[4,64,256]{2,1,0:T(8,128)S(1)} %shard_map.78.refs_0_.refs_1_, bf16[8,2048,256]{2,1,0:T(8,128)(2,1)S(1)} %get-tuple-element.31.refs_1_.refs_3_.refs_2_), custom_call_target="tpu_custom_call" | custom-call | flops 536870912 | tf_op jit(solution)/shard_map/pallas_call | solution.py:71
  14.8 0.8 %shard_map.81 = (f32[64,256]{1,0:T(8,128)S(1)}, f32[64,256]{1,0:T(8,128)S(1)}, f32[64,256]{1,0:T(8,128)S(1)}, f32[64,256]{1,0:T(8,128)S(1)}) custom-call(f32[4,64,256]{2,1,0:T(8,128)S(1)} %collective-permute-done.4.refs_0_, f32[4,64,256]{2,1,0:T(8,128)S(1)} %shard_map.78.refs_0_.refs_1_, f32[3,64,1024]{2,1,0:T(8,128)S(1)} %shard_map.79.refs_2_, ...), custom_call_target="tpu_custom_call" | custom-call | flops 536870912 | tf_op jit(solution)/shard_map/pallas_call | solution.py:71
  15.6 0.5 collective-permute-start.5
  16.1 1.7 %collective-permute-start.6 = (f32[64,256]{1,0:T(8,128)S(1)}, f32[64,256]{1,0:T(8,128)S(1)}, u32[]{:S(2)}, u32[]{:S(2)}) collective-permute-start(f32[64,256]{1,0:T(8,128)S(1)} %get-tuple-element.35.refs_5_), channel_id=1, source_target_pairs={{0,2},{1,3},{2,0},{3,1},{4,6},{5,7},{6,4},{7,5},{8,10},{9,11},{10,... | collective-permute-start | bytes 196616 | tf_op jit(solution)/shard_map/ppermute | solution.py:60
  17.8 2.3 %collective-permute-start.7 = (f32[64,256]{1,0:T(8,128)S(1)}, f32[64,256]{1,0:T(8,128)S(1)}, u32[]{:S(2)}, u32[]{:S(2)}) collective-permute-start(f32[64,256]{1,0:T(8,128)S(1)} %get-tuple-element.36.refs_4_), channel_id=1, source_target_pairs={{0,1},{1,0},{2,3},{3,2},{4,5},{5,4},{6,7},{7,6},{8,9},{9,8},{10,11... | collective-permute-start | bytes 196616 | tf_op jit(solution)/shard_map/ppermute | solution.py:60
  20.1 2.7 %shard_map.82 = (f32[4,64,256]{2,1,0:T(8,128)S(1)}, f32[4,68,256]{2,1,0:T(8,128)S(1)}, f32[16,256]{1,0:T(8,128)S(1)}) custom-call(f32[2,64,256]{2,1,0:T(8,128)S(1)} %shard_map.80.refs_4_.refs_0_, f32[2,64,256]{2,1,0:T(8,128)S(1)} %collective-permute-done.8.refs_1_, bf16[8,2048,256]{2,1,0:T(8,128)(2,1)S(1)} %get-tuple-element.31.refs_1_.refs_3_.refs_2_, ...), custom_call_target="tpu_custom_call" | custom-call | flops 1073741824 | tf_op jit(solution)/shard_map/pallas_call | solution.py:71
  22.8 0.1 collective-permute-start.13
  22.9 1.4 %collective-permute-done.6.refs_2_ = f32[64,256]{1,0:T(8,128)S(1)} collective-permute-done((f32[64,256]{1,0:T(8,128)S(1)}, f32[64,256]{1,0:T(8,128)S(1)}, u32[]{:S(2)}, u32[]{:S(2)}) %collective-permute-start.6) | collective-permute-done | bytes 65568 | tf_op jit(solution)/shard_map/ppermute | solution.py:60
  24.3 1.6 %collective-permute-start.11 = (f32[64,256]{1,0:T(8,128)S(1)}, f32[64,256]{1,0:T(8,128)S(1)}, u32[]{:S(2)}, u32[]{:S(2)}) collective-permute-start(f32[64,256]{1,0:T(8,128)S(1)} %shard_map.83.refs_0_.refs_4_), channel_id=1, source_target_pairs={{24,0},{28,4},{16,8},{20,12},{8,16},{12,20},{0,24},{4,28},{25,1},{... | collective-permute-start | bytes 196616 | tf_op jit(solution)/shard_map/ppermute | solution.py:54
  25.9 1.4 %collective-permute-start.10 = (f32[64,256]{1,0:T(8,128)S(1)}, f32[64,256]{1,0:T(8,128)S(1)}, u32[]{:S(2)}, u32[]{:S(2)}) collective-permute-start(f32[64,256]{1,0:T(8,128)S(1)} %shard_map.83.refs_0_.refs_4_), channel_id=1, source_target_pairs={{16,0},{20,4},{24,8},{28,12},{0,16},{4,20},{8,24},{12,28},{17,1},{... | collective-permute-start | bytes 196616 | tf_op jit(solution)/shard_map/ppermute | solution.py:54
  27.2 0.6 collective-permute-start.9
  27.9 2.4 %collective-permute-done.11.refs_3_ = f32[64,256]{1,0:T(8,128)S(1)} collective-permute-done((f32[64,256]{1,0:T(8,128)S(1)}, f32[64,256]{1,0:T(8,128)S(1)}, u32[]{:S(2)}, u32[]{:S(2)}) %collective-permute-start.11) | collective-permute-done | bytes 65568 | tf_op jit(solution)/shard_map/ppermute | solution.py:54
  30.2 0.3 collective-permute-done.10.refs_2_
  30.5 0.9 %collective-permute-done.9.refs_1_ = f32[64,256]{1,0:T(8,128)S(1)} collective-permute-done((f32[64,256]{1,0:T(8,128)S(1)}, f32[64,256]{1,0:T(8,128)S(1)}, u32[]{:S(2)}, u32[]{:S(2)}) %collective-permute-start.9) | collective-permute-done | bytes 65568 | tf_op jit(solution)/shard_map/ppermute | solution.py:54
  31.6 0.7 %collective-permute-start.17 = (f32[2,72,256]{2,1,0:T(8,128)S(1)}, f32[2,72,256]{2,1,0:T(8,128)S(1)}, u32[]{:S(2)}, u32[]{:S(2)}) collective-permute-start(f32[2,72,256]{2,1,0:T(8,128)S(1)} %get-tuple-element.45), channel_id=1, source_target_pairs={{8,0},{12,4},{0,8},{4,12},{24,16},{28,20},{16,24},{20,28},{9,1},{1... | collective-permute-start | bytes 442376 | tf_op jit(solution)/shard_map/ppermute | solution.py:54
  32.3 0.7 %shard_map.85.refs_2_ = f32[3,64,1024]{2,1,0:T(8,128)S(1)} custom-call(f32[4,64,256]{2,1,0:T(8,128)S(1)} %shard_map.84.refs_0_.refs_1_, bf16[8,2048,256]{2,1,0:T(8,128)(2,1)S(1)} %get-tuple-element.31.refs_1_.refs_3_.refs_2_), custom_call_target="tpu_custom_call" | custom-call | flops 536870912 | tf_op jit(solution)/shard_map/pallas_call | solution.py:71
  33.1 0.8 %shard_map.86 = (f32[64,256]{1,0:T(8,128)S(1)}, f32[64,256]{1,0:T(8,128)S(1)}, f32[64,256]{1,0:T(8,128)S(1)}, f32[64,256]{1,0:T(8,128)S(1)}) custom-call(f32[4,64,256]{2,1,0:T(8,128)S(1)} %collective-permute-done.12.refs_0_, f32[4,64,256]{2,1,0:T(8,128)S(1)} %shard_map.84.refs_0_.refs_1_, f32[3,64,1024]{2,1,0:T(8,128)S(1)} %shard_map.85.refs_2_, ...), custom_call_target="tpu_custom_call" | custom-call | flops 536870912 | tf_op jit(solution)/shard_map/pallas_call | solution.py:71
  33.9 1.8 %collective-permute-start.14 = (f32[64,256]{1,0:T(8,128)S(1)}, f32[64,256]{1,0:T(8,128)S(1)}, u32[]{:S(2)}, u32[]{:S(2)}) collective-permute-start(f32[64,256]{1,0:T(8,128)S(1)} %get-tuple-element.39), channel_id=1, source_target_pairs={{0,3},{1,2},{2,1},{3,0},{4,7},{5,6},{6,5},{7,4},{8,11},{9,10},{10,... | collective-permute-start | bytes 196616 | tf_op jit(solution)/shard_map/ppermute | solution.py:60
  35.7 2.7 %collective-permute-start.16 = (f32[64,256]{1,0:T(8,128)S(1)}, f32[64,256]{1,0:T(8,128)S(1)}, u32[]{:S(2)}, u32[]{:S(2)}) collective-permute-start(f32[64,256]{1,0:T(8,128)S(1)} %get-tuple-element.41), channel_id=1, source_target_pairs={{0,1},{1,0},{2,3},{3,2},{4,5},{5,4},{6,7},{7,6},{8,9},{9,8},{10,11... | collective-permute-start | bytes 196616 | tf_op jit(solution)/shard_map/ppermute | solution.py:60
  38.4 1.2 %collective-permute-start.18 = (f32[1,64,256]{2,1,0:T(8,128)S(1)}, f32[1,64,256]{2,1,0:T(8,128)S(1)}, u32[]{:S(2)}, u32[]{:S(2)}) collective-permute-start(f32[1,64,256]{2,1,0:T(8,128)S(1)} %get-tuple-element.48), channel_id=1, source_target_pairs={{16,0},{20,4},{24,8},{28,12},{0,16},{4,20},{8,24},{12,28},{17,1},{... | collective-permute-start | bytes 196616 | tf_op jit(solution)/shard_map/ppermute | solution.py:54
  39.6 0.9 %collective-permute-start.19 = (f32[16,256]{1,0:T(8,128)S(1)}, f32[16,256]{1,0:T(8,128)S(1)}, u32[]{:S(2)}, u32[]{:S(2)}) collective-permute-start(f32[16,256]{1,0:T(8,128)S(1)} %get-tuple-element.49.refs_7_), channel_id=1, source_target_pairs={{16,0},{20,4},{24,8},{28,12},{0,16},{4,20},{8,24},{12,28},{17,1},{... | collective-permute-start | bytes 49160 | tf_op jit(solution)/shard_map/ppermute | solution.py:54
  40.5 2.8 %collective-permute-done.19.refs_8_ = f32[16,256]{1,0:T(8,128)S(1)} collective-permute-done((f32[16,256]{1,0:T(8,128)S(1)}, f32[16,256]{1,0:T(8,128)S(1)}, u32[]{:S(2)}, u32[]{:S(2)}) %collective-permute-start.19) | collective-permute-done | bytes 16416 | tf_op jit(solution)/shard_map/ppermute | solution.py:54
  43.3 0.5 shard_map.89
  43.8 1.8 %collective-permute-start.22 = (f32[96,256]{1,0:T(8,128)S(1)}, f32[96,256]{1,0:T(8,128)S(1)}, u32[]{:S(2)}, u32[]{:S(2)}) collective-permute-start(f32[96,256]{1,0:T(8,128)S(1)} %get-tuple-element.50.refs_0_), channel_id=1, source_target_pairs={{24,0},{28,4},{16,8},{20,12},{8,16},{12,20},{0,24},{4,28},{25,1},{... | collective-permute-start | bytes 294920 | tf_op jit(solution)/shard_map/ppermute | solution.py:54
  45.6 0.7 %collective-permute-start.21 = (f32[96,256]{1,0:T(8,128)S(1)}, f32[96,256]{1,0:T(8,128)S(1)}, u32[]{:S(2)}, u32[]{:S(2)}) collective-permute-start(f32[96,256]{1,0:T(8,128)S(1)} %get-tuple-element.50.refs_0_), channel_id=1, source_target_pairs={{16,0},{20,4},{24,8},{28,12},{0,16},{4,20},{8,24},{12,28},{17,1},{... | collective-permute-start | bytes 294920 | tf_op jit(solution)/shard_map/ppermute | solution.py:54
  46.3 1.0 %collective-permute-start.20 = (f32[96,256]{1,0:T(8,128)S(1)}, f32[96,256]{1,0:T(8,128)S(1)}, u32[]{:S(2)}, u32[]{:S(2)}) collective-permute-start(f32[96,256]{1,0:T(8,128)S(1)} %get-tuple-element.50.refs_0_), channel_id=1, source_target_pairs={{8,0},{12,4},{0,8},{4,12},{24,16},{28,20},{16,24},{20,28},{9,1},{1... | collective-permute-start | bytes 294920 | tf_op jit(solution)/shard_map/ppermute | solution.py:54
  47.3 3.1 %collective-permute-done.22.refs_3_ = f32[96,256]{1,0:T(8,128)S(1)} collective-permute-done((f32[96,256]{1,0:T(8,128)S(1)}, f32[96,256]{1,0:T(8,128)S(1)}, u32[]{:S(2)}, u32[]{:S(2)}) %collective-permute-start.22) | collective-permute-done | bytes 98336 | tf_op jit(solution)/shard_map/ppermute | solution.py:54
  50.4 0.6 collective-permute-done.21.refs_2_
  51.1 0.1 collective-permute-start.23
  51.1 0.8 %shard_map.91.refs_2_ = f32[3,64,1024]{2,1,0:T(8,128)S(1)} custom-call(f32[4,96,256]{2,1,0:T(8,128)S(1)} %shard_map.90.refs_0_.refs_1_, bf16[8,2048,256]{2,1,0:T(8,128)(2,1)S(1)} %get-tuple-element.31.refs_1_.refs_3_.refs_2_), custom_call_target="tpu_custom_call" | custom-call | flops 536870912 | tf_op jit(solution)/shard_map/pallas_call | solution.py:71
  51.9 1.0 %collective-permute-done.23.refs_0_ = f32[4,96,256]{2,1,0:T(8,128)S(1)} collective-permute-done((f32[4,96,256]{2,1,0:T(8,128)S(1)}, f32[4,96,256]{2,1,0:T(8,128)S(1)}, u32[]{:S(2)}, u32[]{:S(2)}) %collective-permute-start.23) | collective-permute-done | bytes 393248 | tf_op jit(solution)/shard_map/ppermute | solution.py:54
  52.9 0.8 %shard_map.92 = (f32[88,256]{1,0:T(8,128)S(1)}, f32[88,256]{1,0:T(8,128)S(1)}, f32[88,256]{1,0:T(8,128)S(1)}, f32[88,256]{1,0:T(8,128)S(1)}) custom-call(f32[4,96,256]{2,1,0:T(8,128)S(1)} %collective-permute-done.23.refs_0_, f32[4,96,256]{2,1,0:T(8,128)S(1)} %shard_map.90.refs_0_.refs_1_, f32[3,64,1024]{2,1,0:T(8,128)S(1)} %shard_map.91.refs_2_, ...), custom_call_target="tpu_custom_call" | custom-call | flops 536870912 | tf_op jit(solution)/shard_map/pallas_call | solution.py:71
  53.7 1.8 %collective-permute-start.24 = (f32[88,256]{1,0:T(8,128)S(1)}, f32[88,256]{1,0:T(8,128)S(1)}, u32[]{:S(2)}, u32[]{:S(2)}) collective-permute-start(f32[88,256]{1,0:T(8,128)S(1)} %get-tuple-element.53), channel_id=1, source_target_pairs={{0,3},{1,2},{2,1},{3,0},{4,7},{5,6},{6,5},{7,4},{8,11},{9,10},{10,... | collective-permute-start | bytes 270344 | tf_op jit(solution)/shard_map/ppermute | solution.py:60
  55.4 2.7 %collective-permute-start.26 = (f32[88,256]{1,0:T(8,128)S(1)}, f32[88,256]{1,0:T(8,128)S(1)}, u32[]{:S(2)}, u32[]{:S(2)}) collective-permute-start(f32[88,256]{1,0:T(8,128)S(1)} %get-tuple-element.55), channel_id=1, source_target_pairs={{0,1},{1,0},{2,3},{3,2},{4,5},{5,4},{6,7},{7,6},{8,9},{9,8},{10,11... | collective-permute-start | bytes 270344 | tf_op jit(solution)/shard_map/ppermute | solution.py:60
  58.1 3.0 %collective-permute-done.24 = f32[88,256]{1,0:T(8,128)S(1)} collective-permute-done((f32[88,256]{1,0:T(8,128)S(1)}, f32[88,256]{1,0:T(8,128)S(1)}, u32[]{:S(2)}, u32[]{:S(2)}) %collective-permute-start.24) | collective-permute-done | bytes 90144 | tf_op jit(solution)/shard_map/ppermute | solution.py:60
  61.1 3.0 %collective-permute-done.25 = f32[88,256]{1,0:T(8,128)S(1)} collective-permute-done((f32[88,256]{1,0:T(8,128)S(1)}, f32[88,256]{1,0:T(8,128)S(1)}, u32[]{:S(2)}, u32[]{:S(2)}) %collective-permute-start.25) | collective-permute-done | bytes 90144 | tf_op jit(solution)/shard_map/ppermute | solution.py:60
  64.1 0.1 collective-permute-start.27
  64.1 0.7 %fusion = f32[64,256]{1,0:T(8,128)} fusion(f32[88,256]{1,0:T(8,128)S(1)} %collective-permute-done.26, f32[88,256]{1,0:T(8,128)S(1)} %collective-permute-done.25, f32[88,256]{1,0:T(8,128)S(1)} %collective-permute-done.24, f32[88,256]{1,0:T(8,128)S(1)} %get-tuple-element.52), kind=kLoop, calls=%fused_computation.1 | loop fusion | flops 196608 | bytes 327680 | tf_op jit(solution)/shard_map/mul | solution.py:580
  64.8 0.5 collective-permute-done.27.refs_1_
  65.3 1.4 %shard_map.93 = f32[3,64,64]{2,1,0:T(8,128)} custom-call(f32[24,256]{1,0:T(8,128)S(1)} %slice_add_fusion.3.refs_0_, f32[24,256]{1,0:T(8,128)S(1)} %collective-permute-done.27.refs_1_), custom_call_target="tpu_custom_call" | custom-call | tf_op jit(solution)/shard_map/pallas_call | solution.py:71
  (27 shorter events, 0.3 us)
Async XLA Ops:
  0.6 10.0 %collective-permute-start.3 = (f32[64,256]{1,0:T(8,128)}, f32[64,256]{1,0:T(8,128)S(1)}, u32[]{:S(2)}, u32[]{:S(2)}) collective-permute-start(f32[64,256]{1,0:T(8,128)} %refs_4_.1), channel_id=1, source_target_pairs={{2,0},{3,1},{0,2},{1,3},{6,4},{7,5},{4,6},{5,7},{10,8},{11,9},{8,1... | collective-permute-start | bytes 196616 | tf_op jit(solution)/shard_map/ppermute | solution.py:54
  4.7 5.9 %collective-permute-start = (f32[64,256]{1,0:T(8,128)}, f32[64,256]{1,0:T(8,128)S(1)}, u32[]{:S(2)}, u32[]{:S(2)}) collective-permute-start(f32[64,256]{1,0:T(8,128)} %refs_5_.1), channel_id=1, source_target_pairs={{8,0},{12,4},{0,8},{4,12},{24,16},{28,20},{16,24},{20,28},{9,1},{1... | collective-permute-start | bytes 196616 | tf_op jit(solution)/shard_map/ppermute | solution.py:54
  6.2 5.4 %collective-permute-start.2 = (f32[64,256]{1,0:T(8,128)}, f32[64,256]{1,0:T(8,128)S(1)}, u32[]{:S(2)}, u32[]{:S(2)}) collective-permute-start(f32[64,256]{1,0:T(8,128)} %refs_5_.1), channel_id=1, source_target_pairs={{24,0},{28,4},{16,8},{20,12},{8,16},{12,20},{0,24},{4,28},{25,1},{... | collective-permute-start | bytes 196616 | tf_op jit(solution)/shard_map/ppermute | solution.py:54
  7.7 4.6 %collective-permute-start.1 = (f32[64,256]{1,0:T(8,128)}, f32[64,256]{1,0:T(8,128)S(1)}, u32[]{:S(2)}, u32[]{:S(2)}) collective-permute-start(f32[64,256]{1,0:T(8,128)} %refs_5_.1), channel_id=1, source_target_pairs={{16,0},{20,4},{24,8},{28,12},{0,16},{4,20},{8,24},{12,28},{17,1},{... | collective-permute-start | bytes 196616 | tf_op jit(solution)/shard_map/ppermute | solution.py:54
  12.3 2.5 %collective-permute-start.4 = (f32[4,64,256]{2,1,0:T(8,128)S(1)}, f32[4,64,256]{2,1,0:T(8,128)S(1)}, u32[]{:S(2)}, u32[]{:S(2)}) collective-permute-start(f32[4,64,256]{2,1,0:T(8,128)S(1)} %shard_map.78.refs_0_.refs_1_), channel_id=1, source_target_pairs={{4,0},{0,4},{12,8},{8,12},{20,16},{16,20},{28,24},{24,28},{5,1},{1... | collective-permute-start | bytes 786440 | tf_op jit(solution)/shard_map/ppermute | solution.py:54
  12.4 7.7 %collective-permute-start.8 = (f32[2,64,256]{2,1,0:T(8,128)S(1)}, f32[2,64,256]{2,1,0:T(8,128)S(1)}, u32[]{:S(2)}, u32[]{:S(2)}) collective-permute-start(f32[2,64,256]{2,1,0:T(8,128)S(1)} %shard_map.80.refs_4_.refs_0_), channel_id=1, source_target_pairs={{1,0},{0,1},{3,2},{2,3},{5,4},{4,5},{7,6},{6,7},{9,8},{8,9},{11,10... | collective-permute-start | bytes 393224 | tf_op jit(solution)/shard_map/ppermute | solution.py:54
  15.6 7.2 %collective-permute-start.5 = (f32[64,256]{1,0:T(8,128)S(1)}, f32[64,256]{1,0:T(8,128)S(1)}, u32[]{:S(2)}, u32[]{:S(2)}) collective-permute-start(f32[64,256]{1,0:T(8,128)S(1)} %get-tuple-element.34.refs_6_), channel_id=1, source_target_pairs={{0,3},{1,2},{2,1},{3,0},{4,7},{5,6},{6,5},{7,4},{8,11},{9,10},{10,... | collective-permute-start | bytes 196616 | tf_op jit(solution)/shard_map/ppermute | solution.py:60
  16.1 8.1 %collective-permute-start.6 = (f32[64,256]{1,0:T(8,128)S(1)}, f32[64,256]{1,0:T(8,128)S(1)}, u32[]{:S(2)}, u32[]{:S(2)}) collective-permute-start(f32[64,256]{1,0:T(8,128)S(1)} %get-tuple-element.35.refs_5_), channel_id=1, source_target_pairs={{0,2},{1,3},{2,0},{3,1},{4,6},{5,7},{6,4},{7,5},{8,10},{9,11},{10,... | collective-permute-start | bytes 196616 | tf_op jit(solution)/shard_map/ppermute | solution.py:60
  17.8 6.5 %collective-permute-start.7 = (f32[64,256]{1,0:T(8,128)S(1)}, f32[64,256]{1,0:T(8,128)S(1)}, u32[]{:S(2)}, u32[]{:S(2)}) collective-permute-start(f32[64,256]{1,0:T(8,128)S(1)} %get-tuple-element.36.refs_4_), channel_id=1, source_target_pairs={{0,1},{1,0},{2,3},{3,2},{4,5},{5,4},{6,7},{7,6},{8,9},{9,8},{10,11... | collective-permute-start | bytes 196616 | tf_op jit(solution)/shard_map/ppermute | solution.py:60
  22.8 8.8 %collective-permute-start.13 = (f32[4,68,256]{2,1,0:T(8,128)S(1)}, f32[4,68,256]{2,1,0:T(8,128)S(1)}, u32[]{:S(2)}, u32[]{:S(2)}) collective-permute-start(f32[4,68,256]{2,1,0:T(8,128)S(1)} %get-tuple-element.37.refs_4_), channel_id=1, source_target_pairs={{4,0},{0,4},{12,8},{8,12},{20,16},{16,20},{28,24},{24,28},{5,1},{1... | collective-permute-start | bytes 835592 | tf_op jit(solution)/shard_map/ppermute | solution.py:54
  24.3 5.9 %collective-permute-start.11 = (f32[64,256]{1,0:T(8,128)S(1)}, f32[64,256]{1,0:T(8,128)S(1)}, u32[]{:S(2)}, u32[]{:S(2)}) collective-permute-start(f32[64,256]{1,0:T(8,128)S(1)} %shard_map.83.refs_0_.refs_4_), channel_id=1, source_target_pairs={{24,0},{28,4},{16,8},{20,12},{8,16},{12,20},{0,24},{4,28},{25,1},{... | collective-permute-start | bytes 196616 | tf_op jit(solution)/shard_map/ppermute | solution.py:54
  25.9 4.7 %collective-permute-start.10 = (f32[64,256]{1,0:T(8,128)S(1)}, f32[64,256]{1,0:T(8,128)S(1)}, u32[]{:S(2)}, u32[]{:S(2)}) collective-permute-start(f32[64,256]{1,0:T(8,128)S(1)} %shard_map.83.refs_0_.refs_4_), channel_id=1, source_target_pairs={{16,0},{20,4},{24,8},{28,12},{0,16},{4,20},{8,24},{12,28},{17,1},{... | collective-permute-start | bytes 196616 | tf_op jit(solution)/shard_map/ppermute | solution.py:54
  27.2 4.3 %collective-permute-start.9 = (f32[64,256]{1,0:T(8,128)S(1)}, f32[64,256]{1,0:T(8,128)S(1)}, u32[]{:S(2)}, u32[]{:S(2)}) collective-permute-start(f32[64,256]{1,0:T(8,128)S(1)} %shard_map.83.refs_0_.refs_4_), channel_id=1, source_target_pairs={{8,0},{12,4},{0,8},{4,12},{24,16},{28,20},{16,24},{20,28},{9,1},{1... | collective-permute-start | bytes 196616 | tf_op jit(solution)/shard_map/ppermute | solution.py:54
  31.5 1.6 %collective-permute-start.12 = (f32[4,64,256]{2,1,0:T(8,128)S(1)}, f32[4,64,256]{2,1,0:T(8,128)S(1)}, u32[]{:S(2)}, u32[]{:S(2)}) collective-permute-start(f32[4,64,256]{2,1,0:T(8,128)S(1)} %shard_map.84.refs_0_.refs_1_), channel_id=1, source_target_pairs={{4,0},{0,4},{12,8},{8,12},{20,16},{16,20},{28,24},{24,28},{5,1},{1... | collective-permute-start | bytes 786440 | tf_op jit(solution)/shard_map/ppermute | solution.py:54
  31.6 6.7 %collective-permute-start.17 = (f32[2,72,256]{2,1,0:T(8,128)S(1)}, f32[2,72,256]{2,1,0:T(8,128)S(1)}, u32[]{:S(2)}, u32[]{:S(2)}) collective-permute-start(f32[2,72,256]{2,1,0:T(8,128)S(1)} %get-tuple-element.45), channel_id=1, source_target_pairs={{8,0},{12,4},{0,8},{4,12},{24,16},{28,20},{16,24},{20,28},{9,1},{1... | collective-permute-start | bytes 442376 | tf_op jit(solution)/shard_map/ppermute | solution.py:54
  33.9 9.4 %collective-permute-start.14 = (f32[64,256]{1,0:T(8,128)S(1)}, f32[64,256]{1,0:T(8,128)S(1)}, u32[]{:S(2)}, u32[]{:S(2)}) collective-permute-start(f32[64,256]{1,0:T(8,128)S(1)} %get-tuple-element.39), channel_id=1, source_target_pairs={{0,3},{1,2},{2,1},{3,0},{4,7},{5,6},{6,5},{7,4},{8,11},{9,10},{10,... | collective-permute-start | bytes 196616 | tf_op jit(solution)/shard_map/ppermute | solution.py:60
  35.7 7.6 %collective-permute-start.15 = (f32[64,256]{1,0:T(8,128)S(1)}, f32[64,256]{1,0:T(8,128)S(1)}, u32[]{:S(2)}, u32[]{:S(2)}) collective-permute-start(f32[64,256]{1,0:T(8,128)S(1)} %get-tuple-element.40), channel_id=1, source_target_pairs={{0,2},{1,3},{2,0},{3,1},{4,6},{5,7},{6,4},{7,5},{8,10},{9,11},{10,... | collective-permute-start | bytes 196616 | tf_op jit(solution)/shard_map/ppermute | solution.py:60
  35.7 7.6 %collective-permute-start.16 = (f32[64,256]{1,0:T(8,128)S(1)}, f32[64,256]{1,0:T(8,128)S(1)}, u32[]{:S(2)}, u32[]{:S(2)}) collective-permute-start(f32[64,256]{1,0:T(8,128)S(1)} %get-tuple-element.41), channel_id=1, source_target_pairs={{0,1},{1,0},{2,3},{3,2},{4,5},{5,4},{6,7},{7,6},{8,9},{9,8},{10,11... | collective-permute-start | bytes 196616 | tf_op jit(solution)/shard_map/ppermute | solution.py:60
  38.4 4.9 %collective-permute-start.18 = (f32[1,64,256]{2,1,0:T(8,128)S(1)}, f32[1,64,256]{2,1,0:T(8,128)S(1)}, u32[]{:S(2)}, u32[]{:S(2)}) collective-permute-start(f32[1,64,256]{2,1,0:T(8,128)S(1)} %get-tuple-element.48), channel_id=1, source_target_pairs={{16,0},{20,4},{24,8},{28,12},{0,16},{4,20},{8,24},{12,28},{17,1},{... | collective-permute-start | bytes 196616 | tf_op jit(solution)/shard_map/ppermute | solution.py:54
  39.6 3.7 %collective-permute-start.19 = (f32[16,256]{1,0:T(8,128)S(1)}, f32[16,256]{1,0:T(8,128)S(1)}, u32[]{:S(2)}, u32[]{:S(2)}) collective-permute-start(f32[16,256]{1,0:T(8,128)S(1)} %get-tuple-element.49.refs_7_), channel_id=1, source_target_pairs={{16,0},{20,4},{24,8},{28,12},{0,16},{4,20},{8,24},{12,28},{17,1},{... | collective-permute-start | bytes 49160 | tf_op jit(solution)/shard_map/ppermute | solution.py:54
  43.8 6.6 %collective-permute-start.22 = (f32[96,256]{1,0:T(8,128)S(1)}, f32[96,256]{1,0:T(8,128)S(1)}, u32[]{:S(2)}, u32[]{:S(2)}) collective-permute-start(f32[96,256]{1,0:T(8,128)S(1)} %get-tuple-element.50.refs_0_), channel_id=1, source_target_pairs={{24,0},{28,4},{16,8},{20,12},{8,16},{12,20},{0,24},{4,28},{25,1},{... | collective-permute-start | bytes 294920 | tf_op jit(solution)/shard_map/ppermute | solution.py:54
  45.6 5.4 %collective-permute-start.21 = (f32[96,256]{1,0:T(8,128)S(1)}, f32[96,256]{1,0:T(8,128)S(1)}, u32[]{:S(2)}, u32[]{:S(2)}) collective-permute-start(f32[96,256]{1,0:T(8,128)S(1)} %get-tuple-element.50.refs_0_), channel_id=1, source_target_pairs={{16,0},{20,4},{24,8},{28,12},{0,16},{4,20},{8,24},{12,28},{17,1},{... | collective-permute-start | bytes 294920 | tf_op jit(solution)/shard_map/ppermute | solution.py:54
  46.3 4.8 %collective-permute-start.20 = (f32[96,256]{1,0:T(8,128)S(1)}, f32[96,256]{1,0:T(8,128)S(1)}, u32[]{:S(2)}, u32[]{:S(2)}) collective-permute-start(f32[96,256]{1,0:T(8,128)S(1)} %get-tuple-element.50.refs_0_), channel_id=1, source_target_pairs={{8,0},{12,4},{0,8},{4,12},{24,16},{28,20},{16,24},{20,28},{9,1},{1... | collective-permute-start | bytes 294920 | tf_op jit(solution)/shard_map/ppermute | solution.py:54
  51.1 1.8 %collective-permute-start.23 = (f32[4,96,256]{2,1,0:T(8,128)S(1)}, f32[4,96,256]{2,1,0:T(8,128)S(1)}, u32[]{:S(2)}, u32[]{:S(2)}) collective-permute-start(f32[4,96,256]{2,1,0:T(8,128)S(1)} %shard_map.90.refs_0_.refs_1_), channel_id=1, source_target_pairs={{4,0},{0,4},{12,8},{8,12},{20,16},{16,20},{28,24},{24,28},{5,1},{1... | collective-permute-start | bytes 1179656 | tf_op jit(solution)/shard_map/ppermute | solution.py:54
  53.7 7.4 %collective-permute-start.24 = (f32[88,256]{1,0:T(8,128)S(1)}, f32[88,256]{1,0:T(8,128)S(1)}, u32[]{:S(2)}, u32[]{:S(2)}) collective-permute-start(f32[88,256]{1,0:T(8,128)S(1)} %get-tuple-element.53), channel_id=1, source_target_pairs={{0,3},{1,2},{2,1},{3,0},{4,7},{5,6},{6,5},{7,4},{8,11},{9,10},{10,... | collective-permute-start | bytes 270344 | tf_op jit(solution)/shard_map/ppermute | solution.py:60
  55.4 8.6 %collective-permute-start.25 = (f32[88,256]{1,0:T(8,128)S(1)}, f32[88,256]{1,0:T(8,128)S(1)}, u32[]{:S(2)}, u32[]{:S(2)}) collective-permute-start(f32[88,256]{1,0:T(8,128)S(1)} %get-tuple-element.54), channel_id=1, source_target_pairs={{0,2},{1,3},{2,0},{3,1},{4,6},{5,7},{6,4},{7,5},{8,10},{9,11},{10,... | collective-permute-start | bytes 270344 | tf_op jit(solution)/shard_map/ppermute | solution.py:60
  55.4 8.6 %collective-permute-start.26 = (f32[88,256]{1,0:T(8,128)S(1)}, f32[88,256]{1,0:T(8,128)S(1)}, u32[]{:S(2)}, u32[]{:S(2)}) collective-permute-start(f32[88,256]{1,0:T(8,128)S(1)} %get-tuple-element.55), channel_id=1, source_target_pairs={{0,1},{1,0},{2,3},{3,2},{4,5},{5,4},{6,7},{7,6},{8,9},{9,8},{10,11... | collective-permute-start | bytes 270344 | tf_op jit(solution)/shard_map/ppermute | solution.py:60
  64.1 1.3 %collective-permute-start.27 = (f32[24,256]{1,0:T(8,128)S(1)}, f32[24,256]{1,0:T(8,128)S(1)}, u32[]{:S(2)}, u32[]{:S(2)}) collective-permute-start(f32[24,256]{1,0:T(8,128)S(1)} %slice_add_fusion.3.refs_0_), channel_id=1, source_target_pairs={{4,0},{0,4},{12,8},{8,12},{20,16},{16,20},{28,24},{24,28},{5,1},{1... | collective-permute-start | bytes 73736 | tf_op jit(solution)/shard_map/ppermute | solution.py:54

commit v17 on v16

--- a/solution.py
+++ b/solution.py
@@ -132,8 +132,7 @@
 
 
 def build_kernel(sizes, *refs):
-    entries_ref, x_ref, y_ref, dense_ref, x_out, y_out, token_ref = refs[3:10]
-    rows_ref, cols_ref, count_ref, tiles, sems = refs[10:]
+    entries_ref, dense_ref, token_ref, rows_ref, cols_ref, count_ref, tiles, sems = refs[3:]
     n_row, n_col, piece_blocks, group = sizes
     _, _, slot_count, tile_len, _ = entries_ref.shape
     me_row, me_col = lax.axis_index("row"), lax.axis_index("col")
@@ -143,12 +142,12 @@
         source = entries_ref.at[0, 0, pl.ds(index * group, group)]
         return pltpu.make_async_copy(source, tiles.at[pl.ds(index * group, group)], sems.at[index])
 
-    small = [*zip(refs[:3], refs[10:13]), (y_ref, y_out), (x_ref, x_out)]
+    small = zip(refs[:3], (rows_ref, cols_ref, count_ref))
     small = [
         pltpu.make_async_copy(source, target, sems.at[chunk_count + index])
         for index, (source, target) in enumerate(small)
     ]
-    for copy in small[:3]:
+    for copy in small:
         copy.start()
     sure_count = min(2, chunk_count)
     for index in range(sure_count):
@@ -160,7 +159,7 @@
 
     half = dense_ref.shape[0] // 2
     lax.fori_loop(0, half, clear, 0)
-    for copy in small[:3]:
+    for copy in small:
         copy.wait()
     used_count = jnp.maximum((count_ref[0, 0] + group - 1) // group, sure_count)
     for index in range(sure_count, chunk_count):
@@ -169,8 +168,6 @@
         def _():
             chunk(index).start()
 
-    for copy in small[3:]:
-        copy.start()
     lax.fori_loop(half, dense_ref.shape[0], clear, 0)
 
     def place(slot):
@@ -192,42 +189,57 @@
         return carry
 
     lax.fori_loop(0, used_count, step, 0)
-    for copy in small[3:]:
-        copy.wait()
     token_ref[...] = jnp.zeros_like(token_ref)
 
 
-def build_dense(tiles, block_x, block_y, sizes):
+def load_pieces(*pieces):
+    def kernel(*refs):
+        count, sems = len(pieces), refs[-1]
+        copies = [
+            pltpu.make_async_copy(refs[index], refs[count + index], sems.at[index])
+            for index in range(count)
+        ]
+        for copy in copies:
+            copy.start()
+        for copy in copies:
+            copy.wait()
+
+    return pl.pallas_call(
+        kernel,
+        in_specs=[pl.BlockSpec(memory_space=pltpu.HBM)] * len(pieces),
+        out_specs=[pl.BlockSpec(memory_space=pltpu.VMEM)] * len(pieces),
+        out_shape=[held(*piece.shape) for piece in pieces],
+        scratch_shapes=[pltpu.SemaphoreType.DMA((len(pieces),))],
+        compiler_params=pltpu.CompilerParams(vmem_limit_bytes=SMALL_LIMIT),
+    )(*(pltpu.with_memory_space_constraint(piece, pltpu.HBM) for piece in pieces))
+
+
+def build_dense(tiles, sizes):
     tile_rows, tile_cols, tile_count, tile_entries = tiles
     n_row, n_col, piece_blocks = sizes
     _, _, slot_count, tile_len, _ = tile_entries.shape
     group = next(size for size in (8, 4, 2, 1) if slot_count % size == 0)
     shape = (n_col * piece_blocks, n_row * piece_blocks * tile_len, 2 * tile_len)
     hbm = pl.BlockSpec(memory_space=pltpu.HBM)
-    rows, cols, entries, x_piece, y_piece = (
+    rows, cols, entries = (
         pltpu.with_memory_space_constraint(part, pltpu.HBM)
-        for part in (tile_rows, tile_cols, tile_entries, block_x, block_y)
+        for part in (tile_rows, tile_cols, tile_entries)
     )
     return pl.pallas_call(
         functools.partial(build_kernel, (*sizes, group)),
-        in_specs=[hbm, hbm, pl.BlockSpec(memory_space=pl.ANY), hbm, hbm, hbm],
-        out_specs=[pl.BlockSpec(memory_space=pltpu.VMEM)] * 4,
-        out_shape=[
-            pltpu.VMEM(shape, jnp.bfloat16),
-            held(*block_x.shape),
-            held(*block_y.shape),
-            held(8, 128),
-        ],
+        in_specs=[hbm, hbm, pl.BlockSpec(memory_space=pl.ANY), hbm],
+        out_specs=[pl.BlockSpec(memory_space=pltpu.VMEM)] * 2,
+        out_shape=[pltpu.VMEM(shape, jnp.bfloat16), held(8, 128)],
         scratch_shapes=[
             *(pltpu.SMEM(part.shape, part.dtype) for part in (tile_rows, tile_cols, tile_count)),
             pltpu.VMEM((slot_count, tile_len, tile_len), jnp.float32),
-            pltpu.SemaphoreType.DMA((slot_count // group + 5,)),
+            pltpu.SemaphoreType.DMA((slot_count // group + 3,)),
         ],
         compiler_params=pltpu.CompilerParams(vmem_limit_bytes=VMEM_LIMIT),
         cost_estimate=pl.CostEstimate(
             flops=8 * tile_entries.size, bytes_accessed=8 * tile_entries.size, transcendentals=0
         ),
-    )(rows, cols, tile_count, entries, x_piece, y_piece)
+    )(rows, cols, tile_count, entries)
 
 
 def half_products(half, span, pieces_ref, dense_ref, digits, block):
@@ -537,11 +549,11 @@
     sizes = (n_row, n_col, piece_blocks)
     is_dense = n_col * piece_blocks * n_row * piece_blocks <= DENSE_CELLS * slot_count
     if is_dense:
-        dense, x_own, y_own, token = build_dense(tiles, block_x, block_y, sizes)
+        dense, token = build_dense(tiles, sizes)
         before = [token]
     else:
         positions, a_digits = sparse_tiles(tiles, sizes)
-        x_own, y_own, before = block_x, block_y, []
+        before = []
 
     def multiply_evens(evens):
         return dense_first(evens, span, dense) if is_dense else evens
@@ -552,8 +564,9 @@
             return dense_second(odds, evens, sums, span, n_col, tails, dense, before)
         return sparse_second(odds, evens, span, n_col, tails, positions, a_digits)
 
-    y_came = fetch_evens(block_y, "row")
-    x_came = fetch_evens(block_x, "col")
+    x_own, y_own = load_pieces(block_x, block_y)
+    y_came = fetch_evens(y_own, "row")
+    x_came = fetch_evens(x_own, "col")
     evens = stack_after([y_own] + y_came, [*before, *x_came])
     x_evens = stack_after([x_own] + x_came)
     outs = multiply(evens, [x_evens])

time: 67 us -> 67.9 us (1.013)
  Pallas kernels: 11.1 us -> 13 us
    pallas_call x1, Pallas kernels: 1.76 us -> 2.79 us  [build_dense(): pl.pallas_call(functools.partial(build_kernel, (*sizes, group)), in_specs...]
    pallas_call x0 -> x1, Pallas kernels: none -> 0.89 us  [load_pieces(): pl.pallas_call(kernel, in_specs=[pl.BlockSpec(memory_space=pltpu.HBM)] *...]
  transfers between devices with their start and end apart: 28 -> 28, of which waited for: 13 -> 13; matrix products, arithmetic and copies ran while one was open for 1% -> 1% of each run, Pallas kernels for 13% -> 14%
where the time goes in v17:
time: 67.9 us; the launch traced here: 67.7 us
  starting transfers between devices  32.5 us (48%)
  waiting for transfers between devices  20 us (29%)
  Pallas kernels  13 us (19%)
  between operations  1.51 us (2%)
  other arithmetic  0.68 us (1%)
    ppermute x19, starting transfers between devices, fetch(): lax.ppermute(piece, axis, [(partner(i, shift, size), i) for i in range(si...  19.2 us
    ppermute x9, starting transfers between devices, scatter_pieces(): lax.ppermute(pieces[shift], axis, [(i, partner(i, shift, size)) for i in...  13.4 us
    ppermute x19, waiting for transfers between devices, fetch(): lax.ppermute(piece, axis, [(partner(i, shift, size), i) for i in range(si...  12.6 us
    pallas_call x16, Pallas kernels, call(): pl.pallas_call(body, in_specs=[vmem] * len(operands) + [pl.BlockSpec(memo...  9.36 us
    ppermute x9, waiting for transfers between devices, scatter_pieces(): lax.ppermute(pieces[shift], axis, [(i, partner(i, shift, size)) for i in...  7.36 us
    pallas_call x1, Pallas kernels, build_dense(): pl.pallas_call(functools.partial(build_kernel, (*sizes, group)), in_specs...  2.79 us
  transfers between devices with their start and end apart: 28, of which 13 were waited for; matrix products, arithmetic and copies ran while one was open for 1% of the time, Pallas kernels for 14%

profile of v17, /device:TPU:0, one launch (start us, length us, event | category | flops | bytes accessed | tf_op | source)
XLA Modules:
  0.0 67.7 jit_solution(11443023559526988911)
XLA Ops:
  0.6 0.9 %shard_map.77 = (f32[64,256]{1,0:T(8,128)S(1)}, f32[64,256]{1,0:T(8,128)S(1)}) custom-call(f32[64,256]{1,0:T(8,128)} %refs_0_.2, f32[64,256]{1,0:T(8,128)} %refs_1_.2), custom_call_target="tpu_custom_call" | custom-call | tf_op jit(solution)/shard_map/pallas_call | solution.py:207
  1.5 4.1 %collective-permute-start.3 = (f32[64,256]{1,0:T(8,128)S(1)}, f32[64,256]{1,0:T(8,128)S(1)}, u32[]{:S(2)}, u32[]{:S(2)}) collective-permute-start(f32[64,256]{1,0:T(8,128)S(1)} %get-tuple-element.31.refs_0_), channel_id=1, source_target_pairs={{2,0},{3,1},{0,2},{1,3},{6,4},{7,5},{4,6},{5,7},{10,8},{11,9},{8,1... | collective-permute-start | bytes 196616 | tf_op jit(solution)/shard_map/ppermute | solution.py:54
  5.6 2.4 %collective-permute-start.2 = (f32[64,256]{1,0:T(8,128)S(1)}, f32[64,256]{1,0:T(8,128)S(1)}, u32[]{:S(2)}, u32[]{:S(2)}) collective-permute-start(f32[64,256]{1,0:T(8,128)S(1)} %get-tuple-element.29.refs_0_), channel_id=1, source_target_pairs={{24,0},{28,4},{16,8},{20,12},{8,16},{12,20},{0,24},{4,28},{25,1},{... | collective-permute-start | bytes 196616 | tf_op jit(solution)/shard_map/ppermute | solution.py:54
  8.1 0.5 collective-permute-start.1
  8.6 0.5 collective-permute-start
  9.8 2.8 %shard_map.78 = (bf16[8,2048,256]{2,1,0:T(8,128)(2,1)S(1)}, f32[8,128]{1,0:T(8,128)S(1)}) custom-call(s32[1,1,64]{2,1,0:T(1,128)} %refs_0_.3, s32[1,1,64]{2,1,0:T(1,128)} %refs_1_.3, s32[1,1]{1,0:T(1,128)S(6)} %copy.8.refs_2_, f32[1,1,64,128,128]{4,3,2,1,0:T(8,128)} %refs_3_.1), custom_call_target="tpu_custom_call" | custom-call | flops 8388608 | bytes 8388608 | tf_op jit(solution)/shard_map/pallas_call | solution.py:228
  12.6 0.2 collective-permute-done.refs_1_
  12.9 0.1 collective-permute-start.4
  13.0 1.7 %collective-permute-start.8 = (f32[2,64,256]{2,1,0:T(8,128)S(1)}, f32[2,64,256]{2,1,0:T(8,128)S(1)}, u32[]{:S(2)}, u32[]{:S(2)}) collective-permute-start(f32[2,64,256]{2,1,0:T(8,128)S(1)} %shard_map.81.refs_4_.refs_0_), channel_id=1, source_target_pairs={{1,0},{0,1},{3,2},{2,3},{5,4},{4,5},{7,6},{6,7},{9,8},{8,9},{11,10... | collective-permute-start | bytes 393224 | tf_op jit(solution)/shard_map/ppermute | solution.py:54
  14.7 0.7 %shard_map.80.refs_2_ = f32[3,64,1024]{2,1,0:T(8,128)S(1)} custom-call(f32[4,64,256]{2,1,0:T(8,128)S(1)} %shard_map.79.refs_0_.refs_1_, bf16[8,2048,256]{2,1,0:T(8,128)(2,1)S(1)} %get-tuple-element.32.refs_1_.refs_3_.refs_2_), custom_call_target="tpu_custom_call" | custom-call | flops 536870912 | tf_op jit(solution)/shard_map/pallas_call | solution.py:71
  15.4 0.8 %shard_map.82 = (f32[64,256]{1,0:T(8,128)S(1)}, f32[64,256]{1,0:T(8,128)S(1)}, f32[64,256]{1,0:T(8,128)S(1)}, f32[64,256]{1,0:T(8,128)S(1)}) custom-call(f32[4,64,256]{2,1,0:T(8,128)S(1)} %collective-permute-done.4.refs_0_, f32[4,64,256]{2,1,0:T(8,128)S(1)} %shard_map.79.refs_0_.refs_1_, f32[3,64,1024]{2,1,0:T(8,128)S(1)} %shard_map.80.refs_2_, ...), custom_call_target="tpu_custom_call" | custom-call | flops 536870912 | tf_op jit(solution)/shard_map/pallas_call | solution.py:71
  16.2 0.4 collective-permute-start.5
  16.7 1.8 %collective-permute-start.6 = (f32[64,256]{1,0:T(8,128)S(1)}, f32[64,256]{1,0:T(8,128)S(1)}, u32[]{:S(2)}, u32[]{:S(2)}) collective-permute-start(f32[64,256]{1,0:T(8,128)S(1)} %get-tuple-element.35.refs_5_), channel_id=1, source_target_pairs={{0,2},{1,3},{2,0},{3,1},{4,6},{5,7},{6,4},{7,5},{8,10},{9,11},{10,... | collective-permute-start | bytes 196616 | tf_op jit(solution)/shard_map/ppermute | solution.py:60
  18.4 2.3 %collective-permute-start.7 = (f32[64,256]{1,0:T(8,128)S(1)}, f32[64,256]{1,0:T(8,128)S(1)}, u32[]{:S(2)}, u32[]{:S(2)}) collective-permute-start(f32[64,256]{1,0:T(8,128)S(1)} %get-tuple-element.36.refs_4_), channel_id=1, source_target_pairs={{0,1},{1,0},{2,3},{3,2},{4,5},{5,4},{6,7},{7,6},{8,9},{9,8},{10,11... | collective-permute-start | bytes 196616 | tf_op jit(solution)/shard_map/ppermute | solution.py:60
  20.7 2.7 %shard_map.83 = (f32[4,64,256]{2,1,0:T(8,128)S(1)}, f32[4,68,256]{2,1,0:T(8,128)S(1)}, f32[16,256]{1,0:T(8,128)S(1)}) custom-call(f32[2,64,256]{2,1,0:T(8,128)S(1)} %shard_map.81.refs_4_.refs_0_, f32[2,64,256]{2,1,0:T(8,128)S(1)} %collective-permute-done.8.refs_1_, bf16[8,2048,256]{2,1,0:T(8,128)(2,1)S(1)} %get-tuple-element.32.refs_1_.refs_3_.refs_2_, ...), custom_call_target="tpu_custom_call" | custom-call | flops 1073741824 | tf_op jit(solution)/shard_map/pallas_call | solution.py:71
  23.5 1.4 %collective-permute-done.6.refs_2_ = f32[64,256]{1,0:T(8,128)S(1)} collective-permute-done((f32[64,256]{1,0:T(8,128)S(1)}, f32[64,256]{1,0:T(8,128)S(1)}, u32[]{:S(2)}, u32[]{:S(2)}) %collective-permute-start.6) | collective-permute-done | bytes 65568 | tf_op jit(solution)/shard_map/ppermute | solution.py:60
  24.9 1.9 %collective-permute-start.11 = (f32[64,256]{1,0:T(8,128)S(1)}, f32[64,256]{1,0:T(8,128)S(1)}, u32[]{:S(2)}, u32[]{:S(2)}) collective-permute-start(f32[64,256]{1,0:T(8,128)S(1)} %shard_map.84.refs_0_.refs_4_), channel_id=1, source_target_pairs={{24,0},{28,4},{16,8},{20,12},{8,16},{12,20},{0,24},{4,28},{25,1},{... | collective-permute-start | bytes 196616 | tf_op jit(solution)/shard_map/ppermute | solution.py:54
  26.9 1.4 %collective-permute-start.10 = (f32[64,256]{1,0:T(8,128)S(1)}, f32[64,256]{1,0:T(8,128)S(1)}, u32[]{:S(2)}, u32[]{:S(2)}) collective-permute-start(f32[64,256]{1,0:T(8,128)S(1)} %shard_map.84.refs_0_.refs_4_), channel_id=1, source_target_pairs={{16,0},{20,4},{24,8},{28,12},{0,16},{4,20},{8,24},{12,28},{17,1},{... | collective-permute-start | bytes 196616 | tf_op jit(solution)/shard_map/ppermute | solution.py:54
  28.2 0.2 collective-permute-start.9
  28.5 1.8 %collective-permute-done.11.refs_3_ = f32[64,256]{1,0:T(8,128)S(1)} collective-permute-done((f32[64,256]{1,0:T(8,128)S(1)}, f32[64,256]{1,0:T(8,128)S(1)}, u32[]{:S(2)}, u32[]{:S(2)}) %collective-permute-start.11) | collective-permute-done | bytes 65568 | tf_op jit(solution)/shard_map/ppermute | solution.py:54
  30.3 0.9 %collective-permute-done.10.refs_2_ = f32[64,256]{1,0:T(8,128)S(1)} collective-permute-done((f32[64,256]{1,0:T(8,128)S(1)}, f32[64,256]{1,0:T(8,128)S(1)}, u32[]{:S(2)}, u32[]{:S(2)}) %collective-permute-start.10) | collective-permute-done | bytes 65568 | tf_op jit(solution)/shard_map/ppermute | solution.py:54
  31.1 1.4 %collective-permute-done.9.refs_1_ = f32[64,256]{1,0:T(8,128)S(1)} collective-permute-done((f32[64,256]{1,0:T(8,128)S(1)}, f32[64,256]{1,0:T(8,128)S(1)}, u32[]{:S(2)}, u32[]{:S(2)}) %collective-permute-start.9) | collective-permute-done | bytes 65568 | tf_op jit(solution)/shard_map/ppermute | solution.py:54
  32.7 0.3 collective-permute-start.17
  33.0 0.7 %shard_map.86.refs_2_ = f32[3,64,1024]{2,1,0:T(8,128)S(1)} custom-call(f32[4,64,256]{2,1,0:T(8,128)S(1)} %shard_map.85.refs_0_.refs_1_, bf16[8,2048,256]{2,1,0:T(8,128)(2,1)S(1)} %get-tuple-element.32.refs_1_.refs_3_.refs_2_), custom_call_target="tpu_custom_call" | custom-call | flops 536870912 | tf_op jit(solution)/shard_map/pallas_call | solution.py:71
  33.7 0.4 collective-permute-done.12.refs_0_
  34.1 0.8 %shard_map.87 = (f32[64,256]{1,0:T(8,128)S(1)}, f32[64,256]{1,0:T(8,128)S(1)}, f32[64,256]{1,0:T(8,128)S(1)}, f32[64,256]{1,0:T(8,128)S(1)}) custom-call(f32[4,64,256]{2,1,0:T(8,128)S(1)} %collective-permute-done.12.refs_0_, f32[4,64,256]{2,1,0:T(8,128)S(1)} %shard_map.85.refs_0_.refs_1_, f32[3,64,1024]{2,1,0:T(8,128)S(1)} %shard_map.86.refs_2_, ...), custom_call_target="tpu_custom_call" | custom-call | flops 536870912 | tf_op jit(solution)/shard_map/pallas_call | solution.py:71
  34.9 1.7 %collective-permute-start.14 = (f32[64,256]{1,0:T(8,128)S(1)}, f32[64,256]{1,0:T(8,128)S(1)}, u32[]{:S(2)}, u32[]{:S(2)}) collective-permute-start(f32[64,256]{1,0:T(8,128)S(1)} %get-tuple-element.39), channel_id=1, source_target_pairs={{0,3},{1,2},{2,1},{3,0},{4,7},{5,6},{6,5},{7,4},{8,11},{9,10},{10,... | collective-permute-start | bytes 196616 | tf_op jit(solution)/shard_map/ppermute | solution.py:60
  36.7 2.7 %collective-permute-start.16 = (f32[64,256]{1,0:T(8,128)S(1)}, f32[64,256]{1,0:T(8,128)S(1)}, u32[]{:S(2)}, u32[]{:S(2)}) collective-permute-start(f32[64,256]{1,0:T(8,128)S(1)} %get-tuple-element.41), channel_id=1, source_target_pairs={{0,1},{1,0},{2,3},{3,2},{4,5},{5,4},{6,7},{7,6},{8,9},{9,8},{10,11... | collective-permute-start | bytes 196616 | tf_op jit(solution)/shard_map/ppermute | solution.py:60
  39.4 1.1 %collective-permute-start.18 = (f32[1,64,256]{2,1,0:T(8,128)S(1)}, f32[1,64,256]{2,1,0:T(8,128)S(1)}, u32[]{:S(2)}, u32[]{:S(2)}) collective-permute-start(f32[1,64,256]{2,1,0:T(8,128)S(1)} %get-tuple-element.48), channel_id=1, source_target_pairs={{16,0},{20,4},{24,8},{28,12},{0,16},{4,20},{8,24},{12,28},{17,1},{... | collective-permute-start | bytes 196616 | tf_op jit(solution)/shard_map/ppermute | solution.py:54
  40.5 1.0 %collective-permute-start.19 = (f32[16,256]{1,0:T(8,128)S(1)}, f32[16,256]{1,0:T(8,128)S(1)}, u32[]{:S(2)}, u32[]{:S(2)}) collective-permute-start(f32[16,256]{1,0:T(8,128)S(1)} %get-tuple-element.49.refs_7_), channel_id=1, source_target_pairs={{16,0},{20,4},{24,8},{28,12},{0,16},{4,20},{8,24},{12,28},{17,1},{... | collective-permute-start | bytes 49160 | tf_op jit(solution)/shard_map/ppermute | solution.py:54
  41.5 2.8 %collective-permute-done.19.refs_8_ = f32[16,256]{1,0:T(8,128)S(1)} collective-permute-done((f32[16,256]{1,0:T(8,128)S(1)}, f32[16,256]{1,0:T(8,128)S(1)}, u32[]{:S(2)}, u32[]{:S(2)}) %collective-permute-start.19) | collective-permute-done | bytes 16416 | tf_op jit(solution)/shard_map/ppermute | solution.py:54
  44.3 0.5 shard_map.90
  44.7 1.9 %collective-permute-start.22 = (f32[96,256]{1,0:T(8,128)S(1)}, f32[96,256]{1,0:T(8,128)S(1)}, u32[]{:S(2)}, u32[]{:S(2)}) collective-permute-start(f32[96,256]{1,0:T(8,128)S(1)} %get-tuple-element.50.refs_0_), channel_id=1, source_target_pairs={{24,0},{28,4},{16,8},{20,12},{8,16},{12,20},{0,24},{4,28},{25,1},{... | collective-permute-start | bytes 294920 | tf_op jit(solution)/shard_map/ppermute | solution.py:54
  46.6 0.7 %collective-permute-start.21 = (f32[96,256]{1,0:T(8,128)S(1)}, f32[96,256]{1,0:T(8,128)S(1)}, u32[]{:S(2)}, u32[]{:S(2)}) collective-permute-start(f32[96,256]{1,0:T(8,128)S(1)} %get-tuple-element.50.refs_0_), channel_id=1, source_target_pairs={{16,0},{20,4},{24,8},{28,12},{0,16},{4,20},{8,24},{12,28},{17,1},{... | collective-permute-start | bytes 294920 | tf_op jit(solution)/shard_map/ppermute | solution.py:54
  47.3 1.0 %collective-permute-start.20 = (f32[96,256]{1,0:T(8,128)S(1)}, f32[96,256]{1,0:T(8,128)S(1)}, u32[]{:S(2)}, u32[]{:S(2)}) collective-permute-start(f32[96,256]{1,0:T(8,128)S(1)} %get-tuple-element.50.refs_0_), channel_id=1, source_target_pairs={{8,0},{12,4},{0,8},{4,12},{24,16},{28,20},{16,24},{20,28},{9,1},{1... | collective-permute-start | bytes 294920 | tf_op jit(solution)/shard_map/ppermute | solution.py:54
  48.3 3.0 %collective-permute-done.22.refs_3_ = f32[96,256]{1,0:T(8,128)S(1)} collective-permute-done((f32[96,256]{1,0:T(8,128)S(1)}, f32[96,256]{1,0:T(8,128)S(1)}, u32[]{:S(2)}, u32[]{:S(2)}) %collective-permute-start.22) | collective-permute-done | bytes 98336 | tf_op jit(solution)/shard_map/ppermute | solution.py:54
  51.3 0.6 collective-permute-done.21.refs_2_
  52.1 0.8 %shard_map.92.refs_2_ = f32[3,64,1024]{2,1,0:T(8,128)S(1)} custom-call(f32[4,96,256]{2,1,0:T(8,128)S(1)} %shard_map.91.refs_0_.refs_1_, bf16[8,2048,256]{2,1,0:T(8,128)(2,1)S(1)} %get-tuple-element.32.refs_1_.refs_3_.refs_2_), custom_call_target="tpu_custom_call" | custom-call | flops 536870912 | tf_op jit(solution)/shard_map/pallas_call | solution.py:71
  52.8 1.0 %collective-permute-done.23.refs_0_ = f32[4,96,256]{2,1,0:T(8,128)S(1)} collective-permute-done((f32[4,96,256]{2,1,0:T(8,128)S(1)}, f32[4,96,256]{2,1,0:T(8,128)S(1)}, u32[]{:S(2)}, u32[]{:S(2)}) %collective-permute-start.23) | collective-permute-done | bytes 393248 | tf_op jit(solution)/shard_map/ppermute | solution.py:54
  53.8 0.8 %shard_map.93 = (f32[88,256]{1,0:T(8,128)S(1)}, f32[88,256]{1,0:T(8,128)S(1)}, f32[88,256]{1,0:T(8,128)S(1)}, f32[88,256]{1,0:T(8,128)S(1)}) custom-call(f32[4,96,256]{2,1,0:T(8,128)S(1)} %collective-permute-done.23.refs_0_, f32[4,96,256]{2,1,0:T(8,128)S(1)} %shard_map.91.refs_0_.refs_1_, f32[3,64,1024]{2,1,0:T(8,128)S(1)} %shard_map.92.refs_2_, ...), custom_call_target="tpu_custom_call" | custom-call | flops 536870912 | tf_op jit(solution)/shard_map/pallas_call | solution.py:71
  54.6 1.7 %collective-permute-start.24 = (f32[88,256]{1,0:T(8,128)S(1)}, f32[88,256]{1,0:T(8,128)S(1)}, u32[]{:S(2)}, u32[]{:S(2)}) collective-permute-start(f32[88,256]{1,0:T(8,128)S(1)} %get-tuple-element.53), channel_id=1, source_target_pairs={{0,3},{1,2},{2,1},{3,0},{4,7},{5,6},{6,5},{7,4},{8,11},{9,10},{10,... | collective-permute-start | bytes 270344 | tf_op jit(solution)/shard_map/ppermute | solution.py:60
  56.4 2.7 %collective-permute-start.26 = (f32[88,256]{1,0:T(8,128)S(1)}, f32[88,256]{1,0:T(8,128)S(1)}, u32[]{:S(2)}, u32[]{:S(2)}) collective-permute-start(f32[88,256]{1,0:T(8,128)S(1)} %get-tuple-element.55), channel_id=1, source_target_pairs={{0,1},{1,0},{2,3},{3,2},{4,5},{5,4},{6,7},{7,6},{8,9},{9,8},{10,11... | collective-permute-start | bytes 270344 | tf_op jit(solution)/shard_map/ppermute | solution.py:60
  59.1 3.0 %collective-permute-done.24 = f32[88,256]{1,0:T(8,128)S(1)} collective-permute-done((f32[88,256]{1,0:T(8,128)S(1)}, f32[88,256]{1,0:T(8,128)S(1)}, u32[]{:S(2)}, u32[]{:S(2)}) %collective-permute-start.24) | collective-permute-done | bytes 90144 | tf_op jit(solution)/shard_map/ppermute | solution.py:60
  62.0 3.0 %collective-permute-done.25 = f32[88,256]{1,0:T(8,128)S(1)} collective-permute-done((f32[88,256]{1,0:T(8,128)S(1)}, f32[88,256]{1,0:T(8,128)S(1)}, u32[]{:S(2)}, u32[]{:S(2)}) %collective-permute-start.25) | collective-permute-done | bytes 90144 | tf_op jit(solution)/shard_map/ppermute | solution.py:60
  65.0 0.1 collective-permute-start.27
  65.1 0.7 fusion
  65.8 0.5 collective-permute-done.27.refs_1_
  66.3 1.4 %shard_map.94 = f32[3,64,64]{2,1,0:T(8,128)} custom-call(f32[24,256]{1,0:T(8,128)S(1)} %slice_add_fusion.3.refs_0_, f32[24,256]{1,0:T(8,128)S(1)} %collective-permute-done.27.refs_1_), custom_call_target="tpu_custom_call" | custom-call | tf_op jit(solution)/shard_map/pallas_call | solution.py:71
  (28 shorter events, 0.4 us)
Async XLA Ops:
  1.5 11.0 %collective-permute-start.3 = (f32[64,256]{1,0:T(8,128)S(1)}, f32[64,256]{1,0:T(8,128)S(1)}, u32[]{:S(2)}, u32[]{:S(2)}) collective-permute-start(f32[64,256]{1,0:T(8,128)S(1)} %get-tuple-element.31.refs_0_), channel_id=1, source_target_pairs={{2,0},{3,1},{0,2},{1,3},{6,4},{7,5},{4,6},{5,7},{10,8},{11,9},{8,1... | collective-permute-start | bytes 196616 | tf_op jit(solution)/shard_map/ppermute | solution.py:54
  5.6 7.0 %collective-permute-start.2 = (f32[64,256]{1,0:T(8,128)S(1)}, f32[64,256]{1,0:T(8,128)S(1)}, u32[]{:S(2)}, u32[]{:S(2)}) collective-permute-start(f32[64,256]{1,0:T(8,128)S(1)} %get-tuple-element.29.refs_0_), channel_id=1, source_target_pairs={{24,0},{28,4},{16,8},{20,12},{8,16},{12,20},{0,24},{4,28},{25,1},{... | collective-permute-start | bytes 196616 | tf_op jit(solution)/shard_map/ppermute | solution.py:54
  8.1 4.5 %collective-permute-start.1 = (f32[64,256]{1,0:T(8,128)S(1)}, f32[64,256]{1,0:T(8,128)S(1)}, u32[]{:S(2)}, u32[]{:S(2)}) collective-permute-start(f32[64,256]{1,0:T(8,128)S(1)} %get-tuple-element.29.refs_0_), channel_id=1, source_target_pairs={{16,0},{20,4},{24,8},{28,12},{0,16},{4,20},{8,24},{12,28},{17,1},{... | collective-permute-start | bytes 196616 | tf_op jit(solution)/shard_map/ppermute | solution.py:54
  8.6 4.3 %collective-permute-start = (f32[64,256]{1,0:T(8,128)S(1)}, f32[64,256]{1,0:T(8,128)S(1)}, u32[]{:S(2)}, u32[]{:S(2)}) collective-permute-start(f32[64,256]{1,0:T(8,128)S(1)} %get-tuple-element.29.refs_0_), channel_id=1, source_target_pairs={{8,0},{12,4},{0,8},{4,12},{24,16},{28,20},{16,24},{20,28},{9,1},{1... | collective-permute-start | bytes 196616 | tf_op jit(solution)/shard_map/ppermute | solution.py:54
  12.9 2.6 %collective-permute-start.4 = (f32[4,64,256]{2,1,0:T(8,128)S(1)}, f32[4,64,256]{2,1,0:T(8,128)S(1)}, u32[]{:S(2)}, u32[]{:S(2)}) collective-permute-start(f32[4,64,256]{2,1,0:T(8,128)S(1)} %shard_map.79.refs_0_.refs_1_), channel_id=1, source_target_pairs={{4,0},{0,4},{12,8},{8,12},{20,16},{16,20},{28,24},{24,28},{5,1},{1... | collective-permute-start | bytes 786440 | tf_op jit(solution)/shard_map/ppermute | solution.py:54
  13.0 7.7 %collective-permute-start.8 = (f32[2,64,256]{2,1,0:T(8,128)S(1)}, f32[2,64,256]{2,1,0:T(8,128)S(1)}, u32[]{:S(2)}, u32[]{:S(2)}) collective-permute-start(f32[2,64,256]{2,1,0:T(8,128)S(1)} %shard_map.81.refs_4_.refs_0_), channel_id=1, source_target_pairs={{1,0},{0,1},{3,2},{2,3},{5,4},{4,5},{7,6},{6,7},{9,8},{8,9},{11,10... | collective-permute-start | bytes 393224 | tf_op jit(solution)/shard_map/ppermute | solution.py:54
  16.2 7.2 %collective-permute-start.5 = (f32[64,256]{1,0:T(8,128)S(1)}, f32[64,256]{1,0:T(8,128)S(1)}, u32[]{:S(2)}, u32[]{:S(2)}) collective-permute-start(f32[64,256]{1,0:T(8,128)S(1)} %get-tuple-element.34.refs_6_), channel_id=1, source_target_pairs={{0,3},{1,2},{2,1},{3,0},{4,7},{5,6},{6,5},{7,4},{8,11},{9,10},{10,... | collective-permute-start | bytes 196616 | tf_op jit(solution)/shard_map/ppermute | solution.py:60
  16.7 8.2 %collective-permute-start.6 = (f32[64,256]{1,0:T(8,128)S(1)}, f32[64,256]{1,0:T(8,128)S(1)}, u32[]{:S(2)}, u32[]{:S(2)}) collective-permute-start(f32[64,256]{1,0:T(8,128)S(1)} %get-tuple-element.35.refs_5_), channel_id=1, source_target_pairs={{0,2},{1,3},{2,0},{3,1},{4,6},{5,7},{6,4},{7,5},{8,10},{9,11},{10,... | collective-permute-start | bytes 196616 | tf_op jit(solution)/shard_map/ppermute | solution.py:60
  18.4 6.5 %collective-permute-start.7 = (f32[64,256]{1,0:T(8,128)S(1)}, f32[64,256]{1,0:T(8,128)S(1)}, u32[]{:S(2)}, u32[]{:S(2)}) collective-permute-start(f32[64,256]{1,0:T(8,128)S(1)} %get-tuple-element.36.refs_4_), channel_id=1, source_target_pairs={{0,1},{1,0},{2,3},{3,2},{4,5},{5,4},{6,7},{7,6},{8,9},{9,8},{10,11... | collective-permute-start | bytes 196616 | tf_op jit(solution)/shard_map/ppermute | solution.py:60
  23.4 9.2 %collective-permute-start.13 = (f32[4,68,256]{2,1,0:T(8,128)S(1)}, f32[4,68,256]{2,1,0:T(8,128)S(1)}, u32[]{:S(2)}, u32[]{:S(2)}) collective-permute-start(f32[4,68,256]{2,1,0:T(8,128)S(1)} %get-tuple-element.37.refs_4_), channel_id=1, source_target_pairs={{4,0},{0,4},{12,8},{8,12},{20,16},{16,20},{28,24},{24,28},{5,1},{1... | collective-permute-start | bytes 835592 | tf_op jit(solution)/shard_map/ppermute | solution.py:54
  24.9 5.3 %collective-permute-start.11 = (f32[64,256]{1,0:T(8,128)S(1)}, f32[64,256]{1,0:T(8,128)S(1)}, u32[]{:S(2)}, u32[]{:S(2)}) collective-permute-start(f32[64,256]{1,0:T(8,128)S(1)} %shard_map.84.refs_0_.refs_4_), channel_id=1, source_target_pairs={{24,0},{28,4},{16,8},{20,12},{8,16},{12,20},{0,24},{4,28},{25,1},{... | collective-permute-start | bytes 196616 | tf_op jit(solution)/shard_map/ppermute | solution.py:54
  26.9 4.3 %collective-permute-start.10 = (f32[64,256]{1,0:T(8,128)S(1)}, f32[64,256]{1,0:T(8,128)S(1)}, u32[]{:S(2)}, u32[]{:S(2)}) collective-permute-start(f32[64,256]{1,0:T(8,128)S(1)} %shard_map.84.refs_0_.refs_4_), channel_id=1, source_target_pairs={{16,0},{20,4},{24,8},{28,12},{0,16},{4,20},{8,24},{12,28},{17,1},{... | collective-permute-start | bytes 196616 | tf_op jit(solution)/shard_map/ppermute | solution.py:54
  28.2 4.3 %collective-permute-start.9 = (f32[64,256]{1,0:T(8,128)S(1)}, f32[64,256]{1,0:T(8,128)S(1)}, u32[]{:S(2)}, u32[]{:S(2)}) collective-permute-start(f32[64,256]{1,0:T(8,128)S(1)} %shard_map.84.refs_0_.refs_4_), channel_id=1, source_target_pairs={{8,0},{12,4},{0,8},{4,12},{24,16},{28,20},{16,24},{20,28},{9,1},{1... | collective-permute-start | bytes 196616 | tf_op jit(solution)/shard_map/ppermute | solution.py:54
  32.5 1.6 %collective-permute-start.12 = (f32[4,64,256]{2,1,0:T(8,128)S(1)}, f32[4,64,256]{2,1,0:T(8,128)S(1)}, u32[]{:S(2)}, u32[]{:S(2)}) collective-permute-start(f32[4,64,256]{2,1,0:T(8,128)S(1)} %shard_map.85.refs_0_.refs_1_), channel_id=1, source_target_pairs={{4,0},{0,4},{12,8},{8,12},{20,16},{16,20},{28,24},{24,28},{5,1},{1... | collective-permute-start | bytes 786440 | tf_op jit(solution)/shard_map/ppermute | solution.py:54
  32.7 6.7 %collective-permute-start.17 = (f32[2,72,256]{2,1,0:T(8,128)S(1)}, f32[2,72,256]{2,1,0:T(8,128)S(1)}, u32[]{:S(2)}, u32[]{:S(2)}) collective-permute-start(f32[2,72,256]{2,1,0:T(8,128)S(1)} %get-tuple-element.45), channel_id=1, source_target_pairs={{8,0},{12,4},{0,8},{4,12},{24,16},{28,20},{16,24},{20,28},{9,1},{1... | collective-permute-start | bytes 442376 | tf_op jit(solution)/shard_map/ppermute | solution.py:54
  34.9 9.3 %collective-permute-start.14 = (f32[64,256]{1,0:T(8,128)S(1)}, f32[64,256]{1,0:T(8,128)S(1)}, u32[]{:S(2)}, u32[]{:S(2)}) collective-permute-start(f32[64,256]{1,0:T(8,128)S(1)} %get-tuple-element.39), channel_id=1, source_target_pairs={{0,3},{1,2},{2,1},{3,0},{4,7},{5,6},{6,5},{7,4},{8,11},{9,10},{10,... | collective-permute-start | bytes 196616 | tf_op jit(solution)/shard_map/ppermute | solution.py:60
  36.7 7.6 %collective-permute-start.15 = (f32[64,256]{1,0:T(8,128)S(1)}, f32[64,256]{1,0:T(8,128)S(1)}, u32[]{:S(2)}, u32[]{:S(2)}) collective-permute-start(f32[64,256]{1,0:T(8,128)S(1)} %get-tuple-element.40), channel_id=1, source_target_pairs={{0,2},{1,3},{2,0},{3,1},{4,6},{5,7},{6,4},{7,5},{8,10},{9,11},{10,... | collective-permute-start | bytes 196616 | tf_op jit(solution)/shard_map/ppermute | solution.py:60
  36.7 7.6 %collective-permute-start.16 = (f32[64,256]{1,0:T(8,128)S(1)}, f32[64,256]{1,0:T(8,128)S(1)}, u32[]{:S(2)}, u32[]{:S(2)}) collective-permute-start(f32[64,256]{1,0:T(8,128)S(1)} %get-tuple-element.41), channel_id=1, source_target_pairs={{0,1},{1,0},{2,3},{3,2},{4,5},{5,4},{6,7},{7,6},{8,9},{9,8},{10,11... | collective-permute-start | bytes 196616 | tf_op jit(solution)/shard_map/ppermute | solution.py:60
  39.4 4.9 %collective-permute-start.18 = (f32[1,64,256]{2,1,0:T(8,128)S(1)}, f32[1,64,256]{2,1,0:T(8,128)S(1)}, u32[]{:S(2)}, u32[]{:S(2)}) collective-permute-start(f32[1,64,256]{2,1,0:T(8,128)S(1)} %get-tuple-element.48), channel_id=1, source_target_pairs={{16,0},{20,4},{24,8},{28,12},{0,16},{4,20},{8,24},{12,28},{17,1},{... | collective-permute-start | bytes 196616 | tf_op jit(solution)/shard_map/ppermute | solution.py:54
  40.5 3.7 %collective-permute-start.19 = (f32[16,256]{1,0:T(8,128)S(1)}, f32[16,256]{1,0:T(8,128)S(1)}, u32[]{:S(2)}, u32[]{:S(2)}) collective-permute-start(f32[16,256]{1,0:T(8,128)S(1)} %get-tuple-element.49.refs_7_), channel_id=1, source_target_pairs={{16,0},{20,4},{24,8},{28,12},{0,16},{4,20},{8,24},{12,28},{17,1},{... | collective-permute-start | bytes 49160 | tf_op jit(solution)/shard_map/ppermute | solution.py:54
  44.7 6.6 %collective-permute-start.22 = (f32[96,256]{1,0:T(8,128)S(1)}, f32[96,256]{1,0:T(8,128)S(1)}, u32[]{:S(2)}, u32[]{:S(2)}) collective-permute-start(f32[96,256]{1,0:T(8,128)S(1)} %get-tuple-element.50.refs_0_), channel_id=1, source_target_pairs={{24,0},{28,4},{16,8},{20,12},{8,16},{12,20},{0,24},{4,28},{25,1},{... | collective-permute-start | bytes 294920 | tf_op jit(solution)/shard_map/ppermute | solution.py:54
  46.6 5.4 %collective-permute-start.21 = (f32[96,256]{1,0:T(8,128)S(1)}, f32[96,256]{1,0:T(8,128)S(1)}, u32[]{:S(2)}, u32[]{:S(2)}) collective-permute-start(f32[96,256]{1,0:T(8,128)S(1)} %get-tuple-element.50.refs_0_), channel_id=1, source_target_pairs={{16,0},{20,4},{24,8},{28,12},{0,16},{4,20},{8,24},{12,28},{17,1},{... | collective-permute-start | bytes 294920 | tf_op jit(solution)/shard_map/ppermute | solution.py:54
  47.3 4.7 %collective-permute-start.20 = (f32[96,256]{1,0:T(8,128)S(1)}, f32[96,256]{1,0:T(8,128)S(1)}, u32[]{:S(2)}, u32[]{:S(2)}) collective-permute-start(f32[96,256]{1,0:T(8,128)S(1)} %get-tuple-element.50.refs_0_), channel_id=1, source_target_pairs={{8,0},{12,4},{0,8},{4,12},{24,16},{28,20},{16,24},{20,28},{9,1},{1... | collective-permute-start | bytes 294920 | tf_op jit(solution)/shard_map/ppermute | solution.py:54
  52.0 1.8 %collective-permute-start.23 = (f32[4,96,256]{2,1,0:T(8,128)S(1)}, f32[4,96,256]{2,1,0:T(8,128)S(1)}, u32[]{:S(2)}, u32[]{:S(2)}) collective-permute-start(f32[4,96,256]{2,1,0:T(8,128)S(1)} %shard_map.91.refs_0_.refs_1_), channel_id=1, source_target_pairs={{4,0},{0,4},{12,8},{8,12},{20,16},{16,20},{28,24},{24,28},{5,1},{1... | collective-permute-start | bytes 1179656 | tf_op jit(solution)/shard_map/ppermute | solution.py:54
  54.6 7.4 %collective-permute-start.24 = (f32[88,256]{1,0:T(8,128)S(1)}, f32[88,256]{1,0:T(8,128)S(1)}, u32[]{:S(2)}, u32[]{:S(2)}) collective-permute-start(f32[88,256]{1,0:T(8,128)S(1)} %get-tuple-element.53), channel_id=1, source_target_pairs={{0,3},{1,2},{2,1},{3,0},{4,7},{5,6},{6,5},{7,4},{8,11},{9,10},{10,... | collective-permute-start | bytes 270344 | tf_op jit(solution)/shard_map/ppermute | solution.py:60
  56.4 8.6 %collective-permute-start.25 = (f32[88,256]{1,0:T(8,128)S(1)}, f32[88,256]{1,0:T(8,128)S(1)}, u32[]{:S(2)}, u32[]{:S(2)}) collective-permute-start(f32[88,256]{1,0:T(8,128)S(1)} %get-tuple-element.54), channel_id=1, source_target_pairs={{0,2},{1,3},{2,0},{3,1},{4,6},{5,7},{6,4},{7,5},{8,10},{9,11},{10,... | collective-permute-start | bytes 270344 | tf_op jit(solution)/shard_map/ppermute | solution.py:60
  56.4 8.6 %collective-permute-start.26 = (f32[88,256]{1,0:T(8,128)S(1)}, f32[88,256]{1,0:T(8,128)S(1)}, u32[]{:S(2)}, u32[]{:S(2)}) collective-permute-start(f32[88,256]{1,0:T(8,128)S(1)} %get-tuple-element.55), channel_id=1, source_target_pairs={{0,1},{1,0},{2,3},{3,2},{4,5},{5,4},{6,7},{7,6},{8,9},{9,8},{10,11... | collective-permute-start | bytes 270344 | tf_op jit(solution)/shard_map/ppermute | solution.py:60
  65.0 1.3 %collective-permute-start.27 = (f32[24,256]{1,0:T(8,128)S(1)}, f32[24,256]{1,0:T(8,128)S(1)}, u32[]{:S(2)}, u32[]{:S(2)}) collective-permute-start(f32[24,256]{1,0:T(8,128)S(1)} %slice_add_fusion.3.refs_0_), channel_id=1, source_target_pairs={{4,0},{0,4},{12,8},{8,12},{20,16},{16,20},{28,24},{24,28},{5,1},{1... | collective-permute-start | bytes 73736 | tf_op jit(solution)/shard_map/ppermute | solution.py:54

commit v18 on v16

--- a/solution.py
+++ b/solution.py
@@ -555,8 +555,8 @@
     y_came = fetch_evens(block_y, "row")
     x_came = fetch_evens(block_x, "col")
     evens = stack_after([y_own] + y_came, [*before, *x_came])
-    x_evens = stack_after([x_own] + x_came)
-    outs = multiply(evens, [x_evens])
+    outs = multiply(evens)
+    x_evens = stack_after([x_own] + x_came, [outs[0]])
     x_pairs = [x_evens, gather_odds(x_evens, "col")]
     if is_dense:
         w_kept, w_odds, term = dense_left(x_pairs, outs, n_row, dense)

time: 67 us -> 68.3 us (1.019); the launches traced: 66.8 us -> 68.8 us
  starting transfers between devices: 32.9 us -> 34.7 us
  Pallas kernels: 11.1 us -> 12.2 us
  waiting for transfers between devices: 20.6 us -> 19.8 us
    ppermute x19, starting transfers between devices: 19.5 us -> 21.4 us  [fetch(): lax.ppermute(piece, axis, [(partner(i, shift, size), i) for i in range(si...]
    ppermute x19, waiting for transfers between devices: 13.3 us -> 12.2 us  [fetch(): lax.ppermute(piece, axis, [(partner(i, shift, size), i) for i in range(si...]
    pallas_call x1, Pallas kernels: 1.76 us -> 2.81 us  [build_dense(): pl.pallas_call(functools.partial(build_kernel, (*sizes, group)), in_specs...]
  transfers between devices with their start and end apart: 28 -> 28, of which waited for: 13 -> 16; matrix products, arithmetic and copies ran while one was open for 1% -> 1% of each run, Pallas kernels for 13% -> 13%
where the time goes in v18:
time: 68.3 us; the launch traced here: 68.8 us
  starting transfers between devices  34.7 us (51%)
  waiting for transfers between devices  19.8 us (29%)
  Pallas kernels  12.2 us (18%)
  between operations  1.5 us (2%)
    ppermute x19, starting transfers between devices, fetch(): lax.ppermute(piece, axis, [(partner(i, shift, size), i) for i in range(si...  21.4 us
    ppermute x9, starting transfers between devices, scatter_pieces(): lax.ppermute(pieces[shift], axis, [(i, partner(i, shift, size)) for i in...  13.3 us
    ppermute x19, waiting for transfers between devices, fetch(): lax.ppermute(piece, axis, [(partner(i, shift, size), i) for i in range(si...  12.2 us
    pallas_call x16, Pallas kernels, call(): pl.pallas_call(body, in_specs=[vmem] * len(operands) + [pl.BlockSpec(memo...  9.35 us
    ppermute x9, waiting for transfers between devices, scatter_pieces(): lax.ppermute(pieces[shift], axis, [(i, partner(i, shift, size)) for i in...  7.58 us
    pallas_call x1, Pallas kernels, build_dense(): pl.pallas_call(functools.partial(build_kernel, (*sizes, group)), in_specs...  2.81 us
  transfers between devices with their start and end apart: 28, of which 16 were waited for; matrix products, arithmetic and copies ran while one was open for 1% of the time, Pallas kernels for 13%

profile of v18, /device:TPU:0, one launch (start us, length us, event | category | flops | bytes accessed | tf_op | source)
XLA Modules:
  0.0 68.8 jit_solution(10202403773108090086)
XLA Ops:
  0.6 4.1 %collective-permute-start.3 = (f32[64,256]{1,0:T(8,128)}, f32[64,256]{1,0:T(8,128)S(1)}, u32[]{:S(2)}, u32[]{:S(2)}) collective-permute-start(f32[64,256]{1,0:T(8,128)} %refs_4_.1), channel_id=1, source_target_pairs={{2,0},{3,1},{0,2},{1,3},{6,4},{7,5},{4,6},{5,7},{10,8},{11,9},{8,1... | collective-permute-start | bytes 196616 | tf_op jit(solution)/shard_map/ppermute | solution.py:54
  4.7 1.5 %collective-permute-start = (f32[64,256]{1,0:T(8,128)}, f32[64,256]{1,0:T(8,128)S(1)}, u32[]{:S(2)}, u32[]{:S(2)}) collective-permute-start(f32[64,256]{1,0:T(8,128)} %refs_5_.1), channel_id=1, source_target_pairs={{8,0},{12,4},{0,8},{4,12},{24,16},{28,20},{16,24},{20,28},{9,1},{1... | collective-permute-start | bytes 196616 | tf_op jit(solution)/shard_map/ppermute | solution.py:54
  6.2 1.5 %collective-permute-start.2 = (f32[64,256]{1,0:T(8,128)}, f32[64,256]{1,0:T(8,128)S(1)}, u32[]{:S(2)}, u32[]{:S(2)}) collective-permute-start(f32[64,256]{1,0:T(8,128)} %refs_5_.1), channel_id=1, source_target_pairs={{24,0},{28,4},{16,8},{20,12},{8,16},{12,20},{0,24},{4,28},{25,1},{... | collective-permute-start | bytes 196616 | tf_op jit(solution)/shard_map/ppermute | solution.py:54
  7.7 0.5 collective-permute-start.1
  8.9 2.8 %shard_map.77 = (bf16[8,2048,256]{2,1,0:T(8,128)(2,1)S(1)}, f32[64,256]{1,0:T(8,128)S(1)}, f32[64,256]{1,0:T(8,128)S(1)}, f32[8,128]{1,0:T(8,128)S(1)}) custom-call(s32[1,1,64]{2,1,0:T(1,128)} %refs_0_.1, s32[1,1,64]{2,1,0:T(1,128)} %refs_1_.1, s32[1,1]{1,0:T(1,128)S(6)} %copy.8.refs_2_, f32[1,1,64,128,128]{4,3,2,1,0:T(8,128)} %refs_3_.1, ...), custom_call_target="tpu_custom_call" | custom-call | flops 8388608 | bytes 8388608 | tf_op jit(solution)/shard_map/pallas_call | solution.py:211
  11.7 0.6 collective-permute-done.1.refs_2_
  12.4 0.8 %shard_map.79.refs_2_ = f32[3,64,1024]{2,1,0:T(8,128)S(1)} custom-call(f32[4,64,256]{2,1,0:T(8,128)S(1)} %shard_map.78.refs_0_.refs_1_, bf16[8,2048,256]{2,1,0:T(8,128)(2,1)S(1)} %get-tuple-element.31.refs_1_.refs_3_.refs_2_), custom_call_target="tpu_custom_call" | custom-call | flops 536870912 | tf_op jit(solution)/shard_map/pallas_call | solution.py:71
  13.2 0.8 %collective-permute-done.4.refs_0_ = f32[4,64,256]{2,1,0:T(8,128)S(1)} collective-permute-done((f32[4,64,256]{2,1,0:T(8,128)S(1)}, f32[4,64,256]{2,1,0:T(8,128)S(1)}, u32[]{:S(2)}, u32[]{:S(2)}) %collective-permute-start.4) | collective-permute-done | bytes 262176 | tf_op jit(solution)/shard_map/ppermute | solution.py:54
  13.9 0.8 %shard_map.80 = (f32[64,256]{1,0:T(8,128)S(1)}, f32[64,256]{1,0:T(8,128)S(1)}, f32[64,256]{1,0:T(8,128)S(1)}, f32[64,256]{1,0:T(8,128)S(1)}) custom-call(f32[4,64,256]{2,1,0:T(8,128)S(1)} %collective-permute-done.4.refs_0_, f32[4,64,256]{2,1,0:T(8,128)S(1)} %shard_map.78.refs_0_.refs_1_, f32[3,64,1024]{2,1,0:T(8,128)S(1)} %shard_map.79.refs_2_, ...), custom_call_target="tpu_custom_call" | custom-call | flops 536870912 | tf_op jit(solution)/shard_map/pallas_call | solution.py:71
  14.7 1.6 %collective-permute-start.8 = (f32[2,64,256]{2,1,0:T(8,128)S(1)}, f32[2,64,256]{2,1,0:T(8,128)S(1)}, u32[]{:S(2)}, u32[]{:S(2)}) collective-permute-start(f32[2,64,256]{2,1,0:T(8,128)S(1)} %shard_map.81.refs_0_), channel_id=1, source_target_pairs={{1,0},{0,1},{3,2},{2,3},{5,4},{4,5},{7,6},{6,7},{9,8},{8,9},{11,10... | collective-permute-start | bytes 393224 | tf_op jit(solution)/shard_map/ppermute | solution.py:54
  16.4 0.2 collective-permute-start.5
  16.6 1.7 %collective-permute-start.6 = (f32[64,256]{1,0:T(8,128)S(1)}, f32[64,256]{1,0:T(8,128)S(1)}, u32[]{:S(2)}, u32[]{:S(2)}) collective-permute-start(f32[64,256]{1,0:T(8,128)S(1)} %get-tuple-element.34.refs_5_), channel_id=1, source_target_pairs={{0,2},{1,3},{2,0},{3,1},{4,6},{5,7},{6,4},{7,5},{8,10},{9,11},{10,... | collective-permute-start | bytes 196616 | tf_op jit(solution)/shard_map/ppermute | solution.py:60
  18.3 2.5 %collective-permute-start.7 = (f32[64,256]{1,0:T(8,128)S(1)}, f32[64,256]{1,0:T(8,128)S(1)}, u32[]{:S(2)}, u32[]{:S(2)}) collective-permute-start(f32[64,256]{1,0:T(8,128)S(1)} %get-tuple-element.35.refs_4_), channel_id=1, source_target_pairs={{0,1},{1,0},{2,3},{3,2},{4,5},{5,4},{6,7},{7,6},{8,9},{9,8},{10,11... | collective-permute-start | bytes 196616 | tf_op jit(solution)/shard_map/ppermute | solution.py:60
  20.8 0.9 %collective-permute-done.8.refs_1_ = f32[2,64,256]{2,1,0:T(8,128)S(1)} collective-permute-done((f32[2,64,256]{2,1,0:T(8,128)S(1)}, f32[2,64,256]{2,1,0:T(8,128)S(1)}, u32[]{:S(2)}, u32[]{:S(2)}) %collective-permute-start.8) | collective-permute-done | bytes 131104 | tf_op jit(solution)/shard_map/ppermute | solution.py:54
  21.7 2.7 %shard_map.82 = (f32[4,64,256]{2,1,0:T(8,128)S(1)}, f32[4,68,256]{2,1,0:T(8,128)S(1)}, f32[16,256]{1,0:T(8,128)S(1)}) custom-call(f32[2,64,256]{2,1,0:T(8,128)S(1)} %shard_map.81.refs_0_, f32[2,64,256]{2,1,0:T(8,128)S(1)} %collective-permute-done.8.refs_1_, bf16[8,2048,256]{2,1,0:T(8,128)(2,1)S(1)} %get-tuple-element.31.refs_1_.refs_3_.refs_2_, ...), custom_call_target="tpu_custom_call" | custom-call | flops 1073741824 | tf_op jit(solution)/shard_map/pallas_call | solution.py:71
  24.7 3.8 %collective-permute-start.11 = (f32[64,256]{1,0:T(8,128)S(1)}, f32[64,256]{1,0:T(8,128)S(1)}, u32[]{:S(2)}, u32[]{:S(2)}) collective-permute-start(f32[64,256]{1,0:T(8,128)S(1)} %shard_map.83.refs_0_.refs_4_), channel_id=1, source_target_pairs={{24,0},{28,4},{16,8},{20,12},{8,16},{12,20},{0,24},{4,28},{25,1},{... | collective-permute-start | bytes 196616 | tf_op jit(solution)/shard_map/ppermute | solution.py:54
  28.5 0.6 collective-permute-start.9
  29.1 2.1 %collective-permute-done.11.refs_3_ = f32[64,256]{1,0:T(8,128)S(1)} collective-permute-done((f32[64,256]{1,0:T(8,128)S(1)}, f32[64,256]{1,0:T(8,128)S(1)}, u32[]{:S(2)}, u32[]{:S(2)}) %collective-permute-start.11) | collective-permute-done | bytes 65568 | tf_op jit(solution)/shard_map/ppermute | solution.py:54
  31.2 1.5 %collective-permute-done.10.refs_2_ = f32[64,256]{1,0:T(8,128)S(1)} collective-permute-done((f32[64,256]{1,0:T(8,128)S(1)}, f32[64,256]{1,0:T(8,128)S(1)}, u32[]{:S(2)}, u32[]{:S(2)}) %collective-permute-start.10) | collective-permute-done | bytes 65568 | tf_op jit(solution)/shard_map/ppermute | solution.py:54
  32.9 1.7 %collective-permute-start.17 = (f32[2,72,256]{2,1,0:T(8,128)S(1)}, f32[2,72,256]{2,1,0:T(8,128)S(1)}, u32[]{:S(2)}, u32[]{:S(2)}) collective-permute-start(f32[2,72,256]{2,1,0:T(8,128)S(1)} %get-tuple-element.45), channel_id=1, source_target_pairs={{8,0},{12,4},{0,8},{4,12},{24,16},{28,20},{16,24},{20,28},{9,1},{1... | collective-permute-start | bytes 442376 | tf_op jit(solution)/shard_map/ppermute | solution.py:54
  34.6 0.8 %shard_map.85.refs_2_ = f32[3,64,1024]{2,1,0:T(8,128)S(1)} custom-call(f32[4,64,256]{2,1,0:T(8,128)S(1)} %shard_map.84.refs_0_.refs_1_, bf16[8,2048,256]{2,1,0:T(8,128)(2,1)S(1)} %get-tuple-element.31.refs_1_.refs_3_.refs_2_), custom_call_target="tpu_custom_call" | custom-call | flops 536870912 | tf_op jit(solution)/shard_map/pallas_call | solution.py:71
  35.4 0.8 %shard_map.86 = (f32[64,256]{1,0:T(8,128)S(1)}, f32[64,256]{1,0:T(8,128)S(1)}, f32[64,256]{1,0:T(8,128)S(1)}, f32[64,256]{1,0:T(8,128)S(1)}) custom-call(f32[4,64,256]{2,1,0:T(8,128)S(1)} %collective-permute-done.12.refs_0_, f32[4,64,256]{2,1,0:T(8,128)S(1)} %shard_map.84.refs_0_.refs_1_, f32[3,64,1024]{2,1,0:T(8,128)S(1)} %shard_map.85.refs_2_, ...), custom_call_target="tpu_custom_call" | custom-call | flops 536870912 | tf_op jit(solution)/shard_map/pallas_call | solution.py:71
  36.2 0.8 %collective-permute-start.14 = (f32[64,256]{1,0:T(8,128)S(1)}, f32[64,256]{1,0:T(8,128)S(1)}, u32[]{:S(2)}, u32[]{:S(2)}) collective-permute-start(f32[64,256]{1,0:T(8,128)S(1)} %get-tuple-element.39), channel_id=1, source_target_pairs={{0,3},{1,2},{2,1},{3,0},{4,7},{5,6},{6,5},{7,4},{8,11},{9,10},{10,... | collective-permute-start | bytes 196616 | tf_op jit(solution)/shard_map/ppermute | solution.py:60
  37.0 0.3 collective-permute-start.15
  37.3 3.3 %collective-permute-start.16 = (f32[64,256]{1,0:T(8,128)S(1)}, f32[64,256]{1,0:T(8,128)S(1)}, u32[]{:S(2)}, u32[]{:S(2)}) collective-permute-start(f32[64,256]{1,0:T(8,128)S(1)} %get-tuple-element.41), channel_id=1, source_target_pairs={{0,1},{1,0},{2,3},{3,2},{4,5},{5,4},{6,7},{7,6},{8,9},{9,8},{10,11... | collective-permute-start | bytes 196616 | tf_op jit(solution)/shard_map/ppermute | solution.py:60
  40.7 1.1 %collective-permute-start.18 = (f32[1,64,256]{2,1,0:T(8,128)S(1)}, f32[1,64,256]{2,1,0:T(8,128)S(1)}, u32[]{:S(2)}, u32[]{:S(2)}) collective-permute-start(f32[1,64,256]{2,1,0:T(8,128)S(1)} %get-tuple-element.48), channel_id=1, source_target_pairs={{16,0},{20,4},{24,8},{28,12},{0,16},{4,20},{8,24},{12,28},{17,1},{... | collective-permute-start | bytes 196616 | tf_op jit(solution)/shard_map/ppermute | solution.py:54
  41.7 1.0 %collective-permute-start.19 = (f32[16,256]{1,0:T(8,128)S(1)}, f32[16,256]{1,0:T(8,128)S(1)}, u32[]{:S(2)}, u32[]{:S(2)}) collective-permute-start(f32[16,256]{1,0:T(8,128)S(1)} %get-tuple-element.49.refs_7_), channel_id=1, source_target_pairs={{16,0},{20,4},{24,8},{28,12},{0,16},{4,20},{8,24},{12,28},{17,1},{... | collective-permute-start | bytes 49160 | tf_op jit(solution)/shard_map/ppermute | solution.py:54
  42.8 0.3 collective-permute-done.14.refs_1_
  43.1 1.6 %collective-permute-done.15.refs_2_ = f32[64,256]{1,0:T(8,128)S(1)} collective-permute-done((f32[64,256]{1,0:T(8,128)S(1)}, f32[64,256]{1,0:T(8,128)S(1)}, u32[]{:S(2)}, u32[]{:S(2)}) %collective-permute-start.15) | collective-permute-done | bytes 65568 | tf_op jit(solution)/shard_map/ppermute | solution.py:60
  44.6 0.8 %collective-permute-done.19.refs_8_ = f32[16,256]{1,0:T(8,128)S(1)} collective-permute-done((f32[16,256]{1,0:T(8,128)S(1)}, f32[16,256]{1,0:T(8,128)S(1)}, u32[]{:S(2)}, u32[]{:S(2)}) %collective-permute-start.19) | collective-permute-done | bytes 16416 | tf_op jit(solution)/shard_map/ppermute | solution.py:54
  45.5 0.4 shard_map.89
  45.9 1.6 %collective-permute-start.22 = (f32[96,256]{1,0:T(8,128)S(1)}, f32[96,256]{1,0:T(8,128)S(1)}, u32[]{:S(2)}, u32[]{:S(2)}) collective-permute-start(f32[96,256]{1,0:T(8,128)S(1)} %get-tuple-element.50.refs_0_), channel_id=1, source_target_pairs={{24,0},{28,4},{16,8},{20,12},{8,16},{12,20},{0,24},{4,28},{25,1},{... | collective-permute-start | bytes 294920 | tf_op jit(solution)/shard_map/ppermute | solution.py:54
  47.5 1.3 %collective-permute-start.21 = (f32[96,256]{1,0:T(8,128)S(1)}, f32[96,256]{1,0:T(8,128)S(1)}, u32[]{:S(2)}, u32[]{:S(2)}) collective-permute-start(f32[96,256]{1,0:T(8,128)S(1)} %get-tuple-element.50.refs_0_), channel_id=1, source_target_pairs={{16,0},{20,4},{24,8},{28,12},{0,16},{4,20},{8,24},{12,28},{17,1},{... | collective-permute-start | bytes 294920 | tf_op jit(solution)/shard_map/ppermute | solution.py:54
  48.9 0.6 collective-permute-start.20
  49.5 2.5 %collective-permute-done.22.refs_3_ = f32[96,256]{1,0:T(8,128)S(1)} collective-permute-done((f32[96,256]{1,0:T(8,128)S(1)}, f32[96,256]{1,0:T(8,128)S(1)}, u32[]{:S(2)}, u32[]{:S(2)}) %collective-permute-start.22) | collective-permute-done | bytes 98336 | tf_op jit(solution)/shard_map/ppermute | solution.py:54
  52.0 0.8 %collective-permute-done.21.refs_2_ = f32[96,256]{1,0:T(8,128)S(1)} collective-permute-done((f32[96,256]{1,0:T(8,128)S(1)}, f32[96,256]{1,0:T(8,128)S(1)}, u32[]{:S(2)}, u32[]{:S(2)}) %collective-permute-start.21) | collective-permute-done | bytes 98336 | tf_op jit(solution)/shard_map/ppermute | solution.py:54
  52.9 0.6 collective-permute-done.20.refs_1_
  53.6 0.7 %shard_map.91.refs_2_ = f32[3,64,1024]{2,1,0:T(8,128)S(1)} custom-call(f32[4,96,256]{2,1,0:T(8,128)S(1)} %shard_map.90.refs_0_.refs_1_, bf16[8,2048,256]{2,1,0:T(8,128)(2,1)S(1)} %get-tuple-element.31.refs_1_.refs_3_.refs_2_), custom_call_target="tpu_custom_call" | custom-call | flops 536870912 | tf_op jit(solution)/shard_map/pallas_call | solution.py:71
  54.3 1.0 %collective-permute-done.23.refs_0_ = f32[4,96,256]{2,1,0:T(8,128)S(1)} collective-permute-done((f32[4,96,256]{2,1,0:T(8,128)S(1)}, f32[4,96,256]{2,1,0:T(8,128)S(1)}, u32[]{:S(2)}, u32[]{:S(2)}) %collective-permute-start.23) | collective-permute-done | bytes 393248 | tf_op jit(solution)/shard_map/ppermute | solution.py:54
  55.3 0.8 %shard_map.92 = (f32[88,256]{1,0:T(8,128)S(1)}, f32[88,256]{1,0:T(8,128)S(1)}, f32[88,256]{1,0:T(8,128)S(1)}, f32[88,256]{1,0:T(8,128)S(1)}) custom-call(f32[4,96,256]{2,1,0:T(8,128)S(1)} %collective-permute-done.23.refs_0_, f32[4,96,256]{2,1,0:T(8,128)S(1)} %shard_map.90.refs_0_.refs_1_, f32[3,64,1024]{2,1,0:T(8,128)S(1)} %shard_map.91.refs_2_, ...), custom_call_target="tpu_custom_call" | custom-call | flops 536870912 | tf_op jit(solution)/shard_map/pallas_call | solution.py:71
  56.1 0.7 %collective-permute-start.24 = (f32[88,256]{1,0:T(8,128)S(1)}, f32[88,256]{1,0:T(8,128)S(1)}, u32[]{:S(2)}, u32[]{:S(2)}) collective-permute-start(f32[88,256]{1,0:T(8,128)S(1)} %get-tuple-element.53), channel_id=1, source_target_pairs={{0,3},{1,2},{2,1},{3,0},{4,7},{5,6},{6,5},{7,4},{8,11},{9,10},{10,... | collective-permute-start | bytes 270344 | tf_op jit(solution)/shard_map/ppermute | solution.py:60
  56.8 0.8 %collective-permute-start.25 = (f32[88,256]{1,0:T(8,128)S(1)}, f32[88,256]{1,0:T(8,128)S(1)}, u32[]{:S(2)}, u32[]{:S(2)}) collective-permute-start(f32[88,256]{1,0:T(8,128)S(1)} %get-tuple-element.54), channel_id=1, source_target_pairs={{0,2},{1,3},{2,0},{3,1},{4,6},{5,7},{6,4},{7,5},{8,10},{9,11},{10,... | collective-permute-start | bytes 270344 | tf_op jit(solution)/shard_map/ppermute | solution.py:60
  57.6 2.9 %collective-permute-start.26 = (f32[88,256]{1,0:T(8,128)S(1)}, f32[88,256]{1,0:T(8,128)S(1)}, u32[]{:S(2)}, u32[]{:S(2)}) collective-permute-start(f32[88,256]{1,0:T(8,128)S(1)} %get-tuple-element.55), channel_id=1, source_target_pairs={{0,1},{1,0},{2,3},{3,2},{4,5},{5,4},{6,7},{7,6},{8,9},{9,8},{10,11... | collective-permute-start | bytes 270344 | tf_op jit(solution)/shard_map/ppermute | solution.py:60
  60.6 3.0 %collective-permute-done.24 = f32[88,256]{1,0:T(8,128)S(1)} collective-permute-done((f32[88,256]{1,0:T(8,128)S(1)}, f32[88,256]{1,0:T(8,128)S(1)}, u32[]{:S(2)}, u32[]{:S(2)}) %collective-permute-start.24) | collective-permute-done | bytes 90144 | tf_op jit(solution)/shard_map/ppermute | solution.py:60
  63.5 2.5 %collective-permute-done.25 = f32[88,256]{1,0:T(8,128)S(1)} collective-permute-done((f32[88,256]{1,0:T(8,128)S(1)}, f32[88,256]{1,0:T(8,128)S(1)}, u32[]{:S(2)}, u32[]{:S(2)}) %collective-permute-start.25) | collective-permute-done | bytes 90144 | tf_op jit(solution)/shard_map/ppermute | solution.py:60
  66.2 0.7 fusion
  66.8 0.5 collective-permute-done.27.refs_1_
  67.3 1.4 %shard_map.93 = f32[3,64,64]{2,1,0:T(8,128)} custom-call(f32[24,256]{1,0:T(8,128)S(1)} %slice_add_fusion.3.refs_0_, f32[24,256]{1,0:T(8,128)S(1)} %collective-permute-done.27.refs_1_), custom_call_target="tpu_custom_call" | custom-call | tf_op jit(solution)/shard_map/pallas_call | solution.py:71
  (27 shorter events, 0.7 us)
Async XLA Ops:
  0.6 11.1 %collective-permute-start.3 = (f32[64,256]{1,0:T(8,128)}, f32[64,256]{1,0:T(8,128)S(1)}, u32[]{:S(2)}, u32[]{:S(2)}) collective-permute-start(f32[64,256]{1,0:T(8,128)} %refs_4_.1), channel_id=1, source_target_pairs={{2,0},{3,1},{0,2},{1,3},{6,4},{7,5},{4,6},{5,7},{10,8},{11,9},{8,1... | collective-permute-start | bytes 196616 | tf_op jit(solution)/shard_map/ppermute | solution.py:54
  4.7 7.0 %collective-permute-start = (f32[64,256]{1,0:T(8,128)}, f32[64,256]{1,0:T(8,128)S(1)}, u32[]{:S(2)}, u32[]{:S(2)}) collective-permute-start(f32[64,256]{1,0:T(8,128)} %refs_5_.1), channel_id=1, source_target_pairs={{8,0},{12,4},{0,8},{4,12},{24,16},{28,20},{16,24},{20,28},{9,1},{1... | collective-permute-start | bytes 196616 | tf_op jit(solution)/shard_map/ppermute | solution.py:54
  6.2 5.5 %collective-permute-start.2 = (f32[64,256]{1,0:T(8,128)}, f32[64,256]{1,0:T(8,128)S(1)}, u32[]{:S(2)}, u32[]{:S(2)}) collective-permute-start(f32[64,256]{1,0:T(8,128)} %refs_5_.1), channel_id=1, source_target_pairs={{24,0},{28,4},{16,8},{20,12},{8,16},{12,20},{0,24},{4,28},{25,1},{... | collective-permute-start | bytes 196616 | tf_op jit(solution)/shard_map/ppermute | solution.py:54
  7.7 4.6 %collective-permute-start.1 = (f32[64,256]{1,0:T(8,128)}, f32[64,256]{1,0:T(8,128)S(1)}, u32[]{:S(2)}, u32[]{:S(2)}) collective-permute-start(f32[64,256]{1,0:T(8,128)} %refs_5_.1), channel_id=1, source_target_pairs={{16,0},{20,4},{24,8},{28,12},{0,16},{4,20},{8,24},{12,28},{17,1},{... | collective-permute-start | bytes 196616 | tf_op jit(solution)/shard_map/ppermute | solution.py:54
  12.3 1.6 %collective-permute-start.4 = (f32[4,64,256]{2,1,0:T(8,128)S(1)}, f32[4,64,256]{2,1,0:T(8,128)S(1)}, u32[]{:S(2)}, u32[]{:S(2)}) collective-permute-start(f32[4,64,256]{2,1,0:T(8,128)S(1)} %shard_map.78.refs_0_.refs_1_), channel_id=1, source_target_pairs={{4,0},{0,4},{12,8},{8,12},{20,16},{16,20},{28,24},{24,28},{5,1},{1... | collective-permute-start | bytes 786440 | tf_op jit(solution)/shard_map/ppermute | solution.py:54
  14.7 6.9 %collective-permute-start.8 = (f32[2,64,256]{2,1,0:T(8,128)S(1)}, f32[2,64,256]{2,1,0:T(8,128)S(1)}, u32[]{:S(2)}, u32[]{:S(2)}) collective-permute-start(f32[2,64,256]{2,1,0:T(8,128)S(1)} %shard_map.81.refs_0_), channel_id=1, source_target_pairs={{1,0},{0,1},{3,2},{2,3},{5,4},{4,5},{7,6},{6,7},{9,8},{8,9},{11,10... | collective-permute-start | bytes 393224 | tf_op jit(solution)/shard_map/ppermute | solution.py:54
  16.4 8.1 %collective-permute-start.5 = (f32[64,256]{1,0:T(8,128)S(1)}, f32[64,256]{1,0:T(8,128)S(1)}, u32[]{:S(2)}, u32[]{:S(2)}) collective-permute-start(f32[64,256]{1,0:T(8,128)S(1)} %get-tuple-element.33.refs_6_), channel_id=1, source_target_pairs={{0,3},{1,2},{2,1},{3,0},{4,7},{5,6},{6,5},{7,4},{8,11},{9,10},{10,... | collective-permute-start | bytes 196616 | tf_op jit(solution)/shard_map/ppermute | solution.py:60
  16.6 8.0 %collective-permute-start.6 = (f32[64,256]{1,0:T(8,128)S(1)}, f32[64,256]{1,0:T(8,128)S(1)}, u32[]{:S(2)}, u32[]{:S(2)}) collective-permute-start(f32[64,256]{1,0:T(8,128)S(1)} %get-tuple-element.34.refs_5_), channel_id=1, source_target_pairs={{0,2},{1,3},{2,0},{3,1},{4,6},{5,7},{6,4},{7,5},{8,10},{9,11},{10,... | collective-permute-start | bytes 196616 | tf_op jit(solution)/shard_map/ppermute | solution.py:60
  18.3 6.4 %collective-permute-start.7 = (f32[64,256]{1,0:T(8,128)S(1)}, f32[64,256]{1,0:T(8,128)S(1)}, u32[]{:S(2)}, u32[]{:S(2)}) collective-permute-start(f32[64,256]{1,0:T(8,128)S(1)} %get-tuple-element.35.refs_4_), channel_id=1, source_target_pairs={{0,1},{1,0},{2,3},{3,2},{4,5},{5,4},{6,7},{7,6},{8,9},{9,8},{10,11... | collective-permute-start | bytes 196616 | tf_op jit(solution)/shard_map/ppermute | solution.py:60
  24.4 8.5 %collective-permute-start.13 = (f32[4,68,256]{2,1,0:T(8,128)S(1)}, f32[4,68,256]{2,1,0:T(8,128)S(1)}, u32[]{:S(2)}, u32[]{:S(2)}) collective-permute-start(f32[4,68,256]{2,1,0:T(8,128)S(1)} %get-tuple-element.37.refs_4_), channel_id=1, source_target_pairs={{4,0},{0,4},{12,8},{8,12},{20,16},{16,20},{28,24},{24,28},{5,1},{1... | collective-permute-start | bytes 835592 | tf_op jit(solution)/shard_map/ppermute | solution.py:54
  24.7 6.5 %collective-permute-start.11 = (f32[64,256]{1,0:T(8,128)S(1)}, f32[64,256]{1,0:T(8,128)S(1)}, u32[]{:S(2)}, u32[]{:S(2)}) collective-permute-start(f32[64,256]{1,0:T(8,128)S(1)} %shard_map.83.refs_0_.refs_4_), channel_id=1, source_target_pairs={{24,0},{28,4},{16,8},{20,12},{8,16},{12,20},{0,24},{4,28},{25,1},{... | collective-permute-start | bytes 196616 | tf_op jit(solution)/shard_map/ppermute | solution.py:54
  28.5 4.3 %collective-permute-start.10 = (f32[64,256]{1,0:T(8,128)S(1)}, f32[64,256]{1,0:T(8,128)S(1)}, u32[]{:S(2)}, u32[]{:S(2)}) collective-permute-start(f32[64,256]{1,0:T(8,128)S(1)} %shard_map.83.refs_0_.refs_4_), channel_id=1, source_target_pairs={{16,0},{20,4},{24,8},{28,12},{0,16},{4,20},{8,24},{12,28},{17,1},{... | collective-permute-start | bytes 196616 | tf_op jit(solution)/shard_map/ppermute | solution.py:54
  28.5 4.3 %collective-permute-start.9 = (f32[64,256]{1,0:T(8,128)S(1)}, f32[64,256]{1,0:T(8,128)S(1)}, u32[]{:S(2)}, u32[]{:S(2)}) collective-permute-start(f32[64,256]{1,0:T(8,128)S(1)} %shard_map.83.refs_0_.refs_4_), channel_id=1, source_target_pairs={{8,0},{12,4},{0,8},{4,12},{24,16},{28,20},{16,24},{20,28},{9,1},{1... | collective-permute-start | bytes 196616 | tf_op jit(solution)/shard_map/ppermute | solution.py:54
  32.8 2.6 %collective-permute-start.12 = (f32[4,64,256]{2,1,0:T(8,128)S(1)}, f32[4,64,256]{2,1,0:T(8,128)S(1)}, u32[]{:S(2)}, u32[]{:S(2)}) collective-permute-start(f32[4,64,256]{2,1,0:T(8,128)S(1)} %shard_map.84.refs_0_.refs_1_), channel_id=1, source_target_pairs={{4,0},{0,4},{12,8},{8,12},{20,16},{16,20},{28,24},{24,28},{5,1},{1... | collective-permute-start | bytes 786440 | tf_op jit(solution)/shard_map/ppermute | solution.py:54
  32.9 7.8 %collective-permute-start.17 = (f32[2,72,256]{2,1,0:T(8,128)S(1)}, f32[2,72,256]{2,1,0:T(8,128)S(1)}, u32[]{:S(2)}, u32[]{:S(2)}) collective-permute-start(f32[2,72,256]{2,1,0:T(8,128)S(1)} %get-tuple-element.45), channel_id=1, source_target_pairs={{8,0},{12,4},{0,8},{4,12},{24,16},{28,20},{16,24},{20,28},{9,1},{1... | collective-permute-start | bytes 442376 | tf_op jit(solution)/shard_map/ppermute | solution.py:54
  36.2 6.9 %collective-permute-start.14 = (f32[64,256]{1,0:T(8,128)S(1)}, f32[64,256]{1,0:T(8,128)S(1)}, u32[]{:S(2)}, u32[]{:S(2)}) collective-permute-start(f32[64,256]{1,0:T(8,128)S(1)} %get-tuple-element.39), channel_id=1, source_target_pairs={{0,3},{1,2},{2,1},{3,0},{4,7},{5,6},{6,5},{7,4},{8,11},{9,10},{10,... | collective-permute-start | bytes 196616 | tf_op jit(solution)/shard_map/ppermute | solution.py:60
  37.0 7.6 %collective-permute-start.15 = (f32[64,256]{1,0:T(8,128)S(1)}, f32[64,256]{1,0:T(8,128)S(1)}, u32[]{:S(2)}, u32[]{:S(2)}) collective-permute-start(f32[64,256]{1,0:T(8,128)S(1)} %get-tuple-element.40), channel_id=1, source_target_pairs={{0,2},{1,3},{2,0},{3,1},{4,6},{5,7},{6,4},{7,5},{8,10},{9,11},{10,... | collective-permute-start | bytes 196616 | tf_op jit(solution)/shard_map/ppermute | solution.py:60
  37.3 7.3 %collective-permute-start.16 = (f32[64,256]{1,0:T(8,128)S(1)}, f32[64,256]{1,0:T(8,128)S(1)}, u32[]{:S(2)}, u32[]{:S(2)}) collective-permute-start(f32[64,256]{1,0:T(8,128)S(1)} %get-tuple-element.41), channel_id=1, source_target_pairs={{0,1},{1,0},{2,3},{3,2},{4,5},{5,4},{6,7},{7,6},{8,9},{9,8},{10,11... | collective-permute-start | bytes 196616 | tf_op jit(solution)/shard_map/ppermute | solution.py:60
  40.7 4.8 %collective-permute-start.18 = (f32[1,64,256]{2,1,0:T(8,128)S(1)}, f32[1,64,256]{2,1,0:T(8,128)S(1)}, u32[]{:S(2)}, u32[]{:S(2)}) collective-permute-start(f32[1,64,256]{2,1,0:T(8,128)S(1)} %get-tuple-element.48), channel_id=1, source_target_pairs={{16,0},{20,4},{24,8},{28,12},{0,16},{4,20},{8,24},{12,28},{17,1},{... | collective-permute-start | bytes 196616 | tf_op jit(solution)/shard_map/ppermute | solution.py:54
  41.7 3.7 %collective-permute-start.19 = (f32[16,256]{1,0:T(8,128)S(1)}, f32[16,256]{1,0:T(8,128)S(1)}, u32[]{:S(2)}, u32[]{:S(2)}) collective-permute-start(f32[16,256]{1,0:T(8,128)S(1)} %get-tuple-element.49.refs_7_), channel_id=1, source_target_pairs={{16,0},{20,4},{24,8},{28,12},{0,16},{4,20},{8,24},{12,28},{17,1},{... | collective-permute-start | bytes 49160 | tf_op jit(solution)/shard_map/ppermute | solution.py:54
  45.9 6.1 %collective-permute-start.22 = (f32[96,256]{1,0:T(8,128)S(1)}, f32[96,256]{1,0:T(8,128)S(1)}, u32[]{:S(2)}, u32[]{:S(2)}) collective-permute-start(f32[96,256]{1,0:T(8,128)S(1)} %get-tuple-element.50.refs_0_), channel_id=1, source_target_pairs={{24,0},{28,4},{16,8},{20,12},{8,16},{12,20},{0,24},{4,28},{25,1},{... | collective-permute-start | bytes 294920 | tf_op jit(solution)/shard_map/ppermute | solution.py:54
  47.5 5.3 %collective-permute-start.21 = (f32[96,256]{1,0:T(8,128)S(1)}, f32[96,256]{1,0:T(8,128)S(1)}, u32[]{:S(2)}, u32[]{:S(2)}) collective-permute-start(f32[96,256]{1,0:T(8,128)S(1)} %get-tuple-element.50.refs_0_), channel_id=1, source_target_pairs={{16,0},{20,4},{24,8},{28,12},{0,16},{4,20},{8,24},{12,28},{17,1},{... | collective-permute-start | bytes 294920 | tf_op jit(solution)/shard_map/ppermute | solution.py:54
  48.9 4.6 %collective-permute-start.20 = (f32[96,256]{1,0:T(8,128)S(1)}, f32[96,256]{1,0:T(8,128)S(1)}, u32[]{:S(2)}, u32[]{:S(2)}) collective-permute-start(f32[96,256]{1,0:T(8,128)S(1)} %get-tuple-element.50.refs_0_), channel_id=1, source_target_pairs={{8,0},{12,4},{0,8},{4,12},{24,16},{28,20},{16,24},{20,28},{9,1},{1... | collective-permute-start | bytes 294920 | tf_op jit(solution)/shard_map/ppermute | solution.py:54
  53.5 1.8 %collective-permute-start.23 = (f32[4,96,256]{2,1,0:T(8,128)S(1)}, f32[4,96,256]{2,1,0:T(8,128)S(1)}, u32[]{:S(2)}, u32[]{:S(2)}) collective-permute-start(f32[4,96,256]{2,1,0:T(8,128)S(1)} %shard_map.90.refs_0_.refs_1_), channel_id=1, source_target_pairs={{4,0},{0,4},{12,8},{8,12},{20,16},{16,20},{28,24},{24,28},{5,1},{1... | collective-permute-start | bytes 1179656 | tf_op jit(solution)/shard_map/ppermute | solution.py:54
  56.1 7.4 %collective-permute-start.24 = (f32[88,256]{1,0:T(8,128)S(1)}, f32[88,256]{1,0:T(8,128)S(1)}, u32[]{:S(2)}, u32[]{:S(2)}) collective-permute-start(f32[88,256]{1,0:T(8,128)S(1)} %get-tuple-element.53), channel_id=1, source_target_pairs={{0,3},{1,2},{2,1},{3,0},{4,7},{5,6},{6,5},{7,4},{8,11},{9,10},{10,... | collective-permute-start | bytes 270344 | tf_op jit(solution)/shard_map/ppermute | solution.py:60
  56.8 9.2 %collective-permute-start.25 = (f32[88,256]{1,0:T(8,128)S(1)}, f32[88,256]{1,0:T(8,128)S(1)}, u32[]{:S(2)}, u32[]{:S(2)}) collective-permute-start(f32[88,256]{1,0:T(8,128)S(1)} %get-tuple-element.54), channel_id=1, source_target_pairs={{0,2},{1,3},{2,0},{3,1},{4,6},{5,7},{6,4},{7,5},{8,10},{9,11},{10,... | collective-permute-start | bytes 270344 | tf_op jit(solution)/shard_map/ppermute | solution.py:60
  57.6 8.4 %collective-permute-start.26 = (f32[88,256]{1,0:T(8,128)S(1)}, f32[88,256]{1,0:T(8,128)S(1)}, u32[]{:S(2)}, u32[]{:S(2)}) collective-permute-start(f32[88,256]{1,0:T(8,128)S(1)} %get-tuple-element.55), channel_id=1, source_target_pairs={{0,1},{1,0},{2,3},{3,2},{4,5},{5,4},{6,7},{7,6},{8,9},{9,8},{10,11... | collective-permute-start | bytes 270344 | tf_op jit(solution)/shard_map/ppermute | solution.py:60
  66.1 1.3 %collective-permute-start.27 = (f32[24,256]{1,0:T(8,128)S(1)}, f32[24,256]{1,0:T(8,128)S(1)}, u32[]{:S(2)}, u32[]{:S(2)}) collective-permute-start(f32[24,256]{1,0:T(8,128)S(1)} %slice_add_fusion.3.refs_0_), channel_id=1, source_target_pairs={{4,0},{0,4},{12,8},{8,12},{20,16},{16,20},{28,24},{24,28},{5,1},{1... | collective-permute-start | bytes 73736 | tf_op jit(solution)/shard_map/ppermute | solution.py:54

commit v19 on v16

--- a/solution.py
+++ b/solution.py
@@ -12,6 +12,7 @@
 MODULUS = 65521.0
 HALF_MODULUS = 32760.0
 BASE = 256.0
+ROUND_TO_BASE = 1.5 * 2.0**31
 EXACT_DEPTH = 1024
 DENSE_CELLS = 4
 VMEM_LIMIT = 16 * 1024 * 1024
@@ -173,17 +174,22 @@
         copy.start()
     lax.fori_loop(half, dense_ref.shape[0], clear, 0)
 
-    def place(slot):
+    def cell(slot):
         row, col = rows_ref[0, 0, slot], cols_ref[0, 0, slot]
         row_shift = shift_of(me_col, row // piece_blocks, n_col)
         col_shift = shift_of(me_row, col // piece_blocks, n_row)
         col_place = col_shift % 2 * (n_row // 2) + col_shift // 2
         block = row_shift * piece_blocks + row % piece_blocks
         start = (col_place * piece_blocks + col % piece_blocks) * tile_len
-        values = jnp.where(slot < count_ref[0, 0], tiles[slot], 0.0)
+        return block, pl.ds(pl.multiple_of(start, tile_len), tile_len)
+
+    def place(slot):
+        values = tiles[slot]
         values = jnp.where(values > HALF_MODULUS, values - MODULUS, values).T
-        both = jnp.concatenate(balanced_digits(values), 1).astype(jnp.bfloat16)
-        dense_ref[block, pl.ds(pl.multiple_of(start, tile_len), tile_len), :] = both
+        rounded = (values + ROUND_TO_BASE) - ROUND_TO_BASE
+        both = jnp.concatenate([rounded * (1.0 / BASE), values - rounded], 1)
+        block, columns = cell(slot)
+        dense_ref[block, columns, :] = both.astype(jnp.bfloat16)
 
     def step(index, carry):
         chunk(index).wait()
@@ -192,6 +198,13 @@
         return carry
 
     lax.fori_loop(0, used_count, step, 0)
+
+    def erase(slot, carry):
+        block, columns = cell(slot)
+        dense_ref[block, columns, :] = jnp.zeros((tile_len, 2 * tile_len), dense_ref.dtype)
+        return carry
+
+    lax.fori_loop(count_ref[0, 0], used_count * group, erase, 0)
     for copy in small[3:]:
         copy.wait()
     token_ref[...] = jnp.zeros_like(token_ref)

time: 67 us -> 66.9 us (level)
  waiting for transfers between devices: 20.6 us -> 19.5 us
  Pallas kernels: 11.1 us -> 12.2 us
    ppermute x19, waiting for transfers between devices: 13.3 us -> 12.2 us  [fetch(): lax.ppermute(piece, axis, [(partner(i, shift, size), i) for i in range(si...]
    pallas_call x1, Pallas kernels: 1.76 us -> 2.81 us  [build_dense(): pl.pallas_call(functools.partial(build_kernel, (*sizes, group)), in_specs...]
  transfers between devices with their start and end apart: 28 -> 28, of which waited for: 13 -> 12; matrix products, arithmetic and copies ran while one was open for 1% -> 1% of each run, Pallas kernels for 13% -> 14%
where the time goes in v19:
time: 66.9 us; the launch traced here: 66.8 us
  starting transfers between devices  32.9 us (49%)
  waiting for transfers between devices  19.5 us (29%)
  Pallas kernels  12.2 us (18%)
  between operations  1.51 us (2%)
  other arithmetic  0.68 us (1%)
    ppermute x19, starting transfers between devices, fetch(): lax.ppermute(piece, axis, [(partner(i, shift, size), i) for i in range(si...  19.5 us
    ppermute x9, starting transfers between devices, scatter_pieces(): lax.ppermute(pieces[shift], axis, [(i, partner(i, shift, size)) for i in...  13.4 us
    ppermute x19, waiting for transfers between devices, fetch(): lax.ppermute(piece, axis, [(partner(i, shift, size), i) for i in range(si...  12.2 us
    pallas_call x16, Pallas kernels, call(): pl.pallas_call(body, in_specs=[vmem] * len(operands) + [pl.BlockSpec(memo...  9.37 us
    ppermute x9, waiting for transfers between devices, scatter_pieces(): lax.ppermute(pieces[shift], axis, [(i, partner(i, shift, size)) for i in...  7.34 us
    pallas_call x1, Pallas kernels, build_dense(): pl.pallas_call(functools.partial(build_kernel, (*sizes, group)), in_specs...  2.81 us
  transfers between devices with their start and end apart: 28, of which 12 were waited for; matrix products, arithmetic and copies ran while one was open for 1% of the time, Pallas kernels for 14%

profile of v19, /device:TPU:0, one launch (start us, length us, event | category | flops | bytes accessed | tf_op | source)
XLA Modules:
  0.0 66.8 jit_solution(4931536766214866378)
XLA Ops:
  0.6 4.1 %collective-permute-start.3 = (f32[64,256]{1,0:T(8,128)}, f32[64,256]{1,0:T(8,128)S(1)}, u32[]{:S(2)}, u32[]{:S(2)}) collective-permute-start(f32[64,256]{1,0:T(8,128)} %refs_4_.1), channel_id=1, source_target_pairs={{2,0},{3,1},{0,2},{1,3},{6,4},{7,5},{4,6},{5,7},{10,8},{11,9},{8,1... | collective-permute-start | bytes 196616 | tf_op jit(solution)/shard_map/ppermute | solution.py:55
  4.7 1.5 %collective-permute-start = (f32[64,256]{1,0:T(8,128)}, f32[64,256]{1,0:T(8,128)S(1)}, u32[]{:S(2)}, u32[]{:S(2)}) collective-permute-start(f32[64,256]{1,0:T(8,128)} %refs_5_.1), channel_id=1, source_target_pairs={{8,0},{12,4},{0,8},{4,12},{24,16},{28,20},{16,24},{20,28},{9,1},{1... | collective-permute-start | bytes 196616 | tf_op jit(solution)/shard_map/ppermute | solution.py:55
  6.2 1.5 %collective-permute-start.2 = (f32[64,256]{1,0:T(8,128)}, f32[64,256]{1,0:T(8,128)S(1)}, u32[]{:S(2)}, u32[]{:S(2)}) collective-permute-start(f32[64,256]{1,0:T(8,128)} %refs_5_.1), channel_id=1, source_target_pairs={{24,0},{28,4},{16,8},{20,12},{8,16},{12,20},{0,24},{4,28},{25,1},{... | collective-permute-start | bytes 196616 | tf_op jit(solution)/shard_map/ppermute | solution.py:55
  7.7 0.5 collective-permute-start.1
  8.9 2.8 %shard_map.77 = (bf16[8,2048,256]{2,1,0:T(8,128)(2,1)S(1)}, f32[64,256]{1,0:T(8,128)S(1)}, f32[64,256]{1,0:T(8,128)S(1)}, f32[8,128]{1,0:T(8,128)S(1)}) custom-call(s32[1,1,64]{2,1,0:T(1,128)} %refs_0_.1, s32[1,1,64]{2,1,0:T(1,128)} %refs_1_.1, s32[1,1]{1,0:T(1,128)S(6)} %copy.8.refs_2_, f32[1,1,64,128,128]{4,3,2,1,0:T(8,128)} %refs_3_.1, ...), custom_call_target="tpu_custom_call" | custom-call | flops 8388608 | bytes 8388608 | tf_op jit(solution)/shard_map/pallas_call | solution.py:224
  11.7 0.6 collective-permute-done.1.refs_2_
  12.3 0.1 collective-permute-start.4
  12.4 1.6 %collective-permute-start.8 = (f32[2,64,256]{2,1,0:T(8,128)S(1)}, f32[2,64,256]{2,1,0:T(8,128)S(1)}, u32[]{:S(2)}, u32[]{:S(2)}) collective-permute-start(f32[2,64,256]{2,1,0:T(8,128)S(1)} %shard_map.80.refs_4_.refs_0_), channel_id=1, source_target_pairs={{1,0},{0,1},{3,2},{2,3},{5,4},{4,5},{7,6},{6,7},{9,8},{8,9},{11,10... | collective-permute-start | bytes 393224 | tf_op jit(solution)/shard_map/ppermute | solution.py:55
  14.1 0.7 %shard_map.79.refs_2_ = f32[3,64,1024]{2,1,0:T(8,128)S(1)} custom-call(f32[4,64,256]{2,1,0:T(8,128)S(1)} %shard_map.78.refs_0_.refs_1_, bf16[8,2048,256]{2,1,0:T(8,128)(2,1)S(1)} %get-tuple-element.31.refs_1_.refs_3_.refs_2_), custom_call_target="tpu_custom_call" | custom-call | flops 536870912 | tf_op jit(solution)/shard_map/pallas_call | solution.py:72
  14.8 0.8 %shard_map.81 = (f32[64,256]{1,0:T(8,128)S(1)}, f32[64,256]{1,0:T(8,128)S(1)}, f32[64,256]{1,0:T(8,128)S(1)}, f32[64,256]{1,0:T(8,128)S(1)}) custom-call(f32[4,64,256]{2,1,0:T(8,128)S(1)} %collective-permute-done.4.refs_0_, f32[4,64,256]{2,1,0:T(8,128)S(1)} %shard_map.78.refs_0_.refs_1_, f32[3,64,1024]{2,1,0:T(8,128)S(1)} %shard_map.79.refs_2_, ...), custom_call_target="tpu_custom_call" | custom-call | flops 536870912 | tf_op jit(solution)/shard_map/pallas_call | solution.py:72
  15.6 0.5 collective-permute-start.5
  16.1 1.7 %collective-permute-start.6 = (f32[64,256]{1,0:T(8,128)S(1)}, f32[64,256]{1,0:T(8,128)S(1)}, u32[]{:S(2)}, u32[]{:S(2)}) collective-permute-start(f32[64,256]{1,0:T(8,128)S(1)} %get-tuple-element.35.refs_5_), channel_id=1, source_target_pairs={{0,2},{1,3},{2,0},{3,1},{4,6},{5,7},{6,4},{7,5},{8,10},{9,11},{10,... | collective-permute-start | bytes 196616 | tf_op jit(solution)/shard_map/ppermute | solution.py:61
  17.8 2.3 %collective-permute-start.7 = (f32[64,256]{1,0:T(8,128)S(1)}, f32[64,256]{1,0:T(8,128)S(1)}, u32[]{:S(2)}, u32[]{:S(2)}) collective-permute-start(f32[64,256]{1,0:T(8,128)S(1)} %get-tuple-element.36.refs_4_), channel_id=1, source_target_pairs={{0,1},{1,0},{2,3},{3,2},{4,5},{5,4},{6,7},{7,6},{8,9},{9,8},{10,11... | collective-permute-start | bytes 196616 | tf_op jit(solution)/shard_map/ppermute | solution.py:61
  20.1 2.7 %shard_map.82 = (f32[4,64,256]{2,1,0:T(8,128)S(1)}, f32[4,68,256]{2,1,0:T(8,128)S(1)}, f32[16,256]{1,0:T(8,128)S(1)}) custom-call(f32[2,64,256]{2,1,0:T(8,128)S(1)} %shard_map.80.refs_4_.refs_0_, f32[2,64,256]{2,1,0:T(8,128)S(1)} %collective-permute-done.8.refs_1_, bf16[8,2048,256]{2,1,0:T(8,128)(2,1)S(1)} %get-tuple-element.31.refs_1_.refs_3_.refs_2_, ...), custom_call_target="tpu_custom_call" | custom-call | flops 1073741824 | tf_op jit(solution)/shard_map/pallas_call | solution.py:72
  22.8 0.1 collective-permute-start.13
  22.9 1.4 %collective-permute-done.6.refs_2_ = f32[64,256]{1,0:T(8,128)S(1)} collective-permute-done((f32[64,256]{1,0:T(8,128)S(1)}, f32[64,256]{1,0:T(8,128)S(1)}, u32[]{:S(2)}, u32[]{:S(2)}) %collective-permute-start.6) | collective-permute-done | bytes 65568 | tf_op jit(solution)/shard_map/ppermute | solution.py:61
  24.3 1.6 %collective-permute-start.11 = (f32[64,256]{1,0:T(8,128)S(1)}, f32[64,256]{1,0:T(8,128)S(1)}, u32[]{:S(2)}, u32[]{:S(2)}) collective-permute-start(f32[64,256]{1,0:T(8,128)S(1)} %shard_map.83.refs_0_.refs_4_), channel_id=1, source_target_pairs={{24,0},{28,4},{16,8},{20,12},{8,16},{12,20},{0,24},{4,28},{25,1},{... | collective-permute-start | bytes 196616 | tf_op jit(solution)/shard_map/ppermute | solution.py:55
  25.9 1.4 %collective-permute-start.10 = (f32[64,256]{1,0:T(8,128)S(1)}, f32[64,256]{1,0:T(8,128)S(1)}, u32[]{:S(2)}, u32[]{:S(2)}) collective-permute-start(f32[64,256]{1,0:T(8,128)S(1)} %shard_map.83.refs_0_.refs_4_), channel_id=1, source_target_pairs={{16,0},{20,4},{24,8},{28,12},{0,16},{4,20},{8,24},{12,28},{17,1},{... | collective-permute-start | bytes 196616 | tf_op jit(solution)/shard_map/ppermute | solution.py:55
  27.2 0.6 collective-permute-start.9
  27.9 2.2 %collective-permute-done.11.refs_3_ = f32[64,256]{1,0:T(8,128)S(1)} collective-permute-done((f32[64,256]{1,0:T(8,128)S(1)}, f32[64,256]{1,0:T(8,128)S(1)}, u32[]{:S(2)}, u32[]{:S(2)}) %collective-permute-start.11) | collective-permute-done | bytes 65568 | tf_op jit(solution)/shard_map/ppermute | solution.py:55
  30.0 0.4 collective-permute-done.10.refs_2_
  30.4 1.0 %collective-permute-done.9.refs_1_ = f32[64,256]{1,0:T(8,128)S(1)} collective-permute-done((f32[64,256]{1,0:T(8,128)S(1)}, f32[64,256]{1,0:T(8,128)S(1)}, u32[]{:S(2)}, u32[]{:S(2)}) %collective-permute-start.9) | collective-permute-done | bytes 65568 | tf_op jit(solution)/shard_map/ppermute | solution.py:55
  31.5 0.1 collective-permute-start.12
  31.6 0.7 %collective-permute-start.17 = (f32[2,72,256]{2,1,0:T(8,128)S(1)}, f32[2,72,256]{2,1,0:T(8,128)S(1)}, u32[]{:S(2)}, u32[]{:S(2)}) collective-permute-start(f32[2,72,256]{2,1,0:T(8,128)S(1)} %get-tuple-element.45), channel_id=1, source_target_pairs={{8,0},{12,4},{0,8},{4,12},{24,16},{28,20},{16,24},{20,28},{9,1},{1... | collective-permute-start | bytes 442376 | tf_op jit(solution)/shard_map/ppermute | solution.py:55
  32.3 0.7 %shard_map.85.refs_2_ = f32[3,64,1024]{2,1,0:T(8,128)S(1)} custom-call(f32[4,64,256]{2,1,0:T(8,128)S(1)} %shard_map.84.refs_0_.refs_1_, bf16[8,2048,256]{2,1,0:T(8,128)(2,1)S(1)} %get-tuple-element.31.refs_1_.refs_3_.refs_2_), custom_call_target="tpu_custom_call" | custom-call | flops 536870912 | tf_op jit(solution)/shard_map/pallas_call | solution.py:72
  33.1 0.8 %shard_map.86 = (f32[64,256]{1,0:T(8,128)S(1)}, f32[64,256]{1,0:T(8,128)S(1)}, f32[64,256]{1,0:T(8,128)S(1)}, f32[64,256]{1,0:T(8,128)S(1)}) custom-call(f32[4,64,256]{2,1,0:T(8,128)S(1)} %collective-permute-done.12.refs_0_, f32[4,64,256]{2,1,0:T(8,128)S(1)} %shard_map.84.refs_0_.refs_1_, f32[3,64,1024]{2,1,0:T(8,128)S(1)} %shard_map.85.refs_2_, ...), custom_call_target="tpu_custom_call" | custom-call | flops 536870912 | tf_op jit(solution)/shard_map/pallas_call | solution.py:72
  33.9 1.8 %collective-permute-start.14 = (f32[64,256]{1,0:T(8,128)S(1)}, f32[64,256]{1,0:T(8,128)S(1)}, u32[]{:S(2)}, u32[]{:S(2)}) collective-permute-start(f32[64,256]{1,0:T(8,128)S(1)} %get-tuple-element.39), channel_id=1, source_target_pairs={{0,3},{1,2},{2,1},{3,0},{4,7},{5,6},{6,5},{7,4},{8,11},{9,10},{10,... | collective-permute-start | bytes 196616 | tf_op jit(solution)/shard_map/ppermute | solution.py:61
  35.7 2.7 %collective-permute-start.16 = (f32[64,256]{1,0:T(8,128)S(1)}, f32[64,256]{1,0:T(8,128)S(1)}, u32[]{:S(2)}, u32[]{:S(2)}) collective-permute-start(f32[64,256]{1,0:T(8,128)S(1)} %get-tuple-element.41), channel_id=1, source_target_pairs={{0,1},{1,0},{2,3},{3,2},{4,5},{5,4},{6,7},{7,6},{8,9},{9,8},{10,11... | collective-permute-start | bytes 196616 | tf_op jit(solution)/shard_map/ppermute | solution.py:61
  38.4 1.2 %collective-permute-start.18 = (f32[1,64,256]{2,1,0:T(8,128)S(1)}, f32[1,64,256]{2,1,0:T(8,128)S(1)}, u32[]{:S(2)}, u32[]{:S(2)}) collective-permute-start(f32[1,64,256]{2,1,0:T(8,128)S(1)} %get-tuple-element.48), channel_id=1, source_target_pairs={{16,0},{20,4},{24,8},{28,12},{0,16},{4,20},{8,24},{12,28},{17,1},{... | collective-permute-start | bytes 196616 | tf_op jit(solution)/shard_map/ppermute | solution.py:55
  39.6 0.9 %collective-permute-start.19 = (f32[16,256]{1,0:T(8,128)S(1)}, f32[16,256]{1,0:T(8,128)S(1)}, u32[]{:S(2)}, u32[]{:S(2)}) collective-permute-start(f32[16,256]{1,0:T(8,128)S(1)} %get-tuple-element.49.refs_7_), channel_id=1, source_target_pairs={{16,0},{20,4},{24,8},{28,12},{0,16},{4,20},{8,24},{12,28},{17,1},{... | collective-permute-start | bytes 49160 | tf_op jit(solution)/shard_map/ppermute | solution.py:55
  40.5 2.8 %collective-permute-done.19.refs_8_ = f32[16,256]{1,0:T(8,128)S(1)} collective-permute-done((f32[16,256]{1,0:T(8,128)S(1)}, f32[16,256]{1,0:T(8,128)S(1)}, u32[]{:S(2)}, u32[]{:S(2)}) %collective-permute-start.19) | collective-permute-done | bytes 16416 | tf_op jit(solution)/shard_map/ppermute | solution.py:55
  43.3 0.5 shard_map.89
  43.8 1.8 %collective-permute-start.22 = (f32[96,256]{1,0:T(8,128)S(1)}, f32[96,256]{1,0:T(8,128)S(1)}, u32[]{:S(2)}, u32[]{:S(2)}) collective-permute-start(f32[96,256]{1,0:T(8,128)S(1)} %get-tuple-element.50.refs_0_), channel_id=1, source_target_pairs={{24,0},{28,4},{16,8},{20,12},{8,16},{12,20},{0,24},{4,28},{25,1},{... | collective-permute-start | bytes 294920 | tf_op jit(solution)/shard_map/ppermute | solution.py:55
  45.6 0.7 %collective-permute-start.21 = (f32[96,256]{1,0:T(8,128)S(1)}, f32[96,256]{1,0:T(8,128)S(1)}, u32[]{:S(2)}, u32[]{:S(2)}) collective-permute-start(f32[96,256]{1,0:T(8,128)S(1)} %get-tuple-element.50.refs_0_), channel_id=1, source_target_pairs={{16,0},{20,4},{24,8},{28,12},{0,16},{4,20},{8,24},{12,28},{17,1},{... | collective-permute-start | bytes 294920 | tf_op jit(solution)/shard_map/ppermute | solution.py:55
  46.3 1.0 %collective-permute-start.20 = (f32[96,256]{1,0:T(8,128)S(1)}, f32[96,256]{1,0:T(8,128)S(1)}, u32[]{:S(2)}, u32[]{:S(2)}) collective-permute-start(f32[96,256]{1,0:T(8,128)S(1)} %get-tuple-element.50.refs_0_), channel_id=1, source_target_pairs={{8,0},{12,4},{0,8},{4,12},{24,16},{28,20},{16,24},{20,28},{9,1},{1... | collective-permute-start | bytes 294920 | tf_op jit(solution)/shard_map/ppermute | solution.py:55
  47.3 3.1 %collective-permute-done.22.refs_3_ = f32[96,256]{1,0:T(8,128)S(1)} collective-permute-done((f32[96,256]{1,0:T(8,128)S(1)}, f32[96,256]{1,0:T(8,128)S(1)}, u32[]{:S(2)}, u32[]{:S(2)}) %collective-permute-start.22) | collective-permute-done | bytes 98336 | tf_op jit(solution)/shard_map/ppermute | solution.py:55
  50.4 0.6 collective-permute-done.21.refs_2_
  51.1 0.8 %shard_map.91.refs_2_ = f32[3,64,1024]{2,1,0:T(8,128)S(1)} custom-call(f32[4,96,256]{2,1,0:T(8,128)S(1)} %shard_map.90.refs_0_.refs_1_, bf16[8,2048,256]{2,1,0:T(8,128)(2,1)S(1)} %get-tuple-element.31.refs_1_.refs_3_.refs_2_), custom_call_target="tpu_custom_call" | custom-call | flops 536870912 | tf_op jit(solution)/shard_map/pallas_call | solution.py:72
  51.9 1.0 %collective-permute-done.23.refs_0_ = f32[4,96,256]{2,1,0:T(8,128)S(1)} collective-permute-done((f32[4,96,256]{2,1,0:T(8,128)S(1)}, f32[4,96,256]{2,1,0:T(8,128)S(1)}, u32[]{:S(2)}, u32[]{:S(2)}) %collective-permute-start.23) | collective-permute-done | bytes 393248 | tf_op jit(solution)/shard_map/ppermute | solution.py:55
  52.9 0.8 %shard_map.92 = (f32[88,256]{1,0:T(8,128)S(1)}, f32[88,256]{1,0:T(8,128)S(1)}, f32[88,256]{1,0:T(8,128)S(1)}, f32[88,256]{1,0:T(8,128)S(1)}) custom-call(f32[4,96,256]{2,1,0:T(8,128)S(1)} %collective-permute-done.23.refs_0_, f32[4,96,256]{2,1,0:T(8,128)S(1)} %shard_map.90.refs_0_.refs_1_, f32[3,64,1024]{2,1,0:T(8,128)S(1)} %shard_map.91.refs_2_, ...), custom_call_target="tpu_custom_call" | custom-call | flops 536870912 | tf_op jit(solution)/shard_map/pallas_call | solution.py:72
  53.7 1.8 %collective-permute-start.24 = (f32[88,256]{1,0:T(8,128)S(1)}, f32[88,256]{1,0:T(8,128)S(1)}, u32[]{:S(2)}, u32[]{:S(2)}) collective-permute-start(f32[88,256]{1,0:T(8,128)S(1)} %get-tuple-element.53), channel_id=1, source_target_pairs={{0,3},{1,2},{2,1},{3,0},{4,7},{5,6},{6,5},{7,4},{8,11},{9,10},{10,... | collective-permute-start | bytes 270344 | tf_op jit(solution)/shard_map/ppermute | solution.py:61
  55.4 2.7 %collective-permute-start.26 = (f32[88,256]{1,0:T(8,128)S(1)}, f32[88,256]{1,0:T(8,128)S(1)}, u32[]{:S(2)}, u32[]{:S(2)}) collective-permute-start(f32[88,256]{1,0:T(8,128)S(1)} %get-tuple-element.55), channel_id=1, source_target_pairs={{0,1},{1,0},{2,3},{3,2},{4,5},{5,4},{6,7},{7,6},{8,9},{9,8},{10,11... | collective-permute-start | bytes 270344 | tf_op jit(solution)/shard_map/ppermute | solution.py:61
  58.1 3.0 %collective-permute-done.24 = f32[88,256]{1,0:T(8,128)S(1)} collective-permute-done((f32[88,256]{1,0:T(8,128)S(1)}, f32[88,256]{1,0:T(8,128)S(1)}, u32[]{:S(2)}, u32[]{:S(2)}) %collective-permute-start.24) | collective-permute-done | bytes 90144 | tf_op jit(solution)/shard_map/ppermute | solution.py:61
  61.1 3.0 %collective-permute-done.25 = f32[88,256]{1,0:T(8,128)S(1)} collective-permute-done((f32[88,256]{1,0:T(8,128)S(1)}, f32[88,256]{1,0:T(8,128)S(1)}, u32[]{:S(2)}, u32[]{:S(2)}) %collective-permute-start.25) | collective-permute-done | bytes 90144 | tf_op jit(solution)/shard_map/ppermute | solution.py:61
  64.1 0.1 collective-permute-start.27
  64.1 0.7 %fusion = f32[64,256]{1,0:T(8,128)} fusion(f32[88,256]{1,0:T(8,128)S(1)} %collective-permute-done.26, f32[88,256]{1,0:T(8,128)S(1)} %collective-permute-done.25, f32[88,256]{1,0:T(8,128)S(1)} %collective-permute-done.24, f32[88,256]{1,0:T(8,128)S(1)} %get-tuple-element.52), kind=kLoop, calls=%fused_computation.1 | loop fusion | flops 196608 | bytes 327680 | tf_op jit(solution)/shard_map/mul | solution.py:593
  64.8 0.5 collective-permute-done.27.refs_1_
  65.3 1.4 %shard_map.93 = f32[3,64,64]{2,1,0:T(8,128)} custom-call(f32[24,256]{1,0:T(8,128)S(1)} %slice_add_fusion.3.refs_0_, f32[24,256]{1,0:T(8,128)S(1)} %collective-permute-done.27.refs_1_), custom_call_target="tpu_custom_call" | custom-call | tf_op jit(solution)/shard_map/pallas_call | solution.py:72
  (27 shorter events, 0.3 us)
Async XLA Ops:
  0.6 11.1 %collective-permute-start.3 = (f32[64,256]{1,0:T(8,128)}, f32[64,256]{1,0:T(8,128)S(1)}, u32[]{:S(2)}, u32[]{:S(2)}) collective-permute-start(f32[64,256]{1,0:T(8,128)} %refs_4_.1), channel_id=1, source_target_pairs={{2,0},{3,1},{0,2},{1,3},{6,4},{7,5},{4,6},{5,7},{10,8},{11,9},{8,1... | collective-permute-start | bytes 196616 | tf_op jit(solution)/shard_map/ppermute | solution.py:55
  4.7 7.0 %collective-permute-start = (f32[64,256]{1,0:T(8,128)}, f32[64,256]{1,0:T(8,128)S(1)}, u32[]{:S(2)}, u32[]{:S(2)}) collective-permute-start(f32[64,256]{1,0:T(8,128)} %refs_5_.1), channel_id=1, source_target_pairs={{8,0},{12,4},{0,8},{4,12},{24,16},{28,20},{16,24},{20,28},{9,1},{1... | collective-permute-start | bytes 196616 | tf_op jit(solution)/shard_map/ppermute | solution.py:55
  6.2 5.5 %collective-permute-start.2 = (f32[64,256]{1,0:T(8,128)}, f32[64,256]{1,0:T(8,128)S(1)}, u32[]{:S(2)}, u32[]{:S(2)}) collective-permute-start(f32[64,256]{1,0:T(8,128)} %refs_5_.1), channel_id=1, source_target_pairs={{24,0},{28,4},{16,8},{20,12},{8,16},{12,20},{0,24},{4,28},{25,1},{... | collective-permute-start | bytes 196616 | tf_op jit(solution)/shard_map/ppermute | solution.py:55
  7.7 4.6 %collective-permute-start.1 = (f32[64,256]{1,0:T(8,128)}, f32[64,256]{1,0:T(8,128)S(1)}, u32[]{:S(2)}, u32[]{:S(2)}) collective-permute-start(f32[64,256]{1,0:T(8,128)} %refs_5_.1), channel_id=1, source_target_pairs={{16,0},{20,4},{24,8},{28,12},{0,16},{4,20},{8,24},{12,28},{17,1},{... | collective-permute-start | bytes 196616 | tf_op jit(solution)/shard_map/ppermute | solution.py:55
  12.3 2.5 %collective-permute-start.4 = (f32[4,64,256]{2,1,0:T(8,128)S(1)}, f32[4,64,256]{2,1,0:T(8,128)S(1)}, u32[]{:S(2)}, u32[]{:S(2)}) collective-permute-start(f32[4,64,256]{2,1,0:T(8,128)S(1)} %shard_map.78.refs_0_.refs_1_), channel_id=1, source_target_pairs={{4,0},{0,4},{12,8},{8,12},{20,16},{16,20},{28,24},{24,28},{5,1},{1... | collective-permute-start | bytes 786440 | tf_op jit(solution)/shard_map/ppermute | solution.py:55
  12.4 7.7 %collective-permute-start.8 = (f32[2,64,256]{2,1,0:T(8,128)S(1)}, f32[2,64,256]{2,1,0:T(8,128)S(1)}, u32[]{:S(2)}, u32[]{:S(2)}) collective-permute-start(f32[2,64,256]{2,1,0:T(8,128)S(1)} %shard_map.80.refs_4_.refs_0_), channel_id=1, source_target_pairs={{1,0},{0,1},{3,2},{2,3},{5,4},{4,5},{7,6},{6,7},{9,8},{8,9},{11,10... | collective-permute-start | bytes 393224 | tf_op jit(solution)/shard_map/ppermute | solution.py:55
  15.6 7.2 %collective-permute-start.5 = (f32[64,256]{1,0:T(8,128)S(1)}, f32[64,256]{1,0:T(8,128)S(1)}, u32[]{:S(2)}, u32[]{:S(2)}) collective-permute-start(f32[64,256]{1,0:T(8,128)S(1)} %get-tuple-element.34.refs_6_), channel_id=1, source_target_pairs={{0,3},{1,2},{2,1},{3,0},{4,7},{5,6},{6,5},{7,4},{8,11},{9,10},{10,... | collective-permute-start | bytes 196616 | tf_op jit(solution)/shard_map/ppermute | solution.py:61
  16.1 8.1 %collective-permute-start.6 = (f32[64,256]{1,0:T(8,128)S(1)}, f32[64,256]{1,0:T(8,128)S(1)}, u32[]{:S(2)}, u32[]{:S(2)}) collective-permute-start(f32[64,256]{1,0:T(8,128)S(1)} %get-tuple-element.35.refs_5_), channel_id=1, source_target_pairs={{0,2},{1,3},{2,0},{3,1},{4,6},{5,7},{6,4},{7,5},{8,10},{9,11},{10,... | collective-permute-start | bytes 196616 | tf_op jit(solution)/shard_map/ppermute | solution.py:61
  17.8 6.5 %collective-permute-start.7 = (f32[64,256]{1,0:T(8,128)S(1)}, f32[64,256]{1,0:T(8,128)S(1)}, u32[]{:S(2)}, u32[]{:S(2)}) collective-permute-start(f32[64,256]{1,0:T(8,128)S(1)} %get-tuple-element.36.refs_4_), channel_id=1, source_target_pairs={{0,1},{1,0},{2,3},{3,2},{4,5},{5,4},{6,7},{7,6},{8,9},{9,8},{10,11... | collective-permute-start | bytes 196616 | tf_op jit(solution)/shard_map/ppermute | solution.py:61
  22.8 8.8 %collective-permute-start.13 = (f32[4,68,256]{2,1,0:T(8,128)S(1)}, f32[4,68,256]{2,1,0:T(8,128)S(1)}, u32[]{:S(2)}, u32[]{:S(2)}) collective-permute-start(f32[4,68,256]{2,1,0:T(8,128)S(1)} %get-tuple-element.37.refs_4_), channel_id=1, source_target_pairs={{4,0},{0,4},{12,8},{8,12},{20,16},{16,20},{28,24},{24,28},{5,1},{1... | collective-permute-start | bytes 835592 | tf_op jit(solution)/shard_map/ppermute | solution.py:55
  24.3 5.7 %collective-permute-start.11 = (f32[64,256]{1,0:T(8,128)S(1)}, f32[64,256]{1,0:T(8,128)S(1)}, u32[]{:S(2)}, u32[]{:S(2)}) collective-permute-start(f32[64,256]{1,0:T(8,128)S(1)} %shard_map.83.refs_0_.refs_4_), channel_id=1, source_target_pairs={{24,0},{28,4},{16,8},{20,12},{8,16},{12,20},{0,24},{4,28},{25,1},{... | collective-permute-start | bytes 196616 | tf_op jit(solution)/shard_map/ppermute | solution.py:55
  25.9 4.6 %collective-permute-start.10 = (f32[64,256]{1,0:T(8,128)S(1)}, f32[64,256]{1,0:T(8,128)S(1)}, u32[]{:S(2)}, u32[]{:S(2)}) collective-permute-start(f32[64,256]{1,0:T(8,128)S(1)} %shard_map.83.refs_0_.refs_4_), channel_id=1, source_target_pairs={{16,0},{20,4},{24,8},{28,12},{0,16},{4,20},{8,24},{12,28},{17,1},{... | collective-permute-start | bytes 196616 | tf_op jit(solution)/shard_map/ppermute | solution.py:55
  27.2 4.3 %collective-permute-start.9 = (f32[64,256]{1,0:T(8,128)S(1)}, f32[64,256]{1,0:T(8,128)S(1)}, u32[]{:S(2)}, u32[]{:S(2)}) collective-permute-start(f32[64,256]{1,0:T(8,128)S(1)} %shard_map.83.refs_0_.refs_4_), channel_id=1, source_target_pairs={{8,0},{12,4},{0,8},{4,12},{24,16},{28,20},{16,24},{20,28},{9,1},{1... | collective-permute-start | bytes 196616 | tf_op jit(solution)/shard_map/ppermute | solution.py:55
  31.5 1.6 %collective-permute-start.12 = (f32[4,64,256]{2,1,0:T(8,128)S(1)}, f32[4,64,256]{2,1,0:T(8,128)S(1)}, u32[]{:S(2)}, u32[]{:S(2)}) collective-permute-start(f32[4,64,256]{2,1,0:T(8,128)S(1)} %shard_map.84.refs_0_.refs_1_), channel_id=1, source_target_pairs={{4,0},{0,4},{12,8},{8,12},{20,16},{16,20},{28,24},{24,28},{5,1},{1... | collective-permute-start | bytes 786440 | tf_op jit(solution)/shard_map/ppermute | solution.py:55
  31.6 6.7 %collective-permute-start.17 = (f32[2,72,256]{2,1,0:T(8,128)S(1)}, f32[2,72,256]{2,1,0:T(8,128)S(1)}, u32[]{:S(2)}, u32[]{:S(2)}) collective-permute-start(f32[2,72,256]{2,1,0:T(8,128)S(1)} %get-tuple-element.45), channel_id=1, source_target_pairs={{8,0},{12,4},{0,8},{4,12},{24,16},{28,20},{16,24},{20,28},{9,1},{1... | collective-permute-start | bytes 442376 | tf_op jit(solution)/shard_map/ppermute | solution.py:55
  33.9 9.4 %collective-permute-start.14 = (f32[64,256]{1,0:T(8,128)S(1)}, f32[64,256]{1,0:T(8,128)S(1)}, u32[]{:S(2)}, u32[]{:S(2)}) collective-permute-start(f32[64,256]{1,0:T(8,128)S(1)} %get-tuple-element.39), channel_id=1, source_target_pairs={{0,3},{1,2},{2,1},{3,0},{4,7},{5,6},{6,5},{7,4},{8,11},{9,10},{10,... | collective-permute-start | bytes 196616 | tf_op jit(solution)/shard_map/ppermute | solution.py:61
  35.7 7.6 %collective-permute-start.15 = (f32[64,256]{1,0:T(8,128)S(1)}, f32[64,256]{1,0:T(8,128)S(1)}, u32[]{:S(2)}, u32[]{:S(2)}) collective-permute-start(f32[64,256]{1,0:T(8,128)S(1)} %get-tuple-element.40), channel_id=1, source_target_pairs={{0,2},{1,3},{2,0},{3,1},{4,6},{5,7},{6,4},{7,5},{8,10},{9,11},{10,... | collective-permute-start | bytes 196616 | tf_op jit(solution)/shard_map/ppermute | solution.py:61
  35.7 7.6 %collective-permute-start.16 = (f32[64,256]{1,0:T(8,128)S(1)}, f32[64,256]{1,0:T(8,128)S(1)}, u32[]{:S(2)}, u32[]{:S(2)}) collective-permute-start(f32[64,256]{1,0:T(8,128)S(1)} %get-tuple-element.41), channel_id=1, source_target_pairs={{0,1},{1,0},{2,3},{3,2},{4,5},{5,4},{6,7},{7,6},{8,9},{9,8},{10,11... | collective-permute-start | bytes 196616 | tf_op jit(solution)/shard_map/ppermute | solution.py:61
  38.4 4.9 %collective-permute-start.18 = (f32[1,64,256]{2,1,0:T(8,128)S(1)}, f32[1,64,256]{2,1,0:T(8,128)S(1)}, u32[]{:S(2)}, u32[]{:S(2)}) collective-permute-start(f32[1,64,256]{2,1,0:T(8,128)S(1)} %get-tuple-element.48), channel_id=1, source_target_pairs={{16,0},{20,4},{24,8},{28,12},{0,16},{4,20},{8,24},{12,28},{17,1},{... | collective-permute-start | bytes 196616 | tf_op jit(solution)/shard_map/ppermute | solution.py:55
  39.6 3.7 %collective-permute-start.19 = (f32[16,256]{1,0:T(8,128)S(1)}, f32[16,256]{1,0:T(8,128)S(1)}, u32[]{:S(2)}, u32[]{:S(2)}) collective-permute-start(f32[16,256]{1,0:T(8,128)S(1)} %get-tuple-element.49.refs_7_), channel_id=1, source_target_pairs={{16,0},{20,4},{24,8},{28,12},{0,16},{4,20},{8,24},{12,28},{17,1},{... | collective-permute-start | bytes 49160 | tf_op jit(solution)/shard_map/ppermute | solution.py:55
  43.8 6.6 %collective-permute-start.22 = (f32[96,256]{1,0:T(8,128)S(1)}, f32[96,256]{1,0:T(8,128)S(1)}, u32[]{:S(2)}, u32[]{:S(2)}) collective-permute-start(f32[96,256]{1,0:T(8,128)S(1)} %get-tuple-element.50.refs_0_), channel_id=1, source_target_pairs={{24,0},{28,4},{16,8},{20,12},{8,16},{12,20},{0,24},{4,28},{25,1},{... | collective-permute-start | bytes 294920 | tf_op jit(solution)/shard_map/ppermute | solution.py:55
  45.6 5.4 %collective-permute-start.21 = (f32[96,256]{1,0:T(8,128)S(1)}, f32[96,256]{1,0:T(8,128)S(1)}, u32[]{:S(2)}, u32[]{:S(2)}) collective-permute-start(f32[96,256]{1,0:T(8,128)S(1)} %get-tuple-element.50.refs_0_), channel_id=1, source_target_pairs={{16,0},{20,4},{24,8},{28,12},{0,16},{4,20},{8,24},{12,28},{17,1},{... | collective-permute-start | bytes 294920 | tf_op jit(solution)/shard_map/ppermute | solution.py:55
  46.3 4.8 %collective-permute-start.20 = (f32[96,256]{1,0:T(8,128)S(1)}, f32[96,256]{1,0:T(8,128)S(1)}, u32[]{:S(2)}, u32[]{:S(2)}) collective-permute-start(f32[96,256]{1,0:T(8,128)S(1)} %get-tuple-element.50.refs_0_), channel_id=1, source_target_pairs={{8,0},{12,4},{0,8},{4,12},{24,16},{28,20},{16,24},{20,28},{9,1},{1... | collective-permute-start | bytes 294920 | tf_op jit(solution)/shard_map/ppermute | solution.py:55
  51.1 1.8 %collective-permute-start.23 = (f32[4,96,256]{2,1,0:T(8,128)S(1)}, f32[4,96,256]{2,1,0:T(8,128)S(1)}, u32[]{:S(2)}, u32[]{:S(2)}) collective-permute-start(f32[4,96,256]{2,1,0:T(8,128)S(1)} %shard_map.90.refs_0_.refs_1_), channel_id=1, source_target_pairs={{4,0},{0,4},{12,8},{8,12},{20,16},{16,20},{28,24},{24,28},{5,1},{1... | collective-permute-start | bytes 1179656 | tf_op jit(solution)/shard_map/ppermute | solution.py:55
  53.7 7.4 %collective-permute-start.24 = (f32[88,256]{1,0:T(8,128)S(1)}, f32[88,256]{1,0:T(8,128)S(1)}, u32[]{:S(2)}, u32[]{:S(2)}) collective-permute-start(f32[88,256]{1,0:T(8,128)S(1)} %get-tuple-element.53), channel_id=1, source_target_pairs={{0,3},{1,2},{2,1},{3,0},{4,7},{5,6},{6,5},{7,4},{8,11},{9,10},{10,... | collective-permute-start | bytes 270344 | tf_op jit(solution)/shard_map/ppermute | solution.py:61
  55.4 8.6 %collective-permute-start.25 = (f32[88,256]{1,0:T(8,128)S(1)}, f32[88,256]{1,0:T(8,128)S(1)}, u32[]{:S(2)}, u32[]{:S(2)}) collective-permute-start(f32[88,256]{1,0:T(8,128)S(1)} %get-tuple-element.54), channel_id=1, source_target_pairs={{0,2},{1,3},{2,0},{3,1},{4,6},{5,7},{6,4},{7,5},{8,10},{9,11},{10,... | collective-permute-start | bytes 270344 | tf_op jit(solution)/shard_map/ppermute | solution.py:61
  55.4 8.6 %collective-permute-start.26 = (f32[88,256]{1,0:T(8,128)S(1)}, f32[88,256]{1,0:T(8,128)S(1)}, u32[]{:S(2)}, u32[]{:S(2)}) collective-permute-start(f32[88,256]{1,0:T(8,128)S(1)} %get-tuple-element.55), channel_id=1, source_target_pairs={{0,1},{1,0},{2,3},{3,2},{4,5},{5,4},{6,7},{7,6},{8,9},{9,8},{10,11... | collective-permute-start | bytes 270344 | tf_op jit(solution)/shard_map/ppermute | solution.py:61
  64.1 1.3 %collective-permute-start.27 = (f32[24,256]{1,0:T(8,128)S(1)}, f32[24,256]{1,0:T(8,128)S(1)}, u32[]{:S(2)}, u32[]{:S(2)}) collective-permute-start(f32[24,256]{1,0:T(8,128)S(1)} %slice_add_fusion.3.refs_0_), channel_id=1, source_target_pairs={{4,0},{0,4},{12,8},{8,12},{20,16},{16,20},{28,24},{24,28},{5,1},{1... | collective-permute-start | bytes 73736 | tf_op jit(solution)/shard_map/ppermute | solution.py:55

commit v20 on v19

--- a/solution.py
+++ b/solution.py
@@ -302,6 +302,37 @@
         packed = half_of_core(jnp.concatenate([packed, *(tail[...] for tail in tails)], 0))
         for out in outs:
             out[span:, :] = packed
+
+
+def whole_kernel(span, odds_ref, evens_ref, dense_ref, *refs):
+    outs, even_digits, odd_digits = refs[:-2], refs[-2], refs[-1]
+    fill_digits(span, evens_ref, even_digits)
+    fill_digits(span, odds_ref, odd_digits)
+    tile_len = dense_ref.shape[2] // 2
+    piece_blocks = dense_ref.shape[0] // len(outs)
+    for e in reversed(range(len(outs))):
+        for sub in range(piece_blocks):
+            block = e * piece_blocks + sub
+            first = half_products(0, span, evens_ref, dense_ref, even_digits, block)
+            second = half_products(1, span, odds_ref, dense_ref, odd_digits, block)
+            parts = (left + right for left, right in zip(first, second))
+            outs[e][:, sub * tile_len : (sub + 1) * tile_len] = combine(*parts)
+
+
+def dense_whole(odds, evens, span, n_col, dense, before):
+    _, depth, _ = dense.shape
+    _, _, piece_len = odds.shape
+    return list(
+        call(
+            functools.partial(whole_kernel, span),
+            [odds, evens, dense],
+            [held(span, piece_len)] * n_col,
+            before,
+            scratch=[pltpu.VMEM((2 * span, depth // 2), jnp.bfloat16)] * 2,
+            limit=VMEM_LIMIT,
+            flops=4 * span * dense.size,
+        )
+    )
 
 
 def dense_first(evens, span, dense):
@@ -577,7 +608,11 @@
         w_kept, w_odds, term = sparse_left(x_pairs, outs, n_row, positions, a_digits)
     vector_1 = sum_after(scatter_pieces(outs, "col"), [w_odds])
     w_came = fetch(w_odds, "row", 1)
-    outs = multiply(gather_evens(vector_1, "row"), [w_came])
+    evens = gather_evens(vector_1, "row")
+    if is_dense:
+        outs = dense_whole(gather_odds(evens, "row"), evens, span, n_col, dense, [w_came])
+    else:
+        outs = multiply(evens)
     pieces = scatter_pieces(outs, "col")
     shift, before = 2, []
     while shift < n_row:

time: 66.9 us -> 67.5 us (level)
    pallas_call x16 -> x15, Pallas kernels: 9.37 us -> 9.23 us  [call(): pl.pallas_call(body, in_specs=[vmem] * len(operands) + [pl.BlockSpec(memo...]
  transfers between devices with their start and end apart: 28 -> 28, of which waited for: 12 -> 13; matrix products, arithmetic and copies ran while one was open for 1% -> 1% of each run, Pallas kernels for 14% -> 15%
where the time goes in v20:
time: 67.5 us; the launch traced here: 67.3 us
  starting transfers between devices  32.8 us (49%)
  waiting for transfers between devices  19.8 us (29%)
  Pallas kernels  12.5 us (19%)
  between operations  1.48 us (2%)
  other arithmetic  0.68 us (1%)
    ppermute x19, starting transfers between devices, fetch(): lax.ppermute(piece, axis, [(partner(i, shift, size), i) for i in range(si...  19.4 us
    ppermute x9, starting transfers between devices, scatter_pieces(): lax.ppermute(pieces[shift], axis, [(i, partner(i, shift, size)) for i in...  13.4 us
    ppermute x19, waiting for transfers between devices, fetch(): lax.ppermute(piece, axis, [(partner(i, shift, size), i) for i in range(si...  12.4 us
    pallas_call x15, Pallas kernels, call(): pl.pallas_call(body, in_specs=[vmem] * len(operands) + [pl.BlockSpec(memo...  9.23 us
    ppermute x9, waiting for transfers between devices, scatter_pieces(): lax.ppermute(pieces[shift], axis, [(i, partner(i, shift, size)) for i in...  7.42 us
    pallas_call x1, Pallas kernels, build_dense(): pl.pallas_call(functools.partial(build_kernel, (*sizes, group)), in_specs...  3.28 us
  transfers between devices with their start and end apart: 28, of which 13 were waited for; matrix products, arithmetic and copies ran while one was open for 1% of the time, Pallas kernels for 15%

profile of v20, /device:TPU:0, one launch (start us, length us, event | category | flops | bytes accessed | tf_op | source)
XLA Modules:
  0.0 67.3 jit_solution(12473984190611703215)
XLA Ops:
  0.6 4.1 %collective-permute-start.3 = (f32[64,256]{1,0:T(8,128)}, f32[64,256]{1,0:T(8,128)S(1)}, u32[]{:S(2)}, u32[]{:S(2)}) collective-permute-start(f32[64,256]{1,0:T(8,128)} %refs_4_.1), channel_id=1, source_target_pairs={{2,0},{3,1},{0,2},{1,3},{6,4},{7,5},{4,6},{5,7},{10,8},{11,9},{8,1... | collective-permute-start | bytes 196616 | tf_op jit(solution)/shard_map/ppermute | solution.py:55
  4.7 1.5 %collective-permute-start = (f32[64,256]{1,0:T(8,128)}, f32[64,256]{1,0:T(8,128)S(1)}, u32[]{:S(2)}, u32[]{:S(2)}) collective-permute-start(f32[64,256]{1,0:T(8,128)} %refs_5_.1), channel_id=1, source_target_pairs={{8,0},{12,4},{0,8},{4,12},{24,16},{28,20},{16,24},{20,28},{9,1},{1... | collective-permute-start | bytes 196616 | tf_op jit(solution)/shard_map/ppermute | solution.py:55
  6.2 1.5 %collective-permute-start.2 = (f32[64,256]{1,0:T(8,128)}, f32[64,256]{1,0:T(8,128)S(1)}, u32[]{:S(2)}, u32[]{:S(2)}) collective-permute-start(f32[64,256]{1,0:T(8,128)} %refs_5_.1), channel_id=1, source_target_pairs={{24,0},{28,4},{16,8},{20,12},{8,16},{12,20},{0,24},{4,28},{25,1},{... | collective-permute-start | bytes 196616 | tf_op jit(solution)/shard_map/ppermute | solution.py:55
  7.7 0.5 collective-permute-start.1
  8.9 3.3 %shard_map.77 = (bf16[8,2048,256]{2,1,0:T(8,128)(2,1)S(1)}, f32[64,256]{1,0:T(8,128)S(1)}, f32[64,256]{1,0:T(8,128)S(1)}, f32[8,128]{1,0:T(8,128)S(1)}) custom-call(s32[1,1,64]{2,1,0:T(1,128)} %refs_0_.1, s32[1,1,64]{2,1,0:T(1,128)} %refs_1_.1, s32[1,1]{1,0:T(1,128)S(6)} %copy.8.refs_2_, f32[1,1,64,128,128]{4,3,2,1,0:T(8,128)} %refs_3_.1, ...), custom_call_target="tpu_custom_call" | custom-call | flops 8388608 | bytes 8388608 | tf_op jit(solution)/shard_map/pallas_call | solution.py:224
  12.2 0.1 collective-permute-done.1.refs_2_
  12.3 0.1 collective-permute-start.4
  12.4 1.6 %collective-permute-start.8 = (f32[2,64,256]{2,1,0:T(8,128)S(1)}, f32[2,64,256]{2,1,0:T(8,128)S(1)}, u32[]{:S(2)}, u32[]{:S(2)}) collective-permute-start(f32[2,64,256]{2,1,0:T(8,128)S(1)} %shard_map.80.refs_4_.refs_0_), channel_id=1, source_target_pairs={{1,0},{0,1},{3,2},{2,3},{5,4},{4,5},{7,6},{6,7},{9,8},{8,9},{11,10... | collective-permute-start | bytes 393224 | tf_op jit(solution)/shard_map/ppermute | solution.py:55
  14.1 0.7 %shard_map.79.refs_2_ = f32[3,64,1024]{2,1,0:T(8,128)S(1)} custom-call(f32[4,64,256]{2,1,0:T(8,128)S(1)} %shard_map.78.refs_0_.refs_1_, bf16[8,2048,256]{2,1,0:T(8,128)(2,1)S(1)} %get-tuple-element.31.refs_1_.refs_3_.refs_2_), custom_call_target="tpu_custom_call" | custom-call | flops 536870912 | tf_op jit(solution)/shard_map/pallas_call | solution.py:72
  14.8 0.8 %shard_map.81 = (f32[64,256]{1,0:T(8,128)S(1)}, f32[64,256]{1,0:T(8,128)S(1)}, f32[64,256]{1,0:T(8,128)S(1)}, f32[64,256]{1,0:T(8,128)S(1)}) custom-call(f32[4,64,256]{2,1,0:T(8,128)S(1)} %collective-permute-done.4.refs_0_, f32[4,64,256]{2,1,0:T(8,128)S(1)} %shard_map.78.refs_0_.refs_1_, f32[3,64,1024]{2,1,0:T(8,128)S(1)} %shard_map.79.refs_2_, ...), custom_call_target="tpu_custom_call" | custom-call | flops 536870912 | tf_op jit(solution)/shard_map/pallas_call | solution.py:72
  15.6 0.5 collective-permute-start.5
  16.1 1.7 %collective-permute-start.6 = (f32[64,256]{1,0:T(8,128)S(1)}, f32[64,256]{1,0:T(8,128)S(1)}, u32[]{:S(2)}, u32[]{:S(2)}) collective-permute-start(f32[64,256]{1,0:T(8,128)S(1)} %get-tuple-element.35.refs_5_), channel_id=1, source_target_pairs={{0,2},{1,3},{2,0},{3,1},{4,6},{5,7},{6,4},{7,5},{8,10},{9,11},{10,... | collective-permute-start | bytes 196616 | tf_op jit(solution)/shard_map/ppermute | solution.py:61
  17.8 2.3 %collective-permute-start.7 = (f32[64,256]{1,0:T(8,128)S(1)}, f32[64,256]{1,0:T(8,128)S(1)}, u32[]{:S(2)}, u32[]{:S(2)}) collective-permute-start(f32[64,256]{1,0:T(8,128)S(1)} %get-tuple-element.36.refs_4_), channel_id=1, source_target_pairs={{0,1},{1,0},{2,3},{3,2},{4,5},{5,4},{6,7},{7,6},{8,9},{9,8},{10,11... | collective-permute-start | bytes 196616 | tf_op jit(solution)/shard_map/ppermute | solution.py:61
  20.1 2.7 %shard_map.82 = (f32[4,64,256]{2,1,0:T(8,128)S(1)}, f32[4,68,256]{2,1,0:T(8,128)S(1)}, f32[16,256]{1,0:T(8,128)S(1)}) custom-call(f32[2,64,256]{2,1,0:T(8,128)S(1)} %shard_map.80.refs_4_.refs_0_, f32[2,64,256]{2,1,0:T(8,128)S(1)} %collective-permute-done.8.refs_1_, bf16[8,2048,256]{2,1,0:T(8,128)(2,1)S(1)} %get-tuple-element.31.refs_1_.refs_3_.refs_2_, ...), custom_call_target="tpu_custom_call" | custom-call | flops 1073741824 | tf_op jit(solution)/shard_map/pallas_call | solution.py:72
  22.8 1.5 %collective-permute-done.6.refs_2_ = f32[64,256]{1,0:T(8,128)S(1)} collective-permute-done((f32[64,256]{1,0:T(8,128)S(1)}, f32[64,256]{1,0:T(8,128)S(1)}, u32[]{:S(2)}, u32[]{:S(2)}) %collective-permute-start.6) | collective-permute-done | bytes 65568 | tf_op jit(solution)/shard_map/ppermute | solution.py:61
  24.3 1.6 %collective-permute-start.11 = (f32[64,256]{1,0:T(8,128)S(1)}, f32[64,256]{1,0:T(8,128)S(1)}, u32[]{:S(2)}, u32[]{:S(2)}) collective-permute-start(f32[64,256]{1,0:T(8,128)S(1)} %shard_map.83.refs_0_.refs_4_), channel_id=1, source_target_pairs={{24,0},{28,4},{16,8},{20,12},{8,16},{12,20},{0,24},{4,28},{25,1},{... | collective-permute-start | bytes 196616 | tf_op jit(solution)/shard_map/ppermute | solution.py:55
  25.9 1.4 %collective-permute-start.10 = (f32[64,256]{1,0:T(8,128)S(1)}, f32[64,256]{1,0:T(8,128)S(1)}, u32[]{:S(2)}, u32[]{:S(2)}) collective-permute-start(f32[64,256]{1,0:T(8,128)S(1)} %shard_map.83.refs_0_.refs_4_), channel_id=1, source_target_pairs={{16,0},{20,4},{24,8},{28,12},{0,16},{4,20},{8,24},{12,28},{17,1},{... | collective-permute-start | bytes 196616 | tf_op jit(solution)/shard_map/ppermute | solution.py:55
  27.2 0.6 collective-permute-start.9
  27.9 2.1 %collective-permute-done.11.refs_3_ = f32[64,256]{1,0:T(8,128)S(1)} collective-permute-done((f32[64,256]{1,0:T(8,128)S(1)}, f32[64,256]{1,0:T(8,128)S(1)}, u32[]{:S(2)}, u32[]{:S(2)}) %collective-permute-start.11) | collective-permute-done | bytes 65568 | tf_op jit(solution)/shard_map/ppermute | solution.py:55
  29.9 0.5 collective-permute-done.10.refs_2_
  30.4 1.1 %collective-permute-done.9.refs_1_ = f32[64,256]{1,0:T(8,128)S(1)} collective-permute-done((f32[64,256]{1,0:T(8,128)S(1)}, f32[64,256]{1,0:T(8,128)S(1)}, u32[]{:S(2)}, u32[]{:S(2)}) %collective-permute-start.9) | collective-permute-done | bytes 65568 | tf_op jit(solution)/shard_map/ppermute | solution.py:55
  31.5 0.1 collective-permute-start.12
  31.6 0.7 %collective-permute-start.17 = (f32[2,72,256]{2,1,0:T(8,128)S(1)}, f32[2,72,256]{2,1,0:T(8,128)S(1)}, u32[]{:S(2)}, u32[]{:S(2)}) collective-permute-start(f32[2,72,256]{2,1,0:T(8,128)S(1)} %get-tuple-element.45), channel_id=1, source_target_pairs={{8,0},{12,4},{0,8},{4,12},{24,16},{28,20},{16,24},{20,28},{9,1},{1... | collective-permute-start | bytes 442376 | tf_op jit(solution)/shard_map/ppermute | solution.py:55
  32.3 0.8 %collective-permute-done.12.refs_0_ = f32[4,64,256]{2,1,0:T(8,128)S(1)} collective-permute-done((f32[4,64,256]{2,1,0:T(8,128)S(1)}, f32[4,64,256]{2,1,0:T(8,128)S(1)}, u32[]{:S(2)}, u32[]{:S(2)}) %collective-permute-start.12) | collective-permute-done | bytes 262176 | tf_op jit(solution)/shard_map/ppermute | solution.py:55
  33.1 1.4 %shard_map.85 = (f32[64,256]{1,0:T(8,128)S(1)}, f32[64,256]{1,0:T(8,128)S(1)}, f32[64,256]{1,0:T(8,128)S(1)}, f32[64,256]{1,0:T(8,128)S(1)}) custom-call(f32[4,64,256]{2,1,0:T(8,128)S(1)} %collective-permute-done.12.refs_0_, f32[4,64,256]{2,1,0:T(8,128)S(1)} %shard_map.84.refs_1_, bf16[8,2048,256]{2,1,0:T(8,128)(2,1)S(1)} %get-tuple-element.31.refs_1_.refs_3_.refs_2_, ...), custom_call_target="tpu_custom_call" | custom-call | flops 1073741824 | tf_op jit(solution)/shard_map/pallas_call | solution.py:72
  34.5 1.7 %collective-permute-start.14 = (f32[64,256]{1,0:T(8,128)S(1)}, f32[64,256]{1,0:T(8,128)S(1)}, u32[]{:S(2)}, u32[]{:S(2)}) collective-permute-start(f32[64,256]{1,0:T(8,128)S(1)} %get-tuple-element.39), channel_id=1, source_target_pairs={{0,3},{1,2},{2,1},{3,0},{4,7},{5,6},{6,5},{7,4},{8,11},{9,10},{10,... | collective-permute-start | bytes 196616 | tf_op jit(solution)/shard_map/ppermute | solution.py:61
  36.3 2.7 %collective-permute-start.16 = (f32[64,256]{1,0:T(8,128)S(1)}, f32[64,256]{1,0:T(8,128)S(1)}, u32[]{:S(2)}, u32[]{:S(2)}) collective-permute-start(f32[64,256]{1,0:T(8,128)S(1)} %get-tuple-element.41), channel_id=1, source_target_pairs={{0,1},{1,0},{2,3},{3,2},{4,5},{5,4},{6,7},{7,6},{8,9},{9,8},{10,11... | collective-permute-start | bytes 196616 | tf_op jit(solution)/shard_map/ppermute | solution.py:61
  39.0 0.8 %collective-permute-start.18 = (f32[1,64,256]{2,1,0:T(8,128)S(1)}, f32[1,64,256]{2,1,0:T(8,128)S(1)}, u32[]{:S(2)}, u32[]{:S(2)}) collective-permute-start(f32[1,64,256]{2,1,0:T(8,128)S(1)} %get-tuple-element.48), channel_id=1, source_target_pairs={{16,0},{20,4},{24,8},{28,12},{0,16},{4,20},{8,24},{12,28},{17,1},{... | collective-permute-start | bytes 196616 | tf_op jit(solution)/shard_map/ppermute | solution.py:55
  39.8 1.3 %collective-permute-start.19 = (f32[16,256]{1,0:T(8,128)S(1)}, f32[16,256]{1,0:T(8,128)S(1)}, u32[]{:S(2)}, u32[]{:S(2)}) collective-permute-start(f32[16,256]{1,0:T(8,128)S(1)} %get-tuple-element.49.refs_7_), channel_id=1, source_target_pairs={{16,0},{20,4},{24,8},{28,12},{0,16},{4,20},{8,24},{12,28},{17,1},{... | collective-permute-start | bytes 49160 | tf_op jit(solution)/shard_map/ppermute | solution.py:55
  41.1 2.4 %collective-permute-done.19.refs_8_ = f32[16,256]{1,0:T(8,128)S(1)} collective-permute-done((f32[16,256]{1,0:T(8,128)S(1)}, f32[16,256]{1,0:T(8,128)S(1)}, u32[]{:S(2)}, u32[]{:S(2)}) %collective-permute-start.19) | collective-permute-done | bytes 16416 | tf_op jit(solution)/shard_map/ppermute | solution.py:55
  43.5 0.4 shard_map.88
  44.0 1.5 %collective-permute-start.22 = (f32[96,256]{1,0:T(8,128)S(1)}, f32[96,256]{1,0:T(8,128)S(1)}, u32[]{:S(2)}, u32[]{:S(2)}) collective-permute-start(f32[96,256]{1,0:T(8,128)S(1)} %get-tuple-element.50.refs_0_), channel_id=1, source_target_pairs={{24,0},{28,4},{16,8},{20,12},{8,16},{12,20},{0,24},{4,28},{25,1},{... | collective-permute-start | bytes 294920 | tf_op jit(solution)/shard_map/ppermute | solution.py:55
  45.5 1.1 %collective-permute-start.21 = (f32[96,256]{1,0:T(8,128)S(1)}, f32[96,256]{1,0:T(8,128)S(1)}, u32[]{:S(2)}, u32[]{:S(2)}) collective-permute-start(f32[96,256]{1,0:T(8,128)S(1)} %get-tuple-element.50.refs_0_), channel_id=1, source_target_pairs={{16,0},{20,4},{24,8},{28,12},{0,16},{4,20},{8,24},{12,28},{17,1},{... | collective-permute-start | bytes 294920 | tf_op jit(solution)/shard_map/ppermute | solution.py:55
  46.6 1.0 %collective-permute-start.20 = (f32[96,256]{1,0:T(8,128)S(1)}, f32[96,256]{1,0:T(8,128)S(1)}, u32[]{:S(2)}, u32[]{:S(2)}) collective-permute-start(f32[96,256]{1,0:T(8,128)S(1)} %get-tuple-element.50.refs_0_), channel_id=1, source_target_pairs={{8,0},{12,4},{0,8},{4,12},{24,16},{28,20},{16,24},{20,28},{9,1},{1... | collective-permute-start | bytes 294920 | tf_op jit(solution)/shard_map/ppermute | solution.py:55
  47.5 3.0 %collective-permute-done.22.refs_3_ = f32[96,256]{1,0:T(8,128)S(1)} collective-permute-done((f32[96,256]{1,0:T(8,128)S(1)}, f32[96,256]{1,0:T(8,128)S(1)}, u32[]{:S(2)}, u32[]{:S(2)}) %collective-permute-start.22) | collective-permute-done | bytes 98336 | tf_op jit(solution)/shard_map/ppermute | solution.py:55
  50.6 1.0 %collective-permute-done.21.refs_2_ = f32[96,256]{1,0:T(8,128)S(1)} collective-permute-done((f32[96,256]{1,0:T(8,128)S(1)}, f32[96,256]{1,0:T(8,128)S(1)}, u32[]{:S(2)}, u32[]{:S(2)}) %collective-permute-start.21) | collective-permute-done | bytes 98336 | tf_op jit(solution)/shard_map/ppermute | solution.py:55
  51.6 0.1 collective-permute-start.23
  51.7 0.8 %shard_map.90.refs_2_ = f32[3,64,1024]{2,1,0:T(8,128)S(1)} custom-call(f32[4,96,256]{2,1,0:T(8,128)S(1)} %shard_map.89.refs_0_.refs_1_, bf16[8,2048,256]{2,1,0:T(8,128)(2,1)S(1)} %get-tuple-element.31.refs_1_.refs_3_.refs_2_), custom_call_target="tpu_custom_call" | custom-call | flops 536870912 | tf_op jit(solution)/shard_map/pallas_call | solution.py:72
  52.4 1.0 %collective-permute-done.23.refs_0_ = f32[4,96,256]{2,1,0:T(8,128)S(1)} collective-permute-done((f32[4,96,256]{2,1,0:T(8,128)S(1)}, f32[4,96,256]{2,1,0:T(8,128)S(1)}, u32[]{:S(2)}, u32[]{:S(2)}) %collective-permute-start.23) | collective-permute-done | bytes 393248 | tf_op jit(solution)/shard_map/ppermute | solution.py:55
  53.4 0.8 %shard_map.91 = (f32[88,256]{1,0:T(8,128)S(1)}, f32[88,256]{1,0:T(8,128)S(1)}, f32[88,256]{1,0:T(8,128)S(1)}, f32[88,256]{1,0:T(8,128)S(1)}) custom-call(f32[4,96,256]{2,1,0:T(8,128)S(1)} %collective-permute-done.23.refs_0_, f32[4,96,256]{2,1,0:T(8,128)S(1)} %shard_map.89.refs_0_.refs_1_, f32[3,64,1024]{2,1,0:T(8,128)S(1)} %shard_map.90.refs_2_, ...), custom_call_target="tpu_custom_call" | custom-call | flops 536870912 | tf_op jit(solution)/shard_map/pallas_call | solution.py:72
  54.2 1.8 %collective-permute-start.24 = (f32[88,256]{1,0:T(8,128)S(1)}, f32[88,256]{1,0:T(8,128)S(1)}, u32[]{:S(2)}, u32[]{:S(2)}) collective-permute-start(f32[88,256]{1,0:T(8,128)S(1)} %get-tuple-element.53), channel_id=1, source_target_pairs={{0,3},{1,2},{2,1},{3,0},{4,7},{5,6},{6,5},{7,4},{8,11},{9,10},{10,... | collective-permute-start | bytes 270344 | tf_op jit(solution)/shard_map/ppermute | solution.py:61
  56.0 2.7 %collective-permute-start.26 = (f32[88,256]{1,0:T(8,128)S(1)}, f32[88,256]{1,0:T(8,128)S(1)}, u32[]{:S(2)}, u32[]{:S(2)}) collective-permute-start(f32[88,256]{1,0:T(8,128)S(1)} %get-tuple-element.55), channel_id=1, source_target_pairs={{0,1},{1,0},{2,3},{3,2},{4,5},{5,4},{6,7},{7,6},{8,9},{9,8},{10,11... | collective-permute-start | bytes 270344 | tf_op jit(solution)/shard_map/ppermute | solution.py:61
  58.7 3.0 %collective-permute-done.24 = f32[88,256]{1,0:T(8,128)S(1)} collective-permute-done((f32[88,256]{1,0:T(8,128)S(1)}, f32[88,256]{1,0:T(8,128)S(1)}, u32[]{:S(2)}, u32[]{:S(2)}) %collective-permute-start.24) | collective-permute-done | bytes 90144 | tf_op jit(solution)/shard_map/ppermute | solution.py:61
  61.6 3.0 %collective-permute-done.25 = f32[88,256]{1,0:T(8,128)S(1)} collective-permute-done((f32[88,256]{1,0:T(8,128)S(1)}, f32[88,256]{1,0:T(8,128)S(1)}, u32[]{:S(2)}, u32[]{:S(2)}) %collective-permute-start.25) | collective-permute-done | bytes 90144 | tf_op jit(solution)/shard_map/ppermute | solution.py:61
  64.6 0.1 collective-permute-start.27
  64.7 0.7 fusion
  65.4 0.5 collective-permute-done.27.refs_1_
  65.9 1.4 %shard_map.92 = f32[3,64,64]{2,1,0:T(8,128)} custom-call(f32[24,256]{1,0:T(8,128)S(1)} %slice_add_fusion.3.refs_0_, f32[24,256]{1,0:T(8,128)S(1)} %collective-permute-done.27.refs_1_), custom_call_target="tpu_custom_call" | custom-call | tf_op jit(solution)/shard_map/pallas_call | solution.py:72
  (26 shorter events, 0.2 us)
Async XLA Ops:
  0.6 11.5 %collective-permute-start.3 = (f32[64,256]{1,0:T(8,128)}, f32[64,256]{1,0:T(8,128)S(1)}, u32[]{:S(2)}, u32[]{:S(2)}) collective-permute-start(f32[64,256]{1,0:T(8,128)} %refs_4_.1), channel_id=1, source_target_pairs={{2,0},{3,1},{0,2},{1,3},{6,4},{7,5},{4,6},{5,7},{10,8},{11,9},{8,1... | collective-permute-start | bytes 196616 | tf_op jit(solution)/shard_map/ppermute | solution.py:55
  4.7 7.4 %collective-permute-start = (f32[64,256]{1,0:T(8,128)}, f32[64,256]{1,0:T(8,128)S(1)}, u32[]{:S(2)}, u32[]{:S(2)}) collective-permute-start(f32[64,256]{1,0:T(8,128)} %refs_5_.1), channel_id=1, source_target_pairs={{8,0},{12,4},{0,8},{4,12},{24,16},{28,20},{16,24},{20,28},{9,1},{1... | collective-permute-start | bytes 196616 | tf_op jit(solution)/shard_map/ppermute | solution.py:55
  6.2 6.0 %collective-permute-start.2 = (f32[64,256]{1,0:T(8,128)}, f32[64,256]{1,0:T(8,128)S(1)}, u32[]{:S(2)}, u32[]{:S(2)}) collective-permute-start(f32[64,256]{1,0:T(8,128)} %refs_5_.1), channel_id=1, source_target_pairs={{24,0},{28,4},{16,8},{20,12},{8,16},{12,20},{0,24},{4,28},{25,1},{... | collective-permute-start | bytes 196616 | tf_op jit(solution)/shard_map/ppermute | solution.py:55
  7.7 4.6 %collective-permute-start.1 = (f32[64,256]{1,0:T(8,128)}, f32[64,256]{1,0:T(8,128)S(1)}, u32[]{:S(2)}, u32[]{:S(2)}) collective-permute-start(f32[64,256]{1,0:T(8,128)} %refs_5_.1), channel_id=1, source_target_pairs={{16,0},{20,4},{24,8},{28,12},{0,16},{4,20},{8,24},{12,28},{17,1},{... | collective-permute-start | bytes 196616 | tf_op jit(solution)/shard_map/ppermute | solution.py:55
  12.3 2.5 %collective-permute-start.4 = (f32[4,64,256]{2,1,0:T(8,128)S(1)}, f32[4,64,256]{2,1,0:T(8,128)S(1)}, u32[]{:S(2)}, u32[]{:S(2)}) collective-permute-start(f32[4,64,256]{2,1,0:T(8,128)S(1)} %shard_map.78.refs_0_.refs_1_), channel_id=1, source_target_pairs={{4,0},{0,4},{12,8},{8,12},{20,16},{16,20},{28,24},{24,28},{5,1},{1... | collective-permute-start | bytes 786440 | tf_op jit(solution)/shard_map/ppermute | solution.py:55
  12.4 7.7 %collective-permute-start.8 = (f32[2,64,256]{2,1,0:T(8,128)S(1)}, f32[2,64,256]{2,1,0:T(8,128)S(1)}, u32[]{:S(2)}, u32[]{:S(2)}) collective-permute-start(f32[2,64,256]{2,1,0:T(8,128)S(1)} %shard_map.80.refs_4_.refs_0_), channel_id=1, source_target_pairs={{1,0},{0,1},{3,2},{2,3},{5,4},{4,5},{7,6},{6,7},{9,8},{8,9},{11,10... | collective-permute-start | bytes 393224 | tf_op jit(solution)/shard_map/ppermute | solution.py:55
  15.6 7.2 %collective-permute-start.5 = (f32[64,256]{1,0:T(8,128)S(1)}, f32[64,256]{1,0:T(8,128)S(1)}, u32[]{:S(2)}, u32[]{:S(2)}) collective-permute-start(f32[64,256]{1,0:T(8,128)S(1)} %get-tuple-element.34.refs_6_), channel_id=1, source_target_pairs={{0,3},{1,2},{2,1},{3,0},{4,7},{5,6},{6,5},{7,4},{8,11},{9,10},{10,... | collective-permute-start | bytes 196616 | tf_op jit(solution)/shard_map/ppermute | solution.py:61
  16.1 8.1 %collective-permute-start.6 = (f32[64,256]{1,0:T(8,128)S(1)}, f32[64,256]{1,0:T(8,128)S(1)}, u32[]{:S(2)}, u32[]{:S(2)}) collective-permute-start(f32[64,256]{1,0:T(8,128)S(1)} %get-tuple-element.35.refs_5_), channel_id=1, source_target_pairs={{0,2},{1,3},{2,0},{3,1},{4,6},{5,7},{6,4},{7,5},{8,10},{9,11},{10,... | collective-permute-start | bytes 196616 | tf_op jit(solution)/shard_map/ppermute | solution.py:61
  17.8 6.5 %collective-permute-start.7 = (f32[64,256]{1,0:T(8,128)S(1)}, f32[64,256]{1,0:T(8,128)S(1)}, u32[]{:S(2)}, u32[]{:S(2)}) collective-permute-start(f32[64,256]{1,0:T(8,128)S(1)} %get-tuple-element.36.refs_4_), channel_id=1, source_target_pairs={{0,1},{1,0},{2,3},{3,2},{4,5},{5,4},{6,7},{7,6},{8,9},{9,8},{10,11... | collective-permute-start | bytes 196616 | tf_op jit(solution)/shard_map/ppermute | solution.py:61
  24.3 5.6 %collective-permute-start.11 = (f32[64,256]{1,0:T(8,128)S(1)}, f32[64,256]{1,0:T(8,128)S(1)}, u32[]{:S(2)}, u32[]{:S(2)}) collective-permute-start(f32[64,256]{1,0:T(8,128)S(1)} %shard_map.83.refs_0_.refs_4_), channel_id=1, source_target_pairs={{24,0},{28,4},{16,8},{20,12},{8,16},{12,20},{0,24},{4,28},{25,1},{... | collective-permute-start | bytes 196616 | tf_op jit(solution)/shard_map/ppermute | solution.py:55
  25.9 4.5 %collective-permute-start.10 = (f32[64,256]{1,0:T(8,128)S(1)}, f32[64,256]{1,0:T(8,128)S(1)}, u32[]{:S(2)}, u32[]{:S(2)}) collective-permute-start(f32[64,256]{1,0:T(8,128)S(1)} %shard_map.83.refs_0_.refs_4_), channel_id=1, source_target_pairs={{16,0},{20,4},{24,8},{28,12},{0,16},{4,20},{8,24},{12,28},{17,1},{... | collective-permute-start | bytes 196616 | tf_op jit(solution)/shard_map/ppermute | solution.py:55
  27.2 4.3 %collective-permute-start.9 = (f32[64,256]{1,0:T(8,128)S(1)}, f32[64,256]{1,0:T(8,128)S(1)}, u32[]{:S(2)}, u32[]{:S(2)}) collective-permute-start(f32[64,256]{1,0:T(8,128)S(1)} %shard_map.83.refs_0_.refs_4_), channel_id=1, source_target_pairs={{8,0},{12,4},{0,8},{4,12},{24,16},{28,20},{16,24},{20,28},{9,1},{1... | collective-permute-start | bytes 196616 | tf_op jit(solution)/shard_map/ppermute | solution.py:55
  27.9 3.7 %collective-permute-start.13 = (f32[4,68,256]{2,1,0:T(8,128)S(1)}, f32[4,68,256]{2,1,0:T(8,128)S(1)}, u32[]{:S(2)}, u32[]{:S(2)}) collective-permute-start(f32[4,68,256]{2,1,0:T(8,128)S(1)} %get-tuple-element.37.refs_4_), channel_id=1, source_target_pairs={{4,0},{0,4},{12,8},{8,12},{20,16},{16,20},{28,24},{24,28},{5,1},{1... | collective-permute-start | bytes 835592 | tf_op jit(solution)/shard_map/ppermute | solution.py:55
  31.5 1.6 %collective-permute-start.12 = (f32[4,64,256]{2,1,0:T(8,128)S(1)}, f32[4,64,256]{2,1,0:T(8,128)S(1)}, u32[]{:S(2)}, u32[]{:S(2)}) collective-permute-start(f32[4,64,256]{2,1,0:T(8,128)S(1)} %shard_map.84.refs_1_), channel_id=1, source_target_pairs={{4,0},{0,4},{12,8},{8,12},{20,16},{16,20},{28,24},{24,28},{5,1},{1... | collective-permute-start | bytes 786440 | tf_op jit(solution)/shard_map/ppermute | solution.py:55
  31.6 7.4 %collective-permute-start.17 = (f32[2,72,256]{2,1,0:T(8,128)S(1)}, f32[2,72,256]{2,1,0:T(8,128)S(1)}, u32[]{:S(2)}, u32[]{:S(2)}) collective-permute-start(f32[2,72,256]{2,1,0:T(8,128)S(1)} %get-tuple-element.45), channel_id=1, source_target_pairs={{8,0},{12,4},{0,8},{4,12},{24,16},{28,20},{16,24},{20,28},{9,1},{1... | collective-permute-start | bytes 442376 | tf_op jit(solution)/shard_map/ppermute | solution.py:55
  34.5 9.0 %collective-permute-start.14 = (f32[64,256]{1,0:T(8,128)S(1)}, f32[64,256]{1,0:T(8,128)S(1)}, u32[]{:S(2)}, u32[]{:S(2)}) collective-permute-start(f32[64,256]{1,0:T(8,128)S(1)} %get-tuple-element.39), channel_id=1, source_target_pairs={{0,3},{1,2},{2,1},{3,0},{4,7},{5,6},{6,5},{7,4},{8,11},{9,10},{10,... | collective-permute-start | bytes 196616 | tf_op jit(solution)/shard_map/ppermute | solution.py:61
  36.3 7.2 %collective-permute-start.15 = (f32[64,256]{1,0:T(8,128)S(1)}, f32[64,256]{1,0:T(8,128)S(1)}, u32[]{:S(2)}, u32[]{:S(2)}) collective-permute-start(f32[64,256]{1,0:T(8,128)S(1)} %get-tuple-element.40), channel_id=1, source_target_pairs={{0,2},{1,3},{2,0},{3,1},{4,6},{5,7},{6,4},{7,5},{8,10},{9,11},{10,... | collective-permute-start | bytes 196616 | tf_op jit(solution)/shard_map/ppermute | solution.py:61
  36.3 7.2 %collective-permute-start.16 = (f32[64,256]{1,0:T(8,128)S(1)}, f32[64,256]{1,0:T(8,128)S(1)}, u32[]{:S(2)}, u32[]{:S(2)}) collective-permute-start(f32[64,256]{1,0:T(8,128)S(1)} %get-tuple-element.41), channel_id=1, source_target_pairs={{0,1},{1,0},{2,3},{3,2},{4,5},{5,4},{6,7},{7,6},{8,9},{9,8},{10,11... | collective-permute-start | bytes 196616 | tf_op jit(solution)/shard_map/ppermute | solution.py:61
  39.0 4.5 %collective-permute-start.18 = (f32[1,64,256]{2,1,0:T(8,128)S(1)}, f32[1,64,256]{2,1,0:T(8,128)S(1)}, u32[]{:S(2)}, u32[]{:S(2)}) collective-permute-start(f32[1,64,256]{2,1,0:T(8,128)S(1)} %get-tuple-element.48), channel_id=1, source_target_pairs={{16,0},{20,4},{24,8},{28,12},{0,16},{4,20},{8,24},{12,28},{17,1},{... | collective-permute-start | bytes 196616 | tf_op jit(solution)/shard_map/ppermute | solution.py:55
  39.8 3.8 %collective-permute-start.19 = (f32[16,256]{1,0:T(8,128)S(1)}, f32[16,256]{1,0:T(8,128)S(1)}, u32[]{:S(2)}, u32[]{:S(2)}) collective-permute-start(f32[16,256]{1,0:T(8,128)S(1)} %get-tuple-element.49.refs_7_), channel_id=1, source_target_pairs={{16,0},{20,4},{24,8},{28,12},{0,16},{4,20},{8,24},{12,28},{17,1},{... | collective-permute-start | bytes 49160 | tf_op jit(solution)/shard_map/ppermute | solution.py:55
  44.0 6.6 %collective-permute-start.22 = (f32[96,256]{1,0:T(8,128)S(1)}, f32[96,256]{1,0:T(8,128)S(1)}, u32[]{:S(2)}, u32[]{:S(2)}) collective-permute-start(f32[96,256]{1,0:T(8,128)S(1)} %get-tuple-element.50.refs_0_), channel_id=1, source_target_pairs={{24,0},{28,4},{16,8},{20,12},{8,16},{12,20},{0,24},{4,28},{25,1},{... | collective-permute-start | bytes 294920 | tf_op jit(solution)/shard_map/ppermute | solution.py:55
  45.5 6.1 %collective-permute-start.21 = (f32[96,256]{1,0:T(8,128)S(1)}, f32[96,256]{1,0:T(8,128)S(1)}, u32[]{:S(2)}, u32[]{:S(2)}) collective-permute-start(f32[96,256]{1,0:T(8,128)S(1)} %get-tuple-element.50.refs_0_), channel_id=1, source_target_pairs={{16,0},{20,4},{24,8},{28,12},{0,16},{4,20},{8,24},{12,28},{17,1},{... | collective-permute-start | bytes 294920 | tf_op jit(solution)/shard_map/ppermute | solution.py:55
  46.6 5.0 %collective-permute-start.20 = (f32[96,256]{1,0:T(8,128)S(1)}, f32[96,256]{1,0:T(8,128)S(1)}, u32[]{:S(2)}, u32[]{:S(2)}) collective-permute-start(f32[96,256]{1,0:T(8,128)S(1)} %get-tuple-element.50.refs_0_), channel_id=1, source_target_pairs={{8,0},{12,4},{0,8},{4,12},{24,16},{28,20},{16,24},{20,28},{9,1},{1... | collective-permute-start | bytes 294920 | tf_op jit(solution)/shard_map/ppermute | solution.py:55
  51.6 1.8 %collective-permute-start.23 = (f32[4,96,256]{2,1,0:T(8,128)S(1)}, f32[4,96,256]{2,1,0:T(8,128)S(1)}, u32[]{:S(2)}, u32[]{:S(2)}) collective-permute-start(f32[4,96,256]{2,1,0:T(8,128)S(1)} %shard_map.89.refs_0_.refs_1_), channel_id=1, source_target_pairs={{4,0},{0,4},{12,8},{8,12},{20,16},{16,20},{28,24},{24,28},{5,1},{1... | collective-permute-start | bytes 1179656 | tf_op jit(solution)/shard_map/ppermute | solution.py:55
  54.2 7.4 %collective-permute-start.24 = (f32[88,256]{1,0:T(8,128)S(1)}, f32[88,256]{1,0:T(8,128)S(1)}, u32[]{:S(2)}, u32[]{:S(2)}) collective-permute-start(f32[88,256]{1,0:T(8,128)S(1)} %get-tuple-element.53), channel_id=1, source_target_pairs={{0,3},{1,2},{2,1},{3,0},{4,7},{5,6},{6,5},{7,4},{8,11},{9,10},{10,... | collective-permute-start | bytes 270344 | tf_op jit(solution)/shard_map/ppermute | solution.py:61
  56.0 8.6 %collective-permute-start.25 = (f32[88,256]{1,0:T(8,128)S(1)}, f32[88,256]{1,0:T(8,128)S(1)}, u32[]{:S(2)}, u32[]{:S(2)}) collective-permute-start(f32[88,256]{1,0:T(8,128)S(1)} %get-tuple-element.54), channel_id=1, source_target_pairs={{0,2},{1,3},{2,0},{3,1},{4,6},{5,7},{6,4},{7,5},{8,10},{9,11},{10,... | collective-permute-start | bytes 270344 | tf_op jit(solution)/shard_map/ppermute | solution.py:61
  56.0 8.6 %collective-permute-start.26 = (f32[88,256]{1,0:T(8,128)S(1)}, f32[88,256]{1,0:T(8,128)S(1)}, u32[]{:S(2)}, u32[]{:S(2)}) collective-permute-start(f32[88,256]{1,0:T(8,128)S(1)} %get-tuple-element.55), channel_id=1, source_target_pairs={{0,1},{1,0},{2,3},{3,2},{4,5},{5,4},{6,7},{7,6},{8,9},{9,8},{10,11... | collective-permute-start | bytes 270344 | tf_op jit(solution)/shard_map/ppermute | solution.py:61
  64.6 1.3 %collective-permute-start.27 = (f32[24,256]{1,0:T(8,128)S(1)}, f32[24,256]{1,0:T(8,128)S(1)}, u32[]{:S(2)}, u32[]{:S(2)}) collective-permute-start(f32[24,256]{1,0:T(8,128)S(1)} %slice_add_fusion.3.refs_0_), channel_id=1, source_target_pairs={{4,0},{0,4},{12,8},{8,12},{20,16},{16,20},{28,24},{24,28},{5,1},{1... | collective-permute-start | bytes 73736 | tf_op jit(solution)/shard_map/ppermute | solution.py:55

commit v21 on v20

--- a/solution.py
+++ b/solution.py
@@ -273,8 +273,7 @@
     tile_len = dense_ref.shape[2] // 2
     for block in range(dense_ref.shape[0]):
         parts = half_products(0, span, pieces_ref, dense_ref, digits, block)
-        for index, part in enumerate(parts):
-            sums_ref[index, :, block * tile_len : (block + 1) * tile_len] = part
+        sums_ref[:, block * tile_len : (block + 1) * tile_len] = combine(*parts)
 
 
 def half_of_core(packed):
@@ -292,11 +291,8 @@
         for sub in range(piece_blocks):
             block = e * piece_blocks + sub
             parts = half_products(1, span, pieces_ref, dense_ref, digits, block)
-            parts = (
-                part + sums_ref[index, :, block * tile_len : (block + 1) * tile_len]
-                for index, part in enumerate(parts)
-            )
-            outs[e][:span, sub * tile_len : (sub + 1) * tile_len] = combine(*parts)
+            first = sums_ref[:, block * tile_len : (block + 1) * tile_len]
+            outs[e][:span, sub * tile_len : (sub + 1) * tile_len] = combine(*parts) + first
     if outs[0].shape[0] > span:
         packed = jnp.sum(pieces_ref[:, span:, :], 0) + jnp.sum(evens_ref[:, span:, :], 0)
         packed = half_of_core(jnp.concatenate([packed, *(tail[...] for tail in tails)], 0))
@@ -340,7 +336,7 @@
     return call(
         functools.partial(first_half_kernel, span),
         [evens, dense],
-        [held(3, span, row_blocks * width // 2)],
+        [held(span, row_blocks * width // 2)],
         scratch=[pltpu.VMEM((2 * span, depth // 2), jnp.bfloat16)],
         limit=VMEM_LIMIT,
         flops=2 * span * dense.size,
@@ -385,7 +381,8 @@
         centred_digits((x_odds if e % 2 else x_evens)[e // 2])
         for e in range(row_blocks // piece_blocks)
     ]
-    term = project([(x, stacked_digits(ref[...])) for x, ref in zip(x_digits, rows_refs)])
+    rows = [stacked_digits(reduce_centered(ref[...])) for ref in rows_refs]
+    term = project([*zip(x_digits, rows)])
     term_ref[...] = term
     part_rows = term.shape[0] // odds_ref.shape[0]
     for place in range(n_row):

time: 67.5 us -> 68.2 us (1.010)
  starting transfers between devices: 32.8 us -> 33.5 us
  transfers between devices with their start and end apart: 28 -> 28, of which waited for: 13 -> 14; matrix products, arithmetic and copies ran while one was open for 1% -> 1% of each run, Pallas kernels for 15% -> 14%
where the time goes in v21:
time: 68.2 us; the launch traced here: 68.1 us
  starting transfers between devices  33.5 us (49%)
  waiting for transfers between devices  20.1 us (29%)
  Pallas kernels  12.4 us (18%)
  between operations  1.47 us (2%)
    ppermute x19, starting transfers between devices, fetch(): lax.ppermute(piece, axis, [(partner(i, shift, size), i) for i in range(si...  20.1 us
    ppermute x9, starting transfers between devices, scatter_pieces(): lax.ppermute(pieces[shift], axis, [(i, partner(i, shift, size)) for i in...  13.4 us
    ppermute x19, waiting for transfers between devices, fetch(): lax.ppermute(piece, axis, [(partner(i, shift, size), i) for i in range(si...  12.7 us
    pallas_call x15, Pallas kernels, call(): pl.pallas_call(body, in_specs=[vmem] * len(operands) + [pl.BlockSpec(memo...  9.33 us
    ppermute x9, waiting for transfers between devices, scatter_pieces(): lax.ppermute(pieces[shift], axis, [(i, partner(i, shift, size)) for i in...  7.36 us
    pallas_call x1, Pallas kernels, build_dense(): pl.pallas_call(functools.partial(build_kernel, (*sizes, group)), in_specs...  3.04 us
  transfers between devices with their start and end apart: 28, of which 14 were waited for; matrix products, arithmetic and copies ran while one was open for 1% of the time, Pallas kernels for 14%

profile of v21, /device:TPU:0, one launch (start us, length us, event | category | flops | bytes accessed | tf_op | source)
XLA Modules:
  0.0 68.1 jit_solution(18336656251555380050)
XLA Ops:
  0.6 4.1 %collective-permute-start.3 = (f32[64,256]{1,0:T(8,128)}, f32[64,256]{1,0:T(8,128)S(1)}, u32[]{:S(2)}, u32[]{:S(2)}) collective-permute-start(f32[64,256]{1,0:T(8,128)} %refs_4_.1), channel_id=1, source_target_pairs={{2,0},{3,1},{0,2},{1,3},{6,4},{7,5},{4,6},{5,7},{10,8},{11,9},{8,1... | collective-permute-start | bytes 196616 | tf_op jit(solution)/shard_map/ppermute | solution.py:55
  4.7 1.5 %collective-permute-start = (f32[64,256]{1,0:T(8,128)}, f32[64,256]{1,0:T(8,128)S(1)}, u32[]{:S(2)}, u32[]{:S(2)}) collective-permute-start(f32[64,256]{1,0:T(8,128)} %refs_5_.1), channel_id=1, source_target_pairs={{8,0},{12,4},{0,8},{4,12},{24,16},{28,20},{16,24},{20,28},{9,1},{1... | collective-permute-start | bytes 196616 | tf_op jit(solution)/shard_map/ppermute | solution.py:55
  6.2 1.5 %collective-permute-start.1 = (f32[64,256]{1,0:T(8,128)}, f32[64,256]{1,0:T(8,128)S(1)}, u32[]{:S(2)}, u32[]{:S(2)}) collective-permute-start(f32[64,256]{1,0:T(8,128)} %refs_5_.1), channel_id=1, source_target_pairs={{16,0},{20,4},{24,8},{28,12},{0,16},{4,20},{8,24},{12,28},{17,1},{... | collective-permute-start | bytes 196616 | tf_op jit(solution)/shard_map/ppermute | solution.py:55
  7.7 0.5 collective-permute-start.2
  8.9 3.0 %shard_map.77 = (bf16[8,2048,256]{2,1,0:T(8,128)(2,1)S(1)}, f32[64,256]{1,0:T(8,128)S(1)}, f32[64,256]{1,0:T(8,128)S(1)}, f32[8,128]{1,0:T(8,128)S(1)}) custom-call(s32[1,1,64]{2,1,0:T(1,128)} %refs_0_.1, s32[1,1,64]{2,1,0:T(1,128)} %refs_1_.1, s32[1,1]{1,0:T(1,128)S(6)} %copy.8.refs_2_, f32[1,1,64,128,128]{4,3,2,1,0:T(8,128)} %refs_3_.1, ...), custom_call_target="tpu_custom_call" | custom-call | flops 8388608 | bytes 8388608 | tf_op jit(solution)/shard_map/pallas_call | solution.py:224
  12.0 1.2 %collective-permute-done.2.refs_3_ = f32[64,256]{1,0:T(8,128)S(1)} collective-permute-done((f32[64,256]{1,0:T(8,128)}, f32[64,256]{1,0:T(8,128)S(1)}, u32[]{:S(2)}, u32[]{:S(2)}) %collective-permute-start.2) | collective-permute-done | bytes 65568 | tf_op jit(solution)/shard_map/ppermute | solution.py:55
  13.1 0.1 collective-permute-start.4
  13.2 1.6 %collective-permute-start.8 = (f32[2,64,256]{2,1,0:T(8,128)S(1)}, f32[2,64,256]{2,1,0:T(8,128)S(1)}, u32[]{:S(2)}, u32[]{:S(2)}) collective-permute-start(f32[2,64,256]{2,1,0:T(8,128)S(1)} %shard_map.80.refs_4_.refs_0_), channel_id=1, source_target_pairs={{1,0},{0,1},{3,2},{2,3},{5,4},{4,5},{7,6},{6,7},{9,8},{8,9},{11,10... | collective-permute-start | bytes 393224 | tf_op jit(solution)/shard_map/ppermute | solution.py:55
  14.9 0.8 %shard_map.79.refs_2_ = f32[64,1024]{1,0:T(8,128)S(1)} custom-call(f32[4,64,256]{2,1,0:T(8,128)S(1)} %shard_map.78.refs_0_.refs_1_, bf16[8,2048,256]{2,1,0:T(8,128)(2,1)S(1)} %get-tuple-element.31.refs_1_.refs_3_.refs_2_), custom_call_target="tpu_custom_call" | custom-call | flops 536870912 | tf_op jit(solution)/shard_map/pallas_call | solution.py:72
  15.7 0.8 %shard_map.81 = (f32[64,256]{1,0:T(8,128)S(1)}, f32[64,256]{1,0:T(8,128)S(1)}, f32[64,256]{1,0:T(8,128)S(1)}, f32[64,256]{1,0:T(8,128)S(1)}) custom-call(f32[4,64,256]{2,1,0:T(8,128)S(1)} %collective-permute-done.4.refs_0_, f32[4,64,256]{2,1,0:T(8,128)S(1)} %shard_map.78.refs_0_.refs_1_, f32[64,1024]{1,0:T(8,128)S(1)} %shard_map.79.refs_2_, ...), custom_call_target="tpu_custom_call" | custom-call | flops 536870912 | tf_op jit(solution)/shard_map/pallas_call | solution.py:72
  16.5 0.5 collective-permute-start.5
  17.0 1.7 %collective-permute-start.6 = (f32[64,256]{1,0:T(8,128)S(1)}, f32[64,256]{1,0:T(8,128)S(1)}, u32[]{:S(2)}, u32[]{:S(2)}) collective-permute-start(f32[64,256]{1,0:T(8,128)S(1)} %get-tuple-element.35.refs_5_), channel_id=1, source_target_pairs={{0,2},{1,3},{2,0},{3,1},{4,6},{5,7},{6,4},{7,5},{8,10},{9,11},{10,... | collective-permute-start | bytes 196616 | tf_op jit(solution)/shard_map/ppermute | solution.py:61
  18.6 2.3 %collective-permute-start.7 = (f32[64,256]{1,0:T(8,128)S(1)}, f32[64,256]{1,0:T(8,128)S(1)}, u32[]{:S(2)}, u32[]{:S(2)}) collective-permute-start(f32[64,256]{1,0:T(8,128)S(1)} %get-tuple-element.36.refs_4_), channel_id=1, source_target_pairs={{0,1},{1,0},{2,3},{3,2},{4,5},{5,4},{6,7},{7,6},{8,9},{9,8},{10,11... | collective-permute-start | bytes 196616 | tf_op jit(solution)/shard_map/ppermute | solution.py:61
  20.9 2.7 %shard_map.82 = (f32[4,64,256]{2,1,0:T(8,128)S(1)}, f32[4,68,256]{2,1,0:T(8,128)S(1)}, f32[16,256]{1,0:T(8,128)S(1)}) custom-call(f32[2,64,256]{2,1,0:T(8,128)S(1)} %shard_map.80.refs_4_.refs_0_, f32[2,64,256]{2,1,0:T(8,128)S(1)} %collective-permute-done.8.refs_1_, bf16[8,2048,256]{2,1,0:T(8,128)(2,1)S(1)} %get-tuple-element.31.refs_1_.refs_3_.refs_2_, ...), custom_call_target="tpu_custom_call" | custom-call | flops 1073741824 | tf_op jit(solution)/shard_map/pallas_call | solution.py:72
  23.7 1.4 %collective-permute-done.6.refs_2_ = f32[64,256]{1,0:T(8,128)S(1)} collective-permute-done((f32[64,256]{1,0:T(8,128)S(1)}, f32[64,256]{1,0:T(8,128)S(1)}, u32[]{:S(2)}, u32[]{:S(2)}) %collective-permute-start.6) | collective-permute-done | bytes 65568 | tf_op jit(solution)/shard_map/ppermute | solution.py:61
  25.1 0.6 collective-permute-start.10
  25.7 1.5 %collective-permute-start.11 = (f32[64,256]{1,0:T(8,128)S(1)}, f32[64,256]{1,0:T(8,128)S(1)}, u32[]{:S(2)}, u32[]{:S(2)}) collective-permute-start(f32[64,256]{1,0:T(8,128)S(1)} %shard_map.83.refs_0_.refs_4_), channel_id=1, source_target_pairs={{24,0},{28,4},{16,8},{20,12},{8,16},{12,20},{0,24},{4,28},{25,1},{... | collective-permute-start | bytes 196616 | tf_op jit(solution)/shard_map/ppermute | solution.py:55
  27.2 1.5 %collective-permute-start.9 = (f32[64,256]{1,0:T(8,128)S(1)}, f32[64,256]{1,0:T(8,128)S(1)}, u32[]{:S(2)}, u32[]{:S(2)}) collective-permute-start(f32[64,256]{1,0:T(8,128)S(1)} %shard_map.83.refs_0_.refs_4_), channel_id=1, source_target_pairs={{8,0},{12,4},{0,8},{4,12},{24,16},{28,20},{16,24},{20,28},{9,1},{1... | collective-permute-start | bytes 196616 | tf_op jit(solution)/shard_map/ppermute | solution.py:55
  28.7 1.0 %collective-permute-done.10.refs_2_ = f32[64,256]{1,0:T(8,128)S(1)} collective-permute-done((f32[64,256]{1,0:T(8,128)S(1)}, f32[64,256]{1,0:T(8,128)S(1)}, u32[]{:S(2)}, u32[]{:S(2)}) %collective-permute-start.10) | collective-permute-done | bytes 65568 | tf_op jit(solution)/shard_map/ppermute | solution.py:55
  29.7 1.2 %collective-permute-done.11.refs_3_ = f32[64,256]{1,0:T(8,128)S(1)} collective-permute-done((f32[64,256]{1,0:T(8,128)S(1)}, f32[64,256]{1,0:T(8,128)S(1)}, u32[]{:S(2)}, u32[]{:S(2)}) %collective-permute-start.11) | collective-permute-done | bytes 65568 | tf_op jit(solution)/shard_map/ppermute | solution.py:55
  30.9 0.8 %collective-permute-done.9.refs_1_ = f32[64,256]{1,0:T(8,128)S(1)} collective-permute-done((f32[64,256]{1,0:T(8,128)S(1)}, f32[64,256]{1,0:T(8,128)S(1)}, u32[]{:S(2)}, u32[]{:S(2)}) %collective-permute-start.9) | collective-permute-done | bytes 65568 | tf_op jit(solution)/shard_map/ppermute | solution.py:55
  31.8 1.4 %collective-permute-start.17 = (f32[2,72,256]{2,1,0:T(8,128)S(1)}, f32[2,72,256]{2,1,0:T(8,128)S(1)}, u32[]{:S(2)}, u32[]{:S(2)}) collective-permute-start(f32[2,72,256]{2,1,0:T(8,128)S(1)} %get-tuple-element.45), channel_id=1, source_target_pairs={{8,0},{12,4},{0,8},{4,12},{24,16},{28,20},{16,24},{20,28},{9,1},{1... | collective-permute-start | bytes 442376 | tf_op jit(solution)/shard_map/ppermute | solution.py:55
  33.2 0.1 collective-permute-done.12.refs_0_
  33.2 1.4 %shard_map.85 = (f32[64,256]{1,0:T(8,128)S(1)}, f32[64,256]{1,0:T(8,128)S(1)}, f32[64,256]{1,0:T(8,128)S(1)}, f32[64,256]{1,0:T(8,128)S(1)}) custom-call(f32[4,64,256]{2,1,0:T(8,128)S(1)} %collective-permute-done.12.refs_0_, f32[4,64,256]{2,1,0:T(8,128)S(1)} %shard_map.84.refs_1_, bf16[8,2048,256]{2,1,0:T(8,128)(2,1)S(1)} %get-tuple-element.31.refs_1_.refs_3_.refs_2_, ...), custom_call_target="tpu_custom_call" | custom-call | flops 1073741824 | tf_op jit(solution)/shard_map/pallas_call | solution.py:72
  34.7 1.9 %collective-permute-start.14 = (f32[64,256]{1,0:T(8,128)S(1)}, f32[64,256]{1,0:T(8,128)S(1)}, u32[]{:S(2)}, u32[]{:S(2)}) collective-permute-start(f32[64,256]{1,0:T(8,128)S(1)} %get-tuple-element.39), channel_id=1, source_target_pairs={{0,3},{1,2},{2,1},{3,0},{4,7},{5,6},{6,5},{7,4},{8,11},{9,10},{10,... | collective-permute-start | bytes 196616 | tf_op jit(solution)/shard_map/ppermute | solution.py:61
  36.6 2.5 %collective-permute-start.16 = (f32[64,256]{1,0:T(8,128)S(1)}, f32[64,256]{1,0:T(8,128)S(1)}, u32[]{:S(2)}, u32[]{:S(2)}) collective-permute-start(f32[64,256]{1,0:T(8,128)S(1)} %get-tuple-element.41), channel_id=1, source_target_pairs={{0,1},{1,0},{2,3},{3,2},{4,5},{5,4},{6,7},{7,6},{8,9},{9,8},{10,11... | collective-permute-start | bytes 196616 | tf_op jit(solution)/shard_map/ppermute | solution.py:61
  39.1 1.1 %collective-permute-start.18 = (f32[1,64,256]{2,1,0:T(8,128)S(1)}, f32[1,64,256]{2,1,0:T(8,128)S(1)}, u32[]{:S(2)}, u32[]{:S(2)}) collective-permute-start(f32[1,64,256]{2,1,0:T(8,128)S(1)} %get-tuple-element.48), channel_id=1, source_target_pairs={{16,0},{20,4},{24,8},{28,12},{0,16},{4,20},{8,24},{12,28},{17,1},{... | collective-permute-start | bytes 196616 | tf_op jit(solution)/shard_map/ppermute | solution.py:55
  40.2 1.0 %collective-permute-start.19 = (f32[16,256]{1,0:T(8,128)S(1)}, f32[16,256]{1,0:T(8,128)S(1)}, u32[]{:S(2)}, u32[]{:S(2)}) collective-permute-start(f32[16,256]{1,0:T(8,128)S(1)} %get-tuple-element.49.refs_7_), channel_id=1, source_target_pairs={{16,0},{20,4},{24,8},{28,12},{0,16},{4,20},{8,24},{12,28},{17,1},{... | collective-permute-start | bytes 49160 | tf_op jit(solution)/shard_map/ppermute | solution.py:55
  41.2 2.7 %collective-permute-done.19.refs_8_ = f32[16,256]{1,0:T(8,128)S(1)} collective-permute-done((f32[16,256]{1,0:T(8,128)S(1)}, f32[16,256]{1,0:T(8,128)S(1)}, u32[]{:S(2)}, u32[]{:S(2)}) %collective-permute-start.19) | collective-permute-done | bytes 16416 | tf_op jit(solution)/shard_map/ppermute | solution.py:55
  44.0 0.5 shard_map.88
  44.4 1.1 %collective-permute-start.20 = (f32[96,256]{1,0:T(8,128)S(1)}, f32[96,256]{1,0:T(8,128)S(1)}, u32[]{:S(2)}, u32[]{:S(2)}) collective-permute-start(f32[96,256]{1,0:T(8,128)S(1)} %get-tuple-element.50.refs_0_), channel_id=1, source_target_pairs={{8,0},{12,4},{0,8},{4,12},{24,16},{28,20},{16,24},{20,28},{9,1},{1... | collective-permute-start | bytes 294920 | tf_op jit(solution)/shard_map/ppermute | solution.py:55
  45.5 1.3 %collective-permute-start.21 = (f32[96,256]{1,0:T(8,128)S(1)}, f32[96,256]{1,0:T(8,128)S(1)}, u32[]{:S(2)}, u32[]{:S(2)}) collective-permute-start(f32[96,256]{1,0:T(8,128)S(1)} %get-tuple-element.50.refs_0_), channel_id=1, source_target_pairs={{16,0},{20,4},{24,8},{28,12},{0,16},{4,20},{8,24},{12,28},{17,1},{... | collective-permute-start | bytes 294920 | tf_op jit(solution)/shard_map/ppermute | solution.py:55
  46.8 1.2 %collective-permute-start.22 = (f32[96,256]{1,0:T(8,128)S(1)}, f32[96,256]{1,0:T(8,128)S(1)}, u32[]{:S(2)}, u32[]{:S(2)}) collective-permute-start(f32[96,256]{1,0:T(8,128)S(1)} %get-tuple-element.50.refs_0_), channel_id=1, source_target_pairs={{24,0},{28,4},{16,8},{20,12},{8,16},{12,20},{0,24},{4,28},{25,1},{... | collective-permute-start | bytes 294920 | tf_op jit(solution)/shard_map/ppermute | solution.py:55
  48.0 1.5 %collective-permute-done.20.refs_1_ = f32[96,256]{1,0:T(8,128)S(1)} collective-permute-done((f32[96,256]{1,0:T(8,128)S(1)}, f32[96,256]{1,0:T(8,128)S(1)}, u32[]{:S(2)}, u32[]{:S(2)}) %collective-permute-start.20) | collective-permute-done | bytes 98336 | tf_op jit(solution)/shard_map/ppermute | solution.py:55
  49.5 1.6 %collective-permute-done.21.refs_2_ = f32[96,256]{1,0:T(8,128)S(1)} collective-permute-done((f32[96,256]{1,0:T(8,128)S(1)}, f32[96,256]{1,0:T(8,128)S(1)}, u32[]{:S(2)}, u32[]{:S(2)}) %collective-permute-start.21) | collective-permute-done | bytes 98336 | tf_op jit(solution)/shard_map/ppermute | solution.py:55
  51.0 1.3 %collective-permute-done.22.refs_3_ = f32[96,256]{1,0:T(8,128)S(1)} collective-permute-done((f32[96,256]{1,0:T(8,128)S(1)}, f32[96,256]{1,0:T(8,128)S(1)}, u32[]{:S(2)}, u32[]{:S(2)}) %collective-permute-start.22) | collective-permute-done | bytes 98336 | tf_op jit(solution)/shard_map/ppermute | solution.py:55
  52.4 0.1 collective-permute-start.23
  52.5 0.8 %shard_map.90.refs_2_ = f32[64,1024]{1,0:T(8,128)S(1)} custom-call(f32[4,96,256]{2,1,0:T(8,128)S(1)} %shard_map.89.refs_0_.refs_1_, bf16[8,2048,256]{2,1,0:T(8,128)(2,1)S(1)} %get-tuple-element.31.refs_1_.refs_3_.refs_2_), custom_call_target="tpu_custom_call" | custom-call | flops 536870912 | tf_op jit(solution)/shard_map/pallas_call | solution.py:72
  53.2 0.9 %collective-permute-done.23.refs_0_ = f32[4,96,256]{2,1,0:T(8,128)S(1)} collective-permute-done((f32[4,96,256]{2,1,0:T(8,128)S(1)}, f32[4,96,256]{2,1,0:T(8,128)S(1)}, u32[]{:S(2)}, u32[]{:S(2)}) %collective-permute-start.23) | collective-permute-done | bytes 393248 | tf_op jit(solution)/shard_map/ppermute | solution.py:55
  54.2 0.8 %shard_map.91 = (f32[88,256]{1,0:T(8,128)S(1)}, f32[88,256]{1,0:T(8,128)S(1)}, f32[88,256]{1,0:T(8,128)S(1)}, f32[88,256]{1,0:T(8,128)S(1)}) custom-call(f32[4,96,256]{2,1,0:T(8,128)S(1)} %collective-permute-done.23.refs_0_, f32[4,96,256]{2,1,0:T(8,128)S(1)} %shard_map.89.refs_0_.refs_1_, f32[64,1024]{1,0:T(8,128)S(1)} %shard_map.90.refs_2_, ...), custom_call_target="tpu_custom_call" | custom-call | flops 536870912 | tf_op jit(solution)/shard_map/pallas_call | solution.py:72
  55.0 1.8 %collective-permute-start.24 = (f32[88,256]{1,0:T(8,128)S(1)}, f32[88,256]{1,0:T(8,128)S(1)}, u32[]{:S(2)}, u32[]{:S(2)}) collective-permute-start(f32[88,256]{1,0:T(8,128)S(1)} %get-tuple-element.53), channel_id=1, source_target_pairs={{0,3},{1,2},{2,1},{3,0},{4,7},{5,6},{6,5},{7,4},{8,11},{9,10},{10,... | collective-permute-start | bytes 270344 | tf_op jit(solution)/shard_map/ppermute | solution.py:61
  56.7 2.7 %collective-permute-start.26 = (f32[88,256]{1,0:T(8,128)S(1)}, f32[88,256]{1,0:T(8,128)S(1)}, u32[]{:S(2)}, u32[]{:S(2)}) collective-permute-start(f32[88,256]{1,0:T(8,128)S(1)} %get-tuple-element.55), channel_id=1, source_target_pairs={{0,1},{1,0},{2,3},{3,2},{4,5},{5,4},{6,7},{7,6},{8,9},{9,8},{10,11... | collective-permute-start | bytes 270344 | tf_op jit(solution)/shard_map/ppermute | solution.py:61
  59.4 3.0 %collective-permute-done.24 = f32[88,256]{1,0:T(8,128)S(1)} collective-permute-done((f32[88,256]{1,0:T(8,128)S(1)}, f32[88,256]{1,0:T(8,128)S(1)}, u32[]{:S(2)}, u32[]{:S(2)}) %collective-permute-start.24) | collective-permute-done | bytes 90144 | tf_op jit(solution)/shard_map/ppermute | solution.py:61
  62.4 3.0 %collective-permute-done.25 = f32[88,256]{1,0:T(8,128)S(1)} collective-permute-done((f32[88,256]{1,0:T(8,128)S(1)}, f32[88,256]{1,0:T(8,128)S(1)}, u32[]{:S(2)}, u32[]{:S(2)}) %collective-permute-start.25) | collective-permute-done | bytes 90144 | tf_op jit(solution)/shard_map/ppermute | solution.py:61
  65.4 0.1 collective-permute-start.27
  65.4 0.7 fusion
  66.1 0.5 collective-permute-done.27.refs_1_
  66.6 1.4 %shard_map.92 = f32[3,64,64]{2,1,0:T(8,128)} custom-call(f32[24,256]{1,0:T(8,128)S(1)} %slice_add_fusion.3.refs_0_, f32[24,256]{1,0:T(8,128)S(1)} %collective-permute-done.27.refs_1_), custom_call_target="tpu_custom_call" | custom-call | tf_op jit(solution)/shard_map/pallas_call | solution.py:72
  (26 shorter events, 0.3 us)
Async XLA Ops:
  0.6 11.3 %collective-permute-start.3 = (f32[64,256]{1,0:T(8,128)}, f32[64,256]{1,0:T(8,128)S(1)}, u32[]{:S(2)}, u32[]{:S(2)}) collective-permute-start(f32[64,256]{1,0:T(8,128)} %refs_4_.1), channel_id=1, source_target_pairs={{2,0},{3,1},{0,2},{1,3},{6,4},{7,5},{4,6},{5,7},{10,8},{11,9},{8,1... | collective-permute-start | bytes 196616 | tf_op jit(solution)/shard_map/ppermute | solution.py:55
  4.7 7.2 %collective-permute-start = (f32[64,256]{1,0:T(8,128)}, f32[64,256]{1,0:T(8,128)S(1)}, u32[]{:S(2)}, u32[]{:S(2)}) collective-permute-start(f32[64,256]{1,0:T(8,128)} %refs_5_.1), channel_id=1, source_target_pairs={{8,0},{12,4},{0,8},{4,12},{24,16},{28,20},{16,24},{20,28},{9,1},{1... | collective-permute-start | bytes 196616 | tf_op jit(solution)/shard_map/ppermute | solution.py:55
  6.2 5.7 %collective-permute-start.1 = (f32[64,256]{1,0:T(8,128)}, f32[64,256]{1,0:T(8,128)S(1)}, u32[]{:S(2)}, u32[]{:S(2)}) collective-permute-start(f32[64,256]{1,0:T(8,128)} %refs_5_.1), channel_id=1, source_target_pairs={{16,0},{20,4},{24,8},{28,12},{0,16},{4,20},{8,24},{12,28},{17,1},{... | collective-permute-start | bytes 196616 | tf_op jit(solution)/shard_map/ppermute | solution.py:55
  7.7 5.4 %collective-permute-start.2 = (f32[64,256]{1,0:T(8,128)}, f32[64,256]{1,0:T(8,128)S(1)}, u32[]{:S(2)}, u32[]{:S(2)}) collective-permute-start(f32[64,256]{1,0:T(8,128)} %refs_5_.1), channel_id=1, source_target_pairs={{24,0},{28,4},{16,8},{20,12},{8,16},{12,20},{0,24},{4,28},{25,1},{... | collective-permute-start | bytes 196616 | tf_op jit(solution)/shard_map/ppermute | solution.py:55
  13.1 2.5 %collective-permute-start.4 = (f32[4,64,256]{2,1,0:T(8,128)S(1)}, f32[4,64,256]{2,1,0:T(8,128)S(1)}, u32[]{:S(2)}, u32[]{:S(2)}) collective-permute-start(f32[4,64,256]{2,1,0:T(8,128)S(1)} %shard_map.78.refs_0_.refs_1_), channel_id=1, source_target_pairs={{4,0},{0,4},{12,8},{8,12},{20,16},{16,20},{28,24},{24,28},{5,1},{1... | collective-permute-start | bytes 786440 | tf_op jit(solution)/shard_map/ppermute | solution.py:55
  13.2 7.7 %collective-permute-start.8 = (f32[2,64,256]{2,1,0:T(8,128)S(1)}, f32[2,64,256]{2,1,0:T(8,128)S(1)}, u32[]{:S(2)}, u32[]{:S(2)}) collective-permute-start(f32[2,64,256]{2,1,0:T(8,128)S(1)} %shard_map.80.refs_4_.refs_0_), channel_id=1, source_target_pairs={{1,0},{0,1},{3,2},{2,3},{5,4},{4,5},{7,6},{6,7},{9,8},{8,9},{11,10... | collective-permute-start | bytes 393224 | tf_op jit(solution)/shard_map/ppermute | solution.py:55
  16.5 7.2 %collective-permute-start.5 = (f32[64,256]{1,0:T(8,128)S(1)}, f32[64,256]{1,0:T(8,128)S(1)}, u32[]{:S(2)}, u32[]{:S(2)}) collective-permute-start(f32[64,256]{1,0:T(8,128)S(1)} %get-tuple-element.34.refs_6_), channel_id=1, source_target_pairs={{0,3},{1,2},{2,1},{3,0},{4,7},{5,6},{6,5},{7,4},{8,11},{9,10},{10,... | collective-permute-start | bytes 196616 | tf_op jit(solution)/shard_map/ppermute | solution.py:61
  17.0 8.1 %collective-permute-start.6 = (f32[64,256]{1,0:T(8,128)S(1)}, f32[64,256]{1,0:T(8,128)S(1)}, u32[]{:S(2)}, u32[]{:S(2)}) collective-permute-start(f32[64,256]{1,0:T(8,128)S(1)} %get-tuple-element.35.refs_5_), channel_id=1, source_target_pairs={{0,2},{1,3},{2,0},{3,1},{4,6},{5,7},{6,4},{7,5},{8,10},{9,11},{10,... | collective-permute-start | bytes 196616 | tf_op jit(solution)/shard_map/ppermute | solution.py:61
  18.6 6.5 %collective-permute-start.7 = (f32[64,256]{1,0:T(8,128)S(1)}, f32[64,256]{1,0:T(8,128)S(1)}, u32[]{:S(2)}, u32[]{:S(2)}) collective-permute-start(f32[64,256]{1,0:T(8,128)S(1)} %get-tuple-element.36.refs_4_), channel_id=1, source_target_pairs={{0,1},{1,0},{2,3},{3,2},{4,5},{5,4},{6,7},{7,6},{8,9},{9,8},{10,11... | collective-permute-start | bytes 196616 | tf_op jit(solution)/shard_map/ppermute | solution.py:61
  25.1 4.5 %collective-permute-start.10 = (f32[64,256]{1,0:T(8,128)S(1)}, f32[64,256]{1,0:T(8,128)S(1)}, u32[]{:S(2)}, u32[]{:S(2)}) collective-permute-start(f32[64,256]{1,0:T(8,128)S(1)} %shard_map.83.refs_0_.refs_4_), channel_id=1, source_target_pairs={{16,0},{20,4},{24,8},{28,12},{0,16},{4,20},{8,24},{12,28},{17,1},{... | collective-permute-start | bytes 196616 | tf_op jit(solution)/shard_map/ppermute | solution.py:55
  25.7 5.2 %collective-permute-start.11 = (f32[64,256]{1,0:T(8,128)S(1)}, f32[64,256]{1,0:T(8,128)S(1)}, u32[]{:S(2)}, u32[]{:S(2)}) collective-permute-start(f32[64,256]{1,0:T(8,128)S(1)} %shard_map.83.refs_0_.refs_4_), channel_id=1, source_target_pairs={{24,0},{28,4},{16,8},{20,12},{8,16},{12,20},{0,24},{4,28},{25,1},{... | collective-permute-start | bytes 196616 | tf_op jit(solution)/shard_map/ppermute | solution.py:55
  27.2 4.4 %collective-permute-start.9 = (f32[64,256]{1,0:T(8,128)S(1)}, f32[64,256]{1,0:T(8,128)S(1)}, u32[]{:S(2)}, u32[]{:S(2)}) collective-permute-start(f32[64,256]{1,0:T(8,128)S(1)} %shard_map.83.refs_0_.refs_4_), channel_id=1, source_target_pairs={{8,0},{12,4},{0,8},{4,12},{24,16},{28,20},{16,24},{20,28},{9,1},{1... | collective-permute-start | bytes 196616 | tf_op jit(solution)/shard_map/ppermute | solution.py:55
  28.7 3.0 %collective-permute-start.13 = (f32[4,68,256]{2,1,0:T(8,128)S(1)}, f32[4,68,256]{2,1,0:T(8,128)S(1)}, u32[]{:S(2)}, u32[]{:S(2)}) collective-permute-start(f32[4,68,256]{2,1,0:T(8,128)S(1)} %get-tuple-element.37.refs_4_), channel_id=1, source_target_pairs={{4,0},{0,4},{12,8},{8,12},{20,16},{16,20},{28,24},{24,28},{5,1},{1... | collective-permute-start | bytes 835592 | tf_op jit(solution)/shard_map/ppermute | solution.py:55
  31.6 1.6 %collective-permute-start.12 = (f32[4,64,256]{2,1,0:T(8,128)S(1)}, f32[4,64,256]{2,1,0:T(8,128)S(1)}, u32[]{:S(2)}, u32[]{:S(2)}) collective-permute-start(f32[4,64,256]{2,1,0:T(8,128)S(1)} %shard_map.84.refs_1_), channel_id=1, source_target_pairs={{4,0},{0,4},{12,8},{8,12},{20,16},{16,20},{28,24},{24,28},{5,1},{1... | collective-permute-start | bytes 786440 | tf_op jit(solution)/shard_map/ppermute | solution.py:55
  31.8 7.3 %collective-permute-start.17 = (f32[2,72,256]{2,1,0:T(8,128)S(1)}, f32[2,72,256]{2,1,0:T(8,128)S(1)}, u32[]{:S(2)}, u32[]{:S(2)}) collective-permute-start(f32[2,72,256]{2,1,0:T(8,128)S(1)} %get-tuple-element.45), channel_id=1, source_target_pairs={{8,0},{12,4},{0,8},{4,12},{24,16},{28,20},{16,24},{20,28},{9,1},{1... | collective-permute-start | bytes 442376 | tf_op jit(solution)/shard_map/ppermute | solution.py:55
  34.7 9.3 %collective-permute-start.14 = (f32[64,256]{1,0:T(8,128)S(1)}, f32[64,256]{1,0:T(8,128)S(1)}, u32[]{:S(2)}, u32[]{:S(2)}) collective-permute-start(f32[64,256]{1,0:T(8,128)S(1)} %get-tuple-element.39), channel_id=1, source_target_pairs={{0,3},{1,2},{2,1},{3,0},{4,7},{5,6},{6,5},{7,4},{8,11},{9,10},{10,... | collective-permute-start | bytes 196616 | tf_op jit(solution)/shard_map/ppermute | solution.py:61
  36.6 7.4 %collective-permute-start.15 = (f32[64,256]{1,0:T(8,128)S(1)}, f32[64,256]{1,0:T(8,128)S(1)}, u32[]{:S(2)}, u32[]{:S(2)}) collective-permute-start(f32[64,256]{1,0:T(8,128)S(1)} %get-tuple-element.40), channel_id=1, source_target_pairs={{0,2},{1,3},{2,0},{3,1},{4,6},{5,7},{6,4},{7,5},{8,10},{9,11},{10,... | collective-permute-start | bytes 196616 | tf_op jit(solution)/shard_map/ppermute | solution.py:61
  36.6 7.4 %collective-permute-start.16 = (f32[64,256]{1,0:T(8,128)S(1)}, f32[64,256]{1,0:T(8,128)S(1)}, u32[]{:S(2)}, u32[]{:S(2)}) collective-permute-start(f32[64,256]{1,0:T(8,128)S(1)} %get-tuple-element.41), channel_id=1, source_target_pairs={{0,1},{1,0},{2,3},{3,2},{4,5},{5,4},{6,7},{7,6},{8,9},{9,8},{10,11... | collective-permute-start | bytes 196616 | tf_op jit(solution)/shard_map/ppermute | solution.py:61
  39.1 4.8 %collective-permute-start.18 = (f32[1,64,256]{2,1,0:T(8,128)S(1)}, f32[1,64,256]{2,1,0:T(8,128)S(1)}, u32[]{:S(2)}, u32[]{:S(2)}) collective-permute-start(f32[1,64,256]{2,1,0:T(8,128)S(1)} %get-tuple-element.48), channel_id=1, source_target_pairs={{16,0},{20,4},{24,8},{28,12},{0,16},{4,20},{8,24},{12,28},{17,1},{... | collective-permute-start | bytes 196616 | tf_op jit(solution)/shard_map/ppermute | solution.py:55
  40.2 3.7 %collective-permute-start.19 = (f32[16,256]{1,0:T(8,128)S(1)}, f32[16,256]{1,0:T(8,128)S(1)}, u32[]{:S(2)}, u32[]{:S(2)}) collective-permute-start(f32[16,256]{1,0:T(8,128)S(1)} %get-tuple-element.49.refs_7_), channel_id=1, source_target_pairs={{16,0},{20,4},{24,8},{28,12},{0,16},{4,20},{8,24},{12,28},{17,1},{... | collective-permute-start | bytes 49160 | tf_op jit(solution)/shard_map/ppermute | solution.py:55
  44.4 5.0 %collective-permute-start.20 = (f32[96,256]{1,0:T(8,128)S(1)}, f32[96,256]{1,0:T(8,128)S(1)}, u32[]{:S(2)}, u32[]{:S(2)}) collective-permute-start(f32[96,256]{1,0:T(8,128)S(1)} %get-tuple-element.50.refs_0_), channel_id=1, source_target_pairs={{8,0},{12,4},{0,8},{4,12},{24,16},{28,20},{16,24},{20,28},{9,1},{1... | collective-permute-start | bytes 294920 | tf_op jit(solution)/shard_map/ppermute | solution.py:55
  45.5 5.5 %collective-permute-start.21 = (f32[96,256]{1,0:T(8,128)S(1)}, f32[96,256]{1,0:T(8,128)S(1)}, u32[]{:S(2)}, u32[]{:S(2)}) collective-permute-start(f32[96,256]{1,0:T(8,128)S(1)} %get-tuple-element.50.refs_0_), channel_id=1, source_target_pairs={{16,0},{20,4},{24,8},{28,12},{0,16},{4,20},{8,24},{12,28},{17,1},{... | collective-permute-start | bytes 294920 | tf_op jit(solution)/shard_map/ppermute | solution.py:55
  46.8 5.5 %collective-permute-start.22 = (f32[96,256]{1,0:T(8,128)S(1)}, f32[96,256]{1,0:T(8,128)S(1)}, u32[]{:S(2)}, u32[]{:S(2)}) collective-permute-start(f32[96,256]{1,0:T(8,128)S(1)} %get-tuple-element.50.refs_0_), channel_id=1, source_target_pairs={{24,0},{28,4},{16,8},{20,12},{8,16},{12,20},{0,24},{4,28},{25,1},{... | collective-permute-start | bytes 294920 | tf_op jit(solution)/shard_map/ppermute | solution.py:55
  52.4 1.8 %collective-permute-start.23 = (f32[4,96,256]{2,1,0:T(8,128)S(1)}, f32[4,96,256]{2,1,0:T(8,128)S(1)}, u32[]{:S(2)}, u32[]{:S(2)}) collective-permute-start(f32[4,96,256]{2,1,0:T(8,128)S(1)} %shard_map.89.refs_0_.refs_1_), channel_id=1, source_target_pairs={{4,0},{0,4},{12,8},{8,12},{20,16},{16,20},{28,24},{24,28},{5,1},{1... | collective-permute-start | bytes 1179656 | tf_op jit(solution)/shard_map/ppermute | solution.py:55
  55.0 7.4 %collective-permute-start.24 = (f32[88,256]{1,0:T(8,128)S(1)}, f32[88,256]{1,0:T(8,128)S(1)}, u32[]{:S(2)}, u32[]{:S(2)}) collective-permute-start(f32[88,256]{1,0:T(8,128)S(1)} %get-tuple-element.53), channel_id=1, source_target_pairs={{0,3},{1,2},{2,1},{3,0},{4,7},{5,6},{6,5},{7,4},{8,11},{9,10},{10,... | collective-permute-start | bytes 270344 | tf_op jit(solution)/shard_map/ppermute | solution.py:61
  56.7 8.6 %collective-permute-start.25 = (f32[88,256]{1,0:T(8,128)S(1)}, f32[88,256]{1,0:T(8,128)S(1)}, u32[]{:S(2)}, u32[]{:S(2)}) collective-permute-start(f32[88,256]{1,0:T(8,128)S(1)} %get-tuple-element.54), channel_id=1, source_target_pairs={{0,2},{1,3},{2,0},{3,1},{4,6},{5,7},{6,4},{7,5},{8,10},{9,11},{10,... | collective-permute-start | bytes 270344 | tf_op jit(solution)/shard_map/ppermute | solution.py:61
  56.7 8.6 %collective-permute-start.26 = (f32[88,256]{1,0:T(8,128)S(1)}, f32[88,256]{1,0:T(8,128)S(1)}, u32[]{:S(2)}, u32[]{:S(2)}) collective-permute-start(f32[88,256]{1,0:T(8,128)S(1)} %get-tuple-element.55), channel_id=1, source_target_pairs={{0,1},{1,0},{2,3},{3,2},{4,5},{5,4},{6,7},{7,6},{8,9},{9,8},{10,11... | collective-permute-start | bytes 270344 | tf_op jit(solution)/shard_map/ppermute | solution.py:61
  65.4 1.3 %collective-permute-start.27 = (f32[24,256]{1,0:T(8,128)S(1)}, f32[24,256]{1,0:T(8,128)S(1)}, u32[]{:S(2)}, u32[]{:S(2)}) collective-permute-start(f32[24,256]{1,0:T(8,128)S(1)} %slice_add_fusion.3.refs_0_), channel_id=1, source_target_pairs={{4,0},{0,4},{12,8},{8,12},{20,16},{16,20},{28,24},{24,28},{5,1},{1... | collective-permute-start | bytes 73736 | tf_op jit(solution)/shard_map/ppermute | solution.py:55
